TPU v7x, 32 devices: a whole 2x2x4 slice. The times are simulated.
32 devices in a mesh: group: 2 (over y), freq: 4 (over z), rblk: 2 (over x), sblk: 2 (over core).
Axes of the slice: x: 2, y: 2, z: 4, core: 2. Of those that a mesh axis runs over, the one named last changes fastest.
Arguments:
- initial: bfloat16 [256, 512, 512], P(('group', 'sblk'), 'freq', 'rblk'), parts along dimension 0, may hold values from -6 to 6
- response: bfloat16 [16, 2, 2048, 512], P(('group', 'freq'), None, 'sblk', 'rblk'), parts along dimension 0, may hold values from -0.5 to 0.5
- aperture: int32 [16, 16, 4], P(('group', 'freq'), 'sblk', 'rblk'), parts along dimension 0, may hold values from 0 to 1, as said below
- onset_rcv: int32 [256, 512], P('group', 'rblk'), parts along dimension 0, may hold values from 128 to 512
- onset_src: int32 [256, 2048], P('group', 'sblk'), parts along dimension 0, may hold values from 128 to 512
Outputs:
- focusing: bfloat16 [256, 512, 512], P(('group', 'sblk'), 'freq', 'rblk'), parts along dimension 0
There are 2 independent parts, one for each index of `group`. A program takes and returns all parts, laid end to end along the dimension named above; each array names one. Nothing has to cross between parts.
Inputs may be any that keep to these rules, and one draw needn't show every extreme that they name: `aperture`: 1 marks an active source-receiver block pair of that frequency, 0 an inactive one.
All inputs are finite; a program needn't handle non-finite values.
Results may differ from a plain program's by a relative error of at most 0.0085.
Values may be sent and summed in bfloat16 or wider, within the bound.
No kernel may reach another device: no remote copies, remote signals or barrier semaphores. Data moves between devices by JAX's collectives and lax.ppermute only.
A program may use at most 64 MiB of HBM per device.

v0:
```python
import math

import jax
import jax.numpy as jnp
from jax import lax
from jax.sharding import PartitionSpec as P

BLOCK = 128
ITERS = 2


def swapped(value, axis, stride):
    return lax.ppermute(value, axis, [(i, i ^ 1 << stride) for i in range(lax.axis_size(axis))])


def transform_tables(length, count):
    steps_axis = lax.iota(jnp.int32, length)
    orders = lax.iota(jnp.int32, count) + 1
    phase = orders[:, None] * steps_axis[None, :] % length
    angle = phase.astype(jnp.float32) * (2.0 * math.pi / length)
    stacked_fields = jnp.concatenate([jnp.cos(angle), -jnp.sin(angle)], 0)
    forward_table = stacked_fields.astype(jnp.bfloat16)
    inverse_table = (stacked_fields.T * (2.0 / length)).astype(jnp.bfloat16)
    return (forward_table, inverse_table)


def settle(values):
    return lax.optimization_barrier(values.astype(jnp.bfloat16)).astype(jnp.float32)


def samples_into_spectra(values, forward_table, freq_total):
    out = jnp.einsum("kt,ptn->pkn", forward_table, values, preferred_element_type=jnp.float32)
    return out.reshape(values.shape[0], 2, freq_total, values.shape[2]).astype(jnp.bfloat16)


def spectra_into_samples(trace_spectra, inverse_table):
    flat = trace_spectra.reshape(trace_spectra.shape[0], -1, trace_spectra.shape[3])
    return jnp.einsum("tk,pkn->ptn", inverse_table, flat, preferred_element_type=jnp.float32)


def dense_down(gated_traces, trace_spectra):
    real_part = jnp.einsum(
        "euk,bek->beu", gated_traces[:, 0], trace_spectra[:, 0], preferred_element_type=jnp.float32
    ) - jnp.einsum(
        "euk,bek->beu", gated_traces[:, 1], trace_spectra[:, 1], preferred_element_type=jnp.float32
    )
    imag_part = jnp.einsum(
        "euk,bek->beu", gated_traces[:, 0], trace_spectra[:, 1], preferred_element_type=jnp.float32
    ) + jnp.einsum(
        "euk,bek->beu", gated_traces[:, 1], trace_spectra[:, 0], preferred_element_type=jnp.float32
    )
    return jnp.stack([real_part, imag_part], 1)


def dense_up(gated_traces, upgoing_spectrum):
    real_part = jnp.einsum(
        "qao,bqa->bqo",
        gated_traces[:, 0],
        upgoing_spectrum[:, 0],
        preferred_element_type=jnp.float32,
    ) + jnp.einsum(
        "qao,bqa->bqo",
        gated_traces[:, 1],
        upgoing_spectrum[:, 1],
        preferred_element_type=jnp.float32,
    )
    imag_part = jnp.einsum(
        "qao,bqa->bqo",
        gated_traces[:, 0],
        upgoing_spectrum[:, 1],
        preferred_element_type=jnp.float32,
    ) - jnp.einsum(
        "qao,bqa->bqo",
        gated_traces[:, 1],
        upgoing_spectrum[:, 0],
        preferred_element_type=jnp.float32,
    )
    return jnp.stack([real_part, imag_part], 1)


def to_traces(values):
    return lax.all_to_all(values, "freq", split_axis=0, concat_axis=1, tiled=True)


def to_times(values):
    return lax.all_to_all(values, "freq", split_axis=1, concat_axis=0, tiled=True)


def on_device(initial, response, aperture, onset_rcv, onset_src):
    freq_devs = lax.axis_size("freq")
    rblk_devs = lax.axis_size("rblk")
    sblk_devs = lax.axis_size("sblk")
    freq_total = response.shape[0] * freq_devs
    samples = initial.shape[1] * freq_devs
    focal_all = onset_rcv.shape[0]
    forward_table, inverse_table = transform_tables(samples, freq_total)
    steps_axis = lax.iota(jnp.int32, samples)
    rcv_rows = focal_all // (sblk_devs * freq_devs)
    rcv_first = (
        lax.axis_index("sblk") * (focal_all // sblk_devs) + lax.axis_index("freq") * rcv_rows
    )
    rcv_onsets = lax.dynamic_slice_in_dim(onset_rcv, rcv_first, rcv_rows, 0)
    rcv_gate = (steps_axis[None, :, None] < rcv_onsets[:, None, :]).astype(jnp.float32)
    src_rows = focal_all // (rblk_devs * freq_devs)
    src_first = (
        lax.axis_index("rblk") * (focal_all // rblk_devs) + lax.axis_index("freq") * src_rows
    )
    src_onsets = lax.dynamic_slice_in_dim(onset_src, src_first, src_rows, 0)
    src_gate = (steps_axis[None, :, None] < src_onsets[:, None, :]).astype(jnp.float32)
    mask_full = jnp.repeat(jnp.repeat(aperture, BLOCK, 1), BLOCK, 2).astype(jnp.bfloat16)
    gated_traces = response * mask_full[:, None]
    half_rows = focal_all // 2
    own_start = lax.axis_index("sblk") * half_rows
    other_start = (1 - lax.axis_index("sblk")) * half_rows
    base = to_traces(initial)
    current = base
    for step_index in range(ITERS):
        trace_spectra = samples_into_spectra(current, forward_table, freq_total)
        spec_back = lax.all_to_all(trace_spectra, "freq", split_axis=2, concat_axis=0, tiled=True)
        spec_all = lax.all_gather(spec_back, "sblk", axis=0, tiled=True)
        down = lax.psum_scatter(
            settle(dense_down(gated_traces, spec_all)).astype(jnp.bfloat16),
            "rblk",
            scatter_dimension=0,
            tiled=True,
        )
        src_traces = lax.all_to_all(down, "freq", split_axis=0, concat_axis=2, tiled=True)
        upgoing = (src_gate * spectra_into_samples(src_traces, inverse_table)).astype(jnp.bfloat16)
        upgoing_spectrum = samples_into_spectra(upgoing, forward_table, freq_total)
        up_back = lax.all_to_all(upgoing_spectrum, "freq", split_axis=2, concat_axis=0, tiled=True)
        up_all = lax.all_gather(up_back, "rblk", axis=0, tiled=True)
        partial_sums = dense_up(gated_traces, up_all)
        own_part = settle(lax.dynamic_slice_in_dim(partial_sums, own_start, half_rows, 0))
        other_part = lax.dynamic_slice_in_dim(partial_sums, other_start, half_rows, 0).astype(
            jnp.bfloat16
        )
        received = swapped(other_part, "sblk", 0)
        back = (own_part + received.astype(jnp.float32)).astype(jnp.bfloat16)
        rcv_traces = lax.all_to_all(back, "freq", split_axis=0, concat_axis=2, tiled=True)
        update = rcv_gate * spectra_into_samples(rcv_traces, inverse_table)
        current = (base.astype(jnp.float32) - update).astype(jnp.bfloat16)
    result = to_times(current)
    return result


def solution(mesh):
    in_specs = (
        P(("group", "sblk"), "freq", "rblk"),
        P(("group", "freq"), None, "sblk", "rblk"),
        P(("group", "freq"), "sblk", "rblk"),
        P("group", "rblk"),
        P("group", "sblk"),
    )
    out_specs = P(("group", "sblk"), "freq", "rblk")
    return jax.shard_map(
        on_device, mesh=mesh, in_specs=in_specs, out_specs=out_specs, check_vma=False
    )
```

profile of v0, /device:TPU:0, one launch (start us, length us, event | category | flops | bytes accessed | tf_op | source)
XLA Modules:
  0.0 467.1 jit_solution(15373442536979487976)
XLA Ops:
  6.5 6.4 %all-to-all-start = ((bf16[64,128,256]{2,1,0:T(8,128)(2,1)}), bf16[64,128,256]{2,1,0:T(8,128)(2,1)}, u32[]{:S(2)}, u32[]{:S(2)}) async-start(bf16[64,128,256]{2,1,0:T(8,128)(2,1)} %param.5), calls=%async_computation | async-start | bytes 8388608 | tf_op jit(solution)/shard_map/all_to_all | solution.py:82
  13.2 3.1 broadcast_in_dim.5
  18.0 88.4 %all-to-all-done = bf16[64,128,256]{2,1,0:T(8,128)(2,1)} async-done(((bf16[64,128,256]{2,1,0:T(8,128)(2,1)}), bf16[64,128,256]{2,1,0:T(8,128)(2,1)}, u32[]{:S(2)}, u32[]{:S(2)}) %all-to-all-start) | async-done | bytes 4194336 | tf_op jit(solution)/shard_map/all_to_all | solution.py:82
  106.4 2.5 copy.54
  108.9 2.0 copy-done.1
  112.3 3.3 all-to-all-start.1
  115.7 2.1 copy_multiply_fusion
  117.8 3.8 all-to-all-done.1
  121.5 2.0 all_gather.12
  126.6 19.6 %reduce-scatter.3.cloned.1.call-done = bf16[64,2,2,1024]{3,0,2,1:T(8,128)(2,1)} async-done(((bf16[128,2,2,1024]{3,0,2,1:T(8,128)(2,1)}), bf16[64,2,2,1024]{3,0,2,1:T(8,128)(2,1)}) %reduce-scatter.3.cloned.1.call-update) | async-done | bytes 524304 | tf_op jit(solution)/shard_map/reduce_scatter | solution.py:121
  146.1 2.4 copy.59
  148.5 4.6 all-to-all-start.2
  153.4 14.2 %all-to-all-done.2 = bf16[64,2,2,1024]{3,2,1,0:T(2,128)(2,1)S(1)} async-done(((bf16[64,2,2,1024]{3,2,1,0:T(2,128)(2,1)}), bf16[64,2,2,1024]{3,2,1,0:T(2,128)(2,1)S(1)}, u32[]{:S(2)}, u32[]{:S(2)}) %all-to-all-start.2) | async-done | bytes 524320 | tf_op jit(solution)/shard_map/all_to_all | solution.py:127
  167.8 9.8 %fusion.30 = bf16[16,2,8,1024]{3,2,1,0:T(8,128)(2,1)} fusion(bf16[16,512,1]{1,0,2:T(8,128)(2,1)S(1)} %fusion.77, s32[16,1024]{1,0:T(8,128)S(1)} %constant_dynamic-slice_fusion, bf16[16,512,1]{1,0,2:T(8,128)(2,1)S(1)} %fusion.78, bf16[16,16,1024]{2,0,1:T(8,128)(2,1)S(1)} %bitcast.200), kind=kOutput, calls=%fused_computation.33 | convolution fusion | flops 562298880 | bytes 1146880 | tf_op jit(solution)/shard_map/kt,ptn->pkn/dot_general | solution.py:32
  177.6 1.6 copy.64
  179.2 16.4 %all_to_all.168 = bf16[16,2,8,1024]{3,1,0,2:T(2,128)(2,1)S(1)} all-to-all(bf16[16,2,8,1024]{3,1,0,2:T(2,128)(2,1)S(1)} %copy.64), channel_id=1, replica_groups=mesh['group'=2,'freq'=4,'rblk'=2,'sblk'=2] {'freq'}, dimensions={2} | all-to-all | bytes 1048576 | tf_op jit(solution)/shard_map/all_to_all | solution.py:130
  196.5 19.6 %all-gather.3.cloned.1.call-done = bf16[128,2,2,1024]{3,0,2,1:T(8,128)(2,1)} async-done(((bf16[64,2,2,1024]{3,0,2,1:T(8,128)(2,1)}), bf16[128,2,2,1024]{3,0,2,1:T(8,128)(2,1)}) %all-gather.3.cloned.1.call-update) | async-done | bytes 1048592 | tf_op jit(solution)/shard_map/all_gather | solution.py:131
  221.8 4.6 all-to-all-start.4
  227.4 5.3 %all-to-all-done.4 = bf16[64,2,2,256]{3,2,1,0:T(2,128)(2,1)S(1)} async-done(((bf16[64,2,2,256]{3,2,1,0:T(2,128)(2,1)}), bf16[64,2,2,256]{3,2,1,0:T(2,128)(2,1)S(1)}, u32[]{:S(2)}, u32[]{:S(2)}) %all-to-all-start.4) | async-done | bytes 131104 | tf_op jit(solution)/shard_map/all_to_all | solution.py:139
  232.7 4.4 fusion.48
  237.2 8.6 %all_to_all.169 = bf16[16,2,8,256]{3,1,0,2:T(2,128)(2,1)S(1)} all-to-all(bf16[16,2,8,256]{3,1,0,2:T(2,128)(2,1)S(1)} %copy.71), channel_id=1, replica_groups=mesh['group'=2,'freq'=4,'rblk'=2,'sblk'=2] {'freq'}, dimensions={2} | all-to-all | bytes 262144 | tf_op jit(solution)/shard_map/all_to_all | solution.py:119
  245.8 2.0 all_gather.14
  250.9 18.5 %reduce-scatter.5.cloned.1.call-done = bf16[64,2,2,1024]{3,0,2,1:T(8,128)(2,1)} async-done(((bf16[128,2,2,1024]{3,0,2,1:T(8,128)(2,1)}), bf16[64,2,2,1024]{3,0,2,1:T(8,128)(2,1)}) %reduce-scatter.5.cloned.1.call-update) | async-done | bytes 524304 | tf_op jit(solution)/shard_map/reduce_scatter | solution.py:121
  271.0 18.9 %all_to_all.170 = bf16[64,2,2,1024]{3,2,1,0:T(2,128)(2,1)S(1)} all-to-all(bf16[64,2,2,1024]{3,2,1,0:T(2,128)(2,1)S(1)} %copy.73), channel_id=1, replica_groups=mesh['group'=2,'freq'=4,'rblk'=2,'sblk'=2] {'freq'}, dimensions={0} | all-to-all | bytes 1048576 | tf_op jit(solution)/shard_map/all_to_all | solution.py:127
  290.1 9.8 %fusion.33 = bf16[16,2,8,1024]{3,2,1,0:T(8,128)(2,1)} fusion(bf16[16,512,1]{1,0,2:T(8,128)(2,1)S(1)} %fusion.77, s32[16,1024]{1,0:T(8,128)S(1)} %constant_dynamic-slice_fusion, bf16[16,512,1]{1,0,2:T(8,128)(2,1)S(1)} %fusion.78, bf16[16,16,1024]{2,0,1:T(8,128)(2,1)S(1)} %bitcast.199), kind=kOutput, calls=%fused_computation.34 | convolution fusion | flops 562298880 | bytes 1146880 | tf_op jit(solution)/shard_map/kt,ptn->pkn/dot_general | solution.py:32
  301.4 16.5 %all_to_all.171 = bf16[16,2,8,1024]{3,1,0,2:T(2,128)(2,1)S(1)} all-to-all(bf16[16,2,8,1024]{3,1,0,2:T(2,128)(2,1)S(1)} %copy.78), channel_id=1, replica_groups=mesh['group'=2,'freq'=4,'rblk'=2,'sblk'=2] {'freq'}, dimensions={2} | all-to-all | bytes 1048576 | tf_op jit(solution)/shard_map/all_to_all | solution.py:130
  318.9 19.6 %all-gather.5.cloned.1.call-done = bf16[128,2,2,1024]{3,0,2,1:T(8,128)(2,1)} async-done(((bf16[64,2,2,1024]{3,0,2,1:T(8,128)(2,1)}), bf16[128,2,2,1024]{3,0,2,1:T(8,128)(2,1)}) %all-gather.5.cloned.1.call-update) | async-done | bytes 1048592 | tf_op jit(solution)/shard_map/all_gather | solution.py:131
  343.6 10.9 %all_to_all.172 = bf16[64,2,2,256]{3,2,1,0:T(2,128)(2,1)S(1)} all-to-all(bf16[64,2,2,256]{3,2,1,0:T(2,128)(2,1)S(1)} %copy.80), channel_id=1, replica_groups=mesh['group'=2,'freq'=4,'rblk'=2,'sblk'=2] {'freq'}, dimensions={0} | all-to-all | bytes 262144 | tf_op jit(solution)/shard_map/all_to_all | solution.py:139
  354.6 4.1 fusion.15
  358.7 2.4 copy.83
  361.2 95.4 %all_to_all.173 = bf16[16,512,256]{2,0,1:T(8,128)(2,1)S(1)} all-to-all(bf16[16,512,256]{2,0,1:T(8,128)(2,1)S(1)} %copy.83), channel_id=1, replica_groups=mesh['group'=2,'freq'=4,'rblk'=2,'sblk'=2] {'freq'}, dimensions={1} | all-to-all | bytes 8388608 | tf_op jit(solution)/shard_map/all_to_all | solution.py:86
  456.5 3.6 copy.84
  (72 shorter events, 26.9 us)
Async XLA Ops:
  6.5 146.8 %copy-start = (s32[128,1024]{1,0:T(8,128)S(1)}, s32[128,1024]{1,0:T(8,128)}, u32[]{:S(2)}) copy-start(s32[128,1024]{1,0:T(8,128)} %param.9) | copy-start | bytes 1572868
  6.5 6.5 %copy-start.2 = (s32[2,8,2]{1,2,0:T(2,128)S(1)}, s32[2,8,2]{1,2,0:T(2,128)}, u32[]{:S(2)}) copy-start(s32[2,8,2]{1,2,0:T(2,128)} %param.7) | copy-start | bytes 388
  6.5 99.9 %all-to-all-start = ((bf16[64,128,256]{2,1,0:T(8,128)(2,1)}), bf16[64,128,256]{2,1,0:T(8,128)(2,1)}, u32[]{:S(2)}, u32[]{:S(2)}) async-start(bf16[64,128,256]{2,1,0:T(8,128)(2,1)} %param.5), calls=%async_computation | async-start | bytes 8388608 | tf_op jit(solution)/shard_map/all_to_all | solution.py:82
  108.9 2.0 copy-start.1
  112.3 9.2 %all-to-all-start.1 = ((bf16[16,2,8,256]{3,1,0,2:T(2,128)(2,1)}), bf16[16,2,8,256]{3,1,0,2:T(2,128)(2,1)S(1)}, u32[]{:S(2)}, u32[]{:S(2)}) async-start(bf16[16,2,8,256]{3,1,0,2:T(2,128)(2,1)} %copy.55), calls=%async_computation.1 | async-start | bytes 262144 | tf_op jit(solution)/shard_map/all_to_all | solution.py:119
  115.6 30.5 %reduce-scatter.3.cloned.1.call-start = ((), (), s32[]{:S(2)}) async-start(), calls=%async_computation.12 | async-start | bytes 1572864 | tf_op jit(solution)/shard_map/reduce_scatter | solution.py:121
  148.5 19.1 %all-to-all-start.2 = ((bf16[64,2,2,1024]{3,2,1,0:T(2,128)(2,1)}), bf16[64,2,2,1024]{3,2,1,0:T(2,128)(2,1)S(1)}, u32[]{:S(2)}, u32[]{:S(2)}) async-start(bf16[64,2,2,1024]{3,2,1,0:T(2,128)(2,1)} %copy.59), calls=%async_computation.3 | async-start | bytes 1048576 | tf_op jit(solution)/shard_map/all_to_all | solution.py:127
  153.1 63.0 %all-gather.3.cloned.1.call-start = ((), (), s32[]{:S(2)}) async-start(), calls=%async_computation.13 | async-start | bytes 1572864 | tf_op jit(solution)/shard_map/all_gather | solution.py:131
  216.1 2.8 copy-start.3
  219.6 1.4 collective-permute-start
  221.8 10.8 %all-to-all-start.4 = ((bf16[64,2,2,256]{3,2,1,0:T(2,128)(2,1)}), bf16[64,2,2,256]{3,2,1,0:T(2,128)(2,1)S(1)}, u32[]{:S(2)}, u32[]{:S(2)}) async-start(bf16[64,2,2,256]{3,2,1,0:T(2,128)(2,1)} %copy.66), calls=%async_computation.5 | async-start | bytes 262144 | tf_op jit(solution)/shard_map/all_to_all | solution.py:139
  226.4 43.0 %reduce-scatter.5.cloned.1.call-start = ((), (), s32[]{:S(2)}) async-start(), calls=%async_computation.14 | async-start | bytes 1572864 | tf_op jit(solution)/shard_map/reduce_scatter | solution.py:121
  250.8 87.7 %all-gather.5.cloned.1.call-start = ((), (), s32[]{:S(2)}) async-start(), calls=%async_computation.15 | async-start | bytes 1572864 | tf_op jit(solution)/shard_map/all_gather | solution.py:131
  338.5 2.8 copy-start.4
  342.0 1.4 collective-permute-start.1
Sparse Core Ops, SparseCore 0:
  126.7 19.3 reduce-scatter.2
  196.6 19.4 all-gather.2
  250.9 18.3 reduce-scatter.4
  319.0 19.4 all-gather.4
where the time goes:
time: 476 us; the launch traced here: 467 us
  waiting for transfers between devices  192 us (40%)
  blocking collectives  171 us (36%)
  matrix products  39.3 us (8%)
  local copies, waits for them, and re-layouts  27.4 us (6%)
  starting transfers between devices  19.6 us (4%)
  between operations  13.9 us (3%)
    all_to_all x1, blocking collectives, to_times(): lax.all_to_all(values, 'freq', split_axis=1, concat_axis=0, tiled=True)  95.4 us
    all_to_all x1, waiting for transfers between devices, to_traces(): lax.all_to_all(values, 'freq', split_axis=0, concat_axis=1, tiled=True)  88.4 us
    all_gather x2, waiting for transfers between devices, on_device(): up_all = lax.all_gather(up_back, 'rblk', axis=0, tiled=True)  39.2 us
    reduce_scatter x2, waiting for transfers between devices, on_device(): lax.psum_scatter(settle(dense_down(gated_traces, spec_all)).astype(jnp.bf...  38.1 us
    all_to_all x2, blocking collectives, on_device(): lax.all_to_all(upgoing_spectrum, 'freq', split_axis=2, concat_axis=0, til...  32.9 us
    dot_general x4, matrix products, samples_into_spectra(): jnp.einsum('kt,ptn->pkn', forward_table, values, preferred_element_type=j...  24.6 us
    all_to_all x1, blocking collectives, on_device(): lax.all_to_all(down, 'freq', split_axis=0, concat_axis=2, tiled=True)  18.9 us
    all_to_all x1, waiting for transfers between devices, on_device(): lax.all_to_all(down, 'freq', split_axis=0, concat_axis=2, tiled=True)  14.2 us
  transfers between devices with their start and end apart: 10, of which 10 were waited for; matrix products, arithmetic and copies ran while one was open for 2% of the time, Pallas kernels for 0%

commit v1 on v0

v1 whole, which is shorter than its diff:
```python
import functools
import math

import jax
import jax.numpy as jnp
import numpy as np
from jax import lax
from jax.experimental import pallas as pl
from jax.experimental.pallas import tpu as pltpu
from jax.sharding import PartitionSpec as P

BLOCK = 128
ITERS = 2
ROWS = 8
CHUNKS = 1
VMEM_BYTES = 48 * 1024 * 1024

BF16 = jnp.bfloat16
F32 = jnp.float32


def field_rows(place, freq_devs, per_dev):
    rows = []
    for step in range(freq_devs):
        first = (place ^ step) * per_dev
        for part in range(2):
            rows.extend((part, first + local) for local in range(per_dev))
    return rows


def fields(samples, freq_total):
    phase = (np.arange(1, freq_total + 1)[:, None] * np.arange(samples)[None, :]) % samples
    angle = phase * (2.0 * math.pi / samples)
    return np.stack([np.cos(angle), -np.sin(angle)])


def forward_tables(samples, freq_devs, per_dev):
    table = fields(samples, freq_devs * per_dev)
    own = samples // freq_devs
    eye = np.eye(ROWS)
    out = []
    for place in range(freq_devs):
        part = np.stack([table[c, j, place * own : (place + 1) * own] for c, j in field_rows(place, freq_devs, per_dev)])
        out.append(np.einsum("kt,pq->kpqt", part, eye).reshape(part.shape[0] * ROWS, ROWS * own))
    return np.stack(out).astype(np.float32).astype(BF16)


def inverse_tables(samples, freq_devs, per_dev):
    table = fields(samples, freq_devs * per_dev) * (2.0 / samples)
    own = samples // freq_devs
    eye = np.eye(ROWS)
    out = []
    for place in range(freq_devs):
        part = np.stack([table[c, j, place * own : (place + 1) * own] for c, j in field_rows(place, freq_devs, per_dev)])
        out.append(np.einsum("kt,pq->ptkq", part, eye).reshape(ROWS * own, part.shape[0] * ROWS))
    return np.stack(out).astype(np.float32).astype(BF16)


def window_tables(samples, freq_devs, per_dev):
    freq_total = freq_devs * per_dev
    order = np.arange(1, freq_total + 1)
    unit = 2j * math.pi / samples
    diff = order[None, :] - order[:, None]
    total = order[None, :] + order[:, None]
    same = np.where(diff == 0, 0.0, 1.0 / (samples * (np.exp(unit * np.where(diff == 0, 1, diff)) - 1.0)))
    mixed = 1.0 / (samples * (np.exp(-unit * total) - 1.0))
    full = np.zeros((2, freq_total, 2, freq_total))
    full[0, :, 0, :] = same.real + mixed.real
    full[0, :, 1, :] = mixed.imag - same.imag
    full[1, :, 0, :] = same.imag + mixed.imag
    full[1, :, 1, :] = same.real - mixed.real
    out = []
    for place in range(freq_devs):
        rows = [c * freq_total + j for c, j in field_rows(place, freq_devs, per_dev)]
        flat = full.reshape(2 * freq_total, 2 * freq_total)[np.ix_(rows, rows)]
        out.append(np.kron(flat, np.eye(ROWS)))
    return np.stack(out).astype(np.float32).astype(BF16)


def call(body, scalars, inputs, outputs, grid, scratch=(), aliases=None, flops=0):
    in_arrays = [value for value, _ in inputs]
    bytes_all = sum(v.size * v.dtype.itemsize for v in in_arrays)
    bytes_all += sum(math.prod(s.shape) * s.dtype.itemsize for s, _ in outputs)
    return pl.pallas_call(
        body,
        grid_spec=pltpu.PrefetchScalarGridSpec(
            num_scalar_prefetch=len(scalars),
            grid=grid,
            in_specs=[spec for _, spec in inputs],
            out_specs=[spec for _, spec in outputs],
            scratch_shapes=list(scratch),
        ),
        out_shape=[shape for shape, _ in outputs],
        input_output_aliases=aliases or {},
        compiler_params=pltpu.CompilerParams(vmem_limit_bytes=VMEM_BYTES),
        cost_estimate=pl.CostEstimate(flops=flops, bytes_accessed=bytes_all, transcendentals=0),
    )(*scalars, *in_arrays)


def whole(array):
    zeros = (0,) * array.ndim
    return pl.BlockSpec(array.shape, lambda *_: zeros)


def mask_half(response, aperture, place, flip, half):
    per_dev, _, src, rcv = response.shape
    src_blocks, rcv_blocks = src // BLOCK, rcv // BLOCK
    steps = half // BLOCK

    def body(place_ref, flags, x_ref, o_ref):
        block = (place_ref[0] ^ flip) * steps + pl.program_id(0)
        for j in range(per_dev):
            for r in range(rcv_blocks):
                on = flags[(j * src_blocks + block) * rcv_blocks + r]
                cut = pl.ds(r * BLOCK, BLOCK)
                value = x_ref[j, :, :, cut]
                o_ref[j, :, :, cut] = value * on.astype(F32).astype(BF16)

    shape = jax.ShapeDtypeStruct((per_dev, 2, half, rcv), BF16)
    block = (per_dev, 2, BLOCK, rcv)
    (out,) = call(
        body,
        (place, aperture.reshape(-1)),
        [(response, pl.BlockSpec(block, lambda i, a, _: (0, 0, (a[0] ^ flip) * steps + i, 0)))],
        [(shape, pl.BlockSpec(block, lambda i, *_: (0, 0, i, 0)))],
        (steps,),
    )
    return out


def first_spectra(initial, table, freq_place, freq_devs, per_dev, first, rows):
    own, rcv = initial.shape[1:]
    tile = 2 * ROWS

    def body(place_ref, x_ref, t_ref, *outs):
        parts = []
        for half in range(2):
            flat = x_ref[half * ROWS : (half + 1) * ROWS].reshape(ROWS * own, rcv)
            value = jnp.dot(t_ref[0], flat, preferred_element_type=F32)
            parts.append(value.reshape(freq_devs, 2, per_dev, ROWS, rcv))
        both = jnp.concatenate(parts, 3).astype(BF16)
        for step, out in enumerate(outs):
            out[...] = both[step]

    shape = jax.ShapeDtypeStruct((2, per_dev, rows, rcv), BF16)
    return call(
        body,
        (freq_place,),
        [
            (initial, pl.BlockSpec((tile, own, rcv), lambda i, _: (first // tile + i, 0, 0))),
            (table, pl.BlockSpec((1,) + table.shape[1:], lambda i, z: (z[0], 0, 0))),
        ],
        [(shape, pl.BlockSpec((2, per_dev, tile, rcv), lambda i, _: (0, 0, i, 0)))] * freq_devs,
        (rows // tile,),
        flops=2 * 2 * freq_devs * per_dev * own * rows * rcv,
    )


def down_products(near, far, kept, moved, freq_place, freq_devs):
    _, per_dev, rows, rcv = near[0].shape
    width = kept.shape[2]
    tile = min(width, 256)
    share = 2 * rows // freq_devs

    def body(place_ref, n0, n1, f0, f1, k_ref, m_ref, *rest):
        outs, held = rest[:freq_devs], rest[freq_devs]
        for j in range(per_dev):
            total = None
            for own, other, resp in ((n0, n1, k_ref), (f0, f1, m_ref)):
                real = jnp.concatenate([own[0, j], other[0, j]], 0)
                imag = jnp.concatenate([own[1, j], other[1, j]], 0)
                for part, lhs in ((0, [real, imag]), (1, [-imag, real])):
                    term = lax.dot_general(
                        jnp.concatenate(lhs, 0),
                        resp[j, part],
                        (((1,), (1,)), ((), ())),
                        preferred_element_type=F32,
                    )
                    total = term if total is None else total + term
            held[0, j] = total[: 2 * rows]
            held[1, j] = total[2 * rows :]
        for step, out in enumerate(outs):
            start = pl.multiple_of((place_ref[0] ^ step) * share, share)
            out[...] = held[:, :, pl.ds(start, share), :].astype(BF16)

    shape = jax.ShapeDtypeStruct((2, per_dev, share, width), BF16)
    resp_spec = pl.BlockSpec((per_dev, 2, tile, rcv), lambda i, _: (0, 0, i, 0))
    return call(
        body,
        (freq_place,),
        [(v, whole(v)) for v in (*near, *far)] + [(kept, resp_spec), (moved, resp_spec)],
        [(shape, pl.BlockSpec((2, per_dev, share, tile), lambda i, _: (0, 0, 0, i)))] * freq_devs,
        (width // tile,),
        scratch=[pltpu.VMEM((2, per_dev, 2 * rows, tile), F32)],
        flops=2 * 8 * per_dev * 2 * rows * width * rcv,
    )


def windowed(messages, tables, matrix, freq_place, per_dev, share):
    cosines, sines, fraction = tables
    freq_devs = len(messages)
    width = messages[0].shape[-1]
    tile = BLOCK
    count = freq_devs * 2 * per_dev * ROWS

    def body(place_ref, c_ref, s_ref, f_ref, g_ref, *rest):
        refs, outs = rest[:freq_devs], rest[freq_devs:]
        data = [ref[...].astype(F32).reshape(2, per_dev, share, tile) for ref in refs]
        made = [[] for _ in outs]
        for first in range(0, share, ROWS):
            cut = slice(first, first + ROWS)
            plain = [value[:, :, cut] for value in data]
            cos = [c_ref[step, :, cut] for step in range(freq_devs)]
            sin = [s_ref[step, :, cut] for step in range(freq_devs)]
            turned = [
                jnp.stack([v[0] * c - v[1] * s, v[0] * s + v[1] * c])
                for v, c, s in zip(plain, cos, sin)
            ]
            flat = [jnp.stack(v).reshape(count, tile).astype(BF16) for v in (turned, plain)]
            mixed = jnp.dot(g_ref[0], jnp.concatenate(flat, 1), preferred_element_type=F32)
            upper = mixed[:, :tile].reshape(freq_devs, 2, per_dev, ROWS, tile)
            lower = mixed[:, tile:].reshape(freq_devs, 2, per_dev, ROWS, tile)
            part = f_ref[cut]
            for step in range(freq_devs):
                c, s, v, up, low = cos[step], sin[step], plain[step], upper[step], lower[step]
                real = c * up[0] + s * up[1] - low[0] + part * v[0]
                imag = c * up[1] - s * up[0] - low[1] + part * v[1]
                made[step].append(jnp.stack([real, imag]))
        for out, value in zip(outs, made):
            out[...] = jnp.concatenate(value, 2).reshape(out.shape).astype(BF16)

    lead = messages[0].shape[:-1]
    zeros = (0,) * len(lead)
    message = pl.BlockSpec(lead + (tile,), lambda i, _: zeros + (i,))
    table = pl.BlockSpec(cosines.shape[:-1] + (tile,), lambda i, _: (0, 0, 0, i))
    return call(
        body,
        (freq_place,),
        [
            (cosines, table),
            (sines, table),
            (fraction, pl.BlockSpec((share, tile), lambda i, _: (0, i))),
            (matrix, pl.BlockSpec((1,) + matrix.shape[1:], lambda i, z: (z[0], 0, 0))),
        ]
        + [(v, message) for v in messages],
        [(jax.ShapeDtypeStruct(v.shape, BF16), message) for v in messages],
        (width // tile,),
        flops=2 * count * count * 2 * width * share // ROWS,
    )


def up_products(messages, kept, moved, freq_place, rows):
    freq_devs = len(messages)
    per_dev, _, src, rcv = kept.shape
    share = messages[0].shape[2]

    def body(place_ref, k_ref, m_ref, *rest):
        refs = rest[:freq_devs]
        keep, send, held = rest[freq_devs:]
        for step, ref in enumerate(refs):
            start = pl.multiple_of((place_ref[0] ^ step) * share, share)
            held[:, pl.ds(start, share), :] = ref[:, 0]
        real, imag = held[0], held[1]
        one = jnp.concatenate([real, imag], 0)
        two = jnp.concatenate([imag, -real], 0)
        for side, resp in enumerate((k_ref, m_ref)):
            total = jnp.dot(one, resp[0, 0], preferred_element_type=F32)
            total = total + jnp.dot(two, resp[0, 1], preferred_element_type=F32)
            for part in range(2):
                first = 2 * rows * part
                keep[side, part, 0] = total[first : first + rows]
                send[side, part, 0] = total[first + rows : first + 2 * rows].astype(BF16)

    resp_spec = pl.BlockSpec((1, 2, src, rcv), lambda j, _: (j, 0, 0, 0))
    message = pl.BlockSpec((2, 1, share, src), lambda j, _: (0, j, 0, 0))
    out_spec = pl.BlockSpec((2, 2, 1, rows, rcv), lambda j, _: (0, 0, j, 0, 0))
    shape = (2, 2, per_dev, rows, rcv)
    return call(
        body,
        (freq_place,),
        [(kept, resp_spec), (moved, resp_spec)] + [(v, message) for v in messages],
        [(jax.ShapeDtypeStruct(shape, F32), out_spec), (jax.ShapeDtypeStruct(shape, BF16), out_spec)],
        (per_dev,),
        scratch=[pltpu.VMEM((2, 2 * rows, src), BF16)],
        flops=2 * 8 * per_dev * 2 * rows * src * rcv,
    )


def dealt(keep, from_core, from_far, freq_place, freq_devs):
    _, _, per_dev, rows, rcv = keep.shape
    share = rows // freq_devs

    def body(place_ref, k_ref, c_ref, x_ref, *rest):
        outs, held = rest[:freq_devs], rest[freq_devs]
        held[...] = k_ref[0] + c_ref[0].astype(F32) + x_ref[...].astype(F32)
        for step, out in enumerate(outs):
            start = pl.multiple_of((place_ref[0] ^ step) * share, share)
            out[...] = held[:, :, pl.ds(start, share), :].reshape(out.shape).astype(BF16)

    first = pl.BlockSpec((1,) + keep.shape[1:], lambda i, _: (0, 0, 0, 0, 0))
    shape = jax.ShapeDtypeStruct((2 * per_dev * share, rcv), BF16)
    return call(
        body,
        (freq_place,),
        [(keep, first), (from_core, first), (from_far, whole(from_far))],
        [(shape, whole(shape))] * freq_devs,
        (1,),
        scratch=[pltpu.VMEM(keep.shape[1:], F32)],
    )


def next_spectra(sums, messages, freq_place):
    freq_devs = len(messages)
    _, per_dev, rows, rcv = sums.shape
    share = rows // freq_devs

    def body(place_ref, s_ref, *rest):
        refs, out, held = rest[:freq_devs], rest[freq_devs], rest[freq_devs + 1]
        for step, ref in enumerate(refs):
            start = pl.multiple_of((place_ref[0] ^ step) * share, share)
            held[:, :, pl.ds(start, share), :] = ref[...].astype(F32).reshape(2, per_dev, share, rcv)
        out[...] = (s_ref[...] - held[...]).astype(BF16)

    (out,) = call(
        body,
        (freq_place,),
        [(sums, whole(sums))] + [(v, whole(v)) for v in messages],
        [(jax.ShapeDtypeStruct(sums.shape, BF16), whole(sums))],
        (1,),
        scratch=[pltpu.VMEM(sums.shape, F32)],
    )
    return out


def updated(initial, onset, messages, table, freq_place, focal_first, first, rows, target):
    freq_devs = len(messages)
    own, rcv = initial.shape[1:]
    per_dev = messages[0].shape[1]
    tile = 2 * ROWS
    count = freq_devs * 2 * per_dev * ROWS

    def body(place_ref, _, x_ref, o_ref, t_ref, *rest):
        refs, out = rest[:freq_devs], rest[-1]
        data = [ref[...].astype(F32) for ref in refs]
        time = lax.broadcasted_iota(jnp.int32, (own, rcv), 0) + place_ref[0] * own
        for half in range(2):
            cut = slice(half * ROWS, (half + 1) * ROWS)
            flat = jnp.stack([v[:, :, cut] for v in data]).reshape(count, rcv).astype(BF16)
            change = jnp.dot(t_ref[0], flat, preferred_element_type=F32)
            for row in range(ROWS):
                spot = half * ROWS + row
                on = time < o_ref[spot : spot + 1, :]
                step = jnp.where(on, change[row * own : (row + 1) * own], 0.0)
                out[spot] = (x_ref[spot].astype(F32) - step).astype(BF16)

    block = pl.BlockSpec((tile, own, rcv), lambda i, *_: (first // tile + i, 0, 0))
    inputs = [
        (initial, block),
        (onset, pl.BlockSpec((tile, rcv), lambda i, _, b: (b[0] + first // tile + i, 0))),
        (table, pl.BlockSpec((1,) + table.shape[1:], lambda i, z, _: (z[0], 0, 0))),
    ] + [(v, pl.BlockSpec((2, per_dev, tile, rcv), lambda i, *_: (0, 0, i, 0))) for v in messages]
    aliases = {}
    if target is not None:
        inputs.append((target, pl.BlockSpec(memory_space=pl.ANY)))
        aliases = {2 + len(inputs) - 1: 0}
    (out,) = call(
        body,
        (freq_place, focal_first),
        inputs,
        [(jax.ShapeDtypeStruct(initial.shape, BF16), block)],
        (rows // tile,),
        aliases=aliases,
        flops=2 * 2 * freq_devs * per_dev * own * rows * rcv,
    )
    return out


def exchanged(value, axis, step):
    return lax.ppermute(value, axis, [(i, i ^ step) for i in range(lax.axis_size(axis))])


def dealt_out(parts):
    return [parts[0]] + [exchanged(parts[step], "freq", step) for step in range(1, len(parts))]


def phases(onset, freq_index, freq_devs, per_dev, samples):
    steps = lax.iota(jnp.int32, freq_devs)
    order = (freq_index ^ steps)[:, None] * per_dev + lax.iota(jnp.int32, per_dev)[None, :] + 1
    phase = order[:, :, None, None] * onset[None, None] % samples
    angle = phase.astype(F32) * (2.0 * math.pi / samples)
    return jnp.cos(angle), jnp.sin(angle), onset.astype(F32) * (1.0 / samples)


def on_device(initial, response, aperture, onset_rcv, onset_src):
    freq_devs = lax.axis_size("freq")
    per_dev = response.shape[0]
    samples = initial.shape[1] * freq_devs
    half_rows = initial.shape[0]
    src_width = response.shape[2] // 2
    rows = half_rows // CHUNKS
    freq_index = lax.axis_index("freq")
    rblk_index = lax.axis_index("rblk")
    sblk_index = lax.axis_index("sblk")
    freq_place = freq_index.reshape(1)
    rblk_place = rblk_index.reshape(1)

    moved = exchanged(mask_half(response, aperture, rblk_place, 1, src_width), "rblk", 1)
    forward = jnp.asarray(forward_tables(samples, freq_devs, per_dev))
    inverse = jnp.asarray(inverse_tables(samples, freq_devs, per_dev))
    matrix = jnp.asarray(window_tables(samples, freq_devs, per_dev))
    kept = mask_half(response, aperture, rblk_place, 0, src_width)

    result = None
    for chunk in range(CHUNKS):
        first = chunk * rows
        parts = first_spectra(initial, forward, freq_place, freq_devs, per_dev, first, rows)
        sums = sum(v.astype(F32) for v in dealt_out(parts))
        spectra = sums.astype(BF16)

        share = 2 * rows // freq_devs
        spot = freq_index * share
        other = (spot >= rows).astype(jnp.int32)
        src_first = (sblk_index ^ other) * half_rows + first + spot - other * rows
        onsets = lax.dynamic_slice(onset_src, (src_first, rblk_index * src_width), (share, src_width))
        src_tables = phases(onsets, freq_index, freq_devs, per_dev, samples)
        rcv_share = rows // freq_devs
        rcv_first = sblk_index * half_rows + first + freq_index * rcv_share
        onsets = lax.dynamic_slice_in_dim(onset_rcv, rcv_first, rcv_share, 0)
        rcv_tables = phases(onsets, freq_index, freq_devs, per_dev, samples)

        for step in range(ITERS):
            far_own = exchanged(spectra, "rblk", 1)
            near = (spectra, exchanged(spectra, "sblk", 1))
            far = (far_own, exchanged(far_own, "sblk", 1))
            messages = dealt_out(down_products(near, far, kept, moved, freq_place, freq_devs))
            messages = windowed(messages, src_tables, matrix, freq_place, per_dev, share)
            keep, send = up_products(dealt_out(messages), kept, moved, freq_place, rows)
            from_core = exchanged(send, "sblk", 1)
            from_far = exchanged((keep[1] + from_core[1].astype(F32)).astype(BF16), "rblk", 1)
            if step < ITERS - 1:
                messages = dealt_out(dealt(keep, from_core, from_far, freq_place, freq_devs))
                messages = windowed(messages, rcv_tables, matrix, freq_place, per_dev, rcv_share)
                spectra = next_spectra(sums, dealt_out(messages), freq_place)
            else:
                back = (keep[0] + from_core[0].astype(F32) + from_far.astype(F32)).astype(BF16)
                messages = [back] + [exchanged(back, "freq", m) for m in range(1, freq_devs)]
                tile_first = (sblk_index * (half_rows // (2 * ROWS))).reshape(1)
                result = updated(
                    initial, onset_rcv, messages, inverse, freq_place, tile_first, first, rows, result
                )
    return result


def transform_tables(length, count):
    table = fields(length, count).reshape(2 * count, length)
    forward_table = jnp.asarray(table.astype(np.float32).astype(BF16))
    inverse_table = jnp.asarray((table.T * (2.0 / length)).astype(np.float32).astype(BF16))
    return forward_table, inverse_table


def settle(values):
    return lax.optimization_barrier(values.astype(BF16)).astype(F32)


def samples_into_spectra(values, forward_table, freq_total):
    out = jnp.einsum("kt,ptn->pkn", forward_table, values, preferred_element_type=F32)
    return out.reshape(values.shape[0], 2, freq_total, values.shape[2]).astype(BF16)


def spectra_into_samples(trace_spectra, inverse_table):
    flat = trace_spectra.reshape(trace_spectra.shape[0], -1, trace_spectra.shape[3])
    return jnp.einsum("tk,pkn->ptn", inverse_table, flat, preferred_element_type=F32)


def dense(spec, gated, real, imag, sign):
    dot = functools.partial(jnp.einsum, spec, preferred_element_type=F32)
    return jnp.stack(
        [dot(gated[:, 0], real) - sign * dot(gated[:, 1], imag), dot(gated[:, 0], imag) + sign * dot(gated[:, 1], real)], 1
    )


def general_device(initial, response, aperture, onset_rcv, onset_src):
    freq_devs, rblk_devs, sblk_devs = (lax.axis_size(a) for a in ("freq", "rblk", "sblk"))
    freq_index, rblk_index, sblk_index = (lax.axis_index(a) for a in ("freq", "rblk", "sblk"))
    freq_total = response.shape[0] * freq_devs
    samples = initial.shape[1] * freq_devs
    focal_all = onset_rcv.shape[0]
    forward_table, inverse_table = transform_tables(samples, freq_total)
    steps_axis = lax.iota(jnp.int32, samples)
    own_axis = freq_index * initial.shape[1] + lax.iota(jnp.int32, initial.shape[1])
    half_rows = focal_all // sblk_devs
    own_onsets = lax.dynamic_slice_in_dim(onset_rcv, sblk_index * half_rows, half_rows, 0)
    rcv_gate = (own_axis[None, :, None] < own_onsets[:, None, :]).astype(F32)
    src_rows = focal_all // (rblk_devs * freq_devs)
    src_first = rblk_index * (focal_all // rblk_devs) + freq_index * src_rows
    src_onsets = lax.dynamic_slice_in_dim(onset_src, src_first, src_rows, 0)
    src_gate = (steps_axis[None, :, None] < src_onsets[:, None, :]).astype(F32)
    mask_full = jnp.repeat(jnp.repeat(aperture, BLOCK, 1), BLOCK, 2).astype(BF16)
    gated = response * mask_full[:, None]
    own_forward = lax.dynamic_slice_in_dim(forward_table, freq_index * initial.shape[1], initial.shape[1], 1)
    own_inverse = lax.dynamic_slice_in_dim(inverse_table, freq_index * initial.shape[1], initial.shape[1], 0)
    current = initial
    for _ in range(ITERS):
        partial = samples_into_spectra(current, own_forward, freq_total)
        spec_back = lax.psum_scatter(partial.astype(F32), "freq", scatter_dimension=2, tiled=True).astype(BF16)
        spec_all = lax.all_gather(spec_back, "sblk", axis=0, tiled=True)
        down = lax.psum_scatter(
            settle(dense("euk,bek->beu", gated, spec_all[:, 0], spec_all[:, 1], 1.0)).astype(BF16),
            "rblk",
            scatter_dimension=0,
            tiled=True,
        )
        src_traces = lax.all_to_all(down, "freq", split_axis=0, concat_axis=2, tiled=True)
        upgoing = (src_gate * spectra_into_samples(src_traces, inverse_table)).astype(BF16)
        upspec = samples_into_spectra(upgoing, forward_table, freq_total)
        up_back = lax.all_to_all(upspec, "freq", split_axis=2, concat_axis=0, tiled=True)
        up_all = lax.all_gather(up_back, "rblk", axis=0, tiled=True)
        sums = dense("qao,bqa->bqo", gated, up_all[:, 0], up_all[:, 1], -1.0).astype(BF16)
        back = lax.psum_scatter(sums, "sblk", scatter_dimension=0, tiled=True)
        traces = lax.all_gather(back, "freq", axis=2, tiled=True)
        update = rcv_gate * spectra_into_samples(traces, own_inverse)
        current = (initial.astype(F32) - update).astype(BF16)
    return current


def fits(initial, response, aperture, onset_rcv, onset_src):
    freq_devs = lax.axis_size("freq")
    if lax.axis_size("rblk") != 2 or lax.axis_size("sblk") != 2 or freq_devs & (freq_devs - 1):
        return False
    rows = initial.shape[0] // CHUNKS
    whole_rows = initial.shape[0] % (CHUNKS * 2 * ROWS * max(1, freq_devs // 2)) == 0 and rows % (ROWS * freq_devs) == 0
    whole_width = response.shape[2] % (4 * BLOCK) == 0 and response.shape[3] % BLOCK == 0
    return whole_rows and whole_width and onset_rcv.shape[0] == 2 * initial.shape[0]


def chosen(*arrays):
    return on_device(*arrays) if fits(*arrays) else general_device(*arrays)


def solution(mesh):
    in_specs = (
        P(("group", "sblk"), "freq", "rblk"),
        P(("group", "freq"), None, "sblk", "rblk"),
        P(("group", "freq"), "sblk", "rblk"),
        P("group", "rblk"),
        P("group", "sblk"),
    )
    out_specs = P(("group", "sblk"), "freq", "rblk")
    return jax.shard_map(chosen, mesh=mesh, in_specs=in_specs, out_specs=out_specs, check_vma=False)
```

time: 476 us -> 168 us (0.35); the launches traced: 467 us -> 167 us
  blocking collectives: 171 us -> 0 us
  waiting for transfers between devices: 192 us -> 84.9 us
  matrix products: 39.3 us -> 0 us
  starting transfers between devices: 19.6 us -> 45.4 us
  Pallas kernels: 0 us -> 16.5 us
  between operations: 13.9 us -> 0.26 us
  local copies, waits for them, and re-layouts: 27.4 us -> 14.6 us
    all_to_all x6 -> x0, blocking collectives: 167 us -> none  [the longest x1 95.4 us: to_times(): lax.all_to_all(values, 'freq', split_axis=1, concat_axis=0, tiled=True)]
    all_to_all x4 -> x0, waiting for transfers between devices: 112 us -> none  [the longest x1 88.4 us: to_traces(): lax.all_to_all(values, 'freq', split_axis=0, concat_axis=1, tiled=True)]
    ppermute x2 -> x35, waiting for transfers between devices: 2.67 us -> 84.9 us  [exchanged(): lax.ppermute(value, axis, [(i, i ^ step) for i in range(lax.axis_size(axi...]
    ppermute x2 -> x35, starting transfers between devices: 0.14 us -> 45.4 us  [exchanged(): lax.ppermute(value, axis, [(i, i ^ step) for i in range(lax.axis_size(axi...]
    dot_general x21 -> x0, matrix products: 39.3 us -> none  [the longest x4 24.6 us: samples_into_spectra(): jnp.einsum('kt,ptn->pkn', forward_table, values, preferred_element_type=j...]
    all_gather x2 -> x0, waiting for transfers between devices: 39.2 us -> none  [on_device(): up_all = lax.all_gather(up_back, 'rblk', axis=0, tiled=True)]
    reduce_scatter x2 -> x0, waiting for transfers between devices: 38.1 us -> none  [on_device(): lax.psum_scatter(settle(dense_down(gated_traces, spec_all)).astype(jnp.bf...]
    all_to_all x4 -> x0, starting transfers between devices: 19 us -> none  [the longest x1 6.45 us: to_traces(): lax.all_to_all(values, 'freq', split_axis=0, concat_axis=1, tiled=True)]
  transfers between devices with their start and end apart: 10 -> 35, of which waited for: 10 -> 23; matrix products, arithmetic and copies ran while one was open for 2% -> 3% of each run, Pallas kernels for 0% -> 1%
where the time goes in v1:
time: 168 us; the launch traced here: 167 us
  waiting for transfers between devices  84.9 us (51%)
  starting transfers between devices  45.4 us (27%)
  Pallas kernels  16.5 us (10%)
  local copies, waits for them, and re-layouts  14.6 us (9%)
  other arithmetic  5.88 us (4%)
    ppermute x35, waiting for transfers between devices, exchanged(): lax.ppermute(value, axis, [(i, i ^ step) for i in range(lax.axis_size(axi...  84.9 us
    ppermute x35, starting transfers between devices, exchanged(): lax.ppermute(value, axis, [(i, i ^ step) for i in range(lax.axis_size(axi...  45.4 us
    pallas_call x13, Pallas kernels, call(): pl.pallas_call(body, grid_spec=pltpu.PrefetchScalarGridSpec(num_scalar_pr...  16.5 us
    unnamed x29, local copies, waits for them, and re-layouts  14.5 us
  transfers between devices with their start and end apart: 35, of which 23 were waited for; matrix products, arithmetic and copies ran while one was open for 3% of the time, Pallas kernels for 1%

profile of v1, /device:TPU:0, one launch (start us, length us, event | category | flops | bytes accessed | tf_op | source)
XLA Modules:
  0.0 167.5 jit_solution(2497723115906805559)
XLA Ops:
  3.5 3.0 %collective-permute-start = (bf16[2,2,512,256]{3,2,1,0:T(8,128)(2,1)S(1)}, bf16[2,2,512,256]{3,2,1,0:T(8,128)(2,1)S(1)}, u32[]{:S(2)}, u32[]{:S(2)}) collective-permute-start(bf16[2,2,512,256]{3,2,1,0:T(8,128)(2,1)S(1)} %shard_map.83), channel_id=1, source_target_pairs={{0,2},{2,0},{1,3},{3,1},{4,6},{6,4},{5,7},{7,5},{8,10},{10,8},{9,1... | collective-permute-start | bytes 3145736 | tf_op jit(solution)/shard_map/ppermute | solution.py:379
  6.5 2.2 %copy-done = bf16[64,128,256]{2,1,0:T(8,128)(2,1)S(1)} copy-done((bf16[64,128,256]{2,1,0:T(8,128)(2,1)S(1)}, bf16[64,128,256]{2,1,0:T(8,128)(2,1)}, u32[]{:S(2)}) %copy-start) | copy-done | bytes 4194328
  12.9 2.6 %collective-permute-start.2 = (bf16[2,2,64,256]{3,2,1,0:T(8,128)(2,1)S(1)}, bf16[2,2,64,256]{3,2,1,0:T(8,128)(2,1)S(1)}, u32[]{:S(2)}, u32[]{:S(2)}) collective-permute-start(bf16[2,2,64,256]{3,2,1,0:T(8,128)(2,1)S(1)} %get-tuple-element.39), channel_id=1, source_target_pairs={{0,8},{4,12},{8,0},{12,4},{1,9},{5,13},{9,1},{13,5},{2,10},{6,14},... | collective-permute-start | bytes 393224 | tf_op jit(solution)/shard_map/ppermute | solution.py:379
  15.7 2.0 %collective-permute-done.1 = bf16[2,2,64,256]{3,2,1,0:T(8,128)(2,1)S(1)} collective-permute-done((bf16[2,2,64,256]{3,2,1,0:T(8,128)(2,1)S(1)}, bf16[2,2,64,256]{3,2,1,0:T(8,128)(2,1)S(1)}, u32[]{:S(2)}, u32[]{:S(2)}) %collective-permute-start.1) | collective-permute-done | bytes 131104 | tf_op jit(solution)/shard_map/ppermute | solution.py:379
  17.8 7.8 %collective-permute-done.2 = bf16[2,2,64,256]{3,2,1,0:T(8,128)(2,1)S(1)} collective-permute-done((bf16[2,2,64,256]{3,2,1,0:T(8,128)(2,1)S(1)}, bf16[2,2,64,256]{3,2,1,0:T(8,128)(2,1)S(1)}, u32[]{:S(2)}, u32[]{:S(2)}) %collective-permute-start.2) | collective-permute-done | bytes 131104 | tf_op jit(solution)/shard_map/ppermute | solution.py:379
  26.8 5.7 %collective-permute-done.5.f0 = bf16[2,2,64,256]{3,2,1,0:T(8,128)(2,1)} collective-permute-done((bf16[2,2,64,256]{3,2,1,0:T(8,128)(2,1)}, bf16[2,2,64,256]{3,2,1,0:T(8,128)(2,1)}, u32[]{:S(2)}, u32[]{:S(2)}) %collective-permute-start.5) | collective-permute-done | bytes 131104 | tf_op jit(solution)/shard_map/ppermute | solution.py:379
  36.2 2.3 %shard_map.85 = (bf16[2,2,32,512]{3,2,1,0:T(8,128)(2,1)S(1)}, bf16[2,2,32,512]{3,2,1,0:T(8,128)(2,1)S(1)}, bf16[2,2,32,512]{3,2,1,0:T(8,128)(2,1)S(1)}, bf16[2,2,32,512]{3,2,1,0:T(8,128)(2,1)S(1)}) custom-call(s32[1]{0:T(128)} %bitcast.place_ref, bf16[2,2,64,256]{3,2,1,0:T(8,128)(2,1)} %get-tuple-element.69.n0, ...), custom_call_target="tpu_custom_call" | custom-call | flops 536870912 | bytes 3145728 | tf_op jit(solution)/shard_map/pallas_call | solution.py:84
  38.5 1.9 %collective-permute-start.7 = (bf16[2,2,32,512]{3,2,1,0:T(8,128)(2,1)S(1)}, bf16[2,2,32,512]{3,2,1,0:T(8,128)(2,1)S(1)}, u32[]{:S(2)}, u32[]{:S(2)}) collective-permute-start(bf16[2,2,32,512]{3,2,1,0:T(8,128)(2,1)S(1)} %get-tuple-element.42), channel_id=1, source_target_pairs={{0,4},{4,0},{8,12},{12,8},{1,5},{5,1},{9,13},{13,9},{2,6},{6,2},{1... | collective-permute-start | bytes 393224 | tf_op jit(solution)/shard_map/ppermute | solution.py:379
  40.4 2.6 %collective-permute-start.8 = (bf16[2,2,32,512]{3,2,1,0:T(8,128)(2,1)S(1)}, bf16[2,2,32,512]{3,2,1,0:T(8,128)(2,1)S(1)}, u32[]{:S(2)}, u32[]{:S(2)}) collective-permute-start(bf16[2,2,32,512]{3,2,1,0:T(8,128)(2,1)S(1)} %get-tuple-element.43), channel_id=1, source_target_pairs={{0,8},{4,12},{8,0},{12,4},{1,9},{5,13},{9,1},{13,5},{2,10},{6,14},... | collective-permute-start | bytes 393224 | tf_op jit(solution)/shard_map/ppermute | solution.py:379
  43.0 2.1 %fusion.4 = (f32[4,2,32,512]{3,2,1,0:T(8,128)S(1)}, f32[4,2,32,512]{3,2,1,0:T(8,128)S(1)}) fusion(s32[32,512]{1,0:T(8,128)S(1)} %get-tuple-element.74, s32[4,2]{1,0:T(4,128)S(1)} %add_add_fusion), kind=kLoop, calls=%fused_computation.13 | loop fusion | flops 1835008 | bytes 1114144 | tf_op jit(solution)/shard_map/sin | solution.py:391
  46.8 6.5 %collective-permute-done.8.rest_2_ = bf16[2,2,32,512]{3,2,1,0:T(8,128)(2,1)S(1)} collective-permute-done((bf16[2,2,32,512]{3,2,1,0:T(8,128)(2,1)S(1)}, bf16[2,2,32,512]{3,2,1,0:T(8,128)(2,1)S(1)}, u32[]{:S(2)}, u32[]{:S(2)}) %collective-permute-start.8) | collective-permute-done | bytes 131104 | tf_op jit(solution)/shard_map/ppermute | solution.py:379
  54.6 2.7 %collective-permute-start.10 = (bf16[2,2,32,512]{3,2,1,0:T(8,128)(2,1)S(1)}, bf16[2,2,32,512]{3,2,1,0:T(8,128)(2,1)S(1)}, u32[]{:S(2)}, u32[]{:S(2)}) collective-permute-start(bf16[2,2,32,512]{3,2,1,0:T(8,128)(2,1)S(1)} %get-tuple-element.46), channel_id=1, source_target_pairs={{0,4},{4,0},{8,12},{12,8},{1,5},{5,1},{9,13},{13,9},{2,6},{6,2},{1... | collective-permute-start | bytes 393224 | tf_op jit(solution)/shard_map/ppermute | solution.py:379
  59.9 2.0 %collective-permute-done.10.rest_1_ = bf16[2,2,32,512]{3,2,1,0:T(8,128)(2,1)S(1)} collective-permute-done((bf16[2,2,32,512]{3,2,1,0:T(8,128)(2,1)S(1)}, bf16[2,2,32,512]{3,2,1,0:T(8,128)(2,1)S(1)}, u32[]{:S(2)}, u32[]{:S(2)}) %collective-permute-start.10) | collective-permute-done | bytes 131104 | tf_op jit(solution)/shard_map/ppermute | solution.py:379
  61.8 8.1 %collective-permute-done.11.rest_2_ = bf16[2,2,32,512]{3,2,1,0:T(8,128)(2,1)S(1)} collective-permute-done((bf16[2,2,32,512]{3,2,1,0:T(8,128)(2,1)S(1)}, bf16[2,2,32,512]{3,2,1,0:T(8,128)(2,1)S(1)}, u32[]{:S(2)}, u32[]{:S(2)}) %collective-permute-start.11) | collective-permute-done | bytes 131104 | tf_op jit(solution)/shard_map/ppermute | solution.py:379
  76.3 3.6 %collective-permute-done.14.x_ref = bf16[2,2,64,256]{3,2,1,0:T(8,128)(2,1)} collective-permute-done((bf16[2,2,64,256]{3,2,1,0:T(8,128)(2,1)}, bf16[2,2,64,256]{3,2,1,0:T(8,128)(2,1)}, u32[]{:S(2)}, u32[]{:S(2)}) %collective-permute-start.14) | collective-permute-done | bytes 131104 | tf_op jit(solution)/shard_map/ppermute | solution.py:379
  82.9 2.0 %collective-permute-start.15 = (bf16[64,256]{1,0:T(8,128)(2,1)S(1)}, bf16[64,256]{1,0:T(8,128)(2,1)S(1)}, u32[]{:S(2)}, u32[]{:S(2)}) collective-permute-start(bf16[64,256]{1,0:T(8,128)(2,1)S(1)} %get-tuple-element.52), channel_id=1, source_target_pairs={{0,4},{4,0},{8,12},{12,8},{1,5},{5,1},{9,13},{13,9},{2,6},{6,2},{1... | collective-permute-start | bytes 98312 | tf_op jit(solution)/shard_map/ppermute | solution.py:379
  88.0 2.3 %collective-permute-done.16.rest_2_ = bf16[64,256]{1,0:T(8,128)(2,1)S(1)} collective-permute-done((bf16[64,256]{1,0:T(8,128)(2,1)S(1)}, bf16[64,256]{1,0:T(8,128)(2,1)S(1)}, u32[]{:S(2)}, u32[]{:S(2)}) %collective-permute-start.16) | collective-permute-done | bytes 32800 | tf_op jit(solution)/shard_map/ppermute | solution.py:379
  92.4 1.8 %collective-permute-start.19 = (bf16[64,256]{1,0:T(8,128)(2,1)S(1)}, bf16[64,256]{1,0:T(8,128)(2,1)S(1)}, u32[]{:S(2)}, u32[]{:S(2)}) collective-permute-start(bf16[64,256]{1,0:T(8,128)(2,1)S(1)} %get-tuple-element.57), channel_id=1, source_target_pairs={{0,8},{4,12},{8,0},{12,4},{1,9},{5,13},{9,1},{13,5},{2,10},{6,14},... | collective-permute-start | bytes 98312 | tf_op jit(solution)/shard_map/ppermute | solution.py:379
  94.2 2.4 %collective-permute-start.20 = (bf16[64,256]{1,0:T(8,128)(2,1)S(1)}, bf16[64,256]{1,0:T(8,128)(2,1)S(1)}, u32[]{:S(2)}, u32[]{:S(2)}) collective-permute-start(bf16[64,256]{1,0:T(8,128)(2,1)S(1)} %get-tuple-element.58), channel_id=1, source_target_pairs={{0,12},{4,8},{8,4},{12,0},{1,13},{5,9},{9,5},{13,1},{2,14},{6,10},... | collective-permute-start | bytes 98312 | tf_op jit(solution)/shard_map/ppermute | solution.py:379
  97.2 2.7 %collective-permute-done.20.rest_3_ = bf16[64,256]{1,0:T(8,128)(2,1)S(1)} collective-permute-done((bf16[64,256]{1,0:T(8,128)(2,1)S(1)}, bf16[64,256]{1,0:T(8,128)(2,1)S(1)}, u32[]{:S(2)}, u32[]{:S(2)}) %collective-permute-start.20) | collective-permute-done | bytes 32800 | tf_op jit(solution)/shard_map/ppermute | solution.py:379
  101.6 3.5 %collective-permute-done.22.f0 = bf16[2,2,64,256]{3,2,1,0:T(8,128)(2,1)S(1)} collective-permute-done((bf16[2,2,64,256]{3,2,1,0:T(8,128)(2,1)S(1)}, bf16[2,2,64,256]{3,2,1,0:T(8,128)(2,1)S(1)}, u32[]{:S(2)}, u32[]{:S(2)}) %collective-permute-start.22) | collective-permute-done | bytes 131104 | tf_op jit(solution)/shard_map/ppermute | solution.py:379
  107.7 3.0 %collective-permute-start.25 = (bf16[2,2,32,512]{3,2,1,0:T(8,128)(2,1)S(1)}, bf16[2,2,32,512]{3,2,1,0:T(8,128)(2,1)S(1)}, u32[]{:S(2)}, u32[]{:S(2)}) collective-permute-start(bf16[2,2,32,512]{3,2,1,0:T(8,128)(2,1)S(1)} %get-tuple-element.61), channel_id=1, source_target_pairs={{0,8},{4,12},{8,0},{12,4},{1,9},{5,13},{9,1},{13,5},{2,10},{6,14},... | collective-permute-start | bytes 393224 | tf_op jit(solution)/shard_map/ppermute | solution.py:379
  112.1 3.5 %collective-permute-done.24.rest_1_ = bf16[2,2,32,512]{3,2,1,0:T(8,128)(2,1)S(1)} collective-permute-done((bf16[2,2,32,512]{3,2,1,0:T(8,128)(2,1)S(1)}, bf16[2,2,32,512]{3,2,1,0:T(8,128)(2,1)S(1)}, u32[]{:S(2)}, u32[]{:S(2)}) %collective-permute-start.24) | collective-permute-done | bytes 131104 | tf_op jit(solution)/shard_map/ppermute | solution.py:379
  115.5 5.1 %collective-permute-done.25.rest_2_ = bf16[2,2,32,512]{3,2,1,0:T(8,128)(2,1)S(1)} collective-permute-done((bf16[2,2,32,512]{3,2,1,0:T(8,128)(2,1)S(1)}, bf16[2,2,32,512]{3,2,1,0:T(8,128)(2,1)S(1)}, u32[]{:S(2)}, u32[]{:S(2)}) %collective-permute-start.25) | collective-permute-done | bytes 131104 | tf_op jit(solution)/shard_map/ppermute | solution.py:379
  122.0 2.6 %collective-permute-start.27 = (bf16[2,2,32,512]{3,2,1,0:T(8,128)(2,1)S(1)}, bf16[2,2,32,512]{3,2,1,0:T(8,128)(2,1)S(1)}, u32[]{:S(2)}, u32[]{:S(2)}) collective-permute-start(bf16[2,2,32,512]{3,2,1,0:T(8,128)(2,1)S(1)} %get-tuple-element.64), channel_id=1, source_target_pairs={{0,4},{4,0},{8,12},{12,8},{1,5},{5,1},{9,13},{13,9},{2,6},{6,2},{1... | collective-permute-start | bytes 393224 | tf_op jit(solution)/shard_map/ppermute | solution.py:379
  127.1 1.8 %collective-permute-done.27.rest_1_ = bf16[2,2,32,512]{3,2,1,0:T(8,128)(2,1)S(1)} collective-permute-done((bf16[2,2,32,512]{3,2,1,0:T(8,128)(2,1)S(1)}, bf16[2,2,32,512]{3,2,1,0:T(8,128)(2,1)S(1)}, u32[]{:S(2)}, u32[]{:S(2)}) %collective-permute-start.27) | collective-permute-done | bytes 131104 | tf_op jit(solution)/shard_map/ppermute | solution.py:379
  128.9 8.2 %collective-permute-done.28.rest_2_ = bf16[2,2,32,512]{3,2,1,0:T(8,128)(2,1)S(1)} collective-permute-done((bf16[2,2,32,512]{3,2,1,0:T(8,128)(2,1)S(1)}, bf16[2,2,32,512]{3,2,1,0:T(8,128)(2,1)S(1)}, u32[]{:S(2)}, u32[]{:S(2)}) %collective-permute-start.28) | collective-permute-done | bytes 131104 | tf_op jit(solution)/shard_map/ppermute | solution.py:379
  141.3 4.0 %collective-permute-done.31 = bf16[2,2,64,256]{3,2,1,0:T(8,128)(2,1)S(1)} collective-permute-done((bf16[2,2,64,256]{3,2,1,0:T(8,128)(2,1)S(1)}, bf16[2,2,64,256]{3,2,1,0:T(8,128)(2,1)S(1)}, u32[]{:S(2)}, u32[]{:S(2)}) %collective-permute-start.31) | collective-permute-done | bytes 131104 | tf_op jit(solution)/shard_map/ppermute | solution.py:379
  145.4 2.0 %collective-permute-start.32 = (bf16[2,2,64,256]{3,2,1,0:T(8,128)(2,1)S(1)}, bf16[2,2,64,256]{3,2,1,0:T(8,128)(2,1)S(1)}, u32[]{:S(2)}, u32[]{:S(2)}) collective-permute-start(bf16[2,2,64,256]{3,2,1,0:T(8,128)(2,1)S(1)} %fusion.3.rest_0_), channel_id=1, source_target_pairs={{0,4},{4,0},{8,12},{12,8},{1,5},{5,1},{9,13},{13,9},{2,6},{6,2},{1... | collective-permute-start | bytes 393224 | tf_op jit(solution)/shard_map/ppermute | solution.py:379
  151.6 8.2 %collective-permute-done.33.rest_2_ = bf16[2,2,64,256]{3,2,1,0:T(8,128)(2,1)S(1)} collective-permute-done((bf16[2,2,64,256]{3,2,1,0:T(8,128)(2,1)S(1)}, bf16[2,2,64,256]{3,2,1,0:T(8,128)(2,1)S(1)}, u32[]{:S(2)}, u32[]{:S(2)}) %collective-permute-start.33) | collective-permute-done | bytes 131104 | tf_op jit(solution)/shard_map/ppermute | solution.py:379
  159.8 2.2 %copy-done.1 = bf16[64,128,256]{2,1,0:T(8,128)(2,1)S(1)} copy-done((bf16[64,128,256]{2,1,0:T(8,128)(2,1)S(1)}, bf16[64,128,256]{2,1,0:T(8,128)(2,1)}, u32[]{:S(2)}) %copy-start.1) | copy-done | bytes 4194328
  164.1 3.4 %shard_map.94 = bf16[64,128,256]{2,1,0:T(8,128)(2,1)} custom-call(s32[1]{0:T(128)} %bitcast.place_ref, s32[1]{0:T(128)} %bitcast.1._, bf16[64,128,256]{2,1,0:T(8,128)(2,1)S(1)} %copy-done.1, s32[128,256]{1,0:T(8,128)S(1)} %copy-done.13, bf16[4,1024,128]{2,1,0:T(8,128)(2,1)S(1)} %copy-done.8, bf16[2,2,64,256]{3,2,1,0:T(8,128)(2,1)S(1)} %fusion.3.rest_0_, ...), custom_call_target="tpu_custom_call" | custom-call | flops 67108864 | bytes 10092544 | tf_op jit(solution)/shard_map/pallas_call | solution.py:84
  (91 shorter events, 53.4 us)
Async XLA Ops:
  3.5 32.7 %collective-permute-start = (bf16[2,2,512,256]{3,2,1,0:T(8,128)(2,1)S(1)}, bf16[2,2,512,256]{3,2,1,0:T(8,128)(2,1)S(1)}, u32[]{:S(2)}, u32[]{:S(2)}) collective-permute-start(bf16[2,2,512,256]{3,2,1,0:T(8,128)(2,1)S(1)} %shard_map.83), channel_id=1, source_target_pairs={{0,2},{2,0},{1,3},{3,1},{4,6},{6,4},{5,7},{7,5},{8,10},{10,8},{9,1... | collective-permute-start | bytes 3145736 | tf_op jit(solution)/shard_map/ppermute | solution.py:379
  11.2 6.5 %collective-permute-start.1 = (bf16[2,2,64,256]{3,2,1,0:T(8,128)(2,1)S(1)}, bf16[2,2,64,256]{3,2,1,0:T(8,128)(2,1)S(1)}, u32[]{:S(2)}, u32[]{:S(2)}) collective-permute-start(bf16[2,2,64,256]{3,2,1,0:T(8,128)(2,1)S(1)} %get-tuple-element.38), channel_id=1, source_target_pairs={{0,4},{4,0},{8,12},{12,8},{1,5},{5,1},{9,13},{13,9},{2,6},{6,2},{1... | collective-permute-start | bytes 393224 | tf_op jit(solution)/shard_map/ppermute | solution.py:379
  12.9 12.6 %collective-permute-start.2 = (bf16[2,2,64,256]{3,2,1,0:T(8,128)(2,1)S(1)}, bf16[2,2,64,256]{3,2,1,0:T(8,128)(2,1)S(1)}, u32[]{:S(2)}, u32[]{:S(2)}) collective-permute-start(bf16[2,2,64,256]{3,2,1,0:T(8,128)(2,1)S(1)} %get-tuple-element.39), channel_id=1, source_target_pairs={{0,8},{4,12},{8,0},{12,4},{1,9},{5,13},{9,1},{13,5},{2,10},{6,14},... | collective-permute-start | bytes 393224 | tf_op jit(solution)/shard_map/ppermute | solution.py:379
  15.5 10.1 %collective-permute-start.3 = (bf16[2,2,64,256]{3,2,1,0:T(8,128)(2,1)S(1)}, bf16[2,2,64,256]{3,2,1,0:T(8,128)(2,1)S(1)}, u32[]{:S(2)}, u32[]{:S(2)}) collective-permute-start(bf16[2,2,64,256]{3,2,1,0:T(8,128)(2,1)S(1)} %get-tuple-element.40), channel_id=1, source_target_pairs={{0,12},{4,8},{8,4},{12,0},{1,13},{5,9},{9,5},{13,1},{2,14},{6,10},... | collective-permute-start | bytes 393224 | tf_op jit(solution)/shard_map/ppermute | solution.py:379
  26.3 6.3 %collective-permute-start.5 = (bf16[2,2,64,256]{3,2,1,0:T(8,128)(2,1)}, bf16[2,2,64,256]{3,2,1,0:T(8,128)(2,1)}, u32[]{:S(2)}, u32[]{:S(2)}) collective-permute-start(bf16[2,2,64,256]{3,2,1,0:T(8,128)(2,1)} %get-tuple-element.69.n0), channel_id=1, source_target_pairs={{0,2},{2,0},{1,3},{3,1},{4,6},{6,4},{5,7},{7,5},{8,10},{10,8},{9,1... | collective-permute-start | bytes 393224 | tf_op jit(solution)/shard_map/ppermute | solution.py:379
  26.8 9.3 %collective-permute-start.4 = (bf16[2,2,64,256]{3,2,1,0:T(8,128)(2,1)}, bf16[2,2,64,256]{3,2,1,0:T(8,128)(2,1)}, u32[]{:S(2)}, u32[]{:S(2)}) collective-permute-start(bf16[2,2,64,256]{3,2,1,0:T(8,128)(2,1)} %get-tuple-element.69.n0), channel_id=1, source_target_pairs={{0,1},{1,0},{2,3},{3,2},{4,5},{5,4},{6,7},{7,6},{8,9},{9,8},{10,11... | collective-permute-start | bytes 393224 | tf_op jit(solution)/shard_map/ppermute | solution.py:379
  32.6 3.6 %collective-permute-start.6 = (bf16[2,2,64,256]{3,2,1,0:T(8,128)(2,1)}, bf16[2,2,64,256]{3,2,1,0:T(8,128)(2,1)}, u32[]{:S(2)}, u32[]{:S(2)}) collective-permute-start(bf16[2,2,64,256]{3,2,1,0:T(8,128)(2,1)} %collective-permute-done.5.f0), channel_id=1, source_target_pairs={{0,1},{1,0},{2,3},{3,2},{4,5},{5,4},{6,7},{7,6},{8,9},{9,8},{10,11... | collective-permute-start | bytes 393224 | tf_op jit(solution)/shard_map/ppermute | solution.py:379
  38.5 8.3 %collective-permute-start.7 = (bf16[2,2,32,512]{3,2,1,0:T(8,128)(2,1)S(1)}, bf16[2,2,32,512]{3,2,1,0:T(8,128)(2,1)S(1)}, u32[]{:S(2)}, u32[]{:S(2)}) collective-permute-start(bf16[2,2,32,512]{3,2,1,0:T(8,128)(2,1)S(1)} %get-tuple-element.42), channel_id=1, source_target_pairs={{0,4},{4,0},{8,12},{12,8},{1,5},{5,1},{9,13},{13,9},{2,6},{6,2},{1... | collective-permute-start | bytes 393224 | tf_op jit(solution)/shard_map/ppermute | solution.py:379
  40.4 12.9 %collective-permute-start.8 = (bf16[2,2,32,512]{3,2,1,0:T(8,128)(2,1)S(1)}, bf16[2,2,32,512]{3,2,1,0:T(8,128)(2,1)S(1)}, u32[]{:S(2)}, u32[]{:S(2)}) collective-permute-start(bf16[2,2,32,512]{3,2,1,0:T(8,128)(2,1)S(1)} %get-tuple-element.43), channel_id=1, source_target_pairs={{0,8},{4,12},{8,0},{12,4},{1,9},{5,13},{9,1},{13,5},{2,10},{6,14},... | collective-permute-start | bytes 393224 | tf_op jit(solution)/shard_map/ppermute | solution.py:379
  43.0 10.3 %collective-permute-start.9 = (bf16[2,2,32,512]{3,2,1,0:T(8,128)(2,1)S(1)}, bf16[2,2,32,512]{3,2,1,0:T(8,128)(2,1)S(1)}, u32[]{:S(2)}, u32[]{:S(2)}) collective-permute-start(bf16[2,2,32,512]{3,2,1,0:T(8,128)(2,1)S(1)} %get-tuple-element.44), channel_id=1, source_target_pairs={{0,12},{4,8},{8,4},{12,0},{1,13},{5,9},{9,5},{13,1},{2,14},{6,10},... | collective-permute-start | bytes 393224 | tf_op jit(solution)/shard_map/ppermute | solution.py:379
  54.6 7.2 %collective-permute-start.10 = (bf16[2,2,32,512]{3,2,1,0:T(8,128)(2,1)S(1)}, bf16[2,2,32,512]{3,2,1,0:T(8,128)(2,1)S(1)}, u32[]{:S(2)}, u32[]{:S(2)}) collective-permute-start(bf16[2,2,32,512]{3,2,1,0:T(8,128)(2,1)S(1)} %get-tuple-element.46), channel_id=1, source_target_pairs={{0,4},{4,0},{8,12},{12,8},{1,5},{5,1},{9,13},{13,9},{2,6},{6,2},{1... | collective-permute-start | bytes 393224 | tf_op jit(solution)/shard_map/ppermute | solution.py:379
  57.4 12.5 %collective-permute-start.11 = (bf16[2,2,32,512]{3,2,1,0:T(8,128)(2,1)S(1)}, bf16[2,2,32,512]{3,2,1,0:T(8,128)(2,1)S(1)}, u32[]{:S(2)}, u32[]{:S(2)}) collective-permute-start(bf16[2,2,32,512]{3,2,1,0:T(8,128)(2,1)S(1)} %get-tuple-element.47), channel_id=1, source_target_pairs={{0,8},{4,12},{8,0},{12,4},{1,9},{5,13},{9,1},{13,5},{2,10},{6,14},... | collective-permute-start | bytes 393224 | tf_op jit(solution)/shard_map/ppermute | solution.py:379
  58.5 11.4 %collective-permute-start.12 = (bf16[2,2,32,512]{3,2,1,0:T(8,128)(2,1)S(1)}, bf16[2,2,32,512]{3,2,1,0:T(8,128)(2,1)S(1)}, u32[]{:S(2)}, u32[]{:S(2)}) collective-permute-start(bf16[2,2,32,512]{3,2,1,0:T(8,128)(2,1)S(1)} %get-tuple-element.48), channel_id=1, source_target_pairs={{0,12},{4,8},{8,4},{12,0},{1,13},{5,9},{9,5},{13,1},{2,14},{6,10},... | collective-permute-start | bytes 393224 | tf_op jit(solution)/shard_map/ppermute | solution.py:379
  74.0 5.9 %collective-permute-start.14 = (bf16[2,2,64,256]{3,2,1,0:T(8,128)(2,1)}, bf16[2,2,64,256]{3,2,1,0:T(8,128)(2,1)}, u32[]{:S(2)}, u32[]{:S(2)}) collective-permute-start(bf16[2,2,64,256]{3,2,1,0:T(8,128)(2,1)} %fusion.9), channel_id=1, source_target_pairs={{0,2},{2,0},{1,3},{3,1},{4,6},{6,4},{5,7},{7,5},{8,10},{10,8},{9,1... | collective-permute-start | bytes 393224 | tf_op jit(solution)/shard_map/ppermute | solution.py:379
  82.9 5.1 %collective-permute-start.15 = (bf16[64,256]{1,0:T(8,128)(2,1)S(1)}, bf16[64,256]{1,0:T(8,128)(2,1)S(1)}, u32[]{:S(2)}, u32[]{:S(2)}) collective-permute-start(bf16[64,256]{1,0:T(8,128)(2,1)S(1)} %get-tuple-element.52), channel_id=1, source_target_pairs={{0,4},{4,0},{8,12},{12,8},{1,5},{5,1},{9,13},{13,9},{2,6},{6,2},{1... | collective-permute-start | bytes 98312 | tf_op jit(solution)/shard_map/ppermute | solution.py:379
  84.9 5.4 %collective-permute-start.16 = (bf16[64,256]{1,0:T(8,128)(2,1)S(1)}, bf16[64,256]{1,0:T(8,128)(2,1)S(1)}, u32[]{:S(2)}, u32[]{:S(2)}) collective-permute-start(bf16[64,256]{1,0:T(8,128)(2,1)S(1)} %get-tuple-element.53), channel_id=1, source_target_pairs={{0,8},{4,12},{8,0},{12,4},{1,9},{5,13},{9,1},{13,5},{2,10},{6,14},... | collective-permute-start | bytes 98312 | tf_op jit(solution)/shard_map/ppermute | solution.py:379
  86.0 5.7 %collective-permute-start.17 = (bf16[64,256]{1,0:T(8,128)(2,1)S(1)}, bf16[64,256]{1,0:T(8,128)(2,1)S(1)}, u32[]{:S(2)}, u32[]{:S(2)}) collective-permute-start(bf16[64,256]{1,0:T(8,128)(2,1)S(1)} %get-tuple-element.54), channel_id=1, source_target_pairs={{0,12},{4,8},{8,4},{12,0},{1,13},{5,9},{9,5},{13,1},{2,14},{6,10},... | collective-permute-start | bytes 98312 | tf_op jit(solution)/shard_map/ppermute | solution.py:379
  92.2 4.5 %collective-permute-start.18 = (bf16[64,256]{1,0:T(8,128)(2,1)S(1)}, bf16[64,256]{1,0:T(8,128)(2,1)S(1)}, u32[]{:S(2)}, u32[]{:S(2)}) collective-permute-start(bf16[64,256]{1,0:T(8,128)(2,1)S(1)} %get-tuple-element.56), channel_id=1, source_target_pairs={{0,4},{4,0},{8,12},{12,8},{1,5},{5,1},{9,13},{13,9},{2,6},{6,2},{1... | collective-permute-start | bytes 98312 | tf_op jit(solution)/shard_map/ppermute | solution.py:379
  92.4 4.8 %collective-permute-start.19 = (bf16[64,256]{1,0:T(8,128)(2,1)S(1)}, bf16[64,256]{1,0:T(8,128)(2,1)S(1)}, u32[]{:S(2)}, u32[]{:S(2)}) collective-permute-start(bf16[64,256]{1,0:T(8,128)(2,1)S(1)} %get-tuple-element.57), channel_id=1, source_target_pairs={{0,8},{4,12},{8,0},{12,4},{1,9},{5,13},{9,1},{13,5},{2,10},{6,14},... | collective-permute-start | bytes 98312 | tf_op jit(solution)/shard_map/ppermute | solution.py:379
  94.2 5.7 %collective-permute-start.20 = (bf16[64,256]{1,0:T(8,128)(2,1)S(1)}, bf16[64,256]{1,0:T(8,128)(2,1)S(1)}, u32[]{:S(2)}, u32[]{:S(2)}) collective-permute-start(bf16[64,256]{1,0:T(8,128)(2,1)S(1)} %get-tuple-element.58), channel_id=1, source_target_pairs={{0,12},{4,8},{8,4},{12,0},{1,13},{5,9},{9,5},{13,1},{2,14},{6,10},... | collective-permute-start | bytes 98312 | tf_op jit(solution)/shard_map/ppermute | solution.py:379
  100.0 5.0 %collective-permute-start.22 = (bf16[2,2,64,256]{3,2,1,0:T(8,128)(2,1)S(1)}, bf16[2,2,64,256]{3,2,1,0:T(8,128)(2,1)S(1)}, u32[]{:S(2)}, u32[]{:S(2)}) collective-permute-start(bf16[2,2,64,256]{3,2,1,0:T(8,128)(2,1)S(1)} %shard_map.90.n0), channel_id=1, source_target_pairs={{0,2},{2,0},{1,3},{3,1},{4,6},{6,4},{5,7},{7,5},{8,10},{10,8},{9,1... | collective-permute-start | bytes 393224 | tf_op jit(solution)/shard_map/ppermute | solution.py:379
  101.6 3.5 %collective-permute-start.21 = (bf16[2,2,64,256]{3,2,1,0:T(8,128)(2,1)S(1)}, bf16[2,2,64,256]{3,2,1,0:T(8,128)(2,1)S(1)}, u32[]{:S(2)}, u32[]{:S(2)}) collective-permute-start(bf16[2,2,64,256]{3,2,1,0:T(8,128)(2,1)S(1)} %shard_map.90.n0), channel_id=1, source_target_pairs={{0,1},{1,0},{2,3},{3,2},{4,5},{5,4},{6,7},{7,6},{8,9},{9,8},{10,11... | collective-permute-start | bytes 393224 | tf_op jit(solution)/shard_map/ppermute | solution.py:379
  107.6 7.9 %collective-permute-start.24 = (bf16[2,2,32,512]{3,2,1,0:T(8,128)(2,1)S(1)}, bf16[2,2,32,512]{3,2,1,0:T(8,128)(2,1)S(1)}, u32[]{:S(2)}, u32[]{:S(2)}) collective-permute-start(bf16[2,2,32,512]{3,2,1,0:T(8,128)(2,1)S(1)} %get-tuple-element.60), channel_id=1, source_target_pairs={{0,4},{4,0},{8,12},{12,8},{1,5},{5,1},{9,13},{13,9},{2,6},{6,2},{1... | collective-permute-start | bytes 393224 | tf_op jit(solution)/shard_map/ppermute | solution.py:379
  107.7 13.0 %collective-permute-start.25 = (bf16[2,2,32,512]{3,2,1,0:T(8,128)(2,1)S(1)}, bf16[2,2,32,512]{3,2,1,0:T(8,128)(2,1)S(1)}, u32[]{:S(2)}, u32[]{:S(2)}) collective-permute-start(bf16[2,2,32,512]{3,2,1,0:T(8,128)(2,1)S(1)} %get-tuple-element.61), channel_id=1, source_target_pairs={{0,8},{4,12},{8,0},{12,4},{1,9},{5,13},{9,1},{13,5},{2,10},{6,14},... | collective-permute-start | bytes 393224 | tf_op jit(solution)/shard_map/ppermute | solution.py:379
  110.7 10.0 %collective-permute-start.26 = (bf16[2,2,32,512]{3,2,1,0:T(8,128)(2,1)S(1)}, bf16[2,2,32,512]{3,2,1,0:T(8,128)(2,1)S(1)}, u32[]{:S(2)}, u32[]{:S(2)}) collective-permute-start(bf16[2,2,32,512]{3,2,1,0:T(8,128)(2,1)S(1)} %get-tuple-element.62), channel_id=1, source_target_pairs={{0,12},{4,8},{8,4},{12,0},{1,13},{5,9},{9,5},{13,1},{2,14},{6,10},... | collective-permute-start | bytes 393224 | tf_op jit(solution)/shard_map/ppermute | solution.py:379
  122.0 6.9 %collective-permute-start.27 = (bf16[2,2,32,512]{3,2,1,0:T(8,128)(2,1)S(1)}, bf16[2,2,32,512]{3,2,1,0:T(8,128)(2,1)S(1)}, u32[]{:S(2)}, u32[]{:S(2)}) collective-permute-start(bf16[2,2,32,512]{3,2,1,0:T(8,128)(2,1)S(1)} %get-tuple-element.64), channel_id=1, source_target_pairs={{0,4},{4,0},{8,12},{12,8},{1,5},{5,1},{9,13},{13,9},{2,6},{6,2},{1... | collective-permute-start | bytes 393224 | tf_op jit(solution)/shard_map/ppermute | solution.py:379
  124.7 12.4 %collective-permute-start.28 = (bf16[2,2,32,512]{3,2,1,0:T(8,128)(2,1)S(1)}, bf16[2,2,32,512]{3,2,1,0:T(8,128)(2,1)S(1)}, u32[]{:S(2)}, u32[]{:S(2)}) collective-permute-start(bf16[2,2,32,512]{3,2,1,0:T(8,128)(2,1)S(1)} %get-tuple-element.65), channel_id=1, source_target_pairs={{0,8},{4,12},{8,0},{12,4},{1,9},{5,13},{9,1},{13,5},{2,10},{6,14},... | collective-permute-start | bytes 393224 | tf_op jit(solution)/shard_map/ppermute | solution.py:379
  125.7 11.4 %collective-permute-start.29 = (bf16[2,2,32,512]{3,2,1,0:T(8,128)(2,1)S(1)}, bf16[2,2,32,512]{3,2,1,0:T(8,128)(2,1)S(1)}, u32[]{:S(2)}, u32[]{:S(2)}) collective-permute-start(bf16[2,2,32,512]{3,2,1,0:T(8,128)(2,1)S(1)} %get-tuple-element.66), channel_id=1, source_target_pairs={{0,12},{4,8},{8,4},{12,0},{1,13},{5,9},{9,5},{13,1},{2,14},{6,10},... | collective-permute-start | bytes 393224 | tf_op jit(solution)/shard_map/ppermute | solution.py:379
  139.7 5.6 %collective-permute-start.31 = (bf16[2,2,64,256]{3,2,1,0:T(8,128)(2,1)S(1)}, bf16[2,2,64,256]{3,2,1,0:T(8,128)(2,1)S(1)}, u32[]{:S(2)}, u32[]{:S(2)}) collective-permute-start(bf16[2,2,64,256]{3,2,1,0:T(8,128)(2,1)S(1)} %fusion.10), channel_id=1, source_target_pairs={{0,2},{2,0},{1,3},{3,1},{4,6},{6,4},{5,7},{7,5},{8,10},{10,8},{9,1... | collective-permute-start | bytes 393224 | tf_op jit(solution)/shard_map/ppermute | solution.py:379
  145.4 6.2 %collective-permute-start.32 = (bf16[2,2,64,256]{3,2,1,0:T(8,128)(2,1)S(1)}, bf16[2,2,64,256]{3,2,1,0:T(8,128)(2,1)S(1)}, u32[]{:S(2)}, u32[]{:S(2)}) collective-permute-start(bf16[2,2,64,256]{3,2,1,0:T(8,128)(2,1)S(1)} %fusion.3.rest_0_), channel_id=1, source_target_pairs={{0,4},{4,0},{8,12},{12,8},{1,5},{5,1},{9,13},{13,9},{2,6},{6,2},{1... | collective-permute-start | bytes 393224 | tf_op jit(solution)/shard_map/ppermute | solution.py:379
  147.4 12.4 %collective-permute-start.33 = (bf16[2,2,64,256]{3,2,1,0:T(8,128)(2,1)S(1)}, bf16[2,2,64,256]{3,2,1,0:T(8,128)(2,1)S(1)}, u32[]{:S(2)}, u32[]{:S(2)}) collective-permute-start(bf16[2,2,64,256]{3,2,1,0:T(8,128)(2,1)S(1)} %fusion.3.rest_0_), channel_id=1, source_target_pairs={{0,8},{4,12},{8,0},{12,4},{1,9},{5,13},{9,1},{13,5},{2,10},{6,14},... | collective-permute-start | bytes 393224 | tf_op jit(solution)/shard_map/ppermute | solution.py:379
  148.4 11.4 %collective-permute-start.34 = (bf16[2,2,64,256]{3,2,1,0:T(8,128)(2,1)S(1)}, bf16[2,2,64,256]{3,2,1,0:T(8,128)(2,1)S(1)}, u32[]{:S(2)}, u32[]{:S(2)}) collective-permute-start(bf16[2,2,64,256]{3,2,1,0:T(8,128)(2,1)S(1)} %fusion.3.rest_0_), channel_id=1, source_target_pairs={{0,12},{4,8},{8,4},{12,0},{1,13},{5,9},{9,5},{13,1},{2,14},{6,10},... | collective-permute-start | bytes 393224 | tf_op jit(solution)/shard_map/ppermute | solution.py:379
  (17 other events, 133.6 us)

commit v2 on v1

--- a/solution.py
+++ b/solution.py
@@ -13,7 +13,7 @@
 ITERS = 2
 ROWS = 8
 CHUNKS = 1
-VMEM_BYTES = 48 * 1024 * 1024
+VMEM_BYTES = 62 * 1024 * 1024
 
 BF16 = jnp.bfloat16
 F32 = jnp.float32
@@ -103,15 +103,15 @@
 
 
 def mask_half(response, aperture, place, flip, half):
-    per_dev, _, src, rcv = response.shape
-    src_blocks, rcv_blocks = src // BLOCK, rcv // BLOCK
+    per_dev, _, _, rcv = response.shape
+    rcv_blocks = rcv // BLOCK
     steps = half // BLOCK
 
     def body(place_ref, flags, x_ref, o_ref):
         block = (place_ref[0] ^ flip) * steps + pl.program_id(0)
         for j in range(per_dev):
             for r in range(rcv_blocks):
-                on = flags[(j * src_blocks + block) * rcv_blocks + r]
+                on = flags[j, block, r]
                 cut = pl.ds(r * BLOCK, BLOCK)
                 value = x_ref[j, :, :, cut]
                 o_ref[j, :, :, cut] = value * on.astype(F32).astype(BF16)
@@ -120,7 +120,7 @@
     block = (per_dev, 2, BLOCK, rcv)
     (out,) = call(
         body,
-        (place, aperture.reshape(-1)),
+        (place, aperture),
         [(response, pl.BlockSpec(block, lambda i, a, _: (0, 0, (a[0] ^ flip) * steps + i, 0)))],
         [(shape, pl.BlockSpec(block, lambda i, *_: (0, 0, i, 0)))],
         (steps,),
@@ -286,48 +286,53 @@
     )
 
 
-def dealt(keep, from_core, from_far, freq_place, freq_devs):
-    _, _, per_dev, rows, rcv = keep.shape
-    share = rows // freq_devs
-
-    def body(place_ref, k_ref, c_ref, x_ref, *rest):
-        outs, held = rest[:freq_devs], rest[freq_devs]
-        held[...] = k_ref[0] + c_ref[0].astype(F32) + x_ref[...].astype(F32)
-        for step, out in enumerate(outs):
-            start = pl.multiple_of((place_ref[0] ^ step) * share, share)
-            out[...] = held[:, :, pl.ds(start, share), :].reshape(out.shape).astype(BF16)
-
-    first = pl.BlockSpec((1,) + keep.shape[1:], lambda i, _: (0, 0, 0, 0, 0))
-    shape = jax.ShapeDtypeStruct((2 * per_dev * share, rcv), BF16)
-    return call(
-        body,
-        (freq_place,),
-        [(keep, first), (from_core, first), (from_far, whole(from_far))],
-        [(shape, whole(shape))] * freq_devs,
-        (1,),
-        scratch=[pltpu.VMEM(keep.shape[1:], F32)],
-    )
-
-
-def next_spectra(sums, messages, freq_place):
+def next_spectra(sums, messages, tables, matrix, freq_place):
+    cosines, sines, fraction = tables
     freq_devs = len(messages)
     _, per_dev, rows, rcv = sums.shape
-    share = rows // freq_devs
-
-    def body(place_ref, s_ref, *rest):
-        refs, out, held = rest[:freq_devs], rest[freq_devs], rest[freq_devs + 1]
-        for step, ref in enumerate(refs):
-            start = pl.multiple_of((place_ref[0] ^ step) * share, share)
-            held[:, :, pl.ds(start, share), :] = ref[...].astype(F32).reshape(2, per_dev, share, rcv)
-        out[...] = (s_ref[...] - held[...]).astype(BF16)
-
+    tile = BLOCK
+    count = freq_devs * 2 * per_dev * ROWS
+    own = 2 * per_dev * ROWS
+
+    def body(place_ref, u_ref, c_ref, s_ref, f_ref, g_ref, *rest):
+        refs, out = rest[:freq_devs], rest[freq_devs]
+        data = [ref[...].astype(F32) for ref in refs]
+        made = []
+        for first in range(0, rows, ROWS):
+            cut = slice(first, first + ROWS)
+            plain = [value[:, :, cut] for value in data]
+            cos = [c_ref[step, :, cut] for step in range(freq_devs)]
+            sin = [s_ref[step, :, cut] for step in range(freq_devs)]
+            turned = [
+                jnp.stack([v[0] * c - v[1] * s, v[0] * s + v[1] * c])
+                for v, c, s in zip(plain, cos, sin)
+            ]
+            flat = [jnp.stack(v).reshape(count, tile).astype(BF16) for v in (turned, plain)]
+            mixed = jnp.dot(g_ref[0], jnp.concatenate(flat, 1), preferred_element_type=F32)
+            up = mixed[:, :tile].reshape(2, per_dev, ROWS, tile)
+            low = mixed[:, tile:].reshape(2, per_dev, ROWS, tile)
+            c, s, v, part = cos[0], sin[0], plain[0], f_ref[cut]
+            real = c * up[0] + s * up[1] - low[0] + part * v[0]
+            imag = c * up[1] - s * up[0] - low[1] + part * v[1]
+            made.append(jnp.stack([real, imag]))
+        out[...] = (u_ref[...] - jnp.concatenate(made, 2)).astype(BF16)
+
+    block = pl.BlockSpec((2, per_dev, rows, tile), lambda i, _: (0, 0, 0, i))
+    table = pl.BlockSpec(cosines.shape[:-1] + (tile,), lambda i, _: (0, 0, 0, i))
     (out,) = call(
         body,
         (freq_place,),
-        [(sums, whole(sums))] + [(v, whole(v)) for v in messages],
-        [(jax.ShapeDtypeStruct(sums.shape, BF16), whole(sums))],
-        (1,),
-        scratch=[pltpu.VMEM(sums.shape, F32)],
+        [
+            (sums, block),
+            (cosines, table),
+            (sines, table),
+            (fraction, pl.BlockSpec((rows, tile), lambda i, _: (0, i))),
+            (matrix, pl.BlockSpec((1, own, count), lambda i, z: (z[0], 0, 0))),
+        ]
+        + [(v, block) for v in messages],
+        [(jax.ShapeDtypeStruct(sums.shape, BF16), block)],
+        (rcv // tile,),
+        flops=2 * own * count * 2 * rcv * rows // ROWS,
     )
     return out
 
@@ -379,8 +384,19 @@
     return lax.ppermute(value, axis, [(i, i ^ step) for i in range(lax.axis_size(axis))])
 
 
+def partners(count):
+    return sorted(range(1, count), key=lambda step: (step.bit_length() < count.bit_length() - 1, step))
+
+
 def dealt_out(parts):
-    return [parts[0]] + [exchanged(parts[step], "freq", step) for step in range(1, len(parts))]
+    out = list(parts)
+    for step in partners(len(parts)):
+        out[step] = exchanged(parts[step], "freq", step)
+    return out
+
+
+def spread(value, count):
+    return dealt_out([value] * count)
 
 
 def phases(onset, freq_index, freq_devs, per_dev, samples):
@@ -423,9 +439,7 @@
         src_first = (sblk_index ^ other) * half_rows + first + spot - other * rows
         onsets = lax.dynamic_slice(onset_src, (src_first, rblk_index * src_width), (share, src_width))
         src_tables = phases(onsets, freq_index, freq_devs, per_dev, samples)
-        rcv_share = rows // freq_devs
-        rcv_first = sblk_index * half_rows + first + freq_index * rcv_share
-        onsets = lax.dynamic_slice_in_dim(onset_rcv, rcv_first, rcv_share, 0)
+        onsets = lax.dynamic_slice_in_dim(onset_rcv, sblk_index * half_rows + first, rows, 0)
         rcv_tables = phases(onsets, freq_index, freq_devs, per_dev, samples)
 
         for step in range(ITERS):
@@ -437,13 +451,11 @@
             keep, send = up_products(dealt_out(messages), kept, moved, freq_place, rows)
             from_core = exchanged(send, "sblk", 1)
             from_far = exchanged((keep[1] + from_core[1].astype(F32)).astype(BF16), "rblk", 1)
+            back = (keep[0] + from_core[0].astype(F32) + from_far.astype(F32)).astype(BF16)
+            messages = spread(back, freq_devs)
             if step < ITERS - 1:
-                messages = dealt_out(dealt(keep, from_core, from_far, freq_place, freq_devs))
-                messages = windowed(messages, rcv_tables, matrix, freq_place, per_dev, rcv_share)
-                spectra = next_spectra(sums, dealt_out(messages), freq_place)
+                spectra = next_spectra(sums, messages, rcv_tables, matrix, freq_place)
             else:
-                back = (keep[0] + from_core[0].astype(F32) + from_far.astype(F32)).astype(BF16)
-                messages = [back] + [exchanged(back, "freq", m) for m in range(1, freq_devs)]
                 tile_first = (sblk_index * (half_rows // (2 * ROWS))).reshape(1)
                 result = updated(
                     initial, onset_rcv, messages, inverse, freq_place, tile_first, first, rows, result
@@ -528,7 +540,7 @@
     if lax.axis_size("rblk") != 2 or lax.axis_size("sblk") != 2 or freq_devs & (freq_devs - 1):
         return False
     rows = initial.shape[0] // CHUNKS
-    whole_rows = initial.shape[0] % (CHUNKS * 2 * ROWS * max(1, freq_devs // 2)) == 0 and rows % (ROWS * freq_devs) == 0
+    whole_rows = initial.shape[0] % (CHUNKS * 2 * ROWS * max(1, freq_devs // 2)) == 0 and rows % (2 * ROWS) == 0
     whole_width = response.shape[2] % (4 * BLOCK) == 0 and response.shape[3] % BLOCK == 0
     return whole_rows and whole_width and onset_rcv.shape[0] == 2 * initial.shape[0]
 

time: 168 us -> 190 us (1.13)
  Pallas kernels: 16.5 us -> 40.8 us
  other arithmetic: 5.88 us -> 14.3 us
  local copies, waits for them, and re-layouts: 14.6 us -> 7.9 us
  starting transfers between devices: 45.4 us -> 40.1 us
    pallas_call x13 -> x11, Pallas kernels: 16.5 us -> 40.8 us  [call(): pl.pallas_call(body, grid_spec=pltpu.PrefetchScalarGridSpec(num_scalar_pr...]
    unnamed x29 -> x59, local copies, waits for them, and re-layouts: 14.5 us -> 7.9 us
    ppermute x35 -> x32, starting transfers between devices: 45.4 us -> 40.1 us  [exchanged(): lax.ppermute(value, axis, [(i, i ^ step) for i in range(lax.axis_size(axi...]
    sin x2, other arithmetic: 2.69 us -> 6.43 us  [phases(): return (jnp.cos(angle), jnp.sin(angle), onset.astype(F32) * (1.0 / samples))]
    convert_element_type x1 -> x2, other arithmetic: 0.05 us -> 2 us  [on_device(): (keep[0] + from_core[0].astype(F32) + from_far.astype(F32)).astype(BF16)]
    ppermute x35 -> x32, waiting for transfers between devices: 84.9 us -> 85.8 us  [exchanged(): lax.ppermute(value, axis, [(i, i ^ step) for i in range(lax.axis_size(axi...]
  transfers between devices with their start and end apart: 35 -> 32, of which waited for: 23 -> 20; matrix products, arithmetic and copies ran while one was open for 3% -> 5% of each run, Pallas kernels for 1% -> 5%
where the time goes in v2:
time: 190 us; the launch traced here: 189 us
  waiting for transfers between devices  85.8 us (45%)
  Pallas kernels  40.8 us (21%)
  starting transfers between devices  40.1 us (21%)
  other arithmetic  14.3 us (8%)
  local copies, waits for them, and re-layouts  7.9 us (4%)
    ppermute x32, waiting for transfers between devices, exchanged(): lax.ppermute(value, axis, [(i, i ^ step) for i in range(lax.axis_size(axi...  85.8 us
    pallas_call x11, Pallas kernels, call(): pl.pallas_call(body, grid_spec=pltpu.PrefetchScalarGridSpec(num_scalar_pr...  40.8 us
    ppermute x32, starting transfers between devices, exchanged(): lax.ppermute(value, axis, [(i, i ^ step) for i in range(lax.axis_size(axi...  40.1 us
    unnamed x59, local copies, waits for them, and re-layouts  7.9 us
    sin x2, other arithmetic, phases(): return (jnp.cos(angle), jnp.sin(angle), onset.astype(F32) * (1.0 / samples))  6.43 us
  transfers between devices with their start and end apart: 32, of which 20 were waited for; matrix products, arithmetic and copies ran while one was open for 5% of the time, Pallas kernels for 5%

profile of v2, /device:TPU:0, one launch (start us, length us, event | category | flops | bytes accessed | tf_op | source)
XLA Modules:
  0.0 189.0 jit_solution(1654875994592535276)
XLA Ops:
  1.4 4.2 %shard_map.83 = bf16[2,2,512,256]{3,2,1,0:T(8,128)(2,1)} custom-call(s32[1]{0:T(128)} %bitcast.2.place_ref, s32[2,8,2]{2,1,0:T(8,128)} %copy.9.flags, bf16[2,2,1024,256]{3,2,1,0:T(8,128)(2,1)} %x_ref.5), custom_call_target="tpu_custom_call" | custom-call | bytes 3145728 | tf_op jit(solution)/shard_map/pallas_call | solution.py:84
  5.6 2.9 %collective-permute-start = (bf16[2,2,512,256]{3,2,1,0:T(8,128)(2,1)}, bf16[2,2,512,256]{3,2,1,0:T(8,128)(2,1)S(1)}, u32[]{:S(2)}, u32[]{:S(2)}) collective-permute-start(bf16[2,2,512,256]{3,2,1,0:T(8,128)(2,1)} %shard_map.83), channel_id=1, source_target_pairs={{0,2},{2,0},{1,3},{3,1},{4,6},{6,4},{5,7},{7,5},{8,10},{10,8},{9,1... | collective-permute-start | bytes 3145736 | tf_op jit(solution)/shard_map/ppermute | solution.py:384
  8.5 4.5 %shard_map.84 = (bf16[2,2,64,256]{3,2,1,0:T(8,128)(2,1)}, bf16[2,2,64,256]{3,2,1,0:T(8,128)(2,1)}, bf16[2,2,64,256]{3,2,1,0:T(8,128)(2,1)}, bf16[2,2,64,256]{3,2,1,0:T(8,128)(2,1)}) custom-call(s32[1]{0:T(128)} %bitcast.place_ref, bf16[64,128,256]{2,1,0:T(8,128)(2,1)} %x_ref.7, bf16[4,128,1024]{2,1,0:T(8,128)(2,1)} %constant.62.clone.t_ref), custom_call_target="tpu_custom_call" | custom-call | flops 67108864 | bytes 5767168 | tf_op jit(solution)/shard_map/pallas_call | solution.py:84
  14.6 2.6 %collective-permute-start.2 = (bf16[2,2,64,256]{3,2,1,0:T(8,128)(2,1)}, bf16[2,2,64,256]{3,2,1,0:T(8,128)(2,1)S(1)}, u32[]{:S(2)}, u32[]{:S(2)}) collective-permute-start(bf16[2,2,64,256]{3,2,1,0:T(8,128)(2,1)} %get-tuple-element.31), channel_id=1, source_target_pairs={{0,8},{4,12},{8,0},{12,4},{1,9},{5,13},{9,1},{13,5},{2,10},{6,14},... | collective-permute-start | bytes 393224 | tf_op jit(solution)/shard_map/ppermute | solution.py:384
  17.4 2.3 %collective-permute-done.1 = bf16[2,2,64,256]{3,2,1,0:T(8,128)(2,1)S(1)} collective-permute-done((bf16[2,2,64,256]{3,2,1,0:T(8,128)(2,1)}, bf16[2,2,64,256]{3,2,1,0:T(8,128)(2,1)S(1)}, u32[]{:S(2)}, u32[]{:S(2)}) %collective-permute-start.1) | collective-permute-done | bytes 131104 | tf_op jit(solution)/shard_map/ppermute | solution.py:384
  19.7 7.8 %collective-permute-done.2 = bf16[2,2,64,256]{3,2,1,0:T(8,128)(2,1)S(1)} collective-permute-done((bf16[2,2,64,256]{3,2,1,0:T(8,128)(2,1)}, bf16[2,2,64,256]{3,2,1,0:T(8,128)(2,1)S(1)}, u32[]{:S(2)}, u32[]{:S(2)}) %collective-permute-start.2) | collective-permute-done | bytes 131104 | tf_op jit(solution)/shard_map/ppermute | solution.py:384
  29.7 5.0 %collective-permute-done.5.f0 = bf16[2,2,64,256]{3,2,1,0:T(8,128)(2,1)S(1)} collective-permute-done((bf16[2,2,64,256]{3,2,1,0:T(8,128)(2,1)S(1)}, bf16[2,2,64,256]{3,2,1,0:T(8,128)(2,1)S(1)}, u32[]{:S(2)}, u32[]{:S(2)}) %collective-permute-start.5) | collective-permute-done | bytes 131104 | tf_op jit(solution)/shard_map/ppermute | solution.py:384
  34.8 4.2 %shard_map.82.k_ref = bf16[2,2,512,256]{3,2,1,0:T(8,128)(2,1)} custom-call(s32[1]{0:T(128)} %bitcast.2.place_ref, s32[2,8,2]{2,1,0:T(8,128)} %copy.9.flags, bf16[2,2,1024,256]{3,2,1,0:T(8,128)(2,1)} %x_ref.5), custom_call_target="tpu_custom_call" | custom-call | bytes 3145728 | tf_op jit(solution)/shard_map/pallas_call | solution.py:84
  42.2 3.1 %shard_map.85 = (bf16[2,2,32,512]{3,2,1,0:T(8,128)(2,1)}, bf16[2,2,32,512]{3,2,1,0:T(8,128)(2,1)}, bf16[2,2,32,512]{3,2,1,0:T(8,128)(2,1)}, bf16[2,2,32,512]{3,2,1,0:T(8,128)(2,1)}) custom-call(s32[1]{0:T(128)} %bitcast.place_ref, bf16[2,2,64,256]{3,2,1,0:T(8,128)(2,1)} %copy-done.1, bf16[2,2,64,256]{3,2,1,0:T(8,128)(2,1)} %copy-done.6, ...), custom_call_target="tpu_custom_call" | custom-call | flops 536870912 | bytes 3145728 | tf_op jit(solution)/shard_map/pallas_call | solution.py:84
  47.2 2.6 %collective-permute-start.8 = (bf16[2,2,32,512]{3,2,1,0:T(8,128)(2,1)}, bf16[2,2,32,512]{3,2,1,0:T(8,128)(2,1)S(1)}, u32[]{:S(2)}, u32[]{:S(2)}) collective-permute-start(bf16[2,2,32,512]{3,2,1,0:T(8,128)(2,1)} %get-tuple-element.35), channel_id=1, source_target_pairs={{0,8},{4,12},{8,0},{12,4},{1,9},{5,13},{9,1},{13,5},{2,10},{6,14},... | collective-permute-start | bytes 393224 | tf_op jit(solution)/shard_map/ppermute | solution.py:384
  49.7 3.2 %fusion.10 = (f32[4,2,32,512]{3,2,1,0:T(8,128)}, f32[4,2,32,512]{3,2,1,0:T(8,128)}) fusion(s32[32,512]{1,0:T(8,128)S(1)} %get-tuple-element.58, s32[4,2]{1,0:T(4,128)S(1)} %add_add_fusion), kind=kLoop, calls=%fused_computation.25 | loop fusion | flops 1835008 | bytes 1114144 | tf_op jit(solution)/shard_map/sin | solution.py:407
  53.8 6.4 %collective-permute-done.8.rest_2_ = bf16[2,2,32,512]{3,2,1,0:T(8,128)(2,1)S(1)} collective-permute-done((bf16[2,2,32,512]{3,2,1,0:T(8,128)(2,1)}, bf16[2,2,32,512]{3,2,1,0:T(8,128)(2,1)S(1)}, u32[]{:S(2)}, u32[]{:S(2)}) %collective-permute-start.8) | collective-permute-done | bytes 131104 | tf_op jit(solution)/shard_map/ppermute | solution.py:384
  61.0 3.9 %shard_map.86 = (bf16[2,2,32,512]{3,2,1,0:T(8,128)(2,1)}, bf16[2,2,32,512]{3,2,1,0:T(8,128)(2,1)}, bf16[2,2,32,512]{3,2,1,0:T(8,128)(2,1)}, bf16[2,2,32,512]{3,2,1,0:T(8,128)(2,1)}) custom-call(s32[1]{0:T(128)} %bitcast.place_ref, f32[4,2,32,512]{3,2,1,0:T(8,128)} %get-tuple-element.62.c_ref, f32[4,2,32,512]{3,2,1,0:T(8,128)} %get-tuple-element.61.s_ref, ...), custom_call_target="tpu_custom_call" | custom-call | flops 134217728 | bytes 2293760 | tf_op jit(solution)/shard_map/pallas_call | solution.py:84
  64.8 2.7 %collective-permute-start.10 = (bf16[2,2,32,512]{3,2,1,0:T(8,128)(2,1)}, bf16[2,2,32,512]{3,2,1,0:T(8,128)(2,1)S(1)}, u32[]{:S(2)}, u32[]{:S(2)}) collective-permute-start(bf16[2,2,32,512]{3,2,1,0:T(8,128)(2,1)} %get-tuple-element.38), channel_id=1, source_target_pairs={{0,4},{4,0},{8,12},{12,8},{1,5},{5,1},{9,13},{13,9},{2,6},{6,2},{1... | collective-permute-start | bytes 393224 | tf_op jit(solution)/shard_map/ppermute | solution.py:384
  70.0 2.2 %collective-permute-done.10.rest_1_ = bf16[2,2,32,512]{3,2,1,0:T(8,128)(2,1)S(1)} collective-permute-done((bf16[2,2,32,512]{3,2,1,0:T(8,128)(2,1)}, bf16[2,2,32,512]{3,2,1,0:T(8,128)(2,1)S(1)}, u32[]{:S(2)}, u32[]{:S(2)}) %collective-permute-start.10) | collective-permute-done | bytes 131104 | tf_op jit(solution)/shard_map/ppermute | solution.py:384
  72.2 8.1 %collective-permute-done.11.rest_2_ = bf16[2,2,32,512]{3,2,1,0:T(8,128)(2,1)S(1)} collective-permute-done((bf16[2,2,32,512]{3,2,1,0:T(8,128)(2,1)}, bf16[2,2,32,512]{3,2,1,0:T(8,128)(2,1)S(1)}, u32[]{:S(2)}, u32[]{:S(2)}) %collective-permute-start.11) | collective-permute-done | bytes 131104 | tf_op jit(solution)/shard_map/ppermute | solution.py:384
  80.9 2.9 %shard_map.87 = (f32[2,2,2,64,256]{4,3,2,1,0:T(8,128)}, bf16[2,2,2,64,256]{4,3,2,1,0:T(8,128)(2,1)}) custom-call(s32[1]{0:T(128)} %bitcast.place_ref, bf16[2,2,512,256]{3,2,1,0:T(8,128)(2,1)} %shard_map.82.k_ref, bf16[2,2,512,256]{3,2,1,0:T(8,128)(2,1)} %copy-done, bf16[2,2,32,512]{3,2,1,0:T(8,128)(2,1)} %get-tuple-element.37.rest_0_, ...), custom_call_target="tpu_custom_call" | custom-call | flops 536870912 | bytes 3407872 | tf_op jit(solution)/shard_map/pallas_call | solution.py:84
  88.8 3.4 %collective-permute-done.14 = bf16[2,2,64,256]{3,2,1,0:T(8,128)(2,1)S(1)} collective-permute-done((bf16[2,2,64,256]{3,2,1,0:T(8,128)(2,1)S(1)}, bf16[2,2,64,256]{3,2,1,0:T(8,128)(2,1)S(1)}, u32[]{:S(2)}, u32[]{:S(2)}) %collective-permute-start.14) | collective-permute-done | bytes 131104 | tf_op jit(solution)/shard_map/ppermute | solution.py:384
  97.6 3.2 %fusion.8 = (f32[4,2,64,256]{3,2,1,0:T(8,128)}, f32[4,2,64,256]{3,2,1,0:T(8,128)}) fusion(s32[64,256]{1,0:T(8,128)S(1)} %get-tuple-element.56, s32[4,2]{1,0:T(4,128)S(1)} %add_add_fusion), kind=kLoop, calls=%fused_computation.22 | loop fusion | flops 1835008 | bytes 1114144 | tf_op jit(solution)/shard_map/sin | solution.py:407
  100.9 6.7 %collective-permute-done.16.rest_2_ = bf16[2,2,64,256]{3,2,1,0:T(8,128)(2,1)S(1)} collective-permute-done((bf16[2,2,64,256]{3,2,1,0:T(8,128)(2,1)S(1)}, bf16[2,2,64,256]{3,2,1,0:T(8,128)(2,1)S(1)}, u32[]{:S(2)}, u32[]{:S(2)}) %collective-permute-start.16) | collective-permute-done | bytes 131104 | tf_op jit(solution)/shard_map/ppermute | solution.py:384
  108.3 2.4 %shard_map.88.n0 = bf16[2,2,64,256]{3,2,1,0:T(8,128)(2,1)} custom-call(s32[1]{0:T(128)} %bitcast.place_ref, f32[2,2,64,256]{3,2,1,0:T(8,128)} %get-tuple-element.54.u_ref, f32[4,2,64,256]{3,2,1,0:T(8,128)} %get-tuple-element.60.c_ref, f32[4,2,64,256]{3,2,1,0:T(8,128)} %get-tuple-element.59.s_ref, f32[64,256]{1,0:T(8,128)} %get-tuple-element.55.f_ref, ...), custom_call_target="tpu_custom_call" | custom-call | flops 33554432 | bytes 2162688 | tf_op jit(solution)/shard_map/pallas_call | solution.py:84
  112.1 3.7 %collective-permute-done.19.f0 = bf16[2,2,64,256]{3,2,1,0:T(8,128)(2,1)S(1)} collective-permute-done((bf16[2,2,64,256]{3,2,1,0:T(8,128)(2,1)}, bf16[2,2,64,256]{3,2,1,0:T(8,128)(2,1)S(1)}, u32[]{:S(2)}, u32[]{:S(2)}) %collective-permute-start.19) | collective-permute-done | bytes 131104 | tf_op jit(solution)/shard_map/ppermute | solution.py:384
  117.8 3.1 %shard_map.89 = (bf16[2,2,32,512]{3,2,1,0:T(8,128)(2,1)}, bf16[2,2,32,512]{3,2,1,0:T(8,128)(2,1)}, bf16[2,2,32,512]{3,2,1,0:T(8,128)(2,1)}, bf16[2,2,32,512]{3,2,1,0:T(8,128)(2,1)}) custom-call(s32[1]{0:T(128)} %bitcast.place_ref, bf16[2,2,64,256]{3,2,1,0:T(8,128)(2,1)} %shard_map.88.n0, bf16[2,2,64,256]{3,2,1,0:T(8,128)(2,1)} %copy-done.17, ...), custom_call_target="tpu_custom_call" | custom-call | flops 536870912 | bytes 3145728 | tf_op jit(solution)/shard_map/pallas_call | solution.py:84
  125.3 3.4 %collective-permute-done.21.rest_1_ = bf16[2,2,32,512]{3,2,1,0:T(8,128)(2,1)S(1)} collective-permute-done((bf16[2,2,32,512]{3,2,1,0:T(8,128)(2,1)}, bf16[2,2,32,512]{3,2,1,0:T(8,128)(2,1)S(1)}, u32[]{:S(2)}, u32[]{:S(2)}) %collective-permute-start.21) | collective-permute-done | bytes 131104 | tf_op jit(solution)/shard_map/ppermute | solution.py:384
  128.8 7.2 %collective-permute-done.22.rest_2_ = bf16[2,2,32,512]{3,2,1,0:T(8,128)(2,1)S(1)} collective-permute-done((bf16[2,2,32,512]{3,2,1,0:T(8,128)(2,1)}, bf16[2,2,32,512]{3,2,1,0:T(8,128)(2,1)S(1)}, u32[]{:S(2)}, u32[]{:S(2)}) %collective-permute-start.22) | collective-permute-done | bytes 131104 | tf_op jit(solution)/shard_map/ppermute | solution.py:384
  136.7 3.9 %shard_map.90 = (bf16[2,2,32,512]{3,2,1,0:T(8,128)(2,1)}, bf16[2,2,32,512]{3,2,1,0:T(8,128)(2,1)}, bf16[2,2,32,512]{3,2,1,0:T(8,128)(2,1)}, bf16[2,2,32,512]{3,2,1,0:T(8,128)(2,1)}) custom-call(s32[1]{0:T(128)} %bitcast.place_ref, f32[4,2,32,512]{3,2,1,0:T(8,128)} %get-tuple-element.62.c_ref, f32[4,2,32,512]{3,2,1,0:T(8,128)} %get-tuple-element.61.s_ref, ...), custom_call_target="tpu_custom_call" | custom-call | flops 134217728 | bytes 2293760 | tf_op jit(solution)/shard_map/pallas_call | solution.py:84
  140.6 2.3 %collective-permute-start.24 = (bf16[2,2,32,512]{3,2,1,0:T(8,128)(2,1)}, bf16[2,2,32,512]{3,2,1,0:T(8,128)(2,1)S(1)}, u32[]{:S(2)}, u32[]{:S(2)}) collective-permute-start(bf16[2,2,32,512]{3,2,1,0:T(8,128)(2,1)} %get-tuple-element.48), channel_id=1, source_target_pairs={{0,4},{4,0},{8,12},{12,8},{1,5},{5,1},{9,13},{13,9},{2,6},{6,2},{1... | collective-permute-start | bytes 393224 | tf_op jit(solution)/shard_map/ppermute | solution.py:384
  147.3 7.9 %collective-permute-done.25.rest_2_ = bf16[2,2,32,512]{3,2,1,0:T(8,128)(2,1)S(1)} collective-permute-done((bf16[2,2,32,512]{3,2,1,0:T(8,128)(2,1)}, bf16[2,2,32,512]{3,2,1,0:T(8,128)(2,1)S(1)}, u32[]{:S(2)}, u32[]{:S(2)}) %collective-permute-start.25) | collective-permute-done | bytes 131104 | tf_op jit(solution)/shard_map/ppermute | solution.py:384
  155.9 3.0 %shard_map.91 = (f32[2,2,2,64,256]{4,3,2,1,0:T(8,128)}, bf16[2,2,2,64,256]{4,3,2,1,0:T(8,128)(2,1)}) custom-call(s32[1]{0:T(128)} %bitcast.place_ref, bf16[2,2,512,256]{3,2,1,0:T(8,128)(2,1)} %shard_map.82.k_ref, bf16[2,2,512,256]{3,2,1,0:T(8,128)(2,1)} %copy-done, bf16[2,2,32,512]{3,2,1,0:T(8,128)(2,1)} %get-tuple-element.47.rest_0_, ...), custom_call_target="tpu_custom_call" | custom-call | flops 536870912 | bytes 3407872 | tf_op jit(solution)/shard_map/pallas_call | solution.py:84
  163.2 4.1 %collective-permute-done.28 = bf16[2,2,64,256]{3,2,1,0:T(8,128)(2,1)S(1)} collective-permute-done((bf16[2,2,64,256]{3,2,1,0:T(8,128)(2,1)S(1)}, bf16[2,2,64,256]{3,2,1,0:T(8,128)(2,1)S(1)}, u32[]{:S(2)}, u32[]{:S(2)}) %collective-permute-start.28) | collective-permute-done | bytes 131104 | tf_op jit(solution)/shard_map/ppermute | solution.py:384
  174.5 8.1 %collective-permute-done.30.rest_2_ = bf16[2,2,64,256]{3,2,1,0:T(8,128)(2,1)S(1)} collective-permute-done((bf16[2,2,64,256]{3,2,1,0:T(8,128)(2,1)S(1)}, bf16[2,2,64,256]{3,2,1,0:T(8,128)(2,1)S(1)}, u32[]{:S(2)}, u32[]{:S(2)}) %collective-permute-start.30) | collective-permute-done | bytes 131104 | tf_op jit(solution)/shard_map/ppermute | solution.py:384
  183.3 5.7 %shard_map.92 = bf16[64,128,256]{2,1,0:T(8,128)(2,1)} custom-call(s32[1]{0:T(128)} %bitcast.place_ref, s32[1]{0:T(128)} %bitcast.1._, bf16[64,128,256]{2,1,0:T(8,128)(2,1)} %x_ref.7, s32[128,256]{1,0:T(8,128)} %o_ref.1, bf16[4,1024,128]{2,1,0:T(8,128)(2,1)} %constant.63.clone.t_ref, bf16[2,2,64,256]{3,2,1,0:T(8,128)(2,1)} %copy-done.3, ...), custom_call_target="tpu_custom_call" | custom-call | flops 67108864 | bytes 10092544 | tf_op jit(solution)/shard_map/pallas_call | solution.py:84
  (113 shorter events, 52.3 us)
Async XLA Ops:
  5.6 34.9 %collective-permute-start = (bf16[2,2,512,256]{3,2,1,0:T(8,128)(2,1)}, bf16[2,2,512,256]{3,2,1,0:T(8,128)(2,1)S(1)}, u32[]{:S(2)}, u32[]{:S(2)}) collective-permute-start(bf16[2,2,512,256]{3,2,1,0:T(8,128)(2,1)} %shard_map.83), channel_id=1, source_target_pairs={{0,2},{2,0},{1,3},{3,1},{4,6},{6,4},{5,7},{7,5},{8,10},{10,8},{9,1... | collective-permute-start | bytes 3145736 | tf_op jit(solution)/shard_map/ppermute | solution.py:384
  13.0 6.6 %collective-permute-start.1 = (bf16[2,2,64,256]{3,2,1,0:T(8,128)(2,1)}, bf16[2,2,64,256]{3,2,1,0:T(8,128)(2,1)S(1)}, u32[]{:S(2)}, u32[]{:S(2)}) collective-permute-start(bf16[2,2,64,256]{3,2,1,0:T(8,128)(2,1)} %get-tuple-element.30), channel_id=1, source_target_pairs={{0,4},{4,0},{8,12},{12,8},{1,5},{5,1},{9,13},{13,9},{2,6},{6,2},{1... | collective-permute-start | bytes 393224 | tf_op jit(solution)/shard_map/ppermute | solution.py:384
  14.6 12.8 %collective-permute-start.2 = (bf16[2,2,64,256]{3,2,1,0:T(8,128)(2,1)}, bf16[2,2,64,256]{3,2,1,0:T(8,128)(2,1)S(1)}, u32[]{:S(2)}, u32[]{:S(2)}) collective-permute-start(bf16[2,2,64,256]{3,2,1,0:T(8,128)(2,1)} %get-tuple-element.31), channel_id=1, source_target_pairs={{0,8},{4,12},{8,0},{12,4},{1,9},{5,13},{9,1},{13,5},{2,10},{6,14},... | collective-permute-start | bytes 393224 | tf_op jit(solution)/shard_map/ppermute | solution.py:384
  17.2 10.3 %collective-permute-start.3 = (bf16[2,2,64,256]{3,2,1,0:T(8,128)(2,1)}, bf16[2,2,64,256]{3,2,1,0:T(8,128)(2,1)S(1)}, u32[]{:S(2)}, u32[]{:S(2)}) collective-permute-start(bf16[2,2,64,256]{3,2,1,0:T(8,128)(2,1)} %get-tuple-element.32), channel_id=1, source_target_pairs={{0,12},{4,8},{8,4},{12,0},{1,13},{5,9},{9,5},{13,1},{2,14},{6,10},... | collective-permute-start | bytes 393224 | tf_op jit(solution)/shard_map/ppermute | solution.py:384
  29.1 5.6 %collective-permute-start.5 = (bf16[2,2,64,256]{3,2,1,0:T(8,128)(2,1)S(1)}, bf16[2,2,64,256]{3,2,1,0:T(8,128)(2,1)S(1)}, u32[]{:S(2)}, u32[]{:S(2)}) collective-permute-start(bf16[2,2,64,256]{3,2,1,0:T(8,128)(2,1)S(1)} %get-tuple-element.53.n0), channel_id=1, source_target_pairs={{0,2},{2,0},{1,3},{3,1},{4,6},{6,4},{5,7},{7,5},{8,10},{10,8},{9,1... | collective-permute-start | bytes 393224 | tf_op jit(solution)/shard_map/ppermute | solution.py:384
  29.7 10.8 %collective-permute-start.4 = (bf16[2,2,64,256]{3,2,1,0:T(8,128)(2,1)S(1)}, bf16[2,2,64,256]{3,2,1,0:T(8,128)(2,1)S(1)}, u32[]{:S(2)}, u32[]{:S(2)}) collective-permute-start(bf16[2,2,64,256]{3,2,1,0:T(8,128)(2,1)S(1)} %get-tuple-element.53.n0), channel_id=1, source_target_pairs={{0,1},{1,0},{2,3},{3,2},{4,5},{5,4},{6,7},{7,6},{8,9},{9,8},{10,11... | collective-permute-start | bytes 393224 | tf_op jit(solution)/shard_map/ppermute | solution.py:384
  34.7 5.8 %collective-permute-start.6 = (bf16[2,2,64,256]{3,2,1,0:T(8,128)(2,1)S(1)}, bf16[2,2,64,256]{3,2,1,0:T(8,128)(2,1)S(1)}, u32[]{:S(2)}, u32[]{:S(2)}) collective-permute-start(bf16[2,2,64,256]{3,2,1,0:T(8,128)(2,1)S(1)} %collective-permute-done.5.f0), channel_id=1, source_target_pairs={{0,1},{1,0},{2,3},{3,2},{4,5},{5,4},{6,7},{7,6},{8,9},{9,8},{10,11... | collective-permute-start | bytes 393224 | tf_op jit(solution)/shard_map/ppermute | solution.py:384
  45.3 8.5 %collective-permute-start.7 = (bf16[2,2,32,512]{3,2,1,0:T(8,128)(2,1)}, bf16[2,2,32,512]{3,2,1,0:T(8,128)(2,1)S(1)}, u32[]{:S(2)}, u32[]{:S(2)}) collective-permute-start(bf16[2,2,32,512]{3,2,1,0:T(8,128)(2,1)} %get-tuple-element.34), channel_id=1, source_target_pairs={{0,4},{4,0},{8,12},{12,8},{1,5},{5,1},{9,13},{13,9},{2,6},{6,2},{1... | collective-permute-start | bytes 393224 | tf_op jit(solution)/shard_map/ppermute | solution.py:384
  47.2 13.1 %collective-permute-start.8 = (bf16[2,2,32,512]{3,2,1,0:T(8,128)(2,1)}, bf16[2,2,32,512]{3,2,1,0:T(8,128)(2,1)S(1)}, u32[]{:S(2)}, u32[]{:S(2)}) collective-permute-start(bf16[2,2,32,512]{3,2,1,0:T(8,128)(2,1)} %get-tuple-element.35), channel_id=1, source_target_pairs={{0,8},{4,12},{8,0},{12,4},{1,9},{5,13},{9,1},{13,5},{2,10},{6,14},... | collective-permute-start | bytes 393224 | tf_op jit(solution)/shard_map/ppermute | solution.py:384
  49.7 10.5 %collective-permute-start.9 = (bf16[2,2,32,512]{3,2,1,0:T(8,128)(2,1)}, bf16[2,2,32,512]{3,2,1,0:T(8,128)(2,1)S(1)}, u32[]{:S(2)}, u32[]{:S(2)}) collective-permute-start(bf16[2,2,32,512]{3,2,1,0:T(8,128)(2,1)} %get-tuple-element.36), channel_id=1, source_target_pairs={{0,12},{4,8},{8,4},{12,0},{1,13},{5,9},{9,5},{13,1},{2,14},{6,10},... | collective-permute-start | bytes 393224 | tf_op jit(solution)/shard_map/ppermute | solution.py:384
  64.8 7.3 %collective-permute-start.10 = (bf16[2,2,32,512]{3,2,1,0:T(8,128)(2,1)}, bf16[2,2,32,512]{3,2,1,0:T(8,128)(2,1)S(1)}, u32[]{:S(2)}, u32[]{:S(2)}) collective-permute-start(bf16[2,2,32,512]{3,2,1,0:T(8,128)(2,1)} %get-tuple-element.38), channel_id=1, source_target_pairs={{0,4},{4,0},{8,12},{12,8},{1,5},{5,1},{9,13},{13,9},{2,6},{6,2},{1... | collective-permute-start | bytes 393224 | tf_op jit(solution)/shard_map/ppermute | solution.py:384
  67.5 12.7 %collective-permute-start.11 = (bf16[2,2,32,512]{3,2,1,0:T(8,128)(2,1)}, bf16[2,2,32,512]{3,2,1,0:T(8,128)(2,1)S(1)}, u32[]{:S(2)}, u32[]{:S(2)}) collective-permute-start(bf16[2,2,32,512]{3,2,1,0:T(8,128)(2,1)} %get-tuple-element.39), channel_id=1, source_target_pairs={{0,8},{4,12},{8,0},{12,4},{1,9},{5,13},{9,1},{13,5},{2,10},{6,14},... | collective-permute-start | bytes 393224 | tf_op jit(solution)/shard_map/ppermute | solution.py:384
  68.6 11.6 %collective-permute-start.12 = (bf16[2,2,32,512]{3,2,1,0:T(8,128)(2,1)}, bf16[2,2,32,512]{3,2,1,0:T(8,128)(2,1)S(1)}, u32[]{:S(2)}, u32[]{:S(2)}) collective-permute-start(bf16[2,2,32,512]{3,2,1,0:T(8,128)(2,1)} %get-tuple-element.40), channel_id=1, source_target_pairs={{0,12},{4,8},{8,4},{12,0},{1,13},{5,9},{9,5},{13,1},{2,14},{6,10},... | collective-permute-start | bytes 393224 | tf_op jit(solution)/shard_map/ppermute | solution.py:384
  83.8 1.7 collective-permute-start.13
  86.6 5.6 %collective-permute-start.14 = (bf16[2,2,64,256]{3,2,1,0:T(8,128)(2,1)S(1)}, bf16[2,2,64,256]{3,2,1,0:T(8,128)(2,1)S(1)}, u32[]{:S(2)}, u32[]{:S(2)}) collective-permute-start(bf16[2,2,64,256]{3,2,1,0:T(8,128)(2,1)S(1)} %fusion.12), channel_id=1, source_target_pairs={{0,2},{2,0},{1,3},{3,1},{4,6},{6,4},{5,7},{7,5},{8,10},{10,8},{9,1... | collective-permute-start | bytes 393224 | tf_op jit(solution)/shard_map/ppermute | solution.py:384
  93.2 7.7 %collective-permute-start.15 = (bf16[2,2,64,256]{3,2,1,0:T(8,128)(2,1)S(1)}, bf16[2,2,64,256]{3,2,1,0:T(8,128)(2,1)S(1)}, u32[]{:S(2)}, u32[]{:S(2)}) collective-permute-start(bf16[2,2,64,256]{3,2,1,0:T(8,128)(2,1)S(1)} %fusion.7.rest_0_), channel_id=1, source_target_pairs={{0,4},{4,0},{8,12},{12,8},{1,5},{5,1},{9,13},{13,9},{2,6},{6,2},{1... | collective-permute-start | bytes 393224 | tf_op jit(solution)/shard_map/ppermute | solution.py:384
  95.2 12.4 %collective-permute-start.16 = (bf16[2,2,64,256]{3,2,1,0:T(8,128)(2,1)S(1)}, bf16[2,2,64,256]{3,2,1,0:T(8,128)(2,1)S(1)}, u32[]{:S(2)}, u32[]{:S(2)}) collective-permute-start(bf16[2,2,64,256]{3,2,1,0:T(8,128)(2,1)S(1)} %fusion.7.rest_0_), channel_id=1, source_target_pairs={{0,8},{4,12},{8,0},{12,4},{1,9},{5,13},{9,1},{13,5},{2,10},{6,14},... | collective-permute-start | bytes 393224 | tf_op jit(solution)/shard_map/ppermute | solution.py:384
  96.2 11.4 %collective-permute-start.17 = (bf16[2,2,64,256]{3,2,1,0:T(8,128)(2,1)S(1)}, bf16[2,2,64,256]{3,2,1,0:T(8,128)(2,1)S(1)}, u32[]{:S(2)}, u32[]{:S(2)}) collective-permute-start(bf16[2,2,64,256]{3,2,1,0:T(8,128)(2,1)S(1)} %fusion.7.rest_0_), channel_id=1, source_target_pairs={{0,12},{4,8},{8,4},{12,0},{1,13},{5,9},{9,5},{13,1},{2,14},{6,10},... | collective-permute-start | bytes 393224 | tf_op jit(solution)/shard_map/ppermute | solution.py:384
  110.7 5.2 %collective-permute-start.19 = (bf16[2,2,64,256]{3,2,1,0:T(8,128)(2,1)}, bf16[2,2,64,256]{3,2,1,0:T(8,128)(2,1)S(1)}, u32[]{:S(2)}, u32[]{:S(2)}) collective-permute-start(bf16[2,2,64,256]{3,2,1,0:T(8,128)(2,1)} %shard_map.88.n0), channel_id=1, source_target_pairs={{0,2},{2,0},{1,3},{3,1},{4,6},{6,4},{5,7},{7,5},{8,10},{10,8},{9,1... | collective-permute-start | bytes 393224 | tf_op jit(solution)/shard_map/ppermute | solution.py:384
  112.1 3.7 %collective-permute-start.18 = (bf16[2,2,64,256]{3,2,1,0:T(8,128)(2,1)}, bf16[2,2,64,256]{3,2,1,0:T(8,128)(2,1)S(1)}, u32[]{:S(2)}, u32[]{:S(2)}) collective-permute-start(bf16[2,2,64,256]{3,2,1,0:T(8,128)(2,1)} %shard_map.88.n0), channel_id=1, source_target_pairs={{0,1},{1,0},{2,3},{3,2},{4,5},{5,4},{6,7},{7,6},{8,9},{9,8},{10,11... | collective-permute-start | bytes 393224 | tf_op jit(solution)/shard_map/ppermute | solution.py:384
  115.8 1.3 collective-permute-start.20
  120.9 7.8 %collective-permute-start.21 = (bf16[2,2,32,512]{3,2,1,0:T(8,128)(2,1)}, bf16[2,2,32,512]{3,2,1,0:T(8,128)(2,1)S(1)}, u32[]{:S(2)}, u32[]{:S(2)}) collective-permute-start(bf16[2,2,32,512]{3,2,1,0:T(8,128)(2,1)} %get-tuple-element.44), channel_id=1, source_target_pairs={{0,4},{4,0},{8,12},{12,8},{1,5},{5,1},{9,13},{13,9},{2,6},{6,2},{1... | collective-permute-start | bytes 393224 | tf_op jit(solution)/shard_map/ppermute | solution.py:384
  122.9 13.1 %collective-permute-start.22 = (bf16[2,2,32,512]{3,2,1,0:T(8,128)(2,1)}, bf16[2,2,32,512]{3,2,1,0:T(8,128)(2,1)S(1)}, u32[]{:S(2)}, u32[]{:S(2)}) collective-permute-start(bf16[2,2,32,512]{3,2,1,0:T(8,128)(2,1)} %get-tuple-element.45), channel_id=1, source_target_pairs={{0,8},{4,12},{8,0},{12,4},{1,9},{5,13},{9,1},{13,5},{2,10},{6,14},... | collective-permute-start | bytes 393224 | tf_op jit(solution)/shard_map/ppermute | solution.py:384
  123.9 12.1 %collective-permute-start.23 = (bf16[2,2,32,512]{3,2,1,0:T(8,128)(2,1)}, bf16[2,2,32,512]{3,2,1,0:T(8,128)(2,1)S(1)}, u32[]{:S(2)}, u32[]{:S(2)}) collective-permute-start(bf16[2,2,32,512]{3,2,1,0:T(8,128)(2,1)} %get-tuple-element.46), channel_id=1, source_target_pairs={{0,12},{4,8},{8,4},{12,0},{1,13},{5,9},{9,5},{13,1},{2,14},{6,10},... | collective-permute-start | bytes 393224 | tf_op jit(solution)/shard_map/ppermute | solution.py:384
  140.6 6.7 %collective-permute-start.24 = (bf16[2,2,32,512]{3,2,1,0:T(8,128)(2,1)}, bf16[2,2,32,512]{3,2,1,0:T(8,128)(2,1)S(1)}, u32[]{:S(2)}, u32[]{:S(2)}) collective-permute-start(bf16[2,2,32,512]{3,2,1,0:T(8,128)(2,1)} %get-tuple-element.48), channel_id=1, source_target_pairs={{0,4},{4,0},{8,12},{12,8},{1,5},{5,1},{9,13},{13,9},{2,6},{6,2},{1... | collective-permute-start | bytes 393224 | tf_op jit(solution)/shard_map/ppermute | solution.py:384
  142.9 12.3 %collective-permute-start.25 = (bf16[2,2,32,512]{3,2,1,0:T(8,128)(2,1)}, bf16[2,2,32,512]{3,2,1,0:T(8,128)(2,1)S(1)}, u32[]{:S(2)}, u32[]{:S(2)}) collective-permute-start(bf16[2,2,32,512]{3,2,1,0:T(8,128)(2,1)} %get-tuple-element.49), channel_id=1, source_target_pairs={{0,8},{4,12},{8,0},{12,4},{1,9},{5,13},{9,1},{13,5},{2,10},{6,14},... | collective-permute-start | bytes 393224 | tf_op jit(solution)/shard_map/ppermute | solution.py:384
  143.8 11.4 %collective-permute-start.26 = (bf16[2,2,32,512]{3,2,1,0:T(8,128)(2,1)}, bf16[2,2,32,512]{3,2,1,0:T(8,128)(2,1)S(1)}, u32[]{:S(2)}, u32[]{:S(2)}) collective-permute-start(bf16[2,2,32,512]{3,2,1,0:T(8,128)(2,1)} %get-tuple-element.50), channel_id=1, source_target_pairs={{0,12},{4,8},{8,4},{12,0},{1,13},{5,9},{9,5},{13,1},{2,14},{6,10},... | collective-permute-start | bytes 393224 | tf_op jit(solution)/shard_map/ppermute | solution.py:384
  158.9 1.7 collective-permute-start.27
  161.6 5.6 %collective-permute-start.28 = (bf16[2,2,64,256]{3,2,1,0:T(8,128)(2,1)S(1)}, bf16[2,2,64,256]{3,2,1,0:T(8,128)(2,1)S(1)}, u32[]{:S(2)}, u32[]{:S(2)}) collective-permute-start(bf16[2,2,64,256]{3,2,1,0:T(8,128)(2,1)S(1)} %fusion.13), channel_id=1, source_target_pairs={{0,2},{2,0},{1,3},{3,1},{4,6},{6,4},{5,7},{7,5},{8,10},{10,8},{9,1... | collective-permute-start | bytes 393224 | tf_op jit(solution)/shard_map/ppermute | solution.py:384
  168.2 6.3 %collective-permute-start.29 = (bf16[2,2,64,256]{3,2,1,0:T(8,128)(2,1)S(1)}, bf16[2,2,64,256]{3,2,1,0:T(8,128)(2,1)S(1)}, u32[]{:S(2)}, u32[]{:S(2)}) collective-permute-start(bf16[2,2,64,256]{3,2,1,0:T(8,128)(2,1)S(1)} %fusion.6.rest_0_), channel_id=1, source_target_pairs={{0,4},{4,0},{8,12},{12,8},{1,5},{5,1},{9,13},{13,9},{2,6},{6,2},{1... | collective-permute-start | bytes 393224 | tf_op jit(solution)/shard_map/ppermute | solution.py:384
  170.2 12.4 %collective-permute-start.30 = (bf16[2,2,64,256]{3,2,1,0:T(8,128)(2,1)S(1)}, bf16[2,2,64,256]{3,2,1,0:T(8,128)(2,1)S(1)}, u32[]{:S(2)}, u32[]{:S(2)}) collective-permute-start(bf16[2,2,64,256]{3,2,1,0:T(8,128)(2,1)S(1)} %fusion.6.rest_0_), channel_id=1, source_target_pairs={{0,8},{4,12},{8,0},{12,4},{1,9},{5,13},{9,1},{13,5},{2,10},{6,14},... | collective-permute-start | bytes 393224 | tf_op jit(solution)/shard_map/ppermute | solution.py:384
  171.2 11.4 %collective-permute-start.31 = (bf16[2,2,64,256]{3,2,1,0:T(8,128)(2,1)S(1)}, bf16[2,2,64,256]{3,2,1,0:T(8,128)(2,1)S(1)}, u32[]{:S(2)}, u32[]{:S(2)}) collective-permute-start(bf16[2,2,64,256]{3,2,1,0:T(8,128)(2,1)S(1)} %fusion.6.rest_0_), channel_id=1, source_target_pairs={{0,12},{4,8},{8,4},{12,0},{1,13},{5,9},{9,5},{13,1},{2,14},{6,10},... | collective-permute-start | bytes 393224 | tf_op jit(solution)/shard_map/ppermute | solution.py:384
  (29 other events, 152.0 us)

commit v3 on v2

--- a/solution.py
+++ b/solution.py
@@ -13,7 +13,7 @@
 ITERS = 2
 ROWS = 8
 CHUNKS = 1
-VMEM_BYTES = 62 * 1024 * 1024
+VMEM_BYTES = 16 * 1024 * 1024
 
 BF16 = jnp.bfloat16
 F32 = jnp.float32

time: 190 us -> 165 us (0.87)
  Pallas kernels: 40.8 us -> 16 us
  other arithmetic: 14.3 us -> 8.64 us
  local copies, waits for them, and re-layouts: 7.9 us -> 11.7 us
    pallas_call x11, Pallas kernels: 40.8 us -> 16 us  [call(): pl.pallas_call(body, grid_spec=pltpu.PrefetchScalarGridSpec(num_scalar_pr...]
    unnamed x59 -> x25, local copies, waits for them, and re-layouts: 7.9 us -> 11.7 us
    sin x2, other arithmetic: 6.43 us -> 4.21 us  [phases(): return (jnp.cos(angle), jnp.sin(angle), onset.astype(F32) * (1.0 / samples))]
  transfers between devices with their start and end apart: 32 -> 32, of which waited for: 20 -> 20; matrix products, arithmetic and copies ran while one was open for 5% -> 4% of each run, Pallas kernels for 5% -> 2%
where the time goes in v3:
time: 165 us; the launch traced here: 164 us
  waiting for transfers between devices  87.2 us (53%)
  starting transfers between devices  40.6 us (25%)
  Pallas kernels  16 us (10%)
  local copies, waits for them, and re-layouts  11.7 us (7%)
  other arithmetic  8.64 us (5%)
    ppermute x32, waiting for transfers between devices, exchanged(): lax.ppermute(value, axis, [(i, i ^ step) for i in range(lax.axis_size(axi...  87.2 us
    ppermute x32, starting transfers between devices, exchanged(): lax.ppermute(value, axis, [(i, i ^ step) for i in range(lax.axis_size(axi...  40.6 us
    pallas_call x11, Pallas kernels, call(): pl.pallas_call(body, grid_spec=pltpu.PrefetchScalarGridSpec(num_scalar_pr...  16 us
    unnamed x25, local copies, waits for them, and re-layouts  11.7 us
    sin x2, other arithmetic, phases(): return (jnp.cos(angle), jnp.sin(angle), onset.astype(F32) * (1.0 / samples))  4.21 us
  transfers between devices with their start and end apart: 32, of which 20 were waited for; matrix products, arithmetic and copies ran while one was open for 4% of the time, Pallas kernels for 2%

profile of v3, /device:TPU:0, one launch (start us, length us, event | category | flops | bytes accessed | tf_op | source)
XLA Modules:
  0.0 164.4 jit_solution(11661039102130712202)
XLA Ops:
  3.5 3.0 %collective-permute-start = (bf16[2,2,512,256]{3,2,1,0:T(8,128)(2,1)S(1)}, bf16[2,2,512,256]{3,2,1,0:T(8,128)(2,1)S(1)}, u32[]{:S(2)}, u32[]{:S(2)}) collective-permute-start(bf16[2,2,512,256]{3,2,1,0:T(8,128)(2,1)S(1)} %shard_map.83), channel_id=1, source_target_pairs={{0,2},{2,0},{1,3},{3,1},{4,6},{6,4},{5,7},{7,5},{8,10},{10,8},{9,1... | collective-permute-start | bytes 3145736 | tf_op jit(solution)/shard_map/ppermute | solution.py:384
  6.5 2.2 %copy-done = bf16[64,128,256]{2,1,0:T(8,128)(2,1)S(1)} copy-done((bf16[64,128,256]{2,1,0:T(8,128)(2,1)S(1)}, bf16[64,128,256]{2,1,0:T(8,128)(2,1)}, u32[]{:S(2)}) %copy-start) | copy-done | bytes 4194328
  12.9 2.6 %collective-permute-start.2 = (bf16[2,2,64,256]{3,2,1,0:T(8,128)(2,1)S(1)}, bf16[2,2,64,256]{3,2,1,0:T(8,128)(2,1)S(1)}, u32[]{:S(2)}, u32[]{:S(2)}) collective-permute-start(bf16[2,2,64,256]{3,2,1,0:T(8,128)(2,1)S(1)} %get-tuple-element.31), channel_id=1, source_target_pairs={{0,8},{4,12},{8,0},{12,4},{1,9},{5,13},{9,1},{13,5},{2,10},{6,14},... | collective-permute-start | bytes 393224 | tf_op jit(solution)/shard_map/ppermute | solution.py:384
  15.7 2.0 %collective-permute-done.1 = bf16[2,2,64,256]{3,2,1,0:T(8,128)(2,1)S(1)} collective-permute-done((bf16[2,2,64,256]{3,2,1,0:T(8,128)(2,1)S(1)}, bf16[2,2,64,256]{3,2,1,0:T(8,128)(2,1)S(1)}, u32[]{:S(2)}, u32[]{:S(2)}) %collective-permute-start.1) | collective-permute-done | bytes 131104 | tf_op jit(solution)/shard_map/ppermute | solution.py:384
  17.8 7.8 %collective-permute-done.2 = bf16[2,2,64,256]{3,2,1,0:T(8,128)(2,1)S(1)} collective-permute-done((bf16[2,2,64,256]{3,2,1,0:T(8,128)(2,1)S(1)}, bf16[2,2,64,256]{3,2,1,0:T(8,128)(2,1)S(1)}, u32[]{:S(2)}, u32[]{:S(2)}) %collective-permute-start.2) | collective-permute-done | bytes 131104 | tf_op jit(solution)/shard_map/ppermute | solution.py:384
  26.8 5.7 %collective-permute-done.5.f0 = bf16[2,2,64,256]{3,2,1,0:T(8,128)(2,1)} collective-permute-done((bf16[2,2,64,256]{3,2,1,0:T(8,128)(2,1)}, bf16[2,2,64,256]{3,2,1,0:T(8,128)(2,1)}, u32[]{:S(2)}, u32[]{:S(2)}) %collective-permute-start.5) | collective-permute-done | bytes 131104 | tf_op jit(solution)/shard_map/ppermute | solution.py:384
  36.3 2.3 %shard_map.85 = (bf16[2,2,32,512]{3,2,1,0:T(8,128)(2,1)S(1)}, bf16[2,2,32,512]{3,2,1,0:T(8,128)(2,1)S(1)}, bf16[2,2,32,512]{3,2,1,0:T(8,128)(2,1)S(1)}, bf16[2,2,32,512]{3,2,1,0:T(8,128)(2,1)S(1)}) custom-call(s32[1]{0:T(128)} %bitcast.place_ref, bf16[2,2,64,256]{3,2,1,0:T(8,128)(2,1)} %get-tuple-element.53.n0, ...), custom_call_target="tpu_custom_call" | custom-call | flops 536870912 | bytes 3145728 | tf_op jit(solution)/shard_map/pallas_call | solution.py:84
  38.6 1.9 %collective-permute-start.7 = (bf16[2,2,32,512]{3,2,1,0:T(8,128)(2,1)S(1)}, bf16[2,2,32,512]{3,2,1,0:T(8,128)(2,1)S(1)}, u32[]{:S(2)}, u32[]{:S(2)}) collective-permute-start(bf16[2,2,32,512]{3,2,1,0:T(8,128)(2,1)S(1)} %get-tuple-element.34), channel_id=1, source_target_pairs={{0,4},{4,0},{8,12},{12,8},{1,5},{5,1},{9,13},{13,9},{2,6},{6,2},{1... | collective-permute-start | bytes 393224 | tf_op jit(solution)/shard_map/ppermute | solution.py:384
  40.5 2.6 %collective-permute-start.8 = (bf16[2,2,32,512]{3,2,1,0:T(8,128)(2,1)S(1)}, bf16[2,2,32,512]{3,2,1,0:T(8,128)(2,1)S(1)}, u32[]{:S(2)}, u32[]{:S(2)}) collective-permute-start(bf16[2,2,32,512]{3,2,1,0:T(8,128)(2,1)S(1)} %get-tuple-element.35), channel_id=1, source_target_pairs={{0,8},{4,12},{8,0},{12,4},{1,9},{5,13},{9,1},{13,5},{2,10},{6,14},... | collective-permute-start | bytes 393224 | tf_op jit(solution)/shard_map/ppermute | solution.py:384
  43.1 2.1 %fusion.10 = (f32[4,2,32,512]{3,2,1,0:T(8,128)S(1)}, f32[4,2,32,512]{3,2,1,0:T(8,128)S(1)}) fusion(s32[32,512]{1,0:T(8,128)S(1)} %get-tuple-element.58, s32[4,2]{1,0:T(4,128)S(1)} %add_add_fusion), kind=kLoop, calls=%fused_computation.25 | loop fusion | flops 1835008 | bytes 1114144 | tf_op jit(solution)/shard_map/sin | solution.py:407
  45.2 1.7 %collective-permute-done.7.rest_1_ = bf16[2,2,32,512]{3,2,1,0:T(8,128)(2,1)S(1)} collective-permute-done((bf16[2,2,32,512]{3,2,1,0:T(8,128)(2,1)S(1)}, bf16[2,2,32,512]{3,2,1,0:T(8,128)(2,1)S(1)}, u32[]{:S(2)}, u32[]{:S(2)}) %collective-permute-start.7) | collective-permute-done | bytes 131104 | tf_op jit(solution)/shard_map/ppermute | solution.py:384
  47.0 6.5 %collective-permute-done.8.rest_2_ = bf16[2,2,32,512]{3,2,1,0:T(8,128)(2,1)S(1)} collective-permute-done((bf16[2,2,32,512]{3,2,1,0:T(8,128)(2,1)S(1)}, bf16[2,2,32,512]{3,2,1,0:T(8,128)(2,1)S(1)}, u32[]{:S(2)}, u32[]{:S(2)}) %collective-permute-start.8) | collective-permute-done | bytes 131104 | tf_op jit(solution)/shard_map/ppermute | solution.py:384
  54.8 2.7 %collective-permute-start.10 = (bf16[2,2,32,512]{3,2,1,0:T(8,128)(2,1)S(1)}, bf16[2,2,32,512]{3,2,1,0:T(8,128)(2,1)S(1)}, u32[]{:S(2)}, u32[]{:S(2)}) collective-permute-start(bf16[2,2,32,512]{3,2,1,0:T(8,128)(2,1)S(1)} %get-tuple-element.38), channel_id=1, source_target_pairs={{0,4},{4,0},{8,12},{12,8},{1,5},{5,1},{9,13},{13,9},{2,6},{6,2},{1... | collective-permute-start | bytes 393224 | tf_op jit(solution)/shard_map/ppermute | solution.py:384
  60.0 2.0 %collective-permute-done.10.rest_1_ = bf16[2,2,32,512]{3,2,1,0:T(8,128)(2,1)S(1)} collective-permute-done((bf16[2,2,32,512]{3,2,1,0:T(8,128)(2,1)S(1)}, bf16[2,2,32,512]{3,2,1,0:T(8,128)(2,1)S(1)}, u32[]{:S(2)}, u32[]{:S(2)}) %collective-permute-start.10) | collective-permute-done | bytes 131104 | tf_op jit(solution)/shard_map/ppermute | solution.py:384
  62.0 8.1 %collective-permute-done.11.rest_2_ = bf16[2,2,32,512]{3,2,1,0:T(8,128)(2,1)S(1)} collective-permute-done((bf16[2,2,32,512]{3,2,1,0:T(8,128)(2,1)S(1)}, bf16[2,2,32,512]{3,2,1,0:T(8,128)(2,1)S(1)}, u32[]{:S(2)}, u32[]{:S(2)}) %collective-permute-start.11) | collective-permute-done | bytes 131104 | tf_op jit(solution)/shard_map/ppermute | solution.py:384
  75.8 3.5 %collective-permute-done.14 = bf16[2,2,64,256]{3,2,1,0:T(8,128)(2,1)} collective-permute-done((bf16[2,2,64,256]{3,2,1,0:T(8,128)(2,1)}, bf16[2,2,64,256]{3,2,1,0:T(8,128)(2,1)}, u32[]{:S(2)}, u32[]{:S(2)}) %collective-permute-start.14) | collective-permute-done | bytes 131104 | tf_op jit(solution)/shard_map/ppermute | solution.py:384
  80.4 2.0 %collective-permute-start.15 = (bf16[2,2,64,256]{3,2,1,0:T(8,128)(2,1)S(1)}, bf16[2,2,64,256]{3,2,1,0:T(8,128)(2,1)S(1)}, u32[]{:S(2)}, u32[]{:S(2)}) collective-permute-start(bf16[2,2,64,256]{3,2,1,0:T(8,128)(2,1)S(1)} %fusion.7.rest_0_), channel_id=1, source_target_pairs={{0,4},{4,0},{8,12},{12,8},{1,5},{5,1},{9,13},{13,9},{2,6},{6,2},{1... | collective-permute-start | bytes 393224 | tf_op jit(solution)/shard_map/ppermute | solution.py:384
  84.8 2.1 %fusion.8 = (f32[4,2,64,256]{3,2,1,0:T(8,128)S(1)}, f32[4,2,64,256]{3,2,1,0:T(8,128)S(1)}) fusion(s32[64,256]{1,0:T(8,128)S(1)} %get-tuple-element.56, s32[4,2]{1,0:T(4,128)S(1)} %add_add_fusion), kind=kLoop, calls=%fused_computation.22 | loop fusion | flops 1835008 | bytes 1114144 | tf_op jit(solution)/shard_map/sin | solution.py:407
  87.0 7.8 %collective-permute-done.16.rest_2_ = bf16[2,2,64,256]{3,2,1,0:T(8,128)(2,1)S(1)} collective-permute-done((bf16[2,2,64,256]{3,2,1,0:T(8,128)(2,1)S(1)}, bf16[2,2,64,256]{3,2,1,0:T(8,128)(2,1)S(1)}, u32[]{:S(2)}, u32[]{:S(2)}) %collective-permute-start.16) | collective-permute-done | bytes 131104 | tf_op jit(solution)/shard_map/ppermute | solution.py:384
  97.1 3.5 %collective-permute-done.19.f0 = bf16[2,2,64,256]{3,2,1,0:T(8,128)(2,1)S(1)} collective-permute-done((bf16[2,2,64,256]{3,2,1,0:T(8,128)(2,1)S(1)}, bf16[2,2,64,256]{3,2,1,0:T(8,128)(2,1)S(1)}, u32[]{:S(2)}, u32[]{:S(2)}) %collective-permute-start.19) | collective-permute-done | bytes 131104 | tf_op jit(solution)/shard_map/ppermute | solution.py:384
  103.2 2.0 %collective-permute-start.21 = (bf16[2,2,32,512]{3,2,1,0:T(8,128)(2,1)S(1)}, bf16[2,2,32,512]{3,2,1,0:T(8,128)(2,1)S(1)}, u32[]{:S(2)}, u32[]{:S(2)}) collective-permute-start(bf16[2,2,32,512]{3,2,1,0:T(8,128)(2,1)S(1)} %get-tuple-element.44), channel_id=1, source_target_pairs={{0,4},{4,0},{8,12},{12,8},{1,5},{5,1},{9,13},{13,9},{2,6},{6,2},{1... | collective-permute-start | bytes 393224 | tf_op jit(solution)/shard_map/ppermute | solution.py:384
  107.6 3.2 %collective-permute-done.21.rest_1_ = bf16[2,2,32,512]{3,2,1,0:T(8,128)(2,1)S(1)} collective-permute-done((bf16[2,2,32,512]{3,2,1,0:T(8,128)(2,1)S(1)}, bf16[2,2,32,512]{3,2,1,0:T(8,128)(2,1)S(1)}, u32[]{:S(2)}, u32[]{:S(2)}) %collective-permute-start.21) | collective-permute-done | bytes 131104 | tf_op jit(solution)/shard_map/ppermute | solution.py:384
  110.9 7.2 %collective-permute-done.22.rest_2_ = bf16[2,2,32,512]{3,2,1,0:T(8,128)(2,1)S(1)} collective-permute-done((bf16[2,2,32,512]{3,2,1,0:T(8,128)(2,1)S(1)}, bf16[2,2,32,512]{3,2,1,0:T(8,128)(2,1)S(1)}, u32[]{:S(2)}, u32[]{:S(2)}) %collective-permute-start.22) | collective-permute-done | bytes 131104 | tf_op jit(solution)/shard_map/ppermute | solution.py:384
  119.5 2.4 %collective-permute-start.24 = (bf16[2,2,32,512]{3,2,1,0:T(8,128)(2,1)S(1)}, bf16[2,2,32,512]{3,2,1,0:T(8,128)(2,1)S(1)}, u32[]{:S(2)}, u32[]{:S(2)}) collective-permute-start(bf16[2,2,32,512]{3,2,1,0:T(8,128)(2,1)S(1)} %get-tuple-element.48), channel_id=1, source_target_pairs={{0,4},{4,0},{8,12},{12,8},{1,5},{5,1},{9,13},{13,9},{2,6},{6,2},{1... | collective-permute-start | bytes 393224 | tf_op jit(solution)/shard_map/ppermute | solution.py:384
  124.3 1.8 %collective-permute-done.24.rest_1_ = bf16[2,2,32,512]{3,2,1,0:T(8,128)(2,1)S(1)} collective-permute-done((bf16[2,2,32,512]{3,2,1,0:T(8,128)(2,1)S(1)}, bf16[2,2,32,512]{3,2,1,0:T(8,128)(2,1)S(1)}, u32[]{:S(2)}, u32[]{:S(2)}) %collective-permute-start.24) | collective-permute-done | bytes 131104 | tf_op jit(solution)/shard_map/ppermute | solution.py:384
  126.1 7.9 %collective-permute-done.25.rest_2_ = bf16[2,2,32,512]{3,2,1,0:T(8,128)(2,1)S(1)} collective-permute-done((bf16[2,2,32,512]{3,2,1,0:T(8,128)(2,1)S(1)}, bf16[2,2,32,512]{3,2,1,0:T(8,128)(2,1)S(1)}, u32[]{:S(2)}, u32[]{:S(2)}) %collective-permute-start.25) | collective-permute-done | bytes 131104 | tf_op jit(solution)/shard_map/ppermute | solution.py:384
  138.2 4.0 %collective-permute-done.28 = bf16[2,2,64,256]{3,2,1,0:T(8,128)(2,1)S(1)} collective-permute-done((bf16[2,2,64,256]{3,2,1,0:T(8,128)(2,1)S(1)}, bf16[2,2,64,256]{3,2,1,0:T(8,128)(2,1)S(1)}, u32[]{:S(2)}, u32[]{:S(2)}) %collective-permute-start.28) | collective-permute-done | bytes 131104 | tf_op jit(solution)/shard_map/ppermute | solution.py:384
  142.3 2.0 %collective-permute-start.29 = (bf16[2,2,64,256]{3,2,1,0:T(8,128)(2,1)S(1)}, bf16[2,2,64,256]{3,2,1,0:T(8,128)(2,1)S(1)}, u32[]{:S(2)}, u32[]{:S(2)}) collective-permute-start(bf16[2,2,64,256]{3,2,1,0:T(8,128)(2,1)S(1)} %fusion.6.rest_0_), channel_id=1, source_target_pairs={{0,4},{4,0},{8,12},{12,8},{1,5},{5,1},{9,13},{13,9},{2,6},{6,2},{1... | collective-permute-start | bytes 393224 | tf_op jit(solution)/shard_map/ppermute | solution.py:384
  146.8 1.8 %collective-permute-done.29.rest_1_ = bf16[2,2,64,256]{3,2,1,0:T(8,128)(2,1)S(1)} collective-permute-done((bf16[2,2,64,256]{3,2,1,0:T(8,128)(2,1)S(1)}, bf16[2,2,64,256]{3,2,1,0:T(8,128)(2,1)S(1)}, u32[]{:S(2)}, u32[]{:S(2)}) %collective-permute-start.29) | collective-permute-done | bytes 131104 | tf_op jit(solution)/shard_map/ppermute | solution.py:384
  148.5 8.2 %collective-permute-done.30.rest_2_ = bf16[2,2,64,256]{3,2,1,0:T(8,128)(2,1)S(1)} collective-permute-done((bf16[2,2,64,256]{3,2,1,0:T(8,128)(2,1)S(1)}, bf16[2,2,64,256]{3,2,1,0:T(8,128)(2,1)S(1)}, u32[]{:S(2)}, u32[]{:S(2)}) %collective-permute-start.30) | collective-permute-done | bytes 131104 | tf_op jit(solution)/shard_map/ppermute | solution.py:384
  156.7 2.2 %copy-done.1 = bf16[64,128,256]{2,1,0:T(8,128)(2,1)S(1)} copy-done((bf16[64,128,256]{2,1,0:T(8,128)(2,1)S(1)}, bf16[64,128,256]{2,1,0:T(8,128)(2,1)}, u32[]{:S(2)}) %copy-start.1) | copy-done | bytes 4194328
  161.0 3.4 %shard_map.92 = bf16[64,128,256]{2,1,0:T(8,128)(2,1)} custom-call(s32[1]{0:T(128)} %bitcast.place_ref, s32[1]{0:T(128)} %bitcast.1._, bf16[64,128,256]{2,1,0:T(8,128)(2,1)S(1)} %copy-done.1, s32[128,256]{1,0:T(8,128)S(1)} %copy-done.10, bf16[4,1024,128]{2,1,0:T(8,128)(2,1)S(1)} %copy-done.6, bf16[2,2,64,256]{3,2,1,0:T(8,128)(2,1)S(1)} %fusion.6.rest_0_, ...), custom_call_target="tpu_custom_call" | custom-call | flops 67108864 | bytes 10092544 | tf_op jit(solution)/shard_map/pallas_call | solution.py:84
  (79 shorter events, 45.9 us)
Async XLA Ops:
  3.5 32.8 %collective-permute-start = (bf16[2,2,512,256]{3,2,1,0:T(8,128)(2,1)S(1)}, bf16[2,2,512,256]{3,2,1,0:T(8,128)(2,1)S(1)}, u32[]{:S(2)}, u32[]{:S(2)}) collective-permute-start(bf16[2,2,512,256]{3,2,1,0:T(8,128)(2,1)S(1)} %shard_map.83), channel_id=1, source_target_pairs={{0,2},{2,0},{1,3},{3,1},{4,6},{6,4},{5,7},{7,5},{8,10},{10,8},{9,1... | collective-permute-start | bytes 3145736 | tf_op jit(solution)/shard_map/ppermute | solution.py:384
  11.3 6.5 %collective-permute-start.1 = (bf16[2,2,64,256]{3,2,1,0:T(8,128)(2,1)S(1)}, bf16[2,2,64,256]{3,2,1,0:T(8,128)(2,1)S(1)}, u32[]{:S(2)}, u32[]{:S(2)}) collective-permute-start(bf16[2,2,64,256]{3,2,1,0:T(8,128)(2,1)S(1)} %get-tuple-element.30), channel_id=1, source_target_pairs={{0,4},{4,0},{8,12},{12,8},{1,5},{5,1},{9,13},{13,9},{2,6},{6,2},{1... | collective-permute-start | bytes 393224 | tf_op jit(solution)/shard_map/ppermute | solution.py:384
  12.9 12.6 %collective-permute-start.2 = (bf16[2,2,64,256]{3,2,1,0:T(8,128)(2,1)S(1)}, bf16[2,2,64,256]{3,2,1,0:T(8,128)(2,1)S(1)}, u32[]{:S(2)}, u32[]{:S(2)}) collective-permute-start(bf16[2,2,64,256]{3,2,1,0:T(8,128)(2,1)S(1)} %get-tuple-element.31), channel_id=1, source_target_pairs={{0,8},{4,12},{8,0},{12,4},{1,9},{5,13},{9,1},{13,5},{2,10},{6,14},... | collective-permute-start | bytes 393224 | tf_op jit(solution)/shard_map/ppermute | solution.py:384
  15.5 10.1 %collective-permute-start.3 = (bf16[2,2,64,256]{3,2,1,0:T(8,128)(2,1)S(1)}, bf16[2,2,64,256]{3,2,1,0:T(8,128)(2,1)S(1)}, u32[]{:S(2)}, u32[]{:S(2)}) collective-permute-start(bf16[2,2,64,256]{3,2,1,0:T(8,128)(2,1)S(1)} %get-tuple-element.32), channel_id=1, source_target_pairs={{0,12},{4,8},{8,4},{12,0},{1,13},{5,9},{9,5},{13,1},{2,14},{6,10},... | collective-permute-start | bytes 393224 | tf_op jit(solution)/shard_map/ppermute | solution.py:384
  26.3 6.3 %collective-permute-start.5 = (bf16[2,2,64,256]{3,2,1,0:T(8,128)(2,1)}, bf16[2,2,64,256]{3,2,1,0:T(8,128)(2,1)}, u32[]{:S(2)}, u32[]{:S(2)}) collective-permute-start(bf16[2,2,64,256]{3,2,1,0:T(8,128)(2,1)} %get-tuple-element.53.n0), channel_id=1, source_target_pairs={{0,2},{2,0},{1,3},{3,1},{4,6},{6,4},{5,7},{7,5},{8,10},{10,8},{9,1... | collective-permute-start | bytes 393224 | tf_op jit(solution)/shard_map/ppermute | solution.py:384
  26.8 9.5 %collective-permute-start.4 = (bf16[2,2,64,256]{3,2,1,0:T(8,128)(2,1)}, bf16[2,2,64,256]{3,2,1,0:T(8,128)(2,1)}, u32[]{:S(2)}, u32[]{:S(2)}) collective-permute-start(bf16[2,2,64,256]{3,2,1,0:T(8,128)(2,1)} %get-tuple-element.53.n0), channel_id=1, source_target_pairs={{0,1},{1,0},{2,3},{3,2},{4,5},{5,4},{6,7},{7,6},{8,9},{9,8},{10,11... | collective-permute-start | bytes 393224 | tf_op jit(solution)/shard_map/ppermute | solution.py:384
  32.6 3.7 %collective-permute-start.6 = (bf16[2,2,64,256]{3,2,1,0:T(8,128)(2,1)}, bf16[2,2,64,256]{3,2,1,0:T(8,128)(2,1)}, u32[]{:S(2)}, u32[]{:S(2)}) collective-permute-start(bf16[2,2,64,256]{3,2,1,0:T(8,128)(2,1)} %collective-permute-done.5.f0), channel_id=1, source_target_pairs={{0,1},{1,0},{2,3},{3,2},{4,5},{5,4},{6,7},{7,6},{8,9},{9,8},{10,11... | collective-permute-start | bytes 393224 | tf_op jit(solution)/shard_map/ppermute | solution.py:384
  38.6 8.3 %collective-permute-start.7 = (bf16[2,2,32,512]{3,2,1,0:T(8,128)(2,1)S(1)}, bf16[2,2,32,512]{3,2,1,0:T(8,128)(2,1)S(1)}, u32[]{:S(2)}, u32[]{:S(2)}) collective-permute-start(bf16[2,2,32,512]{3,2,1,0:T(8,128)(2,1)S(1)} %get-tuple-element.34), channel_id=1, source_target_pairs={{0,4},{4,0},{8,12},{12,8},{1,5},{5,1},{9,13},{13,9},{2,6},{6,2},{1... | collective-permute-start | bytes 393224 | tf_op jit(solution)/shard_map/ppermute | solution.py:384
  40.5 12.9 %collective-permute-start.8 = (bf16[2,2,32,512]{3,2,1,0:T(8,128)(2,1)S(1)}, bf16[2,2,32,512]{3,2,1,0:T(8,128)(2,1)S(1)}, u32[]{:S(2)}, u32[]{:S(2)}) collective-permute-start(bf16[2,2,32,512]{3,2,1,0:T(8,128)(2,1)S(1)} %get-tuple-element.35), channel_id=1, source_target_pairs={{0,8},{4,12},{8,0},{12,4},{1,9},{5,13},{9,1},{13,5},{2,10},{6,14},... | collective-permute-start | bytes 393224 | tf_op jit(solution)/shard_map/ppermute | solution.py:384
  43.1 10.3 %collective-permute-start.9 = (bf16[2,2,32,512]{3,2,1,0:T(8,128)(2,1)S(1)}, bf16[2,2,32,512]{3,2,1,0:T(8,128)(2,1)S(1)}, u32[]{:S(2)}, u32[]{:S(2)}) collective-permute-start(bf16[2,2,32,512]{3,2,1,0:T(8,128)(2,1)S(1)} %get-tuple-element.36), channel_id=1, source_target_pairs={{0,12},{4,8},{8,4},{12,0},{1,13},{5,9},{9,5},{13,1},{2,14},{6,10},... | collective-permute-start | bytes 393224 | tf_op jit(solution)/shard_map/ppermute | solution.py:384
  54.8 7.1 %collective-permute-start.10 = (bf16[2,2,32,512]{3,2,1,0:T(8,128)(2,1)S(1)}, bf16[2,2,32,512]{3,2,1,0:T(8,128)(2,1)S(1)}, u32[]{:S(2)}, u32[]{:S(2)}) collective-permute-start(bf16[2,2,32,512]{3,2,1,0:T(8,128)(2,1)S(1)} %get-tuple-element.38), channel_id=1, source_target_pairs={{0,4},{4,0},{8,12},{12,8},{1,5},{5,1},{9,13},{13,9},{2,6},{6,2},{1... | collective-permute-start | bytes 393224 | tf_op jit(solution)/shard_map/ppermute | solution.py:384
  57.5 12.5 %collective-permute-start.11 = (bf16[2,2,32,512]{3,2,1,0:T(8,128)(2,1)S(1)}, bf16[2,2,32,512]{3,2,1,0:T(8,128)(2,1)S(1)}, u32[]{:S(2)}, u32[]{:S(2)}) collective-permute-start(bf16[2,2,32,512]{3,2,1,0:T(8,128)(2,1)S(1)} %get-tuple-element.39), channel_id=1, source_target_pairs={{0,8},{4,12},{8,0},{12,4},{1,9},{5,13},{9,1},{13,5},{2,10},{6,14},... | collective-permute-start | bytes 393224 | tf_op jit(solution)/shard_map/ppermute | solution.py:384
  58.6 11.4 %collective-permute-start.12 = (bf16[2,2,32,512]{3,2,1,0:T(8,128)(2,1)S(1)}, bf16[2,2,32,512]{3,2,1,0:T(8,128)(2,1)S(1)}, u32[]{:S(2)}, u32[]{:S(2)}) collective-permute-start(bf16[2,2,32,512]{3,2,1,0:T(8,128)(2,1)S(1)} %get-tuple-element.40), channel_id=1, source_target_pairs={{0,12},{4,8},{8,4},{12,0},{1,13},{5,9},{9,5},{13,1},{2,14},{6,10},... | collective-permute-start | bytes 393224 | tf_op jit(solution)/shard_map/ppermute | solution.py:384
  71.1 1.6 collective-permute-start.13
  73.4 5.9 %collective-permute-start.14 = (bf16[2,2,64,256]{3,2,1,0:T(8,128)(2,1)}, bf16[2,2,64,256]{3,2,1,0:T(8,128)(2,1)}, u32[]{:S(2)}, u32[]{:S(2)}) collective-permute-start(bf16[2,2,64,256]{3,2,1,0:T(8,128)(2,1)} %fusion.12), channel_id=1, source_target_pairs={{0,2},{2,0},{1,3},{3,1},{4,6},{6,4},{5,7},{7,5},{8,10},{10,8},{9,1... | collective-permute-start | bytes 393224 | tf_op jit(solution)/shard_map/ppermute | solution.py:384
  80.4 6.6 %collective-permute-start.15 = (bf16[2,2,64,256]{3,2,1,0:T(8,128)(2,1)S(1)}, bf16[2,2,64,256]{3,2,1,0:T(8,128)(2,1)S(1)}, u32[]{:S(2)}, u32[]{:S(2)}) collective-permute-start(bf16[2,2,64,256]{3,2,1,0:T(8,128)(2,1)S(1)} %fusion.7.rest_0_), channel_id=1, source_target_pairs={{0,4},{4,0},{8,12},{12,8},{1,5},{5,1},{9,13},{13,9},{2,6},{6,2},{1... | collective-permute-start | bytes 393224 | tf_op jit(solution)/shard_map/ppermute | solution.py:384
  82.4 12.4 %collective-permute-start.16 = (bf16[2,2,64,256]{3,2,1,0:T(8,128)(2,1)S(1)}, bf16[2,2,64,256]{3,2,1,0:T(8,128)(2,1)S(1)}, u32[]{:S(2)}, u32[]{:S(2)}) collective-permute-start(bf16[2,2,64,256]{3,2,1,0:T(8,128)(2,1)S(1)} %fusion.7.rest_0_), channel_id=1, source_target_pairs={{0,8},{4,12},{8,0},{12,4},{1,9},{5,13},{9,1},{13,5},{2,10},{6,14},... | collective-permute-start | bytes 393224 | tf_op jit(solution)/shard_map/ppermute | solution.py:384
  83.4 11.4 %collective-permute-start.17 = (bf16[2,2,64,256]{3,2,1,0:T(8,128)(2,1)S(1)}, bf16[2,2,64,256]{3,2,1,0:T(8,128)(2,1)S(1)}, u32[]{:S(2)}, u32[]{:S(2)}) collective-permute-start(bf16[2,2,64,256]{3,2,1,0:T(8,128)(2,1)S(1)} %fusion.7.rest_0_), channel_id=1, source_target_pairs={{0,12},{4,8},{8,4},{12,0},{1,13},{5,9},{9,5},{13,1},{2,14},{6,10},... | collective-permute-start | bytes 393224 | tf_op jit(solution)/shard_map/ppermute | solution.py:384
  95.6 5.0 %collective-permute-start.19 = (bf16[2,2,64,256]{3,2,1,0:T(8,128)(2,1)S(1)}, bf16[2,2,64,256]{3,2,1,0:T(8,128)(2,1)S(1)}, u32[]{:S(2)}, u32[]{:S(2)}) collective-permute-start(bf16[2,2,64,256]{3,2,1,0:T(8,128)(2,1)S(1)} %shard_map.88.n0), channel_id=1, source_target_pairs={{0,2},{2,0},{1,3},{3,1},{4,6},{6,4},{5,7},{7,5},{8,10},{10,8},{9,1... | collective-permute-start | bytes 393224 | tf_op jit(solution)/shard_map/ppermute | solution.py:384
  97.1 3.5 %collective-permute-start.18 = (bf16[2,2,64,256]{3,2,1,0:T(8,128)(2,1)S(1)}, bf16[2,2,64,256]{3,2,1,0:T(8,128)(2,1)S(1)}, u32[]{:S(2)}, u32[]{:S(2)}) collective-permute-start(bf16[2,2,64,256]{3,2,1,0:T(8,128)(2,1)S(1)} %shard_map.88.n0), channel_id=1, source_target_pairs={{0,1},{1,0},{2,3},{3,2},{4,5},{5,4},{6,7},{7,6},{8,9},{9,8},{10,11... | collective-permute-start | bytes 393224 | tf_op jit(solution)/shard_map/ppermute | solution.py:384
  100.6 1.3 collective-permute-start.20
  103.2 7.7 %collective-permute-start.21 = (bf16[2,2,32,512]{3,2,1,0:T(8,128)(2,1)S(1)}, bf16[2,2,32,512]{3,2,1,0:T(8,128)(2,1)S(1)}, u32[]{:S(2)}, u32[]{:S(2)}) collective-permute-start(bf16[2,2,32,512]{3,2,1,0:T(8,128)(2,1)S(1)} %get-tuple-element.44), channel_id=1, source_target_pairs={{0,4},{4,0},{8,12},{12,8},{1,5},{5,1},{9,13},{13,9},{2,6},{6,2},{1... | collective-permute-start | bytes 393224 | tf_op jit(solution)/shard_map/ppermute | solution.py:384
  105.2 12.9 %collective-permute-start.22 = (bf16[2,2,32,512]{3,2,1,0:T(8,128)(2,1)S(1)}, bf16[2,2,32,512]{3,2,1,0:T(8,128)(2,1)S(1)}, u32[]{:S(2)}, u32[]{:S(2)}) collective-permute-start(bf16[2,2,32,512]{3,2,1,0:T(8,128)(2,1)S(1)} %get-tuple-element.45), channel_id=1, source_target_pairs={{0,8},{4,12},{8,0},{12,4},{1,9},{5,13},{9,1},{13,5},{2,10},{6,14},... | collective-permute-start | bytes 393224 | tf_op jit(solution)/shard_map/ppermute | solution.py:384
  106.2 11.9 %collective-permute-start.23 = (bf16[2,2,32,512]{3,2,1,0:T(8,128)(2,1)S(1)}, bf16[2,2,32,512]{3,2,1,0:T(8,128)(2,1)S(1)}, u32[]{:S(2)}, u32[]{:S(2)}) collective-permute-start(bf16[2,2,32,512]{3,2,1,0:T(8,128)(2,1)S(1)} %get-tuple-element.46), channel_id=1, source_target_pairs={{0,12},{4,8},{8,4},{12,0},{1,13},{5,9},{9,5},{13,1},{2,14},{6,10},... | collective-permute-start | bytes 393224 | tf_op jit(solution)/shard_map/ppermute | solution.py:384
  119.5 6.6 %collective-permute-start.24 = (bf16[2,2,32,512]{3,2,1,0:T(8,128)(2,1)S(1)}, bf16[2,2,32,512]{3,2,1,0:T(8,128)(2,1)S(1)}, u32[]{:S(2)}, u32[]{:S(2)}) collective-permute-start(bf16[2,2,32,512]{3,2,1,0:T(8,128)(2,1)S(1)} %get-tuple-element.48), channel_id=1, source_target_pairs={{0,4},{4,0},{8,12},{12,8},{1,5},{5,1},{9,13},{13,9},{2,6},{6,2},{1... | collective-permute-start | bytes 393224 | tf_op jit(solution)/shard_map/ppermute | solution.py:384
  121.8 12.1 %collective-permute-start.25 = (bf16[2,2,32,512]{3,2,1,0:T(8,128)(2,1)S(1)}, bf16[2,2,32,512]{3,2,1,0:T(8,128)(2,1)S(1)}, u32[]{:S(2)}, u32[]{:S(2)}) collective-permute-start(bf16[2,2,32,512]{3,2,1,0:T(8,128)(2,1)S(1)} %get-tuple-element.49), channel_id=1, source_target_pairs={{0,8},{4,12},{8,0},{12,4},{1,9},{5,13},{9,1},{13,5},{2,10},{6,14},... | collective-permute-start | bytes 393224 | tf_op jit(solution)/shard_map/ppermute | solution.py:384
  122.8 11.2 %collective-permute-start.26 = (bf16[2,2,32,512]{3,2,1,0:T(8,128)(2,1)S(1)}, bf16[2,2,32,512]{3,2,1,0:T(8,128)(2,1)S(1)}, u32[]{:S(2)}, u32[]{:S(2)}) collective-permute-start(bf16[2,2,32,512]{3,2,1,0:T(8,128)(2,1)S(1)} %get-tuple-element.50), channel_id=1, source_target_pairs={{0,12},{4,8},{8,4},{12,0},{1,13},{5,9},{9,5},{13,1},{2,14},{6,10},... | collective-permute-start | bytes 393224 | tf_op jit(solution)/shard_map/ppermute | solution.py:384
  135.0 1.6 collective-permute-start.27
  136.6 5.6 %collective-permute-start.28 = (bf16[2,2,64,256]{3,2,1,0:T(8,128)(2,1)S(1)}, bf16[2,2,64,256]{3,2,1,0:T(8,128)(2,1)S(1)}, u32[]{:S(2)}, u32[]{:S(2)}) collective-permute-start(bf16[2,2,64,256]{3,2,1,0:T(8,128)(2,1)S(1)} %fusion.13), channel_id=1, source_target_pairs={{0,2},{2,0},{1,3},{3,1},{4,6},{6,4},{5,7},{7,5},{8,10},{10,8},{9,1... | collective-permute-start | bytes 393224 | tf_op jit(solution)/shard_map/ppermute | solution.py:384
  142.3 6.2 %collective-permute-start.29 = (bf16[2,2,64,256]{3,2,1,0:T(8,128)(2,1)S(1)}, bf16[2,2,64,256]{3,2,1,0:T(8,128)(2,1)S(1)}, u32[]{:S(2)}, u32[]{:S(2)}) collective-permute-start(bf16[2,2,64,256]{3,2,1,0:T(8,128)(2,1)S(1)} %fusion.6.rest_0_), channel_id=1, source_target_pairs={{0,4},{4,0},{8,12},{12,8},{1,5},{5,1},{9,13},{13,9},{2,6},{6,2},{1... | collective-permute-start | bytes 393224 | tf_op jit(solution)/shard_map/ppermute | solution.py:384
  144.3 12.4 %collective-permute-start.30 = (bf16[2,2,64,256]{3,2,1,0:T(8,128)(2,1)S(1)}, bf16[2,2,64,256]{3,2,1,0:T(8,128)(2,1)S(1)}, u32[]{:S(2)}, u32[]{:S(2)}) collective-permute-start(bf16[2,2,64,256]{3,2,1,0:T(8,128)(2,1)S(1)} %fusion.6.rest_0_), channel_id=1, source_target_pairs={{0,8},{4,12},{8,0},{12,4},{1,9},{5,13},{9,1},{13,5},{2,10},{6,14},... | collective-permute-start | bytes 393224 | tf_op jit(solution)/shard_map/ppermute | solution.py:384
  145.3 11.4 %collective-permute-start.31 = (bf16[2,2,64,256]{3,2,1,0:T(8,128)(2,1)S(1)}, bf16[2,2,64,256]{3,2,1,0:T(8,128)(2,1)S(1)}, u32[]{:S(2)}, u32[]{:S(2)}) collective-permute-start(bf16[2,2,64,256]{3,2,1,0:T(8,128)(2,1)S(1)} %fusion.6.rest_0_), channel_id=1, source_target_pairs={{0,12},{4,8},{8,4},{12,0},{1,13},{5,9},{9,5},{13,1},{2,14},{6,10},... | collective-permute-start | bytes 393224 | tf_op jit(solution)/shard_map/ppermute | solution.py:384
  (12 other events, 115.8 us)

commit v4 on v3

--- a/solution.py
+++ b/solution.py
@@ -12,7 +12,7 @@
 BLOCK = 128
 ITERS = 2
 ROWS = 8
-CHUNKS = 1
+CHUNKS = 2
 VMEM_BYTES = 16 * 1024 * 1024
 
 BF16 = jnp.bfloat16

time: 165 us -> 160 us (0.970)
  waiting for transfers between devices: 87.2 us -> 29.6 us
  starting transfers between devices: 40.6 us -> 82.2 us
  Pallas kernels: 16 us -> 24.3 us
  local copies, waits for them, and re-layouts: 11.7 us -> 15.1 us
    ppermute x32 -> x63, waiting for transfers between devices: 87.2 us -> 29.6 us  [exchanged(): lax.ppermute(value, axis, [(i, i ^ step) for i in range(lax.axis_size(axi...]
    ppermute x32 -> x63, starting transfers between devices: 40.6 us -> 82.2 us  [exchanged(): lax.ppermute(value, axis, [(i, i ^ step) for i in range(lax.axis_size(axi...]
    pallas_call x11 -> x20, Pallas kernels: 16 us -> 24.3 us  [call(): pl.pallas_call(body, grid_spec=pltpu.PrefetchScalarGridSpec(num_scalar_pr...]
    unnamed x25 -> x43, local copies, waits for them, and re-layouts: 11.7 us -> 15.1 us
  transfers between devices with their start and end apart: 32 -> 63, of which waited for: 20 -> 18; matrix products, arithmetic and copies ran while one was open for 4% -> 5% of each run, Pallas kernels for 2% -> 13%
where the time goes in v4:
time: 160 us; the launch traced here: 159 us
  starting transfers between devices  82.2 us (51%)
  waiting for transfers between devices  29.6 us (18%)
  Pallas kernels  24.3 us (15%)
  local copies, waits for them, and re-layouts  15.1 us (9%)
  other arithmetic  7.2 us (4%)
    ppermute x63, starting transfers between devices, exchanged(): lax.ppermute(value, axis, [(i, i ^ step) for i in range(lax.axis_size(axi...  82.2 us
    ppermute x63, waiting for transfers between devices, exchanged(): lax.ppermute(value, axis, [(i, i ^ step) for i in range(lax.axis_size(axi...  29.6 us
    pallas_call x20, Pallas kernels, call(): pl.pallas_call(body, grid_spec=pltpu.PrefetchScalarGridSpec(num_scalar_pr...  24.3 us
    unnamed x43, local copies, waits for them, and re-layouts  15.1 us
    sin x2, other arithmetic, phases(): return (jnp.cos(angle), jnp.sin(angle), onset.astype(F32) * (1.0 / samples))  4.2 us
  transfers between devices with their start and end apart: 63, of which 18 were waited for; matrix products, arithmetic and copies ran while one was open for 5% of the time, Pallas kernels for 13%

profile of v4, /device:TPU:0, one launch (start us, length us, event | category | flops | bytes accessed | tf_op | source)
XLA Modules:
  0.0 158.9 jit_solution(8430342813079476737)
XLA Ops:
  3.5 3.0 %collective-permute-start = (bf16[2,2,512,256]{3,2,1,0:T(8,128)(2,1)S(1)}, bf16[2,2,512,256]{3,2,1,0:T(8,128)(2,1)S(1)}, u32[]{:S(2)}, u32[]{:S(2)}) collective-permute-start(bf16[2,2,512,256]{3,2,1,0:T(8,128)(2,1)S(1)} %shard_map.83), channel_id=1, source_target_pairs={{0,2},{2,0},{1,3},{3,1},{4,6},{6,4},{5,7},{7,5},{8,10},{10,8},{9,1... | collective-permute-start | bytes 3145736 | tf_op jit(solution)/shard_map/ppermute | solution.py:384
  6.5 2.2 %copy-done = bf16[64,128,256]{2,1,0:T(8,128)(2,1)S(1)} copy-done((bf16[64,128,256]{2,1,0:T(8,128)(2,1)S(1)}, bf16[64,128,256]{2,1,0:T(8,128)(2,1)}, u32[]{:S(2)}) %copy-start) | copy-done | bytes 4194328
  12.2 2.6 %collective-permute-start.33 = (bf16[2,2,32,256]{3,2,1,0:T(8,128)(2,1)S(1)}, bf16[2,2,32,256]{3,2,1,0:T(8,128)(2,1)S(1)}, u32[]{:S(2)}, u32[]{:S(2)}) collective-permute-start(bf16[2,2,32,256]{3,2,1,0:T(8,128)(2,1)S(1)} %get-tuple-element.79), channel_id=1, source_target_pairs={{0,8},{4,12},{8,0},{12,4},{1,9},{5,13},{9,1},{13,5},{2,10},{6,14},... | collective-permute-start | bytes 196616 | tf_op jit(solution)/shard_map/ppermute | solution.py:384
  16.5 3.5 %collective-permute-start.2 = (bf16[2,2,32,256]{3,2,1,0:T(8,128)(2,1)S(1)}, bf16[2,2,32,256]{3,2,1,0:T(8,128)(2,1)S(1)}, u32[]{:S(2)}, u32[]{:S(2)}) collective-permute-start(bf16[2,2,32,256]{3,2,1,0:T(8,128)(2,1)S(1)} %get-tuple-element.55), channel_id=1, source_target_pairs={{0,8},{4,12},{8,0},{12,4},{1,9},{5,13},{9,1},{13,5},{2,10},{6,14},... | collective-permute-start | bytes 196616 | tf_op jit(solution)/shard_map/ppermute | solution.py:384
  20.0 2.8 %collective-permute-start.3 = (bf16[2,2,32,256]{3,2,1,0:T(8,128)(2,1)S(1)}, bf16[2,2,32,256]{3,2,1,0:T(8,128)(2,1)S(1)}, u32[]{:S(2)}, u32[]{:S(2)}) collective-permute-start(bf16[2,2,32,256]{3,2,1,0:T(8,128)(2,1)S(1)} %get-tuple-element.56), channel_id=1, source_target_pairs={{0,12},{4,8},{8,4},{12,0},{1,13},{5,9},{9,5},{13,1},{2,14},{6,10},... | collective-permute-start | bytes 196616 | tf_op jit(solution)/shard_map/ppermute | solution.py:384
  27.9 3.8 %collective-permute-done.36.f0 = bf16[2,2,32,256]{3,2,1,0:T(8,128)(2,1)S(1)} collective-permute-done((bf16[2,2,32,256]{3,2,1,0:T(8,128)(2,1)S(1)}, bf16[2,2,32,256]{3,2,1,0:T(8,128)(2,1)S(1)}, u32[]{:S(2)}, u32[]{:S(2)}) %collective-permute-start.36) | collective-permute-done | bytes 65568 | tf_op jit(solution)/shard_map/ppermute | solution.py:384
  41.8 2.8 %collective-permute-start.39 = (bf16[2,2,16,512]{3,2,1,0:T(8,128)(2,1)S(1)}, bf16[2,2,16,512]{3,2,1,0:T(8,128)(2,1)S(1)}, u32[]{:S(2)}, u32[]{:S(2)}) collective-permute-start(bf16[2,2,16,512]{3,2,1,0:T(8,128)(2,1)S(1)} %get-tuple-element.83), channel_id=1, source_target_pairs={{0,8},{4,12},{8,0},{12,4},{1,9},{5,13},{9,1},{13,5},{2,10},{6,14},... | collective-permute-start | bytes 196616 | tf_op jit(solution)/shard_map/ppermute | solution.py:384
  46.0 2.1 %fusion.20 = (f32[4,2,16,512]{3,2,1,0:T(8,128)S(1)}, f32[4,2,16,512]{3,2,1,0:T(8,128)S(1)}, f32[4,2,16,512]{3,2,1,0:T(8,128)S(1)}, f32[4,2,16,512]{3,2,1,0:T(8,128)S(1)}) fusion(s32[16,512]{1,0:T(8,128)S(1)} %get-tuple-element.106, s32[4,2]{1,0:T(4,128)S(1)} %add_add_fusion, s32[16,512]{1,0:T(8,128)S(1)} %get-tuple-element.114), kind=kLoop, calls=%fused_computation.50 | loop fusion | flops 1835008 | bytes 1114144 | tf_op jit(solution)/shard_map/sin | solution.py:407
  50.8 2.1 %shard_map.94 = (bf16[2,2,16,512]{3,2,1,0:T(8,128)(2,1)S(1)}, bf16[2,2,16,512]{3,2,1,0:T(8,128)(2,1)}, bf16[2,2,16,512]{3,2,1,0:T(8,128)(2,1)}, bf16[2,2,16,512]{3,2,1,0:T(8,128)(2,1)}) custom-call(s32[1]{0:T(128)} %bitcast.place_ref, f32[4,2,16,512]{3,2,1,0:T(8,128)S(1)} %get-tuple-element.120.c_ref, f32[4,2,16,512]{3,2,1,0:T(8,128)S(1)} %get-tuple-element.119.s_ref, ...), custom_call_target="tpu_custom_call" | custom-call | flops 67108864 | bytes 1212416 | tf_op jit(solution)/shard_map/pallas_call | solution.py:84
  53.5 4.1 %collective-permute-start.41 = (bf16[2,2,16,512]{3,2,1,0:T(8,128)(2,1)}, bf16[2,2,16,512]{3,2,1,0:T(8,128)(2,1)}, u32[]{:S(2)}, u32[]{:S(2)}) collective-permute-start(bf16[2,2,16,512]{3,2,1,0:T(8,128)(2,1)} %get-tuple-element.86), channel_id=1, source_target_pairs={{0,4},{4,0},{8,12},{12,8},{1,5},{5,1},{9,13},{13,9},{2,6},{6,2},{1... | collective-permute-start | bytes 196616 | tf_op jit(solution)/shard_map/ppermute | solution.py:384
  57.6 2.0 %collective-permute-start.42 = (bf16[2,2,16,512]{3,2,1,0:T(8,128)(2,1)}, bf16[2,2,16,512]{3,2,1,0:T(8,128)(2,1)}, u32[]{:S(2)}, u32[]{:S(2)}) collective-permute-start(bf16[2,2,16,512]{3,2,1,0:T(8,128)(2,1)} %get-tuple-element.87), channel_id=1, source_target_pairs={{0,8},{4,12},{8,0},{12,4},{1,9},{5,13},{9,1},{13,5},{2,10},{6,14},... | collective-permute-start | bytes 196616 | tf_op jit(solution)/shard_map/ppermute | solution.py:384
  63.2 2.3 %shard_map.86 = (bf16[2,2,16,512]{3,2,1,0:T(8,128)(2,1)S(1)}, bf16[2,2,16,512]{3,2,1,0:T(8,128)(2,1)S(1)}, bf16[2,2,16,512]{3,2,1,0:T(8,128)(2,1)S(1)}, bf16[2,2,16,512]{3,2,1,0:T(8,128)(2,1)S(1)}) custom-call(s32[1]{0:T(128)} %bitcast.place_ref, f32[4,2,16,512]{3,2,1,0:T(8,128)S(1)} %get-tuple-element.127.c_ref, ...), custom_call_target="tpu_custom_call" | custom-call | flops 67108864 | bytes 1212416 | tf_op jit(solution)/shard_map/pallas_call | solution.py:84
  66.1 2.4 %collective-permute-start.11 = (bf16[2,2,16,512]{3,2,1,0:T(8,128)(2,1)S(1)}, bf16[2,2,16,512]{3,2,1,0:T(8,128)(2,1)S(1)}, u32[]{:S(2)}, u32[]{:S(2)}) collective-permute-start(bf16[2,2,16,512]{3,2,1,0:T(8,128)(2,1)S(1)} %get-tuple-element.63), channel_id=1, source_target_pairs={{0,8},{4,12},{8,0},{12,4},{1,9},{5,13},{9,1},{13,5},{2,10},{6,14},... | collective-permute-start | bytes 196616 | tf_op jit(solution)/shard_map/ppermute | solution.py:384
  72.5 2.1 %collective-permute-done.12.rest_3_ = bf16[2,2,16,512]{3,2,1,0:T(8,128)(2,1)S(1)} collective-permute-done((bf16[2,2,16,512]{3,2,1,0:T(8,128)(2,1)S(1)}, bf16[2,2,16,512]{3,2,1,0:T(8,128)(2,1)S(1)}, u32[]{:S(2)}, u32[]{:S(2)}) %collective-permute-start.12) | collective-permute-done | bytes 65568 | tf_op jit(solution)/shard_map/ppermute | solution.py:384
  81.8 2.8 %collective-permute-start.46 = (bf16[2,2,32,256]{3,2,1,0:T(8,128)(2,1)S(1)}, bf16[2,2,32,256]{3,2,1,0:T(8,128)(2,1)S(1)}, u32[]{:S(2)}, u32[]{:S(2)}) collective-permute-start(bf16[2,2,32,256]{3,2,1,0:T(8,128)(2,1)S(1)} %fusion.13.rest_0_), channel_id=1, source_target_pairs={{0,4},{4,0},{8,12},{12,8},{1,5},{5,1},{9,13},{13,9},{2,6},{6,2},{1... | collective-permute-start | bytes 196616 | tf_op jit(solution)/shard_map/ppermute | solution.py:384
  84.6 2.1 %fusion.16 = (f32[4,2,32,256]{3,2,1,0:T(8,128)S(1)}, f32[4,2,32,256]{3,2,1,0:T(8,128)S(1)}, f32[4,2,32,256]{3,2,1,0:T(8,128)S(1)}, f32[4,2,32,256]{3,2,1,0:T(8,128)S(1)}) fusion(s32[32,256]{1,0:T(8,128)S(1)} %get-tuple-element.104, s32[4,2]{1,0:T(4,128)S(1)} %add_add_fusion, s32[32,256]{1,0:T(8,128)S(1)} %get-tuple-element.116), kind=kLoop, calls=%fused_computation.45 | loop fusion | flops 1835008 | bytes 1114144 | tf_op jit(solution)/shard_map/sin | solution.py:407
  91.4 2.3 %collective-permute-start.17 = (bf16[2,2,32,256]{3,2,1,0:T(8,128)(2,1)S(1)}, bf16[2,2,32,256]{3,2,1,0:T(8,128)(2,1)S(1)}, u32[]{:S(2)}, u32[]{:S(2)}) collective-permute-start(bf16[2,2,32,256]{3,2,1,0:T(8,128)(2,1)S(1)} %fusion.15.rest_0_), channel_id=1, source_target_pairs={{0,12},{4,8},{8,4},{12,0},{1,13},{5,9},{9,5},{13,1},{2,14},{6,10},... | collective-permute-start | bytes 196616 | tf_op jit(solution)/shard_map/ppermute | solution.py:384
  93.8 2.1 %collective-permute-start.15 = (bf16[2,2,32,256]{3,2,1,0:T(8,128)(2,1)S(1)}, bf16[2,2,32,256]{3,2,1,0:T(8,128)(2,1)S(1)}, u32[]{:S(2)}, u32[]{:S(2)}) collective-permute-start(bf16[2,2,32,256]{3,2,1,0:T(8,128)(2,1)S(1)} %fusion.15.rest_0_), channel_id=1, source_target_pairs={{0,4},{4,0},{8,12},{12,8},{1,5},{5,1},{9,13},{13,9},{2,6},{6,2},{1... | collective-permute-start | bytes 196616 | tf_op jit(solution)/shard_map/ppermute | solution.py:384
  102.6 2.0 %collective-permute-start.53 = (bf16[2,2,16,512]{3,2,1,0:T(8,128)(2,1)S(1)}, bf16[2,2,16,512]{3,2,1,0:T(8,128)(2,1)S(1)}, u32[]{:S(2)}, u32[]{:S(2)}) collective-permute-start(bf16[2,2,16,512]{3,2,1,0:T(8,128)(2,1)S(1)} %get-tuple-element.93), channel_id=1, source_target_pairs={{0,8},{4,12},{8,0},{12,4},{1,9},{5,13},{9,1},{13,5},{2,10},{6,14},... | collective-permute-start | bytes 196616 | tf_op jit(solution)/shard_map/ppermute | solution.py:384
  104.6 2.1 %collective-permute-start.54 = (bf16[2,2,16,512]{3,2,1,0:T(8,128)(2,1)S(1)}, bf16[2,2,16,512]{3,2,1,0:T(8,128)(2,1)S(1)}, u32[]{:S(2)}, u32[]{:S(2)}) collective-permute-start(bf16[2,2,16,512]{3,2,1,0:T(8,128)(2,1)S(1)} %get-tuple-element.94), channel_id=1, source_target_pairs={{0,12},{4,8},{8,4},{12,0},{1,13},{5,9},{9,5},{13,1},{2,14},{6,10},... | collective-permute-start | bytes 196616 | tf_op jit(solution)/shard_map/ppermute | solution.py:384
  107.2 2.5 %collective-permute-done.53.rest_2_ = bf16[2,2,16,512]{3,2,1,0:T(8,128)(2,1)S(1)} collective-permute-done((bf16[2,2,16,512]{3,2,1,0:T(8,128)(2,1)S(1)}, bf16[2,2,16,512]{3,2,1,0:T(8,128)(2,1)S(1)}, u32[]{:S(2)}, u32[]{:S(2)}) %collective-permute-start.53) | collective-permute-done | bytes 65568 | tf_op jit(solution)/shard_map/ppermute | solution.py:384
  117.8 2.6 %collective-permute-start.22 = (bf16[2,2,16,512]{3,2,1,0:T(8,128)(2,1)S(1)}, bf16[2,2,16,512]{3,2,1,0:T(8,128)(2,1)S(1)}, u32[]{:S(2)}, u32[]{:S(2)}) collective-permute-start(bf16[2,2,16,512]{3,2,1,0:T(8,128)(2,1)S(1)} %get-tuple-element.69), channel_id=1, source_target_pairs={{0,8},{4,12},{8,0},{12,4},{1,9},{5,13},{9,1},{13,5},{2,10},{6,14},... | collective-permute-start | bytes 196616 | tf_op jit(solution)/shard_map/ppermute | solution.py:384
  127.6 2.3 %collective-permute-start.25 = (bf16[2,2,16,512]{3,2,1,0:T(8,128)(2,1)S(1)}, bf16[2,2,16,512]{3,2,1,0:T(8,128)(2,1)S(1)}, u32[]{:S(2)}, u32[]{:S(2)}) collective-permute-start(bf16[2,2,16,512]{3,2,1,0:T(8,128)(2,1)S(1)} %get-tuple-element.73), channel_id=1, source_target_pairs={{0,8},{4,12},{8,0},{12,4},{1,9},{5,13},{9,1},{13,5},{2,10},{6,14},... | collective-permute-start | bytes 196616 | tf_op jit(solution)/shard_map/ppermute | solution.py:384
  129.9 2.1 %collective-permute-start.26 = (bf16[2,2,16,512]{3,2,1,0:T(8,128)(2,1)S(1)}, bf16[2,2,16,512]{3,2,1,0:T(8,128)(2,1)S(1)}, u32[]{:S(2)}, u32[]{:S(2)}) collective-permute-start(bf16[2,2,16,512]{3,2,1,0:T(8,128)(2,1)S(1)} %get-tuple-element.74), channel_id=1, source_target_pairs={{0,12},{4,8},{8,4},{12,0},{1,13},{5,9},{9,5},{13,1},{2,14},{6,10},... | collective-permute-start | bytes 196616 | tf_op jit(solution)/shard_map/ppermute | solution.py:384
  133.3 2.7 %collective-permute-done.26.rest_3_ = bf16[2,2,16,512]{3,2,1,0:T(8,128)(2,1)S(1)} collective-permute-done((bf16[2,2,16,512]{3,2,1,0:T(8,128)(2,1)S(1)}, bf16[2,2,16,512]{3,2,1,0:T(8,128)(2,1)S(1)}, u32[]{:S(2)}, u32[]{:S(2)}) %collective-permute-start.26) | collective-permute-done | bytes 65568 | tf_op jit(solution)/shard_map/ppermute | solution.py:384
  141.5 2.5 %collective-permute-start.62 = (bf16[2,2,32,256]{3,2,1,0:T(8,128)(2,1)S(1)}, bf16[2,2,32,256]{3,2,1,0:T(8,128)(2,1)S(1)}, u32[]{:S(2)}, u32[]{:S(2)}) collective-permute-start(bf16[2,2,32,256]{3,2,1,0:T(8,128)(2,1)S(1)} %fusion.12.rest_0_), channel_id=1, source_target_pairs={{0,12},{4,8},{8,4},{12,0},{1,13},{5,9},{9,5},{13,1},{2,14},{6,10},... | collective-permute-start | bytes 196616 | tf_op jit(solution)/shard_map/ppermute | solution.py:384
  144.0 2.0 %collective-permute-start.60 = (bf16[2,2,32,256]{3,2,1,0:T(8,128)(2,1)S(1)}, bf16[2,2,32,256]{3,2,1,0:T(8,128)(2,1)S(1)}, u32[]{:S(2)}, u32[]{:S(2)}) collective-permute-start(bf16[2,2,32,256]{3,2,1,0:T(8,128)(2,1)S(1)} %fusion.12.rest_0_), channel_id=1, source_target_pairs={{0,4},{4,0},{8,12},{12,8},{1,5},{5,1},{9,13},{13,9},{2,6},{6,2},{1... | collective-permute-start | bytes 196616 | tf_op jit(solution)/shard_map/ppermute | solution.py:384
  146.0 2.5 %collective-permute-start.31 = (bf16[2,2,32,256]{3,2,1,0:T(8,128)(2,1)S(1)}, bf16[2,2,32,256]{3,2,1,0:T(8,128)(2,1)S(1)}, u32[]{:S(2)}, u32[]{:S(2)}) collective-permute-start(bf16[2,2,32,256]{3,2,1,0:T(8,128)(2,1)S(1)} %fusion.14.rest_0_), channel_id=1, source_target_pairs={{0,12},{4,8},{8,4},{12,0},{1,13},{5,9},{9,5},{13,1},{2,14},{6,10},... | collective-permute-start | bytes 196616 | tf_op jit(solution)/shard_map/ppermute | solution.py:384
  148.5 2.0 %collective-permute-start.29 = (bf16[2,2,32,256]{3,2,1,0:T(8,128)(2,1)S(1)}, bf16[2,2,32,256]{3,2,1,0:T(8,128)(2,1)S(1)}, u32[]{:S(2)}, u32[]{:S(2)}) collective-permute-start(bf16[2,2,32,256]{3,2,1,0:T(8,128)(2,1)S(1)} %fusion.14.rest_0_), channel_id=1, source_target_pairs={{0,4},{4,0},{8,12},{12,8},{1,5},{5,1},{9,13},{13,9},{2,6},{6,2},{1... | collective-permute-start | bytes 196616 | tf_op jit(solution)/shard_map/ppermute | solution.py:384
  151.9 2.2 %copy-done.1 = bf16[64,128,256]{2,1,0:T(8,128)(2,1)S(1)} copy-done((bf16[64,128,256]{2,1,0:T(8,128)(2,1)S(1)}, bf16[64,128,256]{2,1,0:T(8,128)(2,1)}, u32[]{:S(2)}) %copy-start.1) | copy-done | bytes 4194328
  155.0 1.9 %shard_map.100.rest_4_ = bf16[64,128,256]{2,1,0:T(8,128)(2,1)} custom-call(s32[1]{0:T(128)} %bitcast.place_ref, s32[1]{0:T(128)} %bitcast.1._, bf16[64,128,256]{2,1,0:T(8,128)(2,1)S(1)} %copy-done.1, s32[128,256]{1,0:T(8,128)S(1)} %copy-done.10, bf16[4,1024,128]{2,1,0:T(8,128)(2,1)S(1)} %copy-done.5, bf16[2,2,32,256]{3,2,1,0:T(8,128)(2,1)S(1)} %fusion.12.rest_0_, ...), custom_call_target="tpu_custom_call" | custom-call | flops 33554432 | bytes 9830400 | tf_op jit(solution)/shard_map/pallas_call | solution.py:84
  156.9 2.0 %shard_map.101 = bf16[64,128,256]{2,1,0:T(8,128)(2,1)} custom-call(s32[1]{0:T(128)} %bitcast.place_ref, s32[1]{0:T(128)} %bitcast.1._, bf16[64,128,256]{2,1,0:T(8,128)(2,1)S(1)} %copy-done.1, s32[128,256]{1,0:T(8,128)S(1)} %copy-done.10, bf16[4,1024,128]{2,1,0:T(8,128)(2,1)S(1)} %copy-done.5, ...), custom_call_target="tpu_custom_call", output_to_operand_aliasing={{}: (9, {})} | custom-call | flops 33554432 | bytes 14024704 | tf_op jit(solution)/shard_map/pallas_call | solution.py:84
  (173 shorter events, 80.0 us)
Async XLA Ops:
  3.5 33.1 %collective-permute-start = (bf16[2,2,512,256]{3,2,1,0:T(8,128)(2,1)S(1)}, bf16[2,2,512,256]{3,2,1,0:T(8,128)(2,1)S(1)}, u32[]{:S(2)}, u32[]{:S(2)}) collective-permute-start(bf16[2,2,512,256]{3,2,1,0:T(8,128)(2,1)S(1)} %shard_map.83), channel_id=1, source_target_pairs={{0,2},{2,0},{1,3},{3,1},{4,6},{6,4},{5,7},{7,5},{8,10},{10,8},{9,1... | collective-permute-start | bytes 3145736 | tf_op jit(solution)/shard_map/ppermute | solution.py:384
  12.2 7.7 %collective-permute-start.33 = (bf16[2,2,32,256]{3,2,1,0:T(8,128)(2,1)S(1)}, bf16[2,2,32,256]{3,2,1,0:T(8,128)(2,1)S(1)}, u32[]{:S(2)}, u32[]{:S(2)}) collective-permute-start(bf16[2,2,32,256]{3,2,1,0:T(8,128)(2,1)S(1)} %get-tuple-element.79), channel_id=1, source_target_pairs={{0,8},{4,12},{8,0},{12,4},{1,9},{5,13},{9,1},{13,5},{2,10},{6,14},... | collective-permute-start | bytes 196616 | tf_op jit(solution)/shard_map/ppermute | solution.py:384
  14.8 8.0 %collective-permute-start.34 = (bf16[2,2,32,256]{3,2,1,0:T(8,128)(2,1)S(1)}, bf16[2,2,32,256]{3,2,1,0:T(8,128)(2,1)S(1)}, u32[]{:S(2)}, u32[]{:S(2)}) collective-permute-start(bf16[2,2,32,256]{3,2,1,0:T(8,128)(2,1)S(1)} %get-tuple-element.80), channel_id=1, source_target_pairs={{0,12},{4,8},{8,4},{12,0},{1,13},{5,9},{9,5},{13,1},{2,14},{6,10},... | collective-permute-start | bytes 196616 | tf_op jit(solution)/shard_map/ppermute | solution.py:384
  15.7 8.3 %collective-permute-start.1 = (bf16[2,2,32,256]{3,2,1,0:T(8,128)(2,1)S(1)}, bf16[2,2,32,256]{3,2,1,0:T(8,128)(2,1)S(1)}, u32[]{:S(2)}, u32[]{:S(2)}) collective-permute-start(bf16[2,2,32,256]{3,2,1,0:T(8,128)(2,1)S(1)} %get-tuple-element.54), channel_id=1, source_target_pairs={{0,4},{4,0},{8,12},{12,8},{1,5},{5,1},{9,13},{13,9},{2,6},{6,2},{1... | collective-permute-start | bytes 196616 | tf_op jit(solution)/shard_map/ppermute | solution.py:384
  16.5 8.3 %collective-permute-start.2 = (bf16[2,2,32,256]{3,2,1,0:T(8,128)(2,1)S(1)}, bf16[2,2,32,256]{3,2,1,0:T(8,128)(2,1)S(1)}, u32[]{:S(2)}, u32[]{:S(2)}) collective-permute-start(bf16[2,2,32,256]{3,2,1,0:T(8,128)(2,1)S(1)} %get-tuple-element.55), channel_id=1, source_target_pairs={{0,8},{4,12},{8,0},{12,4},{1,9},{5,13},{9,1},{13,5},{2,10},{6,14},... | collective-permute-start | bytes 196616 | tf_op jit(solution)/shard_map/ppermute | solution.py:384
  23.5 8.3 %collective-permute-start.36 = (bf16[2,2,32,256]{3,2,1,0:T(8,128)(2,1)S(1)}, bf16[2,2,32,256]{3,2,1,0:T(8,128)(2,1)S(1)}, u32[]{:S(2)}, u32[]{:S(2)}) collective-permute-start(bf16[2,2,32,256]{3,2,1,0:T(8,128)(2,1)S(1)} %get-tuple-element.101.n0), channel_id=1, source_target_pairs={{0,2},{2,0},{1,3},{3,1},{4,6},{6,4},{5,7},{7,5},{8,10},{10,8},{9,1... | collective-permute-start | bytes 196616 | tf_op jit(solution)/shard_map/ppermute | solution.py:384
  27.4 12.9 %collective-permute-start.35 = (bf16[2,2,32,256]{3,2,1,0:T(8,128)(2,1)S(1)}, bf16[2,2,32,256]{3,2,1,0:T(8,128)(2,1)S(1)}, u32[]{:S(2)}, u32[]{:S(2)}) collective-permute-start(bf16[2,2,32,256]{3,2,1,0:T(8,128)(2,1)S(1)} %get-tuple-element.101.n0), channel_id=1, source_target_pairs={{0,1},{1,0},{2,3},{3,2},{4,5},{5,4},{6,7},{7,6},{8,9},{9,8},{10,11... | collective-permute-start | bytes 196616 | tf_op jit(solution)/shard_map/ppermute | solution.py:384
  27.4 9.2 %collective-permute-start.4 = (bf16[2,2,32,256]{3,2,1,0:T(8,128)(2,1)S(1)}, bf16[2,2,32,256]{3,2,1,0:T(8,128)(2,1)S(1)}, u32[]{:S(2)}, u32[]{:S(2)}) collective-permute-start(bf16[2,2,32,256]{3,2,1,0:T(8,128)(2,1)S(1)} %get-tuple-element.107.n0), channel_id=1, source_target_pairs={{0,1},{1,0},{2,3},{3,2},{4,5},{5,4},{6,7},{7,6},{8,9},{9,8},{10,11... | collective-permute-start | bytes 196616 | tf_op jit(solution)/shard_map/ppermute | solution.py:384
  31.8 8.5 %collective-permute-start.37 = (bf16[2,2,32,256]{3,2,1,0:T(8,128)(2,1)S(1)}, bf16[2,2,32,256]{3,2,1,0:T(8,128)(2,1)S(1)}, u32[]{:S(2)}, u32[]{:S(2)}) collective-permute-start(bf16[2,2,32,256]{3,2,1,0:T(8,128)(2,1)S(1)} %collective-permute-done.36.f0), channel_id=1, source_target_pairs={{0,1},{1,0},{2,3},{3,2},{4,5},{5,4},{6,7},{7,6},{8,9},{9,8},{10,11... | collective-permute-start | bytes 196616 | tf_op jit(solution)/shard_map/ppermute | solution.py:384
  38.5 21.0 %collective-permute-start.7 = (bf16[2,2,16,512]{3,2,1,0:T(8,128)(2,1)S(1)}, bf16[2,2,16,512]{3,2,1,0:T(8,128)(2,1)S(1)}, u32[]{:S(2)}, u32[]{:S(2)}) collective-permute-start(bf16[2,2,16,512]{3,2,1,0:T(8,128)(2,1)S(1)} %get-tuple-element.58), channel_id=1, source_target_pairs={{0,4},{4,0},{8,12},{12,8},{1,5},{5,1},{9,13},{13,9},{2,6},{6,2},{1... | collective-permute-start | bytes 196616 | tf_op jit(solution)/shard_map/ppermute | solution.py:384
  41.5 8.3 %collective-permute-start.38 = (bf16[2,2,16,512]{3,2,1,0:T(8,128)(2,1)S(1)}, bf16[2,2,16,512]{3,2,1,0:T(8,128)(2,1)S(1)}, u32[]{:S(2)}, u32[]{:S(2)}) collective-permute-start(bf16[2,2,16,512]{3,2,1,0:T(8,128)(2,1)S(1)} %get-tuple-element.82), channel_id=1, source_target_pairs={{0,4},{4,0},{8,12},{12,8},{1,5},{5,1},{9,13},{13,9},{2,6},{6,2},{1... | collective-permute-start | bytes 196616 | tf_op jit(solution)/shard_map/ppermute | solution.py:384
  41.8 9.0 %collective-permute-start.39 = (bf16[2,2,16,512]{3,2,1,0:T(8,128)(2,1)S(1)}, bf16[2,2,16,512]{3,2,1,0:T(8,128)(2,1)S(1)}, u32[]{:S(2)}, u32[]{:S(2)}) collective-permute-start(bf16[2,2,16,512]{3,2,1,0:T(8,128)(2,1)S(1)} %get-tuple-element.83), channel_id=1, source_target_pairs={{0,8},{4,12},{8,0},{12,4},{1,9},{5,13},{9,1},{13,5},{2,10},{6,14},... | collective-permute-start | bytes 196616 | tf_op jit(solution)/shard_map/ppermute | solution.py:384
  48.1 13.5 %collective-permute-start.8 = (bf16[2,2,16,512]{3,2,1,0:T(8,128)(2,1)}, bf16[2,2,16,512]{3,2,1,0:T(8,128)(2,1)}, u32[]{:S(2)}, u32[]{:S(2)}) collective-permute-start(bf16[2,2,16,512]{3,2,1,0:T(8,128)(2,1)} %get-tuple-element.59), channel_id=1, source_target_pairs={{0,8},{4,12},{8,0},{12,4},{1,9},{5,13},{9,1},{13,5},{2,10},{6,14},... | collective-permute-start | bytes 196616 | tf_op jit(solution)/shard_map/ppermute | solution.py:384
  49.9 11.7 %collective-permute-start.9 = (bf16[2,2,16,512]{3,2,1,0:T(8,128)(2,1)}, bf16[2,2,16,512]{3,2,1,0:T(8,128)(2,1)}, u32[]{:S(2)}, u32[]{:S(2)}) collective-permute-start(bf16[2,2,16,512]{3,2,1,0:T(8,128)(2,1)} %get-tuple-element.60), channel_id=1, source_target_pairs={{0,12},{4,8},{8,4},{12,0},{1,13},{5,9},{9,5},{13,1},{2,14},{6,10},... | collective-permute-start | bytes 196616 | tf_op jit(solution)/shard_map/ppermute | solution.py:384
  53.5 15.0 %collective-permute-start.41 = (bf16[2,2,16,512]{3,2,1,0:T(8,128)(2,1)}, bf16[2,2,16,512]{3,2,1,0:T(8,128)(2,1)}, u32[]{:S(2)}, u32[]{:S(2)}) collective-permute-start(bf16[2,2,16,512]{3,2,1,0:T(8,128)(2,1)} %get-tuple-element.86), channel_id=1, source_target_pairs={{0,4},{4,0},{8,12},{12,8},{1,5},{5,1},{9,13},{13,9},{2,6},{6,2},{1... | collective-permute-start | bytes 196616 | tf_op jit(solution)/shard_map/ppermute | solution.py:384
  57.6 12.4 %collective-permute-start.42 = (bf16[2,2,16,512]{3,2,1,0:T(8,128)(2,1)}, bf16[2,2,16,512]{3,2,1,0:T(8,128)(2,1)}, u32[]{:S(2)}, u32[]{:S(2)}) collective-permute-start(bf16[2,2,16,512]{3,2,1,0:T(8,128)(2,1)} %get-tuple-element.87), channel_id=1, source_target_pairs={{0,8},{4,12},{8,0},{12,4},{1,9},{5,13},{9,1},{13,5},{2,10},{6,14},... | collective-permute-start | bytes 196616 | tf_op jit(solution)/shard_map/ppermute | solution.py:384
  60.1 9.8 %collective-permute-start.43 = (bf16[2,2,16,512]{3,2,1,0:T(8,128)(2,1)}, bf16[2,2,16,512]{3,2,1,0:T(8,128)(2,1)}, u32[]{:S(2)}, u32[]{:S(2)}) collective-permute-start(bf16[2,2,16,512]{3,2,1,0:T(8,128)(2,1)} %get-tuple-element.88), channel_id=1, source_target_pairs={{0,12},{4,8},{8,4},{12,0},{1,13},{5,9},{9,5},{13,1},{2,14},{6,10},... | collective-permute-start | bytes 196616 | tf_op jit(solution)/shard_map/ppermute | solution.py:384
  77.0 14.4 %collective-permute-start.14 = (bf16[2,2,32,256]{3,2,1,0:T(8,128)(2,1)S(1)}, bf16[2,2,32,256]{3,2,1,0:T(8,128)(2,1)S(1)}, u32[]{:S(2)}, u32[]{:S(2)}) collective-permute-start(bf16[2,2,32,256]{3,2,1,0:T(8,128)(2,1)S(1)} %fusion.24), channel_id=1, source_target_pairs={{0,2},{2,0},{1,3},{3,1},{4,6},{6,4},{5,7},{7,5},{8,10},{10,8},{9,1... | collective-permute-start | bytes 196616 | tf_op jit(solution)/shard_map/ppermute | solution.py:384
  102.6 7.1 %collective-permute-start.53 = (bf16[2,2,16,512]{3,2,1,0:T(8,128)(2,1)S(1)}, bf16[2,2,16,512]{3,2,1,0:T(8,128)(2,1)S(1)}, u32[]{:S(2)}, u32[]{:S(2)}) collective-permute-start(bf16[2,2,16,512]{3,2,1,0:T(8,128)(2,1)S(1)} %get-tuple-element.93), channel_id=1, source_target_pairs={{0,8},{4,12},{8,0},{12,4},{1,9},{5,13},{9,1},{13,5},{2,10},{6,14},... | collective-permute-start | bytes 196616 | tf_op jit(solution)/shard_map/ppermute | solution.py:384
  106.7 9.6 %collective-permute-start.18 = (bf16[2,2,32,256]{3,2,1,0:T(8,128)(2,1)S(1)}, bf16[2,2,32,256]{3,2,1,0:T(8,128)(2,1)S(1)}, u32[]{:S(2)}, u32[]{:S(2)}) collective-permute-start(bf16[2,2,32,256]{3,2,1,0:T(8,128)(2,1)S(1)} %shard_map.88.n0), channel_id=1, source_target_pairs={{0,1},{1,0},{2,3},{3,2},{4,5},{5,4},{6,7},{7,6},{8,9},{9,8},{10,11... | collective-permute-start | bytes 196616 | tf_op jit(solution)/shard_map/ppermute | solution.py:384
  106.7 9.6 %collective-permute-start.20 = (bf16[2,2,32,256]{3,2,1,0:T(8,128)(2,1)S(1)}, bf16[2,2,32,256]{3,2,1,0:T(8,128)(2,1)S(1)}, u32[]{:S(2)}, u32[]{:S(2)}) collective-permute-start(bf16[2,2,32,256]{3,2,1,0:T(8,128)(2,1)S(1)} %collective-permute-done.19.f0), channel_id=1, source_target_pairs={{0,1},{1,0},{2,3},{3,2},{4,5},{5,4},{6,7},{7,6},{8,9},{9,8},{10,11... | collective-permute-start | bytes 196616 | tf_op jit(solution)/shard_map/ppermute | solution.py:384
  111.9 8.6 %collective-permute-start.55 = (bf16[2,2,16,512]{3,2,1,0:T(8,128)(2,1)S(1)}, bf16[2,2,16,512]{3,2,1,0:T(8,128)(2,1)S(1)}, u32[]{:S(2)}, u32[]{:S(2)}) collective-permute-start(bf16[2,2,16,512]{3,2,1,0:T(8,128)(2,1)S(1)} %get-tuple-element.96), channel_id=1, source_target_pairs={{0,4},{4,0},{8,12},{12,8},{1,5},{5,1},{9,13},{13,9},{2,6},{6,2},{1... | collective-permute-start | bytes 196616 | tf_op jit(solution)/shard_map/ppermute | solution.py:384
  112.8 9.3 %collective-permute-start.56 = (bf16[2,2,16,512]{3,2,1,0:T(8,128)(2,1)S(1)}, bf16[2,2,16,512]{3,2,1,0:T(8,128)(2,1)S(1)}, u32[]{:S(2)}, u32[]{:S(2)}) collective-permute-start(bf16[2,2,16,512]{3,2,1,0:T(8,128)(2,1)S(1)} %get-tuple-element.97), channel_id=1, source_target_pairs={{0,8},{4,12},{8,0},{12,4},{1,9},{5,13},{9,1},{13,5},{2,10},{6,14},... | collective-permute-start | bytes 196616 | tf_op jit(solution)/shard_map/ppermute | solution.py:384
  114.6 7.6 %collective-permute-start.57 = (bf16[2,2,16,512]{3,2,1,0:T(8,128)(2,1)S(1)}, bf16[2,2,16,512]{3,2,1,0:T(8,128)(2,1)S(1)}, u32[]{:S(2)}, u32[]{:S(2)}) collective-permute-start(bf16[2,2,16,512]{3,2,1,0:T(8,128)(2,1)S(1)} %get-tuple-element.98), channel_id=1, source_target_pairs={{0,12},{4,8},{8,4},{12,0},{1,13},{5,9},{9,5},{13,1},{2,14},{6,10},... | collective-permute-start | bytes 196616 | tf_op jit(solution)/shard_map/ppermute | solution.py:384
  122.9 13.9 %collective-permute-start.58 = (bf16[2,2,2,32,256]{4,3,2,1,0:T(8,128)(2,1)S(1)}, bf16[2,2,2,32,256]{4,3,2,1,0:T(8,128)(2,1)S(1)}, u32[]{:S(2)}, u32[]{:S(2)}) collective-permute-start(bf16[2,2,2,32,256]{4,3,2,1,0:T(8,128)(2,1)S(1)} %get-tuple-element.100), channel_id=1, source_target_pairs={{0,1},{1,0},{2,3},{3,2},{4,5},{5,4},{6,7},{7,6},{8,9},{9,8},{10,11... | collective-permute-start | bytes 393224 | tf_op jit(solution)/shard_map/ppermute | solution.py:384
  138.4 7.5 %collective-permute-start.28 = (bf16[2,2,32,256]{3,2,1,0:T(8,128)(2,1)S(1)}, bf16[2,2,32,256]{3,2,1,0:T(8,128)(2,1)S(1)}, u32[]{:S(2)}, u32[]{:S(2)}) collective-permute-start(bf16[2,2,32,256]{3,2,1,0:T(8,128)(2,1)S(1)} %fusion.25), channel_id=1, source_target_pairs={{0,2},{2,0},{1,3},{3,1},{4,6},{6,4},{5,7},{7,5},{8,10},{10,8},{9,1... | collective-permute-start | bytes 196616 | tf_op jit(solution)/shard_map/ppermute | solution.py:384
  141.5 7.0 %collective-permute-start.62 = (bf16[2,2,32,256]{3,2,1,0:T(8,128)(2,1)S(1)}, bf16[2,2,32,256]{3,2,1,0:T(8,128)(2,1)S(1)}, u32[]{:S(2)}, u32[]{:S(2)}) collective-permute-start(bf16[2,2,32,256]{3,2,1,0:T(8,128)(2,1)S(1)} %fusion.12.rest_0_), channel_id=1, source_target_pairs={{0,12},{4,8},{8,4},{12,0},{1,13},{5,9},{9,5},{13,1},{2,14},{6,10},... | collective-permute-start | bytes 196616 | tf_op jit(solution)/shard_map/ppermute | solution.py:384
  144.0 7.9 %collective-permute-start.61 = (bf16[2,2,32,256]{3,2,1,0:T(8,128)(2,1)S(1)}, bf16[2,2,32,256]{3,2,1,0:T(8,128)(2,1)S(1)}, u32[]{:S(2)}, u32[]{:S(2)}) collective-permute-start(bf16[2,2,32,256]{3,2,1,0:T(8,128)(2,1)S(1)} %fusion.12.rest_0_), channel_id=1, source_target_pairs={{0,8},{4,12},{8,0},{12,4},{1,9},{5,13},{9,1},{13,5},{2,10},{6,14},... | collective-permute-start | bytes 196616 | tf_op jit(solution)/shard_map/ppermute | solution.py:384
  144.0 7.9 %collective-permute-start.60 = (bf16[2,2,32,256]{3,2,1,0:T(8,128)(2,1)S(1)}, bf16[2,2,32,256]{3,2,1,0:T(8,128)(2,1)S(1)}, u32[]{:S(2)}, u32[]{:S(2)}) collective-permute-start(bf16[2,2,32,256]{3,2,1,0:T(8,128)(2,1)S(1)} %fusion.12.rest_0_), channel_id=1, source_target_pairs={{0,4},{4,0},{8,12},{12,8},{1,5},{5,1},{9,13},{13,9},{2,6},{6,2},{1... | collective-permute-start | bytes 196616 | tf_op jit(solution)/shard_map/ppermute | solution.py:384
  146.0 10.9 %collective-permute-start.31 = (bf16[2,2,32,256]{3,2,1,0:T(8,128)(2,1)S(1)}, bf16[2,2,32,256]{3,2,1,0:T(8,128)(2,1)S(1)}, u32[]{:S(2)}, u32[]{:S(2)}) collective-permute-start(bf16[2,2,32,256]{3,2,1,0:T(8,128)(2,1)S(1)} %fusion.14.rest_0_), channel_id=1, source_target_pairs={{0,12},{4,8},{8,4},{12,0},{1,13},{5,9},{9,5},{13,1},{2,14},{6,10},... | collective-permute-start | bytes 196616 | tf_op jit(solution)/shard_map/ppermute | solution.py:384
  148.5 8.4 %collective-permute-start.30 = (bf16[2,2,32,256]{3,2,1,0:T(8,128)(2,1)S(1)}, bf16[2,2,32,256]{3,2,1,0:T(8,128)(2,1)S(1)}, u32[]{:S(2)}, u32[]{:S(2)}) collective-permute-start(bf16[2,2,32,256]{3,2,1,0:T(8,128)(2,1)S(1)} %fusion.14.rest_0_), channel_id=1, source_target_pairs={{0,8},{4,12},{8,0},{12,4},{1,9},{5,13},{9,1},{13,5},{2,10},{6,14},... | collective-permute-start | bytes 196616 | tf_op jit(solution)/shard_map/ppermute | solution.py:384
  148.5 8.4 %collective-permute-start.29 = (bf16[2,2,32,256]{3,2,1,0:T(8,128)(2,1)S(1)}, bf16[2,2,32,256]{3,2,1,0:T(8,128)(2,1)S(1)}, u32[]{:S(2)}, u32[]{:S(2)}) collective-permute-start(bf16[2,2,32,256]{3,2,1,0:T(8,128)(2,1)S(1)} %fusion.14.rest_0_), channel_id=1, source_target_pairs={{0,4},{4,0},{8,12},{12,8},{1,5},{5,1},{9,13},{13,9},{2,6},{6,2},{1... | collective-permute-start | bytes 196616 | tf_op jit(solution)/shard_map/ppermute | solution.py:384
  (52 other events, 443.2 us)

commit v5 on v3

--- a/solution.py
+++ b/solution.py
@@ -14,14 +14,20 @@
 ROWS = 8
 CHUNKS = 1
 VMEM_BYTES = 16 * 1024 * 1024
+WIDE_VMEM_BYTES = 60 * 1024 * 1024
 
 BF16 = jnp.bfloat16
 F32 = jnp.float32
 
 
+def ways(count):
+    far = sorted(range(1, count), key=lambda step: (step.bit_length() < count.bit_length() - 1, step))
+    return [0] + far
+
+
 def field_rows(place, freq_devs, per_dev):
     rows = []
-    for step in range(freq_devs):
+    for step in ways(freq_devs):
         first = (place ^ step) * per_dev
         for part in range(2):
             rows.extend((part, first + local) for local in range(per_dev))
@@ -77,7 +83,7 @@
     return np.stack(out).astype(np.float32).astype(BF16)
 
 
-def call(body, scalars, inputs, outputs, grid, scratch=(), aliases=None, flops=0):
+def call(body, scalars, inputs, outputs, grid, scratch=(), aliases=None, flops=0, vmem=VMEM_BYTES):
     in_arrays = [value for value, _ in inputs]
     bytes_all = sum(v.size * v.dtype.itemsize for v in in_arrays)
     bytes_all += sum(math.prod(s.shape) * s.dtype.itemsize for s, _ in outputs)
@@ -92,7 +98,7 @@
         ),
         out_shape=[shape for shape, _ in outputs],
         input_output_aliases=aliases or {},
-        compiler_params=pltpu.CompilerParams(vmem_limit_bytes=VMEM_BYTES),
+        compiler_params=pltpu.CompilerParams(vmem_limit_bytes=vmem),
         cost_estimate=pl.CostEstimate(flops=flops, bytes_accessed=bytes_all, transcendentals=0),
     )(*scalars, *in_arrays)
 
@@ -102,28 +108,48 @@
     return pl.BlockSpec(array.shape, lambda *_: zeros)
 
 
-def mask_half(response, aperture, place, flip, half):
+def streamed(step, steps, copies):
+    @pl.when(step == 0)
+    def _():
+        copies(0).start()
+
+    @pl.when(step + 1 < steps)
+    def _():
+        copies(step + 1).start()
+
+    copies(step).wait()
+
+
+def mask_half(response, aperture, place, flip, half, vmem):
     per_dev, _, _, rcv = response.shape
     rcv_blocks = rcv // BLOCK
     steps = half // BLOCK
 
-    def body(place_ref, flags, x_ref, o_ref):
-        block = (place_ref[0] ^ flip) * steps + pl.program_id(0)
+    def body(place_ref, flags, x_hbm, o_ref, slots, sems):
+        step = pl.program_id(0)
+        base = (place_ref[0] ^ flip) * steps
+
+        def copies(k):
+            rows = pl.ds(pl.multiple_of((base + k) * BLOCK, BLOCK), BLOCK)
+            return pltpu.make_async_copy(x_hbm.at[:, :, rows, :], slots.at[k % 2], sems.at[k % 2])
+
+        streamed(step, steps, copies)
         for j in range(per_dev):
             for r in range(rcv_blocks):
-                on = flags[j, block, r]
+                on = flags[j, base + step, r]
                 cut = pl.ds(r * BLOCK, BLOCK)
-                value = x_ref[j, :, :, cut]
-                o_ref[j, :, :, cut] = value * on.astype(F32).astype(BF16)
+                o_ref[j, :, :, cut] = slots[step % 2, j, :, :, cut] * on.astype(F32).astype(BF16)
 
     shape = jax.ShapeDtypeStruct((per_dev, 2, half, rcv), BF16)
     block = (per_dev, 2, BLOCK, rcv)
     (out,) = call(
         body,
         (place, aperture),
-        [(response, pl.BlockSpec(block, lambda i, a, _: (0, 0, (a[0] ^ flip) * steps + i, 0)))],
+        [(response, pl.BlockSpec(memory_space=pltpu.HBM))],
         [(shape, pl.BlockSpec(block, lambda i, *_: (0, 0, i, 0)))],
         (steps,),
+        scratch=[pltpu.VMEM((2,) + block, BF16), pltpu.SemaphoreType.DMA((2,))],
+        vmem=vmem,
     )
     return out
 
@@ -131,68 +157,108 @@
 def first_spectra(initial, table, freq_place, freq_devs, per_dev, first, rows):
     own, rcv = initial.shape[1:]
     tile = 2 * ROWS
-
-    def body(place_ref, x_ref, t_ref, *outs):
+    steps = rows // tile
+
+    def body(place_ref, x_hbm, t_hbm, *rest):
+        outs = rest[:freq_devs]
+        slots, sems, t_ref, t_sem = rest[freq_devs:]
+        step = pl.program_id(0)
+        fetch = pltpu.make_async_copy(t_hbm.at[place_ref[0]], t_ref, t_sem)
+
+        @pl.when(step == 0)
+        def _():
+            fetch.start()
+
+        def copies(k):
+            cut = pl.ds(first + k * tile, tile)
+            return pltpu.make_async_copy(x_hbm.at[cut], slots.at[k % 2], sems.at[k % 2])
+
+        streamed(step, steps, copies)
+
+        @pl.when(step == 0)
+        def _():
+            fetch.wait()
+
         parts = []
         for half in range(2):
-            flat = x_ref[half * ROWS : (half + 1) * ROWS].reshape(ROWS * own, rcv)
-            value = jnp.dot(t_ref[0], flat, preferred_element_type=F32)
+            flat = slots[step % 2, half * ROWS : (half + 1) * ROWS].reshape(ROWS * own, rcv)
+            value = jnp.dot(t_ref[...], flat, preferred_element_type=F32)
             parts.append(value.reshape(freq_devs, 2, per_dev, ROWS, rcv))
         both = jnp.concatenate(parts, 3).astype(BF16)
-        for step, out in enumerate(outs):
-            out[...] = both[step]
+        for at, out in enumerate(outs):
+            out[...] = both[at]
 
     shape = jax.ShapeDtypeStruct((2, per_dev, rows, rcv), BF16)
+    hbm = pl.BlockSpec(memory_space=pltpu.HBM)
     return call(
         body,
         (freq_place,),
-        [
-            (initial, pl.BlockSpec((tile, own, rcv), lambda i, _: (first // tile + i, 0, 0))),
-            (table, pl.BlockSpec((1,) + table.shape[1:], lambda i, z: (z[0], 0, 0))),
+        [(initial, hbm), (table, hbm)],
+        [(shape, pl.BlockSpec((2, per_dev, tile, rcv), lambda i, _: (0, 0, i, 0)))] * freq_devs,
+        (steps,),
+        scratch=[
+            pltpu.VMEM((2, tile, own, rcv), BF16),
+            pltpu.SemaphoreType.DMA((2,)),
+            pltpu.VMEM(table.shape[1:], BF16),
+            pltpu.SemaphoreType.DMA,
         ],
-        [(shape, pl.BlockSpec((2, per_dev, tile, rcv), lambda i, _: (0, 0, i, 0)))] * freq_devs,
-        (rows // tile,),
         flops=2 * 2 * freq_devs * per_dev * own * rows * rcv,
     )
 
 
-def down_products(near, far, kept, moved, freq_place, freq_devs):
-    _, per_dev, rows, rcv = near[0].shape
-    width = kept.shape[2]
+def down_products(near, far, responses, freq_place, freq_devs):
+    _, per_dev, rows, rcv = near.shape
+    width = responses[0][0].shape[2]
     tile = min(width, 256)
-    share = 2 * rows // freq_devs
-
-    def body(place_ref, n0, n1, f0, f1, k_ref, m_ref, *rest):
+    steps = width // tile
+    share = rows // freq_devs
+
+    def body(place_ref, n_ref, f_ref, k0, m0, k1, m1, *rest):
         outs, held = rest[:freq_devs], rest[freq_devs]
-        for j in range(per_dev):
-            total = None
-            for own, other, resp in ((n0, n1, k_ref), (f0, f1, m_ref)):
-                real = jnp.concatenate([own[0, j], other[0, j]], 0)
-                imag = jnp.concatenate([own[1, j], other[1, j]], 0)
-                for part, lhs in ((0, [real, imag]), (1, [-imag, real])):
-                    term = lax.dot_general(
-                        jnp.concatenate(lhs, 0),
-                        resp[j, part],
-                        (((1,), (1,)), ((), ())),
-                        preferred_element_type=F32,
-                    )
-                    total = term if total is None else total + term
-            held[0, j] = total[: 2 * rows]
-            held[1, j] = total[2 * rows :]
-        for step, out in enumerate(outs):
-            start = pl.multiple_of((place_ref[0] ^ step) * share, share)
+
+        def products(pairs):
+            for j in range(per_dev):
+                total = None
+                for lhs_ref, resp in pairs:
+                    real, imag = lhs_ref[0, j], lhs_ref[1, j]
+                    for part, lhs in ((0, [real, imag]), (1, [-imag, real])):
+                        term = lax.dot_general(
+                            jnp.concatenate(lhs, 0),
+                            resp[j, part],
+                            (((1,), (1,)), ((), ())),
+                            preferred_element_type=F32,
+                        )
+                        total = term if total is None else total + term
+                held[0, j] = total[:rows]
+                held[1, j] = total[rows:]
+
+        step = pl.program_id(0)
+
+        @pl.when(step < steps)
+        def _():
+            products(((n_ref, k0), (f_ref, m0)))
+
+        @pl.when(step >= steps)
+        def _():
+            products(((n_ref, k1), (f_ref, m1)))
+
+        for way, out in zip(ways(freq_devs), outs):
+            start = pl.multiple_of((place_ref[0] ^ way) * share, share)
             out[...] = held[:, :, pl.ds(start, share), :].astype(BF16)
 
-    shape = jax.ShapeDtypeStruct((2, per_dev, share, width), BF16)
-    resp_spec = pl.BlockSpec((per_dev, 2, tile, rcv), lambda i, _: (0, 0, i, 0))
+    shape = jax.ShapeDtypeStruct((2, per_dev, share, 2 * width), BF16)
+    block = (per_dev, 2, tile, rcv)
+    low = pl.BlockSpec(block, lambda i, _: (0, 0, jnp.minimum(i, steps - 1), 0))
+    high = pl.BlockSpec(block, lambda i, _: (0, 0, jnp.maximum(i - steps, 0), 0))
+    (k0, m0), (k1, m1) = responses
     return call(
         body,
         (freq_place,),
-        [(v, whole(v)) for v in (*near, *far)] + [(kept, resp_spec), (moved, resp_spec)],
+        [(near, whole(near)), (far, whole(far)), (k0, low), (m0, low), (k1, high), (m1, high)],
         [(shape, pl.BlockSpec((2, per_dev, share, tile), lambda i, _: (0, 0, 0, i)))] * freq_devs,
-        (width // tile,),
-        scratch=[pltpu.VMEM((2, per_dev, 2 * rows, tile), F32)],
-        flops=2 * 8 * per_dev * 2 * rows * width * rcv,
+        (2 * steps,),
+        scratch=[pltpu.VMEM((2, per_dev, rows, tile), F32)],
+        flops=2 * 8 * per_dev * rows * 2 * width * rcv,
     )
 
 
@@ -249,40 +315,41 @@
     )
 
 
-def up_products(messages, kept, moved, freq_place, rows):
+def up_products(messages, responses, freq_place, rows):
     freq_devs = len(messages)
-    per_dev, _, src, rcv = kept.shape
+    (k0, m0), (k1, m1) = responses
+    per_dev, _, src, rcv = k0.shape
     share = messages[0].shape[2]
 
-    def body(place_ref, k_ref, m_ref, *rest):
+    def body(place_ref, k0_ref, m0_ref, k1_ref, m1_ref, *rest):
         refs = rest[:freq_devs]
         keep, send, held = rest[freq_devs:]
-        for step, ref in enumerate(refs):
-            start = pl.multiple_of((place_ref[0] ^ step) * share, share)
+        for way, ref in zip(ways(freq_devs), refs):
+            start = pl.multiple_of((place_ref[0] ^ way) * share, share)
             held[:, pl.ds(start, share), :] = ref[:, 0]
-        real, imag = held[0], held[1]
-        one = jnp.concatenate([real, imag], 0)
-        two = jnp.concatenate([imag, -real], 0)
-        for side, resp in enumerate((k_ref, m_ref)):
-            total = jnp.dot(one, resp[0, 0], preferred_element_type=F32)
-            total = total + jnp.dot(two, resp[0, 1], preferred_element_type=F32)
+        for out, pair in ((send, (m0_ref, m1_ref)), (keep, (k0_ref, k1_ref))):
+            total = None
+            for half, resp in enumerate(pair):
+                cut = pl.ds(half * src, src)
+                real, imag = held[0, :, cut], held[1, :, cut]
+                for part, lhs in ((0, [real, imag]), (1, [imag, -real])):
+                    term = jnp.dot(jnp.concatenate(lhs, 0), resp[0, part], preferred_element_type=F32)
+                    total = term if total is None else total + term
             for part in range(2):
-                first = 2 * rows * part
-                keep[side, part, 0] = total[first : first + rows]
-                send[side, part, 0] = total[first + rows : first + 2 * rows].astype(BF16)
+                out[part, 0] = total[rows * part : rows * (part + 1)].astype(out.dtype)
 
     resp_spec = pl.BlockSpec((1, 2, src, rcv), lambda j, _: (j, 0, 0, 0))
-    message = pl.BlockSpec((2, 1, share, src), lambda j, _: (0, j, 0, 0))
-    out_spec = pl.BlockSpec((2, 2, 1, rows, rcv), lambda j, _: (0, 0, j, 0, 0))
-    shape = (2, 2, per_dev, rows, rcv)
+    message = pl.BlockSpec((2, 1, share, 2 * src), lambda j, _: (0, j, 0, 0))
+    out_spec = pl.BlockSpec((2, 1, rows, rcv), lambda j, _: (0, j, 0, 0))
+    shape = (2, per_dev, rows, rcv)
     return call(
         body,
         (freq_place,),
-        [(kept, resp_spec), (moved, resp_spec)] + [(v, message) for v in messages],
+        [(v, resp_spec) for v in (k0, m0, k1, m1)] + [(v, message) for v in messages],
         [(jax.ShapeDtypeStruct(shape, F32), out_spec), (jax.ShapeDtypeStruct(shape, BF16), out_spec)],
         (per_dev,),
-        scratch=[pltpu.VMEM((2, 2 * rows, src), BF16)],
-        flops=2 * 8 * per_dev * 2 * rows * src * rcv,
+        scratch=[pltpu.VMEM((2, rows, 2 * src), BF16)],
+        flops=2 * 8 * per_dev * rows * 2 * src * rcv,
     )
 
 
@@ -342,39 +409,65 @@
     own, rcv = initial.shape[1:]
     per_dev = messages[0].shape[1]
     tile = 2 * ROWS
+    steps = rows // tile
     count = freq_devs * 2 * per_dev * ROWS
 
-    def body(place_ref, _, x_ref, o_ref, t_ref, *rest):
-        refs, out = rest[:freq_devs], rest[-1]
+    def body(place_ref, _, x_hbm, t_hbm, o_ref, *rest):
+        refs = rest[:freq_devs]
+        out, slots, sems, t_ref, t_sem = rest[-5:]
+        step = pl.program_id(0)
+        fetch = pltpu.make_async_copy(t_hbm.at[place_ref[0]], t_ref, t_sem)
+
+        @pl.when(step == 0)
+        def _():
+            fetch.start()
+
+        def copies(k):
+            cut = pl.ds(first + k * tile, tile)
+            return pltpu.make_async_copy(x_hbm.at[cut], slots.at[k % 2], sems.at[k % 2])
+
+        streamed(step, steps, copies)
+
+        @pl.when(step == 0)
+        def _():
+            fetch.wait()
+
         data = [ref[...].astype(F32) for ref in refs]
         time = lax.broadcasted_iota(jnp.int32, (own, rcv), 0) + place_ref[0] * own
         for half in range(2):
             cut = slice(half * ROWS, (half + 1) * ROWS)
             flat = jnp.stack([v[:, :, cut] for v in data]).reshape(count, rcv).astype(BF16)
-            change = jnp.dot(t_ref[0], flat, preferred_element_type=F32)
+            change = jnp.dot(t_ref[...], flat, preferred_element_type=F32)
             for row in range(ROWS):
                 spot = half * ROWS + row
                 on = time < o_ref[spot : spot + 1, :]
-                step = jnp.where(on, change[row * own : (row + 1) * own], 0.0)
-                out[spot] = (x_ref[spot].astype(F32) - step).astype(BF16)
-
-    block = pl.BlockSpec((tile, own, rcv), lambda i, *_: (first // tile + i, 0, 0))
+                moved = jnp.where(on, change[row * own : (row + 1) * own], 0.0)
+                out[spot] = (slots[step % 2, spot].astype(F32) - moved).astype(BF16)
+
+    hbm = pl.BlockSpec(memory_space=pltpu.HBM)
     inputs = [
-        (initial, block),
+        (initial, hbm),
+        (table, hbm),
         (onset, pl.BlockSpec((tile, rcv), lambda i, _, b: (b[0] + first // tile + i, 0))),
-        (table, pl.BlockSpec((1,) + table.shape[1:], lambda i, z, _: (z[0], 0, 0))),
     ] + [(v, pl.BlockSpec((2, per_dev, tile, rcv), lambda i, *_: (0, 0, i, 0))) for v in messages]
     aliases = {}
     if target is not None:
-        inputs.append((target, pl.BlockSpec(memory_space=pl.ANY)))
+        inputs.append((target, hbm))
         aliases = {2 + len(inputs) - 1: 0}
     (out,) = call(
         body,
         (freq_place, focal_first),
         inputs,
-        [(jax.ShapeDtypeStruct(initial.shape, BF16), block)],
-        (rows // tile,),
+        [(jax.ShapeDtypeStruct(initial.shape, BF16), pl.BlockSpec((tile, own, rcv), lambda i, *_: (first // tile + i, 0, 0)))],
+        (steps,),
+        scratch=[
+            pltpu.VMEM((2, tile, own, rcv), BF16),
+            pltpu.SemaphoreType.DMA((2,)),
+            pltpu.VMEM(table.shape[1:], BF16),
+            pltpu.SemaphoreType.DMA,
+        ],
         aliases=aliases,
+        vmem=WIDE_VMEM_BYTES,
         flops=2 * 2 * freq_devs * per_dev * own * rows * rcv,
     )
     return out
@@ -384,15 +477,8 @@
     return lax.ppermute(value, axis, [(i, i ^ step) for i in range(lax.axis_size(axis))])
 
 
-def partners(count):
-    return sorted(range(1, count), key=lambda step: (step.bit_length() < count.bit_length() - 1, step))
-
-
 def dealt_out(parts):
-    out = list(parts)
-    for step in partners(len(parts)):
-        out[step] = exchanged(parts[step], "freq", step)
-    return out
+    return [exchanged(part, "freq", step) if step else part for part, step in zip(parts, ways(len(parts)))]
 
 
 def spread(value, count):
@@ -400,7 +486,7 @@
 
 
 def phases(onset, freq_index, freq_devs, per_dev, samples):
-    steps = lax.iota(jnp.int32, freq_devs)
+    steps = jnp.asarray(ways(freq_devs), jnp.int32)
     order = (freq_index ^ steps)[:, None] * per_dev + lax.iota(jnp.int32, per_dev)[None, :] + 1
     phase = order[:, :, None, None] * onset[None, None] % samples
     angle = phase.astype(F32) * (2.0 * math.pi / samples)
@@ -414,17 +500,20 @@
     half_rows = initial.shape[0]
     src_width = response.shape[2] // 2
     rows = half_rows // CHUNKS
+    share = rows // freq_devs
     freq_index = lax.axis_index("freq")
     rblk_index = lax.axis_index("rblk")
     sblk_index = lax.axis_index("sblk")
     freq_place = freq_index.reshape(1)
     rblk_place = rblk_index.reshape(1)
 
-    moved = exchanged(mask_half(response, aperture, rblk_place, 1, src_width), "rblk", 1)
+    moved = exchanged(mask_half(response, aperture, rblk_place, 1, src_width, WIDE_VMEM_BYTES), "rblk", 1)
+    kept = mask_half(response, aperture, rblk_place, 0, src_width, VMEM_BYTES)
+    kept_pair = exchanged(kept, "sblk", 1)
+    responses = None
     forward = jnp.asarray(forward_tables(samples, freq_devs, per_dev))
     inverse = jnp.asarray(inverse_tables(samples, freq_devs, per_dev))
     matrix = jnp.asarray(window_tables(samples, freq_devs, per_dev))
-    kept = mask_half(response, aperture, rblk_place, 0, src_width)
 
     result = None
     for chunk in range(CHUNKS):
@@ -432,26 +521,25 @@
         parts = first_spectra(initial, forward, freq_place, freq_devs, per_dev, first, rows)
         sums = sum(v.astype(F32) for v in dealt_out(parts))
         spectra = sums.astype(BF16)
-
-        share = 2 * rows // freq_devs
-        spot = freq_index * share
-        other = (spot >= rows).astype(jnp.int32)
-        src_first = (sblk_index ^ other) * half_rows + first + spot - other * rows
-        onsets = lax.dynamic_slice(onset_src, (src_first, rblk_index * src_width), (share, src_width))
-        src_tables = phases(onsets, freq_index, freq_devs, per_dev, samples)
+        if responses is None:
+            moved, spectra = lax.optimization_barrier((moved, spectra))
+            responses = ((kept, moved), (kept_pair, exchanged(moved, "sblk", 1)))
+
+        def src_onsets(core):
+            spot = core * half_rows + first + freq_index * share
+            return lax.dynamic_slice(onset_src, (spot, rblk_index * src_width), (share, src_width))
+
+        onsets = [src_onsets(sblk_index), exchanged(src_onsets(1 - sblk_index), "sblk", 1)]
+        src_tables = phases(jnp.concatenate(onsets, 1), freq_index, freq_devs, per_dev, samples)
         onsets = lax.dynamic_slice_in_dim(onset_rcv, sblk_index * half_rows + first, rows, 0)
         rcv_tables = phases(onsets, freq_index, freq_devs, per_dev, samples)
 
         for step in range(ITERS):
-            far_own = exchanged(spectra, "rblk", 1)
-            near = (spectra, exchanged(spectra, "sblk", 1))
-            far = (far_own, exchanged(far_own, "sblk", 1))
-            messages = dealt_out(down_products(near, far, kept, moved, freq_place, freq_devs))
+            far = exchanged(spectra, "rblk", 1)
+            messages = dealt_out(down_products(spectra, far, responses, freq_place, freq_devs))
             messages = windowed(messages, src_tables, matrix, freq_place, per_dev, share)
-            keep, send = up_products(dealt_out(messages), kept, moved, freq_place, rows)
-            from_core = exchanged(send, "sblk", 1)
-            from_far = exchanged((keep[1] + from_core[1].astype(F32)).astype(BF16), "rblk", 1)
-            back = (keep[0] + from_core[0].astype(F32) + from_far.astype(F32)).astype(BF16)
+            keep, send = up_products(dealt_out(messages), responses, freq_place, rows)
+            back = (keep + exchanged(send, "rblk", 1).astype(F32)).astype(BF16)
             messages = spread(back, freq_devs)
             if step < ITERS - 1:
                 spectra = next_spectra(sums, messages, rcv_tables, matrix, freq_place)
@@ -540,7 +628,7 @@
     if lax.axis_size("rblk") != 2 or lax.axis_size("sblk") != 2 or freq_devs & (freq_devs - 1):
         return False
     rows = initial.shape[0] // CHUNKS
-    whole_rows = initial.shape[0] % (CHUNKS * 2 * ROWS * max(1, freq_devs // 2)) == 0 and rows % (2 * ROWS) == 0
+    whole_rows = initial.shape[0] % CHUNKS == 0 and rows % (2 * ROWS * freq_devs) == 0
     whole_width = response.shape[2] % (4 * BLOCK) == 0 and response.shape[3] % BLOCK == 0
     return whole_rows and whole_width and onset_rcv.shape[0] == 2 * initial.shape[0]
 

time: 165 us -> 153 us (0.927)
  waiting for transfers between devices: 87.2 us -> 65.2 us
  Pallas kernels: 16 us -> 31.2 us
  starting transfers between devices: 40.6 us -> 38.3 us
  other arithmetic: 8.64 us -> 6.99 us
    ppermute x32 -> x29, waiting for transfers between devices: 87.2 us -> 65.2 us  [exchanged(): lax.ppermute(value, axis, [(i, i ^ step) for i in range(lax.axis_size(axi...]
    pallas_call x11, Pallas kernels: 16 us -> 31.2 us  [call(): pl.pallas_call(body, grid_spec=pltpu.PrefetchScalarGridSpec(num_scalar_pr...]
    ppermute x32 -> x29, starting transfers between devices: 40.6 us -> 38.3 us  [exchanged(): lax.ppermute(value, axis, [(i, i ^ step) for i in range(lax.axis_size(axi...]
    unnamed x25 -> x37, local copies, waits for them, and re-layouts: 11.7 us -> 9.46 us
  transfers between devices with their start and end apart: 32 -> 29, of which waited for: 20 -> 18; matrix products, arithmetic and copies ran while one was open for 4% -> 4% of each run, Pallas kernels for 2% -> 2%
where the time goes in v5:
time: 153 us; the launch traced here: 152 us
  waiting for transfers between devices  65.2 us (43%)
  starting transfers between devices  38.3 us (25%)
  Pallas kernels  31.2 us (20%)
  local copies, waits for them, and re-layouts  10.2 us (7%)
  other arithmetic  6.99 us (5%)
    ppermute x29, waiting for transfers between devices, exchanged(): lax.ppermute(value, axis, [(i, i ^ step) for i in range(lax.axis_size(axi...  65.2 us
    ppermute x29, starting transfers between devices, exchanged(): lax.ppermute(value, axis, [(i, i ^ step) for i in range(lax.axis_size(axi...  38.3 us
    pallas_call x11, Pallas kernels, call(): pl.pallas_call(body, grid_spec=pltpu.PrefetchScalarGridSpec(num_scalar_pr...  31.2 us
    unnamed x37, local copies, waits for them, and re-layouts  9.46 us
    sin x2, other arithmetic, phases(): return (jnp.cos(angle), jnp.sin(angle), onset.astype(F32) * (1.0 / samples))  4.21 us
  transfers between devices with their start and end apart: 29, of which 18 were waited for; matrix products, arithmetic and copies ran while one was open for 4% of the time, Pallas kernels for 2%

profile of v5, /device:TPU:0, one launch (start us, length us, event | category | flops | bytes accessed | tf_op | source)
XLA Modules:
  0.0 152.2 jit_solution(3345353777781181477)
XLA Ops:
  1.4 4.4 %shard_map.101 = bf16[2,2,512,256]{3,2,1,0:T(8,128)(2,1)} custom-call(s32[1]{0:T(128)} %bitcast.2.place_ref, s32[2,8,2]{2,1,0:T(8,128)} %copy.11.flags, bf16[2,2,1024,256]{3,2,1,0:T(8,128)(2,1)} %x_hbm.5), custom_call_target="tpu_custom_call" | custom-call | bytes 3145728 | tf_op jit(solution)/shard_map/pallas_call | solution.py:90
  5.7 3.0 %collective-permute-start = (bf16[2,2,512,256]{3,2,1,0:T(8,128)(2,1)}, bf16[2,2,512,256]{3,2,1,0:T(8,128)(2,1)S(1)}, u32[]{:S(2)}, u32[]{:S(2)}) collective-permute-start(bf16[2,2,512,256]{3,2,1,0:T(8,128)(2,1)} %shard_map.101), channel_id=1, source_target_pairs={{0,2},{2,0},{1,3},{3,1},{4,6},{6,4},{5,7},{7,5},{8,10},{10,8},{9,1... | collective-permute-start | bytes 3145736 | tf_op jit(solution)/shard_map/ppermute | solution.py:477
  8.7 2.2 %copy-done = bf16[64,128,256]{2,1,0:T(8,128)(2,1)S(1)} copy-done((bf16[64,128,256]{2,1,0:T(8,128)(2,1)S(1)}, bf16[64,128,256]{2,1,0:T(8,128)(2,1)}, u32[]{:S(2)}) %copy-start) | copy-done | bytes 4194328
  13.9 2.7 %collective-permute-start.1 = (bf16[2,2,64,256]{3,2,1,0:T(8,128)(2,1)S(1)}, bf16[2,2,64,256]{3,2,1,0:T(8,128)(2,1)S(1)}, u32[]{:S(2)}, u32[]{:S(2)}) collective-permute-start(bf16[2,2,64,256]{3,2,1,0:T(8,128)(2,1)S(1)} %get-tuple-element.32), channel_id=1, source_target_pairs={{0,8},{4,12},{8,0},{12,4},{1,9},{5,13},{9,1},{13,5},{2,10},{6,14},... | collective-permute-start | bytes 393224 | tf_op jit(solution)/shard_map/ppermute | solution.py:477
  21.0 5.6 %collective-permute-done.1 = bf16[2,2,64,256]{3,2,1,0:T(8,128)(2,1)S(1)} collective-permute-done((bf16[2,2,64,256]{3,2,1,0:T(8,128)(2,1)S(1)}, bf16[2,2,64,256]{3,2,1,0:T(8,128)(2,1)S(1)}, u32[]{:S(2)}, u32[]{:S(2)}) %collective-permute-start.1) | collective-permute-done | bytes 131104 | tf_op jit(solution)/shard_map/ppermute | solution.py:477
  27.5 4.6 %collective-permute-done.m0.m0_ref = bf16[2,2,512,256]{3,2,1,0:T(8,128)(2,1)S(1)} collective-permute-done((bf16[2,2,512,256]{3,2,1,0:T(8,128)(2,1)}, bf16[2,2,512,256]{3,2,1,0:T(8,128)(2,1)S(1)}, u32[]{:S(2)}, u32[]{:S(2)}) %collective-permute-start) | collective-permute-done | bytes 1048608 | tf_op jit(solution)/shard_map/ppermute | solution.py:477
  35.2 3.9 %collective-permute-done.7.f_ref = bf16[2,2,64,256]{3,2,1,0:T(8,128)(2,1)S(1)} collective-permute-done((bf16[2,2,64,256]{3,2,1,0:T(8,128)(2,1)}, bf16[2,2,64,256]{3,2,1,0:T(8,128)(2,1)S(1)}, u32[]{:S(2)}, u32[]{:S(2)}) %collective-permute-start.7) | collective-permute-done | bytes 131104 | tf_op jit(solution)/shard_map/ppermute | solution.py:477
  40.0 3.9 %shard_map.103 = (bf16[2,2,16,1024]{3,2,1,0:T(8,128)(2,1)S(1)}, bf16[2,2,16,1024]{3,2,1,0:T(8,128)(2,1)S(1)}, bf16[2,2,16,1024]{3,2,1,0:T(8,128)(2,1)S(1)}, bf16[2,2,16,1024]{3,2,1,0:T(8,128)(2,1)S(1)}) custom-call(s32[1]{0:T(128)} %bitcast.place_ref, bf16[2,2,64,256]{3,2,1,0:T(8,128)(2,1)S(1)} %copy-done.10, ...), custom_call_target="tpu_custom_call" | custom-call | flops 536870912 | bytes 4980736 | tf_op jit(solution)/shard_map/pallas_call | solution.py:90
  45.8 2.6 %collective-permute-start.8 = (bf16[2,2,16,1024]{3,2,1,0:T(8,128)(2,1)S(1)}, bf16[2,2,16,1024]{3,2,1,0:T(8,128)(2,1)S(1)}, u32[]{:S(2)}, u32[]{:S(2)}) collective-permute-start(bf16[2,2,16,1024]{3,2,1,0:T(8,128)(2,1)S(1)} %get-tuple-element.38), channel_id=1, source_target_pairs={{0,8},{4,12},{8,0},{12,4},{1,9},{5,13},{9,1},{13,5},{2,10},{6,14},... | collective-permute-start | bytes 393224 | tf_op jit(solution)/shard_map/ppermute | solution.py:477
  48.4 2.1 %fusion.8 = (f32[4,2,16,1024]{3,2,1,0:T(8,128)S(1)}, f32[4,2,16,1024]{3,2,1,0:T(8,128)S(1)}) fusion(s32[16,1024]{1,0:T(8,128)S(1)} %pad_add_fusion, s32[4,2]{1,0:T(4,128)S(1)} %add_add_fusion), kind=kLoop, calls=%fused_computation.20 | loop fusion | flops 1835008 | bytes 1114144 | tf_op jit(solution)/shard_map/sin | solution.py:493
  50.5 7.6 %collective-permute-done.8.rest_1_ = bf16[2,2,16,1024]{3,2,1,0:T(8,128)(2,1)S(1)} collective-permute-done((bf16[2,2,16,1024]{3,2,1,0:T(8,128)(2,1)S(1)}, bf16[2,2,16,1024]{3,2,1,0:T(8,128)(2,1)S(1)}, u32[]{:S(2)}, u32[]{:S(2)}) %collective-permute-start.8) | collective-permute-done | bytes 131104 | tf_op jit(solution)/shard_map/ppermute | solution.py:477
  58.1 2.1 %shard_map.104 = (bf16[2,2,16,1024]{3,2,1,0:T(8,128)(2,1)S(1)}, bf16[2,2,16,1024]{3,2,1,0:T(8,128)(2,1)S(1)}, bf16[2,2,16,1024]{3,2,1,0:T(8,128)(2,1)S(1)}, bf16[2,2,16,1024]{3,2,1,0:T(8,128)(2,1)S(1)}) custom-call(s32[1]{0:T(128)} %bitcast.place_ref, f32[4,2,16,1024]{3,2,1,0:T(8,128)S(1)} %get-tuple-element.66.c_ref, ...), custom_call_target="tpu_custom_call" | custom-call | flops 134217728 | bytes 2293760 | tf_op jit(solution)/shard_map/pallas_call | solution.py:90
  61.0 3.0 %collective-permute-start.11 = (bf16[2,2,16,1024]{3,2,1,0:T(8,128)(2,1)S(1)}, bf16[2,2,16,1024]{3,2,1,0:T(8,128)(2,1)S(1)}, u32[]{:S(2)}, u32[]{:S(2)}) collective-permute-start(bf16[2,2,16,1024]{3,2,1,0:T(8,128)(2,1)S(1)} %get-tuple-element.42), channel_id=1, source_target_pairs={{0,8},{4,12},{8,0},{12,4},{1,9},{5,13},{9,1},{13,5},{2,10},{6,14},... | collective-permute-start | bytes 393224 | tf_op jit(solution)/shard_map/ppermute | solution.py:477
  65.4 7.5 %collective-permute-done.11.rest_1_ = bf16[2,2,16,1024]{3,2,1,0:T(8,128)(2,1)S(1)} collective-permute-done((bf16[2,2,16,1024]{3,2,1,0:T(8,128)(2,1)S(1)}, bf16[2,2,16,1024]{3,2,1,0:T(8,128)(2,1)S(1)}, u32[]{:S(2)}, u32[]{:S(2)}) %collective-permute-start.11) | collective-permute-done | bytes 131104 | tf_op jit(solution)/shard_map/ppermute | solution.py:477
  73.0 2.6 %shard_map.105 = (f32[2,2,64,256]{3,2,1,0:T(8,128)S(1)}, bf16[2,2,64,256]{3,2,1,0:T(8,128)(2,1)}) custom-call(s32[1]{0:T(128)} %bitcast.place_ref, bf16[2,2,512,256]{3,2,1,0:T(8,128)(2,1)S(1)} %shard_map.100.k0.k0_ref, bf16[2,2,512,256]{3,2,1,0:T(8,128)(2,1)S(1)} %collective-permute-done.m0.m0_ref, ...), custom_call_target="tpu_custom_call" | custom-call | flops 536870912 | bytes 5111808 | tf_op jit(solution)/shard_map/pallas_call | solution.py:90
  78.8 2.8 %collective-permute-done.14 = bf16[2,2,64,256]{3,2,1,0:T(8,128)(2,1)} collective-permute-done((bf16[2,2,64,256]{3,2,1,0:T(8,128)(2,1)}, bf16[2,2,64,256]{3,2,1,0:T(8,128)(2,1)}, u32[]{:S(2)}, u32[]{:S(2)}) %collective-permute-start.14) | collective-permute-done | bytes 131104 | tf_op jit(solution)/shard_map/ppermute | solution.py:477
  82.6 2.0 %collective-permute-start.15 = (bf16[2,2,64,256]{3,2,1,0:T(8,128)(2,1)S(1)}, bf16[2,2,64,256]{3,2,1,0:T(8,128)(2,1)S(1)}, u32[]{:S(2)}, u32[]{:S(2)}) collective-permute-start(bf16[2,2,64,256]{3,2,1,0:T(8,128)(2,1)S(1)} %add_convert_fusion.1.rest_0_), channel_id=1, source_target_pairs={{0,8},{4,12},{8,0},{12,4},{1,9},{5,13},{9,1},{13,5},{2,10},{6,14},... | collective-permute-start | bytes 393224 | tf_op jit(solution)/shard_map/ppermute | solution.py:477
  84.6 2.4 %collective-permute-start.16 = (bf16[2,2,64,256]{3,2,1,0:T(8,128)(2,1)S(1)}, bf16[2,2,64,256]{3,2,1,0:T(8,128)(2,1)S(1)}, u32[]{:S(2)}, u32[]{:S(2)}) collective-permute-start(bf16[2,2,64,256]{3,2,1,0:T(8,128)(2,1)S(1)} %add_convert_fusion.1.rest_0_), channel_id=1, source_target_pairs={{0,12},{4,8},{8,4},{12,0},{1,13},{5,9},{9,5},{13,1},{2,14},{6,10},... | collective-permute-start | bytes 393224 | tf_op jit(solution)/shard_map/ppermute | solution.py:477
  87.0 2.1 %fusion.6 = (f32[4,2,64,256]{3,2,1,0:T(8,128)S(1)}, f32[4,2,64,256]{3,2,1,0:T(8,128)S(1)}) fusion(s32[64,256]{1,0:T(8,128)S(1)} %get-tuple-element.58, s32[4,2]{1,0:T(4,128)S(1)} %add_add_fusion), kind=kLoop, calls=%fused_computation.18 | loop fusion | flops 1835008 | bytes 1114144 | tf_op jit(solution)/shard_map/sin | solution.py:493
  89.2 3.8 %collective-permute-done.15.rest_1_ = bf16[2,2,64,256]{3,2,1,0:T(8,128)(2,1)S(1)} collective-permute-done((bf16[2,2,64,256]{3,2,1,0:T(8,128)(2,1)S(1)}, bf16[2,2,64,256]{3,2,1,0:T(8,128)(2,1)S(1)}, u32[]{:S(2)}, u32[]{:S(2)}) %collective-permute-start.15) | collective-permute-done | bytes 131104 | tf_op jit(solution)/shard_map/ppermute | solution.py:477
  96.3 3.4 %collective-permute-done.18.f_ref = bf16[2,2,64,256]{3,2,1,0:T(8,128)(2,1)S(1)} collective-permute-done((bf16[2,2,64,256]{3,2,1,0:T(8,128)(2,1)S(1)}, bf16[2,2,64,256]{3,2,1,0:T(8,128)(2,1)S(1)}, u32[]{:S(2)}, u32[]{:S(2)}) %collective-permute-start.18) | collective-permute-done | bytes 131104 | tf_op jit(solution)/shard_map/ppermute | solution.py:477
  99.7 3.9 %shard_map.107 = (bf16[2,2,16,1024]{3,2,1,0:T(8,128)(2,1)S(1)}, bf16[2,2,16,1024]{3,2,1,0:T(8,128)(2,1)S(1)}, bf16[2,2,16,1024]{3,2,1,0:T(8,128)(2,1)S(1)}, bf16[2,2,16,1024]{3,2,1,0:T(8,128)(2,1)S(1)}) custom-call(s32[1]{0:T(128)} %bitcast.place_ref, bf16[2,2,64,256]{3,2,1,0:T(8,128)(2,1)S(1)} %shard_map.106.n_ref, ...), custom_call_target="tpu_custom_call" | custom-call | flops 536870912 | bytes 4980736 | tf_op jit(solution)/shard_map/pallas_call | solution.py:90
  103.6 2.1 %collective-permute-start.19 = (bf16[2,2,16,1024]{3,2,1,0:T(8,128)(2,1)S(1)}, bf16[2,2,16,1024]{3,2,1,0:T(8,128)(2,1)S(1)}, u32[]{:S(2)}, u32[]{:S(2)}) collective-permute-start(bf16[2,2,16,1024]{3,2,1,0:T(8,128)(2,1)S(1)} %get-tuple-element.48), channel_id=1, source_target_pairs={{0,8},{4,12},{8,0},{12,4},{1,9},{5,13},{9,1},{13,5},{2,10},{6,14},... | collective-permute-start | bytes 393224 | tf_op jit(solution)/shard_map/ppermute | solution.py:477
  107.2 6.3 %collective-permute-done.19.rest_1_ = bf16[2,2,16,1024]{3,2,1,0:T(8,128)(2,1)S(1)} collective-permute-done((bf16[2,2,16,1024]{3,2,1,0:T(8,128)(2,1)S(1)}, bf16[2,2,16,1024]{3,2,1,0:T(8,128)(2,1)S(1)}, u32[]{:S(2)}, u32[]{:S(2)}) %collective-permute-start.19) | collective-permute-done | bytes 131104 | tf_op jit(solution)/shard_map/ppermute | solution.py:477
  114.2 2.1 %shard_map.108 = (bf16[2,2,16,1024]{3,2,1,0:T(8,128)(2,1)S(1)}, bf16[2,2,16,1024]{3,2,1,0:T(8,128)(2,1)S(1)}, bf16[2,2,16,1024]{3,2,1,0:T(8,128)(2,1)S(1)}, bf16[2,2,16,1024]{3,2,1,0:T(8,128)(2,1)S(1)}) custom-call(s32[1]{0:T(128)} %bitcast.place_ref, f32[4,2,16,1024]{3,2,1,0:T(8,128)S(1)} %copy-done.5, f32[4,2,16,1024]{3,2,1,0:T(8,128)S(1)} %copy-done.3, ...), custom_call_target="tpu_custom_call" | custom-call | flops 134217728 | bytes 2293760 | tf_op jit(solution)/shard_map/pallas_call | solution.py:90
  117.4 2.5 %collective-permute-start.23 = (bf16[2,2,16,1024]{3,2,1,0:T(8,128)(2,1)S(1)}, bf16[2,2,16,1024]{3,2,1,0:T(8,128)(2,1)S(1)}, u32[]{:S(2)}, u32[]{:S(2)}) collective-permute-start(bf16[2,2,16,1024]{3,2,1,0:T(8,128)(2,1)S(1)} %get-tuple-element.53), channel_id=1, source_target_pairs={{0,12},{4,8},{8,4},{12,0},{1,13},{5,9},{9,5},{13,1},{2,14},{6,10},... | collective-permute-start | bytes 393224 | tf_op jit(solution)/shard_map/ppermute | solution.py:477
  120.0 6.4 %collective-permute-done.22.rest_1_ = bf16[2,2,16,1024]{3,2,1,0:T(8,128)(2,1)S(1)} collective-permute-done((bf16[2,2,16,1024]{3,2,1,0:T(8,128)(2,1)S(1)}, bf16[2,2,16,1024]{3,2,1,0:T(8,128)(2,1)S(1)}, u32[]{:S(2)}, u32[]{:S(2)}) %collective-permute-start.22) | collective-permute-done | bytes 131104 | tf_op jit(solution)/shard_map/ppermute | solution.py:477
  127.2 2.0 %shard_map.109 = (f32[2,2,64,256]{3,2,1,0:T(8,128)S(1)}, bf16[2,2,64,256]{3,2,1,0:T(8,128)(2,1)S(1)}) custom-call(s32[1]{0:T(128)} %bitcast.place_ref, bf16[2,2,512,256]{3,2,1,0:T(8,128)(2,1)S(1)} %shard_map.100.k0.k0_ref, bf16[2,2,512,256]{3,2,1,0:T(8,128)(2,1)S(1)} %collective-permute-done.m0.m0_ref, ...), custom_call_target="tpu_custom_call" | custom-call | flops 536870912 | bytes 5111808 | tf_op jit(solution)/shard_map/pallas_call | solution.py:90
  130.9 3.4 %collective-permute-done.25 = bf16[2,2,64,256]{3,2,1,0:T(8,128)(2,1)S(1)} collective-permute-done((bf16[2,2,64,256]{3,2,1,0:T(8,128)(2,1)S(1)}, bf16[2,2,64,256]{3,2,1,0:T(8,128)(2,1)S(1)}, u32[]{:S(2)}, u32[]{:S(2)}) %collective-permute-start.25) | collective-permute-done | bytes 131104 | tf_op jit(solution)/shard_map/ppermute | solution.py:477
  134.3 2.2 %collective-permute-start.26 = (bf16[2,2,64,256]{3,2,1,0:T(8,128)(2,1)S(1)}, bf16[2,2,64,256]{3,2,1,0:T(8,128)(2,1)S(1)}, u32[]{:S(2)}, u32[]{:S(2)}) collective-permute-start(bf16[2,2,64,256]{3,2,1,0:T(8,128)(2,1)S(1)} %add_convert_fusion.rest_0_), channel_id=1, source_target_pairs={{0,8},{4,12},{8,0},{12,4},{1,9},{5,13},{9,1},{13,5},{2,10},{6,14},... | collective-permute-start | bytes 393224 | tf_op jit(solution)/shard_map/ppermute | solution.py:477
  137.9 6.4 %collective-permute-done.26.rest_1_ = bf16[2,2,64,256]{3,2,1,0:T(8,128)(2,1)S(1)} collective-permute-done((bf16[2,2,64,256]{3,2,1,0:T(8,128)(2,1)S(1)}, bf16[2,2,64,256]{3,2,1,0:T(8,128)(2,1)S(1)}, u32[]{:S(2)}, u32[]{:S(2)}) %collective-permute-start.26) | collective-permute-done | bytes 131104 | tf_op jit(solution)/shard_map/ppermute | solution.py:477
  145.6 6.6 %shard_map.110 = bf16[64,128,256]{2,1,0:T(8,128)(2,1)} custom-call(s32[1]{0:T(128)} %bitcast.place_ref, s32[1]{0:T(128)} %bitcast.1._, bf16[64,128,256]{2,1,0:T(8,128)(2,1)} %x_hbm.7, bf16[4,1024,128]{2,1,0:T(8,128)(2,1)} %constant.65.clone.t_hbm, s32[128,256]{1,0:T(8,128)} %o_ref.1, bf16[2,2,64,256]{3,2,1,0:T(8,128)(2,1)} %copy-done.13, ...), custom_call_target="tpu_custom_call" | custom-call | flops 67108864 | bytes 10092544 | tf_op jit(solution)/shard_map/pallas_call | solution.py:90
  (85 shorter events, 33.9 us)
Async XLA Ops:
  5.7 26.4 %collective-permute-start = (bf16[2,2,512,256]{3,2,1,0:T(8,128)(2,1)}, bf16[2,2,512,256]{3,2,1,0:T(8,128)(2,1)S(1)}, u32[]{:S(2)}, u32[]{:S(2)}) collective-permute-start(bf16[2,2,512,256]{3,2,1,0:T(8,128)(2,1)} %shard_map.101), channel_id=1, source_target_pairs={{0,2},{2,0},{1,3},{3,1},{4,6},{6,4},{5,7},{7,5},{8,10},{10,8},{9,1... | collective-permute-start | bytes 3145736 | tf_op jit(solution)/shard_map/ppermute | solution.py:477
  13.9 12.7 %collective-permute-start.1 = (bf16[2,2,64,256]{3,2,1,0:T(8,128)(2,1)S(1)}, bf16[2,2,64,256]{3,2,1,0:T(8,128)(2,1)S(1)}, u32[]{:S(2)}, u32[]{:S(2)}) collective-permute-start(bf16[2,2,64,256]{3,2,1,0:T(8,128)(2,1)S(1)} %get-tuple-element.32), channel_id=1, source_target_pairs={{0,8},{4,12},{8,0},{12,4},{1,9},{5,13},{9,1},{13,5},{2,10},{6,14},... | collective-permute-start | bytes 393224 | tf_op jit(solution)/shard_map/ppermute | solution.py:477
  16.5 10.1 %collective-permute-start.2 = (bf16[2,2,64,256]{3,2,1,0:T(8,128)(2,1)S(1)}, bf16[2,2,64,256]{3,2,1,0:T(8,128)(2,1)S(1)}, u32[]{:S(2)}, u32[]{:S(2)}) collective-permute-start(bf16[2,2,64,256]{3,2,1,0:T(8,128)(2,1)S(1)} %get-tuple-element.33), channel_id=1, source_target_pairs={{0,12},{4,8},{8,4},{12,0},{1,13},{5,9},{9,5},{13,1},{2,14},{6,10},... | collective-permute-start | bytes 393224 | tf_op jit(solution)/shard_map/ppermute | solution.py:477
  17.9 8.9 %collective-permute-start.3 = (bf16[2,2,64,256]{3,2,1,0:T(8,128)(2,1)S(1)}, bf16[2,2,64,256]{3,2,1,0:T(8,128)(2,1)S(1)}, u32[]{:S(2)}, u32[]{:S(2)}) collective-permute-start(bf16[2,2,64,256]{3,2,1,0:T(8,128)(2,1)S(1)} %get-tuple-element.34), channel_id=1, source_target_pairs={{0,4},{4,0},{8,12},{12,8},{1,5},{5,1},{9,13},{13,9},{2,6},{6,2},{1... | collective-permute-start | bytes 393224 | tf_op jit(solution)/shard_map/ppermute | solution.py:477
  20.9 37.3 %copy-start.6 = (bf16[4,128,128]{2,1,0:T(8,128)(2,1)S(1)}, bf16[4,128,128]{2,1,0:T(8,128)(2,1)}, u32[]{:S(2)}) copy-start(bf16[4,128,128]{2,1,0:T(8,128)(2,1)} %constant.66.clone.g_ref) | copy-start | bytes 393220
  20.9 14.4 %collective-permute-start.4 = (bf16[2,2,512,256]{3,2,1,0:T(8,128)(2,1)S(1)}, bf16[2,2,512,256]{3,2,1,0:T(8,128)(2,1)S(1)}, u32[]{:S(2)}, u32[]{:S(2)}) collective-permute-start(bf16[2,2,512,256]{3,2,1,0:T(8,128)(2,1)S(1)} %shard_map.100.k0.k0_ref), channel_id=1, source_target_pairs={{0,1},{1,0},{2,3},{3,2},{4,5},{5,4},{6,7},{7,6},{8,9},{9,8},{10,11... | collective-permute-start | bytes 3145736 | tf_op jit(solution)/shard_map/ppermute | solution.py:477
  32.1 7.0 %collective-permute-start.5 = (bf16[2,2,512,256]{3,2,1,0:T(8,128)(2,1)S(1)}, bf16[2,2,512,256]{3,2,1,0:T(8,128)(2,1)}, u32[]{:S(2)}, u32[]{:S(2)}) collective-permute-start(bf16[2,2,512,256]{3,2,1,0:T(8,128)(2,1)S(1)} %collective-permute-done.m0.m0_ref), channel_id=1, source_target_pairs={{0,1},{1,0},{2,3},{3,2},{4,5},{5,4},{6,7},{7,6},{8,9},{9,8},{10,11... | collective-permute-start | bytes 3145736 | tf_op jit(solution)/shard_map/ppermute | solution.py:477
  32.9 2.3 %collective-permute-start.6 = (s32[16,512]{1,0:T(8,128)S(1)}, s32[16,512]{1,0:T(8,128)S(1)}, u32[]{:S(2)}, u32[]{:S(2)}) collective-permute-start(s32[16,512]{1,0:T(8,128)S(1)} %get-tuple-element.62), channel_id=1, source_target_pairs={{0,1},{1,0},{2,3},{3,2},{4,5},{5,4},{6,7},{7,6},{8,9},{9,8},{10,11... | collective-permute-start | bytes 98312 | tf_op jit(solution)/shard_map/ppermute | solution.py:477
  33.4 5.7 %collective-permute-start.7 = (bf16[2,2,64,256]{3,2,1,0:T(8,128)(2,1)}, bf16[2,2,64,256]{3,2,1,0:T(8,128)(2,1)S(1)}, u32[]{:S(2)}, u32[]{:S(2)}) collective-permute-start(bf16[2,2,64,256]{3,2,1,0:T(8,128)(2,1)} %get-tuple-element.36.n_ref), channel_id=1, source_target_pairs={{0,2},{2,0},{1,3},{3,1},{4,6},{6,4},{5,7},{7,5},{8,10},{10,8},{9,1... | collective-permute-start | bytes 393224 | tf_op jit(solution)/shard_map/ppermute | solution.py:477
  43.9 6.6 %collective-permute-start.10 = (bf16[2,2,16,1024]{3,2,1,0:T(8,128)(2,1)S(1)}, bf16[2,2,16,1024]{3,2,1,0:T(8,128)(2,1)S(1)}, u32[]{:S(2)}, u32[]{:S(2)}) collective-permute-start(bf16[2,2,16,1024]{3,2,1,0:T(8,128)(2,1)S(1)} %get-tuple-element.40), channel_id=1, source_target_pairs={{0,4},{4,0},{8,12},{12,8},{1,5},{5,1},{9,13},{13,9},{2,6},{6,2},{1... | collective-permute-start | bytes 393224 | tf_op jit(solution)/shard_map/ppermute | solution.py:477
  45.8 12.3 %collective-permute-start.8 = (bf16[2,2,16,1024]{3,2,1,0:T(8,128)(2,1)S(1)}, bf16[2,2,16,1024]{3,2,1,0:T(8,128)(2,1)S(1)}, u32[]{:S(2)}, u32[]{:S(2)}) collective-permute-start(bf16[2,2,16,1024]{3,2,1,0:T(8,128)(2,1)S(1)} %get-tuple-element.38), channel_id=1, source_target_pairs={{0,8},{4,12},{8,0},{12,4},{1,9},{5,13},{9,1},{13,5},{2,10},{6,14},... | collective-permute-start | bytes 393224 | tf_op jit(solution)/shard_map/ppermute | solution.py:477
  48.4 9.7 %collective-permute-start.9 = (bf16[2,2,16,1024]{3,2,1,0:T(8,128)(2,1)S(1)}, bf16[2,2,16,1024]{3,2,1,0:T(8,128)(2,1)S(1)}, u32[]{:S(2)}, u32[]{:S(2)}) collective-permute-start(bf16[2,2,16,1024]{3,2,1,0:T(8,128)(2,1)S(1)} %get-tuple-element.39), channel_id=1, source_target_pairs={{0,12},{4,8},{8,4},{12,0},{1,13},{5,9},{9,5},{13,1},{2,14},{6,10},... | collective-permute-start | bytes 393224 | tf_op jit(solution)/shard_map/ppermute | solution.py:477
  61.0 11.9 %collective-permute-start.11 = (bf16[2,2,16,1024]{3,2,1,0:T(8,128)(2,1)S(1)}, bf16[2,2,16,1024]{3,2,1,0:T(8,128)(2,1)S(1)}, u32[]{:S(2)}, u32[]{:S(2)}) collective-permute-start(bf16[2,2,16,1024]{3,2,1,0:T(8,128)(2,1)S(1)} %get-tuple-element.42), channel_id=1, source_target_pairs={{0,8},{4,12},{8,0},{12,4},{1,9},{5,13},{9,1},{13,5},{2,10},{6,14},... | collective-permute-start | bytes 393224 | tf_op jit(solution)/shard_map/ppermute | solution.py:477
  64.0 8.9 %collective-permute-start.12 = (bf16[2,2,16,1024]{3,2,1,0:T(8,128)(2,1)S(1)}, bf16[2,2,16,1024]{3,2,1,0:T(8,128)(2,1)S(1)}, u32[]{:S(2)}, u32[]{:S(2)}) collective-permute-start(bf16[2,2,16,1024]{3,2,1,0:T(8,128)(2,1)S(1)} %get-tuple-element.43), channel_id=1, source_target_pairs={{0,12},{4,8},{8,4},{12,0},{1,13},{5,9},{9,5},{13,1},{2,14},{6,10},... | collective-permute-start | bytes 393224 | tf_op jit(solution)/shard_map/ppermute | solution.py:477
  65.4 7.6 %collective-permute-start.13 = (bf16[2,2,16,1024]{3,2,1,0:T(8,128)(2,1)S(1)}, bf16[2,2,16,1024]{3,2,1,0:T(8,128)(2,1)S(1)}, u32[]{:S(2)}, u32[]{:S(2)}) collective-permute-start(bf16[2,2,16,1024]{3,2,1,0:T(8,128)(2,1)S(1)} %get-tuple-element.44), channel_id=1, source_target_pairs={{0,4},{4,0},{8,12},{12,8},{1,5},{5,1},{9,13},{13,9},{2,6},{6,2},{1... | collective-permute-start | bytes 393224 | tf_op jit(solution)/shard_map/ppermute | solution.py:477
  76.3 5.3 %collective-permute-start.14 = (bf16[2,2,64,256]{3,2,1,0:T(8,128)(2,1)}, bf16[2,2,64,256]{3,2,1,0:T(8,128)(2,1)}, u32[]{:S(2)}, u32[]{:S(2)}) collective-permute-start(bf16[2,2,64,256]{3,2,1,0:T(8,128)(2,1)} %get-tuple-element.46), channel_id=1, source_target_pairs={{0,2},{2,0},{1,3},{3,1},{4,6},{6,4},{5,7},{7,5},{8,10},{10,8},{9,1... | collective-permute-start | bytes 393224 | tf_op jit(solution)/shard_map/ppermute | solution.py:477
  77.8 36.3 %copy-start.5 = (f32[4,2,16,1024]{3,2,1,0:T(8,128)S(1)}, f32[4,2,16,1024]{3,2,1,0:T(8,128)}, u32[]{:S(2)}) copy-start(f32[4,2,16,1024]{3,2,1,0:T(8,128)} %copy-done.4) | copy-start | bytes 1572868
  77.8 36.3 %copy-start.9 = (f32[16,1024]{1,0:T(8,128)S(1)}, f32[16,1024]{1,0:T(8,128)}, u32[]{:S(2)}) copy-start(f32[16,1024]{1,0:T(8,128)} %copy-done.8) | copy-start | bytes 196612
  82.6 10.4 %collective-permute-start.15 = (bf16[2,2,64,256]{3,2,1,0:T(8,128)(2,1)S(1)}, bf16[2,2,64,256]{3,2,1,0:T(8,128)(2,1)S(1)}, u32[]{:S(2)}, u32[]{:S(2)}) collective-permute-start(bf16[2,2,64,256]{3,2,1,0:T(8,128)(2,1)S(1)} %add_convert_fusion.1.rest_0_), channel_id=1, source_target_pairs={{0,8},{4,12},{8,0},{12,4},{1,9},{5,13},{9,1},{13,5},{2,10},{6,14},... | collective-permute-start | bytes 393224 | tf_op jit(solution)/shard_map/ppermute | solution.py:477
  84.6 8.4 %collective-permute-start.16 = (bf16[2,2,64,256]{3,2,1,0:T(8,128)(2,1)S(1)}, bf16[2,2,64,256]{3,2,1,0:T(8,128)(2,1)S(1)}, u32[]{:S(2)}, u32[]{:S(2)}) collective-permute-start(bf16[2,2,64,256]{3,2,1,0:T(8,128)(2,1)S(1)} %add_convert_fusion.1.rest_0_), channel_id=1, source_target_pairs={{0,12},{4,8},{8,4},{12,0},{1,13},{5,9},{9,5},{13,1},{2,14},{6,10},... | collective-permute-start | bytes 393224 | tf_op jit(solution)/shard_map/ppermute | solution.py:477
  87.0 6.9 %collective-permute-start.17 = (bf16[2,2,64,256]{3,2,1,0:T(8,128)(2,1)S(1)}, bf16[2,2,64,256]{3,2,1,0:T(8,128)(2,1)S(1)}, u32[]{:S(2)}, u32[]{:S(2)}) collective-permute-start(bf16[2,2,64,256]{3,2,1,0:T(8,128)(2,1)S(1)} %add_convert_fusion.1.rest_0_), channel_id=1, source_target_pairs={{0,4},{4,0},{8,12},{12,8},{1,5},{5,1},{9,13},{13,9},{2,6},{6,2},{1... | collective-permute-start | bytes 393224 | tf_op jit(solution)/shard_map/ppermute | solution.py:477
  94.7 5.0 %collective-permute-start.18 = (bf16[2,2,64,256]{3,2,1,0:T(8,128)(2,1)S(1)}, bf16[2,2,64,256]{3,2,1,0:T(8,128)(2,1)S(1)}, u32[]{:S(2)}, u32[]{:S(2)}) collective-permute-start(bf16[2,2,64,256]{3,2,1,0:T(8,128)(2,1)S(1)} %shard_map.106.n_ref), channel_id=1, source_target_pairs={{0,2},{2,0},{1,3},{3,1},{4,6},{6,4},{5,7},{7,5},{8,10},{10,8},{9,1... | collective-permute-start | bytes 393224 | tf_op jit(solution)/shard_map/ppermute | solution.py:477
  103.6 9.8 %collective-permute-start.19 = (bf16[2,2,16,1024]{3,2,1,0:T(8,128)(2,1)S(1)}, bf16[2,2,16,1024]{3,2,1,0:T(8,128)(2,1)S(1)}, u32[]{:S(2)}, u32[]{:S(2)}) collective-permute-start(bf16[2,2,16,1024]{3,2,1,0:T(8,128)(2,1)S(1)} %get-tuple-element.48), channel_id=1, source_target_pairs={{0,8},{4,12},{8,0},{12,4},{1,9},{5,13},{9,1},{13,5},{2,10},{6,14},... | collective-permute-start | bytes 393224 | tf_op jit(solution)/shard_map/ppermute | solution.py:477
  105.7 7.8 %collective-permute-start.20 = (bf16[2,2,16,1024]{3,2,1,0:T(8,128)(2,1)S(1)}, bf16[2,2,16,1024]{3,2,1,0:T(8,128)(2,1)S(1)}, u32[]{:S(2)}, u32[]{:S(2)}) collective-permute-start(bf16[2,2,16,1024]{3,2,1,0:T(8,128)(2,1)S(1)} %get-tuple-element.49), channel_id=1, source_target_pairs={{0,12},{4,8},{8,4},{12,0},{1,13},{5,9},{9,5},{13,1},{2,14},{6,10},... | collective-permute-start | bytes 393224 | tf_op jit(solution)/shard_map/ppermute | solution.py:477
  107.0 7.2 %collective-permute-start.21 = (bf16[2,2,16,1024]{3,2,1,0:T(8,128)(2,1)S(1)}, bf16[2,2,16,1024]{3,2,1,0:T(8,128)(2,1)S(1)}, u32[]{:S(2)}, u32[]{:S(2)}) collective-permute-start(bf16[2,2,16,1024]{3,2,1,0:T(8,128)(2,1)S(1)} %get-tuple-element.50), channel_id=1, source_target_pairs={{0,4},{4,0},{8,12},{12,8},{1,5},{5,1},{9,13},{13,9},{2,6},{6,2},{1... | collective-permute-start | bytes 393224 | tf_op jit(solution)/shard_map/ppermute | solution.py:477
  116.3 10.0 %collective-permute-start.22 = (bf16[2,2,16,1024]{3,2,1,0:T(8,128)(2,1)S(1)}, bf16[2,2,16,1024]{3,2,1,0:T(8,128)(2,1)S(1)}, u32[]{:S(2)}, u32[]{:S(2)}) collective-permute-start(bf16[2,2,16,1024]{3,2,1,0:T(8,128)(2,1)S(1)} %get-tuple-element.52), channel_id=1, source_target_pairs={{0,8},{4,12},{8,0},{12,4},{1,9},{5,13},{9,1},{13,5},{2,10},{6,14},... | collective-permute-start | bytes 393224 | tf_op jit(solution)/shard_map/ppermute | solution.py:477
  117.4 8.9 %collective-permute-start.23 = (bf16[2,2,16,1024]{3,2,1,0:T(8,128)(2,1)S(1)}, bf16[2,2,16,1024]{3,2,1,0:T(8,128)(2,1)S(1)}, u32[]{:S(2)}, u32[]{:S(2)}) collective-permute-start(bf16[2,2,16,1024]{3,2,1,0:T(8,128)(2,1)S(1)} %get-tuple-element.53), channel_id=1, source_target_pairs={{0,12},{4,8},{8,4},{12,0},{1,13},{5,9},{9,5},{13,1},{2,14},{6,10},... | collective-permute-start | bytes 393224 | tf_op jit(solution)/shard_map/ppermute | solution.py:477
  120.0 7.3 %collective-permute-start.24 = (bf16[2,2,16,1024]{3,2,1,0:T(8,128)(2,1)S(1)}, bf16[2,2,16,1024]{3,2,1,0:T(8,128)(2,1)S(1)}, u32[]{:S(2)}, u32[]{:S(2)}) collective-permute-start(bf16[2,2,16,1024]{3,2,1,0:T(8,128)(2,1)S(1)} %get-tuple-element.54), channel_id=1, source_target_pairs={{0,4},{4,0},{8,12},{12,8},{1,5},{5,1},{9,13},{13,9},{2,6},{6,2},{1... | collective-permute-start | bytes 393224 | tf_op jit(solution)/shard_map/ppermute | solution.py:477
  129.3 5.0 %collective-permute-start.25 = (bf16[2,2,64,256]{3,2,1,0:T(8,128)(2,1)S(1)}, bf16[2,2,64,256]{3,2,1,0:T(8,128)(2,1)S(1)}, u32[]{:S(2)}, u32[]{:S(2)}) collective-permute-start(bf16[2,2,64,256]{3,2,1,0:T(8,128)(2,1)S(1)} %get-tuple-element.56), channel_id=1, source_target_pairs={{0,2},{2,0},{1,3},{3,1},{4,6},{6,4},{5,7},{7,5},{8,10},{10,8},{9,1... | collective-permute-start | bytes 393224 | tf_op jit(solution)/shard_map/ppermute | solution.py:477
  134.3 9.9 %collective-permute-start.26 = (bf16[2,2,64,256]{3,2,1,0:T(8,128)(2,1)S(1)}, bf16[2,2,64,256]{3,2,1,0:T(8,128)(2,1)S(1)}, u32[]{:S(2)}, u32[]{:S(2)}) collective-permute-start(bf16[2,2,64,256]{3,2,1,0:T(8,128)(2,1)S(1)} %add_convert_fusion.rest_0_), channel_id=1, source_target_pairs={{0,8},{4,12},{8,0},{12,4},{1,9},{5,13},{9,1},{13,5},{2,10},{6,14},... | collective-permute-start | bytes 393224 | tf_op jit(solution)/shard_map/ppermute | solution.py:477
  136.5 7.8 %collective-permute-start.27 = (bf16[2,2,64,256]{3,2,1,0:T(8,128)(2,1)S(1)}, bf16[2,2,64,256]{3,2,1,0:T(8,128)(2,1)S(1)}, u32[]{:S(2)}, u32[]{:S(2)}) collective-permute-start(bf16[2,2,64,256]{3,2,1,0:T(8,128)(2,1)S(1)} %add_convert_fusion.rest_0_), channel_id=1, source_target_pairs={{0,12},{4,8},{8,4},{12,0},{1,13},{5,9},{9,5},{13,1},{2,14},{6,10},... | collective-permute-start | bytes 393224 | tf_op jit(solution)/shard_map/ppermute | solution.py:477
  137.8 7.2 %collective-permute-start.28 = (bf16[2,2,64,256]{3,2,1,0:T(8,128)(2,1)S(1)}, bf16[2,2,64,256]{3,2,1,0:T(8,128)(2,1)S(1)}, u32[]{:S(2)}, u32[]{:S(2)}) collective-permute-start(bf16[2,2,64,256]{3,2,1,0:T(8,128)(2,1)S(1)} %add_convert_fusion.rest_0_), channel_id=1, source_target_pairs={{0,4},{4,0},{8,12},{12,8},{1,5},{5,1},{9,13},{13,9},{2,6},{6,2},{1... | collective-permute-start | bytes 393224 | tf_op jit(solution)/shard_map/ppermute | solution.py:477
  (15 other events, 114.7 us)

commit v6 on v5

v6 whole, which is shorter than its diff:
```python
import functools
import math

import jax
import jax.numpy as jnp
import numpy as np
from jax import lax
from jax.experimental import pallas as pl
from jax.experimental.pallas import tpu as pltpu
from jax.sharding import PartitionSpec as P

BLOCK = 128
ITERS = 2
ROWS = 8
CHUNKS = 1
VMEM_BYTES = 16 * 1024 * 1024

BF16 = jnp.bfloat16
F32 = jnp.float32


def ways(count):
    far = sorted(range(1, count), key=lambda step: (step.bit_length() < count.bit_length() - 1, step))
    return [0] + far


def field_rows(place, freq_devs, per_dev):
    rows = []
    for step in ways(freq_devs):
        first = (place ^ step) * per_dev
        for part in range(2):
            rows.extend((part, first + local) for local in range(per_dev))
    return rows


def fields(samples, freq_total):
    phase = (np.arange(1, freq_total + 1)[:, None] * np.arange(samples)[None, :]) % samples
    angle = phase * (2.0 * math.pi / samples)
    return np.stack([np.cos(angle), -np.sin(angle)])


def forward_tables(samples, freq_devs, per_dev):
    table = fields(samples, freq_devs * per_dev)
    own = samples // freq_devs
    out = []
    for place in range(freq_devs):
        part = [table[c, j, place * own : (place + 1) * own] for c, j in field_rows(place, freq_devs, per_dev)]
        out.append(np.repeat(np.stack(part), ROWS, 0))
    return np.stack(out).astype(np.float32).astype(BF16)


def inverse_tables(samples, freq_devs, per_dev):
    out = forward_tables(samples, freq_devs, per_dev).astype(np.float32)
    exact = fields(samples, freq_devs * per_dev) * (2.0 / samples)
    own = samples // freq_devs
    for place in range(freq_devs):
        part = [exact[c, j, place * own : (place + 1) * own] for c, j in field_rows(place, freq_devs, per_dev)]
        out[place] = np.repeat(np.stack(part), ROWS, 0)
    return np.swapaxes(out, 1, 2).astype(BF16)


def window_tables(samples, freq_devs, per_dev):
    freq_total = freq_devs * per_dev
    order = np.arange(1, freq_total + 1)
    unit = 2j * math.pi / samples
    diff = order[None, :] - order[:, None]
    total = order[None, :] + order[:, None]
    same = np.where(diff == 0, 0.0, 1.0 / (samples * (np.exp(unit * np.where(diff == 0, 1, diff)) - 1.0)))
    mixed = 1.0 / (samples * (np.exp(-unit * total) - 1.0))
    full = np.zeros((2, freq_total, 2, freq_total))
    full[0, :, 0, :] = same.real + mixed.real
    full[0, :, 1, :] = mixed.imag - same.imag
    full[1, :, 0, :] = same.imag + mixed.imag
    full[1, :, 1, :] = same.real - mixed.real
    out = []
    for place in range(freq_devs):
        rows = [c * freq_total + j for c, j in field_rows(place, freq_devs, per_dev)]
        flat = full.reshape(2 * freq_total, 2 * freq_total)[np.ix_(rows, rows)]
        out.append(np.kron(flat, np.eye(ROWS)))
    return np.stack(out).astype(np.float32).astype(BF16)


def call(body, scalars, inputs, outputs, grid, scratch=(), aliases=None, flops=0):
    in_arrays = [value for value, _ in inputs]
    bytes_all = sum(v.size * v.dtype.itemsize for v in in_arrays)
    bytes_all += sum(math.prod(s.shape) * s.dtype.itemsize for s, _ in outputs)
    return pl.pallas_call(
        body,
        grid_spec=pltpu.PrefetchScalarGridSpec(
            num_scalar_prefetch=len(scalars),
            grid=grid,
            in_specs=[spec for _, spec in inputs],
            out_specs=[spec for _, spec in outputs],
            scratch_shapes=list(scratch),
        ),
        out_shape=[shape for shape, _ in outputs],
        input_output_aliases=aliases or {},
        compiler_params=pltpu.CompilerParams(vmem_limit_bytes=VMEM_BYTES),
        cost_estimate=pl.CostEstimate(flops=flops, bytes_accessed=bytes_all, transcendentals=0),
    )(*scalars, *in_arrays)


def whole(array):
    zeros = (0,) * array.ndim
    return pl.BlockSpec(array.shape, lambda *_: zeros)


def masked_halves(response, aperture, place):
    per_dev, _, src, rcv = response.shape
    half = src // 2
    steps = half // BLOCK

    def body(place_ref, flags, x_ref, keep, send):
        for flip, out in ((1, send), (0, keep)):
            for step in range(steps):
                block = (place_ref[0] ^ flip) * steps + step
                rows = pl.ds(pl.multiple_of(block * BLOCK, BLOCK), BLOCK)
                to = pl.ds(step * BLOCK, BLOCK)
                for j in range(per_dev):
                    for r in range(rcv // BLOCK):
                        on = flags[j, block, r].astype(F32).astype(BF16)
                        at = pl.ds(r * BLOCK, BLOCK)
                        out[j, :, to, at] = x_ref[j, :, rows, at] * on

    shape = jax.ShapeDtypeStruct((per_dev, 2, half, rcv), BF16)
    return call(body, (place, aperture), [(response, whole(response))], [(shape, whole(shape))] * 2, (1,))


def first_spectra(initial, table, freq_place, freq_devs, per_dev, first, rows):
    own, rcv = initial.shape[1:]
    tile = 2 * ROWS
    count = table.shape[1]

    def body(place_ref, x_ref, t_ref, *rest):
        outs, spread_ref = rest[:freq_devs], rest[freq_devs]
        base = t_ref[place_ref[0]].astype(F32)
        lane = lax.broadcasted_iota(jnp.int32, (count, own), 0) % ROWS
        for row in range(ROWS):
            spread_ref[:, row * own : (row + 1) * own] = jnp.where(lane == row, base, 0.0).astype(BF16)
        for at in range(rows // tile):
            parts = []
            for half in range(2):
                start = first + at * tile + half * ROWS
                flat = x_ref[start : start + ROWS].reshape(ROWS * own, rcv)
                value = jnp.dot(spread_ref[...], flat, preferred_element_type=F32)
                parts.append(value.reshape(freq_devs, 2, per_dev, ROWS, rcv))
            both = jnp.concatenate(parts, 3).astype(BF16)
            for step, out in enumerate(outs):
                out[:, :, at * tile : (at + 1) * tile, :] = both[step]

    shape = jax.ShapeDtypeStruct((2, per_dev, rows, rcv), BF16)
    return call(
        body,
        (freq_place,),
        [(initial, whole(initial)), (table, whole(table))],
        [(shape, whole(shape))] * freq_devs,
        (1,),
        scratch=[pltpu.VMEM((count, ROWS * own), BF16)],
        flops=2 * 2 * freq_devs * per_dev * own * rows * rcv,
    )


def down_products(near, far, responses, freq_place, freq_devs):
    _, per_dev, rows, rcv = near.shape
    width = responses[0][0].shape[2]
    tile = min(width, 256)
    share = rows // freq_devs

    def body(place_ref, n_ref, f_ref, k0, m0, k1, m1, *rest):
        outs, held = rest[:freq_devs], rest[freq_devs]
        sides = []
        for ref in (n_ref, f_ref):
            for j in range(per_dev):
                real, imag = ref[0, j], ref[1, j]
                sides.append((jnp.concatenate([real, imag], 0), jnp.concatenate([-imag, real], 0)))
        for half, pair in enumerate(((k0, m0), (k1, m1))):
            for at in range(width // tile):
                cut = slice(at * tile, (at + 1) * tile)
                for j in range(per_dev):
                    total = None
                    for side, resp in enumerate(pair):
                        for part, lhs in enumerate(sides[side * per_dev + j]):
                            term = lax.dot_general(
                                lhs, resp[j, part, cut], (((1,), (1,)), ((), ())), preferred_element_type=F32
                            )
                            total = term if total is None else total + term
                    held[0, j] = total[:rows]
                    held[1, j] = total[rows:]
                to = slice(half * width + at * tile, half * width + (at + 1) * tile)
                for way, out in zip(ways(freq_devs), outs):
                    start = pl.multiple_of((place_ref[0] ^ way) * share, share)
                    out[:, :, :, to] = held[:, :, pl.ds(start, share), :].astype(BF16)

    shape = jax.ShapeDtypeStruct((2, per_dev, share, 2 * width), BF16)
    (k0, m0), (k1, m1) = responses
    return call(
        body,
        (freq_place,),
        [(v, whole(v)) for v in (near, far, k0, m0, k1, m1)],
        [(shape, whole(shape))] * freq_devs,
        (1,),
        scratch=[pltpu.VMEM((2, per_dev, rows, tile), F32)],
        flops=2 * 8 * per_dev * rows * 2 * width * rcv,
    )


def mixed_fields(plain, cos, sin, matrix):
    tile = plain[0].shape[-1]
    turned = [
        jnp.stack([v[0] * c - v[1] * s, v[0] * s + v[1] * c]) for v, c, s in zip(plain, cos, sin)
    ]
    flat = [jnp.stack(v).reshape(matrix.shape[1], tile).astype(BF16) for v in (turned, plain)]
    mixed = jnp.dot(matrix, jnp.concatenate(flat, 1), preferred_element_type=F32)
    shape = (-1, 2) + plain[0].shape[1:]
    return mixed[:, :tile].reshape(shape), mixed[:, tile:].reshape(shape)


def unturned(up, low, value, cos, sin, part):
    real = cos * up[0] + sin * up[1] - low[0] + part * value[0]
    imag = cos * up[1] - sin * up[0] - low[1] + part * value[1]
    return jnp.stack([real, imag])


def tiles(width, body):
    def at(step, carry):
        body(pl.ds(pl.multiple_of(step * BLOCK, BLOCK), BLOCK))
        return carry

    lax.fori_loop(0, width // BLOCK, at, 0)


def windowed(messages, tables, matrix, freq_place, per_dev, share):
    cosines, sines, fraction = tables
    freq_devs = len(messages)
    width = messages[0].shape[-1]
    count = freq_devs * 2 * per_dev * ROWS

    def body(place_ref, c_ref, s_ref, f_ref, g_ref, *rest):
        refs, outs = rest[:freq_devs], rest[freq_devs:]
        matrix_here = g_ref[place_ref[0]]

        def one(at):
            data = [ref[:, :, :, at].astype(F32) for ref in refs]
            made = [[] for _ in outs]
            for first in range(0, share, ROWS):
                cut = slice(first, first + ROWS)
                plain = [value[:, :, cut] for value in data]
                cos = [c_ref[step, :, cut, at] for step in range(freq_devs)]
                sin = [s_ref[step, :, cut, at] for step in range(freq_devs)]
                up, low = mixed_fields(plain, cos, sin, matrix_here)
                part = f_ref[cut, at]
                for step in range(freq_devs):
                    made[step].append(unturned(up[step], low[step], plain[step], cos[step], sin[step], part))
            for out, value in zip(outs, made):
                out[:, :, :, at] = jnp.concatenate(value, 2).astype(BF16)

        tiles(width, one)

    inputs = (cosines, sines, fraction, matrix, *messages)
    return call(
        body,
        (freq_place,),
        [(v, whole(v)) for v in inputs],
        [(jax.ShapeDtypeStruct(v.shape, BF16), whole(v)) for v in messages],
        (1,),
        flops=2 * count * count * 2 * width * share // ROWS,
    )


def up_products(messages, responses, freq_place, rows):
    freq_devs = len(messages)
    (k0, m0), (k1, m1) = responses
    per_dev, _, src, rcv = k0.shape
    share = messages[0].shape[2]

    def body(place_ref, k0_ref, m0_ref, k1_ref, m1_ref, *rest):
        refs = rest[:freq_devs]
        keep, send, held = rest[freq_devs:]
        for way, ref in zip(ways(freq_devs), refs):
            start = pl.multiple_of((place_ref[0] ^ way) * share, share)
            held[:, :, pl.ds(start, share), :] = ref[...]
        for j in range(per_dev):
            for out, pair in ((send, (m0_ref, m1_ref)), (keep, (k0_ref, k1_ref))):
                total = None
                for half, resp in enumerate(pair):
                    cut = slice(half * src, (half + 1) * src)
                    real, imag = held[0, j, :, cut], held[1, j, :, cut]
                    for part, lhs in ((0, [real, imag]), (1, [imag, -real])):
                        term = jnp.dot(jnp.concatenate(lhs, 0), resp[j, part], preferred_element_type=F32)
                        total = term if total is None else total + term
                for part in range(2):
                    out[part, j] = total[rows * part : rows * (part + 1)].astype(out.dtype)

    shapes = [jax.ShapeDtypeStruct((2, per_dev, rows, rcv), kind) for kind in (F32, BF16)]
    return call(
        body,
        (freq_place,),
        [(v, whole(v)) for v in (k0, m0, k1, m1, *messages)],
        [(v, whole(v)) for v in shapes],
        (1,),
        scratch=[pltpu.VMEM((2, per_dev, rows, 2 * src), BF16)],
        flops=2 * 8 * per_dev * rows * 2 * src * rcv,
    )


def next_spectra(sums, messages, tables, matrix, freq_place):
    cosines, sines, fraction = tables
    freq_devs = len(messages)
    _, per_dev, rows, rcv = sums.shape
    count = freq_devs * 2 * per_dev * ROWS
    own = 2 * per_dev * ROWS

    def body(place_ref, u_ref, c_ref, s_ref, f_ref, g_ref, *rest):
        refs, out = rest[:freq_devs], rest[freq_devs]
        matrix_here = g_ref[place_ref[0], :own]

        def one(at):
            for base in range(0, rows, 2 * ROWS):
                pair = slice(base, base + 2 * ROWS)
                data = [ref[:, :, pair, at].astype(F32) for ref in refs]
                made = []
                for half in range(2):
                    plain = [value[:, :, half * ROWS : (half + 1) * ROWS] for value in data]
                    cut = slice(base + half * ROWS, base + (half + 1) * ROWS)
                    cos = [c_ref[step, :, cut, at] for step in range(freq_devs)]
                    sin = [s_ref[step, :, cut, at] for step in range(freq_devs)]
                    up, low = mixed_fields(plain, cos, sin, matrix_here)
                    made.append(unturned(up[0], low[0], plain[0], cos[0], sin[0], f_ref[cut, at]))
                out[:, :, pair, at] = (u_ref[:, :, pair, at] - jnp.concatenate(made, 2)).astype(BF16)

        tiles(rcv, one)

    inputs = (sums, cosines, sines, fraction, matrix, *messages)
    (out,) = call(
        body,
        (freq_place,),
        [(v, whole(v)) for v in inputs],
        [(jax.ShapeDtypeStruct(sums.shape, BF16), whole(sums))],
        (1,),
        flops=2 * own * count * 2 * rcv * rows // ROWS,
    )
    return out


def updated(initial, onset, messages, table, freq_place, focal_first, first, rows, target):
    freq_devs = len(messages)
    own, rcv = initial.shape[1:]
    per_dev = messages[0].shape[1]
    tile = 2 * ROWS
    count = table.shape[2]

    def body(place_ref, focal_ref, x_ref, o_ref, t_ref, *rest):
        refs = rest[:freq_devs]
        out, spread_ref = rest[-2:]
        step = pl.program_id(0)

        @pl.when(step == 0)
        def _():
            base = t_ref[place_ref[0]].astype(F32)
            lane = lax.broadcasted_iota(jnp.int32, (own, count), 1) % ROWS
            for row in range(ROWS):
                spread_ref[row * own : (row + 1) * own] = jnp.where(lane == row, base, 0.0).astype(BF16)

        here = pl.ds(pl.multiple_of(step * tile, tile), tile)
        data = [ref[:, :, here, :].astype(F32) for ref in refs]
        onsets = o_ref[pl.ds(pl.multiple_of(focal_ref[0] + first + step * tile, tile), tile), :]
        time = lax.broadcasted_iota(jnp.int32, (own, rcv), 0) + place_ref[0] * own
        for half in range(2):
            cut = slice(half * ROWS, (half + 1) * ROWS)
            flat = jnp.stack([v[:, :, cut] for v in data]).reshape(count, rcv).astype(BF16)
            change = jnp.dot(spread_ref[...], flat, preferred_element_type=F32)
            for row in range(ROWS):
                spot = half * ROWS + row
                on = time < onsets[spot : spot + 1, :]
                moved = jnp.where(on, change[row * own : (row + 1) * own], 0.0)
                out[spot] = (x_ref[first + step * tile + spot].astype(F32) - moved).astype(BF16)

    inputs = [(v, whole(v)) for v in (initial, onset, table, *messages)]
    aliases = {}
    if target is not None:
        inputs.append((target, pl.BlockSpec(memory_space=pl.ANY)))
        aliases = {2 + len(inputs) - 1: 0}
    (out,) = call(
        body,
        (freq_place, focal_first),
        inputs,
        [(jax.ShapeDtypeStruct(initial.shape, BF16), pl.BlockSpec((tile, own, rcv), lambda i, *_: (first // tile + i, 0, 0)))],
        (rows // tile,),
        scratch=[pltpu.VMEM((ROWS * own, count), BF16)],
        aliases=aliases,
        flops=2 * 2 * freq_devs * per_dev * own * rows * rcv,
    )
    return out


def exchanged(value, axis, step):
    return lax.ppermute(value, axis, [(i, i ^ step) for i in range(lax.axis_size(axis))])


def dealt_out(parts):
    return [exchanged(part, "freq", step) if step else part for part, step in zip(parts, ways(len(parts)))]


def spread(value, count):
    return dealt_out([value] * count)


def phases(onset, freq_index, freq_devs, per_dev, samples):
    steps = jnp.asarray(ways(freq_devs), jnp.int32)
    order = (freq_index ^ steps)[:, None] * per_dev + lax.iota(jnp.int32, per_dev)[None, :] + 1
    phase = order[:, :, None, None] * onset[None, None] % samples
    angle = phase.astype(F32) * (2.0 * math.pi / samples)
    return jnp.cos(angle), jnp.sin(angle), onset.astype(F32) * (1.0 / samples)


def on_device(initial, response, aperture, onset_rcv, onset_src):
    freq_devs = lax.axis_size("freq")
    per_dev = response.shape[0]
    samples = initial.shape[1] * freq_devs
    half_rows = initial.shape[0]
    src_width = response.shape[2] // 2
    rows = half_rows // CHUNKS
    share = rows // freq_devs
    freq_index = lax.axis_index("freq")
    rblk_index = lax.axis_index("rblk")
    sblk_index = lax.axis_index("sblk")
    freq_place = freq_index.reshape(1)
    rblk_place = rblk_index.reshape(1)

    kept, moved = masked_halves(response, aperture, rblk_place)
    moved = exchanged(moved, "rblk", 1)
    kept_pair = exchanged(kept, "sblk", 1)
    responses = None
    forward = jnp.asarray(forward_tables(samples, freq_devs, per_dev))
    inverse = jnp.asarray(inverse_tables(samples, freq_devs, per_dev))
    matrix = jnp.asarray(window_tables(samples, freq_devs, per_dev))

    result = None
    for chunk in range(CHUNKS):
        first = chunk * rows
        parts = first_spectra(initial, forward, freq_place, freq_devs, per_dev, first, rows)
        sums = sum(v.astype(F32) for v in dealt_out(parts))
        spectra = sums.astype(BF16)
        far = exchanged(spectra, "rblk", 1)
        if responses is None:
            moved, far = lax.optimization_barrier((moved, far))
            responses = ((kept, moved), (kept_pair, exchanged(moved, "sblk", 1)))

        def src_onsets(core):
            spot = core * half_rows + first + freq_index * share
            return lax.dynamic_slice(onset_src, (spot, rblk_index * src_width), (share, src_width))

        onsets = [src_onsets(sblk_index), exchanged(src_onsets(1 - sblk_index), "sblk", 1)]
        src_tables = phases(jnp.concatenate(onsets, 1), freq_index, freq_devs, per_dev, samples)
        onsets = lax.dynamic_slice_in_dim(onset_rcv, sblk_index * half_rows + first, rows, 0)
        rcv_tables = phases(onsets, freq_index, freq_devs, per_dev, samples)

        for step in range(ITERS):
            far = far if step == 0 else exchanged(spectra, "rblk", 1)
            messages = dealt_out(down_products(spectra, far, responses, freq_place, freq_devs))
            messages = windowed(messages, src_tables, matrix, freq_place, per_dev, share)
            keep, send = up_products(dealt_out(messages), responses, freq_place, rows)
            back = (keep + exchanged(send, "rblk", 1).astype(F32)).astype(BF16)
            messages = spread(back, freq_devs)
            if step < ITERS - 1:
                spectra = next_spectra(sums, messages, rcv_tables, matrix, freq_place)
            else:
                tile_first = (sblk_index * half_rows).reshape(1)
                result = updated(
                    initial, onset_rcv, messages, inverse, freq_place, tile_first, first, rows, result
                )
    return result


def transform_tables(length, count):
    table = fields(length, count).reshape(2 * count, length)
    forward_table = jnp.asarray(table.astype(np.float32).astype(BF16))
    inverse_table = jnp.asarray((table.T * (2.0 / length)).astype(np.float32).astype(BF16))
    return forward_table, inverse_table


def settle(values):
    return lax.optimization_barrier(values.astype(BF16)).astype(F32)


def samples_into_spectra(values, forward_table, freq_total):
    out = jnp.einsum("kt,ptn->pkn", forward_table, values, preferred_element_type=F32)
    return out.reshape(values.shape[0], 2, freq_total, values.shape[2]).astype(BF16)


def spectra_into_samples(trace_spectra, inverse_table):
    flat = trace_spectra.reshape(trace_spectra.shape[0], -1, trace_spectra.shape[3])
    return jnp.einsum("tk,pkn->ptn", inverse_table, flat, preferred_element_type=F32)


def dense(spec, gated, real, imag, sign):
    dot = functools.partial(jnp.einsum, spec, preferred_element_type=F32)
    return jnp.stack(
        [dot(gated[:, 0], real) - sign * dot(gated[:, 1], imag), dot(gated[:, 0], imag) + sign * dot(gated[:, 1], real)], 1
    )


def general_device(initial, response, aperture, onset_rcv, onset_src):
    freq_devs, rblk_devs, sblk_devs = (lax.axis_size(a) for a in ("freq", "rblk", "sblk"))
    freq_index, rblk_index, sblk_index = (lax.axis_index(a) for a in ("freq", "rblk", "sblk"))
    freq_total = response.shape[0] * freq_devs
    samples = initial.shape[1] * freq_devs
    focal_all = onset_rcv.shape[0]
    forward_table, inverse_table = transform_tables(samples, freq_total)
    steps_axis = lax.iota(jnp.int32, samples)
    own_axis = freq_index * initial.shape[1] + lax.iota(jnp.int32, initial.shape[1])
    half_rows = focal_all // sblk_devs
    own_onsets = lax.dynamic_slice_in_dim(onset_rcv, sblk_index * half_rows, half_rows, 0)
    rcv_gate = (own_axis[None, :, None] < own_onsets[:, None, :]).astype(F32)
    src_rows = focal_all // (rblk_devs * freq_devs)
    src_first = rblk_index * (focal_all // rblk_devs) + freq_index * src_rows
    src_onsets = lax.dynamic_slice_in_dim(onset_src, src_first, src_rows, 0)
    src_gate = (steps_axis[None, :, None] < src_onsets[:, None, :]).astype(F32)
    mask_full = jnp.repeat(jnp.repeat(aperture, BLOCK, 1), BLOCK, 2).astype(BF16)
    gated = response * mask_full[:, None]
    own_forward = lax.dynamic_slice_in_dim(forward_table, freq_index * initial.shape[1], initial.shape[1], 1)
    own_inverse = lax.dynamic_slice_in_dim(inverse_table, freq_index * initial.shape[1], initial.shape[1], 0)
    current = initial
    for _ in range(ITERS):
        partial = samples_into_spectra(current, own_forward, freq_total)
        spec_back = lax.psum_scatter(partial.astype(F32), "freq", scatter_dimension=2, tiled=True).astype(BF16)
        spec_all = lax.all_gather(spec_back, "sblk", axis=0, tiled=True)
        down = lax.psum_scatter(
            settle(dense("euk,bek->beu", gated, spec_all[:, 0], spec_all[:, 1], 1.0)).astype(BF16),
            "rblk",
            scatter_dimension=0,
            tiled=True,
        )
        src_traces = lax.all_to_all(down, "freq", split_axis=0, concat_axis=2, tiled=True)
        upgoing = (src_gate * spectra_into_samples(src_traces, inverse_table)).astype(BF16)
        upspec = samples_into_spectra(upgoing, forward_table, freq_total)
        up_back = lax.all_to_all(upspec, "freq", split_axis=2, concat_axis=0, tiled=True)
        up_all = lax.all_gather(up_back, "rblk", axis=0, tiled=True)
        sums = dense("qao,bqa->bqo", gated, up_all[:, 0], up_all[:, 1], -1.0).astype(BF16)
        back = lax.psum_scatter(sums, "sblk", scatter_dimension=0, tiled=True)
        traces = lax.all_gather(back, "freq", axis=2, tiled=True)
        update = rcv_gate * spectra_into_samples(traces, own_inverse)
        current = (initial.astype(F32) - update).astype(BF16)
    return current


def fits(initial, response, aperture, onset_rcv, onset_src):
    freq_devs = lax.axis_size("freq")
    if lax.axis_size("rblk") != 2 or lax.axis_size("sblk") != 2 or freq_devs & (freq_devs - 1):
        return False
    rows = initial.shape[0] // CHUNKS
    whole_rows = initial.shape[0] % CHUNKS == 0 and rows % (2 * ROWS * freq_devs) == 0
    whole_width = response.shape[2] % (4 * BLOCK) == 0 and response.shape[3] % BLOCK == 0
    return whole_rows and whole_width and onset_rcv.shape[0] == 2 * initial.shape[0]


def chosen(*arrays):
    return on_device(*arrays) if fits(*arrays) else general_device(*arrays)


def solution(mesh):
    in_specs = (
        P(("group", "sblk"), "freq", "rblk"),
        P(("group", "freq"), None, "sblk", "rblk"),
        P(("group", "freq"), "sblk", "rblk"),
        P("group", "rblk"),
        P("group", "sblk"),
    )
    out_specs = P(("group", "sblk"), "freq", "rblk")
    return jax.shard_map(chosen, mesh=mesh, in_specs=in_specs, out_specs=out_specs, check_vma=False)
```

time: 153 us -> 146 us (0.954)
  Pallas kernels: 31.2 us -> 19.9 us
  waiting for transfers between devices: 65.2 us -> 70.5 us
    pallas_call x11 -> x10, Pallas kernels: 31.2 us -> 19.9 us  [call(): pl.pallas_call(body, grid_spec=pltpu.PrefetchScalarGridSpec(num_scalar_pr...]
    ppermute x29, waiting for transfers between devices: 65.2 us -> 70.5 us  [exchanged(): lax.ppermute(value, axis, [(i, i ^ step) for i in range(lax.axis_size(axi...]
    unnamed x37 -> x39, local copies, waits for them, and re-layouts: 9.46 us -> 10.1 us
  transfers between devices with their start and end apart: 29 -> 29, of which waited for: 18 -> 20; matrix products, arithmetic and copies ran while one was open for 4% -> 4% of each run, Pallas kernels for 2% -> 0%
where the time goes in v6:
time: 146 us; the launch traced here: 145 us
  waiting for transfers between devices  70.5 us (48%)
  starting transfers between devices  37.3 us (26%)
  Pallas kernels  19.9 us (14%)
  local copies, waits for them, and re-layouts  10.9 us (7%)
  other arithmetic  6.35 us (4%)
    ppermute x29, waiting for transfers between devices, exchanged(): lax.ppermute(value, axis, [(i, i ^ step) for i in range(lax.axis_size(axi...  70.5 us
    ppermute x29, starting transfers between devices, exchanged(): lax.ppermute(value, axis, [(i, i ^ step) for i in range(lax.axis_size(axi...  37.3 us
    pallas_call x10, Pallas kernels, call(): pl.pallas_call(body, grid_spec=pltpu.PrefetchScalarGridSpec(num_scalar_pr...  19.9 us
    unnamed x39, local copies, waits for them, and re-layouts  10.1 us
    sin x2, other arithmetic, phases(): return (jnp.cos(angle), jnp.sin(angle), onset.astype(F32) * (1.0 / samples))  4.21 us
  transfers between devices with their start and end apart: 29, of which 20 were waited for; matrix products, arithmetic and copies ran while one was open for 4% of the time, Pallas kernels for 0%

profile of v6, /device:TPU:0, one launch (start us, length us, event | category | flops | bytes accessed | tf_op | source)
XLA Modules:
  0.0 145.2 jit_solution(12601780465634925000)
XLA Ops:
  2.4 2.0 %shard_map.100 = (bf16[2,2,512,256]{3,2,1,0:T(8,128)(2,1)S(1)}, bf16[2,2,512,256]{3,2,1,0:T(8,128)(2,1)}) custom-call(s32[1]{0:T(128)} %bitcast.2.place_ref, s32[2,8,2]{2,1,0:T(8,128)S(1)} %copy.11.flags, bf16[2,2,1024,256]{3,2,1,0:T(8,128)(2,1)S(1)} %copy-done.6), custom_call_target="tpu_custom_call" | custom-call | bytes 4194304 | tf_op jit(solution)/shard_map/pallas_call | solution.py:87
  4.4 2.9 %collective-permute-start = (bf16[2,2,512,256]{3,2,1,0:T(8,128)(2,1)}, bf16[2,2,512,256]{3,2,1,0:T(8,128)(2,1)S(1)}, u32[]{:S(2)}, u32[]{:S(2)}) collective-permute-start(bf16[2,2,512,256]{3,2,1,0:T(8,128)(2,1)} %get-tuple-element.34), channel_id=1, source_target_pairs={{0,2},{2,0},{1,3},{3,1},{4,6},{6,4},{5,7},{7,5},{8,10},{10,8},{9,1... | collective-permute-start | bytes 3145736 | tf_op jit(solution)/shard_map/ppermute | solution.py:397
  7.3 2.2 %copy-done = bf16[64,128,256]{2,1,0:T(8,128)(2,1)S(1)} copy-done((bf16[64,128,256]{2,1,0:T(8,128)(2,1)S(1)}, bf16[64,128,256]{2,1,0:T(8,128)(2,1)}, u32[]{:S(2)}) %copy-start) | copy-done | bytes 4194328
  11.2 2.7 %collective-permute-start.1 = (bf16[2,2,64,256]{3,2,1,0:T(8,128)(2,1)S(1)}, bf16[2,2,64,256]{3,2,1,0:T(8,128)(2,1)S(1)}, u32[]{:S(2)}, u32[]{:S(2)}) collective-permute-start(bf16[2,2,64,256]{3,2,1,0:T(8,128)(2,1)S(1)} %get-tuple-element.36), channel_id=1, source_target_pairs={{0,8},{4,12},{8,0},{12,4},{1,9},{5,13},{9,1},{13,5},{2,10},{6,14},... | collective-permute-start | bytes 393224 | tf_op jit(solution)/shard_map/ppermute | solution.py:397
  15.4 8.5 %collective-permute-done.1 = bf16[2,2,64,256]{3,2,1,0:T(8,128)(2,1)S(1)} collective-permute-done((bf16[2,2,64,256]{3,2,1,0:T(8,128)(2,1)S(1)}, bf16[2,2,64,256]{3,2,1,0:T(8,128)(2,1)S(1)}, u32[]{:S(2)}, u32[]{:S(2)}) %collective-permute-start.1) | collective-permute-done | bytes 131104 | tf_op jit(solution)/shard_map/ppermute | solution.py:397
  25.4 8.1 %collective-permute-done.4.f_ref = bf16[2,2,64,256]{3,2,1,0:T(8,128)(2,1)S(1)} collective-permute-done((bf16[2,2,64,256]{3,2,1,0:T(8,128)(2,1)S(1)}, bf16[2,2,64,256]{3,2,1,0:T(8,128)(2,1)S(1)}, u32[]{:S(2)}, u32[]{:S(2)}) %collective-permute-start.4) | collective-permute-done | bytes 131104 | tf_op jit(solution)/shard_map/ppermute | solution.py:397
  38.8 2.7 %shard_map.102 = (bf16[2,2,16,1024]{3,2,1,0:T(8,128)(2,1)S(1)}, bf16[2,2,16,1024]{3,2,1,0:T(8,128)(2,1)S(1)}, bf16[2,2,16,1024]{3,2,1,0:T(8,128)(2,1)S(1)}, bf16[2,2,16,1024]{3,2,1,0:T(8,128)(2,1)S(1)}) custom-call(s32[1]{0:T(128)} %bitcast.place_ref, bf16[2,2,64,256]{3,2,1,0:T(8,128)(2,1)S(1)} %copy-done.11, bf16[2,2,64,256]{3,2,1,0:T(8,128)(2,1)S(1)} %copy-done.16, ...), custom_call_target="tpu_custom_call" | custom-call | flops 536870912 | bytes 4980736 | tf_op jit(solution)/shard_map/pallas_call | solution.py:87
  41.5 1.9 %collective-permute-start.10 = (bf16[2,2,16,1024]{3,2,1,0:T(8,128)(2,1)S(1)}, bf16[2,2,16,1024]{3,2,1,0:T(8,128)(2,1)S(1)}, u32[]{:S(2)}, u32[]{:S(2)}) collective-permute-start(bf16[2,2,16,1024]{3,2,1,0:T(8,128)(2,1)S(1)} %get-tuple-element.44), channel_id=1, source_target_pairs={{0,4},{4,0},{8,12},{12,8},{1,5},{5,1},{9,13},{13,9},{2,6},{6,2},{1... | collective-permute-start | bytes 393224 | tf_op jit(solution)/shard_map/ppermute | solution.py:397
  43.4 2.6 %collective-permute-start.8 = (bf16[2,2,16,1024]{3,2,1,0:T(8,128)(2,1)S(1)}, bf16[2,2,16,1024]{3,2,1,0:T(8,128)(2,1)S(1)}, u32[]{:S(2)}, u32[]{:S(2)}) collective-permute-start(bf16[2,2,16,1024]{3,2,1,0:T(8,128)(2,1)S(1)} %get-tuple-element.42), channel_id=1, source_target_pairs={{0,8},{4,12},{8,0},{12,4},{1,9},{5,13},{9,1},{13,5},{2,10},{6,14},... | collective-permute-start | bytes 393224 | tf_op jit(solution)/shard_map/ppermute | solution.py:397
  46.0 2.1 %fusion.8 = (f32[4,2,16,1024]{3,2,1,0:T(8,128)S(1)}, f32[4,2,16,1024]{3,2,1,0:T(8,128)S(1)}) fusion(s32[16,1024]{1,0:T(8,128)S(1)} %pad_add_fusion, s32[4,2]{1,0:T(4,128)S(1)} %add_add_fusion), kind=kLoop, calls=%fused_computation.20 | loop fusion | flops 1835008 | bytes 1114144 | tf_op jit(solution)/shard_map/sin | solution.py:413
  49.1 7.2 %collective-permute-done.8.rest_1_ = bf16[2,2,16,1024]{3,2,1,0:T(8,128)(2,1)S(1)} collective-permute-done((bf16[2,2,16,1024]{3,2,1,0:T(8,128)(2,1)S(1)}, bf16[2,2,16,1024]{3,2,1,0:T(8,128)(2,1)S(1)}, u32[]{:S(2)}, u32[]{:S(2)}) %collective-permute-start.8) | collective-permute-done | bytes 131104 | tf_op jit(solution)/shard_map/ppermute | solution.py:397
  56.3 1.6 %shard_map.103 = (bf16[2,2,16,1024]{3,2,1,0:T(8,128)(2,1)S(1)}, bf16[2,2,16,1024]{3,2,1,0:T(8,128)(2,1)S(1)}, bf16[2,2,16,1024]{3,2,1,0:T(8,128)(2,1)S(1)}, bf16[2,2,16,1024]{3,2,1,0:T(8,128)(2,1)S(1)}) custom-call(s32[1]{0:T(128)} %bitcast.place_ref, f32[4,2,16,1024]{3,2,1,0:T(8,128)S(1)} %get-tuple-element.70.c_ref, ...), custom_call_target="tpu_custom_call" | custom-call | flops 134217728 | bytes 2293760 | tf_op jit(solution)/shard_map/pallas_call | solution.py:87
  58.7 3.3 %collective-permute-start.11 = (bf16[2,2,16,1024]{3,2,1,0:T(8,128)(2,1)S(1)}, bf16[2,2,16,1024]{3,2,1,0:T(8,128)(2,1)S(1)}, u32[]{:S(2)}, u32[]{:S(2)}) collective-permute-start(bf16[2,2,16,1024]{3,2,1,0:T(8,128)(2,1)S(1)} %get-tuple-element.46), channel_id=1, source_target_pairs={{0,8},{4,12},{8,0},{12,4},{1,9},{5,13},{9,1},{13,5},{2,10},{6,14},... | collective-permute-start | bytes 393224 | tf_op jit(solution)/shard_map/ppermute | solution.py:397
  63.4 8.2 %collective-permute-done.11.rest_1_ = bf16[2,2,16,1024]{3,2,1,0:T(8,128)(2,1)S(1)} collective-permute-done((bf16[2,2,16,1024]{3,2,1,0:T(8,128)(2,1)S(1)}, bf16[2,2,16,1024]{3,2,1,0:T(8,128)(2,1)S(1)}, u32[]{:S(2)}, u32[]{:S(2)}) %collective-permute-start.11) | collective-permute-done | bytes 131104 | tf_op jit(solution)/shard_map/ppermute | solution.py:397
  71.7 2.6 %shard_map.104 = (f32[2,2,64,256]{3,2,1,0:T(8,128)S(1)}, bf16[2,2,64,256]{3,2,1,0:T(8,128)(2,1)}) custom-call(s32[1]{0:T(128)} %bitcast.place_ref, bf16[2,2,512,256]{3,2,1,0:T(8,128)(2,1)S(1)} %get-tuple-element.33.k0.k0_ref, bf16[2,2,512,256]{3,2,1,0:T(8,128)(2,1)S(1)} %collective-permute-done.m0.m0_ref, ...), custom_call_target="tpu_custom_call" | custom-call | flops 536870912 | bytes 5111808 | tf_op jit(solution)/shard_map/pallas_call | solution.py:87
  77.5 2.8 %collective-permute-done.14 = bf16[2,2,64,256]{3,2,1,0:T(8,128)(2,1)} collective-permute-done((bf16[2,2,64,256]{3,2,1,0:T(8,128)(2,1)}, bf16[2,2,64,256]{3,2,1,0:T(8,128)(2,1)}, u32[]{:S(2)}, u32[]{:S(2)}) %collective-permute-start.14) | collective-permute-done | bytes 131104 | tf_op jit(solution)/shard_map/ppermute | solution.py:397
  81.3 2.0 %collective-permute-start.15 = (bf16[2,2,64,256]{3,2,1,0:T(8,128)(2,1)S(1)}, bf16[2,2,64,256]{3,2,1,0:T(8,128)(2,1)S(1)}, u32[]{:S(2)}, u32[]{:S(2)}) collective-permute-start(bf16[2,2,64,256]{3,2,1,0:T(8,128)(2,1)S(1)} %add_convert_fusion.1.rest_0_), channel_id=1, source_target_pairs={{0,8},{4,12},{8,0},{12,4},{1,9},{5,13},{9,1},{13,5},{2,10},{6,14},... | collective-permute-start | bytes 393224 | tf_op jit(solution)/shard_map/ppermute | solution.py:397
  83.3 2.5 %collective-permute-start.16 = (bf16[2,2,64,256]{3,2,1,0:T(8,128)(2,1)S(1)}, bf16[2,2,64,256]{3,2,1,0:T(8,128)(2,1)S(1)}, u32[]{:S(2)}, u32[]{:S(2)}) collective-permute-start(bf16[2,2,64,256]{3,2,1,0:T(8,128)(2,1)S(1)} %add_convert_fusion.1.rest_0_), channel_id=1, source_target_pairs={{0,12},{4,8},{8,4},{12,0},{1,13},{5,9},{9,5},{13,1},{2,14},{6,10},... | collective-permute-start | bytes 393224 | tf_op jit(solution)/shard_map/ppermute | solution.py:397
  85.8 2.1 %fusion.6 = (f32[4,2,64,256]{3,2,1,0:T(8,128)S(1)}, f32[4,2,64,256]{3,2,1,0:T(8,128)S(1)}) fusion(s32[64,256]{1,0:T(8,128)S(1)} %get-tuple-element.62, s32[4,2]{1,0:T(4,128)S(1)} %add_add_fusion), kind=kLoop, calls=%fused_computation.18 | loop fusion | flops 1835008 | bytes 1114144 | tf_op jit(solution)/shard_map/sin | solution.py:413
  87.9 3.9 %collective-permute-done.15.rest_1_ = bf16[2,2,64,256]{3,2,1,0:T(8,128)(2,1)S(1)} collective-permute-done((bf16[2,2,64,256]{3,2,1,0:T(8,128)(2,1)S(1)}, bf16[2,2,64,256]{3,2,1,0:T(8,128)(2,1)S(1)}, u32[]{:S(2)}, u32[]{:S(2)}) %collective-permute-start.15) | collective-permute-done | bytes 131104 | tf_op jit(solution)/shard_map/ppermute | solution.py:397
  94.8 3.4 %collective-permute-done.18.f_ref = bf16[2,2,64,256]{3,2,1,0:T(8,128)(2,1)S(1)} collective-permute-done((bf16[2,2,64,256]{3,2,1,0:T(8,128)(2,1)S(1)}, bf16[2,2,64,256]{3,2,1,0:T(8,128)(2,1)S(1)}, u32[]{:S(2)}, u32[]{:S(2)}) %collective-permute-start.18) | collective-permute-done | bytes 131104 | tf_op jit(solution)/shard_map/ppermute | solution.py:397
  98.2 2.7 %shard_map.106 = (bf16[2,2,16,1024]{3,2,1,0:T(8,128)(2,1)S(1)}, bf16[2,2,16,1024]{3,2,1,0:T(8,128)(2,1)S(1)}, bf16[2,2,16,1024]{3,2,1,0:T(8,128)(2,1)S(1)}, bf16[2,2,16,1024]{3,2,1,0:T(8,128)(2,1)S(1)}) custom-call(s32[1]{0:T(128)} %bitcast.place_ref, bf16[2,2,64,256]{3,2,1,0:T(8,128)(2,1)S(1)} %shard_map.105.n_ref, ...), custom_call_target="tpu_custom_call" | custom-call | flops 536870912 | bytes 4980736 | tf_op jit(solution)/shard_map/pallas_call | solution.py:87
  101.0 2.1 %collective-permute-start.19 = (bf16[2,2,16,1024]{3,2,1,0:T(8,128)(2,1)S(1)}, bf16[2,2,16,1024]{3,2,1,0:T(8,128)(2,1)S(1)}, u32[]{:S(2)}, u32[]{:S(2)}) collective-permute-start(bf16[2,2,16,1024]{3,2,1,0:T(8,128)(2,1)S(1)} %get-tuple-element.52), channel_id=1, source_target_pairs={{0,8},{4,12},{8,0},{12,4},{1,9},{5,13},{9,1},{13,5},{2,10},{6,14},... | collective-permute-start | bytes 393224 | tf_op jit(solution)/shard_map/ppermute | solution.py:397
  104.5 6.3 %collective-permute-done.19.rest_1_ = bf16[2,2,16,1024]{3,2,1,0:T(8,128)(2,1)S(1)} collective-permute-done((bf16[2,2,16,1024]{3,2,1,0:T(8,128)(2,1)S(1)}, bf16[2,2,16,1024]{3,2,1,0:T(8,128)(2,1)S(1)}, u32[]{:S(2)}, u32[]{:S(2)}) %collective-permute-start.19) | collective-permute-done | bytes 131104 | tf_op jit(solution)/shard_map/ppermute | solution.py:397
  111.6 1.6 %shard_map.107 = (bf16[2,2,16,1024]{3,2,1,0:T(8,128)(2,1)S(1)}, bf16[2,2,16,1024]{3,2,1,0:T(8,128)(2,1)S(1)}, bf16[2,2,16,1024]{3,2,1,0:T(8,128)(2,1)S(1)}, bf16[2,2,16,1024]{3,2,1,0:T(8,128)(2,1)S(1)}) custom-call(s32[1]{0:T(128)} %bitcast.place_ref, f32[4,2,16,1024]{3,2,1,0:T(8,128)S(1)} %copy-done.5, f32[4,2,16,1024]{3,2,1,0:T(8,128)S(1)} %copy-done.3, ...), custom_call_target="tpu_custom_call" | custom-call | flops 134217728 | bytes 2293760 | tf_op jit(solution)/shard_map/pallas_call | solution.py:87
  114.3 2.5 %collective-permute-start.23 = (bf16[2,2,16,1024]{3,2,1,0:T(8,128)(2,1)S(1)}, bf16[2,2,16,1024]{3,2,1,0:T(8,128)(2,1)S(1)}, u32[]{:S(2)}, u32[]{:S(2)}) collective-permute-start(bf16[2,2,16,1024]{3,2,1,0:T(8,128)(2,1)S(1)} %get-tuple-element.57), channel_id=1, source_target_pairs={{0,12},{4,8},{8,4},{12,0},{1,13},{5,9},{9,5},{13,1},{2,14},{6,10},... | collective-permute-start | bytes 393224 | tf_op jit(solution)/shard_map/ppermute | solution.py:397
  116.9 6.4 %collective-permute-done.22.rest_1_ = bf16[2,2,16,1024]{3,2,1,0:T(8,128)(2,1)S(1)} collective-permute-done((bf16[2,2,16,1024]{3,2,1,0:T(8,128)(2,1)S(1)}, bf16[2,2,16,1024]{3,2,1,0:T(8,128)(2,1)S(1)}, u32[]{:S(2)}, u32[]{:S(2)}) %collective-permute-start.22) | collective-permute-done | bytes 131104 | tf_op jit(solution)/shard_map/ppermute | solution.py:397
  124.2 1.9 %shard_map.108 = (f32[2,2,64,256]{3,2,1,0:T(8,128)S(1)}, bf16[2,2,64,256]{3,2,1,0:T(8,128)(2,1)S(1)}) custom-call(s32[1]{0:T(128)} %bitcast.place_ref, bf16[2,2,512,256]{3,2,1,0:T(8,128)(2,1)S(1)} %get-tuple-element.33.k0.k0_ref, bf16[2,2,512,256]{3,2,1,0:T(8,128)(2,1)S(1)} %collective-permute-done.m0.m0_ref, ...), custom_call_target="tpu_custom_call" | custom-call | flops 536870912 | bytes 5111808 | tf_op jit(solution)/shard_map/pallas_call | solution.py:87
  127.8 3.4 %collective-permute-done.25 = bf16[2,2,64,256]{3,2,1,0:T(8,128)(2,1)S(1)} collective-permute-done((bf16[2,2,64,256]{3,2,1,0:T(8,128)(2,1)S(1)}, bf16[2,2,64,256]{3,2,1,0:T(8,128)(2,1)S(1)}, u32[]{:S(2)}, u32[]{:S(2)}) %collective-permute-start.25) | collective-permute-done | bytes 131104 | tf_op jit(solution)/shard_map/ppermute | solution.py:397
  131.2 2.2 %collective-permute-start.26 = (bf16[2,2,64,256]{3,2,1,0:T(8,128)(2,1)S(1)}, bf16[2,2,64,256]{3,2,1,0:T(8,128)(2,1)S(1)}, u32[]{:S(2)}, u32[]{:S(2)}) collective-permute-start(bf16[2,2,64,256]{3,2,1,0:T(8,128)(2,1)S(1)} %add_convert_fusion.rest_0_), channel_id=1, source_target_pairs={{0,8},{4,12},{8,0},{12,4},{1,9},{5,13},{9,1},{13,5},{2,10},{6,14},... | collective-permute-start | bytes 393224 | tf_op jit(solution)/shard_map/ppermute | solution.py:397
  134.8 6.4 %collective-permute-done.26.rest_1_ = bf16[2,2,64,256]{3,2,1,0:T(8,128)(2,1)S(1)} collective-permute-done((bf16[2,2,64,256]{3,2,1,0:T(8,128)(2,1)S(1)}, bf16[2,2,64,256]{3,2,1,0:T(8,128)(2,1)S(1)}, u32[]{:S(2)}, u32[]{:S(2)}) %collective-permute-start.26) | collective-permute-done | bytes 131104 | tf_op jit(solution)/shard_map/ppermute | solution.py:397
  141.8 3.4 %shard_map.109 = bf16[64,128,256]{2,1,0:T(8,128)(2,1)} custom-call(s32[1]{0:T(128)} %bitcast.place_ref, s32[1]{0:T(128)} %bitcast.1.focal_ref, bf16[64,128,256]{2,1,0:T(8,128)(2,1)S(1)} %copy-done.1, s32[128,256]{1,0:T(8,128)S(1)} %copy-done.12, bf16[4,128,128]{2,1,0:T(8,128)(2,1)S(1)} %copy-done.14, bf16[2,2,64,256]{3,2,1,0:T(8,128)(2,1)S(1)} %add_convert_fusion.rest_0_, ...), custom_call_target="tpu_custom_call" | custom-call | flops 67108864 | bytes 9175040 | tf_op jit(solution)/shard_map/pallas_call | solution.py:87
  (86 shorter events, 30.6 us)
Async XLA Ops:
  4.4 29.8 %collective-permute-start = (bf16[2,2,512,256]{3,2,1,0:T(8,128)(2,1)}, bf16[2,2,512,256]{3,2,1,0:T(8,128)(2,1)S(1)}, u32[]{:S(2)}, u32[]{:S(2)}) collective-permute-start(bf16[2,2,512,256]{3,2,1,0:T(8,128)(2,1)} %get-tuple-element.34), channel_id=1, source_target_pairs={{0,2},{2,0},{1,3},{3,1},{4,6},{6,4},{5,7},{7,5},{8,10},{10,8},{9,1... | collective-permute-start | bytes 3145736 | tf_op jit(solution)/shard_map/ppermute | solution.py:397
  11.2 45.1 %copy-start.7 = (bf16[4,128,128]{2,1,0:T(8,128)(2,1)S(1)}, bf16[4,128,128]{2,1,0:T(8,128)(2,1)}, u32[]{:S(2)}) copy-start(bf16[4,128,128]{2,1,0:T(8,128)(2,1)} %constant.64.clone.g_ref) | copy-start | bytes 393220
  11.2 12.7 %collective-permute-start.1 = (bf16[2,2,64,256]{3,2,1,0:T(8,128)(2,1)S(1)}, bf16[2,2,64,256]{3,2,1,0:T(8,128)(2,1)S(1)}, u32[]{:S(2)}, u32[]{:S(2)}) collective-permute-start(bf16[2,2,64,256]{3,2,1,0:T(8,128)(2,1)S(1)} %get-tuple-element.36), channel_id=1, source_target_pairs={{0,8},{4,12},{8,0},{12,4},{1,9},{5,13},{9,1},{13,5},{2,10},{6,14},... | collective-permute-start | bytes 393224 | tf_op jit(solution)/shard_map/ppermute | solution.py:397
  13.8 10.1 %collective-permute-start.2 = (bf16[2,2,64,256]{3,2,1,0:T(8,128)(2,1)S(1)}, bf16[2,2,64,256]{3,2,1,0:T(8,128)(2,1)S(1)}, u32[]{:S(2)}, u32[]{:S(2)}) collective-permute-start(bf16[2,2,64,256]{3,2,1,0:T(8,128)(2,1)S(1)} %get-tuple-element.37), channel_id=1, source_target_pairs={{0,12},{4,8},{8,4},{12,0},{1,13},{5,9},{9,5},{13,1},{2,14},{6,10},... | collective-permute-start | bytes 393224 | tf_op jit(solution)/shard_map/ppermute | solution.py:397
  15.2 8.9 %collective-permute-start.3 = (bf16[2,2,64,256]{3,2,1,0:T(8,128)(2,1)S(1)}, bf16[2,2,64,256]{3,2,1,0:T(8,128)(2,1)S(1)}, u32[]{:S(2)}, u32[]{:S(2)}) collective-permute-start(bf16[2,2,64,256]{3,2,1,0:T(8,128)(2,1)S(1)} %get-tuple-element.38), channel_id=1, source_target_pairs={{0,4},{4,0},{8,12},{12,8},{1,5},{5,1},{9,13},{13,9},{2,6},{6,2},{1... | collective-permute-start | bytes 393224 | tf_op jit(solution)/shard_map/ppermute | solution.py:397
  24.2 9.3 %collective-permute-start.4 = (bf16[2,2,64,256]{3,2,1,0:T(8,128)(2,1)S(1)}, bf16[2,2,64,256]{3,2,1,0:T(8,128)(2,1)S(1)}, u32[]{:S(2)}, u32[]{:S(2)}) collective-permute-start(bf16[2,2,64,256]{3,2,1,0:T(8,128)(2,1)S(1)} %get-tuple-element.63.n_ref), channel_id=1, source_target_pairs={{0,2},{2,0},{1,3},{3,1},{4,6},{6,4},{5,7},{7,5},{8,10},{10,8},{9,1... | collective-permute-start | bytes 393224 | tf_op jit(solution)/shard_map/ppermute | solution.py:397
  25.4 11.5 %collective-permute-start.5 = (bf16[2,2,512,256]{3,2,1,0:T(8,128)(2,1)S(1)}, bf16[2,2,512,256]{3,2,1,0:T(8,128)(2,1)S(1)}, u32[]{:S(2)}, u32[]{:S(2)}) collective-permute-start(bf16[2,2,512,256]{3,2,1,0:T(8,128)(2,1)S(1)} %get-tuple-element.33.k0.k0_ref), channel_id=1, source_target_pairs={{0,1},{1,0},{2,3},{3,2},{4,5},{5,4},{6,7},{7,6},{8,9},{9,8},{10,11... | collective-permute-start | bytes 3145736 | tf_op jit(solution)/shard_map/ppermute | solution.py:397
  34.2 2.8 %collective-permute-start.6 = (bf16[2,2,512,256]{3,2,1,0:T(8,128)(2,1)S(1)}, bf16[2,2,512,256]{3,2,1,0:T(8,128)(2,1)}, u32[]{:S(2)}, u32[]{:S(2)}) collective-permute-start(bf16[2,2,512,256]{3,2,1,0:T(8,128)(2,1)S(1)} %collective-permute-done.m0.m0_ref), channel_id=1, source_target_pairs={{0,1},{1,0},{2,3},{3,2},{4,5},{5,4},{6,7},{7,6},{8,9},{9,8},{10,11... | collective-permute-start | bytes 3145736 | tf_op jit(solution)/shard_map/ppermute | solution.py:397
  34.9 1.9 %collective-permute-start.7 = (s32[16,512]{1,0:T(8,128)S(1)}, s32[16,512]{1,0:T(8,128)S(1)}, u32[]{:S(2)}, u32[]{:S(2)}) collective-permute-start(s32[16,512]{1,0:T(8,128)S(1)} %get-tuple-element.66), channel_id=1, source_target_pairs={{0,1},{1,0},{2,3},{3,2},{4,5},{5,4},{6,7},{7,6},{8,9},{9,8},{10,11... | collective-permute-start | bytes 98312 | tf_op jit(solution)/shard_map/ppermute | solution.py:397
  41.5 7.6 %collective-permute-start.10 = (bf16[2,2,16,1024]{3,2,1,0:T(8,128)(2,1)S(1)}, bf16[2,2,16,1024]{3,2,1,0:T(8,128)(2,1)S(1)}, u32[]{:S(2)}, u32[]{:S(2)}) collective-permute-start(bf16[2,2,16,1024]{3,2,1,0:T(8,128)(2,1)S(1)} %get-tuple-element.44), channel_id=1, source_target_pairs={{0,4},{4,0},{8,12},{12,8},{1,5},{5,1},{9,13},{13,9},{2,6},{6,2},{1... | collective-permute-start | bytes 393224 | tf_op jit(solution)/shard_map/ppermute | solution.py:397
  43.4 12.9 %collective-permute-start.8 = (bf16[2,2,16,1024]{3,2,1,0:T(8,128)(2,1)S(1)}, bf16[2,2,16,1024]{3,2,1,0:T(8,128)(2,1)S(1)}, u32[]{:S(2)}, u32[]{:S(2)}) collective-permute-start(bf16[2,2,16,1024]{3,2,1,0:T(8,128)(2,1)S(1)} %get-tuple-element.42), channel_id=1, source_target_pairs={{0,8},{4,12},{8,0},{12,4},{1,9},{5,13},{9,1},{13,5},{2,10},{6,14},... | collective-permute-start | bytes 393224 | tf_op jit(solution)/shard_map/ppermute | solution.py:397
  46.0 10.3 %collective-permute-start.9 = (bf16[2,2,16,1024]{3,2,1,0:T(8,128)(2,1)S(1)}, bf16[2,2,16,1024]{3,2,1,0:T(8,128)(2,1)S(1)}, u32[]{:S(2)}, u32[]{:S(2)}) collective-permute-start(bf16[2,2,16,1024]{3,2,1,0:T(8,128)(2,1)S(1)} %get-tuple-element.43), channel_id=1, source_target_pairs={{0,12},{4,8},{8,4},{12,0},{1,13},{5,9},{9,5},{13,1},{2,14},{6,10},... | collective-permute-start | bytes 393224 | tf_op jit(solution)/shard_map/ppermute | solution.py:397
  58.7 12.9 %collective-permute-start.11 = (bf16[2,2,16,1024]{3,2,1,0:T(8,128)(2,1)S(1)}, bf16[2,2,16,1024]{3,2,1,0:T(8,128)(2,1)S(1)}, u32[]{:S(2)}, u32[]{:S(2)}) collective-permute-start(bf16[2,2,16,1024]{3,2,1,0:T(8,128)(2,1)S(1)} %get-tuple-element.46), channel_id=1, source_target_pairs={{0,8},{4,12},{8,0},{12,4},{1,9},{5,13},{9,1},{13,5},{2,10},{6,14},... | collective-permute-start | bytes 393224 | tf_op jit(solution)/shard_map/ppermute | solution.py:397
  62.0 9.6 %collective-permute-start.12 = (bf16[2,2,16,1024]{3,2,1,0:T(8,128)(2,1)S(1)}, bf16[2,2,16,1024]{3,2,1,0:T(8,128)(2,1)S(1)}, u32[]{:S(2)}, u32[]{:S(2)}) collective-permute-start(bf16[2,2,16,1024]{3,2,1,0:T(8,128)(2,1)S(1)} %get-tuple-element.47), channel_id=1, source_target_pairs={{0,12},{4,8},{8,4},{12,0},{1,13},{5,9},{9,5},{13,1},{2,14},{6,10},... | collective-permute-start | bytes 393224 | tf_op jit(solution)/shard_map/ppermute | solution.py:397
  63.4 8.3 %collective-permute-start.13 = (bf16[2,2,16,1024]{3,2,1,0:T(8,128)(2,1)S(1)}, bf16[2,2,16,1024]{3,2,1,0:T(8,128)(2,1)S(1)}, u32[]{:S(2)}, u32[]{:S(2)}) collective-permute-start(bf16[2,2,16,1024]{3,2,1,0:T(8,128)(2,1)S(1)} %get-tuple-element.48), channel_id=1, source_target_pairs={{0,4},{4,0},{8,12},{12,8},{1,5},{5,1},{9,13},{13,9},{2,6},{6,2},{1... | collective-permute-start | bytes 393224 | tf_op jit(solution)/shard_map/ppermute | solution.py:397
  75.0 5.3 %collective-permute-start.14 = (bf16[2,2,64,256]{3,2,1,0:T(8,128)(2,1)}, bf16[2,2,64,256]{3,2,1,0:T(8,128)(2,1)}, u32[]{:S(2)}, u32[]{:S(2)}) collective-permute-start(bf16[2,2,64,256]{3,2,1,0:T(8,128)(2,1)} %get-tuple-element.50), channel_id=1, source_target_pairs={{0,2},{2,0},{1,3},{3,1},{4,6},{6,4},{5,7},{7,5},{8,10},{10,8},{9,1... | collective-permute-start | bytes 393224 | tf_op jit(solution)/shard_map/ppermute | solution.py:397
  81.3 10.4 %collective-permute-start.15 = (bf16[2,2,64,256]{3,2,1,0:T(8,128)(2,1)S(1)}, bf16[2,2,64,256]{3,2,1,0:T(8,128)(2,1)S(1)}, u32[]{:S(2)}, u32[]{:S(2)}) collective-permute-start(bf16[2,2,64,256]{3,2,1,0:T(8,128)(2,1)S(1)} %add_convert_fusion.1.rest_0_), channel_id=1, source_target_pairs={{0,8},{4,12},{8,0},{12,4},{1,9},{5,13},{9,1},{13,5},{2,10},{6,14},... | collective-permute-start | bytes 393224 | tf_op jit(solution)/shard_map/ppermute | solution.py:397
  83.3 8.5 %collective-permute-start.16 = (bf16[2,2,64,256]{3,2,1,0:T(8,128)(2,1)S(1)}, bf16[2,2,64,256]{3,2,1,0:T(8,128)(2,1)S(1)}, u32[]{:S(2)}, u32[]{:S(2)}) collective-permute-start(bf16[2,2,64,256]{3,2,1,0:T(8,128)(2,1)S(1)} %add_convert_fusion.1.rest_0_), channel_id=1, source_target_pairs={{0,12},{4,8},{8,4},{12,0},{1,13},{5,9},{9,5},{13,1},{2,14},{6,10},... | collective-permute-start | bytes 393224 | tf_op jit(solution)/shard_map/ppermute | solution.py:397
  85.8 6.9 %collective-permute-start.17 = (bf16[2,2,64,256]{3,2,1,0:T(8,128)(2,1)S(1)}, bf16[2,2,64,256]{3,2,1,0:T(8,128)(2,1)S(1)}, u32[]{:S(2)}, u32[]{:S(2)}) collective-permute-start(bf16[2,2,64,256]{3,2,1,0:T(8,128)(2,1)S(1)} %add_convert_fusion.1.rest_0_), channel_id=1, source_target_pairs={{0,4},{4,0},{8,12},{12,8},{1,5},{5,1},{9,13},{13,9},{2,6},{6,2},{1... | collective-permute-start | bytes 393224 | tf_op jit(solution)/shard_map/ppermute | solution.py:397
  93.2 5.0 %collective-permute-start.18 = (bf16[2,2,64,256]{3,2,1,0:T(8,128)(2,1)S(1)}, bf16[2,2,64,256]{3,2,1,0:T(8,128)(2,1)S(1)}, u32[]{:S(2)}, u32[]{:S(2)}) collective-permute-start(bf16[2,2,64,256]{3,2,1,0:T(8,128)(2,1)S(1)} %shard_map.105.n_ref), channel_id=1, source_target_pairs={{0,2},{2,0},{1,3},{3,1},{4,6},{6,4},{5,7},{7,5},{8,10},{10,8},{9,1... | collective-permute-start | bytes 393224 | tf_op jit(solution)/shard_map/ppermute | solution.py:397
  100.9 40.9 %copy-start.1 = (bf16[64,128,256]{2,1,0:T(8,128)(2,1)S(1)}, bf16[64,128,256]{2,1,0:T(8,128)(2,1)}, u32[]{:S(2)}) copy-start(bf16[64,128,256]{2,1,0:T(8,128)(2,1)} %x_ref.5) | copy-start | bytes 12582916
  101.0 40.9 %copy-start.12 = (s32[128,256]{1,0:T(8,128)S(1)}, s32[128,256]{1,0:T(8,128)}, u32[]{:S(2)}) copy-start(s32[128,256]{1,0:T(8,128)} %o_ref.1) | copy-start | bytes 393220
  101.0 9.9 %collective-permute-start.19 = (bf16[2,2,16,1024]{3,2,1,0:T(8,128)(2,1)S(1)}, bf16[2,2,16,1024]{3,2,1,0:T(8,128)(2,1)S(1)}, u32[]{:S(2)}, u32[]{:S(2)}) collective-permute-start(bf16[2,2,16,1024]{3,2,1,0:T(8,128)(2,1)S(1)} %get-tuple-element.52), channel_id=1, source_target_pairs={{0,8},{4,12},{8,0},{12,4},{1,9},{5,13},{9,1},{13,5},{2,10},{6,14},... | collective-permute-start | bytes 393224 | tf_op jit(solution)/shard_map/ppermute | solution.py:397
  103.1 7.8 %collective-permute-start.20 = (bf16[2,2,16,1024]{3,2,1,0:T(8,128)(2,1)S(1)}, bf16[2,2,16,1024]{3,2,1,0:T(8,128)(2,1)S(1)}, u32[]{:S(2)}, u32[]{:S(2)}) collective-permute-start(bf16[2,2,16,1024]{3,2,1,0:T(8,128)(2,1)S(1)} %get-tuple-element.53), channel_id=1, source_target_pairs={{0,12},{4,8},{8,4},{12,0},{1,13},{5,9},{9,5},{13,1},{2,14},{6,10},... | collective-permute-start | bytes 393224 | tf_op jit(solution)/shard_map/ppermute | solution.py:397
  104.4 7.2 %collective-permute-start.21 = (bf16[2,2,16,1024]{3,2,1,0:T(8,128)(2,1)S(1)}, bf16[2,2,16,1024]{3,2,1,0:T(8,128)(2,1)S(1)}, u32[]{:S(2)}, u32[]{:S(2)}) collective-permute-start(bf16[2,2,16,1024]{3,2,1,0:T(8,128)(2,1)S(1)} %get-tuple-element.54), channel_id=1, source_target_pairs={{0,4},{4,0},{8,12},{12,8},{1,5},{5,1},{9,13},{13,9},{2,6},{6,2},{1... | collective-permute-start | bytes 393224 | tf_op jit(solution)/shard_map/ppermute | solution.py:397
  113.2 10.0 %collective-permute-start.22 = (bf16[2,2,16,1024]{3,2,1,0:T(8,128)(2,1)S(1)}, bf16[2,2,16,1024]{3,2,1,0:T(8,128)(2,1)S(1)}, u32[]{:S(2)}, u32[]{:S(2)}) collective-permute-start(bf16[2,2,16,1024]{3,2,1,0:T(8,128)(2,1)S(1)} %get-tuple-element.56), channel_id=1, source_target_pairs={{0,8},{4,12},{8,0},{12,4},{1,9},{5,13},{9,1},{13,5},{2,10},{6,14},... | collective-permute-start | bytes 393224 | tf_op jit(solution)/shard_map/ppermute | solution.py:397
  114.3 8.9 %collective-permute-start.23 = (bf16[2,2,16,1024]{3,2,1,0:T(8,128)(2,1)S(1)}, bf16[2,2,16,1024]{3,2,1,0:T(8,128)(2,1)S(1)}, u32[]{:S(2)}, u32[]{:S(2)}) collective-permute-start(bf16[2,2,16,1024]{3,2,1,0:T(8,128)(2,1)S(1)} %get-tuple-element.57), channel_id=1, source_target_pairs={{0,12},{4,8},{8,4},{12,0},{1,13},{5,9},{9,5},{13,1},{2,14},{6,10},... | collective-permute-start | bytes 393224 | tf_op jit(solution)/shard_map/ppermute | solution.py:397
  116.9 7.3 %collective-permute-start.24 = (bf16[2,2,16,1024]{3,2,1,0:T(8,128)(2,1)S(1)}, bf16[2,2,16,1024]{3,2,1,0:T(8,128)(2,1)S(1)}, u32[]{:S(2)}, u32[]{:S(2)}) collective-permute-start(bf16[2,2,16,1024]{3,2,1,0:T(8,128)(2,1)S(1)} %get-tuple-element.58), channel_id=1, source_target_pairs={{0,4},{4,0},{8,12},{12,8},{1,5},{5,1},{9,13},{13,9},{2,6},{6,2},{1... | collective-permute-start | bytes 393224 | tf_op jit(solution)/shard_map/ppermute | solution.py:397
  126.1 5.0 %collective-permute-start.25 = (bf16[2,2,64,256]{3,2,1,0:T(8,128)(2,1)S(1)}, bf16[2,2,64,256]{3,2,1,0:T(8,128)(2,1)S(1)}, u32[]{:S(2)}, u32[]{:S(2)}) collective-permute-start(bf16[2,2,64,256]{3,2,1,0:T(8,128)(2,1)S(1)} %get-tuple-element.60), channel_id=1, source_target_pairs={{0,2},{2,0},{1,3},{3,1},{4,6},{6,4},{5,7},{7,5},{8,10},{10,8},{9,1... | collective-permute-start | bytes 393224 | tf_op jit(solution)/shard_map/ppermute | solution.py:397
  131.2 9.9 %collective-permute-start.26 = (bf16[2,2,64,256]{3,2,1,0:T(8,128)(2,1)S(1)}, bf16[2,2,64,256]{3,2,1,0:T(8,128)(2,1)S(1)}, u32[]{:S(2)}, u32[]{:S(2)}) collective-permute-start(bf16[2,2,64,256]{3,2,1,0:T(8,128)(2,1)S(1)} %add_convert_fusion.rest_0_), channel_id=1, source_target_pairs={{0,8},{4,12},{8,0},{12,4},{1,9},{5,13},{9,1},{13,5},{2,10},{6,14},... | collective-permute-start | bytes 393224 | tf_op jit(solution)/shard_map/ppermute | solution.py:397
  133.4 7.8 %collective-permute-start.27 = (bf16[2,2,64,256]{3,2,1,0:T(8,128)(2,1)S(1)}, bf16[2,2,64,256]{3,2,1,0:T(8,128)(2,1)S(1)}, u32[]{:S(2)}, u32[]{:S(2)}) collective-permute-start(bf16[2,2,64,256]{3,2,1,0:T(8,128)(2,1)S(1)} %add_convert_fusion.rest_0_), channel_id=1, source_target_pairs={{0,12},{4,8},{8,4},{12,0},{1,13},{5,9},{9,5},{13,1},{2,14},{6,10},... | collective-permute-start | bytes 393224 | tf_op jit(solution)/shard_map/ppermute | solution.py:397
  134.6 7.2 %collective-permute-start.28 = (bf16[2,2,64,256]{3,2,1,0:T(8,128)(2,1)S(1)}, bf16[2,2,64,256]{3,2,1,0:T(8,128)(2,1)S(1)}, u32[]{:S(2)}, u32[]{:S(2)}) collective-permute-start(bf16[2,2,64,256]{3,2,1,0:T(8,128)(2,1)S(1)} %add_convert_fusion.rest_0_), channel_id=1, source_target_pairs={{0,4},{4,0},{8,12},{12,8},{1,5},{5,1},{9,13},{13,9},{2,6},{6,2},{1... | collective-permute-start | bytes 393224 | tf_op jit(solution)/shard_map/ppermute | solution.py:397
  (16 other events, 211.1 us)

commit v7 on v6

--- a/solution.py
+++ b/solution.py
@@ -13,7 +13,7 @@
 ITERS = 2
 ROWS = 8
 CHUNKS = 1
-VMEM_BYTES = 16 * 1024 * 1024
+VMEM_BYTES = 6 * 1024 * 1024
 
 BF16 = jnp.bfloat16
 F32 = jnp.float32
@@ -110,20 +110,31 @@
     half = src // 2
     steps = half // BLOCK
 
-    def body(place_ref, flags, x_ref, keep, send):
-        for flip, out in ((1, send), (0, keep)):
-            for step in range(steps):
-                block = (place_ref[0] ^ flip) * steps + step
-                rows = pl.ds(pl.multiple_of(block * BLOCK, BLOCK), BLOCK)
-                to = pl.ds(step * BLOCK, BLOCK)
-                for j in range(per_dev):
+    def body(place_ref, flags, x_ref, *outs):
+        for flip in (1, 0):
+            for j in range(per_dev):
+                out = outs[flip * per_dev + j]
+                for step in range(steps):
+                    block = (place_ref[0] ^ flip) * steps + step
+                    rows = pl.ds(pl.multiple_of(block * BLOCK, BLOCK), BLOCK)
+                    to = slice(step * BLOCK, (step + 1) * BLOCK)
                     for r in range(rcv // BLOCK):
-                        on = flags[j, block, r].astype(F32).astype(BF16)
-                        at = pl.ds(r * BLOCK, BLOCK)
-                        out[j, :, to, at] = x_ref[j, :, rows, at] * on
-
-    shape = jax.ShapeDtypeStruct((per_dev, 2, half, rcv), BF16)
-    return call(body, (place, aperture), [(response, whole(response))], [(shape, whole(shape))] * 2, (1,))
+                        on = flags[j, block, r] != 0
+                        spots = [(c, slice(r * BLOCK, (r + 1) * BLOCK)) for c in range(2)]
+
+                        @pl.when(on)
+                        def _():
+                            for c, at in spots:
+                                out[to, c * rcv + at.start : c * rcv + at.stop] = x_ref[j, c, rows, at]
+
+                        @pl.when(jnp.logical_not(on))
+                        def _():
+                            for c, at in spots:
+                                out[to, c * rcv + at.start : c * rcv + at.stop] = jnp.zeros((BLOCK, BLOCK), BF16)
+
+    shape = jax.ShapeDtypeStruct((half, 2 * rcv), BF16)
+    outs = call(body, (place, aperture), [(response, whole(response))], [(shape, whole(shape))] * (2 * per_dev), (1,))
+    return outs[:per_dev], outs[per_dev:]
 
 
 def first_spectra(initial, table, freq_place, freq_devs, per_dev, first, rows):
@@ -162,44 +173,41 @@
 
 def down_products(near, far, responses, freq_place, freq_devs):
     _, per_dev, rows, rcv = near.shape
-    width = responses[0][0].shape[2]
+    flat = [v for by_half in responses for pair in by_half for v in pair]
+    width = flat[0].shape[0]
     tile = min(width, 256)
     share = rows // freq_devs
 
-    def body(place_ref, n_ref, f_ref, k0, m0, k1, m1, *rest):
-        outs, held = rest[:freq_devs], rest[freq_devs]
-        sides = []
-        for ref in (n_ref, f_ref):
-            for j in range(per_dev):
+    def body(place_ref, n_ref, f_ref, *rest):
+        resp, outs, held = rest[: len(flat)], rest[len(flat) : -1], rest[-1]
+        for j in range(per_dev):
+            sides = []
+            for ref in (n_ref, f_ref):
                 real, imag = ref[0, j], ref[1, j]
-                sides.append((jnp.concatenate([real, imag], 0), jnp.concatenate([-imag, real], 0)))
-        for half, pair in enumerate(((k0, m0), (k1, m1))):
-            for at in range(width // tile):
-                cut = slice(at * tile, (at + 1) * tile)
-                for j in range(per_dev):
-                    total = None
-                    for side, resp in enumerate(pair):
-                        for part, lhs in enumerate(sides[side * per_dev + j]):
-                            term = lax.dot_general(
-                                lhs, resp[j, part, cut], (((1,), (1,)), ((), ())), preferred_element_type=F32
-                            )
-                            total = term if total is None else total + term
-                    held[0, j] = total[:rows]
-                    held[1, j] = total[rows:]
-                to = slice(half * width + at * tile, half * width + (at + 1) * tile)
-                for way, out in zip(ways(freq_devs), outs):
-                    start = pl.multiple_of((place_ref[0] ^ way) * share, share)
-                    out[:, :, :, to] = held[:, :, pl.ds(start, share), :].astype(BF16)
+                sides.append(jnp.concatenate([jnp.concatenate([real, -imag], 1), jnp.concatenate([imag, real], 1)], 0))
+            for half in range(2):
+                pair = resp[(j * 2 + half) * 2 : (j * 2 + half) * 2 + 2]
+                for at in range(width // tile):
+                    cut = slice(at * tile, (at + 1) * tile)
+                    total = sum(
+                        lax.dot_general(lhs, ref[cut], (((1,), (1,)), ((), ())), preferred_element_type=F32)
+                        for lhs, ref in zip(sides, pair)
+                    )
+                    to = slice(half * width + at * tile, half * width + (at + 1) * tile)
+                    held[0, j, :, to] = total[:rows]
+                    held[1, j, :, to] = total[rows:]
+        for way, out in zip(ways(freq_devs), outs):
+            start = pl.multiple_of((place_ref[0] ^ way) * share, share)
+            out[...] = held[:, :, pl.ds(start, share), :].astype(BF16)
 
     shape = jax.ShapeDtypeStruct((2, per_dev, share, 2 * width), BF16)
-    (k0, m0), (k1, m1) = responses
     return call(
         body,
         (freq_place,),
-        [(v, whole(v)) for v in (near, far, k0, m0, k1, m1)],
+        [(v, whole(v)) for v in (near, far, *flat)],
         [(shape, whole(shape))] * freq_devs,
         (1,),
-        scratch=[pltpu.VMEM((2, per_dev, rows, tile), F32)],
+        scratch=[pltpu.VMEM((2, per_dev, rows, 2 * width), F32)],
         flops=2 * 8 * per_dev * rows * 2 * width * rcv,
     )
 
@@ -226,7 +234,7 @@
         body(pl.ds(pl.multiple_of(step * BLOCK, BLOCK), BLOCK))
         return carry
 
-    lax.fori_loop(0, width // BLOCK, at, 0)
+    lax.fori_loop(0, width // BLOCK, at, 0, unroll=2)
 
 
 def windowed(messages, tables, matrix, freq_place, per_dev, share):
@@ -269,36 +277,38 @@
 
 def up_products(messages, responses, freq_place, rows):
     freq_devs = len(messages)
-    (k0, m0), (k1, m1) = responses
-    per_dev, _, src, rcv = k0.shape
-    share = messages[0].shape[2]
-
-    def body(place_ref, k0_ref, m0_ref, k1_ref, m1_ref, *rest):
-        refs = rest[:freq_devs]
-        keep, send, held = rest[freq_devs:]
+    flat = [v for by_half in responses for pair in by_half for v in pair]
+    src, rcv = flat[0].shape[0], flat[0].shape[1] // 2
+    _, per_dev, share, _ = messages[0].shape
+
+    def body(place_ref, *rest):
+        resp, refs = rest[: len(flat)], rest[len(flat) : len(flat) + freq_devs]
+        keep, send, held = rest[len(flat) + freq_devs :]
         for way, ref in zip(ways(freq_devs), refs):
-            start = pl.multiple_of((place_ref[0] ^ way) * share, share)
-            held[:, :, pl.ds(start, share), :] = ref[...]
+            for part in range(2):
+                start = pl.multiple_of(part * rows + (place_ref[0] ^ way) * share, share)
+                held[:, pl.ds(start, share), :] = ref[part]
         for j in range(per_dev):
-            for out, pair in ((send, (m0_ref, m1_ref)), (keep, (k0_ref, k1_ref))):
-                total = None
-                for half, resp in enumerate(pair):
-                    cut = slice(half * src, (half + 1) * src)
-                    real, imag = held[0, j, :, cut], held[1, j, :, cut]
-                    for part, lhs in ((0, [real, imag]), (1, [imag, -real])):
-                        term = jnp.dot(jnp.concatenate(lhs, 0), resp[j, part], preferred_element_type=F32)
-                        total = term if total is None else total + term
-                for part in range(2):
-                    out[part, j] = total[rows * part : rows * (part + 1)].astype(out.dtype)
+            for side, out in ((1, send), (0, keep)):
+                total = sum(
+                    jnp.dot(
+                        held[j, :, half * src : (half + 1) * src],
+                        resp[(j * 2 + half) * 2 + side][...],
+                        preferred_element_type=F32,
+                    )
+                    for half in range(2)
+                )
+                out[0, j] = (total[:rows, :rcv] + total[rows:, rcv:]).astype(out.dtype)
+                out[1, j] = (total[rows:, :rcv] - total[:rows, rcv:]).astype(out.dtype)
 
     shapes = [jax.ShapeDtypeStruct((2, per_dev, rows, rcv), kind) for kind in (F32, BF16)]
     return call(
         body,
         (freq_place,),
-        [(v, whole(v)) for v in (k0, m0, k1, m1, *messages)],
+        [(v, whole(v)) for v in (*flat, *messages)],
         [(v, whole(v)) for v in shapes],
         (1,),
-        scratch=[pltpu.VMEM((2, per_dev, rows, 2 * src), BF16)],
+        scratch=[pltpu.VMEM((per_dev, 2 * rows, 2 * src), BF16)],
         flops=2 * 8 * per_dev * rows * 2 * src * rcv,
     )
 
@@ -428,8 +438,8 @@
     rblk_place = rblk_index.reshape(1)
 
     kept, moved = masked_halves(response, aperture, rblk_place)
-    moved = exchanged(moved, "rblk", 1)
-    kept_pair = exchanged(kept, "sblk", 1)
+    moved = [exchanged(v, "rblk", 1) for v in moved]
+    kept_pair = [exchanged(v, "sblk", 1) for v in kept]
     responses = None
     forward = jnp.asarray(forward_tables(samples, freq_devs, per_dev))
     inverse = jnp.asarray(inverse_tables(samples, freq_devs, per_dev))
@@ -443,8 +453,13 @@
         spectra = sums.astype(BF16)
         far = exchanged(spectra, "rblk", 1)
         if responses is None:
-            moved, far = lax.optimization_barrier((moved, far))
-            responses = ((kept, moved), (kept_pair, exchanged(moved, "sblk", 1)))
+            before, moved_pair = spectra, []
+            for at in range(per_dev):
+                moved[at], before = lax.optimization_barrier((moved[at], before))
+                spectra, far = (spectra, before) if at else (before, far)
+                moved_pair.append(exchanged(moved[at], "sblk", 1))
+                before = far
+            responses = [((kept[j], moved[j]), (kept_pair[j], moved_pair[j])) for j in range(per_dev)]
 
         def src_onsets(core):
             spot = core * half_rows + first + freq_index * share

time: 146 us -> 142 us (0.973)
  Pallas kernels: 19.9 us -> 15.3 us
  local copies, waits for them, and re-layouts: 10.9 us -> 7.61 us
  starting transfers between devices: 37.3 us -> 40.3 us
    pallas_call x10, Pallas kernels: 19.9 us -> 15.3 us  [call(): pl.pallas_call(body, grid_spec=pltpu.PrefetchScalarGridSpec(num_scalar_pr...]
    unnamed x39, local copies, waits for them, and re-layouts: 10.1 us -> 6.84 us
    ppermute x29 -> x32, starting transfers between devices: 37.3 us -> 40.3 us  [exchanged(): lax.ppermute(value, axis, [(i, i ^ step) for i in range(lax.axis_size(axi...]
    ppermute x29 -> x32, waiting for transfers between devices: 70.5 us -> 70.7 us  [exchanged(): lax.ppermute(value, axis, [(i, i ^ step) for i in range(lax.axis_size(axi...]
  transfers between devices with their start and end apart: 29 -> 32, of which waited for: 20 -> 21; matrix products, arithmetic and copies ran while one was open for 4% -> 5% of each run, Pallas kernels for 0% -> 1%
where the time goes in v7:
time: 142 us; the launch traced here: 141 us
  waiting for transfers between devices  70.7 us (50%)
  starting transfers between devices  40.3 us (28%)
  Pallas kernels  15.3 us (11%)
  local copies, waits for them, and re-layouts  7.61 us (5%)
  other arithmetic  7.06 us (5%)
    ppermute x32, waiting for transfers between devices, exchanged(): lax.ppermute(value, axis, [(i, i ^ step) for i in range(lax.axis_size(axi...  70.7 us
    ppermute x32, starting transfers between devices, exchanged(): lax.ppermute(value, axis, [(i, i ^ step) for i in range(lax.axis_size(axi...  40.3 us
    pallas_call x10, Pallas kernels, call(): pl.pallas_call(body, grid_spec=pltpu.PrefetchScalarGridSpec(num_scalar_pr...  15.3 us
    unnamed x39, local copies, waits for them, and re-layouts  6.84 us
    sin x2, other arithmetic, phases(): return (jnp.cos(angle), jnp.sin(angle), onset.astype(F32) * (1.0 / samples))  4.21 us
  transfers between devices with their start and end apart: 32, of which 21 were waited for; matrix products, arithmetic and copies ran while one was open for 5% of the time, Pallas kernels for 1%

profile of v7, /device:TPU:0, one launch (start us, length us, event | category | flops | bytes accessed | tf_op | source)
XLA Modules:
  0.0 141.2 jit_solution(11796622966459750014)
XLA Ops:
  0.8 1.6 %copy-done.10 = bf16[2,2,1024,256]{3,2,1,0:T(8,128)(2,1)S(1)} copy-done((bf16[2,2,1024,256]{3,2,1,0:T(8,128)(2,1)S(1)}, bf16[2,2,1024,256]{3,2,1,0:T(8,128)(2,1)}, u32[]{:S(2)}) %copy-start.10) | copy-done | bytes 2097176
  2.4 2.4 %shard_map.100 = (bf16[512,512]{1,0:T(8,128)(2,1)S(1)}, bf16[512,512]{1,0:T(8,128)(2,1)S(1)}, bf16[512,512]{1,0:T(8,128)(2,1)}, bf16[512,512]{1,0:T(8,128)(2,1)}) custom-call(s32[1]{0:T(128)} %bitcast.2.place_ref, s32[2,8,2]{2,1,0:T(8,128)S(1)} %copy.11.flags, bf16[2,2,1024,256]{3,2,1,0:T(8,128)(2,1)S(1)} %copy-done.10), custom_call_target="tpu_custom_call" | custom-call | bytes 4194304 | tf_op jit(solution)/shard_map/pallas_call | solution.py:87
  4.8 2.9 %collective-permute-start.6 = (bf16[512,512]{1,0:T(8,128)(2,1)}, bf16[512,512]{1,0:T(8,128)(2,1)S(1)}, u32[]{:S(2)}, u32[]{:S(2)}) collective-permute-start(bf16[512,512]{1,0:T(8,128)(2,1)} %get-tuple-element.45), channel_id=1, source_target_pairs={{0,2},{2,0},{1,3},{3,1},{4,6},{6,4},{5,7},{7,5},{8,10},{10,8},{9,1... | collective-permute-start | bytes 1572872 | tf_op jit(solution)/shard_map/ppermute | solution.py:407
  7.8 2.2 %copy-done = bf16[64,128,256]{2,1,0:T(8,128)(2,1)S(1)} copy-done((bf16[64,128,256]{2,1,0:T(8,128)(2,1)S(1)}, bf16[64,128,256]{2,1,0:T(8,128)(2,1)}, u32[]{:S(2)}) %copy-start) | copy-done | bytes 4194328
  11.6 3.1 %collective-permute-start.1 = (bf16[2,2,64,256]{3,2,1,0:T(8,128)(2,1)S(1)}, bf16[2,2,64,256]{3,2,1,0:T(8,128)(2,1)S(1)}, u32[]{:S(2)}, u32[]{:S(2)}) collective-permute-start(bf16[2,2,64,256]{3,2,1,0:T(8,128)(2,1)S(1)} %get-tuple-element.40), channel_id=1, source_target_pairs={{0,8},{4,12},{8,0},{12,4},{1,9},{5,13},{9,1},{13,5},{2,10},{6,14},... | collective-permute-start | bytes 393224 | tf_op jit(solution)/shard_map/ppermute | solution.py:407
  16.3 8.2 %collective-permute-done.1 = bf16[2,2,64,256]{3,2,1,0:T(8,128)(2,1)S(1)} collective-permute-done((bf16[2,2,64,256]{3,2,1,0:T(8,128)(2,1)S(1)}, bf16[2,2,64,256]{3,2,1,0:T(8,128)(2,1)S(1)}, u32[]{:S(2)}, u32[]{:S(2)}) %collective-permute-start.1) | collective-permute-done | bytes 131104 | tf_op jit(solution)/shard_map/ppermute | solution.py:407
  25.3 1.6 %collective-permute-start.7 = (bf16[2,2,64,256]{3,2,1,0:T(8,128)(2,1)}, bf16[2,2,64,256]{3,2,1,0:T(8,128)(2,1)}, u32[]{:S(2)}, u32[]{:S(2)}) collective-permute-start(bf16[2,2,64,256]{3,2,1,0:T(8,128)(2,1)} %get-tuple-element.47.n_ref), channel_id=1, source_target_pairs={{0,2},{2,0},{1,3},{3,1},{4,6},{6,4},{5,7},{7,5},{8,10},{10,8},{9,1... | collective-permute-start | bytes 393224 | tf_op jit(solution)/shard_map/ppermute | solution.py:407
  28.2 5.8 %collective-permute-done.7.f_ref = bf16[2,2,64,256]{3,2,1,0:T(8,128)(2,1)} collective-permute-done((bf16[2,2,64,256]{3,2,1,0:T(8,128)(2,1)}, bf16[2,2,64,256]{3,2,1,0:T(8,128)(2,1)}, u32[]{:S(2)}, u32[]{:S(2)}) %collective-permute-start.7) | collective-permute-done | bytes 131104 | tf_op jit(solution)/shard_map/ppermute | solution.py:407
  36.8 2.7 %shard_map.102 = (bf16[2,2,16,1024]{3,2,1,0:T(8,128)(2,1)S(1)}, bf16[2,2,16,1024]{3,2,1,0:T(8,128)(2,1)S(1)}, bf16[2,2,16,1024]{3,2,1,0:T(8,128)(2,1)S(1)}, bf16[2,2,16,1024]{3,2,1,0:T(8,128)(2,1)S(1)}) custom-call(s32[1]{0:T(128)} %bitcast.place_ref, bf16[2,2,64,256]{3,2,1,0:T(8,128)(2,1)} %get-tuple-element.47.n_ref, ...), custom_call_target="tpu_custom_call" | custom-call | flops 536870912 | bytes 4980736 | tf_op jit(solution)/shard_map/pallas_call | solution.py:87
  39.5 2.9 %collective-permute-start.11 = (bf16[2,2,16,1024]{3,2,1,0:T(8,128)(2,1)S(1)}, bf16[2,2,16,1024]{3,2,1,0:T(8,128)(2,1)S(1)}, u32[]{:S(2)}, u32[]{:S(2)}) collective-permute-start(bf16[2,2,16,1024]{3,2,1,0:T(8,128)(2,1)S(1)} %get-tuple-element.50), channel_id=1, source_target_pairs={{0,8},{4,12},{8,0},{12,4},{1,9},{5,13},{9,1},{13,5},{2,10},{6,14},... | collective-permute-start | bytes 393224 | tf_op jit(solution)/shard_map/ppermute | solution.py:407
  43.9 2.1 %fusion.8 = (f32[4,2,16,1024]{3,2,1,0:T(8,128)S(1)}, f32[4,2,16,1024]{3,2,1,0:T(8,128)S(1)}) fusion(s32[16,1024]{1,0:T(8,128)S(1)} %pad_add_fusion, s32[4,2]{1,0:T(4,128)S(1)} %add_add_fusion), kind=kLoop, calls=%fused_computation.20 | loop fusion | flops 1835008 | bytes 1114144 | tf_op jit(solution)/shard_map/sin | solution.py:423
  46.1 6.3 %collective-permute-done.11.rest_1_ = bf16[2,2,16,1024]{3,2,1,0:T(8,128)(2,1)S(1)} collective-permute-done((bf16[2,2,16,1024]{3,2,1,0:T(8,128)(2,1)S(1)}, bf16[2,2,16,1024]{3,2,1,0:T(8,128)(2,1)S(1)}, u32[]{:S(2)}, u32[]{:S(2)}) %collective-permute-start.11) | collective-permute-done | bytes 131104 | tf_op jit(solution)/shard_map/ppermute | solution.py:407
  55.0 4.1 %collective-permute-start.14 = (bf16[2,2,16,1024]{3,2,1,0:T(8,128)(2,1)S(1)}, bf16[2,2,16,1024]{3,2,1,0:T(8,128)(2,1)S(1)}, u32[]{:S(2)}, u32[]{:S(2)}) collective-permute-start(bf16[2,2,16,1024]{3,2,1,0:T(8,128)(2,1)S(1)} %get-tuple-element.54), channel_id=1, source_target_pairs={{0,8},{4,12},{8,0},{12,4},{1,9},{5,13},{9,1},{13,5},{2,10},{6,14},... | collective-permute-start | bytes 393224 | tf_op jit(solution)/shard_map/ppermute | solution.py:407
  59.7 9.1 %collective-permute-done.14.rest_9_ = bf16[2,2,16,1024]{3,2,1,0:T(8,128)(2,1)S(1)} collective-permute-done((bf16[2,2,16,1024]{3,2,1,0:T(8,128)(2,1)S(1)}, bf16[2,2,16,1024]{3,2,1,0:T(8,128)(2,1)S(1)}, u32[]{:S(2)}, u32[]{:S(2)}) %collective-permute-start.14) | collective-permute-done | bytes 131104 | tf_op jit(solution)/shard_map/ppermute | solution.py:407
  74.5 2.8 %collective-permute-done.17 = bf16[2,2,64,256]{3,2,1,0:T(8,128)(2,1)} collective-permute-done((bf16[2,2,64,256]{3,2,1,0:T(8,128)(2,1)}, bf16[2,2,64,256]{3,2,1,0:T(8,128)(2,1)}, u32[]{:S(2)}, u32[]{:S(2)}) %collective-permute-start.17) | collective-permute-done | bytes 131104 | tf_op jit(solution)/shard_map/ppermute | solution.py:407
  78.3 1.9 %collective-permute-start.18 = (bf16[2,2,64,256]{3,2,1,0:T(8,128)(2,1)S(1)}, bf16[2,2,64,256]{3,2,1,0:T(8,128)(2,1)S(1)}, u32[]{:S(2)}, u32[]{:S(2)}) collective-permute-start(bf16[2,2,64,256]{3,2,1,0:T(8,128)(2,1)S(1)} %add_convert_fusion.1.rest_0_), channel_id=1, source_target_pairs={{0,8},{4,12},{8,0},{12,4},{1,9},{5,13},{9,1},{13,5},{2,10},{6,14},... | collective-permute-start | bytes 393224 | tf_op jit(solution)/shard_map/ppermute | solution.py:407
  80.2 2.9 %collective-permute-start.19 = (bf16[2,2,64,256]{3,2,1,0:T(8,128)(2,1)S(1)}, bf16[2,2,64,256]{3,2,1,0:T(8,128)(2,1)S(1)}, u32[]{:S(2)}, u32[]{:S(2)}) collective-permute-start(bf16[2,2,64,256]{3,2,1,0:T(8,128)(2,1)S(1)} %add_convert_fusion.1.rest_0_), channel_id=1, source_target_pairs={{0,12},{4,8},{8,4},{12,0},{1,13},{5,9},{9,5},{13,1},{2,14},{6,10},... | collective-permute-start | bytes 393224 | tf_op jit(solution)/shard_map/ppermute | solution.py:407
  83.0 2.1 %fusion.6 = (f32[4,2,64,256]{3,2,1,0:T(8,128)S(1)}, f32[4,2,64,256]{3,2,1,0:T(8,128)S(1)}) fusion(s32[64,256]{1,0:T(8,128)S(1)} %get-tuple-element.70, s32[4,2]{1,0:T(4,128)S(1)} %add_add_fusion), kind=kLoop, calls=%fused_computation.18 | loop fusion | flops 1835008 | bytes 1114144 | tf_op jit(solution)/shard_map/sin | solution.py:423
  85.1 5.1 %collective-permute-done.18.rest_1_ = bf16[2,2,64,256]{3,2,1,0:T(8,128)(2,1)S(1)} collective-permute-done((bf16[2,2,64,256]{3,2,1,0:T(8,128)(2,1)S(1)}, bf16[2,2,64,256]{3,2,1,0:T(8,128)(2,1)S(1)}, u32[]{:S(2)}, u32[]{:S(2)}) %collective-permute-start.18) | collective-permute-done | bytes 131104 | tf_op jit(solution)/shard_map/ppermute | solution.py:407
  91.5 1.6 %collective-permute-start.21 = (bf16[2,2,64,256]{3,2,1,0:T(8,128)(2,1)S(1)}, bf16[2,2,64,256]{3,2,1,0:T(8,128)(2,1)S(1)}, u32[]{:S(2)}, u32[]{:S(2)}) collective-permute-start(bf16[2,2,64,256]{3,2,1,0:T(8,128)(2,1)S(1)} %shard_map.105.n_ref), channel_id=1, source_target_pairs={{0,2},{2,0},{1,3},{3,1},{4,6},{6,4},{5,7},{7,5},{8,10},{10,8},{9,1... | collective-permute-start | bytes 393224 | tf_op jit(solution)/shard_map/ppermute | solution.py:407
  93.0 3.5 %collective-permute-done.21.f_ref = bf16[2,2,64,256]{3,2,1,0:T(8,128)(2,1)S(1)} collective-permute-done((bf16[2,2,64,256]{3,2,1,0:T(8,128)(2,1)S(1)}, bf16[2,2,64,256]{3,2,1,0:T(8,128)(2,1)S(1)}, u32[]{:S(2)}, u32[]{:S(2)}) %collective-permute-start.21) | collective-permute-done | bytes 131104 | tf_op jit(solution)/shard_map/ppermute | solution.py:407
  96.5 1.5 %shard_map.106 = (bf16[2,2,16,1024]{3,2,1,0:T(8,128)(2,1)S(1)}, bf16[2,2,16,1024]{3,2,1,0:T(8,128)(2,1)S(1)}, bf16[2,2,16,1024]{3,2,1,0:T(8,128)(2,1)S(1)}, bf16[2,2,16,1024]{3,2,1,0:T(8,128)(2,1)S(1)}) custom-call(s32[1]{0:T(128)} %bitcast.place_ref, bf16[2,2,64,256]{3,2,1,0:T(8,128)(2,1)S(1)} %shard_map.105.n_ref, ...), custom_call_target="tpu_custom_call" | custom-call | flops 536870912 | bytes 4980736 | tf_op jit(solution)/shard_map/pallas_call | solution.py:87
  98.1 1.8 %collective-permute-start.22 = (bf16[2,2,16,1024]{3,2,1,0:T(8,128)(2,1)S(1)}, bf16[2,2,16,1024]{3,2,1,0:T(8,128)(2,1)S(1)}, u32[]{:S(2)}, u32[]{:S(2)}) collective-permute-start(bf16[2,2,16,1024]{3,2,1,0:T(8,128)(2,1)S(1)} %get-tuple-element.60), channel_id=1, source_target_pairs={{0,8},{4,12},{8,0},{12,4},{1,9},{5,13},{9,1},{13,5},{2,10},{6,14},... | collective-permute-start | bytes 393224 | tf_op jit(solution)/shard_map/ppermute | solution.py:407
  99.8 1.7 %collective-permute-start.23 = (bf16[2,2,16,1024]{3,2,1,0:T(8,128)(2,1)S(1)}, bf16[2,2,16,1024]{3,2,1,0:T(8,128)(2,1)S(1)}, u32[]{:S(2)}, u32[]{:S(2)}) collective-permute-start(bf16[2,2,16,1024]{3,2,1,0:T(8,128)(2,1)S(1)} %get-tuple-element.61), channel_id=1, source_target_pairs={{0,12},{4,8},{8,4},{12,0},{1,13},{5,9},{9,5},{13,1},{2,14},{6,10},... | collective-permute-start | bytes 393224 | tf_op jit(solution)/shard_map/ppermute | solution.py:407
  101.6 7.1 %collective-permute-done.22.rest_1_ = bf16[2,2,16,1024]{3,2,1,0:T(8,128)(2,1)S(1)} collective-permute-done((bf16[2,2,16,1024]{3,2,1,0:T(8,128)(2,1)S(1)}, bf16[2,2,16,1024]{3,2,1,0:T(8,128)(2,1)S(1)}, u32[]{:S(2)}, u32[]{:S(2)}) %collective-permute-start.22) | collective-permute-done | bytes 131104 | tf_op jit(solution)/shard_map/ppermute | solution.py:407
  111.5 3.0 %collective-permute-start.26 = (bf16[2,2,16,1024]{3,2,1,0:T(8,128)(2,1)S(1)}, bf16[2,2,16,1024]{3,2,1,0:T(8,128)(2,1)S(1)}, u32[]{:S(2)}, u32[]{:S(2)}) collective-permute-start(bf16[2,2,16,1024]{3,2,1,0:T(8,128)(2,1)S(1)} %get-tuple-element.65), channel_id=1, source_target_pairs={{0,12},{4,8},{8,4},{12,0},{1,13},{5,9},{9,5},{13,1},{2,14},{6,10},... | collective-permute-start | bytes 393224 | tf_op jit(solution)/shard_map/ppermute | solution.py:407
  114.5 6.0 %collective-permute-done.25.rest_9_ = bf16[2,2,16,1024]{3,2,1,0:T(8,128)(2,1)S(1)} collective-permute-done((bf16[2,2,16,1024]{3,2,1,0:T(8,128)(2,1)S(1)}, bf16[2,2,16,1024]{3,2,1,0:T(8,128)(2,1)S(1)}, u32[]{:S(2)}, u32[]{:S(2)}) %collective-permute-start.25) | collective-permute-done | bytes 131104 | tf_op jit(solution)/shard_map/ppermute | solution.py:407
  122.2 1.6 %collective-permute-start.28 = (bf16[2,2,64,256]{3,2,1,0:T(8,128)(2,1)S(1)}, bf16[2,2,64,256]{3,2,1,0:T(8,128)(2,1)S(1)}, u32[]{:S(2)}, u32[]{:S(2)}) collective-permute-start(bf16[2,2,64,256]{3,2,1,0:T(8,128)(2,1)S(1)} %get-tuple-element.68), channel_id=1, source_target_pairs={{0,2},{2,0},{1,3},{3,1},{4,6},{6,4},{5,7},{7,5},{8,10},{10,8},{9,1... | collective-permute-start | bytes 393224 | tf_op jit(solution)/shard_map/ppermute | solution.py:407
  123.8 3.5 %collective-permute-done.28 = bf16[2,2,64,256]{3,2,1,0:T(8,128)(2,1)S(1)} collective-permute-done((bf16[2,2,64,256]{3,2,1,0:T(8,128)(2,1)S(1)}, bf16[2,2,64,256]{3,2,1,0:T(8,128)(2,1)S(1)}, u32[]{:S(2)}, u32[]{:S(2)}) %collective-permute-start.28) | collective-permute-done | bytes 131104 | tf_op jit(solution)/shard_map/ppermute | solution.py:407
  127.3 2.1 %collective-permute-start.29 = (bf16[2,2,64,256]{3,2,1,0:T(8,128)(2,1)S(1)}, bf16[2,2,64,256]{3,2,1,0:T(8,128)(2,1)S(1)}, u32[]{:S(2)}, u32[]{:S(2)}) collective-permute-start(bf16[2,2,64,256]{3,2,1,0:T(8,128)(2,1)S(1)} %add_convert_fusion.rest_0_), channel_id=1, source_target_pairs={{0,8},{4,12},{8,0},{12,4},{1,9},{5,13},{9,1},{13,5},{2,10},{6,14},... | collective-permute-start | bytes 393224 | tf_op jit(solution)/shard_map/ppermute | solution.py:407
  130.8 6.3 %collective-permute-done.29.rest_1_ = bf16[2,2,64,256]{3,2,1,0:T(8,128)(2,1)S(1)} collective-permute-done((bf16[2,2,64,256]{3,2,1,0:T(8,128)(2,1)S(1)}, bf16[2,2,64,256]{3,2,1,0:T(8,128)(2,1)S(1)}, u32[]{:S(2)}, u32[]{:S(2)}) %collective-permute-start.29) | collective-permute-done | bytes 131104 | tf_op jit(solution)/shard_map/ppermute | solution.py:407
  137.8 3.4 %shard_map.109 = bf16[64,128,256]{2,1,0:T(8,128)(2,1)} custom-call(s32[1]{0:T(128)} %bitcast.place_ref, s32[1]{0:T(128)} %bitcast.1.focal_ref, bf16[64,128,256]{2,1,0:T(8,128)(2,1)S(1)} %copy-done.1, s32[128,256]{1,0:T(8,128)S(1)} %copy-done.14, bf16[4,128,128]{2,1,0:T(8,128)(2,1)S(1)} %copy-done.16, bf16[2,2,64,256]{3,2,1,0:T(8,128)(2,1)S(1)} %add_convert_fusion.rest_0_, ...), custom_call_target="tpu_custom_call" | custom-call | flops 67108864 | bytes 9175040 | tf_op jit(solution)/shard_map/pallas_call | solution.py:87
  (92 shorter events, 28.4 us)
Async XLA Ops:
  4.8 29.2 %collective-permute-start.6 = (bf16[512,512]{1,0:T(8,128)(2,1)}, bf16[512,512]{1,0:T(8,128)(2,1)S(1)}, u32[]{:S(2)}, u32[]{:S(2)}) collective-permute-start(bf16[512,512]{1,0:T(8,128)(2,1)} %get-tuple-element.45), channel_id=1, source_target_pairs={{0,2},{2,0},{1,3},{3,1},{4,6},{6,4},{5,7},{7,5},{8,10},{10,8},{9,1... | collective-permute-start | bytes 1572872 | tf_op jit(solution)/shard_map/ppermute | solution.py:407
  7.7 26.8 %collective-permute-start = (bf16[512,512]{1,0:T(8,128)(2,1)}, bf16[512,512]{1,0:T(8,128)(2,1)S(1)}, u32[]{:S(2)}, u32[]{:S(2)}) collective-permute-start(bf16[512,512]{1,0:T(8,128)(2,1)} %get-tuple-element.38), channel_id=1, source_target_pairs={{0,2},{2,0},{1,3},{3,1},{4,6},{6,4},{5,7},{7,5},{8,10},{10,8},{9,1... | collective-permute-start | bytes 1572872 | tf_op jit(solution)/shard_map/ppermute | solution.py:407
  11.6 12.9 %collective-permute-start.1 = (bf16[2,2,64,256]{3,2,1,0:T(8,128)(2,1)S(1)}, bf16[2,2,64,256]{3,2,1,0:T(8,128)(2,1)S(1)}, u32[]{:S(2)}, u32[]{:S(2)}) collective-permute-start(bf16[2,2,64,256]{3,2,1,0:T(8,128)(2,1)S(1)} %get-tuple-element.40), channel_id=1, source_target_pairs={{0,8},{4,12},{8,0},{12,4},{1,9},{5,13},{9,1},{13,5},{2,10},{6,14},... | collective-permute-start | bytes 393224 | tf_op jit(solution)/shard_map/ppermute | solution.py:407
  14.7 9.8 %collective-permute-start.2 = (bf16[2,2,64,256]{3,2,1,0:T(8,128)(2,1)S(1)}, bf16[2,2,64,256]{3,2,1,0:T(8,128)(2,1)S(1)}, u32[]{:S(2)}, u32[]{:S(2)}) collective-permute-start(bf16[2,2,64,256]{3,2,1,0:T(8,128)(2,1)S(1)} %get-tuple-element.41), channel_id=1, source_target_pairs={{0,12},{4,8},{8,4},{12,0},{1,13},{5,9},{9,5},{13,1},{2,14},{6,10},... | collective-permute-start | bytes 393224 | tf_op jit(solution)/shard_map/ppermute | solution.py:407
  16.0 8.6 %collective-permute-start.3 = (bf16[2,2,64,256]{3,2,1,0:T(8,128)(2,1)S(1)}, bf16[2,2,64,256]{3,2,1,0:T(8,128)(2,1)S(1)}, u32[]{:S(2)}, u32[]{:S(2)}) collective-permute-start(bf16[2,2,64,256]{3,2,1,0:T(8,128)(2,1)S(1)} %get-tuple-element.42), channel_id=1, source_target_pairs={{0,4},{4,0},{8,12},{12,8},{1,5},{5,1},{9,13},{13,9},{2,6},{6,2},{1... | collective-permute-start | bytes 393224 | tf_op jit(solution)/shard_map/ppermute | solution.py:407
  25.3 8.7 %collective-permute-start.7 = (bf16[2,2,64,256]{3,2,1,0:T(8,128)(2,1)}, bf16[2,2,64,256]{3,2,1,0:T(8,128)(2,1)}, u32[]{:S(2)}, u32[]{:S(2)}) collective-permute-start(bf16[2,2,64,256]{3,2,1,0:T(8,128)(2,1)} %get-tuple-element.47.n_ref), channel_id=1, source_target_pairs={{0,2},{2,0},{1,3},{3,1},{4,6},{6,4},{5,7},{7,5},{8,10},{10,8},{9,1... | collective-permute-start | bytes 393224 | tf_op jit(solution)/shard_map/ppermute | solution.py:407
  26.9 8.3 %collective-permute-start.4 = (bf16[512,512]{1,0:T(8,128)(2,1)S(1)}, bf16[512,512]{1,0:T(8,128)(2,1)S(1)}, u32[]{:S(2)}, u32[]{:S(2)}) collective-permute-start(bf16[512,512]{1,0:T(8,128)(2,1)S(1)} %get-tuple-element.37.rest_0_), channel_id=1, source_target_pairs={{0,1},{1,0},{2,3},{3,2},{4,5},{5,4},{6,7},{7,6},{8,9},{9,8},{10,11... | collective-permute-start | bytes 1572872 | tf_op jit(solution)/shard_map/ppermute | solution.py:407
  26.9 8.3 %collective-permute-start.8 = (bf16[512,512]{1,0:T(8,128)(2,1)S(1)}, bf16[512,512]{1,0:T(8,128)(2,1)S(1)}, u32[]{:S(2)}, u32[]{:S(2)}) collective-permute-start(bf16[512,512]{1,0:T(8,128)(2,1)S(1)} %get-tuple-element.44.rest_4_), channel_id=1, source_target_pairs={{0,1},{1,0},{2,3},{3,2},{4,5},{5,4},{6,7},{7,6},{8,9},{9,8},{10,11... | collective-permute-start | bytes 1572872 | tf_op jit(solution)/shard_map/ppermute | solution.py:407
  34.0 1.2 collective-permute-start.10
  34.0 2.0 %collective-permute-start.9 = (bf16[512,512]{1,0:T(8,128)(2,1)S(1)}, bf16[512,512]{1,0:T(8,128)(2,1)S(1)}, u32[]{:S(2)}, u32[]{:S(2)}) collective-permute-start(bf16[512,512]{1,0:T(8,128)(2,1)S(1)} %collective-permute-done.6.rest_5_), channel_id=1, source_target_pairs={{0,1},{1,0},{2,3},{3,2},{4,5},{5,4},{6,7},{7,6},{8,9},{9,8},{10,11... | collective-permute-start | bytes 1572872 | tf_op jit(solution)/shard_map/ppermute | solution.py:407
  34.5 2.3 %collective-permute-start.5 = (bf16[512,512]{1,0:T(8,128)(2,1)S(1)}, bf16[512,512]{1,0:T(8,128)(2,1)S(1)}, u32[]{:S(2)}, u32[]{:S(2)}) collective-permute-start(bf16[512,512]{1,0:T(8,128)(2,1)S(1)} %collective-permute-done.rest_1_), channel_id=1, source_target_pairs={{0,1},{1,0},{2,3},{3,2},{4,5},{5,4},{6,7},{7,6},{8,9},{9,8},{10,11... | collective-permute-start | bytes 1572872 | tf_op jit(solution)/shard_map/ppermute | solution.py:407
  39.5 12.9 %collective-permute-start.11 = (bf16[2,2,16,1024]{3,2,1,0:T(8,128)(2,1)S(1)}, bf16[2,2,16,1024]{3,2,1,0:T(8,128)(2,1)S(1)}, u32[]{:S(2)}, u32[]{:S(2)}) collective-permute-start(bf16[2,2,16,1024]{3,2,1,0:T(8,128)(2,1)S(1)} %get-tuple-element.50), channel_id=1, source_target_pairs={{0,8},{4,12},{8,0},{12,4},{1,9},{5,13},{9,1},{13,5},{2,10},{6,14},... | collective-permute-start | bytes 393224 | tf_op jit(solution)/shard_map/ppermute | solution.py:407
  42.4 10.1 %collective-permute-start.12 = (bf16[2,2,16,1024]{3,2,1,0:T(8,128)(2,1)S(1)}, bf16[2,2,16,1024]{3,2,1,0:T(8,128)(2,1)S(1)}, u32[]{:S(2)}, u32[]{:S(2)}) collective-permute-start(bf16[2,2,16,1024]{3,2,1,0:T(8,128)(2,1)S(1)} %get-tuple-element.51), channel_id=1, source_target_pairs={{0,12},{4,8},{8,4},{12,0},{1,13},{5,9},{9,5},{13,1},{2,14},{6,10},... | collective-permute-start | bytes 393224 | tf_op jit(solution)/shard_map/ppermute | solution.py:407
  43.7 9.7 %collective-permute-start.13 = (bf16[2,2,16,1024]{3,2,1,0:T(8,128)(2,1)S(1)}, bf16[2,2,16,1024]{3,2,1,0:T(8,128)(2,1)S(1)}, u32[]{:S(2)}, u32[]{:S(2)}) collective-permute-start(bf16[2,2,16,1024]{3,2,1,0:T(8,128)(2,1)S(1)} %get-tuple-element.52), channel_id=1, source_target_pairs={{0,4},{4,0},{8,12},{12,8},{1,5},{5,1},{9,13},{13,9},{2,6},{6,2},{1... | collective-permute-start | bytes 393224 | tf_op jit(solution)/shard_map/ppermute | solution.py:407
  55.0 13.8 %collective-permute-start.14 = (bf16[2,2,16,1024]{3,2,1,0:T(8,128)(2,1)S(1)}, bf16[2,2,16,1024]{3,2,1,0:T(8,128)(2,1)S(1)}, u32[]{:S(2)}, u32[]{:S(2)}) collective-permute-start(bf16[2,2,16,1024]{3,2,1,0:T(8,128)(2,1)S(1)} %get-tuple-element.54), channel_id=1, source_target_pairs={{0,8},{4,12},{8,0},{12,4},{1,9},{5,13},{9,1},{13,5},{2,10},{6,14},... | collective-permute-start | bytes 393224 | tf_op jit(solution)/shard_map/ppermute | solution.py:407
  59.1 9.6 %collective-permute-start.15 = (bf16[2,2,16,1024]{3,2,1,0:T(8,128)(2,1)S(1)}, bf16[2,2,16,1024]{3,2,1,0:T(8,128)(2,1)S(1)}, u32[]{:S(2)}, u32[]{:S(2)}) collective-permute-start(bf16[2,2,16,1024]{3,2,1,0:T(8,128)(2,1)S(1)} %get-tuple-element.55), channel_id=1, source_target_pairs={{0,12},{4,8},{8,4},{12,0},{1,13},{5,9},{9,5},{13,1},{2,14},{6,10},... | collective-permute-start | bytes 393224 | tf_op jit(solution)/shard_map/ppermute | solution.py:407
  59.6 10.3 %collective-permute-start.16 = (bf16[2,2,16,1024]{3,2,1,0:T(8,128)(2,1)S(1)}, bf16[2,2,16,1024]{3,2,1,0:T(8,128)(2,1)S(1)}, u32[]{:S(2)}, u32[]{:S(2)}) collective-permute-start(bf16[2,2,16,1024]{3,2,1,0:T(8,128)(2,1)S(1)} %get-tuple-element.56), channel_id=1, source_target_pairs={{0,4},{4,0},{8,12},{12,8},{1,5},{5,1},{9,13},{13,9},{2,6},{6,2},{1... | collective-permute-start | bytes 393224 | tf_op jit(solution)/shard_map/ppermute | solution.py:407
  72.0 5.3 %collective-permute-start.17 = (bf16[2,2,64,256]{3,2,1,0:T(8,128)(2,1)}, bf16[2,2,64,256]{3,2,1,0:T(8,128)(2,1)}, u32[]{:S(2)}, u32[]{:S(2)}) collective-permute-start(bf16[2,2,64,256]{3,2,1,0:T(8,128)(2,1)} %get-tuple-element.58), channel_id=1, source_target_pairs={{0,2},{2,0},{1,3},{3,1},{4,6},{6,4},{5,7},{7,5},{8,10},{10,8},{9,1... | collective-permute-start | bytes 393224 | tf_op jit(solution)/shard_map/ppermute | solution.py:407
  78.3 12.0 %collective-permute-start.18 = (bf16[2,2,64,256]{3,2,1,0:T(8,128)(2,1)S(1)}, bf16[2,2,64,256]{3,2,1,0:T(8,128)(2,1)S(1)}, u32[]{:S(2)}, u32[]{:S(2)}) collective-permute-start(bf16[2,2,64,256]{3,2,1,0:T(8,128)(2,1)S(1)} %add_convert_fusion.1.rest_0_), channel_id=1, source_target_pairs={{0,8},{4,12},{8,0},{12,4},{1,9},{5,13},{9,1},{13,5},{2,10},{6,14},... | collective-permute-start | bytes 393224 | tf_op jit(solution)/shard_map/ppermute | solution.py:407
  80.2 10.1 %collective-permute-start.19 = (bf16[2,2,64,256]{3,2,1,0:T(8,128)(2,1)S(1)}, bf16[2,2,64,256]{3,2,1,0:T(8,128)(2,1)S(1)}, u32[]{:S(2)}, u32[]{:S(2)}) collective-permute-start(bf16[2,2,64,256]{3,2,1,0:T(8,128)(2,1)S(1)} %add_convert_fusion.1.rest_0_), channel_id=1, source_target_pairs={{0,12},{4,8},{8,4},{12,0},{1,13},{5,9},{9,5},{13,1},{2,14},{6,10},... | collective-permute-start | bytes 393224 | tf_op jit(solution)/shard_map/ppermute | solution.py:407
  83.0 8.1 %collective-permute-start.20 = (bf16[2,2,64,256]{3,2,1,0:T(8,128)(2,1)S(1)}, bf16[2,2,64,256]{3,2,1,0:T(8,128)(2,1)S(1)}, u32[]{:S(2)}, u32[]{:S(2)}) collective-permute-start(bf16[2,2,64,256]{3,2,1,0:T(8,128)(2,1)S(1)} %add_convert_fusion.1.rest_0_), channel_id=1, source_target_pairs={{0,4},{4,0},{8,12},{12,8},{1,5},{5,1},{9,13},{13,9},{2,6},{6,2},{1... | collective-permute-start | bytes 393224 | tf_op jit(solution)/shard_map/ppermute | solution.py:407
  91.5 5.0 %collective-permute-start.21 = (bf16[2,2,64,256]{3,2,1,0:T(8,128)(2,1)S(1)}, bf16[2,2,64,256]{3,2,1,0:T(8,128)(2,1)S(1)}, u32[]{:S(2)}, u32[]{:S(2)}) collective-permute-start(bf16[2,2,64,256]{3,2,1,0:T(8,128)(2,1)S(1)} %shard_map.105.n_ref), channel_id=1, source_target_pairs={{0,2},{2,0},{1,3},{3,1},{4,6},{6,4},{5,7},{7,5},{8,10},{10,8},{9,1... | collective-permute-start | bytes 393224 | tf_op jit(solution)/shard_map/ppermute | solution.py:407
  98.1 10.6 %collective-permute-start.22 = (bf16[2,2,16,1024]{3,2,1,0:T(8,128)(2,1)S(1)}, bf16[2,2,16,1024]{3,2,1,0:T(8,128)(2,1)S(1)}, u32[]{:S(2)}, u32[]{:S(2)}) collective-permute-start(bf16[2,2,16,1024]{3,2,1,0:T(8,128)(2,1)S(1)} %get-tuple-element.60), channel_id=1, source_target_pairs={{0,8},{4,12},{8,0},{12,4},{1,9},{5,13},{9,1},{13,5},{2,10},{6,14},... | collective-permute-start | bytes 393224 | tf_op jit(solution)/shard_map/ppermute | solution.py:407
  99.8 8.9 %collective-permute-start.23 = (bf16[2,2,16,1024]{3,2,1,0:T(8,128)(2,1)S(1)}, bf16[2,2,16,1024]{3,2,1,0:T(8,128)(2,1)S(1)}, u32[]{:S(2)}, u32[]{:S(2)}) collective-permute-start(bf16[2,2,16,1024]{3,2,1,0:T(8,128)(2,1)S(1)} %get-tuple-element.61), channel_id=1, source_target_pairs={{0,12},{4,8},{8,4},{12,0},{1,13},{5,9},{9,5},{13,1},{2,14},{6,10},... | collective-permute-start | bytes 393224 | tf_op jit(solution)/shard_map/ppermute | solution.py:407
  101.6 7.5 %collective-permute-start.24 = (bf16[2,2,16,1024]{3,2,1,0:T(8,128)(2,1)S(1)}, bf16[2,2,16,1024]{3,2,1,0:T(8,128)(2,1)S(1)}, u32[]{:S(2)}, u32[]{:S(2)}) collective-permute-start(bf16[2,2,16,1024]{3,2,1,0:T(8,128)(2,1)S(1)} %get-tuple-element.62), channel_id=1, source_target_pairs={{0,4},{4,0},{8,12},{12,8},{1,5},{5,1},{9,13},{13,9},{2,6},{6,2},{1... | collective-permute-start | bytes 393224 | tf_op jit(solution)/shard_map/ppermute | solution.py:407
  110.1 10.4 %collective-permute-start.25 = (bf16[2,2,16,1024]{3,2,1,0:T(8,128)(2,1)S(1)}, bf16[2,2,16,1024]{3,2,1,0:T(8,128)(2,1)S(1)}, u32[]{:S(2)}, u32[]{:S(2)}) collective-permute-start(bf16[2,2,16,1024]{3,2,1,0:T(8,128)(2,1)S(1)} %get-tuple-element.64), channel_id=1, source_target_pairs={{0,8},{4,12},{8,0},{12,4},{1,9},{5,13},{9,1},{13,5},{2,10},{6,14},... | collective-permute-start | bytes 393224 | tf_op jit(solution)/shard_map/ppermute | solution.py:407
  111.5 9.0 %collective-permute-start.26 = (bf16[2,2,16,1024]{3,2,1,0:T(8,128)(2,1)S(1)}, bf16[2,2,16,1024]{3,2,1,0:T(8,128)(2,1)S(1)}, u32[]{:S(2)}, u32[]{:S(2)}) collective-permute-start(bf16[2,2,16,1024]{3,2,1,0:T(8,128)(2,1)S(1)} %get-tuple-element.65), channel_id=1, source_target_pairs={{0,12},{4,8},{8,4},{12,0},{1,13},{5,9},{9,5},{13,1},{2,14},{6,10},... | collective-permute-start | bytes 393224 | tf_op jit(solution)/shard_map/ppermute | solution.py:407
  114.5 6.9 %collective-permute-start.27 = (bf16[2,2,16,1024]{3,2,1,0:T(8,128)(2,1)S(1)}, bf16[2,2,16,1024]{3,2,1,0:T(8,128)(2,1)S(1)}, u32[]{:S(2)}, u32[]{:S(2)}) collective-permute-start(bf16[2,2,16,1024]{3,2,1,0:T(8,128)(2,1)S(1)} %get-tuple-element.66), channel_id=1, source_target_pairs={{0,4},{4,0},{8,12},{12,8},{1,5},{5,1},{9,13},{13,9},{2,6},{6,2},{1... | collective-permute-start | bytes 393224 | tf_op jit(solution)/shard_map/ppermute | solution.py:407
  122.2 5.0 %collective-permute-start.28 = (bf16[2,2,64,256]{3,2,1,0:T(8,128)(2,1)S(1)}, bf16[2,2,64,256]{3,2,1,0:T(8,128)(2,1)S(1)}, u32[]{:S(2)}, u32[]{:S(2)}) collective-permute-start(bf16[2,2,64,256]{3,2,1,0:T(8,128)(2,1)S(1)} %get-tuple-element.68), channel_id=1, source_target_pairs={{0,2},{2,0},{1,3},{3,1},{4,6},{6,4},{5,7},{7,5},{8,10},{10,8},{9,1... | collective-permute-start | bytes 393224 | tf_op jit(solution)/shard_map/ppermute | solution.py:407
  127.3 9.8 %collective-permute-start.29 = (bf16[2,2,64,256]{3,2,1,0:T(8,128)(2,1)S(1)}, bf16[2,2,64,256]{3,2,1,0:T(8,128)(2,1)S(1)}, u32[]{:S(2)}, u32[]{:S(2)}) collective-permute-start(bf16[2,2,64,256]{3,2,1,0:T(8,128)(2,1)S(1)} %add_convert_fusion.rest_0_), channel_id=1, source_target_pairs={{0,8},{4,12},{8,0},{12,4},{1,9},{5,13},{9,1},{13,5},{2,10},{6,14},... | collective-permute-start | bytes 393224 | tf_op jit(solution)/shard_map/ppermute | solution.py:407
  129.4 7.8 %collective-permute-start.30 = (bf16[2,2,64,256]{3,2,1,0:T(8,128)(2,1)S(1)}, bf16[2,2,64,256]{3,2,1,0:T(8,128)(2,1)S(1)}, u32[]{:S(2)}, u32[]{:S(2)}) collective-permute-start(bf16[2,2,64,256]{3,2,1,0:T(8,128)(2,1)S(1)} %add_convert_fusion.rest_0_), channel_id=1, source_target_pairs={{0,12},{4,8},{8,4},{12,0},{1,13},{5,9},{9,5},{13,1},{2,14},{6,10},... | collective-permute-start | bytes 393224 | tf_op jit(solution)/shard_map/ppermute | solution.py:407
  130.7 7.2 %collective-permute-start.31 = (bf16[2,2,64,256]{3,2,1,0:T(8,128)(2,1)S(1)}, bf16[2,2,64,256]{3,2,1,0:T(8,128)(2,1)S(1)}, u32[]{:S(2)}, u32[]{:S(2)}) collective-permute-start(bf16[2,2,64,256]{3,2,1,0:T(8,128)(2,1)S(1)} %add_convert_fusion.rest_0_), channel_id=1, source_target_pairs={{0,4},{4,0},{8,12},{12,8},{1,5},{5,1},{9,13},{13,9},{2,6},{6,2},{1... | collective-permute-start | bytes 393224 | tf_op jit(solution)/shard_map/ppermute | solution.py:407
  (19 other events, 476.1 us)

commit v8 on v7

--- a/solution.py
+++ b/solution.py
@@ -111,29 +111,23 @@
     steps = half // BLOCK
 
     def body(place_ref, flags, x_ref, *outs):
+        lane = lax.broadcasted_iota(jnp.int32, (1, rcv), 1) // BLOCK
         for flip in (1, 0):
             for j in range(per_dev):
                 out = outs[flip * per_dev + j]
                 for step in range(steps):
                     block = (place_ref[0] ^ flip) * steps + step
+                    on = flags[j, pl.ds(block, 1), :].astype(F32)
+                    row = sum(jnp.where(lane == r, on[:, r : r + 1], 0.0) for r in range(rcv // BLOCK))
+                    gate = jnp.broadcast_to(row, (BLOCK, rcv)).astype(BF16)
                     rows = pl.ds(pl.multiple_of(block * BLOCK, BLOCK), BLOCK)
                     to = slice(step * BLOCK, (step + 1) * BLOCK)
-                    for r in range(rcv // BLOCK):
-                        on = flags[j, block, r] != 0
-                        spots = [(c, slice(r * BLOCK, (r + 1) * BLOCK)) for c in range(2)]
-
-                        @pl.when(on)
-                        def _():
-                            for c, at in spots:
-                                out[to, c * rcv + at.start : c * rcv + at.stop] = x_ref[j, c, rows, at]
-
-                        @pl.when(jnp.logical_not(on))
-                        def _():
-                            for c, at in spots:
-                                out[to, c * rcv + at.start : c * rcv + at.stop] = jnp.zeros((BLOCK, BLOCK), BF16)
+                    for c in range(2):
+                        out[to, c * rcv : (c + 1) * rcv] = x_ref[j, c, rows, :] * gate
 
     shape = jax.ShapeDtypeStruct((half, 2 * rcv), BF16)
-    outs = call(body, (place, aperture), [(response, whole(response))], [(shape, whole(shape))] * (2 * per_dev), (1,))
+    inputs = [(v, whole(v)) for v in (aperture, response)]
+    outs = call(body, (place,), inputs, [(shape, whole(shape))] * (2 * per_dev), (1,))
     return outs[:per_dev], outs[per_dev:]
 
 
@@ -169,6 +163,81 @@
         scratch=[pltpu.VMEM((count, ROWS * own), BF16)],
         flops=2 * 2 * freq_devs * per_dev * own * rows * rcv,
     )
+
+
+def summed(parts):
+    def body(*refs):
+        total = sum(ref[...].astype(F32) for ref in refs[:-2])
+        refs[-2][...] = total
+        refs[-1][...] = total.astype(BF16)
+
+    shapes = [jax.ShapeDtypeStruct(parts[0].shape, kind) for kind in (F32, BF16)]
+    return call(body, (), [(v, whole(v)) for v in parts], [(v, whole(v)) for v in shapes], (1,))
+
+
+def added(keep, received):
+    def body(k_ref, r_ref, out):
+        out[...] = (k_ref[...] + r_ref[...].astype(F32)).astype(BF16)
+
+    shape = jax.ShapeDtypeStruct(keep.shape, BF16)
+    (out,) = call(body, (), [(v, whole(v)) for v in (keep, received)], [(shape, whole(shape))], (1,))
+    return out
+
+
+def src_onsets(onset, places, half_rows, first, share, width):
+    def body(freq, rblk, sblk, o_ref, own, other):
+        lanes = pl.ds(pl.multiple_of(rblk[0] * width, BLOCK), width)
+        for core, out in ((sblk[0], own), (1 - sblk[0], other)):
+            spot = pl.multiple_of(core * half_rows + first + freq[0] * share, ROWS)
+            out[...] = o_ref[pl.ds(spot, share), lanes]
+
+    shape = jax.ShapeDtypeStruct((share, width), onset.dtype)
+    return call(body, places, [(onset, whole(onset))], [(shape, whole(shape))] * 2, (1,))
+
+
+def sine_terms():
+    square = (np.cos(np.linspace(0.0, math.pi, 200)) + 1.0) / 32.0
+    y = np.sqrt(np.maximum(square, 1e-12))
+    return [float(v) for v in np.polynomial.polynomial.polyfit(square, np.sin(2.0 * math.pi * y) / y, 6)]
+
+
+def phase_tables(onsets, places, freq_devs, per_dev, samples, rows=None, first=0, half_rows=0):
+    terms = sine_terms()
+    count = rows or onsets[0].shape[0]
+    widths = [v.shape[1] for v in onsets]
+
+    def sine(y):
+        square = y * y
+        total = jnp.full_like(y, terms[-1])
+        for term in terms[-2::-1]:
+            total = total * square + term
+        return total * y
+
+    def body(freq, _, sblk, *refs):
+        cosines, sines, fraction = refs[-3:]
+        at = 0
+        for ref, width in zip(refs, widths):
+            if rows:
+                value = ref[pl.ds(pl.multiple_of(sblk[0] * half_rows + first, ROWS), rows), :]
+            else:
+                value = ref[...]
+            part = value.astype(F32) * (1.0 / samples)
+            to = slice(at, at + width)
+            fraction[:, to] = part
+            for step, way in enumerate(ways(freq_devs)):
+                for j in range(per_dev):
+                    order = ((freq[0] ^ way) * per_dev + j + 1).astype(F32)
+                    turn = part * order
+                    turn = turn - jnp.floor(turn + 0.5)
+                    size = jnp.abs(turn)
+                    folded = jnp.where(size > 0.25, jnp.where(turn > 0.0, 0.5, -0.5) - turn, turn)
+                    cosines[step, j, :, to] = sine(0.25 - size)
+                    sines[step, j, :, to] = sine(folded)
+            at += width
+
+    table = jax.ShapeDtypeStruct((freq_devs, per_dev, count, sum(widths)), F32)
+    shapes = [table, table, jax.ShapeDtypeStruct((count, sum(widths)), F32)]
+    return call(body, places, [(v, whole(v)) for v in onsets], [(v, whole(v)) for v in shapes], (1,))
 
 
 def down_products(near, far, responses, freq_place, freq_devs):
@@ -415,14 +484,6 @@
     return dealt_out([value] * count)
 
 
-def phases(onset, freq_index, freq_devs, per_dev, samples):
-    steps = jnp.asarray(ways(freq_devs), jnp.int32)
-    order = (freq_index ^ steps)[:, None] * per_dev + lax.iota(jnp.int32, per_dev)[None, :] + 1
-    phase = order[:, :, None, None] * onset[None, None] % samples
-    angle = phase.astype(F32) * (2.0 * math.pi / samples)
-    return jnp.cos(angle), jnp.sin(angle), onset.astype(F32) * (1.0 / samples)
-
-
 def on_device(initial, response, aperture, onset_rcv, onset_src):
     freq_devs = lax.axis_size("freq")
     per_dev = response.shape[0]
@@ -435,9 +496,9 @@
     rblk_index = lax.axis_index("rblk")
     sblk_index = lax.axis_index("sblk")
     freq_place = freq_index.reshape(1)
-    rblk_place = rblk_index.reshape(1)
-
-    kept, moved = masked_halves(response, aperture, rblk_place)
+    places = tuple(index.reshape(1) for index in (freq_index, rblk_index, sblk_index))
+
+    kept, moved = masked_halves(response, aperture, places[1])
     moved = [exchanged(v, "rblk", 1) for v in moved]
     kept_pair = [exchanged(v, "sblk", 1) for v in kept]
     responses = None
@@ -449,8 +510,7 @@
     for chunk in range(CHUNKS):
         first = chunk * rows
         parts = first_spectra(initial, forward, freq_place, freq_devs, per_dev, first, rows)
-        sums = sum(v.astype(F32) for v in dealt_out(parts))
-        spectra = sums.astype(BF16)
+        sums, spectra = summed(dealt_out(parts))
         far = exchanged(spectra, "rblk", 1)
         if responses is None:
             before, moved_pair = spectra, []
@@ -461,21 +521,16 @@
                 before = far
             responses = [((kept[j], moved[j]), (kept_pair[j], moved_pair[j])) for j in range(per_dev)]
 
-        def src_onsets(core):
-            spot = core * half_rows + first + freq_index * share
-            return lax.dynamic_slice(onset_src, (spot, rblk_index * src_width), (share, src_width))
-
-        onsets = [src_onsets(sblk_index), exchanged(src_onsets(1 - sblk_index), "sblk", 1)]
-        src_tables = phases(jnp.concatenate(onsets, 1), freq_index, freq_devs, per_dev, samples)
-        onsets = lax.dynamic_slice_in_dim(onset_rcv, sblk_index * half_rows + first, rows, 0)
-        rcv_tables = phases(onsets, freq_index, freq_devs, per_dev, samples)
+        own, other = src_onsets(onset_src, places, half_rows, first, share, src_width)
+        src_tables = phase_tables((own, exchanged(other, "sblk", 1)), places, freq_devs, per_dev, samples)
+        rcv_tables = phase_tables((onset_rcv,), places, freq_devs, per_dev, samples, rows, first, half_rows)
 
         for step in range(ITERS):
             far = far if step == 0 else exchanged(spectra, "rblk", 1)
             messages = dealt_out(down_products(spectra, far, responses, freq_place, freq_devs))
             messages = windowed(messages, src_tables, matrix, freq_place, per_dev, share)
             keep, send = up_products(dealt_out(messages), responses, freq_place, rows)
-            back = (keep + exchanged(send, "rblk", 1).astype(F32)).astype(BF16)
+            back = added(keep, exchanged(send, "rblk", 1))
             messages = spread(back, freq_devs)
             if step < ITERS - 1:
                 spectra = next_spectra(sums, messages, rcv_tables, matrix, freq_place)

time: 142 us -> 143 us (level)
  other arithmetic: 7.06 us -> 0 us
  local copies, waits for them, and re-layouts: 7.61 us -> 12.3 us
  waiting for transfers between devices: 70.7 us -> 74 us
    unnamed x39 -> x33, local copies, waits for them, and re-layouts: 6.84 us -> 12.3 us
    sin x2 -> x0, other arithmetic: 4.21 us -> none  [phases(): return (jnp.cos(angle), jnp.sin(angle), onset.astype(F32) * (1.0 / samples))]
    ppermute x32, waiting for transfers between devices: 70.7 us -> 74 us  [exchanged(): lax.ppermute(value, axis, [(i, i ^ step) for i in range(lax.axis_size(axi...]
    convert_element_type x3 -> x0, other arithmetic: 1.75 us -> none  [the longest x2 1.04 us: on_device(): back = (keep + exchanged(send, 'rblk', 1).astype(F32)).astype(BF16)]
    pallas_call x10 -> x16, Pallas kernels: 15.3 us -> 15.5 us  [call(): pl.pallas_call(body, grid_spec=pltpu.PrefetchScalarGridSpec(num_scalar_pr...]
  transfers between devices with their start and end apart: 32 -> 32, of which waited for: 21 -> 21; matrix products, arithmetic and copies ran while one was open for 5% -> 0% of each run, Pallas kernels for 1% -> 2%
where the time goes in v8:
time: 143 us; the launch traced here: 142 us
  waiting for transfers between devices  74 us (52%)
  starting transfers between devices  40.5 us (28%)
  Pallas kernels  15.5 us (11%)
  local copies, waits for them, and re-layouts  12.3 us (9%)
    ppermute x32, waiting for transfers between devices, exchanged(): lax.ppermute(value, axis, [(i, i ^ step) for i in range(lax.axis_size(axi...  74 us
    ppermute x32, starting transfers between devices, exchanged(): lax.ppermute(value, axis, [(i, i ^ step) for i in range(lax.axis_size(axi...  40.5 us
    pallas_call x16, Pallas kernels, call(): pl.pallas_call(body, grid_spec=pltpu.PrefetchScalarGridSpec(num_scalar_pr...  15.5 us
    unnamed x33, local copies, waits for them, and re-layouts  12.3 us
  transfers between devices with their start and end apart: 32, of which 21 were waited for; matrix products, arithmetic and copies ran while one was open for 0% of the time, Pallas kernels for 2%

profile of v8, /device:TPU:0, one launch (start us, length us, event | category | flops | bytes accessed | tf_op | source)
XLA Modules:
  0.0 142.3 jit_solution(15688413905210718386)
XLA Ops:
  0.8 1.6 %copy-done.8 = bf16[2,2,1024,256]{3,2,1,0:T(8,128)(2,1)S(1)} copy-done((bf16[2,2,1024,256]{3,2,1,0:T(8,128)(2,1)S(1)}, bf16[2,2,1024,256]{3,2,1,0:T(8,128)(2,1)}, u32[]{:S(2)}) %copy-start.8) | copy-done | bytes 2097176
  3.5 2.9 %collective-permute-start.6 = (bf16[512,512]{1,0:T(8,128)(2,1)}, bf16[512,512]{1,0:T(8,128)(2,1)S(1)}, u32[]{:S(2)}, u32[]{:S(2)}) collective-permute-start(bf16[512,512]{1,0:T(8,128)(2,1)} %get-tuple-element.56), channel_id=1, source_target_pairs={{0,2},{2,0},{1,3},{3,1},{4,6},{6,4},{5,7},{7,5},{8,10},{10,8},{9,1... | collective-permute-start | bytes 1572872 | tf_op jit(solution)/shard_map/ppermute | solution.py:476
  6.5 2.2 %copy-done = bf16[64,128,256]{2,1,0:T(8,128)(2,1)S(1)} copy-done((bf16[64,128,256]{2,1,0:T(8,128)(2,1)S(1)}, bf16[64,128,256]{2,1,0:T(8,128)(2,1)}, u32[]{:S(2)}) %copy-start) | copy-done | bytes 4194328
  10.3 3.2 %collective-permute-start.1 = (bf16[2,2,64,256]{3,2,1,0:T(8,128)(2,1)S(1)}, bf16[2,2,64,256]{3,2,1,0:T(8,128)(2,1)S(1)}, u32[]{:S(2)}, u32[]{:S(2)}) collective-permute-start(bf16[2,2,64,256]{3,2,1,0:T(8,128)(2,1)S(1)} %get-tuple-element.50), channel_id=1, source_target_pairs={{0,8},{4,12},{8,0},{12,4},{1,9},{5,13},{9,1},{13,5},{2,10},{6,14},... | collective-permute-start | bytes 393224 | tf_op jit(solution)/shard_map/ppermute | solution.py:476
  15.1 8.2 %collective-permute-done.1.refs_1_ = bf16[2,2,64,256]{3,2,1,0:T(8,128)(2,1)S(1)} collective-permute-done((bf16[2,2,64,256]{3,2,1,0:T(8,128)(2,1)S(1)}, bf16[2,2,64,256]{3,2,1,0:T(8,128)(2,1)S(1)}, u32[]{:S(2)}, u32[]{:S(2)}) %collective-permute-start.1) | collective-permute-done | bytes 131104 | tf_op jit(solution)/shard_map/ppermute | solution.py:476
  24.2 1.5 %collective-permute-start.7 = (bf16[2,2,64,256]{3,2,1,0:T(8,128)(2,1)S(1)}, bf16[2,2,64,256]{3,2,1,0:T(8,128)(2,1)S(1)}, u32[]{:S(2)}, u32[]{:S(2)}) collective-permute-start(bf16[2,2,64,256]{3,2,1,0:T(8,128)(2,1)S(1)} %get-tuple-element.67.n_ref), channel_id=1, source_target_pairs={{0,2},{2,0},{1,3},{3,1},{4,6},{6,4},{5,7},{7,5},{8,10},{10,8},{9,1... | collective-permute-start | bytes 393224 | tf_op jit(solution)/shard_map/ppermute | solution.py:476
  26.2 6.4 %collective-permute-done.7.f_ref = bf16[2,2,64,256]{3,2,1,0:T(8,128)(2,1)S(1)} collective-permute-done((bf16[2,2,64,256]{3,2,1,0:T(8,128)(2,1)S(1)}, bf16[2,2,64,256]{3,2,1,0:T(8,128)(2,1)S(1)}, u32[]{:S(2)}, u32[]{:S(2)}) %collective-permute-start.7) | collective-permute-done | bytes 131104 | tf_op jit(solution)/shard_map/ppermute | solution.py:476
  35.3 2.2 %shard_map.88 = (bf16[2,2,16,1024]{3,2,1,0:T(8,128)(2,1)S(1)}, bf16[2,2,16,1024]{3,2,1,0:T(8,128)(2,1)}, bf16[2,2,16,1024]{3,2,1,0:T(8,128)(2,1)}, bf16[2,2,16,1024]{3,2,1,0:T(8,128)(2,1)}) custom-call(s32[1]{0:T(128)} %bitcast.place_ref.freq, bf16[2,2,64,256]{3,2,1,0:T(8,128)(2,1)S(1)} %get-tuple-element.67.n_ref, ...), custom_call_target="tpu_custom_call" | custom-call | flops 536870912 | bytes 4980736 | tf_op jit(solution)/shard_map/pallas_call | solution.py:87
  38.3 2.8 %collective-permute-start.11 = (bf16[2,2,16,1024]{3,2,1,0:T(8,128)(2,1)}, bf16[2,2,16,1024]{3,2,1,0:T(8,128)(2,1)}, u32[]{:S(2)}, u32[]{:S(2)}) collective-permute-start(bf16[2,2,16,1024]{3,2,1,0:T(8,128)(2,1)} %get-tuple-element.70), channel_id=1, source_target_pairs={{0,8},{4,12},{8,0},{12,4},{1,9},{5,13},{9,1},{13,5},{2,10},{6,14},... | collective-permute-start | bytes 393224 | tf_op jit(solution)/shard_map/ppermute | solution.py:476
  45.7 5.8 %collective-permute-done.11.rest_1_ = bf16[2,2,16,1024]{3,2,1,0:T(8,128)(2,1)} collective-permute-done((bf16[2,2,16,1024]{3,2,1,0:T(8,128)(2,1)}, bf16[2,2,16,1024]{3,2,1,0:T(8,128)(2,1)}, u32[]{:S(2)}, u32[]{:S(2)}) %collective-permute-start.11) | collective-permute-done | bytes 131104 | tf_op jit(solution)/shard_map/ppermute | solution.py:476
  52.3 2.1 %shard_map.89 = (bf16[2,2,16,1024]{3,2,1,0:T(8,128)(2,1)S(1)}, bf16[2,2,16,1024]{3,2,1,0:T(8,128)(2,1)S(1)}, bf16[2,2,16,1024]{3,2,1,0:T(8,128)(2,1)S(1)}, bf16[2,2,16,1024]{3,2,1,0:T(8,128)(2,1)S(1)}) custom-call(s32[1]{0:T(128)} %bitcast.place_ref.freq, f32[4,2,16,1024]{3,2,1,0:T(8,128)S(1)} %get-tuple-element.60.c_ref, ...), custom_call_target="tpu_custom_call" | custom-call | flops 134217728 | bytes 2293760 | tf_op jit(solution)/shard_map/pallas_call | solution.py:87
  54.4 4.2 %collective-permute-start.14 = (bf16[2,2,16,1024]{3,2,1,0:T(8,128)(2,1)S(1)}, bf16[2,2,16,1024]{3,2,1,0:T(8,128)(2,1)S(1)}, u32[]{:S(2)}, u32[]{:S(2)}) collective-permute-start(bf16[2,2,16,1024]{3,2,1,0:T(8,128)(2,1)S(1)} %get-tuple-element.74), channel_id=1, source_target_pairs={{0,8},{4,12},{8,0},{12,4},{1,9},{5,13},{9,1},{13,5},{2,10},{6,14},... | collective-permute-start | bytes 393224 | tf_op jit(solution)/shard_map/ppermute | solution.py:476
  59.3 9.0 %collective-permute-done.14.rest_9_ = bf16[2,2,16,1024]{3,2,1,0:T(8,128)(2,1)S(1)} collective-permute-done((bf16[2,2,16,1024]{3,2,1,0:T(8,128)(2,1)S(1)}, bf16[2,2,16,1024]{3,2,1,0:T(8,128)(2,1)S(1)}, u32[]{:S(2)}, u32[]{:S(2)}) %collective-permute-start.14) | collective-permute-done | bytes 131104 | tf_op jit(solution)/shard_map/ppermute | solution.py:476
  72.2 1.5 %collective-permute-start.17 = (bf16[2,2,64,256]{3,2,1,0:T(8,128)(2,1)S(1)}, bf16[2,2,64,256]{3,2,1,0:T(8,128)(2,1)S(1)}, u32[]{:S(2)}, u32[]{:S(2)}) collective-permute-start(bf16[2,2,64,256]{3,2,1,0:T(8,128)(2,1)S(1)} %get-tuple-element.78), channel_id=1, source_target_pairs={{0,2},{2,0},{1,3},{3,1},{4,6},{6,4},{5,7},{7,5},{8,10},{10,8},{9,1... | collective-permute-start | bytes 393224 | tf_op jit(solution)/shard_map/ppermute | solution.py:476
  73.7 3.5 %collective-permute-done.17.r_ref = bf16[2,2,64,256]{3,2,1,0:T(8,128)(2,1)S(1)} collective-permute-done((bf16[2,2,64,256]{3,2,1,0:T(8,128)(2,1)S(1)}, bf16[2,2,64,256]{3,2,1,0:T(8,128)(2,1)S(1)}, u32[]{:S(2)}, u32[]{:S(2)}) %collective-permute-start.17) | collective-permute-done | bytes 131104 | tf_op jit(solution)/shard_map/ppermute | solution.py:476
  77.2 1.9 %collective-permute-start.18 = (bf16[2,2,64,256]{3,2,1,0:T(8,128)(2,1)S(1)}, bf16[2,2,64,256]{3,2,1,0:T(8,128)(2,1)S(1)}, u32[]{:S(2)}, u32[]{:S(2)}) collective-permute-start(bf16[2,2,64,256]{3,2,1,0:T(8,128)(2,1)S(1)} %shard_map.91.rest_0_), channel_id=1, source_target_pairs={{0,8},{4,12},{8,0},{12,4},{1,9},{5,13},{9,1},{13,5},{2,10},{6,14},... | collective-permute-start | bytes 393224 | tf_op jit(solution)/shard_map/ppermute | solution.py:476
  79.2 2.8 %collective-permute-start.19 = (bf16[2,2,64,256]{3,2,1,0:T(8,128)(2,1)S(1)}, bf16[2,2,64,256]{3,2,1,0:T(8,128)(2,1)S(1)}, u32[]{:S(2)}, u32[]{:S(2)}) collective-permute-start(bf16[2,2,64,256]{3,2,1,0:T(8,128)(2,1)S(1)} %shard_map.91.rest_0_), channel_id=1, source_target_pairs={{0,12},{4,8},{8,4},{12,0},{1,13},{5,9},{9,5},{13,1},{2,14},{6,10},... | collective-permute-start | bytes 393224 | tf_op jit(solution)/shard_map/ppermute | solution.py:476
  82.7 6.5 %collective-permute-done.18.rest_1_ = bf16[2,2,64,256]{3,2,1,0:T(8,128)(2,1)S(1)} collective-permute-done((bf16[2,2,64,256]{3,2,1,0:T(8,128)(2,1)S(1)}, bf16[2,2,64,256]{3,2,1,0:T(8,128)(2,1)S(1)}, u32[]{:S(2)}, u32[]{:S(2)}) %collective-permute-start.18) | collective-permute-done | bytes 131104 | tf_op jit(solution)/shard_map/ppermute | solution.py:476
  90.4 1.5 %collective-permute-start.21 = (bf16[2,2,64,256]{3,2,1,0:T(8,128)(2,1)S(1)}, bf16[2,2,64,256]{3,2,1,0:T(8,128)(2,1)S(1)}, u32[]{:S(2)}, u32[]{:S(2)}) collective-permute-start(bf16[2,2,64,256]{3,2,1,0:T(8,128)(2,1)S(1)} %shard_map.92.n_ref), channel_id=1, source_target_pairs={{0,2},{2,0},{1,3},{3,1},{4,6},{6,4},{5,7},{7,5},{8,10},{10,8},{9,1... | collective-permute-start | bytes 393224 | tf_op jit(solution)/shard_map/ppermute | solution.py:476
  92.0 3.5 %collective-permute-done.21.f_ref = bf16[2,2,64,256]{3,2,1,0:T(8,128)(2,1)S(1)} collective-permute-done((bf16[2,2,64,256]{3,2,1,0:T(8,128)(2,1)S(1)}, bf16[2,2,64,256]{3,2,1,0:T(8,128)(2,1)S(1)}, u32[]{:S(2)}, u32[]{:S(2)}) %collective-permute-start.21) | collective-permute-done | bytes 131104 | tf_op jit(solution)/shard_map/ppermute | solution.py:476
  95.5 1.5 %shard_map.93 = (bf16[2,2,16,1024]{3,2,1,0:T(8,128)(2,1)S(1)}, bf16[2,2,16,1024]{3,2,1,0:T(8,128)(2,1)S(1)}, bf16[2,2,16,1024]{3,2,1,0:T(8,128)(2,1)S(1)}, bf16[2,2,16,1024]{3,2,1,0:T(8,128)(2,1)S(1)}) custom-call(s32[1]{0:T(128)} %bitcast.place_ref.freq, bf16[2,2,64,256]{3,2,1,0:T(8,128)(2,1)S(1)} %shard_map.92.n_ref, ...), custom_call_target="tpu_custom_call" | custom-call | flops 536870912 | bytes 4980736 | tf_op jit(solution)/shard_map/pallas_call | solution.py:87
  97.0 1.8 %collective-permute-start.22 = (bf16[2,2,16,1024]{3,2,1,0:T(8,128)(2,1)S(1)}, bf16[2,2,16,1024]{3,2,1,0:T(8,128)(2,1)S(1)}, u32[]{:S(2)}, u32[]{:S(2)}) collective-permute-start(bf16[2,2,16,1024]{3,2,1,0:T(8,128)(2,1)S(1)} %get-tuple-element.80), channel_id=1, source_target_pairs={{0,8},{4,12},{8,0},{12,4},{1,9},{5,13},{9,1},{13,5},{2,10},{6,14},... | collective-permute-start | bytes 393224 | tf_op jit(solution)/shard_map/ppermute | solution.py:476
  98.8 1.7 %collective-permute-start.23 = (bf16[2,2,16,1024]{3,2,1,0:T(8,128)(2,1)S(1)}, bf16[2,2,16,1024]{3,2,1,0:T(8,128)(2,1)S(1)}, u32[]{:S(2)}, u32[]{:S(2)}) collective-permute-start(bf16[2,2,16,1024]{3,2,1,0:T(8,128)(2,1)S(1)} %get-tuple-element.81), channel_id=1, source_target_pairs={{0,12},{4,8},{8,4},{12,0},{1,13},{5,9},{9,5},{13,1},{2,14},{6,10},... | collective-permute-start | bytes 393224 | tf_op jit(solution)/shard_map/ppermute | solution.py:476
  100.5 7.1 %collective-permute-done.22.rest_1_ = bf16[2,2,16,1024]{3,2,1,0:T(8,128)(2,1)S(1)} collective-permute-done((bf16[2,2,16,1024]{3,2,1,0:T(8,128)(2,1)S(1)}, bf16[2,2,16,1024]{3,2,1,0:T(8,128)(2,1)S(1)}, u32[]{:S(2)}, u32[]{:S(2)}) %collective-permute-start.22) | collective-permute-done | bytes 131104 | tf_op jit(solution)/shard_map/ppermute | solution.py:476
  110.5 3.0 %collective-permute-start.26 = (bf16[2,2,16,1024]{3,2,1,0:T(8,128)(2,1)S(1)}, bf16[2,2,16,1024]{3,2,1,0:T(8,128)(2,1)S(1)}, u32[]{:S(2)}, u32[]{:S(2)}) collective-permute-start(bf16[2,2,16,1024]{3,2,1,0:T(8,128)(2,1)S(1)} %get-tuple-element.85), channel_id=1, source_target_pairs={{0,12},{4,8},{8,4},{12,0},{1,13},{5,9},{9,5},{13,1},{2,14},{6,10},... | collective-permute-start | bytes 393224 | tf_op jit(solution)/shard_map/ppermute | solution.py:476
  113.5 6.0 %collective-permute-done.25.rest_9_ = bf16[2,2,16,1024]{3,2,1,0:T(8,128)(2,1)S(1)} collective-permute-done((bf16[2,2,16,1024]{3,2,1,0:T(8,128)(2,1)S(1)}, bf16[2,2,16,1024]{3,2,1,0:T(8,128)(2,1)S(1)}, u32[]{:S(2)}, u32[]{:S(2)}) %collective-permute-start.25) | collective-permute-done | bytes 131104 | tf_op jit(solution)/shard_map/ppermute | solution.py:476
  121.1 1.5 %collective-permute-start.28 = (bf16[2,2,64,256]{3,2,1,0:T(8,128)(2,1)S(1)}, bf16[2,2,64,256]{3,2,1,0:T(8,128)(2,1)S(1)}, u32[]{:S(2)}, u32[]{:S(2)}) collective-permute-start(bf16[2,2,64,256]{3,2,1,0:T(8,128)(2,1)S(1)} %get-tuple-element.88), channel_id=1, source_target_pairs={{0,2},{2,0},{1,3},{3,1},{4,6},{6,4},{5,7},{7,5},{8,10},{10,8},{9,1... | collective-permute-start | bytes 393224 | tf_op jit(solution)/shard_map/ppermute | solution.py:476
  122.6 3.5 %collective-permute-done.28.r_ref = bf16[2,2,64,256]{3,2,1,0:T(8,128)(2,1)S(1)} collective-permute-done((bf16[2,2,64,256]{3,2,1,0:T(8,128)(2,1)S(1)}, bf16[2,2,64,256]{3,2,1,0:T(8,128)(2,1)S(1)}, u32[]{:S(2)}, u32[]{:S(2)}) %collective-permute-start.28) | collective-permute-done | bytes 131104 | tf_op jit(solution)/shard_map/ppermute | solution.py:476
  126.2 2.1 %collective-permute-start.29 = (bf16[2,2,64,256]{3,2,1,0:T(8,128)(2,1)S(1)}, bf16[2,2,64,256]{3,2,1,0:T(8,128)(2,1)S(1)}, u32[]{:S(2)}, u32[]{:S(2)}) collective-permute-start(bf16[2,2,64,256]{3,2,1,0:T(8,128)(2,1)S(1)} %shard_map.96.rest_0_), channel_id=1, source_target_pairs={{0,8},{4,12},{8,0},{12,4},{1,9},{5,13},{9,1},{13,5},{2,10},{6,14},... | collective-permute-start | bytes 393224 | tf_op jit(solution)/shard_map/ppermute | solution.py:476
  129.7 6.3 %collective-permute-done.29.rest_1_ = bf16[2,2,64,256]{3,2,1,0:T(8,128)(2,1)S(1)} collective-permute-done((bf16[2,2,64,256]{3,2,1,0:T(8,128)(2,1)S(1)}, bf16[2,2,64,256]{3,2,1,0:T(8,128)(2,1)S(1)}, u32[]{:S(2)}, u32[]{:S(2)}) %collective-permute-start.29) | collective-permute-done | bytes 131104 | tf_op jit(solution)/shard_map/ppermute | solution.py:476
  136.8 2.2 %copy-done.1 = bf16[64,128,256]{2,1,0:T(8,128)(2,1)S(1)} copy-done((bf16[64,128,256]{2,1,0:T(8,128)(2,1)S(1)}, bf16[64,128,256]{2,1,0:T(8,128)(2,1)}, u32[]{:S(2)}) %copy-start.1) | copy-done | bytes 4194328
  139.0 3.4 %shard_map.97 = bf16[64,128,256]{2,1,0:T(8,128)(2,1)} custom-call(s32[1]{0:T(128)} %bitcast.place_ref.freq, s32[1]{0:T(128)} %bitcast.1.focal_ref, bf16[64,128,256]{2,1,0:T(8,128)(2,1)S(1)} %copy-done.1, s32[128,256]{1,0:T(8,128)S(1)} %copy-done.10, bf16[4,128,128]{2,1,0:T(8,128)(2,1)S(1)} %copy-done.14, bf16[2,2,64,256]{3,2,1,0:T(8,128)(2,1)S(1)} %shard_map.96.rest_0_, ...), custom_call_target="tpu_custom_call" | custom-call | flops 67108864 | bytes 9175040 | tf_op jit(solution)/shard_map/pallas_call | solution.py:87
  (81 shorter events, 28.6 us)
Async XLA Ops:
  3.5 29.1 %collective-permute-start.6 = (bf16[512,512]{1,0:T(8,128)(2,1)}, bf16[512,512]{1,0:T(8,128)(2,1)S(1)}, u32[]{:S(2)}, u32[]{:S(2)}) collective-permute-start(bf16[512,512]{1,0:T(8,128)(2,1)} %get-tuple-element.56), channel_id=1, source_target_pairs={{0,2},{2,0},{1,3},{3,1},{4,6},{6,4},{5,7},{7,5},{8,10},{10,8},{9,1... | collective-permute-start | bytes 1572872 | tf_op jit(solution)/shard_map/ppermute | solution.py:476
  6.5 26.2 %collective-permute-start = (bf16[512,512]{1,0:T(8,128)(2,1)}, bf16[512,512]{1,0:T(8,128)(2,1)S(1)}, u32[]{:S(2)}, u32[]{:S(2)}) collective-permute-start(bf16[512,512]{1,0:T(8,128)(2,1)} %get-tuple-element.48), channel_id=1, source_target_pairs={{0,2},{2,0},{1,3},{3,1},{4,6},{6,4},{5,7},{7,5},{8,10},{10,8},{9,1... | collective-permute-start | bytes 1572872 | tf_op jit(solution)/shard_map/ppermute | solution.py:476
  10.3 12.9 %collective-permute-start.1 = (bf16[2,2,64,256]{3,2,1,0:T(8,128)(2,1)S(1)}, bf16[2,2,64,256]{3,2,1,0:T(8,128)(2,1)S(1)}, u32[]{:S(2)}, u32[]{:S(2)}) collective-permute-start(bf16[2,2,64,256]{3,2,1,0:T(8,128)(2,1)S(1)} %get-tuple-element.50), channel_id=1, source_target_pairs={{0,8},{4,12},{8,0},{12,4},{1,9},{5,13},{9,1},{13,5},{2,10},{6,14},... | collective-permute-start | bytes 393224 | tf_op jit(solution)/shard_map/ppermute | solution.py:476
  13.5 9.8 %collective-permute-start.2 = (bf16[2,2,64,256]{3,2,1,0:T(8,128)(2,1)S(1)}, bf16[2,2,64,256]{3,2,1,0:T(8,128)(2,1)S(1)}, u32[]{:S(2)}, u32[]{:S(2)}) collective-permute-start(bf16[2,2,64,256]{3,2,1,0:T(8,128)(2,1)S(1)} %get-tuple-element.51), channel_id=1, source_target_pairs={{0,12},{4,8},{8,4},{12,0},{1,13},{5,9},{9,5},{13,1},{2,14},{6,10},... | collective-permute-start | bytes 393224 | tf_op jit(solution)/shard_map/ppermute | solution.py:476
  14.8 8.6 %collective-permute-start.3 = (bf16[2,2,64,256]{3,2,1,0:T(8,128)(2,1)S(1)}, bf16[2,2,64,256]{3,2,1,0:T(8,128)(2,1)S(1)}, u32[]{:S(2)}, u32[]{:S(2)}) collective-permute-start(bf16[2,2,64,256]{3,2,1,0:T(8,128)(2,1)S(1)} %get-tuple-element.52), channel_id=1, source_target_pairs={{0,4},{4,0},{8,12},{12,8},{1,5},{5,1},{9,13},{13,9},{2,6},{6,2},{1... | collective-permute-start | bytes 393224 | tf_op jit(solution)/shard_map/ppermute | solution.py:476
  24.2 8.4 %collective-permute-start.7 = (bf16[2,2,64,256]{3,2,1,0:T(8,128)(2,1)S(1)}, bf16[2,2,64,256]{3,2,1,0:T(8,128)(2,1)S(1)}, u32[]{:S(2)}, u32[]{:S(2)}) collective-permute-start(bf16[2,2,64,256]{3,2,1,0:T(8,128)(2,1)S(1)} %get-tuple-element.67.n_ref), channel_id=1, source_target_pairs={{0,2},{2,0},{1,3},{3,1},{4,6},{6,4},{5,7},{7,5},{8,10},{10,8},{9,1... | collective-permute-start | bytes 393224 | tf_op jit(solution)/shard_map/ppermute | solution.py:476
  25.7 7.4 %collective-permute-start.4 = (bf16[512,512]{1,0:T(8,128)(2,1)S(1)}, bf16[512,512]{1,0:T(8,128)(2,1)S(1)}, u32[]{:S(2)}, u32[]{:S(2)}) collective-permute-start(bf16[512,512]{1,0:T(8,128)(2,1)S(1)} %get-tuple-element.47.rest_0_), channel_id=1, source_target_pairs={{0,1},{1,0},{2,3},{3,2},{4,5},{5,4},{6,7},{7,6},{8,9},{9,8},{10,11... | collective-permute-start | bytes 1572872 | tf_op jit(solution)/shard_map/ppermute | solution.py:476
  25.7 7.4 %collective-permute-start.8 = (bf16[512,512]{1,0:T(8,128)(2,1)S(1)}, bf16[512,512]{1,0:T(8,128)(2,1)S(1)}, u32[]{:S(2)}, u32[]{:S(2)}) collective-permute-start(bf16[512,512]{1,0:T(8,128)(2,1)S(1)} %get-tuple-element.55.rest_4_), channel_id=1, source_target_pairs={{0,1},{1,0},{2,3},{3,2},{4,5},{5,4},{6,7},{7,6},{8,9},{9,8},{10,11... | collective-permute-start | bytes 1572872 | tf_op jit(solution)/shard_map/ppermute | solution.py:476
  32.6 1.9 %collective-permute-start.9 = (bf16[512,512]{1,0:T(8,128)(2,1)S(1)}, bf16[512,512]{1,0:T(8,128)(2,1)S(1)}, u32[]{:S(2)}, u32[]{:S(2)}) collective-permute-start(bf16[512,512]{1,0:T(8,128)(2,1)S(1)} %collective-permute-done.6.rest_5_), channel_id=1, source_target_pairs={{0,1},{1,0},{2,3},{3,2},{4,5},{5,4},{6,7},{7,6},{8,9},{9,8},{10,11... | collective-permute-start | bytes 1572872 | tf_op jit(solution)/shard_map/ppermute | solution.py:476
  32.6 2.7 %collective-permute-start.5 = (bf16[512,512]{1,0:T(8,128)(2,1)S(1)}, bf16[512,512]{1,0:T(8,128)(2,1)S(1)}, u32[]{:S(2)}, u32[]{:S(2)}) collective-permute-start(bf16[512,512]{1,0:T(8,128)(2,1)S(1)} %collective-permute-done.rest_1_), channel_id=1, source_target_pairs={{0,1},{1,0},{2,3},{3,2},{4,5},{5,4},{6,7},{7,6},{8,9},{9,8},{10,11... | collective-permute-start | bytes 1572872 | tf_op jit(solution)/shard_map/ppermute | solution.py:476
  38.3 13.2 %collective-permute-start.11 = (bf16[2,2,16,1024]{3,2,1,0:T(8,128)(2,1)}, bf16[2,2,16,1024]{3,2,1,0:T(8,128)(2,1)}, u32[]{:S(2)}, u32[]{:S(2)}) collective-permute-start(bf16[2,2,16,1024]{3,2,1,0:T(8,128)(2,1)} %get-tuple-element.70), channel_id=1, source_target_pairs={{0,8},{4,12},{8,0},{12,4},{1,9},{5,13},{9,1},{13,5},{2,10},{6,14},... | collective-permute-start | bytes 393224 | tf_op jit(solution)/shard_map/ppermute | solution.py:476
  41.2 10.4 %collective-permute-start.12 = (bf16[2,2,16,1024]{3,2,1,0:T(8,128)(2,1)}, bf16[2,2,16,1024]{3,2,1,0:T(8,128)(2,1)}, u32[]{:S(2)}, u32[]{:S(2)}) collective-permute-start(bf16[2,2,16,1024]{3,2,1,0:T(8,128)(2,1)} %get-tuple-element.71), channel_id=1, source_target_pairs={{0,12},{4,8},{8,4},{12,0},{1,13},{5,9},{9,5},{13,1},{2,14},{6,10},... | collective-permute-start | bytes 393224 | tf_op jit(solution)/shard_map/ppermute | solution.py:476
  42.5 9.7 %collective-permute-start.13 = (bf16[2,2,16,1024]{3,2,1,0:T(8,128)(2,1)}, bf16[2,2,16,1024]{3,2,1,0:T(8,128)(2,1)}, u32[]{:S(2)}, u32[]{:S(2)}) collective-permute-start(bf16[2,2,16,1024]{3,2,1,0:T(8,128)(2,1)} %get-tuple-element.72), channel_id=1, source_target_pairs={{0,4},{4,0},{8,12},{12,8},{1,5},{5,1},{9,13},{13,9},{2,6},{6,2},{1... | collective-permute-start | bytes 393224 | tf_op jit(solution)/shard_map/ppermute | solution.py:476
  43.8 1.3 collective-permute-start.10
  54.4 13.8 %collective-permute-start.14 = (bf16[2,2,16,1024]{3,2,1,0:T(8,128)(2,1)S(1)}, bf16[2,2,16,1024]{3,2,1,0:T(8,128)(2,1)S(1)}, u32[]{:S(2)}, u32[]{:S(2)}) collective-permute-start(bf16[2,2,16,1024]{3,2,1,0:T(8,128)(2,1)S(1)} %get-tuple-element.74), channel_id=1, source_target_pairs={{0,8},{4,12},{8,0},{12,4},{1,9},{5,13},{9,1},{13,5},{2,10},{6,14},... | collective-permute-start | bytes 393224 | tf_op jit(solution)/shard_map/ppermute | solution.py:476
  58.6 9.6 %collective-permute-start.15 = (bf16[2,2,16,1024]{3,2,1,0:T(8,128)(2,1)S(1)}, bf16[2,2,16,1024]{3,2,1,0:T(8,128)(2,1)S(1)}, u32[]{:S(2)}, u32[]{:S(2)}) collective-permute-start(bf16[2,2,16,1024]{3,2,1,0:T(8,128)(2,1)S(1)} %get-tuple-element.75), channel_id=1, source_target_pairs={{0,12},{4,8},{8,4},{12,0},{1,13},{5,9},{9,5},{13,1},{2,14},{6,10},... | collective-permute-start | bytes 393224 | tf_op jit(solution)/shard_map/ppermute | solution.py:476
  59.1 10.3 %collective-permute-start.16 = (bf16[2,2,16,1024]{3,2,1,0:T(8,128)(2,1)S(1)}, bf16[2,2,16,1024]{3,2,1,0:T(8,128)(2,1)S(1)}, u32[]{:S(2)}, u32[]{:S(2)}) collective-permute-start(bf16[2,2,16,1024]{3,2,1,0:T(8,128)(2,1)S(1)} %get-tuple-element.76), channel_id=1, source_target_pairs={{0,4},{4,0},{8,12},{12,8},{1,5},{5,1},{9,13},{13,9},{2,6},{6,2},{1... | collective-permute-start | bytes 393224 | tf_op jit(solution)/shard_map/ppermute | solution.py:476
  72.2 5.0 %collective-permute-start.17 = (bf16[2,2,64,256]{3,2,1,0:T(8,128)(2,1)S(1)}, bf16[2,2,64,256]{3,2,1,0:T(8,128)(2,1)S(1)}, u32[]{:S(2)}, u32[]{:S(2)}) collective-permute-start(bf16[2,2,64,256]{3,2,1,0:T(8,128)(2,1)S(1)} %get-tuple-element.78), channel_id=1, source_target_pairs={{0,2},{2,0},{1,3},{3,1},{4,6},{6,4},{5,7},{7,5},{8,10},{10,8},{9,1... | collective-permute-start | bytes 393224 | tf_op jit(solution)/shard_map/ppermute | solution.py:476
  77.2 12.0 %collective-permute-start.18 = (bf16[2,2,64,256]{3,2,1,0:T(8,128)(2,1)S(1)}, bf16[2,2,64,256]{3,2,1,0:T(8,128)(2,1)S(1)}, u32[]{:S(2)}, u32[]{:S(2)}) collective-permute-start(bf16[2,2,64,256]{3,2,1,0:T(8,128)(2,1)S(1)} %shard_map.91.rest_0_), channel_id=1, source_target_pairs={{0,8},{4,12},{8,0},{12,4},{1,9},{5,13},{9,1},{13,5},{2,10},{6,14},... | collective-permute-start | bytes 393224 | tf_op jit(solution)/shard_map/ppermute | solution.py:476
  79.2 10.0 %collective-permute-start.19 = (bf16[2,2,64,256]{3,2,1,0:T(8,128)(2,1)S(1)}, bf16[2,2,64,256]{3,2,1,0:T(8,128)(2,1)S(1)}, u32[]{:S(2)}, u32[]{:S(2)}) collective-permute-start(bf16[2,2,64,256]{3,2,1,0:T(8,128)(2,1)S(1)} %shard_map.91.rest_0_), channel_id=1, source_target_pairs={{0,12},{4,8},{8,4},{12,0},{1,13},{5,9},{9,5},{13,1},{2,14},{6,10},... | collective-permute-start | bytes 393224 | tf_op jit(solution)/shard_map/ppermute | solution.py:476
  82.0 8.1 %collective-permute-start.20 = (bf16[2,2,64,256]{3,2,1,0:T(8,128)(2,1)S(1)}, bf16[2,2,64,256]{3,2,1,0:T(8,128)(2,1)S(1)}, u32[]{:S(2)}, u32[]{:S(2)}) collective-permute-start(bf16[2,2,64,256]{3,2,1,0:T(8,128)(2,1)S(1)} %shard_map.91.rest_0_), channel_id=1, source_target_pairs={{0,4},{4,0},{8,12},{12,8},{1,5},{5,1},{9,13},{13,9},{2,6},{6,2},{1... | collective-permute-start | bytes 393224 | tf_op jit(solution)/shard_map/ppermute | solution.py:476
  90.4 5.0 %collective-permute-start.21 = (bf16[2,2,64,256]{3,2,1,0:T(8,128)(2,1)S(1)}, bf16[2,2,64,256]{3,2,1,0:T(8,128)(2,1)S(1)}, u32[]{:S(2)}, u32[]{:S(2)}) collective-permute-start(bf16[2,2,64,256]{3,2,1,0:T(8,128)(2,1)S(1)} %shard_map.92.n_ref), channel_id=1, source_target_pairs={{0,2},{2,0},{1,3},{3,1},{4,6},{6,4},{5,7},{7,5},{8,10},{10,8},{9,1... | collective-permute-start | bytes 393224 | tf_op jit(solution)/shard_map/ppermute | solution.py:476
  97.0 10.7 %collective-permute-start.22 = (bf16[2,2,16,1024]{3,2,1,0:T(8,128)(2,1)S(1)}, bf16[2,2,16,1024]{3,2,1,0:T(8,128)(2,1)S(1)}, u32[]{:S(2)}, u32[]{:S(2)}) collective-permute-start(bf16[2,2,16,1024]{3,2,1,0:T(8,128)(2,1)S(1)} %get-tuple-element.80), channel_id=1, source_target_pairs={{0,8},{4,12},{8,0},{12,4},{1,9},{5,13},{9,1},{13,5},{2,10},{6,14},... | collective-permute-start | bytes 393224 | tf_op jit(solution)/shard_map/ppermute | solution.py:476
  98.8 8.9 %collective-permute-start.23 = (bf16[2,2,16,1024]{3,2,1,0:T(8,128)(2,1)S(1)}, bf16[2,2,16,1024]{3,2,1,0:T(8,128)(2,1)S(1)}, u32[]{:S(2)}, u32[]{:S(2)}) collective-permute-start(bf16[2,2,16,1024]{3,2,1,0:T(8,128)(2,1)S(1)} %get-tuple-element.81), channel_id=1, source_target_pairs={{0,12},{4,8},{8,4},{12,0},{1,13},{5,9},{9,5},{13,1},{2,14},{6,10},... | collective-permute-start | bytes 393224 | tf_op jit(solution)/shard_map/ppermute | solution.py:476
  100.5 7.5 %collective-permute-start.24 = (bf16[2,2,16,1024]{3,2,1,0:T(8,128)(2,1)S(1)}, bf16[2,2,16,1024]{3,2,1,0:T(8,128)(2,1)S(1)}, u32[]{:S(2)}, u32[]{:S(2)}) collective-permute-start(bf16[2,2,16,1024]{3,2,1,0:T(8,128)(2,1)S(1)} %get-tuple-element.82), channel_id=1, source_target_pairs={{0,4},{4,0},{8,12},{12,8},{1,5},{5,1},{9,13},{13,9},{2,6},{6,2},{1... | collective-permute-start | bytes 393224 | tf_op jit(solution)/shard_map/ppermute | solution.py:476
  109.1 10.4 %collective-permute-start.25 = (bf16[2,2,16,1024]{3,2,1,0:T(8,128)(2,1)S(1)}, bf16[2,2,16,1024]{3,2,1,0:T(8,128)(2,1)S(1)}, u32[]{:S(2)}, u32[]{:S(2)}) collective-permute-start(bf16[2,2,16,1024]{3,2,1,0:T(8,128)(2,1)S(1)} %get-tuple-element.84), channel_id=1, source_target_pairs={{0,8},{4,12},{8,0},{12,4},{1,9},{5,13},{9,1},{13,5},{2,10},{6,14},... | collective-permute-start | bytes 393224 | tf_op jit(solution)/shard_map/ppermute | solution.py:476
  110.5 9.0 %collective-permute-start.26 = (bf16[2,2,16,1024]{3,2,1,0:T(8,128)(2,1)S(1)}, bf16[2,2,16,1024]{3,2,1,0:T(8,128)(2,1)S(1)}, u32[]{:S(2)}, u32[]{:S(2)}) collective-permute-start(bf16[2,2,16,1024]{3,2,1,0:T(8,128)(2,1)S(1)} %get-tuple-element.85), channel_id=1, source_target_pairs={{0,12},{4,8},{8,4},{12,0},{1,13},{5,9},{9,5},{13,1},{2,14},{6,10},... | collective-permute-start | bytes 393224 | tf_op jit(solution)/shard_map/ppermute | solution.py:476
  113.5 6.9 %collective-permute-start.27 = (bf16[2,2,16,1024]{3,2,1,0:T(8,128)(2,1)S(1)}, bf16[2,2,16,1024]{3,2,1,0:T(8,128)(2,1)S(1)}, u32[]{:S(2)}, u32[]{:S(2)}) collective-permute-start(bf16[2,2,16,1024]{3,2,1,0:T(8,128)(2,1)S(1)} %get-tuple-element.86), channel_id=1, source_target_pairs={{0,4},{4,0},{8,12},{12,8},{1,5},{5,1},{9,13},{13,9},{2,6},{6,2},{1... | collective-permute-start | bytes 393224 | tf_op jit(solution)/shard_map/ppermute | solution.py:476
  121.1 5.0 %collective-permute-start.28 = (bf16[2,2,64,256]{3,2,1,0:T(8,128)(2,1)S(1)}, bf16[2,2,64,256]{3,2,1,0:T(8,128)(2,1)S(1)}, u32[]{:S(2)}, u32[]{:S(2)}) collective-permute-start(bf16[2,2,64,256]{3,2,1,0:T(8,128)(2,1)S(1)} %get-tuple-element.88), channel_id=1, source_target_pairs={{0,2},{2,0},{1,3},{3,1},{4,6},{6,4},{5,7},{7,5},{8,10},{10,8},{9,1... | collective-permute-start | bytes 393224 | tf_op jit(solution)/shard_map/ppermute | solution.py:476
  126.2 9.9 %collective-permute-start.29 = (bf16[2,2,64,256]{3,2,1,0:T(8,128)(2,1)S(1)}, bf16[2,2,64,256]{3,2,1,0:T(8,128)(2,1)S(1)}, u32[]{:S(2)}, u32[]{:S(2)}) collective-permute-start(bf16[2,2,64,256]{3,2,1,0:T(8,128)(2,1)S(1)} %shard_map.96.rest_0_), channel_id=1, source_target_pairs={{0,8},{4,12},{8,0},{12,4},{1,9},{5,13},{9,1},{13,5},{2,10},{6,14},... | collective-permute-start | bytes 393224 | tf_op jit(solution)/shard_map/ppermute | solution.py:476
  128.3 7.8 %collective-permute-start.30 = (bf16[2,2,64,256]{3,2,1,0:T(8,128)(2,1)S(1)}, bf16[2,2,64,256]{3,2,1,0:T(8,128)(2,1)S(1)}, u32[]{:S(2)}, u32[]{:S(2)}) collective-permute-start(bf16[2,2,64,256]{3,2,1,0:T(8,128)(2,1)S(1)} %shard_map.96.rest_0_), channel_id=1, source_target_pairs={{0,12},{4,8},{8,4},{12,0},{1,13},{5,9},{9,5},{13,1},{2,14},{6,10},... | collective-permute-start | bytes 393224 | tf_op jit(solution)/shard_map/ppermute | solution.py:476
  129.6 7.2 %collective-permute-start.31 = (bf16[2,2,64,256]{3,2,1,0:T(8,128)(2,1)S(1)}, bf16[2,2,64,256]{3,2,1,0:T(8,128)(2,1)S(1)}, u32[]{:S(2)}, u32[]{:S(2)}) collective-permute-start(bf16[2,2,64,256]{3,2,1,0:T(8,128)(2,1)S(1)} %shard_map.96.rest_0_), channel_id=1, source_target_pairs={{0,4},{4,0},{8,12},{12,8},{1,5},{5,1},{9,13},{13,9},{2,6},{6,2},{1... | collective-permute-start | bytes 393224 | tf_op jit(solution)/shard_map/ppermute | solution.py:476
  (16 other events, 272.5 us)

commit v9 on v8

--- a/solution.py
+++ b/solution.py
@@ -184,27 +184,15 @@
     return out
 
 
-def src_onsets(onset, places, half_rows, first, share, width):
-    def body(freq, rblk, sblk, o_ref, own, other):
-        lanes = pl.ds(pl.multiple_of(rblk[0] * width, BLOCK), width)
-        for core, out in ((sblk[0], own), (1 - sblk[0], other)):
-            spot = pl.multiple_of(core * half_rows + first + freq[0] * share, ROWS)
-            out[...] = o_ref[pl.ds(spot, share), lanes]
-
-    shape = jax.ShapeDtypeStruct((share, width), onset.dtype)
-    return call(body, places, [(onset, whole(onset))], [(shape, whole(shape))] * 2, (1,))
-
-
 def sine_terms():
     square = (np.cos(np.linspace(0.0, math.pi, 200)) + 1.0) / 32.0
     y = np.sqrt(np.maximum(square, 1e-12))
     return [float(v) for v in np.polynomial.polynomial.polyfit(square, np.sin(2.0 * math.pi * y) / y, 6)]
 
 
-def phase_tables(onsets, places, freq_devs, per_dev, samples, rows=None, first=0, half_rows=0):
+def phase_tables(groups, samples):
     terms = sine_terms()
-    count = rows or onsets[0].shape[0]
-    widths = [v.shape[1] for v in onsets]
+    flat = [v for group in groups for v in group]
 
     def sine(y):
         square = y * y
@@ -213,31 +201,29 @@
             total = total * square + term
         return total * y
 
-    def body(freq, _, sblk, *refs):
-        cosines, sines, fraction = refs[-3:]
-        at = 0
-        for ref, width in zip(refs, widths):
-            if rows:
-                value = ref[pl.ds(pl.multiple_of(sblk[0] * half_rows + first, ROWS), rows), :]
-            else:
-                value = ref[...]
-            part = value.astype(F32) * (1.0 / samples)
-            to = slice(at, at + width)
-            fraction[:, to] = part
-            for step, way in enumerate(ways(freq_devs)):
-                for j in range(per_dev):
-                    order = ((freq[0] ^ way) * per_dev + j + 1).astype(F32)
-                    turn = part * order
-                    turn = turn - jnp.floor(turn + 0.5)
-                    size = jnp.abs(turn)
-                    folded = jnp.where(size > 0.25, jnp.where(turn > 0.0, 0.5, -0.5) - turn, turn)
-                    cosines[step, j, :, to] = sine(0.25 - size)
-                    sines[step, j, :, to] = sine(folded)
-            at += width
-
-    table = jax.ShapeDtypeStruct((freq_devs, per_dev, count, sum(widths)), F32)
-    shapes = [table, table, jax.ShapeDtypeStruct((count, sum(widths)), F32)]
-    return call(body, places, [(v, whole(v)) for v in onsets], [(v, whole(v)) for v in shapes], (1,))
+    def body(*refs):
+        refs, outs = list(refs[: len(flat)]), list(refs[len(flat) :])
+        for group in groups:
+            cosine, sines, fraction = outs[:3]
+            del outs[:3]
+            at = 0
+            for _ in group:
+                ref = refs.pop(0)
+                to = slice(at, at + ref.shape[1])
+                at = to.stop
+                part = ref[...].astype(F32) * (1.0 / samples)
+                turn = part - jnp.floor(part + 0.5)
+                size = jnp.abs(turn)
+                folded = jnp.where(size > 0.25, jnp.where(turn > 0.0, 0.5, -0.5) - turn, turn)
+                cosine[:, to] = sine(0.25 - size)
+                sines[:, to] = sine(folded)
+                fraction[:, to] = part
+
+    shapes = []
+    for group in groups:
+        shapes += [jax.ShapeDtypeStruct((group[0].shape[0], sum(v.shape[1] for v in group)), F32)] * 3
+    outs = call(body, (), [(v, whole(v)) for v in flat], [(v, whole(v)) for v in shapes], (1,))
+    return [tuple(outs[at : at + 3]) for at in range(0, len(outs), 3)]
 
 
 def down_products(near, far, responses, freq_place, freq_devs):
@@ -281,6 +267,24 @@
     )
 
 
+def turn_powers(cosine, sine, place, freq_devs, per_dev):
+    powers = [(cosine, sine)]
+    for _ in range(1, freq_devs * per_dev):
+        real, imag = powers[-1]
+        powers.append((real * cosine - imag * sine, real * sine + imag * cosine))
+    stacked = [jnp.stack([v[part] for v in powers]) for part in range(2)]
+    out = []
+    for value in stacked:
+        groups = [value[g * per_dev : (g + 1) * per_dev] for g in range(freq_devs)]
+        bit = 1
+        while bit < freq_devs:
+            on = jnp.broadcast_to(place & bit, groups[0].shape) != 0
+            groups = [jnp.where(on, groups[g ^ bit], groups[g]) for g in range(freq_devs)]
+            bit *= 2
+        out.append([groups[way] for way in ways(freq_devs)])
+    return out
+
+
 def mixed_fields(plain, cos, sin, matrix):
     tile = plain[0].shape[-1]
     turned = [
@@ -322,8 +326,7 @@
             for first in range(0, share, ROWS):
                 cut = slice(first, first + ROWS)
                 plain = [value[:, :, cut] for value in data]
-                cos = [c_ref[step, :, cut, at] for step in range(freq_devs)]
-                sin = [s_ref[step, :, cut, at] for step in range(freq_devs)]
+                cos, sin = turn_powers(c_ref[cut, at], s_ref[cut, at], place_ref[0], freq_devs, per_dev)
                 up, low = mixed_fields(plain, cos, sin, matrix_here)
                 part = f_ref[cut, at]
                 for step in range(freq_devs):
@@ -401,8 +404,7 @@
                 for half in range(2):
                     plain = [value[:, :, half * ROWS : (half + 1) * ROWS] for value in data]
                     cut = slice(base + half * ROWS, base + (half + 1) * ROWS)
-                    cos = [c_ref[step, :, cut, at] for step in range(freq_devs)]
-                    sin = [s_ref[step, :, cut, at] for step in range(freq_devs)]
+                    cos, sin = turn_powers(c_ref[cut, at], s_ref[cut, at], place_ref[0], freq_devs, per_dev)
                     up, low = mixed_fields(plain, cos, sin, matrix_here)
                     made.append(unturned(up[0], low[0], plain[0], cos[0], sin[0], f_ref[cut, at]))
                 out[:, :, pair, at] = (u_ref[:, :, pair, at] - jnp.concatenate(made, 2)).astype(BF16)
@@ -521,9 +523,13 @@
                 before = far
             responses = [((kept[j], moved[j]), (kept_pair[j], moved_pair[j])) for j in range(per_dev)]
 
-        own, other = src_onsets(onset_src, places, half_rows, first, share, src_width)
-        src_tables = phase_tables((own, exchanged(other, "sblk", 1)), places, freq_devs, per_dev, samples)
-        rcv_tables = phase_tables((onset_rcv,), places, freq_devs, per_dev, samples, rows, first, half_rows)
+        def src_onsets(core):
+            spot = core * half_rows + first + freq_index * share
+            return lax.dynamic_slice(onset_src, (spot, rblk_index * src_width), (share, src_width))
+
+        onsets = (src_onsets(sblk_index), exchanged(src_onsets(1 - sblk_index), "sblk", 1))
+        rcv_onsets = lax.dynamic_slice_in_dim(onset_rcv, sblk_index * half_rows + first, rows, 0)
+        src_tables, rcv_tables = phase_tables((onsets, (rcv_onsets,)), samples)
 
         for step in range(ITERS):
             far = far if step == 0 else exchanged(spectra, "rblk", 1)

time: 143 us -> 150 us (1.049)
  Pallas kernels: 15.5 us -> 20 us
  waiting for transfers between devices: 74 us -> 78.3 us
    pallas_call x16 -> x14, Pallas kernels: 15.5 us -> 20 us  [call(): pl.pallas_call(body, grid_spec=pltpu.PrefetchScalarGridSpec(num_scalar_pr...]
    ppermute x32, waiting for transfers between devices: 74 us -> 78.3 us  [exchanged(): lax.ppermute(value, axis, [(i, i ^ step) for i in range(lax.axis_size(axi...]
    unnamed x33 -> x29, local copies, waits for them, and re-layouts: 12.3 us -> 10.1 us
  transfers between devices with their start and end apart: 32 -> 32, of which waited for: 21 -> 22; matrix products, arithmetic and copies ran while one was open for 0% -> 1% of each run, Pallas kernels for 2% -> 1%
where the time goes in v9:
time: 150 us; the launch traced here: 149 us
  waiting for transfers between devices  78.3 us (52%)
  starting transfers between devices  39.3 us (26%)
  Pallas kernels  20 us (13%)
  local copies, waits for them, and re-layouts  11.5 us (8%)
    ppermute x32, waiting for transfers between devices, exchanged(): lax.ppermute(value, axis, [(i, i ^ step) for i in range(lax.axis_size(axi...  78.3 us
    ppermute x32, starting transfers between devices, exchanged(): lax.ppermute(value, axis, [(i, i ^ step) for i in range(lax.axis_size(axi...  39.3 us
    pallas_call x14, Pallas kernels, call(): pl.pallas_call(body, grid_spec=pltpu.PrefetchScalarGridSpec(num_scalar_pr...  20 us
    unnamed x29, local copies, waits for them, and re-layouts  10.1 us
  transfers between devices with their start and end apart: 32, of which 22 were waited for; matrix products, arithmetic and copies ran while one was open for 1% of the time, Pallas kernels for 1%

profile of v9, /device:TPU:0, one launch (start us, length us, event | category | flops | bytes accessed | tf_op | source)
XLA Modules:
  0.0 149.2 jit_solution(16062172430962251186)
XLA Ops:
  3.5 2.9 %collective-permute-start = (bf16[512,512]{1,0:T(8,128)(2,1)}, bf16[512,512]{1,0:T(8,128)(2,1)S(1)}, u32[]{:S(2)}, u32[]{:S(2)}) collective-permute-start(bf16[512,512]{1,0:T(8,128)(2,1)} %get-tuple-element.46), channel_id=1, source_target_pairs={{0,2},{2,0},{1,3},{3,1},{4,6},{6,4},{5,7},{7,5},{8,10},{10,8},{9,1... | collective-permute-start | bytes 1572872 | tf_op jit(solution)/shard_map/ppermute | solution.py:478
  6.5 2.2 %copy-done = bf16[64,128,256]{2,1,0:T(8,128)(2,1)S(1)} copy-done((bf16[64,128,256]{2,1,0:T(8,128)(2,1)S(1)}, bf16[64,128,256]{2,1,0:T(8,128)(2,1)}, u32[]{:S(2)}) %copy-start) | copy-done | bytes 4194328
  10.3 3.2 %collective-permute-start.1 = (bf16[2,2,64,256]{3,2,1,0:T(8,128)(2,1)S(1)}, bf16[2,2,64,256]{3,2,1,0:T(8,128)(2,1)S(1)}, u32[]{:S(2)}, u32[]{:S(2)}) collective-permute-start(bf16[2,2,64,256]{3,2,1,0:T(8,128)(2,1)S(1)} %get-tuple-element.48), channel_id=1, source_target_pairs={{0,8},{4,12},{8,0},{12,4},{1,9},{5,13},{9,1},{13,5},{2,10},{6,14},... | collective-permute-start | bytes 393224 | tf_op jit(solution)/shard_map/ppermute | solution.py:478
  15.1 8.2 %collective-permute-done.1.refs_1_ = bf16[2,2,64,256]{3,2,1,0:T(8,128)(2,1)S(1)} collective-permute-done((bf16[2,2,64,256]{3,2,1,0:T(8,128)(2,1)S(1)}, bf16[2,2,64,256]{3,2,1,0:T(8,128)(2,1)S(1)}, u32[]{:S(2)}, u32[]{:S(2)}) %collective-permute-start.1) | collective-permute-done | bytes 131104 | tf_op jit(solution)/shard_map/ppermute | solution.py:478
  26.3 6.4 %collective-permute-done.7.f_ref = bf16[2,2,64,256]{3,2,1,0:T(8,128)(2,1)S(1)} collective-permute-done((bf16[2,2,64,256]{3,2,1,0:T(8,128)(2,1)S(1)}, bf16[2,2,64,256]{3,2,1,0:T(8,128)(2,1)S(1)}, u32[]{:S(2)}, u32[]{:S(2)}) %collective-permute-start.7) | collective-permute-done | bytes 131104 | tf_op jit(solution)/shard_map/ppermute | solution.py:478
  33.3 2.0 %collective-permute-done.9.rest_7_ = bf16[512,512]{1,0:T(8,128)(2,1)} collective-permute-done((bf16[512,512]{1,0:T(8,128)(2,1)S(1)}, bf16[512,512]{1,0:T(8,128)(2,1)}, u32[]{:S(2)}, u32[]{:S(2)}) %collective-permute-start.9) | collective-permute-done | bytes 524320 | tf_op jit(solution)/shard_map/ppermute | solution.py:478
  36.2 3.4 %shard_map.86 = (bf16[2,2,16,1024]{3,2,1,0:T(8,128)(2,1)S(1)}, bf16[2,2,16,1024]{3,2,1,0:T(8,128)(2,1)}, bf16[2,2,16,1024]{3,2,1,0:T(8,128)(2,1)}, bf16[2,2,16,1024]{3,2,1,0:T(8,128)(2,1)}) custom-call(s32[1]{0:T(128)} %bitcast.place_ref, bf16[2,2,64,256]{3,2,1,0:T(8,128)(2,1)S(1)} %get-tuple-element.63.n_ref, bf16[2,2,64,256]{3,2,1,0:T(8,128)(2,1)S(1)} %copy-done.9, ...), custom_call_target="tpu_custom_call" | custom-call | flops 536870912 | bytes 4980736 | tf_op jit(solution)/shard_map/pallas_call | solution.py:87
  40.3 2.9 %collective-permute-start.11 = (bf16[2,2,16,1024]{3,2,1,0:T(8,128)(2,1)}, bf16[2,2,16,1024]{3,2,1,0:T(8,128)(2,1)S(1)}, u32[]{:S(2)}, u32[]{:S(2)}) collective-permute-start(bf16[2,2,16,1024]{3,2,1,0:T(8,128)(2,1)} %get-tuple-element.66), channel_id=1, source_target_pairs={{0,8},{4,12},{8,0},{12,4},{1,9},{5,13},{9,1},{13,5},{2,10},{6,14},... | collective-permute-start | bytes 393224 | tf_op jit(solution)/shard_map/ppermute | solution.py:478
  49.4 4.0 %collective-permute-done.11.rest_1_ = bf16[2,2,16,1024]{3,2,1,0:T(8,128)(2,1)S(1)} collective-permute-done((bf16[2,2,16,1024]{3,2,1,0:T(8,128)(2,1)}, bf16[2,2,16,1024]{3,2,1,0:T(8,128)(2,1)S(1)}, u32[]{:S(2)}, u32[]{:S(2)}) %collective-permute-start.11) | collective-permute-done | bytes 131104 | tf_op jit(solution)/shard_map/ppermute | solution.py:478
  55.2 2.0 %shard_map.87 = (bf16[2,2,16,1024]{3,2,1,0:T(8,128)(2,1)S(1)}, bf16[2,2,16,1024]{3,2,1,0:T(8,128)(2,1)S(1)}, bf16[2,2,16,1024]{3,2,1,0:T(8,128)(2,1)S(1)}, bf16[2,2,16,1024]{3,2,1,0:T(8,128)(2,1)S(1)}) custom-call(s32[1]{0:T(128)} %bitcast.place_ref, f32[16,1024]{1,0:T(8,128)S(1)} %get-tuple-element.56.c_ref, f32[16,1024]{1,0:T(8,128)S(1)} %get-tuple-element.57.s_ref, ...), custom_call_target="tpu_custom_call" | custom-call | flops 134217728 | bytes 1376256 | tf_op jit(solution)/shard_map/pallas_call | solution.py:87
  57.2 4.2 %collective-permute-start.14 = (bf16[2,2,16,1024]{3,2,1,0:T(8,128)(2,1)S(1)}, bf16[2,2,16,1024]{3,2,1,0:T(8,128)(2,1)S(1)}, u32[]{:S(2)}, u32[]{:S(2)}) collective-permute-start(bf16[2,2,16,1024]{3,2,1,0:T(8,128)(2,1)S(1)} %get-tuple-element.70), channel_id=1, source_target_pairs={{0,8},{4,12},{8,0},{12,4},{1,9},{5,13},{9,1},{13,5},{2,10},{6,14},... | collective-permute-start | bytes 393224 | tf_op jit(solution)/shard_map/ppermute | solution.py:478
  62.0 9.0 %collective-permute-done.14.rest_9_ = bf16[2,2,16,1024]{3,2,1,0:T(8,128)(2,1)S(1)} collective-permute-done((bf16[2,2,16,1024]{3,2,1,0:T(8,128)(2,1)S(1)}, bf16[2,2,16,1024]{3,2,1,0:T(8,128)(2,1)S(1)}, u32[]{:S(2)}, u32[]{:S(2)}) %collective-permute-start.14) | collective-permute-done | bytes 131104 | tf_op jit(solution)/shard_map/ppermute | solution.py:478
  72.1 1.9 %shard_map.88 = (f32[2,2,64,256]{3,2,1,0:T(8,128)S(1)}, bf16[2,2,64,256]{3,2,1,0:T(8,128)(2,1)S(1)}) custom-call(s32[1]{0:T(128)} %bitcast.place_ref, bf16[512,512]{1,0:T(8,128)(2,1)S(1)} %get-tuple-element.45.rest_0_, bf16[512,512]{1,0:T(8,128)(2,1)S(1)} %collective-permute-done.rest_1_, bf16[512,512]{1,0:T(8,128)(2,1)S(1)} %collective-permute-done.4.rest_2_, ...), custom_call_target="tpu_custom_call" | custom-call | flops 536870912 | bytes 5111808 | tf_op jit(solution)/shard_map/pallas_call | solution.py:87
  75.6 3.5 %collective-permute-done.17.r_ref = bf16[2,2,64,256]{3,2,1,0:T(8,128)(2,1)S(1)} collective-permute-done((bf16[2,2,64,256]{3,2,1,0:T(8,128)(2,1)S(1)}, bf16[2,2,64,256]{3,2,1,0:T(8,128)(2,1)S(1)}, u32[]{:S(2)}, u32[]{:S(2)}) %collective-permute-start.17) | collective-permute-done | bytes 131104 | tf_op jit(solution)/shard_map/ppermute | solution.py:478
  79.1 2.4 %collective-permute-start.20 = (bf16[2,2,64,256]{3,2,1,0:T(8,128)(2,1)S(1)}, bf16[2,2,64,256]{3,2,1,0:T(8,128)(2,1)S(1)}, u32[]{:S(2)}, u32[]{:S(2)}) collective-permute-start(bf16[2,2,64,256]{3,2,1,0:T(8,128)(2,1)S(1)} %shard_map.89.rest_0_), channel_id=1, source_target_pairs={{0,4},{4,0},{8,12},{12,8},{1,5},{5,1},{9,13},{13,9},{2,6},{6,2},{1... | collective-permute-start | bytes 393224 | tf_op jit(solution)/shard_map/ppermute | solution.py:478
  83.0 3.7 %collective-permute-done.20.rest_3_ = bf16[2,2,64,256]{3,2,1,0:T(8,128)(2,1)S(1)} collective-permute-done((bf16[2,2,64,256]{3,2,1,0:T(8,128)(2,1)S(1)}, bf16[2,2,64,256]{3,2,1,0:T(8,128)(2,1)S(1)}, u32[]{:S(2)}, u32[]{:S(2)}) %collective-permute-start.20) | collective-permute-done | bytes 131104 | tf_op jit(solution)/shard_map/ppermute | solution.py:478
  86.8 2.9 %collective-permute-done.19.rest_2_ = bf16[2,2,64,256]{3,2,1,0:T(8,128)(2,1)S(1)} collective-permute-done((bf16[2,2,64,256]{3,2,1,0:T(8,128)(2,1)S(1)}, bf16[2,2,64,256]{3,2,1,0:T(8,128)(2,1)S(1)}, u32[]{:S(2)}, u32[]{:S(2)}) %collective-permute-start.19) | collective-permute-done | bytes 131104 | tf_op jit(solution)/shard_map/ppermute | solution.py:478
  89.7 4.1 %collective-permute-done.18.rest_1_ = bf16[2,2,64,256]{3,2,1,0:T(8,128)(2,1)S(1)} collective-permute-done((bf16[2,2,64,256]{3,2,1,0:T(8,128)(2,1)S(1)}, bf16[2,2,64,256]{3,2,1,0:T(8,128)(2,1)S(1)}, u32[]{:S(2)}, u32[]{:S(2)}) %collective-permute-start.18) | collective-permute-done | bytes 131104 | tf_op jit(solution)/shard_map/ppermute | solution.py:478
  96.0 3.5 %collective-permute-done.21.f_ref = bf16[2,2,64,256]{3,2,1,0:T(8,128)(2,1)S(1)} collective-permute-done((bf16[2,2,64,256]{3,2,1,0:T(8,128)(2,1)S(1)}, bf16[2,2,64,256]{3,2,1,0:T(8,128)(2,1)S(1)}, u32[]{:S(2)}, u32[]{:S(2)}) %collective-permute-start.21) | collective-permute-done | bytes 131104 | tf_op jit(solution)/shard_map/ppermute | solution.py:478
  99.5 2.7 %shard_map.91 = (bf16[2,2,16,1024]{3,2,1,0:T(8,128)(2,1)S(1)}, bf16[2,2,16,1024]{3,2,1,0:T(8,128)(2,1)S(1)}, bf16[2,2,16,1024]{3,2,1,0:T(8,128)(2,1)S(1)}, bf16[2,2,16,1024]{3,2,1,0:T(8,128)(2,1)S(1)}) custom-call(s32[1]{0:T(128)} %bitcast.place_ref, bf16[2,2,64,256]{3,2,1,0:T(8,128)(2,1)S(1)} %shard_map.90.n_ref, ...), custom_call_target="tpu_custom_call" | custom-call | flops 536870912 | bytes 4980736 | tf_op jit(solution)/shard_map/pallas_call | solution.py:87
  102.3 2.1 %collective-permute-start.23 = (bf16[2,2,16,1024]{3,2,1,0:T(8,128)(2,1)S(1)}, bf16[2,2,16,1024]{3,2,1,0:T(8,128)(2,1)S(1)}, u32[]{:S(2)}, u32[]{:S(2)}) collective-permute-start(bf16[2,2,16,1024]{3,2,1,0:T(8,128)(2,1)S(1)} %get-tuple-element.77), channel_id=1, source_target_pairs={{0,12},{4,8},{8,4},{12,0},{1,13},{5,9},{9,5},{13,1},{2,14},{6,10},... | collective-permute-start | bytes 393224 | tf_op jit(solution)/shard_map/ppermute | solution.py:478
  105.8 6.3 %collective-permute-done.22.rest_1_ = bf16[2,2,16,1024]{3,2,1,0:T(8,128)(2,1)S(1)} collective-permute-done((bf16[2,2,16,1024]{3,2,1,0:T(8,128)(2,1)S(1)}, bf16[2,2,16,1024]{3,2,1,0:T(8,128)(2,1)S(1)}, u32[]{:S(2)}, u32[]{:S(2)}) %collective-permute-start.22) | collective-permute-done | bytes 131104 | tf_op jit(solution)/shard_map/ppermute | solution.py:478
  113.3 2.6 %collective-permute-start.25 = (bf16[2,2,16,1024]{3,2,1,0:T(8,128)(2,1)S(1)}, bf16[2,2,16,1024]{3,2,1,0:T(8,128)(2,1)S(1)}, u32[]{:S(2)}, u32[]{:S(2)}) collective-permute-start(bf16[2,2,16,1024]{3,2,1,0:T(8,128)(2,1)S(1)} %get-tuple-element.80), channel_id=1, source_target_pairs={{0,8},{4,12},{8,0},{12,4},{1,9},{5,13},{9,1},{13,5},{2,10},{6,14},... | collective-permute-start | bytes 393224 | tf_op jit(solution)/shard_map/ppermute | solution.py:478
  115.9 1.8 %collective-permute-start.26 = (bf16[2,2,16,1024]{3,2,1,0:T(8,128)(2,1)S(1)}, bf16[2,2,16,1024]{3,2,1,0:T(8,128)(2,1)S(1)}, u32[]{:S(2)}, u32[]{:S(2)}) collective-permute-start(bf16[2,2,16,1024]{3,2,1,0:T(8,128)(2,1)S(1)} %get-tuple-element.81), channel_id=1, source_target_pairs={{0,12},{4,8},{8,4},{12,0},{1,13},{5,9},{9,5},{13,1},{2,14},{6,10},... | collective-permute-start | bytes 393224 | tf_op jit(solution)/shard_map/ppermute | solution.py:478
  117.7 7.9 %collective-permute-done.25.rest_9_ = bf16[2,2,16,1024]{3,2,1,0:T(8,128)(2,1)S(1)} collective-permute-done((bf16[2,2,16,1024]{3,2,1,0:T(8,128)(2,1)S(1)}, bf16[2,2,16,1024]{3,2,1,0:T(8,128)(2,1)S(1)}, u32[]{:S(2)}, u32[]{:S(2)}) %collective-permute-start.25) | collective-permute-done | bytes 131104 | tf_op jit(solution)/shard_map/ppermute | solution.py:478
  125.6 1.9 %shard_map.93 = (f32[2,2,64,256]{3,2,1,0:T(8,128)S(1)}, bf16[2,2,64,256]{3,2,1,0:T(8,128)(2,1)S(1)}) custom-call(s32[1]{0:T(128)} %bitcast.place_ref, bf16[512,512]{1,0:T(8,128)(2,1)S(1)} %get-tuple-element.45.rest_0_, bf16[512,512]{1,0:T(8,128)(2,1)S(1)} %collective-permute-done.rest_1_, bf16[512,512]{1,0:T(8,128)(2,1)S(1)} %collective-permute-done.4.rest_2_, ...), custom_call_target="tpu_custom_call" | custom-call | flops 536870912 | bytes 5111808 | tf_op jit(solution)/shard_map/pallas_call | solution.py:87
  129.2 3.4 %collective-permute-done.28.r_ref = bf16[2,2,64,256]{3,2,1,0:T(8,128)(2,1)S(1)} collective-permute-done((bf16[2,2,64,256]{3,2,1,0:T(8,128)(2,1)S(1)}, bf16[2,2,64,256]{3,2,1,0:T(8,128)(2,1)S(1)}, u32[]{:S(2)}, u32[]{:S(2)}) %collective-permute-start.28) | collective-permute-done | bytes 131104 | tf_op jit(solution)/shard_map/ppermute | solution.py:478
  132.6 2.0 %collective-permute-start.31 = (bf16[2,2,64,256]{3,2,1,0:T(8,128)(2,1)S(1)}, bf16[2,2,64,256]{3,2,1,0:T(8,128)(2,1)S(1)}, u32[]{:S(2)}, u32[]{:S(2)}) collective-permute-start(bf16[2,2,64,256]{3,2,1,0:T(8,128)(2,1)S(1)} %shard_map.94.rest_0_), channel_id=1, source_target_pairs={{0,4},{4,0},{8,12},{12,8},{1,5},{5,1},{9,13},{13,9},{2,6},{6,2},{1... | collective-permute-start | bytes 393224 | tf_op jit(solution)/shard_map/ppermute | solution.py:478
  136.3 3.0 %collective-permute-done.31.rest_3_ = bf16[2,2,64,256]{3,2,1,0:T(8,128)(2,1)S(1)} collective-permute-done((bf16[2,2,64,256]{3,2,1,0:T(8,128)(2,1)S(1)}, bf16[2,2,64,256]{3,2,1,0:T(8,128)(2,1)S(1)}, u32[]{:S(2)}, u32[]{:S(2)}) %collective-permute-start.31) | collective-permute-done | bytes 131104 | tf_op jit(solution)/shard_map/ppermute | solution.py:478
  139.2 2.4 %collective-permute-done.30.rest_2_ = bf16[2,2,64,256]{3,2,1,0:T(8,128)(2,1)S(1)} collective-permute-done((bf16[2,2,64,256]{3,2,1,0:T(8,128)(2,1)S(1)}, bf16[2,2,64,256]{3,2,1,0:T(8,128)(2,1)S(1)}, u32[]{:S(2)}, u32[]{:S(2)}) %collective-permute-start.30) | collective-permute-done | bytes 131104 | tf_op jit(solution)/shard_map/ppermute | solution.py:478
  141.7 4.2 %collective-permute-done.29.rest_1_ = bf16[2,2,64,256]{3,2,1,0:T(8,128)(2,1)S(1)} collective-permute-done((bf16[2,2,64,256]{3,2,1,0:T(8,128)(2,1)S(1)}, bf16[2,2,64,256]{3,2,1,0:T(8,128)(2,1)S(1)}, u32[]{:S(2)}, u32[]{:S(2)}) %collective-permute-start.29) | collective-permute-done | bytes 131104 | tf_op jit(solution)/shard_map/ppermute | solution.py:478
  145.9 3.4 %shard_map.95 = bf16[64,128,256]{2,1,0:T(8,128)(2,1)} custom-call(s32[1]{0:T(128)} %bitcast.place_ref, s32[1]{0:T(128)} %bitcast.1.focal_ref, bf16[64,128,256]{2,1,0:T(8,128)(2,1)S(1)} %copy-done.1, s32[128,256]{1,0:T(8,128)S(1)} %copy-done.4, bf16[4,128,128]{2,1,0:T(8,128)(2,1)S(1)} %copy-done.7, bf16[2,2,64,256]{3,2,1,0:T(8,128)(2,1)S(1)} %shard_map.94.rest_0_, ...), custom_call_target="tpu_custom_call" | custom-call | flops 67108864 | bytes 9175040 | tf_op jit(solution)/shard_map/pallas_call | solution.py:87
  (77 shorter events, 33.0 us)
Async XLA Ops:
  3.5 22.8 %collective-permute-start = (bf16[512,512]{1,0:T(8,128)(2,1)}, bf16[512,512]{1,0:T(8,128)(2,1)S(1)}, u32[]{:S(2)}, u32[]{:S(2)}) collective-permute-start(bf16[512,512]{1,0:T(8,128)(2,1)} %get-tuple-element.46), channel_id=1, source_target_pairs={{0,2},{2,0},{1,3},{3,1},{4,6},{6,4},{5,7},{7,5},{8,10},{10,8},{9,1... | collective-permute-start | bytes 1572872 | tf_op jit(solution)/shard_map/ppermute | solution.py:478
  6.4 26.8 %collective-permute-start.6 = (bf16[512,512]{1,0:T(8,128)(2,1)}, bf16[512,512]{1,0:T(8,128)(2,1)S(1)}, u32[]{:S(2)}, u32[]{:S(2)}) collective-permute-start(bf16[512,512]{1,0:T(8,128)(2,1)} %get-tuple-element.54), channel_id=1, source_target_pairs={{0,2},{2,0},{1,3},{3,1},{4,6},{6,4},{5,7},{7,5},{8,10},{10,8},{9,1... | collective-permute-start | bytes 1572872 | tf_op jit(solution)/shard_map/ppermute | solution.py:478
  10.3 12.9 %collective-permute-start.1 = (bf16[2,2,64,256]{3,2,1,0:T(8,128)(2,1)S(1)}, bf16[2,2,64,256]{3,2,1,0:T(8,128)(2,1)S(1)}, u32[]{:S(2)}, u32[]{:S(2)}) collective-permute-start(bf16[2,2,64,256]{3,2,1,0:T(8,128)(2,1)S(1)} %get-tuple-element.48), channel_id=1, source_target_pairs={{0,8},{4,12},{8,0},{12,4},{1,9},{5,13},{9,1},{13,5},{2,10},{6,14},... | collective-permute-start | bytes 393224 | tf_op jit(solution)/shard_map/ppermute | solution.py:478
  13.5 9.8 %collective-permute-start.2 = (bf16[2,2,64,256]{3,2,1,0:T(8,128)(2,1)S(1)}, bf16[2,2,64,256]{3,2,1,0:T(8,128)(2,1)S(1)}, u32[]{:S(2)}, u32[]{:S(2)}) collective-permute-start(bf16[2,2,64,256]{3,2,1,0:T(8,128)(2,1)S(1)} %get-tuple-element.49), channel_id=1, source_target_pairs={{0,12},{4,8},{8,4},{12,0},{1,13},{5,9},{9,5},{13,1},{2,14},{6,10},... | collective-permute-start | bytes 393224 | tf_op jit(solution)/shard_map/ppermute | solution.py:478
  14.8 8.6 %collective-permute-start.3 = (bf16[2,2,64,256]{3,2,1,0:T(8,128)(2,1)S(1)}, bf16[2,2,64,256]{3,2,1,0:T(8,128)(2,1)S(1)}, u32[]{:S(2)}, u32[]{:S(2)}) collective-permute-start(bf16[2,2,64,256]{3,2,1,0:T(8,128)(2,1)S(1)} %get-tuple-element.50), channel_id=1, source_target_pairs={{0,4},{4,0},{8,12},{12,8},{1,5},{5,1},{9,13},{13,9},{2,6},{6,2},{1... | collective-permute-start | bytes 393224 | tf_op jit(solution)/shard_map/ppermute | solution.py:478
  24.2 8.4 %collective-permute-start.7 = (bf16[2,2,64,256]{3,2,1,0:T(8,128)(2,1)S(1)}, bf16[2,2,64,256]{3,2,1,0:T(8,128)(2,1)S(1)}, u32[]{:S(2)}, u32[]{:S(2)}) collective-permute-start(bf16[2,2,64,256]{3,2,1,0:T(8,128)(2,1)S(1)} %get-tuple-element.63.n_ref), channel_id=1, source_target_pairs={{0,2},{2,0},{1,3},{3,1},{4,6},{6,4},{5,7},{7,5},{8,10},{10,8},{9,1... | collective-permute-start | bytes 393224 | tf_op jit(solution)/shard_map/ppermute | solution.py:478
  25.7 7.5 %collective-permute-start.4 = (bf16[512,512]{1,0:T(8,128)(2,1)S(1)}, bf16[512,512]{1,0:T(8,128)(2,1)S(1)}, u32[]{:S(2)}, u32[]{:S(2)}) collective-permute-start(bf16[512,512]{1,0:T(8,128)(2,1)S(1)} %get-tuple-element.45.rest_0_), channel_id=1, source_target_pairs={{0,1},{1,0},{2,3},{3,2},{4,5},{5,4},{6,7},{7,6},{8,9},{9,8},{10,11... | collective-permute-start | bytes 1572872 | tf_op jit(solution)/shard_map/ppermute | solution.py:478
  25.7 7.5 %collective-permute-start.8 = (bf16[512,512]{1,0:T(8,128)(2,1)S(1)}, bf16[512,512]{1,0:T(8,128)(2,1)S(1)}, u32[]{:S(2)}, u32[]{:S(2)}) collective-permute-start(bf16[512,512]{1,0:T(8,128)(2,1)S(1)} %get-tuple-element.53.rest_4_), channel_id=1, source_target_pairs={{0,1},{1,0},{2,3},{3,2},{4,5},{5,4},{6,7},{7,6},{8,9},{9,8},{10,11... | collective-permute-start | bytes 1572872 | tf_op jit(solution)/shard_map/ppermute | solution.py:478
  26.3 7.0 %collective-permute-start.5 = (bf16[512,512]{1,0:T(8,128)(2,1)S(1)}, bf16[512,512]{1,0:T(8,128)(2,1)}, u32[]{:S(2)}, u32[]{:S(2)}) collective-permute-start(bf16[512,512]{1,0:T(8,128)(2,1)S(1)} %collective-permute-done.rest_1_), channel_id=1, source_target_pairs={{0,1},{1,0},{2,3},{3,2},{4,5},{5,4},{6,7},{7,6},{8,9},{9,8},{10,11... | collective-permute-start | bytes 1572872 | tf_op jit(solution)/shard_map/ppermute | solution.py:478
  33.3 2.0 %collective-permute-start.9 = (bf16[512,512]{1,0:T(8,128)(2,1)S(1)}, bf16[512,512]{1,0:T(8,128)(2,1)}, u32[]{:S(2)}, u32[]{:S(2)}) collective-permute-start(bf16[512,512]{1,0:T(8,128)(2,1)S(1)} %collective-permute-done.6.rest_5_), channel_id=1, source_target_pairs={{0,1},{1,0},{2,3},{3,2},{4,5},{5,4},{6,7},{7,6},{8,9},{9,8},{10,11... | collective-permute-start | bytes 1572872 | tf_op jit(solution)/shard_map/ppermute | solution.py:478
  40.3 13.1 %collective-permute-start.11 = (bf16[2,2,16,1024]{3,2,1,0:T(8,128)(2,1)}, bf16[2,2,16,1024]{3,2,1,0:T(8,128)(2,1)S(1)}, u32[]{:S(2)}, u32[]{:S(2)}) collective-permute-start(bf16[2,2,16,1024]{3,2,1,0:T(8,128)(2,1)} %get-tuple-element.66), channel_id=1, source_target_pairs={{0,8},{4,12},{8,0},{12,4},{1,9},{5,13},{9,1},{13,5},{2,10},{6,14},... | collective-permute-start | bytes 393224 | tf_op jit(solution)/shard_map/ppermute | solution.py:478
  43.2 10.2 %collective-permute-start.12 = (bf16[2,2,16,1024]{3,2,1,0:T(8,128)(2,1)}, bf16[2,2,16,1024]{3,2,1,0:T(8,128)(2,1)}, u32[]{:S(2)}, u32[]{:S(2)}) collective-permute-start(bf16[2,2,16,1024]{3,2,1,0:T(8,128)(2,1)} %get-tuple-element.67), channel_id=1, source_target_pairs={{0,12},{4,8},{8,4},{12,0},{1,13},{5,9},{9,5},{13,1},{2,14},{6,10},... | collective-permute-start | bytes 393224 | tf_op jit(solution)/shard_map/ppermute | solution.py:478
  44.5 9.7 %collective-permute-start.13 = (bf16[2,2,16,1024]{3,2,1,0:T(8,128)(2,1)}, bf16[2,2,16,1024]{3,2,1,0:T(8,128)(2,1)}, u32[]{:S(2)}, u32[]{:S(2)}) collective-permute-start(bf16[2,2,16,1024]{3,2,1,0:T(8,128)(2,1)} %get-tuple-element.68), channel_id=1, source_target_pairs={{0,4},{4,0},{8,12},{12,8},{1,5},{5,1},{9,13},{13,9},{2,6},{6,2},{1... | collective-permute-start | bytes 393224 | tf_op jit(solution)/shard_map/ppermute | solution.py:478
  46.1 1.6 %collective-permute-start.10 = (s32[16,512]{1,0:T(8,128)}, s32[16,512]{1,0:T(8,128)}, u32[]{:S(2)}, u32[]{:S(2)}) collective-permute-start(s32[16,512]{1,0:T(8,128)} %get-tuple-element.85), channel_id=1, source_target_pairs={{0,1},{1,0},{2,3},{3,2},{4,5},{5,4},{6,7},{7,6},{8,9},{9,8},{10,11... | collective-permute-start | bytes 98312 | tf_op jit(solution)/shard_map/ppermute | solution.py:478
  57.2 13.8 %collective-permute-start.14 = (bf16[2,2,16,1024]{3,2,1,0:T(8,128)(2,1)S(1)}, bf16[2,2,16,1024]{3,2,1,0:T(8,128)(2,1)S(1)}, u32[]{:S(2)}, u32[]{:S(2)}) collective-permute-start(bf16[2,2,16,1024]{3,2,1,0:T(8,128)(2,1)S(1)} %get-tuple-element.70), channel_id=1, source_target_pairs={{0,8},{4,12},{8,0},{12,4},{1,9},{5,13},{9,1},{13,5},{2,10},{6,14},... | collective-permute-start | bytes 393224 | tf_op jit(solution)/shard_map/ppermute | solution.py:478
  61.4 9.6 %collective-permute-start.15 = (bf16[2,2,16,1024]{3,2,1,0:T(8,128)(2,1)S(1)}, bf16[2,2,16,1024]{3,2,1,0:T(8,128)(2,1)S(1)}, u32[]{:S(2)}, u32[]{:S(2)}) collective-permute-start(bf16[2,2,16,1024]{3,2,1,0:T(8,128)(2,1)S(1)} %get-tuple-element.71), channel_id=1, source_target_pairs={{0,12},{4,8},{8,4},{12,0},{1,13},{5,9},{9,5},{13,1},{2,14},{6,10},... | collective-permute-start | bytes 393224 | tf_op jit(solution)/shard_map/ppermute | solution.py:478
  61.8 10.3 %collective-permute-start.16 = (bf16[2,2,16,1024]{3,2,1,0:T(8,128)(2,1)S(1)}, bf16[2,2,16,1024]{3,2,1,0:T(8,128)(2,1)S(1)}, u32[]{:S(2)}, u32[]{:S(2)}) collective-permute-start(bf16[2,2,16,1024]{3,2,1,0:T(8,128)(2,1)S(1)} %get-tuple-element.72), channel_id=1, source_target_pairs={{0,4},{4,0},{8,12},{12,8},{1,5},{5,1},{9,13},{13,9},{2,6},{6,2},{1... | collective-permute-start | bytes 393224 | tf_op jit(solution)/shard_map/ppermute | solution.py:478
  74.1 5.0 %collective-permute-start.17 = (bf16[2,2,64,256]{3,2,1,0:T(8,128)(2,1)S(1)}, bf16[2,2,64,256]{3,2,1,0:T(8,128)(2,1)S(1)}, u32[]{:S(2)}, u32[]{:S(2)}) collective-permute-start(bf16[2,2,64,256]{3,2,1,0:T(8,128)(2,1)S(1)} %get-tuple-element.74), channel_id=1, source_target_pairs={{0,2},{2,0},{1,3},{3,1},{4,6},{6,4},{5,7},{7,5},{8,10},{10,8},{9,1... | collective-permute-start | bytes 393224 | tf_op jit(solution)/shard_map/ppermute | solution.py:478
  79.1 7.6 %collective-permute-start.20 = (bf16[2,2,64,256]{3,2,1,0:T(8,128)(2,1)S(1)}, bf16[2,2,64,256]{3,2,1,0:T(8,128)(2,1)S(1)}, u32[]{:S(2)}, u32[]{:S(2)}) collective-permute-start(bf16[2,2,64,256]{3,2,1,0:T(8,128)(2,1)S(1)} %shard_map.89.rest_0_), channel_id=1, source_target_pairs={{0,4},{4,0},{8,12},{12,8},{1,5},{5,1},{9,13},{13,9},{2,6},{6,2},{1... | collective-permute-start | bytes 393224 | tf_op jit(solution)/shard_map/ppermute | solution.py:478
  81.5 8.2 %collective-permute-start.19 = (bf16[2,2,64,256]{3,2,1,0:T(8,128)(2,1)S(1)}, bf16[2,2,64,256]{3,2,1,0:T(8,128)(2,1)S(1)}, u32[]{:S(2)}, u32[]{:S(2)}) collective-permute-start(bf16[2,2,64,256]{3,2,1,0:T(8,128)(2,1)S(1)} %shard_map.89.rest_0_), channel_id=1, source_target_pairs={{0,12},{4,8},{8,4},{12,0},{1,13},{5,9},{9,5},{13,1},{2,14},{6,10},... | collective-permute-start | bytes 393224 | tf_op jit(solution)/shard_map/ppermute | solution.py:478
  82.5 11.3 %collective-permute-start.18 = (bf16[2,2,64,256]{3,2,1,0:T(8,128)(2,1)S(1)}, bf16[2,2,64,256]{3,2,1,0:T(8,128)(2,1)S(1)}, u32[]{:S(2)}, u32[]{:S(2)}) collective-permute-start(bf16[2,2,64,256]{3,2,1,0:T(8,128)(2,1)S(1)} %shard_map.89.rest_0_), channel_id=1, source_target_pairs={{0,8},{4,12},{8,0},{12,4},{1,9},{5,13},{9,1},{13,5},{2,10},{6,14},... | collective-permute-start | bytes 393224 | tf_op jit(solution)/shard_map/ppermute | solution.py:478
  94.4 5.0 %collective-permute-start.21 = (bf16[2,2,64,256]{3,2,1,0:T(8,128)(2,1)S(1)}, bf16[2,2,64,256]{3,2,1,0:T(8,128)(2,1)S(1)}, u32[]{:S(2)}, u32[]{:S(2)}) collective-permute-start(bf16[2,2,64,256]{3,2,1,0:T(8,128)(2,1)S(1)} %shard_map.90.n_ref), channel_id=1, source_target_pairs={{0,2},{2,0},{1,3},{3,1},{4,6},{6,4},{5,7},{7,5},{8,10},{10,8},{9,1... | collective-permute-start | bytes 393224 | tf_op jit(solution)/shard_map/ppermute | solution.py:478
  102.2 9.8 %collective-permute-start.22 = (bf16[2,2,16,1024]{3,2,1,0:T(8,128)(2,1)S(1)}, bf16[2,2,16,1024]{3,2,1,0:T(8,128)(2,1)S(1)}, u32[]{:S(2)}, u32[]{:S(2)}) collective-permute-start(bf16[2,2,16,1024]{3,2,1,0:T(8,128)(2,1)S(1)} %get-tuple-element.76), channel_id=1, source_target_pairs={{0,8},{4,12},{8,0},{12,4},{1,9},{5,13},{9,1},{13,5},{2,10},{6,14},... | collective-permute-start | bytes 393224 | tf_op jit(solution)/shard_map/ppermute | solution.py:478
  102.3 9.7 %collective-permute-start.23 = (bf16[2,2,16,1024]{3,2,1,0:T(8,128)(2,1)S(1)}, bf16[2,2,16,1024]{3,2,1,0:T(8,128)(2,1)S(1)}, u32[]{:S(2)}, u32[]{:S(2)}) collective-permute-start(bf16[2,2,16,1024]{3,2,1,0:T(8,128)(2,1)S(1)} %get-tuple-element.77), channel_id=1, source_target_pairs={{0,12},{4,8},{8,4},{12,0},{1,13},{5,9},{9,5},{13,1},{2,14},{6,10},... | collective-permute-start | bytes 393224 | tf_op jit(solution)/shard_map/ppermute | solution.py:478
  104.4 7.8 %collective-permute-start.24 = (bf16[2,2,16,1024]{3,2,1,0:T(8,128)(2,1)S(1)}, bf16[2,2,16,1024]{3,2,1,0:T(8,128)(2,1)S(1)}, u32[]{:S(2)}, u32[]{:S(2)}) collective-permute-start(bf16[2,2,16,1024]{3,2,1,0:T(8,128)(2,1)S(1)} %get-tuple-element.78), channel_id=1, source_target_pairs={{0,4},{4,0},{8,12},{12,8},{1,5},{5,1},{9,13},{13,9},{2,6},{6,2},{1... | collective-permute-start | bytes 393224 | tf_op jit(solution)/shard_map/ppermute | solution.py:478
  113.3 12.3 %collective-permute-start.25 = (bf16[2,2,16,1024]{3,2,1,0:T(8,128)(2,1)S(1)}, bf16[2,2,16,1024]{3,2,1,0:T(8,128)(2,1)S(1)}, u32[]{:S(2)}, u32[]{:S(2)}) collective-permute-start(bf16[2,2,16,1024]{3,2,1,0:T(8,128)(2,1)S(1)} %get-tuple-element.80), channel_id=1, source_target_pairs={{0,8},{4,12},{8,0},{12,4},{1,9},{5,13},{9,1},{13,5},{2,10},{6,14},... | collective-permute-start | bytes 393224 | tf_op jit(solution)/shard_map/ppermute | solution.py:478
  115.9 9.7 %collective-permute-start.26 = (bf16[2,2,16,1024]{3,2,1,0:T(8,128)(2,1)S(1)}, bf16[2,2,16,1024]{3,2,1,0:T(8,128)(2,1)S(1)}, u32[]{:S(2)}, u32[]{:S(2)}) collective-permute-start(bf16[2,2,16,1024]{3,2,1,0:T(8,128)(2,1)S(1)} %get-tuple-element.81), channel_id=1, source_target_pairs={{0,12},{4,8},{8,4},{12,0},{1,13},{5,9},{9,5},{13,1},{2,14},{6,10},... | collective-permute-start | bytes 393224 | tf_op jit(solution)/shard_map/ppermute | solution.py:478
  117.7 7.9 %collective-permute-start.27 = (bf16[2,2,16,1024]{3,2,1,0:T(8,128)(2,1)S(1)}, bf16[2,2,16,1024]{3,2,1,0:T(8,128)(2,1)S(1)}, u32[]{:S(2)}, u32[]{:S(2)}) collective-permute-start(bf16[2,2,16,1024]{3,2,1,0:T(8,128)(2,1)S(1)} %get-tuple-element.82), channel_id=1, source_target_pairs={{0,4},{4,0},{8,12},{12,8},{1,5},{5,1},{9,13},{13,9},{2,6},{6,2},{1... | collective-permute-start | bytes 393224 | tf_op jit(solution)/shard_map/ppermute | solution.py:478
  127.5 5.0 %collective-permute-start.28 = (bf16[2,2,64,256]{3,2,1,0:T(8,128)(2,1)S(1)}, bf16[2,2,64,256]{3,2,1,0:T(8,128)(2,1)S(1)}, u32[]{:S(2)}, u32[]{:S(2)}) collective-permute-start(bf16[2,2,64,256]{3,2,1,0:T(8,128)(2,1)S(1)} %get-tuple-element.84), channel_id=1, source_target_pairs={{0,2},{2,0},{1,3},{3,1},{4,6},{6,4},{5,7},{7,5},{8,10},{10,8},{9,1... | collective-permute-start | bytes 393224 | tf_op jit(solution)/shard_map/ppermute | solution.py:478
  132.6 6.6 %collective-permute-start.31 = (bf16[2,2,64,256]{3,2,1,0:T(8,128)(2,1)S(1)}, bf16[2,2,64,256]{3,2,1,0:T(8,128)(2,1)S(1)}, u32[]{:S(2)}, u32[]{:S(2)}) collective-permute-start(bf16[2,2,64,256]{3,2,1,0:T(8,128)(2,1)S(1)} %shard_map.94.rest_0_), channel_id=1, source_target_pairs={{0,4},{4,0},{8,12},{12,8},{1,5},{5,1},{9,13},{13,9},{2,6},{6,2},{1... | collective-permute-start | bytes 393224 | tf_op jit(solution)/shard_map/ppermute | solution.py:478
  134.6 7.1 %collective-permute-start.30 = (bf16[2,2,64,256]{3,2,1,0:T(8,128)(2,1)S(1)}, bf16[2,2,64,256]{3,2,1,0:T(8,128)(2,1)S(1)}, u32[]{:S(2)}, u32[]{:S(2)}) collective-permute-start(bf16[2,2,64,256]{3,2,1,0:T(8,128)(2,1)S(1)} %shard_map.94.rest_0_), channel_id=1, source_target_pairs={{0,12},{4,8},{8,4},{12,0},{1,13},{5,9},{9,5},{13,1},{2,14},{6,10},... | collective-permute-start | bytes 393224 | tf_op jit(solution)/shard_map/ppermute | solution.py:478
  136.3 9.6 %collective-permute-start.29 = (bf16[2,2,64,256]{3,2,1,0:T(8,128)(2,1)S(1)}, bf16[2,2,64,256]{3,2,1,0:T(8,128)(2,1)S(1)}, u32[]{:S(2)}, u32[]{:S(2)}) collective-permute-start(bf16[2,2,64,256]{3,2,1,0:T(8,128)(2,1)S(1)} %shard_map.94.rest_0_), channel_id=1, source_target_pairs={{0,8},{4,12},{8,0},{12,4},{1,9},{5,13},{9,1},{13,5},{2,10},{6,14},... | collective-permute-start | bytes 393224 | tf_op jit(solution)/shard_map/ppermute | solution.py:478
  (14 other events, 241.1 us)

commit v10 on v8

--- a/solution.py
+++ b/solution.py
@@ -105,18 +105,18 @@
     return pl.BlockSpec(array.shape, lambda *_: zeros)
 
 
-def masked_halves(response, aperture, place):
+def masked_halves(response, aperture, places):
     per_dev, _, src, rcv = response.shape
     half = src // 2
     steps = half // BLOCK
 
-    def body(place_ref, flags, x_ref, *outs):
+    def body(_, rblk, __, flags, x_ref, *outs):
         lane = lax.broadcasted_iota(jnp.int32, (1, rcv), 1) // BLOCK
         for flip in (1, 0):
             for j in range(per_dev):
                 out = outs[flip * per_dev + j]
                 for step in range(steps):
-                    block = (place_ref[0] ^ flip) * steps + step
+                    block = (rblk[0] ^ flip) * steps + step
                     on = flags[j, pl.ds(block, 1), :].astype(F32)
                     row = sum(jnp.where(lane == r, on[:, r : r + 1], 0.0) for r in range(rcv // BLOCK))
                     gate = jnp.broadcast_to(row, (BLOCK, rcv)).astype(BF16)
@@ -127,7 +127,7 @@
 
     shape = jax.ShapeDtypeStruct((half, 2 * rcv), BF16)
     inputs = [(v, whole(v)) for v in (aperture, response)]
-    outs = call(body, (place,), inputs, [(shape, whole(shape))] * (2 * per_dev), (1,))
+    outs = call(body, places, inputs, [(shape, whole(shape))] * (2 * per_dev), (1,))
     return outs[:per_dev], outs[per_dev:]
 
 
@@ -421,14 +421,14 @@
     return out
 
 
-def updated(initial, onset, messages, table, freq_place, focal_first, first, rows, target):
+def updated(initial, onset, messages, table, places, first, rows, target):
     freq_devs = len(messages)
-    own, rcv = initial.shape[1:]
+    half_rows, own, rcv = initial.shape
     per_dev = messages[0].shape[1]
     tile = 2 * ROWS
     count = table.shape[2]
 
-    def body(place_ref, focal_ref, x_ref, o_ref, t_ref, *rest):
+    def body(place_ref, _, sblk, x_ref, o_ref, t_ref, *rest):
         refs = rest[:freq_devs]
         out, spread_ref = rest[-2:]
         step = pl.program_id(0)
@@ -442,7 +442,7 @@
 
         here = pl.ds(pl.multiple_of(step * tile, tile), tile)
         data = [ref[:, :, here, :].astype(F32) for ref in refs]
-        onsets = o_ref[pl.ds(pl.multiple_of(focal_ref[0] + first + step * tile, tile), tile), :]
+        onsets = o_ref[pl.ds(pl.multiple_of(sblk[0] * half_rows + first + step * tile, tile), tile), :]
         time = lax.broadcasted_iota(jnp.int32, (own, rcv), 0) + place_ref[0] * own
         for half in range(2):
             cut = slice(half * ROWS, (half + 1) * ROWS)
@@ -458,10 +458,10 @@
     aliases = {}
     if target is not None:
         inputs.append((target, pl.BlockSpec(memory_space=pl.ANY)))
-        aliases = {2 + len(inputs) - 1: 0}
+        aliases = {len(places) + len(inputs) - 1: 0}
     (out,) = call(
         body,
-        (freq_place, focal_first),
+        places,
         inputs,
         [(jax.ShapeDtypeStruct(initial.shape, BF16), pl.BlockSpec((tile, own, rcv), lambda i, *_: (first // tile + i, 0, 0)))],
         (rows // tile,),
@@ -495,10 +495,10 @@
     freq_index = lax.axis_index("freq")
     rblk_index = lax.axis_index("rblk")
     sblk_index = lax.axis_index("sblk")
-    freq_place = freq_index.reshape(1)
     places = tuple(index.reshape(1) for index in (freq_index, rblk_index, sblk_index))
-
-    kept, moved = masked_halves(response, aperture, places[1])
+    freq_place = places[0]
+
+    kept, moved = masked_halves(response, aperture, places)
     moved = [exchanged(v, "rblk", 1) for v in moved]
     kept_pair = [exchanged(v, "sblk", 1) for v in kept]
     responses = None
@@ -535,10 +535,7 @@
             if step < ITERS - 1:
                 spectra = next_spectra(sums, messages, rcv_tables, matrix, freq_place)
             else:
-                tile_first = (sblk_index * half_rows).reshape(1)
-                result = updated(
-                    initial, onset_rcv, messages, inverse, freq_place, tile_first, first, rows, result
-                )
+                result = updated(initial, onset_rcv, messages, inverse, places, first, rows, result)
     return result
 
 

time: 143 us -> 134 us (0.937)
  local copies, waits for them, and re-layouts: 12.3 us -> 5.47 us
  Pallas kernels: 15.5 us -> 12.7 us
    unnamed x33 -> x17, local copies, waits for them, and re-layouts: 12.3 us -> 5.47 us
    pallas_call x16, Pallas kernels: 15.5 us -> 12.7 us  [call(): pl.pallas_call(body, grid_spec=pltpu.PrefetchScalarGridSpec(num_scalar_pr...]
where the time goes in v10:
time: 134 us
  waiting for transfers between devices  75 us (56%)
  starting transfers between devices  40.7 us (30%)
  Pallas kernels  12.7 us (9%)
  local copies, waits for them, and re-layouts  5.47 us (4%)
    ppermute x32, waiting for transfers between devices, exchanged(): lax.ppermute(value, axis, [(i, i ^ step) for i in range(lax.axis_size(axi...  75 us
    ppermute x32, starting transfers between devices, exchanged(): lax.ppermute(value, axis, [(i, i ^ step) for i in range(lax.axis_size(axi...  40.7 us
    pallas_call x16, Pallas kernels, call(): pl.pallas_call(body, grid_spec=pltpu.PrefetchScalarGridSpec(num_scalar_pr...  12.7 us
    unnamed x17, local copies, waits for them, and re-layouts  5.47 us
  transfers between devices with their start and end apart: 32, of which 21 were waited for; matrix products, arithmetic and copies ran while one was open for 0% of the time, Pallas kernels for 2%

profile of v10, /device:TPU:0, one launch (start us, length us, event | category | flops | bytes accessed | tf_op | source)
XLA Modules:
  0.0 134.0 jit_solution(7281139320688429890)
XLA Ops:
  0.8 1.6 %copy-done.2 = bf16[2,2,1024,256]{3,2,1,0:T(8,128)(2,1)S(1)} copy-done((bf16[2,2,1024,256]{3,2,1,0:T(8,128)(2,1)S(1)}, bf16[2,2,1024,256]{3,2,1,0:T(8,128)(2,1)}, u32[]{:S(2)}) %copy-start.2) | copy-done | bytes 2097176
  2.6 3.0 %collective-permute-start.6 = (bf16[512,512]{1,0:T(8,128)(2,1)S(1)}, bf16[512,512]{1,0:T(8,128)(2,1)S(1)}, u32[]{:S(2)}, u32[]{:S(2)}) collective-permute-start(bf16[512,512]{1,0:T(8,128)(2,1)S(1)} %get-tuple-element.56), channel_id=1, source_target_pairs={{0,2},{2,0},{1,3},{3,1},{4,6},{6,4},{5,7},{7,5},{8,10},{10,8},{9,1... | collective-permute-start | bytes 1572872 | tf_op jit(solution)/shard_map/ppermute | solution.py:476
  5.7 2.2 %copy-done = bf16[64,128,256]{2,1,0:T(8,128)(2,1)S(1)} copy-done((bf16[64,128,256]{2,1,0:T(8,128)(2,1)S(1)}, bf16[64,128,256]{2,1,0:T(8,128)(2,1)}, u32[]{:S(2)}) %copy-start) | copy-done | bytes 4194328
  9.5 3.1 %collective-permute-start.1 = (bf16[2,2,64,256]{3,2,1,0:T(8,128)(2,1)S(1)}, bf16[2,2,64,256]{3,2,1,0:T(8,128)(2,1)S(1)}, u32[]{:S(2)}, u32[]{:S(2)}) collective-permute-start(bf16[2,2,64,256]{3,2,1,0:T(8,128)(2,1)S(1)} %get-tuple-element.50), channel_id=1, source_target_pairs={{0,8},{4,12},{8,0},{12,4},{1,9},{5,13},{9,1},{13,5},{2,10},{6,14},... | collective-permute-start | bytes 393224 | tf_op jit(solution)/shard_map/ppermute | solution.py:476
  14.2 8.2 %collective-permute-done.1.refs_1_ = bf16[2,2,64,256]{3,2,1,0:T(8,128)(2,1)S(1)} collective-permute-done((bf16[2,2,64,256]{3,2,1,0:T(8,128)(2,1)S(1)}, bf16[2,2,64,256]{3,2,1,0:T(8,128)(2,1)S(1)}, u32[]{:S(2)}, u32[]{:S(2)}) %collective-permute-start.1) | collective-permute-done | bytes 131104 | tf_op jit(solution)/shard_map/ppermute | solution.py:476
  22.6 1.6 %collective-permute-start.7 = (bf16[2,2,64,256]{3,2,1,0:T(8,128)(2,1)S(1)}, bf16[2,2,64,256]{3,2,1,0:T(8,128)(2,1)S(1)}, u32[]{:S(2)}, u32[]{:S(2)}) collective-permute-start(bf16[2,2,64,256]{3,2,1,0:T(8,128)(2,1)S(1)} %get-tuple-element.67.n_ref), channel_id=1, source_target_pairs={{0,2},{2,0},{1,3},{3,1},{4,6},{6,4},{5,7},{7,5},{8,10},{10,8},{9,1... | collective-permute-start | bytes 393224 | tf_op jit(solution)/shard_map/ppermute | solution.py:476
  24.7 6.8 %collective-permute-done.7.f_ref = bf16[2,2,64,256]{3,2,1,0:T(8,128)(2,1)S(1)} collective-permute-done((bf16[2,2,64,256]{3,2,1,0:T(8,128)(2,1)S(1)}, bf16[2,2,64,256]{3,2,1,0:T(8,128)(2,1)S(1)}, u32[]{:S(2)}, u32[]{:S(2)}) %collective-permute-start.7) | collective-permute-done | bytes 131104 | tf_op jit(solution)/shard_map/ppermute | solution.py:476
  32.1 1.4 %collective-permute-done.9.rest_7_ = bf16[512,512]{1,0:T(8,128)(2,1)S(1)} collective-permute-done((bf16[512,512]{1,0:T(8,128)(2,1)S(1)}, bf16[512,512]{1,0:T(8,128)(2,1)S(1)}, u32[]{:S(2)}, u32[]{:S(2)}) %collective-permute-start.9) | collective-permute-done | bytes 524320 | tf_op jit(solution)/shard_map/ppermute | solution.py:476
  34.2 1.5 %shard_map.88 = (bf16[2,2,16,1024]{3,2,1,0:T(8,128)(2,1)S(1)}, bf16[2,2,16,1024]{3,2,1,0:T(8,128)(2,1)S(1)}, bf16[2,2,16,1024]{3,2,1,0:T(8,128)(2,1)S(1)}, bf16[2,2,16,1024]{3,2,1,0:T(8,128)(2,1)S(1)}) custom-call(s32[1]{0:T(128)} %bitcast._.place_ref.freq, bf16[2,2,64,256]{3,2,1,0:T(8,128)(2,1)S(1)} %get-tuple-element.67.n_ref, ...), custom_call_target="tpu_custom_call" | custom-call | flops 536870912 | bytes 4980736 | tf_op jit(solution)/shard_map/pallas_call | solution.py:87
  35.7 2.9 %collective-permute-start.11 = (bf16[2,2,16,1024]{3,2,1,0:T(8,128)(2,1)S(1)}, bf16[2,2,16,1024]{3,2,1,0:T(8,128)(2,1)S(1)}, u32[]{:S(2)}, u32[]{:S(2)}) collective-permute-start(bf16[2,2,16,1024]{3,2,1,0:T(8,128)(2,1)S(1)} %get-tuple-element.70), channel_id=1, source_target_pairs={{0,8},{4,12},{8,0},{12,4},{1,9},{5,13},{9,1},{13,5},{2,10},{6,14},... | collective-permute-start | bytes 393224 | tf_op jit(solution)/shard_map/ppermute | solution.py:476
  42.2 6.5 %collective-permute-done.11.rest_1_ = bf16[2,2,16,1024]{3,2,1,0:T(8,128)(2,1)S(1)} collective-permute-done((bf16[2,2,16,1024]{3,2,1,0:T(8,128)(2,1)S(1)}, bf16[2,2,16,1024]{3,2,1,0:T(8,128)(2,1)S(1)}, u32[]{:S(2)}, u32[]{:S(2)}) %collective-permute-start.11) | collective-permute-done | bytes 131104 | tf_op jit(solution)/shard_map/ppermute | solution.py:476
  50.5 4.2 %collective-permute-start.14 = (bf16[2,2,16,1024]{3,2,1,0:T(8,128)(2,1)S(1)}, bf16[2,2,16,1024]{3,2,1,0:T(8,128)(2,1)S(1)}, u32[]{:S(2)}, u32[]{:S(2)}) collective-permute-start(bf16[2,2,16,1024]{3,2,1,0:T(8,128)(2,1)S(1)} %get-tuple-element.74), channel_id=1, source_target_pairs={{0,8},{4,12},{8,0},{12,4},{1,9},{5,13},{9,1},{13,5},{2,10},{6,14},... | collective-permute-start | bytes 393224 | tf_op jit(solution)/shard_map/ppermute | solution.py:476
  55.3 9.0 %collective-permute-done.14.rest_9_ = bf16[2,2,16,1024]{3,2,1,0:T(8,128)(2,1)S(1)} collective-permute-done((bf16[2,2,16,1024]{3,2,1,0:T(8,128)(2,1)S(1)}, bf16[2,2,16,1024]{3,2,1,0:T(8,128)(2,1)S(1)}, u32[]{:S(2)}, u32[]{:S(2)}) %collective-permute-start.14) | collective-permute-done | bytes 131104 | tf_op jit(solution)/shard_map/ppermute | solution.py:476
  66.1 1.6 %collective-permute-start.17 = (bf16[2,2,64,256]{3,2,1,0:T(8,128)(2,1)S(1)}, bf16[2,2,64,256]{3,2,1,0:T(8,128)(2,1)S(1)}, u32[]{:S(2)}, u32[]{:S(2)}) collective-permute-start(bf16[2,2,64,256]{3,2,1,0:T(8,128)(2,1)S(1)} %get-tuple-element.78), channel_id=1, source_target_pairs={{0,2},{2,0},{1,3},{3,1},{4,6},{6,4},{5,7},{7,5},{8,10},{10,8},{9,1... | collective-permute-start | bytes 393224 | tf_op jit(solution)/shard_map/ppermute | solution.py:476
  67.7 3.5 %collective-permute-done.17.r_ref = bf16[2,2,64,256]{3,2,1,0:T(8,128)(2,1)S(1)} collective-permute-done((bf16[2,2,64,256]{3,2,1,0:T(8,128)(2,1)S(1)}, bf16[2,2,64,256]{3,2,1,0:T(8,128)(2,1)S(1)}, u32[]{:S(2)}, u32[]{:S(2)}) %collective-permute-start.17) | collective-permute-done | bytes 131104 | tf_op jit(solution)/shard_map/ppermute | solution.py:476
  71.2 1.9 %collective-permute-start.18 = (bf16[2,2,64,256]{3,2,1,0:T(8,128)(2,1)S(1)}, bf16[2,2,64,256]{3,2,1,0:T(8,128)(2,1)S(1)}, u32[]{:S(2)}, u32[]{:S(2)}) collective-permute-start(bf16[2,2,64,256]{3,2,1,0:T(8,128)(2,1)S(1)} %shard_map.91.rest_0_), channel_id=1, source_target_pairs={{0,8},{4,12},{8,0},{12,4},{1,9},{5,13},{9,1},{13,5},{2,10},{6,14},... | collective-permute-start | bytes 393224 | tf_op jit(solution)/shard_map/ppermute | solution.py:476
  73.1 2.8 %collective-permute-start.19 = (bf16[2,2,64,256]{3,2,1,0:T(8,128)(2,1)S(1)}, bf16[2,2,64,256]{3,2,1,0:T(8,128)(2,1)S(1)}, u32[]{:S(2)}, u32[]{:S(2)}) collective-permute-start(bf16[2,2,64,256]{3,2,1,0:T(8,128)(2,1)S(1)} %shard_map.91.rest_0_), channel_id=1, source_target_pairs={{0,12},{4,8},{8,4},{12,0},{1,13},{5,9},{9,5},{13,1},{2,14},{6,10},... | collective-permute-start | bytes 393224 | tf_op jit(solution)/shard_map/ppermute | solution.py:476
  76.6 6.5 %collective-permute-done.18.rest_1_ = bf16[2,2,64,256]{3,2,1,0:T(8,128)(2,1)S(1)} collective-permute-done((bf16[2,2,64,256]{3,2,1,0:T(8,128)(2,1)S(1)}, bf16[2,2,64,256]{3,2,1,0:T(8,128)(2,1)S(1)}, u32[]{:S(2)}, u32[]{:S(2)}) %collective-permute-start.18) | collective-permute-done | bytes 131104 | tf_op jit(solution)/shard_map/ppermute | solution.py:476
  84.3 1.6 %collective-permute-start.21 = (bf16[2,2,64,256]{3,2,1,0:T(8,128)(2,1)S(1)}, bf16[2,2,64,256]{3,2,1,0:T(8,128)(2,1)S(1)}, u32[]{:S(2)}, u32[]{:S(2)}) collective-permute-start(bf16[2,2,64,256]{3,2,1,0:T(8,128)(2,1)S(1)} %shard_map.92.n_ref), channel_id=1, source_target_pairs={{0,2},{2,0},{1,3},{3,1},{4,6},{6,4},{5,7},{7,5},{8,10},{10,8},{9,1... | collective-permute-start | bytes 393224 | tf_op jit(solution)/shard_map/ppermute | solution.py:476
  85.9 3.5 %collective-permute-done.21.f_ref = bf16[2,2,64,256]{3,2,1,0:T(8,128)(2,1)S(1)} collective-permute-done((bf16[2,2,64,256]{3,2,1,0:T(8,128)(2,1)S(1)}, bf16[2,2,64,256]{3,2,1,0:T(8,128)(2,1)S(1)}, u32[]{:S(2)}, u32[]{:S(2)}) %collective-permute-start.21) | collective-permute-done | bytes 131104 | tf_op jit(solution)/shard_map/ppermute | solution.py:476
  89.4 1.5 %shard_map.93 = (bf16[2,2,16,1024]{3,2,1,0:T(8,128)(2,1)S(1)}, bf16[2,2,16,1024]{3,2,1,0:T(8,128)(2,1)S(1)}, bf16[2,2,16,1024]{3,2,1,0:T(8,128)(2,1)S(1)}, bf16[2,2,16,1024]{3,2,1,0:T(8,128)(2,1)S(1)}) custom-call(s32[1]{0:T(128)} %bitcast._.place_ref.freq, bf16[2,2,64,256]{3,2,1,0:T(8,128)(2,1)S(1)} %shard_map.92.n_ref, ...), custom_call_target="tpu_custom_call" | custom-call | flops 536870912 | bytes 4980736 | tf_op jit(solution)/shard_map/pallas_call | solution.py:87
  90.9 1.8 %collective-permute-start.22 = (bf16[2,2,16,1024]{3,2,1,0:T(8,128)(2,1)S(1)}, bf16[2,2,16,1024]{3,2,1,0:T(8,128)(2,1)S(1)}, u32[]{:S(2)}, u32[]{:S(2)}) collective-permute-start(bf16[2,2,16,1024]{3,2,1,0:T(8,128)(2,1)S(1)} %get-tuple-element.80), channel_id=1, source_target_pairs={{0,8},{4,12},{8,0},{12,4},{1,9},{5,13},{9,1},{13,5},{2,10},{6,14},... | collective-permute-start | bytes 393224 | tf_op jit(solution)/shard_map/ppermute | solution.py:476
  92.7 1.7 %collective-permute-start.23 = (bf16[2,2,16,1024]{3,2,1,0:T(8,128)(2,1)S(1)}, bf16[2,2,16,1024]{3,2,1,0:T(8,128)(2,1)S(1)}, u32[]{:S(2)}, u32[]{:S(2)}) collective-permute-start(bf16[2,2,16,1024]{3,2,1,0:T(8,128)(2,1)S(1)} %get-tuple-element.81), channel_id=1, source_target_pairs={{0,12},{4,8},{8,4},{12,0},{1,13},{5,9},{9,5},{13,1},{2,14},{6,10},... | collective-permute-start | bytes 393224 | tf_op jit(solution)/shard_map/ppermute | solution.py:476
  94.5 7.1 %collective-permute-done.22.rest_1_ = bf16[2,2,16,1024]{3,2,1,0:T(8,128)(2,1)S(1)} collective-permute-done((bf16[2,2,16,1024]{3,2,1,0:T(8,128)(2,1)S(1)}, bf16[2,2,16,1024]{3,2,1,0:T(8,128)(2,1)S(1)}, u32[]{:S(2)}, u32[]{:S(2)}) %collective-permute-start.22) | collective-permute-done | bytes 131104 | tf_op jit(solution)/shard_map/ppermute | solution.py:476
  103.0 1.4 %collective-permute-start.25 = (bf16[2,2,16,1024]{3,2,1,0:T(8,128)(2,1)S(1)}, bf16[2,2,16,1024]{3,2,1,0:T(8,128)(2,1)S(1)}, u32[]{:S(2)}, u32[]{:S(2)}) collective-permute-start(bf16[2,2,16,1024]{3,2,1,0:T(8,128)(2,1)S(1)} %get-tuple-element.84), channel_id=1, source_target_pairs={{0,8},{4,12},{8,0},{12,4},{1,9},{5,13},{9,1},{13,5},{2,10},{6,14},... | collective-permute-start | bytes 393224 | tf_op jit(solution)/shard_map/ppermute | solution.py:476
  104.4 3.0 %collective-permute-start.26 = (bf16[2,2,16,1024]{3,2,1,0:T(8,128)(2,1)S(1)}, bf16[2,2,16,1024]{3,2,1,0:T(8,128)(2,1)S(1)}, u32[]{:S(2)}, u32[]{:S(2)}) collective-permute-start(bf16[2,2,16,1024]{3,2,1,0:T(8,128)(2,1)S(1)} %get-tuple-element.85), channel_id=1, source_target_pairs={{0,12},{4,8},{8,4},{12,0},{1,13},{5,9},{9,5},{13,1},{2,14},{6,10},... | collective-permute-start | bytes 393224 | tf_op jit(solution)/shard_map/ppermute | solution.py:476
  107.4 6.0 %collective-permute-done.25.rest_9_ = bf16[2,2,16,1024]{3,2,1,0:T(8,128)(2,1)S(1)} collective-permute-done((bf16[2,2,16,1024]{3,2,1,0:T(8,128)(2,1)S(1)}, bf16[2,2,16,1024]{3,2,1,0:T(8,128)(2,1)S(1)}, u32[]{:S(2)}, u32[]{:S(2)}) %collective-permute-start.25) | collective-permute-done | bytes 131104 | tf_op jit(solution)/shard_map/ppermute | solution.py:476
  115.0 1.6 %collective-permute-start.28 = (bf16[2,2,64,256]{3,2,1,0:T(8,128)(2,1)S(1)}, bf16[2,2,64,256]{3,2,1,0:T(8,128)(2,1)S(1)}, u32[]{:S(2)}, u32[]{:S(2)}) collective-permute-start(bf16[2,2,64,256]{3,2,1,0:T(8,128)(2,1)S(1)} %get-tuple-element.88), channel_id=1, source_target_pairs={{0,2},{2,0},{1,3},{3,1},{4,6},{6,4},{5,7},{7,5},{8,10},{10,8},{9,1... | collective-permute-start | bytes 393224 | tf_op jit(solution)/shard_map/ppermute | solution.py:476
  116.6 3.5 %collective-permute-done.28.r_ref = bf16[2,2,64,256]{3,2,1,0:T(8,128)(2,1)S(1)} collective-permute-done((bf16[2,2,64,256]{3,2,1,0:T(8,128)(2,1)S(1)}, bf16[2,2,64,256]{3,2,1,0:T(8,128)(2,1)S(1)}, u32[]{:S(2)}, u32[]{:S(2)}) %collective-permute-start.28) | collective-permute-done | bytes 131104 | tf_op jit(solution)/shard_map/ppermute | solution.py:476
  120.1 2.1 %collective-permute-start.29 = (bf16[2,2,64,256]{3,2,1,0:T(8,128)(2,1)S(1)}, bf16[2,2,64,256]{3,2,1,0:T(8,128)(2,1)S(1)}, u32[]{:S(2)}, u32[]{:S(2)}) collective-permute-start(bf16[2,2,64,256]{3,2,1,0:T(8,128)(2,1)S(1)} %shard_map.96.rest_0_), channel_id=1, source_target_pairs={{0,8},{4,12},{8,0},{12,4},{1,9},{5,13},{9,1},{13,5},{2,10},{6,14},... | collective-permute-start | bytes 393224 | tf_op jit(solution)/shard_map/ppermute | solution.py:476
  123.6 6.3 %collective-permute-done.29.rest_1_ = bf16[2,2,64,256]{3,2,1,0:T(8,128)(2,1)S(1)} collective-permute-done((bf16[2,2,64,256]{3,2,1,0:T(8,128)(2,1)S(1)}, bf16[2,2,64,256]{3,2,1,0:T(8,128)(2,1)S(1)}, u32[]{:S(2)}, u32[]{:S(2)}) %collective-permute-start.29) | collective-permute-done | bytes 131104 | tf_op jit(solution)/shard_map/ppermute | solution.py:476
  130.7 3.4 %shard_map.97 = bf16[64,128,256]{2,1,0:T(8,128)(2,1)} custom-call(s32[1]{0:T(128)} %bitcast._.place_ref.freq, s32[1]{0:T(128)} %bitcast.1.rblk._, s32[1]{0:T(128)} %bitcast.2.__.sblk, bf16[64,128,256]{2,1,0:T(8,128)(2,1)S(1)} %copy-done.1, s32[128,256]{1,0:T(8,128)S(1)} %copy-done.4, bf16[4,128,128]{2,1,0:T(8,128)(2,1)S(1)} %copy-done.6, ...), custom_call_target="tpu_custom_call" | custom-call | flops 67108864 | bytes 9175040 | tf_op jit(solution)/shard_map/pallas_call | solution.py:87
  (65 shorter events, 21.3 us)
Async XLA Ops:
  2.6 29.0 %collective-permute-start.6 = (bf16[512,512]{1,0:T(8,128)(2,1)S(1)}, bf16[512,512]{1,0:T(8,128)(2,1)S(1)}, u32[]{:S(2)}, u32[]{:S(2)}) collective-permute-start(bf16[512,512]{1,0:T(8,128)(2,1)S(1)} %get-tuple-element.56), channel_id=1, source_target_pairs={{0,2},{2,0},{1,3},{3,1},{4,6},{6,4},{5,7},{7,5},{8,10},{10,8},{9,1... | collective-permute-start | bytes 1572872 | tf_op jit(solution)/shard_map/ppermute | solution.py:476
  5.6 26.0 %collective-permute-start = (bf16[512,512]{1,0:T(8,128)(2,1)S(1)}, bf16[512,512]{1,0:T(8,128)(2,1)S(1)}, u32[]{:S(2)}, u32[]{:S(2)}) collective-permute-start(bf16[512,512]{1,0:T(8,128)(2,1)S(1)} %get-tuple-element.48), channel_id=1, source_target_pairs={{0,2},{2,0},{1,3},{3,1},{4,6},{6,4},{5,7},{7,5},{8,10},{10,8},{9,1... | collective-permute-start | bytes 1572872 | tf_op jit(solution)/shard_map/ppermute | solution.py:476
  9.5 12.9 %collective-permute-start.1 = (bf16[2,2,64,256]{3,2,1,0:T(8,128)(2,1)S(1)}, bf16[2,2,64,256]{3,2,1,0:T(8,128)(2,1)S(1)}, u32[]{:S(2)}, u32[]{:S(2)}) collective-permute-start(bf16[2,2,64,256]{3,2,1,0:T(8,128)(2,1)S(1)} %get-tuple-element.50), channel_id=1, source_target_pairs={{0,8},{4,12},{8,0},{12,4},{1,9},{5,13},{9,1},{13,5},{2,10},{6,14},... | collective-permute-start | bytes 393224 | tf_op jit(solution)/shard_map/ppermute | solution.py:476
  12.6 9.8 %collective-permute-start.2 = (bf16[2,2,64,256]{3,2,1,0:T(8,128)(2,1)S(1)}, bf16[2,2,64,256]{3,2,1,0:T(8,128)(2,1)S(1)}, u32[]{:S(2)}, u32[]{:S(2)}) collective-permute-start(bf16[2,2,64,256]{3,2,1,0:T(8,128)(2,1)S(1)} %get-tuple-element.51), channel_id=1, source_target_pairs={{0,12},{4,8},{8,4},{12,0},{1,13},{5,9},{9,5},{13,1},{2,14},{6,10},... | collective-permute-start | bytes 393224 | tf_op jit(solution)/shard_map/ppermute | solution.py:476
  14.0 8.6 %collective-permute-start.3 = (bf16[2,2,64,256]{3,2,1,0:T(8,128)(2,1)S(1)}, bf16[2,2,64,256]{3,2,1,0:T(8,128)(2,1)S(1)}, u32[]{:S(2)}, u32[]{:S(2)}) collective-permute-start(bf16[2,2,64,256]{3,2,1,0:T(8,128)(2,1)S(1)} %get-tuple-element.52), channel_id=1, source_target_pairs={{0,4},{4,0},{8,12},{12,8},{1,5},{5,1},{9,13},{13,9},{2,6},{6,2},{1... | collective-permute-start | bytes 393224 | tf_op jit(solution)/shard_map/ppermute | solution.py:476
  22.6 8.9 %collective-permute-start.7 = (bf16[2,2,64,256]{3,2,1,0:T(8,128)(2,1)S(1)}, bf16[2,2,64,256]{3,2,1,0:T(8,128)(2,1)S(1)}, u32[]{:S(2)}, u32[]{:S(2)}) collective-permute-start(bf16[2,2,64,256]{3,2,1,0:T(8,128)(2,1)S(1)} %get-tuple-element.67.n_ref), channel_id=1, source_target_pairs={{0,2},{2,0},{1,3},{3,1},{4,6},{6,4},{5,7},{7,5},{8,10},{10,8},{9,1... | collective-permute-start | bytes 393224 | tf_op jit(solution)/shard_map/ppermute | solution.py:476
  24.2 7.8 %collective-permute-start.4 = (bf16[512,512]{1,0:T(8,128)(2,1)S(1)}, bf16[512,512]{1,0:T(8,128)(2,1)S(1)}, u32[]{:S(2)}, u32[]{:S(2)}) collective-permute-start(bf16[512,512]{1,0:T(8,128)(2,1)S(1)} %get-tuple-element.47.rest_0_), channel_id=1, source_target_pairs={{0,1},{1,0},{2,3},{3,2},{4,5},{5,4},{6,7},{7,6},{8,9},{9,8},{10,11... | collective-permute-start | bytes 1572872 | tf_op jit(solution)/shard_map/ppermute | solution.py:476
  24.2 7.8 %collective-permute-start.8 = (bf16[512,512]{1,0:T(8,128)(2,1)S(1)}, bf16[512,512]{1,0:T(8,128)(2,1)S(1)}, u32[]{:S(2)}, u32[]{:S(2)}) collective-permute-start(bf16[512,512]{1,0:T(8,128)(2,1)S(1)} %get-tuple-element.55.rest_4_), channel_id=1, source_target_pairs={{0,1},{1,0},{2,3},{3,2},{4,5},{5,4},{6,7},{7,6},{8,9},{9,8},{10,11... | collective-permute-start | bytes 1572872 | tf_op jit(solution)/shard_map/ppermute | solution.py:476
  31.5 1.9 %collective-permute-start.9 = (bf16[512,512]{1,0:T(8,128)(2,1)S(1)}, bf16[512,512]{1,0:T(8,128)(2,1)S(1)}, u32[]{:S(2)}, u32[]{:S(2)}) collective-permute-start(bf16[512,512]{1,0:T(8,128)(2,1)S(1)} %collective-permute-done.6.rest_5_), channel_id=1, source_target_pairs={{0,1},{1,0},{2,3},{3,2},{4,5},{5,4},{6,7},{7,6},{8,9},{9,8},{10,11... | collective-permute-start | bytes 1572872 | tf_op jit(solution)/shard_map/ppermute | solution.py:476
  31.6 2.7 %collective-permute-start.5 = (bf16[512,512]{1,0:T(8,128)(2,1)S(1)}, bf16[512,512]{1,0:T(8,128)(2,1)S(1)}, u32[]{:S(2)}, u32[]{:S(2)}) collective-permute-start(bf16[512,512]{1,0:T(8,128)(2,1)S(1)} %collective-permute-done.rest_1_), channel_id=1, source_target_pairs={{0,1},{1,0},{2,3},{3,2},{4,5},{5,4},{6,7},{7,6},{8,9},{9,8},{10,11... | collective-permute-start | bytes 1572872 | tf_op jit(solution)/shard_map/ppermute | solution.py:476
  35.7 12.9 %collective-permute-start.11 = (bf16[2,2,16,1024]{3,2,1,0:T(8,128)(2,1)S(1)}, bf16[2,2,16,1024]{3,2,1,0:T(8,128)(2,1)S(1)}, u32[]{:S(2)}, u32[]{:S(2)}) collective-permute-start(bf16[2,2,16,1024]{3,2,1,0:T(8,128)(2,1)S(1)} %get-tuple-element.70), channel_id=1, source_target_pairs={{0,8},{4,12},{8,0},{12,4},{1,9},{5,13},{9,1},{13,5},{2,10},{6,14},... | collective-permute-start | bytes 393224 | tf_op jit(solution)/shard_map/ppermute | solution.py:476
  38.6 10.0 %collective-permute-start.12 = (bf16[2,2,16,1024]{3,2,1,0:T(8,128)(2,1)S(1)}, bf16[2,2,16,1024]{3,2,1,0:T(8,128)(2,1)S(1)}, u32[]{:S(2)}, u32[]{:S(2)}) collective-permute-start(bf16[2,2,16,1024]{3,2,1,0:T(8,128)(2,1)S(1)} %get-tuple-element.71), channel_id=1, source_target_pairs={{0,12},{4,8},{8,4},{12,0},{1,13},{5,9},{9,5},{13,1},{2,14},{6,10},... | collective-permute-start | bytes 393224 | tf_op jit(solution)/shard_map/ppermute | solution.py:476
  40.0 9.5 %collective-permute-start.13 = (bf16[2,2,16,1024]{3,2,1,0:T(8,128)(2,1)S(1)}, bf16[2,2,16,1024]{3,2,1,0:T(8,128)(2,1)S(1)}, u32[]{:S(2)}, u32[]{:S(2)}) collective-permute-start(bf16[2,2,16,1024]{3,2,1,0:T(8,128)(2,1)S(1)} %get-tuple-element.72), channel_id=1, source_target_pairs={{0,4},{4,0},{8,12},{12,8},{1,5},{5,1},{9,13},{13,9},{2,6},{6,2},{1... | collective-permute-start | bytes 393224 | tf_op jit(solution)/shard_map/ppermute | solution.py:476
  40.2 1.3 collective-permute-start.10
  50.5 13.8 %collective-permute-start.14 = (bf16[2,2,16,1024]{3,2,1,0:T(8,128)(2,1)S(1)}, bf16[2,2,16,1024]{3,2,1,0:T(8,128)(2,1)S(1)}, u32[]{:S(2)}, u32[]{:S(2)}) collective-permute-start(bf16[2,2,16,1024]{3,2,1,0:T(8,128)(2,1)S(1)} %get-tuple-element.74), channel_id=1, source_target_pairs={{0,8},{4,12},{8,0},{12,4},{1,9},{5,13},{9,1},{13,5},{2,10},{6,14},... | collective-permute-start | bytes 393224 | tf_op jit(solution)/shard_map/ppermute | solution.py:476
  54.6 9.6 %collective-permute-start.15 = (bf16[2,2,16,1024]{3,2,1,0:T(8,128)(2,1)S(1)}, bf16[2,2,16,1024]{3,2,1,0:T(8,128)(2,1)S(1)}, u32[]{:S(2)}, u32[]{:S(2)}) collective-permute-start(bf16[2,2,16,1024]{3,2,1,0:T(8,128)(2,1)S(1)} %get-tuple-element.75), channel_id=1, source_target_pairs={{0,12},{4,8},{8,4},{12,0},{1,13},{5,9},{9,5},{13,1},{2,14},{6,10},... | collective-permute-start | bytes 393224 | tf_op jit(solution)/shard_map/ppermute | solution.py:476
  55.1 10.3 %collective-permute-start.16 = (bf16[2,2,16,1024]{3,2,1,0:T(8,128)(2,1)S(1)}, bf16[2,2,16,1024]{3,2,1,0:T(8,128)(2,1)S(1)}, u32[]{:S(2)}, u32[]{:S(2)}) collective-permute-start(bf16[2,2,16,1024]{3,2,1,0:T(8,128)(2,1)S(1)} %get-tuple-element.76), channel_id=1, source_target_pairs={{0,4},{4,0},{8,12},{12,8},{1,5},{5,1},{9,13},{13,9},{2,6},{6,2},{1... | collective-permute-start | bytes 393224 | tf_op jit(solution)/shard_map/ppermute | solution.py:476
  66.1 5.0 %collective-permute-start.17 = (bf16[2,2,64,256]{3,2,1,0:T(8,128)(2,1)S(1)}, bf16[2,2,64,256]{3,2,1,0:T(8,128)(2,1)S(1)}, u32[]{:S(2)}, u32[]{:S(2)}) collective-permute-start(bf16[2,2,64,256]{3,2,1,0:T(8,128)(2,1)S(1)} %get-tuple-element.78), channel_id=1, source_target_pairs={{0,2},{2,0},{1,3},{3,1},{4,6},{6,4},{5,7},{7,5},{8,10},{10,8},{9,1... | collective-permute-start | bytes 393224 | tf_op jit(solution)/shard_map/ppermute | solution.py:476
  71.2 12.0 %collective-permute-start.18 = (bf16[2,2,64,256]{3,2,1,0:T(8,128)(2,1)S(1)}, bf16[2,2,64,256]{3,2,1,0:T(8,128)(2,1)S(1)}, u32[]{:S(2)}, u32[]{:S(2)}) collective-permute-start(bf16[2,2,64,256]{3,2,1,0:T(8,128)(2,1)S(1)} %shard_map.91.rest_0_), channel_id=1, source_target_pairs={{0,8},{4,12},{8,0},{12,4},{1,9},{5,13},{9,1},{13,5},{2,10},{6,14},... | collective-permute-start | bytes 393224 | tf_op jit(solution)/shard_map/ppermute | solution.py:476
  73.1 10.1 %collective-permute-start.19 = (bf16[2,2,64,256]{3,2,1,0:T(8,128)(2,1)S(1)}, bf16[2,2,64,256]{3,2,1,0:T(8,128)(2,1)S(1)}, u32[]{:S(2)}, u32[]{:S(2)}) collective-permute-start(bf16[2,2,64,256]{3,2,1,0:T(8,128)(2,1)S(1)} %shard_map.91.rest_0_), channel_id=1, source_target_pairs={{0,12},{4,8},{8,4},{12,0},{1,13},{5,9},{9,5},{13,1},{2,14},{6,10},... | collective-permute-start | bytes 393224 | tf_op jit(solution)/shard_map/ppermute | solution.py:476
  75.9 8.1 %collective-permute-start.20 = (bf16[2,2,64,256]{3,2,1,0:T(8,128)(2,1)S(1)}, bf16[2,2,64,256]{3,2,1,0:T(8,128)(2,1)S(1)}, u32[]{:S(2)}, u32[]{:S(2)}) collective-permute-start(bf16[2,2,64,256]{3,2,1,0:T(8,128)(2,1)S(1)} %shard_map.91.rest_0_), channel_id=1, source_target_pairs={{0,4},{4,0},{8,12},{12,8},{1,5},{5,1},{9,13},{13,9},{2,6},{6,2},{1... | collective-permute-start | bytes 393224 | tf_op jit(solution)/shard_map/ppermute | solution.py:476
  84.3 5.0 %collective-permute-start.21 = (bf16[2,2,64,256]{3,2,1,0:T(8,128)(2,1)S(1)}, bf16[2,2,64,256]{3,2,1,0:T(8,128)(2,1)S(1)}, u32[]{:S(2)}, u32[]{:S(2)}) collective-permute-start(bf16[2,2,64,256]{3,2,1,0:T(8,128)(2,1)S(1)} %shard_map.92.n_ref), channel_id=1, source_target_pairs={{0,2},{2,0},{1,3},{3,1},{4,6},{6,4},{5,7},{7,5},{8,10},{10,8},{9,1... | collective-permute-start | bytes 393224 | tf_op jit(solution)/shard_map/ppermute | solution.py:476
  90.9 10.6 %collective-permute-start.22 = (bf16[2,2,16,1024]{3,2,1,0:T(8,128)(2,1)S(1)}, bf16[2,2,16,1024]{3,2,1,0:T(8,128)(2,1)S(1)}, u32[]{:S(2)}, u32[]{:S(2)}) collective-permute-start(bf16[2,2,16,1024]{3,2,1,0:T(8,128)(2,1)S(1)} %get-tuple-element.80), channel_id=1, source_target_pairs={{0,8},{4,12},{8,0},{12,4},{1,9},{5,13},{9,1},{13,5},{2,10},{6,14},... | collective-permute-start | bytes 393224 | tf_op jit(solution)/shard_map/ppermute | solution.py:476
  92.7 8.9 %collective-permute-start.23 = (bf16[2,2,16,1024]{3,2,1,0:T(8,128)(2,1)S(1)}, bf16[2,2,16,1024]{3,2,1,0:T(8,128)(2,1)S(1)}, u32[]{:S(2)}, u32[]{:S(2)}) collective-permute-start(bf16[2,2,16,1024]{3,2,1,0:T(8,128)(2,1)S(1)} %get-tuple-element.81), channel_id=1, source_target_pairs={{0,12},{4,8},{8,4},{12,0},{1,13},{5,9},{9,5},{13,1},{2,14},{6,10},... | collective-permute-start | bytes 393224 | tf_op jit(solution)/shard_map/ppermute | solution.py:476
  94.4 7.5 %collective-permute-start.24 = (bf16[2,2,16,1024]{3,2,1,0:T(8,128)(2,1)S(1)}, bf16[2,2,16,1024]{3,2,1,0:T(8,128)(2,1)S(1)}, u32[]{:S(2)}, u32[]{:S(2)}) collective-permute-start(bf16[2,2,16,1024]{3,2,1,0:T(8,128)(2,1)S(1)} %get-tuple-element.82), channel_id=1, source_target_pairs={{0,4},{4,0},{8,12},{12,8},{1,5},{5,1},{9,13},{13,9},{2,6},{6,2},{1... | collective-permute-start | bytes 393224 | tf_op jit(solution)/shard_map/ppermute | solution.py:476
  103.0 10.4 %collective-permute-start.25 = (bf16[2,2,16,1024]{3,2,1,0:T(8,128)(2,1)S(1)}, bf16[2,2,16,1024]{3,2,1,0:T(8,128)(2,1)S(1)}, u32[]{:S(2)}, u32[]{:S(2)}) collective-permute-start(bf16[2,2,16,1024]{3,2,1,0:T(8,128)(2,1)S(1)} %get-tuple-element.84), channel_id=1, source_target_pairs={{0,8},{4,12},{8,0},{12,4},{1,9},{5,13},{9,1},{13,5},{2,10},{6,14},... | collective-permute-start | bytes 393224 | tf_op jit(solution)/shard_map/ppermute | solution.py:476
  104.4 9.0 %collective-permute-start.26 = (bf16[2,2,16,1024]{3,2,1,0:T(8,128)(2,1)S(1)}, bf16[2,2,16,1024]{3,2,1,0:T(8,128)(2,1)S(1)}, u32[]{:S(2)}, u32[]{:S(2)}) collective-permute-start(bf16[2,2,16,1024]{3,2,1,0:T(8,128)(2,1)S(1)} %get-tuple-element.85), channel_id=1, source_target_pairs={{0,12},{4,8},{8,4},{12,0},{1,13},{5,9},{9,5},{13,1},{2,14},{6,10},... | collective-permute-start | bytes 393224 | tf_op jit(solution)/shard_map/ppermute | solution.py:476
  107.4 6.9 %collective-permute-start.27 = (bf16[2,2,16,1024]{3,2,1,0:T(8,128)(2,1)S(1)}, bf16[2,2,16,1024]{3,2,1,0:T(8,128)(2,1)S(1)}, u32[]{:S(2)}, u32[]{:S(2)}) collective-permute-start(bf16[2,2,16,1024]{3,2,1,0:T(8,128)(2,1)S(1)} %get-tuple-element.86), channel_id=1, source_target_pairs={{0,4},{4,0},{8,12},{12,8},{1,5},{5,1},{9,13},{13,9},{2,6},{6,2},{1... | collective-permute-start | bytes 393224 | tf_op jit(solution)/shard_map/ppermute | solution.py:476
  115.0 5.0 %collective-permute-start.28 = (bf16[2,2,64,256]{3,2,1,0:T(8,128)(2,1)S(1)}, bf16[2,2,64,256]{3,2,1,0:T(8,128)(2,1)S(1)}, u32[]{:S(2)}, u32[]{:S(2)}) collective-permute-start(bf16[2,2,64,256]{3,2,1,0:T(8,128)(2,1)S(1)} %get-tuple-element.88), channel_id=1, source_target_pairs={{0,2},{2,0},{1,3},{3,1},{4,6},{6,4},{5,7},{7,5},{8,10},{10,8},{9,1... | collective-permute-start | bytes 393224 | tf_op jit(solution)/shard_map/ppermute | solution.py:476
  120.1 9.9 %collective-permute-start.29 = (bf16[2,2,64,256]{3,2,1,0:T(8,128)(2,1)S(1)}, bf16[2,2,64,256]{3,2,1,0:T(8,128)(2,1)S(1)}, u32[]{:S(2)}, u32[]{:S(2)}) collective-permute-start(bf16[2,2,64,256]{3,2,1,0:T(8,128)(2,1)S(1)} %shard_map.96.rest_0_), channel_id=1, source_target_pairs={{0,8},{4,12},{8,0},{12,4},{1,9},{5,13},{9,1},{13,5},{2,10},{6,14},... | collective-permute-start | bytes 393224 | tf_op jit(solution)/shard_map/ppermute | solution.py:476
  122.2 7.8 %collective-permute-start.30 = (bf16[2,2,64,256]{3,2,1,0:T(8,128)(2,1)S(1)}, bf16[2,2,64,256]{3,2,1,0:T(8,128)(2,1)S(1)}, u32[]{:S(2)}, u32[]{:S(2)}) collective-permute-start(bf16[2,2,64,256]{3,2,1,0:T(8,128)(2,1)S(1)} %shard_map.96.rest_0_), channel_id=1, source_target_pairs={{0,12},{4,8},{8,4},{12,0},{1,13},{5,9},{9,5},{13,1},{2,14},{6,10},... | collective-permute-start | bytes 393224 | tf_op jit(solution)/shard_map/ppermute | solution.py:476
  123.5 7.2 %collective-permute-start.31 = (bf16[2,2,64,256]{3,2,1,0:T(8,128)(2,1)S(1)}, bf16[2,2,64,256]{3,2,1,0:T(8,128)(2,1)S(1)}, u32[]{:S(2)}, u32[]{:S(2)}) collective-permute-start(bf16[2,2,64,256]{3,2,1,0:T(8,128)(2,1)S(1)} %shard_map.96.rest_0_), channel_id=1, source_target_pairs={{0,4},{4,0},{8,12},{12,8},{1,5},{5,1},{9,13},{13,9},{2,6},{6,2},{1... | collective-permute-start | bytes 393224 | tf_op jit(solution)/shard_map/ppermute | solution.py:476
  (8 other events, 196.6 us)

commit v11 on v10

--- a/solution.py
+++ b/solution.py
@@ -12,7 +12,8 @@
 BLOCK = 128
 ITERS = 2
 ROWS = 8
-CHUNKS = 1
+CHUNKS = 2
+PARTS = 2
 VMEM_BYTES = 6 * 1024 * 1024
 
 BF16 = jnp.bfloat16
@@ -39,24 +40,14 @@
     return np.stack([np.cos(angle), -np.sin(angle)])
 
 
-def forward_tables(samples, freq_devs, per_dev):
-    table = fields(samples, freq_devs * per_dev)
+def inverse_tables(samples, freq_devs, per_dev):
+    exact = fields(samples, freq_devs * per_dev) * (2.0 / samples)
     own = samples // freq_devs
     out = []
     for place in range(freq_devs):
-        part = [table[c, j, place * own : (place + 1) * own] for c, j in field_rows(place, freq_devs, per_dev)]
-        out.append(np.repeat(np.stack(part), ROWS, 0))
+        part = [exact[c, j, place * own : (place + 1) * own] for c, j in field_rows(place, freq_devs, per_dev)]
+        out.append(np.repeat(np.stack(part), ROWS, 0).T)
     return np.stack(out).astype(np.float32).astype(BF16)
-
-
-def inverse_tables(samples, freq_devs, per_dev):
-    out = forward_tables(samples, freq_devs, per_dev).astype(np.float32)
-    exact = fields(samples, freq_devs * per_dev) * (2.0 / samples)
-    own = samples // freq_devs
-    for place in range(freq_devs):
-        part = [exact[c, j, place * own : (place + 1) * own] for c, j in field_rows(place, freq_devs, per_dev)]
-        out[place] = np.repeat(np.stack(part), ROWS, 0)
-    return np.swapaxes(out, 1, 2).astype(BF16)
 
 
 def window_tables(samples, freq_devs, per_dev):
@@ -105,47 +96,50 @@
     return pl.BlockSpec(array.shape, lambda *_: zeros)
 
 
-def masked_halves(response, aperture, places):
-    per_dev, _, src, rcv = response.shape
-    half = src // 2
-    steps = half // BLOCK
-
-    def body(_, rblk, __, flags, x_ref, *outs):
-        lane = lax.broadcasted_iota(jnp.int32, (1, rcv), 1) // BLOCK
-        for flip in (1, 0):
-            for j in range(per_dev):
-                out = outs[flip * per_dev + j]
-                for step in range(steps):
-                    block = (rblk[0] ^ flip) * steps + step
-                    on = flags[j, pl.ds(block, 1), :].astype(F32)
-                    row = sum(jnp.where(lane == r, on[:, r : r + 1], 0.0) for r in range(rcv // BLOCK))
-                    gate = jnp.broadcast_to(row, (BLOCK, rcv)).astype(BF16)
-                    rows = pl.ds(pl.multiple_of(block * BLOCK, BLOCK), BLOCK)
-                    to = slice(step * BLOCK, (step + 1) * BLOCK)
-                    for c in range(2):
-                        out[to, c * rcv : (c + 1) * rcv] = x_ref[j, c, rows, :] * gate
-
-    shape = jax.ShapeDtypeStruct((half, 2 * rcv), BF16)
-    inputs = [(v, whole(v)) for v in (aperture, response)]
-    outs = call(body, places, inputs, [(shape, whole(shape))] * (2 * per_dev), (1,))
-    return outs[:per_dev], outs[per_dev:]
-
-
-def first_spectra(initial, table, freq_place, freq_devs, per_dev, first, rows):
-    own, rcv = initial.shape[1:]
+def sine_terms():
+    square = (np.cos(np.linspace(0.0, math.pi, 200)) + 1.0) / 32.0
+    y = np.sqrt(np.maximum(square, 1e-12))
+    return [float(v) for v in np.polynomial.polynomial.polyfit(square, np.sin(2.0 * math.pi * y) / y, 6)]
+
+
+def turned(turn):
+    terms = sine_terms()
+
+    def sine(y):
+        square = y * y
+        total = jnp.full_like(y, terms[-1])
+        for term in terms[-2::-1]:
+            total = total * square + term
+        return total * y
+
+    turn = turn - jnp.floor(turn + 0.5)
+    size = jnp.abs(turn)
+    folded = jnp.where(size > 0.25, jnp.where(turn > 0.0, 0.5, -0.5) - turn, turn)
+    return sine(0.25 - size), sine(folded)
+
+
+def first_spectra(initial, places, freq_devs, per_dev):
+    rows, own, rcv = initial.shape
+    samples = own * freq_devs
     tile = 2 * ROWS
-    count = table.shape[1]
-
-    def body(place_ref, x_ref, t_ref, *rest):
+    count = freq_devs * 2 * per_dev * ROWS
+
+    def body(freq, rblk, sblk, x_ref, *rest):
         outs, spread_ref = rest[:freq_devs], rest[freq_devs]
-        base = t_ref[place_ref[0]].astype(F32)
+        time = lax.broadcasted_iota(jnp.int32, (ROWS, own), 1) + freq[0] * own
+        time = time.astype(F32) * (1.0 / samples)
+        table = []
+        for way in ways(freq_devs):
+            waves = [turned(time * ((freq[0] ^ way) * per_dev + j + 1).astype(F32)) for j in range(per_dev)]
+            table += [cosine for cosine, _ in waves] + [-sine for _, sine in waves]
+        table = jnp.concatenate(table, 0)
         lane = lax.broadcasted_iota(jnp.int32, (count, own), 0) % ROWS
         for row in range(ROWS):
-            spread_ref[:, row * own : (row + 1) * own] = jnp.where(lane == row, base, 0.0).astype(BF16)
+            spread_ref[:, row * own : (row + 1) * own] = jnp.where(lane == row, table, 0.0).astype(BF16)
         for at in range(rows // tile):
             parts = []
             for half in range(2):
-                start = first + at * tile + half * ROWS
+                start = at * tile + half * ROWS
                 flat = x_ref[start : start + ROWS].reshape(ROWS * own, rcv)
                 value = jnp.dot(spread_ref[...], flat, preferred_element_type=F32)
                 parts.append(value.reshape(freq_devs, 2, per_dev, ROWS, rcv))
@@ -156,13 +150,39 @@
     shape = jax.ShapeDtypeStruct((2, per_dev, rows, rcv), BF16)
     return call(
         body,
-        (freq_place,),
-        [(initial, whole(initial)), (table, whole(table))],
+        places,
+        [(initial, whole(initial))],
         [(shape, whole(shape))] * freq_devs,
         (1,),
         scratch=[pltpu.VMEM((count, ROWS * own), BF16)],
         flops=2 * 2 * freq_devs * per_dev * own * rows * rcv,
     )
+
+
+def masked_halves(response, aperture, places, after):
+    per_dev, _, src, rcv = response.shape
+    half = src // 2
+    width = half // PARTS
+
+    def body(_, rblk, __, flags, x_ref, ___, *outs):
+        lane = lax.broadcasted_iota(jnp.int32, (1, rcv), 1) // BLOCK
+        for flip in (1, 0):
+            for j in range(per_dev):
+                for step in range(half // BLOCK):
+                    block = (rblk[0] ^ flip) * (half // BLOCK) + step
+                    on = flags[j, pl.ds(block, 1), :].astype(F32)
+                    row = sum(jnp.where(lane == r, on[:, r : r + 1], 0.0) for r in range(rcv // BLOCK))
+                    gate = jnp.broadcast_to(row, (BLOCK, rcv)).astype(BF16)
+                    rows = pl.ds(pl.multiple_of(block * BLOCK, BLOCK), BLOCK)
+                    part, at = divmod(step * BLOCK, width)
+                    out = outs[flip * PARTS + part]
+                    for c in range(2):
+                        out[j, at : at + BLOCK, c * rcv : (c + 1) * rcv] = x_ref[j, c, rows, :] * gate
+
+    shape = jax.ShapeDtypeStruct((per_dev, width, 2 * rcv), BF16)
+    inputs = [(v, whole(v)) for v in (aperture, response)] + [(after, pl.BlockSpec(memory_space=pl.ANY))]
+    outs = call(body, places, inputs, [(shape, whole(shape))] * (2 * PARTS), (1,))
+    return list(outs[:PARTS]), list(outs[PARTS:])
 
 
 def summed(parts):
@@ -184,68 +204,54 @@
     return out
 
 
-def src_onsets(onset, places, half_rows, first, share, width):
+def src_onsets(onset, places, half_rows, share, width):
+    group = half_rows // CHUNKS
+
     def body(freq, rblk, sblk, o_ref, own, other):
         lanes = pl.ds(pl.multiple_of(rblk[0] * width, BLOCK), width)
         for core, out in ((sblk[0], own), (1 - sblk[0], other)):
-            spot = pl.multiple_of(core * half_rows + first + freq[0] * share, ROWS)
-            out[...] = o_ref[pl.ds(spot, share), lanes]
-
-    shape = jax.ShapeDtypeStruct((share, width), onset.dtype)
+            for chunk in range(CHUNKS):
+                spot = pl.multiple_of(core * half_rows + chunk * group + freq[0] * share, ROWS)
+                out[chunk * share : (chunk + 1) * share] = o_ref[pl.ds(spot, share), lanes]
+
+    shape = jax.ShapeDtypeStruct((CHUNKS * share, width), onset.dtype)
     return call(body, places, [(onset, whole(onset))], [(shape, whole(shape))] * 2, (1,))
 
 
-def sine_terms():
-    square = (np.cos(np.linspace(0.0, math.pi, 200)) + 1.0) / 32.0
-    y = np.sqrt(np.maximum(square, 1e-12))
-    return [float(v) for v in np.polynomial.polynomial.polyfit(square, np.sin(2.0 * math.pi * y) / y, 6)]
-
-
-def phase_tables(onsets, places, freq_devs, per_dev, samples, rows=None, first=0, half_rows=0):
-    terms = sine_terms()
+def phase_tables(onsets, places, freq_devs, per_dev, samples, parts=1, rows=None):
     count = rows or onsets[0].shape[0]
-    widths = [v.shape[1] for v in onsets]
-
-    def sine(y):
-        square = y * y
-        total = jnp.full_like(y, terms[-1])
-        for term in terms[-2::-1]:
-            total = total * square + term
-        return total * y
+    width = onsets[0].shape[1] // parts
 
     def body(freq, _, sblk, *refs):
         cosines, sines, fraction = refs[-3:]
-        at = 0
-        for ref, width in zip(refs, widths):
-            if rows:
-                value = ref[pl.ds(pl.multiple_of(sblk[0] * half_rows + first, ROWS), rows), :]
-            else:
-                value = ref[...]
-            part = value.astype(F32) * (1.0 / samples)
-            to = slice(at, at + width)
-            fraction[:, to] = part
-            for step, way in enumerate(ways(freq_devs)):
-                for j in range(per_dev):
-                    order = ((freq[0] ^ way) * per_dev + j + 1).astype(F32)
-                    turn = part * order
-                    turn = turn - jnp.floor(turn + 0.5)
-                    size = jnp.abs(turn)
-                    folded = jnp.where(size > 0.25, jnp.where(turn > 0.0, 0.5, -0.5) - turn, turn)
-                    cosines[step, j, :, to] = sine(0.25 - size)
-                    sines[step, j, :, to] = sine(folded)
-            at += width
-
-    table = jax.ShapeDtypeStruct((freq_devs, per_dev, count, sum(widths)), F32)
-    shapes = [table, table, jax.ShapeDtypeStruct((count, sum(widths)), F32)]
+        for part in range(parts):
+            for spot, ref in enumerate(refs[: len(onsets)]):
+                here = slice(part * width, (part + 1) * width)
+                if rows:
+                    value = ref[pl.ds(pl.multiple_of(sblk[0] * rows, ROWS), rows), here]
+                else:
+                    value = ref[:, here]
+                value = value.astype(F32) * (1.0 / samples)
+                at = (part * len(onsets) + spot) * width
+                to = slice(at, at + width)
+                fraction[:, to] = value
+                for step, way in enumerate(ways(freq_devs)):
+                    for j in range(per_dev):
+                        order = ((freq[0] ^ way) * per_dev + j + 1).astype(F32)
+                        cosines[step, j, :, to], sines[step, j, :, to] = turned(value * order)
+
+    table = jax.ShapeDtypeStruct((freq_devs, per_dev, count, width * parts * len(onsets)), F32)
+    shapes = [table, table, jax.ShapeDtypeStruct(table.shape[2:], F32)]
     return call(body, places, [(v, whole(v)) for v in onsets], [(v, whole(v)) for v in shapes], (1,))
 
 
-def down_products(near, far, responses, freq_place, freq_devs):
+def down_products(near, far, parts, freq_place, freq_devs, groups):
     _, per_dev, rows, rcv = near.shape
-    flat = [v for by_half in responses for pair in by_half for v in pair]
-    width = flat[0].shape[0]
-    tile = min(width, 256)
-    share = rows // freq_devs
+    flat = [v for part in parts for pair in part for v in pair]
+    width = flat[0].shape[1]
+    total_width = width * len(flat) // 2
+    group = rows // groups
+    share = group // freq_devs
 
     def body(place_ref, n_ref, f_ref, *rest):
         resp, outs, held = rest[: len(flat)], rest[len(flat) : -1], rest[-1]
@@ -254,30 +260,30 @@
             for ref in (n_ref, f_ref):
                 real, imag = ref[0, j], ref[1, j]
                 sides.append(jnp.concatenate([jnp.concatenate([real, -imag], 1), jnp.concatenate([imag, real], 1)], 0))
-            for half in range(2):
-                pair = resp[(j * 2 + half) * 2 : (j * 2 + half) * 2 + 2]
-                for at in range(width // tile):
-                    cut = slice(at * tile, (at + 1) * tile)
-                    total = sum(
-                        lax.dot_general(lhs, ref[cut], (((1,), (1,)), ((), ())), preferred_element_type=F32)
-                        for lhs, ref in zip(sides, pair)
-                    )
-                    to = slice(half * width + at * tile, half * width + (at + 1) * tile)
-                    held[0, j, :, to] = total[:rows]
-                    held[1, j, :, to] = total[rows:]
+            for at in range(len(flat) // 2):
+                total = sum(
+                    lax.dot_general(lhs, ref[j], (((1,), (1,)), ((), ())), preferred_element_type=F32)
+                    for lhs, ref in zip(sides, resp[2 * at : 2 * at + 2])
+                )
+                to = slice(at * width, (at + 1) * width)
+                held[0, j, :, to] = total[:rows]
+                held[1, j, :, to] = total[rows:]
         for way, out in zip(ways(freq_devs), outs):
-            start = pl.multiple_of((place_ref[0] ^ way) * share, share)
-            out[...] = held[:, :, pl.ds(start, share), :].astype(BF16)
-
-    shape = jax.ShapeDtypeStruct((2, per_dev, share, 2 * width), BF16)
+            pieces = []
+            for index in range(groups):
+                start = pl.multiple_of(index * group + (place_ref[0] ^ way) * share, ROWS)
+                pieces.append(held[:, :, pl.ds(start, share), :])
+            out[...] = jnp.concatenate(pieces, 2).reshape(out.shape).astype(BF16)
+
+    shape = jax.ShapeDtypeStruct((2 * per_dev * groups * share, total_width), BF16)
     return call(
         body,
         (freq_place,),
         [(v, whole(v)) for v in (near, far, *flat)],
         [(shape, whole(shape))] * freq_devs,
         (1,),
-        scratch=[pltpu.VMEM((2, per_dev, rows, 2 * width), F32)],
-        flops=2 * 8 * per_dev * rows * 2 * width * rcv,
+        scratch=[pltpu.VMEM((2, per_dev, rows, total_width), F32)],
+        flops=2 * 8 * per_dev * rows * total_width * rcv,
     )
 
 
@@ -298,15 +304,16 @@
     return jnp.stack([real, imag])
 
 
-def tiles(width, body):
+def tiles(width, body, first=0):
     def at(step, carry):
-        body(pl.ds(pl.multiple_of(step * BLOCK, BLOCK), BLOCK))
+        here = pl.multiple_of(step * BLOCK, BLOCK)
+        body(pl.ds(here, BLOCK), pl.ds(pl.multiple_of(here + first, BLOCK), BLOCK))
         return carry
 
     lax.fori_loop(0, width // BLOCK, at, 0, unroll=2)
 
 
-def windowed(messages, tables, matrix, freq_place, per_dev, share):
+def windowed(messages, tables, matrix, freq_place, per_dev, share, first_row, first_lane):
     cosines, sines, fraction = tables
     freq_devs = len(messages)
     width = messages[0].shape[-1]
@@ -316,22 +323,22 @@
         refs, outs = rest[:freq_devs], rest[freq_devs:]
         matrix_here = g_ref[place_ref[0]]
 
-        def one(at):
-            data = [ref[:, :, :, at].astype(F32) for ref in refs]
+        def one(at, there):
+            data = [ref[:, at].astype(F32).reshape(2, per_dev, share, BLOCK) for ref in refs]
             made = [[] for _ in outs]
             for first in range(0, share, ROWS):
-                cut = slice(first, first + ROWS)
-                plain = [value[:, :, cut] for value in data]
-                cos = [c_ref[step, :, cut, at] for step in range(freq_devs)]
-                sin = [s_ref[step, :, cut, at] for step in range(freq_devs)]
+                cut = slice(first_row + first, first_row + first + ROWS)
+                plain = [value[:, :, first : first + ROWS] for value in data]
+                cos = [c_ref[step, :, cut, there] for step in range(freq_devs)]
+                sin = [s_ref[step, :, cut, there] for step in range(freq_devs)]
                 up, low = mixed_fields(plain, cos, sin, matrix_here)
-                part = f_ref[cut, at]
+                part = f_ref[cut, there]
                 for step in range(freq_devs):
                     made[step].append(unturned(up[step], low[step], plain[step], cos[step], sin[step], part))
             for out, value in zip(outs, made):
-                out[:, :, :, at] = jnp.concatenate(value, 2).astype(BF16)
-
-        tiles(width, one)
+                out[:, at] = jnp.concatenate(value, 2).reshape(out.shape[0], BLOCK).astype(BF16)
+
+        tiles(width, one, first_lane)
 
     inputs = (cosines, sines, fraction, matrix, *messages)
     return call(
@@ -344,48 +351,60 @@
     )
 
 
-def up_products(messages, responses, freq_place, rows):
-    freq_devs = len(messages)
-    flat = [v for by_half in responses for pair in by_half for v in pair]
-    src, rcv = flat[0].shape[0], flat[0].shape[1] // 2
-    _, per_dev, share, _ = messages[0].shape
+def up_products(by_part, parts, freq_place, rows, groups):
+    freq_devs = len(by_part[0])
+    flat = [v for part in parts for pair in part for v in pair]
+    per_dev, src, rcv = flat[0].shape[0], flat[0].shape[1], flat[0].shape[2] // 2
+    messages = [v for part in by_part for v in part]
+    group = rows // groups
+    share = group // freq_devs
+    total_width = src * len(flat) // 2
 
     def body(place_ref, *rest):
-        resp, refs = rest[: len(flat)], rest[len(flat) : len(flat) + freq_devs]
-        keep, send, held = rest[len(flat) + freq_devs :]
-        for way, ref in zip(ways(freq_devs), refs):
-            for part in range(2):
-                start = pl.multiple_of(part * rows + (place_ref[0] ^ way) * share, share)
-                held[:, pl.ds(start, share), :] = ref[part]
+        resp, refs = rest[: len(flat)], rest[len(flat) : len(flat) + len(messages)]
+        outs, held = rest[len(flat) + len(messages) : -1], rest[-1]
+        lane = 0
+        for part in range(len(by_part)):
+            to = slice(lane, lane + refs[part * freq_devs].shape[1])
+            lane = to.stop
+            for step, way in enumerate(ways(freq_devs)):
+                value = refs[part * freq_devs + step][...].astype(F32)
+                value = value.reshape(2, per_dev, groups, share, value.shape[1])
+                for index in range(groups):
+                    start = pl.multiple_of(index * group + (place_ref[0] ^ way) * share, ROWS)
+                    held[:, :, pl.ds(start, share), to] = value[:, :, index]
         for j in range(per_dev):
-            for side, out in ((1, send), (0, keep)):
+            both = [jnp.concatenate([held[0, j], held[1, j]], 0).astype(BF16)]
+            for side in (1, 0):
                 total = sum(
-                    jnp.dot(
-                        held[j, :, half * src : (half + 1) * src],
-                        resp[(j * 2 + half) * 2 + side][...],
-                        preferred_element_type=F32,
-                    )
-                    for half in range(2)
+                    jnp.dot(both[0][:, at * src : (at + 1) * src], resp[2 * at + side][j], preferred_element_type=F32)
+                    for at in range(len(flat) // 2)
                 )
-                out[0, j] = (total[:rows, :rcv] + total[rows:, rcv:]).astype(out.dtype)
-                out[1, j] = (total[rows:, :rcv] - total[:rows, rcv:]).astype(out.dtype)
-
-    shapes = [jax.ShapeDtypeStruct((2, per_dev, rows, rcv), kind) for kind in (F32, BF16)]
-    return call(
+                real = total[:rows, :rcv] + total[rows:, rcv:]
+                imag = total[rows:, :rcv] - total[:rows, rcv:]
+                for index in range(groups):
+                    out = outs[2 * index + side]
+                    cut = slice(index * group, (index + 1) * group)
+                    out[0, j] = real[cut].astype(out.dtype)
+                    out[1, j] = imag[cut].astype(out.dtype)
+
+    shapes = [jax.ShapeDtypeStruct((2, per_dev, group, rcv), kind) for kind in (F32, BF16)] * groups
+    outs = call(
         body,
         (freq_place,),
         [(v, whole(v)) for v in (*flat, *messages)],
         [(v, whole(v)) for v in shapes],
         (1,),
-        scratch=[pltpu.VMEM((per_dev, 2 * rows, 2 * src), BF16)],
-        flops=2 * 8 * per_dev * rows * 2 * src * rcv,
-    )
-
-
-def next_spectra(sums, messages, tables, matrix, freq_place):
+        scratch=[pltpu.VMEM((2, per_dev, rows, total_width), F32)],
+        flops=2 * 8 * per_dev * rows * total_width * rcv,
+    )
+    return [tuple(outs[2 * index : 2 * index + 2]) for index in range(groups)]
+
+
+def next_spectra(sums, messages, tables, matrix, freq_place, first_row):
     cosines, sines, fraction = tables
     freq_devs = len(messages)
-    _, per_dev, rows, rcv = sums.shape
+    _, per_dev, rows, rcv = messages[0].shape
     count = freq_devs * 2 * per_dev * ROWS
     own = 2 * per_dev * ROWS
 
@@ -393,28 +412,30 @@
         refs, out = rest[:freq_devs], rest[freq_devs]
         matrix_here = g_ref[place_ref[0], :own]
 
-        def one(at):
+        def one(at, _):
             for base in range(0, rows, 2 * ROWS):
                 pair = slice(base, base + 2 * ROWS)
                 data = [ref[:, :, pair, at].astype(F32) for ref in refs]
                 made = []
                 for half in range(2):
                     plain = [value[:, :, half * ROWS : (half + 1) * ROWS] for value in data]
-                    cut = slice(base + half * ROWS, base + (half + 1) * ROWS)
+                    cut = slice(first_row + base + half * ROWS, first_row + base + (half + 1) * ROWS)
                     cos = [c_ref[step, :, cut, at] for step in range(freq_devs)]
                     sin = [s_ref[step, :, cut, at] for step in range(freq_devs)]
                     up, low = mixed_fields(plain, cos, sin, matrix_here)
-                    made.append(unturned(up[0], low[0], plain[0], cos[0], sin[0], f_ref[cut, at]))
-                out[:, :, pair, at] = (u_ref[:, :, pair, at] - jnp.concatenate(made, 2)).astype(BF16)
+                    change = unturned(up[0], low[0], plain[0], cos[0], sin[0], f_ref[cut, at])
+                    made.append(u_ref[:, :, cut, at] - change)
+                out[:, :, pair, at] = jnp.concatenate(made, 2).astype(BF16)
 
         tiles(rcv, one)
 
     inputs = (sums, cosines, sines, fraction, matrix, *messages)
+    shape = jax.ShapeDtypeStruct(messages[0].shape, BF16)
     (out,) = call(
         body,
         (freq_place,),
         [(v, whole(v)) for v in inputs],
-        [(jax.ShapeDtypeStruct(sums.shape, BF16), whole(sums))],
+        [(shape, whole(shape))],
         (1,),
         flops=2 * own * count * 2 * rcv * rows // ROWS,
     )
@@ -492,50 +513,51 @@
     src_width = response.shape[2] // 2
     rows = half_rows // CHUNKS
     share = rows // freq_devs
-    freq_index = lax.axis_index("freq")
-    rblk_index = lax.axis_index("rblk")
-    sblk_index = lax.axis_index("sblk")
-    places = tuple(index.reshape(1) for index in (freq_index, rblk_index, sblk_index))
+    places = tuple(lax.axis_index(axis).reshape(1) for axis in ("freq", "rblk", "sblk"))
     freq_place = places[0]
-
-    kept, moved = masked_halves(response, aperture, places)
-    moved = [exchanged(v, "rblk", 1) for v in moved]
-    kept_pair = [exchanged(v, "sblk", 1) for v in kept]
-    responses = None
-    forward = jnp.asarray(forward_tables(samples, freq_devs, per_dev))
     inverse = jnp.asarray(inverse_tables(samples, freq_devs, per_dev))
     matrix = jnp.asarray(window_tables(samples, freq_devs, per_dev))
 
+    partial = first_spectra(initial, places, freq_devs, per_dev)
+    kept, sent = masked_halves(response, aperture, places, partial[0])
+    moved = exchanged(sent[0], "rblk", 1)
+    moved, partial = lax.optimization_barrier((moved, dealt_out(partial)))
+    sums, spectra = summed(partial)
+    far = exchanged(spectra, "rblk", 1)
+
+    own, other = src_onsets(onset_src, places, half_rows, share, src_width)
+    src_tables = phase_tables((own, exchanged(other, "sblk", 1)), places, freq_devs, per_dev, samples, PARTS)
+    rcv_tables = phase_tables((onset_rcv,), places, freq_devs, per_dev, samples, rows=half_rows)
+
+    parts, by_part = [], []
+    for index in range(PARTS):
+        if index:
+            sent[index], far = lax.optimization_barrier((sent[index], far))
+            moved = exchanged(sent[index], "rblk", 1)
+            received = dealt_out(messages)
+            moved, received[1:-1] = lax.optimization_barrier((moved, received[1:-1]))
+            by_part.append(received)
+        pair = tuple(exchanged(v, "sblk", 1) for v in (kept[index], moved))
+        parts.append(((kept[index], moved), pair))
+        messages = dealt_out(down_products(spectra, far, parts[index:], freq_place, freq_devs, CHUNKS))
+        lane = index * messages[0].shape[-1]
+        messages = windowed(messages, src_tables, matrix, freq_place, per_dev, share * CHUNKS, 0, lane)
+    by_part.append(dealt_out(messages))
+    sums_of = up_products(by_part, parts, freq_place, half_rows, CHUNKS)
+
     result = None
-    for chunk in range(CHUNKS):
+    for chunk, (keep, send) in enumerate(sums_of):
         first = chunk * rows
-        parts = first_spectra(initial, forward, freq_place, freq_devs, per_dev, first, rows)
-        sums, spectra = summed(dealt_out(parts))
-        far = exchanged(spectra, "rblk", 1)
-        if responses is None:
-            before, moved_pair = spectra, []
-            for at in range(per_dev):
-                moved[at], before = lax.optimization_barrier((moved[at], before))
-                spectra, far = (spectra, before) if at else (before, far)
-                moved_pair.append(exchanged(moved[at], "sblk", 1))
-                before = far
-            responses = [((kept[j], moved[j]), (kept_pair[j], moved_pair[j])) for j in range(per_dev)]
-
-        own, other = src_onsets(onset_src, places, half_rows, first, share, src_width)
-        src_tables = phase_tables((own, exchanged(other, "sblk", 1)), places, freq_devs, per_dev, samples)
-        rcv_tables = phase_tables((onset_rcv,), places, freq_devs, per_dev, samples, rows, first, half_rows)
-
-        for step in range(ITERS):
-            far = far if step == 0 else exchanged(spectra, "rblk", 1)
-            messages = dealt_out(down_products(spectra, far, responses, freq_place, freq_devs))
-            messages = windowed(messages, src_tables, matrix, freq_place, per_dev, share)
-            keep, send = up_products(dealt_out(messages), responses, freq_place, rows)
-            back = added(keep, exchanged(send, "rblk", 1))
-            messages = spread(back, freq_devs)
-            if step < ITERS - 1:
-                spectra = next_spectra(sums, messages, rcv_tables, matrix, freq_place)
-            else:
-                result = updated(initial, onset_rcv, messages, inverse, places, first, rows, result)
+        for _ in range(1, ITERS):
+            messages = spread(added(keep, exchanged(send, "rblk", 1)), freq_devs)
+            near = next_spectra(sums, messages, rcv_tables, matrix, freq_place, first)
+            messages = down_products(near, exchanged(near, "rblk", 1), parts, freq_place, freq_devs, 1)
+            messages = windowed(
+                dealt_out(messages), src_tables, matrix, freq_place, per_dev, share, chunk * share, 0
+            )
+            ((keep, send),) = up_products([dealt_out(messages)], parts, freq_place, rows, 1)
+        messages = spread(added(keep, exchanged(send, "rblk", 1)), freq_devs)
+        result = updated(initial, onset_rcv, messages, inverse, places, first, rows, result)
     return result
 
 
@@ -615,9 +637,8 @@
     freq_devs = lax.axis_size("freq")
     if lax.axis_size("rblk") != 2 or lax.axis_size("sblk") != 2 or freq_devs & (freq_devs - 1):
         return False
-    rows = initial.shape[0] // CHUNKS
-    whole_rows = initial.shape[0] % CHUNKS == 0 and rows % (2 * ROWS * freq_devs) == 0
-    whole_width = response.shape[2] % (4 * BLOCK) == 0 and response.shape[3] % BLOCK == 0
+    whole_rows = initial.shape[0] % (max(2, CHUNKS) * ROWS * freq_devs) == 0
+    whole_width = response.shape[2] % (2 * PARTS * BLOCK) == 0 and response.shape[3] % BLOCK == 0
     return whole_rows and whole_width and onset_rcv.shape[0] == 2 * initial.shape[0]
 
 

time: 134 us -> 134 us (level)
  waiting for transfers between devices: 75 us -> 50.1 us
  starting transfers between devices: 40.7 us -> 63.3 us
  Pallas kernels: 12.7 us -> 16.7 us
  local copies, waits for them, and re-layouts: 5.47 us -> 3.77 us
    ppermute x32 -> x53, waiting for transfers between devices: 75 us -> 50.1 us  [exchanged(): lax.ppermute(value, axis, [(i, i ^ step) for i in range(lax.axis_size(axi...]
    ppermute x32 -> x53, starting transfers between devices: 40.7 us -> 63.3 us  [exchanged(): lax.ppermute(value, axis, [(i, i ^ step) for i in range(lax.axis_size(axi...]
    pallas_call x16 -> x25, Pallas kernels: 12.7 us -> 16.7 us  [call(): pl.pallas_call(body, grid_spec=pltpu.PrefetchScalarGridSpec(num_scalar_pr...]
    unnamed x17 -> x15, local copies, waits for them, and re-layouts: 5.47 us -> 3.77 us
  transfers between devices with their start and end apart: 32 -> 53, of which waited for: 21 -> 24; matrix products, arithmetic and copies ran while one was open for 0% -> 0% of each run, Pallas kernels for 2% -> 9%
where the time goes in v11:
time: 134 us
  starting transfers between devices  63.3 us (47%)
  waiting for transfers between devices  50.1 us (37%)
  Pallas kernels  16.7 us (12%)
  local copies, waits for them, and re-layouts  3.77 us (3%)
    ppermute x53, starting transfers between devices, exchanged(): lax.ppermute(value, axis, [(i, i ^ step) for i in range(lax.axis_size(axi...  63.3 us
    ppermute x53, waiting for transfers between devices, exchanged(): lax.ppermute(value, axis, [(i, i ^ step) for i in range(lax.axis_size(axi...  50.1 us
    pallas_call x25, Pallas kernels, call(): pl.pallas_call(body, grid_spec=pltpu.PrefetchScalarGridSpec(num_scalar_pr...  16.7 us
    unnamed x15, local copies, waits for them, and re-layouts  3.77 us
  transfers between devices with their start and end apart: 53, of which 24 were waited for; matrix products, arithmetic and copies ran while one was open for 0% of the time, Pallas kernels for 9%

profile of v11, /device:TPU:0, one launch (start us, length us, event | category | flops | bytes accessed | tf_op | source)
XLA Modules:
  0.0 134.0 jit_solution(10834737143720792471)
XLA Ops:
  0.8 2.2 %copy-done = bf16[64,128,256]{2,1,0:T(8,128)(2,1)S(1)} copy-done((bf16[64,128,256]{2,1,0:T(8,128)(2,1)S(1)}, bf16[64,128,256]{2,1,0:T(8,128)(2,1)}, u32[]{:S(2)}) %copy-start) | copy-done | bytes 4194328
  4.8 3.0 %collective-permute-start = (bf16[2,256,512]{2,1,0:T(8,128)(2,1)S(1)}, bf16[2,256,512]{2,1,0:T(8,128)(2,1)S(1)}, u32[]{:S(2)}, u32[]{:S(2)}) collective-permute-start(bf16[2,256,512]{2,1,0:T(8,128)(2,1)S(1)} %get-tuple-element.75), channel_id=1, source_target_pairs={{0,2},{2,0},{1,3},{3,1},{4,6},{6,4},{5,7},{7,5},{8,10},{10,8},{9,1... | collective-permute-start | bytes 1572872 | tf_op jit(solution)/shard_map/ppermute | solution.py:497
  7.8 2.6 %collective-permute-start.1 = (bf16[2,2,64,256]{3,2,1,0:T(8,128)(2,1)S(1)}, bf16[2,2,64,256]{3,2,1,0:T(8,128)(2,1)S(1)}, u32[]{:S(2)}, u32[]{:S(2)}) collective-permute-start(bf16[2,2,64,256]{3,2,1,0:T(8,128)(2,1)S(1)} %get-tuple-element.76), channel_id=1, source_target_pairs={{0,8},{4,12},{8,0},{12,4},{1,9},{5,13},{9,1},{13,5},{2,10},{6,14},... | collective-permute-start | bytes 393224 | tf_op jit(solution)/shard_map/ppermute | solution.py:497
  11.9 8.5 %collective-permute-done.1.refs_1_ = bf16[2,2,64,256]{3,2,1,0:T(8,128)(2,1)S(1)} collective-permute-done((bf16[2,2,64,256]{3,2,1,0:T(8,128)(2,1)S(1)}, bf16[2,2,64,256]{3,2,1,0:T(8,128)(2,1)S(1)}, u32[]{:S(2)}, u32[]{:S(2)}) %collective-permute-start.1) | collective-permute-done | bytes 131104 | tf_op jit(solution)/shard_map/ppermute | solution.py:497
  21.6 5.1 %collective-permute-done.6.f_ref = bf16[2,2,64,256]{3,2,1,0:T(8,128)(2,1)S(1)} collective-permute-done((bf16[2,2,64,256]{3,2,1,0:T(8,128)(2,1)S(1)}, bf16[2,2,64,256]{3,2,1,0:T(8,128)(2,1)S(1)}, u32[]{:S(2)}, u32[]{:S(2)}) %collective-permute-start.6) | collective-permute-done | bytes 131104 | tf_op jit(solution)/shard_map/ppermute | solution.py:497
  28.3 3.8 %collective-permute-start.9 = (bf16[64,512]{1,0:T(8,128)(2,1)S(1)}, bf16[64,512]{1,0:T(8,128)(2,1)S(1)}, u32[]{:S(2)}, u32[]{:S(2)}) collective-permute-start(bf16[64,512]{1,0:T(8,128)(2,1)S(1)} %get-tuple-element.94), channel_id=1, source_target_pairs={{0,8},{4,12},{8,0},{12,4},{1,9},{5,13},{9,1},{13,5},{2,10},{6,14},... | collective-permute-start | bytes 196616 | tf_op jit(solution)/shard_map/ppermute | solution.py:497
  34.8 1.8 %collective-permute-done.9.rest_1_ = bf16[64,512]{1,0:T(8,128)(2,1)S(1)} collective-permute-done((bf16[64,512]{1,0:T(8,128)(2,1)S(1)}, bf16[64,512]{1,0:T(8,128)(2,1)S(1)}, u32[]{:S(2)}, u32[]{:S(2)}) %collective-permute-start.9) | collective-permute-done | bytes 65568 | tf_op jit(solution)/shard_map/ppermute | solution.py:497
  36.5 1.7 %collective-permute-done.10.rest_2_ = bf16[64,512]{1,0:T(8,128)(2,1)S(1)} collective-permute-done((bf16[64,512]{1,0:T(8,128)(2,1)S(1)}, bf16[64,512]{1,0:T(8,128)(2,1)S(1)}, u32[]{:S(2)}, u32[]{:S(2)}) %collective-permute-start.10) | collective-permute-done | bytes 65568 | tf_op jit(solution)/shard_map/ppermute | solution.py:497
  38.9 1.5 %collective-permute-start.12 = (bf16[64,512]{1,0:T(8,128)(2,1)S(1)}, bf16[64,512]{1,0:T(8,128)(2,1)S(1)}, u32[]{:S(2)}, u32[]{:S(2)}) collective-permute-start(bf16[64,512]{1,0:T(8,128)(2,1)S(1)} %get-tuple-element.97), channel_id=1, source_target_pairs={{0,8},{4,12},{8,0},{12,4},{1,9},{5,13},{9,1},{13,5},{2,10},{6,14},... | collective-permute-start | bytes 196616 | tf_op jit(solution)/shard_map/ppermute | solution.py:497
  41.4 3.6 %collective-permute-done.12.rest_9_ = bf16[64,512]{1,0:T(8,128)(2,1)S(1)} collective-permute-done((bf16[64,512]{1,0:T(8,128)(2,1)S(1)}, bf16[64,512]{1,0:T(8,128)(2,1)S(1)}, u32[]{:S(2)}, u32[]{:S(2)}) %collective-permute-start.12) | collective-permute-done | bytes 65568 | tf_op jit(solution)/shard_map/ppermute | solution.py:497
  46.5 1.9 %collective-permute-done.15.rest_3_.rest_7_ = bf16[2,256,512]{2,1,0:T(8,128)(2,1)S(1)} collective-permute-done((bf16[2,256,512]{2,1,0:T(8,128)(2,1)S(1)}, bf16[2,256,512]{2,1,0:T(8,128)(2,1)S(1)}, u32[]{:S(2)}, u32[]{:S(2)}) %collective-permute-start.15) | collective-permute-done | bytes 524320 | tf_op jit(solution)/shard_map/ppermute | solution.py:497
  53.5 2.7 %collective-permute-done.17.rest_1_ = bf16[64,512]{1,0:T(8,128)(2,1)S(1)} collective-permute-done((bf16[64,512]{1,0:T(8,128)(2,1)S(1)}, bf16[64,512]{1,0:T(8,128)(2,1)S(1)}, u32[]{:S(2)}, u32[]{:S(2)}) %collective-permute-start.17) | collective-permute-done | bytes 65568 | tf_op jit(solution)/shard_map/ppermute | solution.py:497
  59.4 1.9 %collective-permute-start.21 = (bf16[64,512]{1,0:T(8,128)(2,1)S(1)}, bf16[64,512]{1,0:T(8,128)(2,1)S(1)}, u32[]{:S(2)}, u32[]{:S(2)}) collective-permute-start(bf16[64,512]{1,0:T(8,128)(2,1)S(1)} %get-tuple-element.115), channel_id=1, source_target_pairs={{0,12},{4,8},{8,4},{12,0},{1,13},{5,9},{9,5},{13,1},{2,14},{6,10},... | collective-permute-start | bytes 196616 | tf_op jit(solution)/shard_map/ppermute | solution.py:497
  62.0 4.5 %collective-permute-done.20.rest_13_ = bf16[64,512]{1,0:T(8,128)(2,1)S(1)} collective-permute-done((bf16[64,512]{1,0:T(8,128)(2,1)S(1)}, bf16[64,512]{1,0:T(8,128)(2,1)S(1)}, u32[]{:S(2)}, u32[]{:S(2)}) %collective-permute-start.20) | collective-permute-done | bytes 65568 | tf_op jit(solution)/shard_map/ppermute | solution.py:497
  67.5 2.3 %collective-permute-start.38 = (bf16[2,2,32,256]{3,2,1,0:T(8,128)(2,1)S(1)}, bf16[2,2,32,256]{3,2,1,0:T(8,128)(2,1)S(1)}, u32[]{:S(2)}, u32[]{:S(2)}) collective-permute-start(bf16[2,2,32,256]{3,2,1,0:T(8,128)(2,1)S(1)} %get-tuple-element.130), channel_id=1, source_target_pairs={{0,2},{2,0},{1,3},{3,1},{4,6},{6,4},{5,7},{7,5},{8,10},{10,8},{9,1... | collective-permute-start | bytes 196616 | tf_op jit(solution)/shard_map/ppermute | solution.py:497
  69.9 2.7 %collective-permute-done.38.r_ref = bf16[2,2,32,256]{3,2,1,0:T(8,128)(2,1)S(1)} collective-permute-done((bf16[2,2,32,256]{3,2,1,0:T(8,128)(2,1)S(1)}, bf16[2,2,32,256]{3,2,1,0:T(8,128)(2,1)S(1)}, u32[]{:S(2)}, u32[]{:S(2)}) %collective-permute-start.38) | collective-permute-done | bytes 65568 | tf_op jit(solution)/shard_map/ppermute | solution.py:497
  73.4 1.7 %collective-permute-start.40 = (bf16[2,2,32,256]{3,2,1,0:T(8,128)(2,1)S(1)}, bf16[2,2,32,256]{3,2,1,0:T(8,128)(2,1)S(1)}, u32[]{:S(2)}, u32[]{:S(2)}) collective-permute-start(bf16[2,2,32,256]{3,2,1,0:T(8,128)(2,1)S(1)} %shard_map.90.rest_0_), channel_id=1, source_target_pairs={{0,12},{4,8},{8,4},{12,0},{1,13},{5,9},{9,5},{13,1},{2,14},{6,10},... | collective-permute-start | bytes 196616 | tf_op jit(solution)/shard_map/ppermute | solution.py:497
  76.2 1.7 %collective-permute-start.26 = (bf16[2,2,32,256]{3,2,1,0:T(8,128)(2,1)S(1)}, bf16[2,2,32,256]{3,2,1,0:T(8,128)(2,1)S(1)}, u32[]{:S(2)}, u32[]{:S(2)}) collective-permute-start(bf16[2,2,32,256]{3,2,1,0:T(8,128)(2,1)S(1)} %shard_map.84.rest_0_), channel_id=1, source_target_pairs={{0,4},{4,0},{8,12},{12,8},{1,5},{5,1},{9,13},{13,9},{2,6},{6,2},{1... | collective-permute-start | bytes 196616 | tf_op jit(solution)/shard_map/ppermute | solution.py:497
  77.9 1.7 %collective-permute-start.25 = (bf16[2,2,32,256]{3,2,1,0:T(8,128)(2,1)S(1)}, bf16[2,2,32,256]{3,2,1,0:T(8,128)(2,1)S(1)}, u32[]{:S(2)}, u32[]{:S(2)}) collective-permute-start(bf16[2,2,32,256]{3,2,1,0:T(8,128)(2,1)S(1)} %shard_map.84.rest_0_), channel_id=1, source_target_pairs={{0,12},{4,8},{8,4},{12,0},{1,13},{5,9},{9,5},{13,1},{2,14},{6,10},... | collective-permute-start | bytes 196616 | tf_op jit(solution)/shard_map/ppermute | solution.py:497
  80.5 4.7 %collective-permute-done.39.rest_1_ = bf16[2,2,32,256]{3,2,1,0:T(8,128)(2,1)S(1)} collective-permute-done((bf16[2,2,32,256]{3,2,1,0:T(8,128)(2,1)S(1)}, bf16[2,2,32,256]{3,2,1,0:T(8,128)(2,1)S(1)}, u32[]{:S(2)}, u32[]{:S(2)}) %collective-permute-start.39) | collective-permute-done | bytes 65568 | tf_op jit(solution)/shard_map/ppermute | solution.py:497
  85.4 1.8 %collective-permute-start.42 = (bf16[2,2,32,256]{3,2,1,0:T(8,128)(2,1)S(1)}, bf16[2,2,32,256]{3,2,1,0:T(8,128)(2,1)S(1)}, u32[]{:S(2)}, u32[]{:S(2)}) collective-permute-start(bf16[2,2,32,256]{3,2,1,0:T(8,128)(2,1)S(1)} %shard_map.91.n_ref), channel_id=1, source_target_pairs={{0,2},{2,0},{1,3},{3,1},{4,6},{6,4},{5,7},{7,5},{8,10},{10,8},{9,1... | collective-permute-start | bytes 196616 | tf_op jit(solution)/shard_map/ppermute | solution.py:497
  92.6 2.1 %collective-permute-start.45 = (bf16[32,1024]{1,0:T(8,128)(2,1)S(1)}, bf16[32,1024]{1,0:T(8,128)(2,1)S(1)}, u32[]{:S(2)}, u32[]{:S(2)}) collective-permute-start(bf16[32,1024]{1,0:T(8,128)(2,1)S(1)} %get-tuple-element.134), channel_id=1, source_target_pairs={{0,4},{4,0},{8,12},{12,8},{1,5},{5,1},{9,13},{13,9},{2,6},{6,2},{1... | collective-permute-start | bytes 196616 | tf_op jit(solution)/shard_map/ppermute | solution.py:497
  100.5 1.9 %collective-permute-start.46 = (bf16[32,1024]{1,0:T(8,128)(2,1)S(1)}, bf16[32,1024]{1,0:T(8,128)(2,1)S(1)}, u32[]{:S(2)}, u32[]{:S(2)}) collective-permute-start(bf16[32,1024]{1,0:T(8,128)(2,1)S(1)} %get-tuple-element.136), channel_id=1, source_target_pairs={{0,8},{4,12},{8,0},{12,4},{1,9},{5,13},{9,1},{13,5},{2,10},{6,14},... | collective-permute-start | bytes 196616 | tf_op jit(solution)/shard_map/ppermute | solution.py:497
  102.5 3.1 %collective-permute-start.47 = (bf16[32,1024]{1,0:T(8,128)(2,1)S(1)}, bf16[32,1024]{1,0:T(8,128)(2,1)S(1)}, u32[]{:S(2)}, u32[]{:S(2)}) collective-permute-start(bf16[32,1024]{1,0:T(8,128)(2,1)S(1)} %get-tuple-element.137), channel_id=1, source_target_pairs={{0,12},{4,8},{8,4},{12,0},{1,13},{5,9},{9,5},{13,1},{2,14},{6,10},... | collective-permute-start | bytes 196616 | tf_op jit(solution)/shard_map/ppermute | solution.py:497
  107.0 2.1 %collective-permute-start.31 = (bf16[32,1024]{1,0:T(8,128)(2,1)S(1)}, bf16[32,1024]{1,0:T(8,128)(2,1)S(1)}, u32[]{:S(2)}, u32[]{:S(2)}) collective-permute-start(bf16[32,1024]{1,0:T(8,128)(2,1)S(1)} %get-tuple-element.124), channel_id=1, source_target_pairs={{0,8},{4,12},{8,0},{12,4},{1,9},{5,13},{9,1},{13,5},{2,10},{6,14},... | collective-permute-start | bytes 196616 | tf_op jit(solution)/shard_map/ppermute | solution.py:497
  109.1 1.7 %collective-permute-start.32 = (bf16[32,1024]{1,0:T(8,128)(2,1)S(1)}, bf16[32,1024]{1,0:T(8,128)(2,1)S(1)}, u32[]{:S(2)}, u32[]{:S(2)}) collective-permute-start(bf16[32,1024]{1,0:T(8,128)(2,1)S(1)} %get-tuple-element.125), channel_id=1, source_target_pairs={{0,12},{4,8},{8,4},{12,0},{1,13},{5,9},{9,5},{13,1},{2,14},{6,10},... | collective-permute-start | bytes 196616 | tf_op jit(solution)/shard_map/ppermute | solution.py:497
  117.2 2.1 %collective-permute-start.34 = (bf16[2,2,32,256]{3,2,1,0:T(8,128)(2,1)S(1)}, bf16[2,2,32,256]{3,2,1,0:T(8,128)(2,1)S(1)}, u32[]{:S(2)}, u32[]{:S(2)}) collective-permute-start(bf16[2,2,32,256]{3,2,1,0:T(8,128)(2,1)S(1)} %get-tuple-element.128), channel_id=1, source_target_pairs={{0,2},{2,0},{1,3},{3,1},{4,6},{6,4},{5,7},{7,5},{8,10},{10,8},{9,1... | collective-permute-start | bytes 196616 | tf_op jit(solution)/shard_map/ppermute | solution.py:497
  119.5 3.0 %collective-permute-start.51 = (bf16[2,2,32,256]{3,2,1,0:T(8,128)(2,1)S(1)}, bf16[2,2,32,256]{3,2,1,0:T(8,128)(2,1)S(1)}, u32[]{:S(2)}, u32[]{:S(2)}) collective-permute-start(bf16[2,2,32,256]{3,2,1,0:T(8,128)(2,1)S(1)} %shard_map.95.rest_0_), channel_id=1, source_target_pairs={{0,12},{4,8},{8,4},{12,0},{1,13},{5,9},{9,5},{13,1},{2,14},{6,10},... | collective-permute-start | bytes 196616 | tf_op jit(solution)/shard_map/ppermute | solution.py:497
  124.0 2.9 %collective-permute-start.36 = (bf16[2,2,32,256]{3,2,1,0:T(8,128)(2,1)S(1)}, bf16[2,2,32,256]{3,2,1,0:T(8,128)(2,1)S(1)}, u32[]{:S(2)}, u32[]{:S(2)}) collective-permute-start(bf16[2,2,32,256]{3,2,1,0:T(8,128)(2,1)S(1)} %shard_map.89.rest_0_), channel_id=1, source_target_pairs={{0,12},{4,8},{8,4},{12,0},{1,13},{5,9},{9,5},{13,1},{2,14},{6,10},... | collective-permute-start | bytes 196616 | tf_op jit(solution)/shard_map/ppermute | solution.py:497
  128.0 1.9 %shard_map.96.rest_4_ = bf16[64,128,256]{2,1,0:T(8,128)(2,1)} custom-call(s32[1]{0:T(128)} %bitcast.freq._.place_ref, s32[1]{0:T(128)} %bitcast.1.rblk._, s32[1]{0:T(128)} %bitcast.2.sblk.__, bf16[64,128,256]{2,1,0:T(8,128)(2,1)S(1)} %copy-done.1, s32[128,256]{1,0:T(8,128)S(1)} %copy-done.4, bf16[4,128,128]{2,1,0:T(8,128)(2,1)S(1)} %copy-done.5, ...), custom_call_target="tpu_custom_call" | custom-call | flops 33554432 | bytes 8912896 | tf_op jit(solution)/shard_map/pallas_call | solution.py:78
  130.1 2.0 %collective-permute-done.35.rest_1_ = bf16[2,2,32,256]{3,2,1,0:T(8,128)(2,1)S(1)} collective-permute-done((bf16[2,2,32,256]{3,2,1,0:T(8,128)(2,1)S(1)}, bf16[2,2,32,256]{3,2,1,0:T(8,128)(2,1)S(1)}, u32[]{:S(2)}, u32[]{:S(2)}) %collective-permute-start.35) | collective-permute-done | bytes 65568 | tf_op jit(solution)/shard_map/ppermute | solution.py:497
  132.1 1.9 %shard_map.97 = bf16[64,128,256]{2,1,0:T(8,128)(2,1)} custom-call(s32[1]{0:T(128)} %bitcast.freq._.place_ref, s32[1]{0:T(128)} %bitcast.1.rblk._, s32[1]{0:T(128)} %bitcast.2.sblk.__, bf16[64,128,256]{2,1,0:T(8,128)(2,1)S(1)} %copy-done.1, s32[128,256]{1,0:T(8,128)S(1)} %copy-done.4, ...), custom_call_target="tpu_custom_call", output_to_operand_aliasing={{}: (10, {})} | custom-call | flops 33554432 | bytes 13107200 | tf_op jit(solution)/shard_map/pallas_call | solution.py:78
  (114 shorter events, 47.5 us)
Async XLA Ops:
  4.8 15.8 %collective-permute-start = (bf16[2,256,512]{2,1,0:T(8,128)(2,1)S(1)}, bf16[2,256,512]{2,1,0:T(8,128)(2,1)S(1)}, u32[]{:S(2)}, u32[]{:S(2)}) collective-permute-start(bf16[2,256,512]{2,1,0:T(8,128)(2,1)S(1)} %get-tuple-element.75), channel_id=1, source_target_pairs={{0,2},{2,0},{1,3},{3,1},{4,6},{6,4},{5,7},{7,5},{8,10},{10,8},{9,1... | collective-permute-start | bytes 1572872 | tf_op jit(solution)/shard_map/ppermute | solution.py:497
  7.8 12.6 %collective-permute-start.1 = (bf16[2,2,64,256]{3,2,1,0:T(8,128)(2,1)S(1)}, bf16[2,2,64,256]{3,2,1,0:T(8,128)(2,1)S(1)}, u32[]{:S(2)}, u32[]{:S(2)}) collective-permute-start(bf16[2,2,64,256]{3,2,1,0:T(8,128)(2,1)S(1)} %get-tuple-element.76), channel_id=1, source_target_pairs={{0,8},{4,12},{8,0},{12,4},{1,9},{5,13},{9,1},{13,5},{2,10},{6,14},... | collective-permute-start | bytes 393224 | tf_op jit(solution)/shard_map/ppermute | solution.py:497
  10.4 10.1 %collective-permute-start.2 = (bf16[2,2,64,256]{3,2,1,0:T(8,128)(2,1)S(1)}, bf16[2,2,64,256]{3,2,1,0:T(8,128)(2,1)S(1)}, u32[]{:S(2)}, u32[]{:S(2)}) collective-permute-start(bf16[2,2,64,256]{3,2,1,0:T(8,128)(2,1)S(1)} %get-tuple-element.77), channel_id=1, source_target_pairs={{0,12},{4,8},{8,4},{12,0},{1,13},{5,9},{9,5},{13,1},{2,14},{6,10},... | collective-permute-start | bytes 393224 | tf_op jit(solution)/shard_map/ppermute | solution.py:497
  11.7 8.9 %collective-permute-start.3 = (bf16[2,2,64,256]{3,2,1,0:T(8,128)(2,1)S(1)}, bf16[2,2,64,256]{3,2,1,0:T(8,128)(2,1)S(1)}, u32[]{:S(2)}, u32[]{:S(2)}) collective-permute-start(bf16[2,2,64,256]{3,2,1,0:T(8,128)(2,1)S(1)} %get-tuple-element.78), channel_id=1, source_target_pairs={{0,4},{4,0},{8,12},{12,8},{1,5},{5,1},{9,13},{13,9},{2,6},{6,2},{1... | collective-permute-start | bytes 393224 | tf_op jit(solution)/shard_map/ppermute | solution.py:497
  11.9 15.6 %collective-permute-start.4 = (bf16[2,256,512]{2,1,0:T(8,128)(2,1)S(1)}, bf16[2,256,512]{2,1,0:T(8,128)(2,1)S(1)}, u32[]{:S(2)}, u32[]{:S(2)}) collective-permute-start(bf16[2,256,512]{2,1,0:T(8,128)(2,1)S(1)} %get-tuple-element.74.rest_0_), channel_id=1, source_target_pairs={{0,1},{1,0},{2,3},{3,2},{4,5},{5,4},{6,7},{7,6},{8,9},{9,8},{10,11... | collective-permute-start | bytes 1572872 | tf_op jit(solution)/shard_map/ppermute | solution.py:497
  20.6 6.9 %collective-permute-start.5 = (bf16[2,256,512]{2,1,0:T(8,128)(2,1)S(1)}, bf16[2,256,512]{2,1,0:T(8,128)(2,1)S(1)}, u32[]{:S(2)}, u32[]{:S(2)}) collective-permute-start(bf16[2,256,512]{2,1,0:T(8,128)(2,1)S(1)} %collective-permute-done.rest_1_), channel_id=1, source_target_pairs={{0,1},{1,0},{2,3},{3,2},{4,5},{5,4},{6,7},{7,6},{8,9},{9,8},{10,11... | collective-permute-start | bytes 1572872 | tf_op jit(solution)/shard_map/ppermute | solution.py:497
  26.7 14.7 %collective-permute-start.7 = (bf16[2,256,512]{2,1,0:T(8,128)(2,1)S(1)}, bf16[2,256,512]{2,1,0:T(8,128)(2,1)S(1)}, u32[]{:S(2)}, u32[]{:S(2)}) collective-permute-start(bf16[2,256,512]{2,1,0:T(8,128)(2,1)S(1)} %get-tuple-element.87), channel_id=1, source_target_pairs={{0,2},{2,0},{1,3},{3,1},{4,6},{6,4},{5,7},{7,5},{8,10},{10,8},{9,1... | collective-permute-start | bytes 1572872 | tf_op jit(solution)/shard_map/ppermute | solution.py:497
  28.3 8.2 %collective-permute-start.9 = (bf16[64,512]{1,0:T(8,128)(2,1)S(1)}, bf16[64,512]{1,0:T(8,128)(2,1)S(1)}, u32[]{:S(2)}, u32[]{:S(2)}) collective-permute-start(bf16[64,512]{1,0:T(8,128)(2,1)S(1)} %get-tuple-element.94), channel_id=1, source_target_pairs={{0,8},{4,12},{8,0},{12,4},{1,9},{5,13},{9,1},{13,5},{2,10},{6,14},... | collective-permute-start | bytes 196616 | tf_op jit(solution)/shard_map/ppermute | solution.py:497
  49.2 7.0 %collective-permute-start.17 = (bf16[64,512]{1,0:T(8,128)(2,1)S(1)}, bf16[64,512]{1,0:T(8,128)(2,1)S(1)}, u32[]{:S(2)}, u32[]{:S(2)}) collective-permute-start(bf16[64,512]{1,0:T(8,128)(2,1)S(1)} %get-tuple-element.110), channel_id=1, source_target_pairs={{0,8},{4,12},{8,0},{12,4},{1,9},{5,13},{9,1},{13,5},{2,10},{6,14},... | collective-permute-start | bytes 196616 | tf_op jit(solution)/shard_map/ppermute | solution.py:497
  52.8 9.2 %collective-permute-start.16 = (bf16[64,512]{1,0:T(8,128)(2,1)S(1)}, bf16[64,512]{1,0:T(8,128)(2,1)S(1)}, u32[]{:S(2)}, u32[]{:S(2)}) collective-permute-start(bf16[64,512]{1,0:T(8,128)(2,1)S(1)} %get-tuple-element.107), channel_id=1, source_target_pairs={{0,4},{4,0},{8,12},{12,8},{1,5},{5,1},{9,13},{13,9},{2,6},{6,2},{1... | collective-permute-start | bytes 196616 | tf_op jit(solution)/shard_map/ppermute | solution.py:497
  58.4 8.0 %collective-permute-start.20 = (bf16[64,512]{1,0:T(8,128)(2,1)S(1)}, bf16[64,512]{1,0:T(8,128)(2,1)S(1)}, u32[]{:S(2)}, u32[]{:S(2)}) collective-permute-start(bf16[64,512]{1,0:T(8,128)(2,1)S(1)} %get-tuple-element.114), channel_id=1, source_target_pairs={{0,8},{4,12},{8,0},{12,4},{1,9},{5,13},{9,1},{13,5},{2,10},{6,14},... | collective-permute-start | bytes 196616 | tf_op jit(solution)/shard_map/ppermute | solution.py:497
  59.4 7.0 %collective-permute-start.21 = (bf16[64,512]{1,0:T(8,128)(2,1)S(1)}, bf16[64,512]{1,0:T(8,128)(2,1)S(1)}, u32[]{:S(2)}, u32[]{:S(2)}) collective-permute-start(bf16[64,512]{1,0:T(8,128)(2,1)S(1)} %get-tuple-element.115), channel_id=1, source_target_pairs={{0,12},{4,8},{8,4},{12,0},{1,13},{5,9},{9,5},{13,1},{2,14},{6,10},... | collective-permute-start | bytes 196616 | tf_op jit(solution)/shard_map/ppermute | solution.py:497
  72.6 7.0 %collective-permute-start.41 = (bf16[2,2,32,256]{3,2,1,0:T(8,128)(2,1)S(1)}, bf16[2,2,32,256]{3,2,1,0:T(8,128)(2,1)S(1)}, u32[]{:S(2)}, u32[]{:S(2)}) collective-permute-start(bf16[2,2,32,256]{3,2,1,0:T(8,128)(2,1)S(1)} %shard_map.90.rest_0_), channel_id=1, source_target_pairs={{0,4},{4,0},{8,12},{12,8},{1,5},{5,1},{9,13},{13,9},{2,6},{6,2},{1... | collective-permute-start | bytes 196616 | tf_op jit(solution)/shard_map/ppermute | solution.py:497
  73.4 7.0 %collective-permute-start.40 = (bf16[2,2,32,256]{3,2,1,0:T(8,128)(2,1)S(1)}, bf16[2,2,32,256]{3,2,1,0:T(8,128)(2,1)S(1)}, u32[]{:S(2)}, u32[]{:S(2)}) collective-permute-start(bf16[2,2,32,256]{3,2,1,0:T(8,128)(2,1)S(1)} %shard_map.90.rest_0_), channel_id=1, source_target_pairs={{0,12},{4,8},{8,4},{12,0},{1,13},{5,9},{9,5},{13,1},{2,14},{6,10},... | collective-permute-start | bytes 196616 | tf_op jit(solution)/shard_map/ppermute | solution.py:497
  75.1 10.0 %collective-permute-start.39 = (bf16[2,2,32,256]{3,2,1,0:T(8,128)(2,1)S(1)}, bf16[2,2,32,256]{3,2,1,0:T(8,128)(2,1)S(1)}, u32[]{:S(2)}, u32[]{:S(2)}) collective-permute-start(bf16[2,2,32,256]{3,2,1,0:T(8,128)(2,1)S(1)} %shard_map.90.rest_0_), channel_id=1, source_target_pairs={{0,8},{4,12},{8,0},{12,4},{1,9},{5,13},{9,1},{13,5},{2,10},{6,14},... | collective-permute-start | bytes 196616 | tf_op jit(solution)/shard_map/ppermute | solution.py:497
  76.2 11.0 %collective-permute-start.26 = (bf16[2,2,32,256]{3,2,1,0:T(8,128)(2,1)S(1)}, bf16[2,2,32,256]{3,2,1,0:T(8,128)(2,1)S(1)}, u32[]{:S(2)}, u32[]{:S(2)}) collective-permute-start(bf16[2,2,32,256]{3,2,1,0:T(8,128)(2,1)S(1)} %shard_map.84.rest_0_), channel_id=1, source_target_pairs={{0,4},{4,0},{8,12},{12,8},{1,5},{5,1},{9,13},{13,9},{2,6},{6,2},{1... | collective-permute-start | bytes 196616 | tf_op jit(solution)/shard_map/ppermute | solution.py:497
  77.9 9.3 %collective-permute-start.25 = (bf16[2,2,32,256]{3,2,1,0:T(8,128)(2,1)S(1)}, bf16[2,2,32,256]{3,2,1,0:T(8,128)(2,1)S(1)}, u32[]{:S(2)}, u32[]{:S(2)}) collective-permute-start(bf16[2,2,32,256]{3,2,1,0:T(8,128)(2,1)S(1)} %shard_map.84.rest_0_), channel_id=1, source_target_pairs={{0,12},{4,8},{8,4},{12,0},{1,13},{5,9},{9,5},{13,1},{2,14},{6,10},... | collective-permute-start | bytes 196616 | tf_op jit(solution)/shard_map/ppermute | solution.py:497
  79.6 7.6 %collective-permute-start.24 = (bf16[2,2,32,256]{3,2,1,0:T(8,128)(2,1)S(1)}, bf16[2,2,32,256]{3,2,1,0:T(8,128)(2,1)S(1)}, u32[]{:S(2)}, u32[]{:S(2)}) collective-permute-start(bf16[2,2,32,256]{3,2,1,0:T(8,128)(2,1)S(1)} %shard_map.84.rest_0_), channel_id=1, source_target_pairs={{0,8},{4,12},{8,0},{12,4},{1,9},{5,13},{9,1},{13,5},{2,10},{6,14},... | collective-permute-start | bytes 196616 | tf_op jit(solution)/shard_map/ppermute | solution.py:497
  87.5 7.2 %collective-permute-start.27 = (bf16[2,2,32,256]{3,2,1,0:T(8,128)(2,1)S(1)}, bf16[2,2,32,256]{3,2,1,0:T(8,128)(2,1)S(1)}, u32[]{:S(2)}, u32[]{:S(2)}) collective-permute-start(bf16[2,2,32,256]{3,2,1,0:T(8,128)(2,1)S(1)} %shard_map.85.n_ref), channel_id=1, source_target_pairs={{0,2},{2,0},{1,3},{3,1},{4,6},{6,4},{5,7},{7,5},{8,10},{10,8},{9,1... | collective-permute-start | bytes 196616 | tf_op jit(solution)/shard_map/ppermute | solution.py:497
  91.2 7.4 %collective-permute-start.43 = (bf16[32,1024]{1,0:T(8,128)(2,1)S(1)}, bf16[32,1024]{1,0:T(8,128)(2,1)S(1)}, u32[]{:S(2)}, u32[]{:S(2)}) collective-permute-start(bf16[32,1024]{1,0:T(8,128)(2,1)S(1)} %get-tuple-element.132), channel_id=1, source_target_pairs={{0,8},{4,12},{8,0},{12,4},{1,9},{5,13},{9,1},{13,5},{2,10},{6,14},... | collective-permute-start | bytes 196616 | tf_op jit(solution)/shard_map/ppermute | solution.py:497
  91.2 8.5 %collective-permute-start.44 = (bf16[32,1024]{1,0:T(8,128)(2,1)S(1)}, bf16[32,1024]{1,0:T(8,128)(2,1)S(1)}, u32[]{:S(2)}, u32[]{:S(2)}) collective-permute-start(bf16[32,1024]{1,0:T(8,128)(2,1)S(1)} %get-tuple-element.133), channel_id=1, source_target_pairs={{0,12},{4,8},{8,4},{12,0},{1,13},{5,9},{9,5},{13,1},{2,14},{6,10},... | collective-permute-start | bytes 196616 | tf_op jit(solution)/shard_map/ppermute | solution.py:497
  92.6 7.1 %collective-permute-start.45 = (bf16[32,1024]{1,0:T(8,128)(2,1)S(1)}, bf16[32,1024]{1,0:T(8,128)(2,1)S(1)}, u32[]{:S(2)}, u32[]{:S(2)}) collective-permute-start(bf16[32,1024]{1,0:T(8,128)(2,1)S(1)} %get-tuple-element.134), channel_id=1, source_target_pairs={{0,4},{4,0},{8,12},{12,8},{1,5},{5,1},{9,13},{13,9},{2,6},{6,2},{1... | collective-permute-start | bytes 196616 | tf_op jit(solution)/shard_map/ppermute | solution.py:497
  96.1 9.4 %collective-permute-start.28 = (bf16[32,1024]{1,0:T(8,128)(2,1)S(1)}, bf16[32,1024]{1,0:T(8,128)(2,1)S(1)}, u32[]{:S(2)}, u32[]{:S(2)}) collective-permute-start(bf16[32,1024]{1,0:T(8,128)(2,1)S(1)} %get-tuple-element.120), channel_id=1, source_target_pairs={{0,8},{4,12},{8,0},{12,4},{1,9},{5,13},{9,1},{13,5},{2,10},{6,14},... | collective-permute-start | bytes 196616 | tf_op jit(solution)/shard_map/ppermute | solution.py:497
  97.2 8.4 %collective-permute-start.29 = (bf16[32,1024]{1,0:T(8,128)(2,1)S(1)}, bf16[32,1024]{1,0:T(8,128)(2,1)S(1)}, u32[]{:S(2)}, u32[]{:S(2)}) collective-permute-start(bf16[32,1024]{1,0:T(8,128)(2,1)S(1)} %get-tuple-element.121), channel_id=1, source_target_pairs={{0,12},{4,8},{8,4},{12,0},{1,13},{5,9},{9,5},{13,1},{2,14},{6,10},... | collective-permute-start | bytes 196616 | tf_op jit(solution)/shard_map/ppermute | solution.py:497
  98.6 7.6 %collective-permute-start.30 = (bf16[32,1024]{1,0:T(8,128)(2,1)S(1)}, bf16[32,1024]{1,0:T(8,128)(2,1)S(1)}, u32[]{:S(2)}, u32[]{:S(2)}) collective-permute-start(bf16[32,1024]{1,0:T(8,128)(2,1)S(1)} %get-tuple-element.122), channel_id=1, source_target_pairs={{0,4},{4,0},{8,12},{12,8},{1,5},{5,1},{9,13},{13,9},{2,6},{6,2},{1... | collective-permute-start | bytes 196616 | tf_op jit(solution)/shard_map/ppermute | solution.py:497
  100.5 10.3 %collective-permute-start.46 = (bf16[32,1024]{1,0:T(8,128)(2,1)S(1)}, bf16[32,1024]{1,0:T(8,128)(2,1)S(1)}, u32[]{:S(2)}, u32[]{:S(2)}) collective-permute-start(bf16[32,1024]{1,0:T(8,128)(2,1)S(1)} %get-tuple-element.136), channel_id=1, source_target_pairs={{0,8},{4,12},{8,0},{12,4},{1,9},{5,13},{9,1},{13,5},{2,10},{6,14},... | collective-permute-start | bytes 196616 | tf_op jit(solution)/shard_map/ppermute | solution.py:497
  102.5 8.4 %collective-permute-start.47 = (bf16[32,1024]{1,0:T(8,128)(2,1)S(1)}, bf16[32,1024]{1,0:T(8,128)(2,1)S(1)}, u32[]{:S(2)}, u32[]{:S(2)}) collective-permute-start(bf16[32,1024]{1,0:T(8,128)(2,1)S(1)} %get-tuple-element.137), channel_id=1, source_target_pairs={{0,12},{4,8},{8,4},{12,0},{1,13},{5,9},{9,5},{13,1},{2,14},{6,10},... | collective-permute-start | bytes 196616 | tf_op jit(solution)/shard_map/ppermute | solution.py:497
  107.0 6.9 %collective-permute-start.31 = (bf16[32,1024]{1,0:T(8,128)(2,1)S(1)}, bf16[32,1024]{1,0:T(8,128)(2,1)S(1)}, u32[]{:S(2)}, u32[]{:S(2)}) collective-permute-start(bf16[32,1024]{1,0:T(8,128)(2,1)S(1)} %get-tuple-element.124), channel_id=1, source_target_pairs={{0,8},{4,12},{8,0},{12,4},{1,9},{5,13},{9,1},{13,5},{2,10},{6,14},... | collective-permute-start | bytes 196616 | tf_op jit(solution)/shard_map/ppermute | solution.py:497
  112.6 6.8 %collective-permute-start.49 = (bf16[2,2,32,256]{3,2,1,0:T(8,128)(2,1)S(1)}, bf16[2,2,32,256]{3,2,1,0:T(8,128)(2,1)S(1)}, u32[]{:S(2)}, u32[]{:S(2)}) collective-permute-start(bf16[2,2,32,256]{3,2,1,0:T(8,128)(2,1)S(1)} %get-tuple-element.140), channel_id=1, source_target_pairs={{0,2},{2,0},{1,3},{3,1},{4,6},{6,4},{5,7},{7,5},{8,10},{10,8},{9,1... | collective-permute-start | bytes 196616 | tf_op jit(solution)/shard_map/ppermute | solution.py:497
  119.4 7.5 %collective-permute-start.52 = (bf16[2,2,32,256]{3,2,1,0:T(8,128)(2,1)S(1)}, bf16[2,2,32,256]{3,2,1,0:T(8,128)(2,1)S(1)}, u32[]{:S(2)}, u32[]{:S(2)}) collective-permute-start(bf16[2,2,32,256]{3,2,1,0:T(8,128)(2,1)S(1)} %shard_map.95.rest_0_), channel_id=1, source_target_pairs={{0,4},{4,0},{8,12},{12,8},{1,5},{5,1},{9,13},{13,9},{2,6},{6,2},{1... | collective-permute-start | bytes 196616 | tf_op jit(solution)/shard_map/ppermute | solution.py:497
  119.5 7.4 %collective-permute-start.51 = (bf16[2,2,32,256]{3,2,1,0:T(8,128)(2,1)S(1)}, bf16[2,2,32,256]{3,2,1,0:T(8,128)(2,1)S(1)}, u32[]{:S(2)}, u32[]{:S(2)}) collective-permute-start(bf16[2,2,32,256]{3,2,1,0:T(8,128)(2,1)S(1)} %shard_map.95.rest_0_), channel_id=1, source_target_pairs={{0,12},{4,8},{8,4},{12,0},{1,13},{5,9},{9,5},{13,1},{2,14},{6,10},... | collective-permute-start | bytes 196616 | tf_op jit(solution)/shard_map/ppermute | solution.py:497
  123.0 6.9 %collective-permute-start.37 = (bf16[2,2,32,256]{3,2,1,0:T(8,128)(2,1)S(1)}, bf16[2,2,32,256]{3,2,1,0:T(8,128)(2,1)S(1)}, u32[]{:S(2)}, u32[]{:S(2)}) collective-permute-start(bf16[2,2,32,256]{3,2,1,0:T(8,128)(2,1)S(1)} %shard_map.89.rest_0_), channel_id=1, source_target_pairs={{0,4},{4,0},{8,12},{12,8},{1,5},{5,1},{9,13},{13,9},{2,6},{6,2},{1... | collective-permute-start | bytes 196616 | tf_op jit(solution)/shard_map/ppermute | solution.py:497
  (28 other events, 252.6 us)

commit v12 on v11

--- a/solution.py
+++ b/solution.py
@@ -159,12 +159,12 @@
     )
 
 
-def masked_halves(response, aperture, places, after):
+def masked_halves(response, aperture, places):
     per_dev, _, src, rcv = response.shape
     half = src // 2
     width = half // PARTS
 
-    def body(_, rblk, __, flags, x_ref, ___, *outs):
+    def body(_, rblk, __, flags, x_ref, *outs):
         lane = lax.broadcasted_iota(jnp.int32, (1, rcv), 1) // BLOCK
         for flip in (1, 0):
             for j in range(per_dev):
@@ -180,7 +180,7 @@
                         out[j, at : at + BLOCK, c * rcv : (c + 1) * rcv] = x_ref[j, c, rows, :] * gate
 
     shape = jax.ShapeDtypeStruct((per_dev, width, 2 * rcv), BF16)
-    inputs = [(v, whole(v)) for v in (aperture, response)] + [(after, pl.BlockSpec(memory_space=pl.ANY))]
+    inputs = [(v, whole(v)) for v in (aperture, response)]
     outs = call(body, places, inputs, [(shape, whole(shape))] * (2 * PARTS), (1,))
     return list(outs[:PARTS]), list(outs[PARTS:])
 
@@ -205,16 +205,14 @@
 
 
 def src_onsets(onset, places, half_rows, share, width):
-    group = half_rows // CHUNKS
 
     def body(freq, rblk, sblk, o_ref, own, other):
         lanes = pl.ds(pl.multiple_of(rblk[0] * width, BLOCK), width)
         for core, out in ((sblk[0], own), (1 - sblk[0], other)):
-            for chunk in range(CHUNKS):
-                spot = pl.multiple_of(core * half_rows + chunk * group + freq[0] * share, ROWS)
-                out[chunk * share : (chunk + 1) * share] = o_ref[pl.ds(spot, share), lanes]
-
-    shape = jax.ShapeDtypeStruct((CHUNKS * share, width), onset.dtype)
+            spot = pl.multiple_of(core * half_rows + freq[0] * share, ROWS)
+            out[...] = o_ref[pl.ds(spot, share), lanes]
+
+    shape = jax.ShapeDtypeStruct((share, width), onset.dtype)
     return call(body, places, [(onset, whole(onset))], [(shape, whole(shape))] * 2, (1,))
 
 
@@ -245,20 +243,22 @@
     return call(body, places, [(v, whole(v)) for v in onsets], [(v, whole(v)) for v in shapes], (1,))
 
 
-def down_products(near, far, parts, freq_place, freq_devs, groups):
-    _, per_dev, rows, rcv = near.shape
+def down_products(near, far, parts, freq_place, freq_devs):
+    _, per_dev, _, rcv = near[0].shape
+    rows = sum(v.shape[2] for v in near)
     flat = [v for part in parts for pair in part for v in pair]
     width = flat[0].shape[1]
     total_width = width * len(flat) // 2
-    group = rows // groups
-    share = group // freq_devs
-
-    def body(place_ref, n_ref, f_ref, *rest):
+    share = rows // freq_devs
+
+    def body(place_ref, *rest):
+        spectra, rest = rest[: 2 * len(near)], rest[2 * len(near) :]
         resp, outs, held = rest[: len(flat)], rest[len(flat) : -1], rest[-1]
         for j in range(per_dev):
             sides = []
-            for ref in (n_ref, f_ref):
-                real, imag = ref[0, j], ref[1, j]
+            for refs in (spectra[: len(near)], spectra[len(near) :]):
+                real = jnp.concatenate([ref[0, j] for ref in refs], 0)
+                imag = jnp.concatenate([ref[1, j] for ref in refs], 0)
                 sides.append(jnp.concatenate([jnp.concatenate([real, -imag], 1), jnp.concatenate([imag, real], 1)], 0))
             for at in range(len(flat) // 2):
                 total = sum(
@@ -269,17 +269,14 @@
                 held[0, j, :, to] = total[:rows]
                 held[1, j, :, to] = total[rows:]
         for way, out in zip(ways(freq_devs), outs):
-            pieces = []
-            for index in range(groups):
-                start = pl.multiple_of(index * group + (place_ref[0] ^ way) * share, ROWS)
-                pieces.append(held[:, :, pl.ds(start, share), :])
-            out[...] = jnp.concatenate(pieces, 2).reshape(out.shape).astype(BF16)
-
-    shape = jax.ShapeDtypeStruct((2 * per_dev * groups * share, total_width), BF16)
+            start = pl.multiple_of((place_ref[0] ^ way) * share, share)
+            out[...] = held[:, :, pl.ds(start, share), :].reshape(out.shape).astype(BF16)
+
+    shape = jax.ShapeDtypeStruct((2 * per_dev * share, total_width), BF16)
     return call(
         body,
         (freq_place,),
-        [(v, whole(v)) for v in (near, far, *flat)],
+        [(v, whole(v)) for v in (*near, *far, *flat)],
         [(shape, whole(shape))] * freq_devs,
         (1,),
         scratch=[pltpu.VMEM((2, per_dev, rows, total_width), F32)],
@@ -304,16 +301,15 @@
     return jnp.stack([real, imag])
 
 
-def tiles(width, body, first=0):
+def tiles(width, body):
     def at(step, carry):
-        here = pl.multiple_of(step * BLOCK, BLOCK)
-        body(pl.ds(here, BLOCK), pl.ds(pl.multiple_of(here + first, BLOCK), BLOCK))
+        body(pl.ds(pl.multiple_of(step * BLOCK, BLOCK), BLOCK))
         return carry
 
     lax.fori_loop(0, width // BLOCK, at, 0, unroll=2)
 
 
-def windowed(messages, tables, matrix, freq_place, per_dev, share, first_row, first_lane):
+def windowed(messages, tables, matrix, freq_place, per_dev, share):
     cosines, sines, fraction = tables
     freq_devs = len(messages)
     width = messages[0].shape[-1]
@@ -323,22 +319,22 @@
         refs, outs = rest[:freq_devs], rest[freq_devs:]
         matrix_here = g_ref[place_ref[0]]
 
-        def one(at, there):
+        def one(at):
             data = [ref[:, at].astype(F32).reshape(2, per_dev, share, BLOCK) for ref in refs]
             made = [[] for _ in outs]
             for first in range(0, share, ROWS):
-                cut = slice(first_row + first, first_row + first + ROWS)
-                plain = [value[:, :, first : first + ROWS] for value in data]
-                cos = [c_ref[step, :, cut, there] for step in range(freq_devs)]
-                sin = [s_ref[step, :, cut, there] for step in range(freq_devs)]
+                cut = slice(first, first + ROWS)
+                plain = [value[:, :, cut] for value in data]
+                cos = [c_ref[step, :, cut, at] for step in range(freq_devs)]
+                sin = [s_ref[step, :, cut, at] for step in range(freq_devs)]
                 up, low = mixed_fields(plain, cos, sin, matrix_here)
-                part = f_ref[cut, there]
+                part = f_ref[cut, at]
                 for step in range(freq_devs):
                     made[step].append(unturned(up[step], low[step], plain[step], cos[step], sin[step], part))
             for out, value in zip(outs, made):
                 out[:, at] = jnp.concatenate(value, 2).reshape(out.shape[0], BLOCK).astype(BF16)
 
-        tiles(width, one, first_lane)
+        tiles(width, one)
 
     inputs = (cosines, sines, fraction, matrix, *messages)
     return call(
@@ -351,54 +347,47 @@
     )
 
 
-def up_products(by_part, parts, freq_place, rows, groups):
-    freq_devs = len(by_part[0])
-    flat = [v for part in parts for pair in part for v in pair]
+def up_products(messages, parts, freq_place, rows, side):
+    freq_devs = len(messages)
+    flat = [pair[side] for part in parts for pair in part]
     per_dev, src, rcv = flat[0].shape[0], flat[0].shape[1], flat[0].shape[2] // 2
-    messages = [v for part in by_part for v in part]
-    group = rows // groups
-    share = group // freq_devs
-    total_width = src * len(flat) // 2
+    group = rows // CHUNKS
+    share = rows // freq_devs
+    total_width = src * len(flat)
+    kind = BF16 if side else F32
 
     def body(place_ref, *rest):
-        resp, refs = rest[: len(flat)], rest[len(flat) : len(flat) + len(messages)]
-        outs, held = rest[len(flat) + len(messages) : -1], rest[-1]
-        lane = 0
-        for part in range(len(by_part)):
-            to = slice(lane, lane + refs[part * freq_devs].shape[1])
-            lane = to.stop
-            for step, way in enumerate(ways(freq_devs)):
-                value = refs[part * freq_devs + step][...].astype(F32)
-                value = value.reshape(2, per_dev, groups, share, value.shape[1])
-                for index in range(groups):
-                    start = pl.multiple_of(index * group + (place_ref[0] ^ way) * share, ROWS)
-                    held[:, :, pl.ds(start, share), to] = value[:, :, index]
+        resp, refs = rest[: len(flat)], rest[len(flat) : len(flat) + freq_devs]
+        outs, held = rest[len(flat) + freq_devs : -1], rest[-1]
+        for way, ref in zip(ways(freq_devs), refs):
+            start = pl.multiple_of((place_ref[0] ^ way) * share, share)
+            value = ref[...].reshape(2, per_dev, share, total_width)
+            for part in range(2):
+                for j in range(per_dev):
+                    held[part, j, pl.ds(start, share), :] = value[part, j]
         for j in range(per_dev):
-            both = [jnp.concatenate([held[0, j], held[1, j]], 0).astype(BF16)]
-            for side in (1, 0):
-                total = sum(
-                    jnp.dot(both[0][:, at * src : (at + 1) * src], resp[2 * at + side][j], preferred_element_type=F32)
-                    for at in range(len(flat) // 2)
-                )
-                real = total[:rows, :rcv] + total[rows:, rcv:]
-                imag = total[rows:, :rcv] - total[:rows, rcv:]
-                for index in range(groups):
-                    out = outs[2 * index + side]
-                    cut = slice(index * group, (index + 1) * group)
-                    out[0, j] = real[cut].astype(out.dtype)
-                    out[1, j] = imag[cut].astype(out.dtype)
-
-    shapes = [jax.ShapeDtypeStruct((2, per_dev, group, rcv), kind) for kind in (F32, BF16)] * groups
-    outs = call(
+            both = jnp.concatenate([held[0, j], held[1, j]], 0)
+            total = sum(
+                jnp.dot(both[:, at * src : (at + 1) * src], ref[j], preferred_element_type=F32)
+                for at, ref in enumerate(resp)
+            )
+            real = total[:rows, :rcv] + total[rows:, rcv:]
+            imag = total[rows:, :rcv] - total[:rows, rcv:]
+            for index, out in enumerate(outs):
+                cut = slice(index * group, (index + 1) * group)
+                out[0, j] = real[cut].astype(kind)
+                out[1, j] = imag[cut].astype(kind)
+
+    shape = jax.ShapeDtypeStruct((2, per_dev, group, rcv), kind)
+    return call(
         body,
         (freq_place,),
         [(v, whole(v)) for v in (*flat, *messages)],
-        [(v, whole(v)) for v in shapes],
+        [(shape, whole(shape))] * CHUNKS,
         (1,),
-        scratch=[pltpu.VMEM((2, per_dev, rows, total_width), F32)],
-        flops=2 * 8 * per_dev * rows * total_width * rcv,
-    )
-    return [tuple(outs[2 * index : 2 * index + 2]) for index in range(groups)]
+        scratch=[pltpu.VMEM((2, per_dev, rows, total_width), BF16)],
+        flops=2 * 4 * per_dev * rows * total_width * rcv,
+    )
 
 
 def next_spectra(sums, messages, tables, matrix, freq_place, first_row):
@@ -412,7 +401,7 @@
         refs, out = rest[:freq_devs], rest[freq_devs]
         matrix_here = g_ref[place_ref[0], :own]
 
-        def one(at, _):
+        def one(at):
             for base in range(0, rows, 2 * ROWS):
                 pair = slice(base, base + 2 * ROWS)
                 data = [ref[:, :, pair, at].astype(F32) for ref in refs]
@@ -512,52 +501,44 @@
     half_rows = initial.shape[0]
     src_width = response.shape[2] // 2
     rows = half_rows // CHUNKS
-    share = rows // freq_devs
+    share = half_rows // freq_devs
     places = tuple(lax.axis_index(axis).reshape(1) for axis in ("freq", "rblk", "sblk"))
     freq_place = places[0]
     inverse = jnp.asarray(inverse_tables(samples, freq_devs, per_dev))
     matrix = jnp.asarray(window_tables(samples, freq_devs, per_dev))
 
-    partial = first_spectra(initial, places, freq_devs, per_dev)
-    kept, sent = masked_halves(response, aperture, places, partial[0])
-    moved = exchanged(sent[0], "rblk", 1)
-    moved, partial = lax.optimization_barrier((moved, dealt_out(partial)))
-    sums, spectra = summed(partial)
+    kept, sent = masked_halves(response, aperture, places)
+    moved = [exchanged(v, "rblk", 1) for v in sent]
+    kept_pair = [exchanged(v, "sblk", 1) for v in kept]
+    sums, spectra = summed(dealt_out(first_spectra(initial, places, freq_devs, per_dev)))
     far = exchanged(spectra, "rblk", 1)
+    moved_pair = []
+    for index in range(PARTS):
+        if index:
+            moved[index], far = lax.optimization_barrier((moved[index], far))
+        else:
+            moved[index], spectra = lax.optimization_barrier((moved[index], spectra))
+        moved_pair.append(exchanged(moved[index], "sblk", 1))
+    parts = [((kept[i], moved[i]), (kept_pair[i], moved_pair[i])) for i in range(PARTS)]
 
     own, other = src_onsets(onset_src, places, half_rows, share, src_width)
     src_tables = phase_tables((own, exchanged(other, "sblk", 1)), places, freq_devs, per_dev, samples, PARTS)
     rcv_tables = phase_tables((onset_rcv,), places, freq_devs, per_dev, samples, rows=half_rows)
 
-    parts, by_part = [], []
-    for index in range(PARTS):
-        if index:
-            sent[index], far = lax.optimization_barrier((sent[index], far))
-            moved = exchanged(sent[index], "rblk", 1)
-            received = dealt_out(messages)
-            moved, received[1:-1] = lax.optimization_barrier((moved, received[1:-1]))
-            by_part.append(received)
-        pair = tuple(exchanged(v, "sblk", 1) for v in (kept[index], moved))
-        parts.append(((kept[index], moved), pair))
-        messages = dealt_out(down_products(spectra, far, parts[index:], freq_place, freq_devs, CHUNKS))
-        lane = index * messages[0].shape[-1]
-        messages = windowed(messages, src_tables, matrix, freq_place, per_dev, share * CHUNKS, 0, lane)
-    by_part.append(dealt_out(messages))
-    sums_of = up_products(by_part, parts, freq_place, half_rows, CHUNKS)
-
-    result = None
-    for chunk, (keep, send) in enumerate(sums_of):
-        first = chunk * rows
-        for _ in range(1, ITERS):
-            messages = spread(added(keep, exchanged(send, "rblk", 1)), freq_devs)
-            near = next_spectra(sums, messages, rcv_tables, matrix, freq_place, first)
-            messages = down_products(near, exchanged(near, "rblk", 1), parts, freq_place, freq_devs, 1)
-            messages = windowed(
-                dealt_out(messages), src_tables, matrix, freq_place, per_dev, share, chunk * share, 0
-            )
-            ((keep, send),) = up_products([dealt_out(messages)], parts, freq_place, rows, 1)
-        messages = spread(added(keep, exchanged(send, "rblk", 1)), freq_devs)
-        result = updated(initial, onset_rcv, messages, inverse, places, first, rows, result)
+    near, far, result = [spectra], [far], None
+    for step in range(ITERS):
+        messages = dealt_out(down_products(near, far, parts, freq_place, freq_devs))
+        messages = dealt_out(windowed(messages, src_tables, matrix, freq_place, per_dev, share))
+        received = [exchanged(v, "rblk", 1) for v in up_products(messages, parts, freq_place, half_rows, 1)]
+        keep = up_products(messages, parts, freq_place, half_rows, 0)
+        near, far = [], []
+        for chunk in range(CHUNKS):
+            back = spread(added(keep[chunk], received[chunk]), freq_devs)
+            if step < ITERS - 1:
+                near.append(next_spectra(sums, back, rcv_tables, matrix, freq_place, chunk * rows))
+                far.append(exchanged(near[chunk], "rblk", 1))
+            else:
+                result = updated(initial, onset_rcv, back, inverse, places, chunk * rows, rows, result)
     return result
 
 

time: 134 us -> 135 us (level)
  waiting for transfers between devices: 50.1 us -> 65.2 us
  starting transfers between devices: 63.3 us -> 50.9 us
  Pallas kernels: 16.7 us -> 13.8 us
    ppermute x53 -> x41, waiting for transfers between devices: 50.1 us -> 65.2 us  [exchanged(): lax.ppermute(value, axis, [(i, i ^ step) for i in range(lax.axis_size(axi...]
    ppermute x53 -> x41, starting transfers between devices: 63.3 us -> 50.9 us  [exchanged(): lax.ppermute(value, axis, [(i, i ^ step) for i in range(lax.axis_size(axi...]
    pallas_call x25 -> x22, Pallas kernels: 16.7 us -> 13.8 us  [call(): pl.pallas_call(body, grid_spec=pltpu.PrefetchScalarGridSpec(num_scalar_pr...]
  transfers between devices with their start and end apart: 53 -> 41, of which waited for: 24 -> 22; matrix products, arithmetic and copies ran while one was open for 0% -> 0% of each run, Pallas kernels for 9% -> 4%
where the time goes in v12:
time: 135 us
  waiting for transfers between devices  65.2 us (48%)
  starting transfers between devices  50.9 us (38%)
  Pallas kernels  13.8 us (10%)
  local copies, waits for them, and re-layouts  4.57 us (3%)
    ppermute x41, waiting for transfers between devices, exchanged(): lax.ppermute(value, axis, [(i, i ^ step) for i in range(lax.axis_size(axi...  65.2 us
    ppermute x41, starting transfers between devices, exchanged(): lax.ppermute(value, axis, [(i, i ^ step) for i in range(lax.axis_size(axi...  50.9 us
    pallas_call x22, Pallas kernels, call(): pl.pallas_call(body, grid_spec=pltpu.PrefetchScalarGridSpec(num_scalar_pr...  13.8 us
    unnamed x15, local copies, waits for them, and re-layouts  4.57 us
  transfers between devices with their start and end apart: 41, of which 22 were waited for; matrix products, arithmetic and copies ran while one was open for 0% of the time, Pallas kernels for 4%

profile of v12, /device:TPU:0, one launch (start us, length us, event | category | flops | bytes accessed | tf_op | source)
XLA Modules:
  0.0 134.7 jit_solution(11912072796591099962)
XLA Ops:
  0.8 1.6 %copy-done.2 = bf16[2,2,1024,256]{3,2,1,0:T(8,128)(2,1)S(1)} copy-done((bf16[2,2,1024,256]{3,2,1,0:T(8,128)(2,1)S(1)}, bf16[2,2,1024,256]{3,2,1,0:T(8,128)(2,1)}, u32[]{:S(2)}) %copy-start.2) | copy-done | bytes 2097176
  2.6 3.0 %collective-permute-start.6 = (bf16[2,256,512]{2,1,0:T(8,128)(2,1)S(1)}, bf16[2,256,512]{2,1,0:T(8,128)(2,1)S(1)}, u32[]{:S(2)}, u32[]{:S(2)}) collective-permute-start(bf16[2,256,512]{2,1,0:T(8,128)(2,1)S(1)} %get-tuple-element.66), channel_id=1, source_target_pairs={{0,2},{2,0},{1,3},{3,1},{4,6},{6,4},{5,7},{7,5},{8,10},{10,8},{9,1... | collective-permute-start | bytes 1572872 | tf_op jit(solution)/shard_map/ppermute | solution.py:486
  5.7 2.2 %copy-done = bf16[64,128,256]{2,1,0:T(8,128)(2,1)S(1)} copy-done((bf16[64,128,256]{2,1,0:T(8,128)(2,1)S(1)}, bf16[64,128,256]{2,1,0:T(8,128)(2,1)}, u32[]{:S(2)}) %copy-start) | copy-done | bytes 4194328
  8.6 3.1 %collective-permute-start.3 = (bf16[2,2,64,256]{3,2,1,0:T(8,128)(2,1)S(1)}, bf16[2,2,64,256]{3,2,1,0:T(8,128)(2,1)S(1)}, u32[]{:S(2)}, u32[]{:S(2)}) collective-permute-start(bf16[2,2,64,256]{3,2,1,0:T(8,128)(2,1)S(1)} %get-tuple-element.59), channel_id=1, source_target_pairs={{0,8},{4,12},{8,0},{12,4},{1,9},{5,13},{9,1},{13,5},{2,10},{6,14},... | collective-permute-start | bytes 393224 | tf_op jit(solution)/shard_map/ppermute | solution.py:486
  13.3 8.2 %collective-permute-done.3.refs_1_ = bf16[2,2,64,256]{3,2,1,0:T(8,128)(2,1)S(1)} collective-permute-done((bf16[2,2,64,256]{3,2,1,0:T(8,128)(2,1)S(1)}, bf16[2,2,64,256]{3,2,1,0:T(8,128)(2,1)S(1)}, u32[]{:S(2)}, u32[]{:S(2)}) %collective-permute-start.3) | collective-permute-done | bytes 131104 | tf_op jit(solution)/shard_map/ppermute | solution.py:486
  21.8 1.6 %collective-permute-start.8 = (bf16[2,2,64,256]{3,2,1,0:T(8,128)(2,1)S(1)}, bf16[2,2,64,256]{3,2,1,0:T(8,128)(2,1)S(1)}, u32[]{:S(2)}, u32[]{:S(2)}) collective-permute-start(bf16[2,2,64,256]{3,2,1,0:T(8,128)(2,1)S(1)} %get-tuple-element.68.rest_0_), channel_id=1, source_target_pairs={{0,2},{2,0},{1,3},{3,1},{4,6},{6,4},{5,7},{7,5},{8,10},{10,8},{9,1... | collective-permute-start | bytes 393224 | tf_op jit(solution)/shard_map/ppermute | solution.py:486
  23.9 7.7 %collective-permute-done.8.rest_1_ = bf16[2,2,64,256]{3,2,1,0:T(8,128)(2,1)S(1)} collective-permute-done((bf16[2,2,64,256]{3,2,1,0:T(8,128)(2,1)S(1)}, bf16[2,2,64,256]{3,2,1,0:T(8,128)(2,1)S(1)}, u32[]{:S(2)}, u32[]{:S(2)}) %collective-permute-start.8) | collective-permute-done | bytes 131104 | tf_op jit(solution)/shard_map/ppermute | solution.py:486
  31.6 1.9 %collective-permute-done.10.rest_9_.rest_3_.rest_11_ = bf16[2,256,512]{2,1,0:T(8,128)(2,1)S(1)} collective-permute-done((bf16[2,256,512]{2,1,0:T(8,128)(2,1)S(1)}, bf16[2,256,512]{2,1,0:T(8,128)(2,1)S(1)}, u32[]{:S(2)}, u32[]{:S(2)}) %collective-permute-start.10) | collective-permute-done | bytes 524320 | tf_op jit(solution)/shard_map/ppermute | solution.py:486
  33.5 1.5 %shard_map.79 = (bf16[64,1024]{1,0:T(8,128)(2,1)S(1)}, bf16[64,1024]{1,0:T(8,128)(2,1)S(1)}, bf16[64,1024]{1,0:T(8,128)(2,1)S(1)}, bf16[64,1024]{1,0:T(8,128)(2,1)S(1)}) custom-call(s32[1]{0:T(128)} %bitcast._.freq.place_ref, bf16[2,2,64,256]{3,2,1,0:T(8,128)(2,1)S(1)} %get-tuple-element.68.rest_0_, ...), custom_call_target="tpu_custom_call" | custom-call | flops 536870912 | bytes 4980736 | tf_op jit(solution)/shard_map/pallas_call | solution.py:78
  35.0 2.9 %collective-permute-start.11 = (bf16[64,1024]{1,0:T(8,128)(2,1)S(1)}, bf16[64,1024]{1,0:T(8,128)(2,1)S(1)}, u32[]{:S(2)}, u32[]{:S(2)}) collective-permute-start(bf16[64,1024]{1,0:T(8,128)(2,1)S(1)} %get-tuple-element.74), channel_id=1, source_target_pairs={{0,8},{4,12},{8,0},{12,4},{1,9},{5,13},{9,1},{13,5},{2,10},{6,14},... | collective-permute-start | bytes 393224 | tf_op jit(solution)/shard_map/ppermute | solution.py:486
  41.4 6.5 %collective-permute-done.11.rest_1_ = bf16[64,1024]{1,0:T(8,128)(2,1)S(1)} collective-permute-done((bf16[64,1024]{1,0:T(8,128)(2,1)S(1)}, bf16[64,1024]{1,0:T(8,128)(2,1)S(1)}, u32[]{:S(2)}, u32[]{:S(2)}) %collective-permute-start.11) | collective-permute-done | bytes 131104 | tf_op jit(solution)/shard_map/ppermute | solution.py:486
  49.7 4.2 %collective-permute-start.14 = (bf16[64,1024]{1,0:T(8,128)(2,1)S(1)}, bf16[64,1024]{1,0:T(8,128)(2,1)S(1)}, u32[]{:S(2)}, u32[]{:S(2)}) collective-permute-start(bf16[64,1024]{1,0:T(8,128)(2,1)S(1)} %get-tuple-element.78), channel_id=1, source_target_pairs={{0,8},{4,12},{8,0},{12,4},{1,9},{5,13},{9,1},{13,5},{2,10},{6,14},... | collective-permute-start | bytes 393224 | tf_op jit(solution)/shard_map/ppermute | solution.py:486
  54.5 9.0 %collective-permute-done.14.rest_5_ = bf16[64,1024]{1,0:T(8,128)(2,1)S(1)} collective-permute-done((bf16[64,1024]{1,0:T(8,128)(2,1)S(1)}, bf16[64,1024]{1,0:T(8,128)(2,1)S(1)}, u32[]{:S(2)}, u32[]{:S(2)}) %collective-permute-start.14) | collective-permute-done | bytes 131104 | tf_op jit(solution)/shard_map/ppermute | solution.py:486
  65.1 1.6 %collective-permute-start.17 = (bf16[2,2,32,256]{3,2,1,0:T(8,128)(2,1)S(1)}, bf16[2,2,32,256]{3,2,1,0:T(8,128)(2,1)S(1)}, u32[]{:S(2)}, u32[]{:S(2)}) collective-permute-start(bf16[2,2,32,256]{3,2,1,0:T(8,128)(2,1)S(1)} %get-tuple-element.82), channel_id=1, source_target_pairs={{0,2},{2,0},{1,3},{3,1},{4,6},{6,4},{5,7},{7,5},{8,10},{10,8},{9,1... | collective-permute-start | bytes 196616 | tf_op jit(solution)/shard_map/ppermute | solution.py:486
  67.7 1.8 %collective-permute-done.17.r_ref = bf16[2,2,32,256]{3,2,1,0:T(8,128)(2,1)S(1)} collective-permute-done((bf16[2,2,32,256]{3,2,1,0:T(8,128)(2,1)S(1)}, bf16[2,2,32,256]{3,2,1,0:T(8,128)(2,1)S(1)}, u32[]{:S(2)}, u32[]{:S(2)}) %collective-permute-start.17) | collective-permute-done | bytes 65568 | tf_op jit(solution)/shard_map/ppermute | solution.py:486
  69.4 2.7 %collective-permute-start.20 = (bf16[2,2,32,256]{3,2,1,0:T(8,128)(2,1)S(1)}, bf16[2,2,32,256]{3,2,1,0:T(8,128)(2,1)S(1)}, u32[]{:S(2)}, u32[]{:S(2)}) collective-permute-start(bf16[2,2,32,256]{3,2,1,0:T(8,128)(2,1)S(1)} %shard_map.83.rest_0_), channel_id=1, source_target_pairs={{0,4},{4,0},{8,12},{12,8},{1,5},{5,1},{9,13},{13,9},{2,6},{6,2},{1... | collective-permute-start | bytes 196616 | tf_op jit(solution)/shard_map/ppermute | solution.py:486
  73.7 2.9 %collective-permute-start.24 = (bf16[2,2,32,256]{3,2,1,0:T(8,128)(2,1)S(1)}, bf16[2,2,32,256]{3,2,1,0:T(8,128)(2,1)S(1)}, u32[]{:S(2)}, u32[]{:S(2)}) collective-permute-start(bf16[2,2,32,256]{3,2,1,0:T(8,128)(2,1)S(1)} %shard_map.85.rest_0_), channel_id=1, source_target_pairs={{0,4},{4,0},{8,12},{12,8},{1,5},{5,1},{9,13},{13,9},{2,6},{6,2},{1... | collective-permute-start | bytes 196616 | tf_op jit(solution)/shard_map/ppermute | solution.py:486
  78.8 2.7 %collective-permute-done.18.rest_1_ = bf16[2,2,32,256]{3,2,1,0:T(8,128)(2,1)S(1)} collective-permute-done((bf16[2,2,32,256]{3,2,1,0:T(8,128)(2,1)S(1)}, bf16[2,2,32,256]{3,2,1,0:T(8,128)(2,1)S(1)}, u32[]{:S(2)}, u32[]{:S(2)}) %collective-permute-start.18) | collective-permute-done | bytes 65568 | tf_op jit(solution)/shard_map/ppermute | solution.py:486
  81.8 1.5 %collective-permute-start.25 = (bf16[2,2,32,256]{3,2,1,0:T(8,128)(2,1)S(1)}, bf16[2,2,32,256]{3,2,1,0:T(8,128)(2,1)S(1)}, u32[]{:S(2)}, u32[]{:S(2)}) collective-permute-start(bf16[2,2,32,256]{3,2,1,0:T(8,128)(2,1)S(1)} %shard_map.84.rest_0_), channel_id=1, source_target_pairs={{0,2},{2,0},{1,3},{3,1},{4,6},{6,4},{5,7},{7,5},{8,10},{10,8},{9,1... | collective-permute-start | bytes 196616 | tf_op jit(solution)/shard_map/ppermute | solution.py:486
  86.5 2.7 %collective-permute-done.26.rest_3_ = bf16[2,2,32,256]{3,2,1,0:T(8,128)(2,1)S(1)} collective-permute-done((bf16[2,2,32,256]{3,2,1,0:T(8,128)(2,1)S(1)}, bf16[2,2,32,256]{3,2,1,0:T(8,128)(2,1)S(1)}, u32[]{:S(2)}, u32[]{:S(2)}) %collective-permute-start.26) | collective-permute-done | bytes 65568 | tf_op jit(solution)/shard_map/ppermute | solution.py:486
  89.2 1.5 %shard_map.87 = (bf16[64,1024]{1,0:T(8,128)(2,1)S(1)}, bf16[64,1024]{1,0:T(8,128)(2,1)S(1)}, bf16[64,1024]{1,0:T(8,128)(2,1)S(1)}, bf16[64,1024]{1,0:T(8,128)(2,1)S(1)}) custom-call(s32[1]{0:T(128)} %bitcast._.freq.place_ref, bf16[2,2,32,256]{3,2,1,0:T(8,128)(2,1)S(1)} %shard_map.84.rest_0_, bf16[2,2,32,256]{3,2,1,0:T(8,128)(2,1)S(1)} %shard_map.86.rest_1_, ...), custom_call_target="tpu_custom_call" | custom-call | flops 536870912 | bytes 4980736 | tf_op jit(solution)/shard_map/pallas_call | solution.py:78
  90.8 2.2 %collective-permute-start.28 = (bf16[64,1024]{1,0:T(8,128)(2,1)S(1)}, bf16[64,1024]{1,0:T(8,128)(2,1)S(1)}, u32[]{:S(2)}, u32[]{:S(2)}) collective-permute-start(bf16[64,1024]{1,0:T(8,128)(2,1)S(1)} %get-tuple-element.87), channel_id=1, source_target_pairs={{0,12},{4,8},{8,4},{12,0},{1,13},{5,9},{9,5},{13,1},{2,14},{6,10},... | collective-permute-start | bytes 393224 | tf_op jit(solution)/shard_map/ppermute | solution.py:486
  94.3 6.2 %collective-permute-done.27.rest_1_ = bf16[64,1024]{1,0:T(8,128)(2,1)S(1)} collective-permute-done((bf16[64,1024]{1,0:T(8,128)(2,1)S(1)}, bf16[64,1024]{1,0:T(8,128)(2,1)S(1)}, u32[]{:S(2)}, u32[]{:S(2)}) %collective-permute-start.27) | collective-permute-done | bytes 131104 | tf_op jit(solution)/shard_map/ppermute | solution.py:486
  101.7 2.4 %collective-permute-start.30 = (bf16[64,1024]{1,0:T(8,128)(2,1)S(1)}, bf16[64,1024]{1,0:T(8,128)(2,1)S(1)}, u32[]{:S(2)}, u32[]{:S(2)}) collective-permute-start(bf16[64,1024]{1,0:T(8,128)(2,1)S(1)} %get-tuple-element.90), channel_id=1, source_target_pairs={{0,8},{4,12},{8,0},{12,4},{1,9},{5,13},{9,1},{13,5},{2,10},{6,14},... | collective-permute-start | bytes 393224 | tf_op jit(solution)/shard_map/ppermute | solution.py:486
  104.1 1.8 %collective-permute-start.31 = (bf16[64,1024]{1,0:T(8,128)(2,1)S(1)}, bf16[64,1024]{1,0:T(8,128)(2,1)S(1)}, u32[]{:S(2)}, u32[]{:S(2)}) collective-permute-start(bf16[64,1024]{1,0:T(8,128)(2,1)S(1)} %get-tuple-element.91), channel_id=1, source_target_pairs={{0,12},{4,8},{8,4},{12,0},{1,13},{5,9},{9,5},{13,1},{2,14},{6,10},... | collective-permute-start | bytes 393224 | tf_op jit(solution)/shard_map/ppermute | solution.py:486
  105.9 7.4 %collective-permute-done.30.rest_5_ = bf16[64,1024]{1,0:T(8,128)(2,1)S(1)} collective-permute-done((bf16[64,1024]{1,0:T(8,128)(2,1)S(1)}, bf16[64,1024]{1,0:T(8,128)(2,1)S(1)}, u32[]{:S(2)}, u32[]{:S(2)}) %collective-permute-start.30) | collective-permute-done | bytes 131104 | tf_op jit(solution)/shard_map/ppermute | solution.py:486
  116.6 1.8 %collective-permute-done.37.r_ref = bf16[2,2,32,256]{3,2,1,0:T(8,128)(2,1)S(1)} collective-permute-done((bf16[2,2,32,256]{3,2,1,0:T(8,128)(2,1)S(1)}, bf16[2,2,32,256]{3,2,1,0:T(8,128)(2,1)S(1)}, u32[]{:S(2)}, u32[]{:S(2)}) %collective-permute-start.37) | collective-permute-done | bytes 65568 | tf_op jit(solution)/shard_map/ppermute | solution.py:486
  118.4 2.1 %collective-permute-start.40 = (bf16[2,2,32,256]{3,2,1,0:T(8,128)(2,1)S(1)}, bf16[2,2,32,256]{3,2,1,0:T(8,128)(2,1)S(1)}, u32[]{:S(2)}, u32[]{:S(2)}) collective-permute-start(bf16[2,2,32,256]{3,2,1,0:T(8,128)(2,1)S(1)} %shard_map.92.rest_0_), channel_id=1, source_target_pairs={{0,4},{4,0},{8,12},{12,8},{1,5},{5,1},{9,13},{13,9},{2,6},{6,2},{1... | collective-permute-start | bytes 196616 | tf_op jit(solution)/shard_map/ppermute | solution.py:486
  122.0 2.9 %collective-permute-start.36 = (bf16[2,2,32,256]{3,2,1,0:T(8,128)(2,1)S(1)}, bf16[2,2,32,256]{3,2,1,0:T(8,128)(2,1)S(1)}, u32[]{:S(2)}, u32[]{:S(2)}) collective-permute-start(bf16[2,2,32,256]{3,2,1,0:T(8,128)(2,1)S(1)} %shard_map.91.rest_0_), channel_id=1, source_target_pairs={{0,4},{4,0},{8,12},{12,8},{1,5},{5,1},{9,13},{13,9},{2,6},{6,2},{1... | collective-permute-start | bytes 196616 | tf_op jit(solution)/shard_map/ppermute | solution.py:486
  127.2 2.8 %collective-permute-done.38.rest_1_ = bf16[2,2,32,256]{3,2,1,0:T(8,128)(2,1)S(1)} collective-permute-done((bf16[2,2,32,256]{3,2,1,0:T(8,128)(2,1)S(1)}, bf16[2,2,32,256]{3,2,1,0:T(8,128)(2,1)S(1)}, u32[]{:S(2)}, u32[]{:S(2)}) %collective-permute-start.38) | collective-permute-done | bytes 65568 | tf_op jit(solution)/shard_map/ppermute | solution.py:486
  130.0 1.9 %shard_map.93.rest_4_ = bf16[64,128,256]{2,1,0:T(8,128)(2,1)} custom-call(s32[1]{0:T(128)} %bitcast._.freq.place_ref, s32[1]{0:T(128)} %bitcast.1.rblk._, s32[1]{0:T(128)} %bitcast.2.__.sblk, bf16[64,128,256]{2,1,0:T(8,128)(2,1)S(1)} %copy-done.1, s32[128,256]{1,0:T(8,128)S(1)} %copy-done.4, bf16[4,128,128]{2,1,0:T(8,128)(2,1)S(1)} %copy-done.5, ...), custom_call_target="tpu_custom_call" | custom-call | flops 33554432 | bytes 8912896 | tf_op jit(solution)/shard_map/pallas_call | solution.py:78
  132.8 1.9 %shard_map.94 = bf16[64,128,256]{2,1,0:T(8,128)(2,1)} custom-call(s32[1]{0:T(128)} %bitcast._.freq.place_ref, s32[1]{0:T(128)} %bitcast.1.rblk._, s32[1]{0:T(128)} %bitcast.2.__.sblk, bf16[64,128,256]{2,1,0:T(8,128)(2,1)S(1)} %copy-done.1, s32[128,256]{1,0:T(8,128)S(1)} %copy-done.4, ...), custom_call_target="tpu_custom_call", output_to_operand_aliasing={{}: (10, {})} | custom-call | flops 33554432 | bytes 13107200 | tf_op jit(solution)/shard_map/pallas_call | solution.py:78
  (87 shorter events, 30.4 us)
Async XLA Ops:
  2.6 21.3 %collective-permute-start.6 = (bf16[2,256,512]{2,1,0:T(8,128)(2,1)S(1)}, bf16[2,256,512]{2,1,0:T(8,128)(2,1)S(1)}, u32[]{:S(2)}, u32[]{:S(2)}) collective-permute-start(bf16[2,256,512]{2,1,0:T(8,128)(2,1)S(1)} %get-tuple-element.66), channel_id=1, source_target_pairs={{0,2},{2,0},{1,3},{3,1},{4,6},{6,4},{5,7},{7,5},{8,10},{10,8},{9,1... | collective-permute-start | bytes 1572872 | tf_op jit(solution)/shard_map/ppermute | solution.py:486
  5.6 26.0 %collective-permute-start.7 = (bf16[2,256,512]{2,1,0:T(8,128)(2,1)S(1)}, bf16[2,256,512]{2,1,0:T(8,128)(2,1)S(1)}, u32[]{:S(2)}, u32[]{:S(2)}) collective-permute-start(bf16[2,256,512]{2,1,0:T(8,128)(2,1)S(1)} %get-tuple-element.69), channel_id=1, source_target_pairs={{0,2},{2,0},{1,3},{3,1},{4,6},{6,4},{5,7},{7,5},{8,10},{10,8},{9,1... | collective-permute-start | bytes 1572872 | tf_op jit(solution)/shard_map/ppermute | solution.py:486
  8.6 12.9 %collective-permute-start.3 = (bf16[2,2,64,256]{3,2,1,0:T(8,128)(2,1)S(1)}, bf16[2,2,64,256]{3,2,1,0:T(8,128)(2,1)S(1)}, u32[]{:S(2)}, u32[]{:S(2)}) collective-permute-start(bf16[2,2,64,256]{3,2,1,0:T(8,128)(2,1)S(1)} %get-tuple-element.59), channel_id=1, source_target_pairs={{0,8},{4,12},{8,0},{12,4},{1,9},{5,13},{9,1},{13,5},{2,10},{6,14},... | collective-permute-start | bytes 393224 | tf_op jit(solution)/shard_map/ppermute | solution.py:486
  11.7 9.8 %collective-permute-start.4 = (bf16[2,2,64,256]{3,2,1,0:T(8,128)(2,1)S(1)}, bf16[2,2,64,256]{3,2,1,0:T(8,128)(2,1)S(1)}, u32[]{:S(2)}, u32[]{:S(2)}) collective-permute-start(bf16[2,2,64,256]{3,2,1,0:T(8,128)(2,1)S(1)} %get-tuple-element.60), channel_id=1, source_target_pairs={{0,12},{4,8},{8,4},{12,0},{1,13},{5,9},{9,5},{13,1},{2,14},{6,10},... | collective-permute-start | bytes 393224 | tf_op jit(solution)/shard_map/ppermute | solution.py:486
  13.1 8.6 %collective-permute-start.5 = (bf16[2,2,64,256]{3,2,1,0:T(8,128)(2,1)S(1)}, bf16[2,2,64,256]{3,2,1,0:T(8,128)(2,1)S(1)}, u32[]{:S(2)}, u32[]{:S(2)}) collective-permute-start(bf16[2,2,64,256]{3,2,1,0:T(8,128)(2,1)S(1)} %get-tuple-element.61), channel_id=1, source_target_pairs={{0,4},{4,0},{8,12},{12,8},{1,5},{5,1},{9,13},{13,9},{2,6},{6,2},{1... | collective-permute-start | bytes 393224 | tf_op jit(solution)/shard_map/ppermute | solution.py:486
  21.8 9.8 %collective-permute-start.8 = (bf16[2,2,64,256]{3,2,1,0:T(8,128)(2,1)S(1)}, bf16[2,2,64,256]{3,2,1,0:T(8,128)(2,1)S(1)}, u32[]{:S(2)}, u32[]{:S(2)}) collective-permute-start(bf16[2,2,64,256]{3,2,1,0:T(8,128)(2,1)S(1)} %get-tuple-element.68.rest_0_), channel_id=1, source_target_pairs={{0,2},{2,0},{1,3},{3,1},{4,6},{6,4},{5,7},{7,5},{8,10},{10,8},{9,1... | collective-permute-start | bytes 393224 | tf_op jit(solution)/shard_map/ppermute | solution.py:486
  23.4 8.2 %collective-permute-start = (bf16[2,256,512]{2,1,0:T(8,128)(2,1)S(1)}, bf16[2,256,512]{2,1,0:T(8,128)(2,1)S(1)}, u32[]{:S(2)}, u32[]{:S(2)}) collective-permute-start(bf16[2,256,512]{2,1,0:T(8,128)(2,1)S(1)} %get-tuple-element.51.rest_2_.rest_0_.rest_4_), channel_id=1, source_target_pairs={{0,1},{1,0},{2,3},{3,2},{4,5},{5,4},{6,7},{7,6},{8,9},{9,8},{10,11... | collective-permute-start | bytes 1572872 | tf_op jit(solution)/shard_map/ppermute | solution.py:486
  23.4 8.2 %collective-permute-start.1 = (bf16[2,256,512]{2,1,0:T(8,128)(2,1)S(1)}, bf16[2,256,512]{2,1,0:T(8,128)(2,1)S(1)}, u32[]{:S(2)}, u32[]{:S(2)}) collective-permute-start(bf16[2,256,512]{2,1,0:T(8,128)(2,1)S(1)} %get-tuple-element.52.rest_6_.rest_2_.rest_8_), channel_id=1, source_target_pairs={{0,1},{1,0},{2,3},{3,2},{4,5},{5,4},{6,7},{7,6},{8,9},{9,8},{10,11... | collective-permute-start | bytes 1572872 | tf_op jit(solution)/shard_map/ppermute | solution.py:486
  23.9 7.7 %collective-permute-start.9 = (bf16[2,256,512]{2,1,0:T(8,128)(2,1)S(1)}, bf16[2,256,512]{2,1,0:T(8,128)(2,1)S(1)}, u32[]{:S(2)}, u32[]{:S(2)}) collective-permute-start(bf16[2,256,512]{2,1,0:T(8,128)(2,1)S(1)} %collective-permute-done.6.rest_3_.rest_0_.rest_5_), channel_id=1, source_target_pairs={{0,1},{1,0},{2,3},{3,2},{4,5},{5,4},{6,7},{7,6},{8,9},{9,8},{10,11... | collective-permute-start | bytes 1572872 | tf_op jit(solution)/shard_map/ppermute | solution.py:486
  35.0 12.9 %collective-permute-start.11 = (bf16[64,1024]{1,0:T(8,128)(2,1)S(1)}, bf16[64,1024]{1,0:T(8,128)(2,1)S(1)}, u32[]{:S(2)}, u32[]{:S(2)}) collective-permute-start(bf16[64,1024]{1,0:T(8,128)(2,1)S(1)} %get-tuple-element.74), channel_id=1, source_target_pairs={{0,8},{4,12},{8,0},{12,4},{1,9},{5,13},{9,1},{13,5},{2,10},{6,14},... | collective-permute-start | bytes 393224 | tf_op jit(solution)/shard_map/ppermute | solution.py:486
  37.9 10.0 %collective-permute-start.12 = (bf16[64,1024]{1,0:T(8,128)(2,1)S(1)}, bf16[64,1024]{1,0:T(8,128)(2,1)S(1)}, u32[]{:S(2)}, u32[]{:S(2)}) collective-permute-start(bf16[64,1024]{1,0:T(8,128)(2,1)S(1)} %get-tuple-element.75), channel_id=1, source_target_pairs={{0,12},{4,8},{8,4},{12,0},{1,13},{5,9},{9,5},{13,1},{2,14},{6,10},... | collective-permute-start | bytes 393224 | tf_op jit(solution)/shard_map/ppermute | solution.py:486
  39.2 9.5 %collective-permute-start.13 = (bf16[64,1024]{1,0:T(8,128)(2,1)S(1)}, bf16[64,1024]{1,0:T(8,128)(2,1)S(1)}, u32[]{:S(2)}, u32[]{:S(2)}) collective-permute-start(bf16[64,1024]{1,0:T(8,128)(2,1)S(1)} %get-tuple-element.76), channel_id=1, source_target_pairs={{0,4},{4,0},{8,12},{12,8},{1,5},{5,1},{9,13},{13,9},{2,6},{6,2},{1... | collective-permute-start | bytes 393224 | tf_op jit(solution)/shard_map/ppermute | solution.py:486
  49.7 13.8 %collective-permute-start.14 = (bf16[64,1024]{1,0:T(8,128)(2,1)S(1)}, bf16[64,1024]{1,0:T(8,128)(2,1)S(1)}, u32[]{:S(2)}, u32[]{:S(2)}) collective-permute-start(bf16[64,1024]{1,0:T(8,128)(2,1)S(1)} %get-tuple-element.78), channel_id=1, source_target_pairs={{0,8},{4,12},{8,0},{12,4},{1,9},{5,13},{9,1},{13,5},{2,10},{6,14},... | collective-permute-start | bytes 393224 | tf_op jit(solution)/shard_map/ppermute | solution.py:486
  53.9 9.6 %collective-permute-start.15 = (bf16[64,1024]{1,0:T(8,128)(2,1)S(1)}, bf16[64,1024]{1,0:T(8,128)(2,1)S(1)}, u32[]{:S(2)}, u32[]{:S(2)}) collective-permute-start(bf16[64,1024]{1,0:T(8,128)(2,1)S(1)} %get-tuple-element.79), channel_id=1, source_target_pairs={{0,12},{4,8},{8,4},{12,0},{1,13},{5,9},{9,5},{13,1},{2,14},{6,10},... | collective-permute-start | bytes 393224 | tf_op jit(solution)/shard_map/ppermute | solution.py:486
  54.3 10.3 %collective-permute-start.16 = (bf16[64,1024]{1,0:T(8,128)(2,1)S(1)}, bf16[64,1024]{1,0:T(8,128)(2,1)S(1)}, u32[]{:S(2)}, u32[]{:S(2)}) collective-permute-start(bf16[64,1024]{1,0:T(8,128)(2,1)S(1)} %get-tuple-element.80), channel_id=1, source_target_pairs={{0,4},{4,0},{8,12},{12,8},{1,5},{5,1},{9,13},{13,9},{2,6},{6,2},{1... | collective-permute-start | bytes 393224 | tf_op jit(solution)/shard_map/ppermute | solution.py:486
  66.7 7.0 %collective-permute-start.21 = (bf16[2,2,32,256]{3,2,1,0:T(8,128)(2,1)S(1)}, bf16[2,2,32,256]{3,2,1,0:T(8,128)(2,1)S(1)}, u32[]{:S(2)}, u32[]{:S(2)}) collective-permute-start(bf16[2,2,32,256]{3,2,1,0:T(8,128)(2,1)S(1)} %get-tuple-element.84), channel_id=1, source_target_pairs={{0,2},{2,0},{1,3},{3,1},{4,6},{6,4},{5,7},{7,5},{8,10},{10,8},{9,1... | collective-permute-start | bytes 196616 | tf_op jit(solution)/shard_map/ppermute | solution.py:486
  69.4 7.9 %collective-permute-start.20 = (bf16[2,2,32,256]{3,2,1,0:T(8,128)(2,1)S(1)}, bf16[2,2,32,256]{3,2,1,0:T(8,128)(2,1)S(1)}, u32[]{:S(2)}, u32[]{:S(2)}) collective-permute-start(bf16[2,2,32,256]{3,2,1,0:T(8,128)(2,1)S(1)} %shard_map.83.rest_0_), channel_id=1, source_target_pairs={{0,4},{4,0},{8,12},{12,8},{1,5},{5,1},{9,13},{13,9},{2,6},{6,2},{1... | collective-permute-start | bytes 196616 | tf_op jit(solution)/shard_map/ppermute | solution.py:486
  72.8 8.7 %collective-permute-start.18 = (bf16[2,2,32,256]{3,2,1,0:T(8,128)(2,1)S(1)}, bf16[2,2,32,256]{3,2,1,0:T(8,128)(2,1)S(1)}, u32[]{:S(2)}, u32[]{:S(2)}) collective-permute-start(bf16[2,2,32,256]{3,2,1,0:T(8,128)(2,1)S(1)} %shard_map.83.rest_0_), channel_id=1, source_target_pairs={{0,8},{4,12},{8,0},{12,4},{1,9},{5,13},{9,1},{13,5},{2,10},{6,14},... | collective-permute-start | bytes 196616 | tf_op jit(solution)/shard_map/ppermute | solution.py:486
  73.7 9.7 %collective-permute-start.24 = (bf16[2,2,32,256]{3,2,1,0:T(8,128)(2,1)S(1)}, bf16[2,2,32,256]{3,2,1,0:T(8,128)(2,1)S(1)}, u32[]{:S(2)}, u32[]{:S(2)}) collective-permute-start(bf16[2,2,32,256]{3,2,1,0:T(8,128)(2,1)S(1)} %shard_map.85.rest_0_), channel_id=1, source_target_pairs={{0,4},{4,0},{8,12},{12,8},{1,5},{5,1},{9,13},{13,9},{2,6},{6,2},{1... | collective-permute-start | bytes 196616 | tf_op jit(solution)/shard_map/ppermute | solution.py:486
  76.6 6.8 %collective-permute-start.23 = (bf16[2,2,32,256]{3,2,1,0:T(8,128)(2,1)S(1)}, bf16[2,2,32,256]{3,2,1,0:T(8,128)(2,1)S(1)}, u32[]{:S(2)}, u32[]{:S(2)}) collective-permute-start(bf16[2,2,32,256]{3,2,1,0:T(8,128)(2,1)S(1)} %shard_map.85.rest_0_), channel_id=1, source_target_pairs={{0,12},{4,8},{8,4},{12,0},{1,13},{5,9},{9,5},{13,1},{2,14},{6,10},... | collective-permute-start | bytes 196616 | tf_op jit(solution)/shard_map/ppermute | solution.py:486
  77.3 7.3 %collective-permute-start.22 = (bf16[2,2,32,256]{3,2,1,0:T(8,128)(2,1)S(1)}, bf16[2,2,32,256]{3,2,1,0:T(8,128)(2,1)S(1)}, u32[]{:S(2)}, u32[]{:S(2)}) collective-permute-start(bf16[2,2,32,256]{3,2,1,0:T(8,128)(2,1)S(1)} %shard_map.85.rest_0_), channel_id=1, source_target_pairs={{0,8},{4,12},{8,0},{12,4},{1,9},{5,13},{9,1},{13,5},{2,10},{6,14},... | collective-permute-start | bytes 196616 | tf_op jit(solution)/shard_map/ppermute | solution.py:486
  90.7 9.8 %collective-permute-start.27 = (bf16[64,1024]{1,0:T(8,128)(2,1)S(1)}, bf16[64,1024]{1,0:T(8,128)(2,1)S(1)}, u32[]{:S(2)}, u32[]{:S(2)}) collective-permute-start(bf16[64,1024]{1,0:T(8,128)(2,1)S(1)} %get-tuple-element.86), channel_id=1, source_target_pairs={{0,8},{4,12},{8,0},{12,4},{1,9},{5,13},{9,1},{13,5},{2,10},{6,14},... | collective-permute-start | bytes 393224 | tf_op jit(solution)/shard_map/ppermute | solution.py:486
  90.8 9.7 %collective-permute-start.28 = (bf16[64,1024]{1,0:T(8,128)(2,1)S(1)}, bf16[64,1024]{1,0:T(8,128)(2,1)S(1)}, u32[]{:S(2)}, u32[]{:S(2)}) collective-permute-start(bf16[64,1024]{1,0:T(8,128)(2,1)S(1)} %get-tuple-element.87), channel_id=1, source_target_pairs={{0,12},{4,8},{8,4},{12,0},{1,13},{5,9},{9,5},{13,1},{2,14},{6,10},... | collective-permute-start | bytes 393224 | tf_op jit(solution)/shard_map/ppermute | solution.py:486
  93.0 7.7 %collective-permute-start.29 = (bf16[64,1024]{1,0:T(8,128)(2,1)S(1)}, bf16[64,1024]{1,0:T(8,128)(2,1)S(1)}, u32[]{:S(2)}, u32[]{:S(2)}) collective-permute-start(bf16[64,1024]{1,0:T(8,128)(2,1)S(1)} %get-tuple-element.88), channel_id=1, source_target_pairs={{0,4},{4,0},{8,12},{12,8},{1,5},{5,1},{9,13},{13,9},{2,6},{6,2},{1... | collective-permute-start | bytes 393224 | tf_op jit(solution)/shard_map/ppermute | solution.py:486
  101.7 11.6 %collective-permute-start.30 = (bf16[64,1024]{1,0:T(8,128)(2,1)S(1)}, bf16[64,1024]{1,0:T(8,128)(2,1)S(1)}, u32[]{:S(2)}, u32[]{:S(2)}) collective-permute-start(bf16[64,1024]{1,0:T(8,128)(2,1)S(1)} %get-tuple-element.90), channel_id=1, source_target_pairs={{0,8},{4,12},{8,0},{12,4},{1,9},{5,13},{9,1},{13,5},{2,10},{6,14},... | collective-permute-start | bytes 393224 | tf_op jit(solution)/shard_map/ppermute | solution.py:486
  104.1 9.2 %collective-permute-start.31 = (bf16[64,1024]{1,0:T(8,128)(2,1)S(1)}, bf16[64,1024]{1,0:T(8,128)(2,1)S(1)}, u32[]{:S(2)}, u32[]{:S(2)}) collective-permute-start(bf16[64,1024]{1,0:T(8,128)(2,1)S(1)} %get-tuple-element.91), channel_id=1, source_target_pairs={{0,12},{4,8},{8,4},{12,0},{1,13},{5,9},{9,5},{13,1},{2,14},{6,10},... | collective-permute-start | bytes 393224 | tf_op jit(solution)/shard_map/ppermute | solution.py:486
  105.9 7.7 %collective-permute-start.32 = (bf16[64,1024]{1,0:T(8,128)(2,1)S(1)}, bf16[64,1024]{1,0:T(8,128)(2,1)S(1)}, u32[]{:S(2)}, u32[]{:S(2)}) collective-permute-start(bf16[64,1024]{1,0:T(8,128)(2,1)S(1)} %get-tuple-element.92), channel_id=1, source_target_pairs={{0,4},{4,0},{8,12},{12,8},{1,5},{5,1},{9,13},{13,9},{2,6},{6,2},{1... | collective-permute-start | bytes 393224 | tf_op jit(solution)/shard_map/ppermute | solution.py:486
  118.4 7.9 %collective-permute-start.40 = (bf16[2,2,32,256]{3,2,1,0:T(8,128)(2,1)S(1)}, bf16[2,2,32,256]{3,2,1,0:T(8,128)(2,1)S(1)}, u32[]{:S(2)}, u32[]{:S(2)}) collective-permute-start(bf16[2,2,32,256]{3,2,1,0:T(8,128)(2,1)S(1)} %shard_map.92.rest_0_), channel_id=1, source_target_pairs={{0,4},{4,0},{8,12},{12,8},{1,5},{5,1},{9,13},{13,9},{2,6},{6,2},{1... | collective-permute-start | bytes 196616 | tf_op jit(solution)/shard_map/ppermute | solution.py:486
  120.4 6.7 %collective-permute-start.39 = (bf16[2,2,32,256]{3,2,1,0:T(8,128)(2,1)S(1)}, bf16[2,2,32,256]{3,2,1,0:T(8,128)(2,1)S(1)}, u32[]{:S(2)}, u32[]{:S(2)}) collective-permute-start(bf16[2,2,32,256]{3,2,1,0:T(8,128)(2,1)S(1)} %shard_map.92.rest_0_), channel_id=1, source_target_pairs={{0,12},{4,8},{8,4},{12,0},{1,13},{5,9},{9,5},{13,1},{2,14},{6,10},... | collective-permute-start | bytes 196616 | tf_op jit(solution)/shard_map/ppermute | solution.py:486
  121.8 8.2 %collective-permute-start.38 = (bf16[2,2,32,256]{3,2,1,0:T(8,128)(2,1)S(1)}, bf16[2,2,32,256]{3,2,1,0:T(8,128)(2,1)S(1)}, u32[]{:S(2)}, u32[]{:S(2)}) collective-permute-start(bf16[2,2,32,256]{3,2,1,0:T(8,128)(2,1)S(1)} %shard_map.92.rest_0_), channel_id=1, source_target_pairs={{0,8},{4,12},{8,0},{12,4},{1,9},{5,13},{9,1},{13,5},{2,10},{6,14},... | collective-permute-start | bytes 196616 | tf_op jit(solution)/shard_map/ppermute | solution.py:486
  122.0 9.9 %collective-permute-start.36 = (bf16[2,2,32,256]{3,2,1,0:T(8,128)(2,1)S(1)}, bf16[2,2,32,256]{3,2,1,0:T(8,128)(2,1)S(1)}, u32[]{:S(2)}, u32[]{:S(2)}) collective-permute-start(bf16[2,2,32,256]{3,2,1,0:T(8,128)(2,1)S(1)} %shard_map.91.rest_0_), channel_id=1, source_target_pairs={{0,4},{4,0},{8,12},{12,8},{1,5},{5,1},{9,13},{13,9},{2,6},{6,2},{1... | collective-permute-start | bytes 196616 | tf_op jit(solution)/shard_map/ppermute | solution.py:486
  124.9 7.0 %collective-permute-start.35 = (bf16[2,2,32,256]{3,2,1,0:T(8,128)(2,1)S(1)}, bf16[2,2,32,256]{3,2,1,0:T(8,128)(2,1)S(1)}, u32[]{:S(2)}, u32[]{:S(2)}) collective-permute-start(bf16[2,2,32,256]{3,2,1,0:T(8,128)(2,1)S(1)} %shard_map.91.rest_0_), channel_id=1, source_target_pairs={{0,12},{4,8},{8,4},{12,0},{1,13},{5,9},{9,5},{13,1},{2,14},{6,10},... | collective-permute-start | bytes 196616 | tf_op jit(solution)/shard_map/ppermute | solution.py:486
  (16 other events, 238.8 us)

commit v13 on v12

--- a/solution.py
+++ b/solution.py
@@ -491,7 +491,12 @@
 
 
 def spread(value, count):
-    return dealt_out([value] * count)
+    held = {0: value}
+    bit = count // 2
+    while bit:
+        held.update({way | bit: exchanged(held[way], "freq", bit) for way in sorted(held)})
+        bit //= 2
+    return [held[way] for way in ways(count)]
 
 
 def on_device(initial, response, aperture, onset_rcv, onset_src):

time: 135 us -> 132 us (0.978)
  waiting for transfers between devices: 65.2 us -> 58.3 us
  starting transfers between devices: 50.9 us -> 54.5 us
    ppermute x41, waiting for transfers between devices: 65.2 us -> 58.3 us  [exchanged(): lax.ppermute(value, axis, [(i, i ^ step) for i in range(lax.axis_size(axi...]
    ppermute x41, starting transfers between devices: 50.9 us -> 54.5 us  [exchanged(): lax.ppermute(value, axis, [(i, i ^ step) for i in range(lax.axis_size(axi...]
where the time goes in v13:
time: 132 us; the launch traced here: 131 us
  waiting for transfers between devices  58.3 us (44%)
  starting transfers between devices  54.5 us (41%)
  Pallas kernels  13.8 us (10%)
  local copies, waits for them, and re-layouts  4.57 us (3%)
    ppermute x41, waiting for transfers between devices, exchanged(): lax.ppermute(value, axis, [(i, i ^ step) for i in range(lax.axis_size(axi...  58.3 us
    ppermute x41, starting transfers between devices, exchanged(): lax.ppermute(value, axis, [(i, i ^ step) for i in range(lax.axis_size(axi...  54.5 us
    pallas_call x22, Pallas kernels, call(): pl.pallas_call(body, grid_spec=pltpu.PrefetchScalarGridSpec(num_scalar_pr...  13.8 us
    unnamed x15, local copies, waits for them, and re-layouts  4.57 us
  transfers between devices with their start and end apart: 41, of which 22 were waited for; matrix products, arithmetic and copies ran while one was open for 0% of the time, Pallas kernels for 4%

profile of v13, /device:TPU:0, one launch (start us, length us, event | category | flops | bytes accessed | tf_op | source)
XLA Modules:
  0.0 131.3 jit_solution(8713840400967562310)
XLA Ops:
  0.8 1.6 %copy-done.2 = bf16[2,2,1024,256]{3,2,1,0:T(8,128)(2,1)S(1)} copy-done((bf16[2,2,1024,256]{3,2,1,0:T(8,128)(2,1)S(1)}, bf16[2,2,1024,256]{3,2,1,0:T(8,128)(2,1)}, u32[]{:S(2)}) %copy-start.2) | copy-done | bytes 2097176
  2.6 3.0 %collective-permute-start.6 = (bf16[2,256,512]{2,1,0:T(8,128)(2,1)S(1)}, bf16[2,256,512]{2,1,0:T(8,128)(2,1)S(1)}, u32[]{:S(2)}, u32[]{:S(2)}) collective-permute-start(bf16[2,256,512]{2,1,0:T(8,128)(2,1)S(1)} %get-tuple-element.66), channel_id=1, source_target_pairs={{0,2},{2,0},{1,3},{3,1},{4,6},{6,4},{5,7},{7,5},{8,10},{10,8},{9,1... | collective-permute-start | bytes 1572872 | tf_op jit(solution)/shard_map/ppermute | solution.py:486
  5.7 2.2 %copy-done = bf16[64,128,256]{2,1,0:T(8,128)(2,1)S(1)} copy-done((bf16[64,128,256]{2,1,0:T(8,128)(2,1)S(1)}, bf16[64,128,256]{2,1,0:T(8,128)(2,1)}, u32[]{:S(2)}) %copy-start) | copy-done | bytes 4194328
  8.6 3.1 %collective-permute-start.3 = (bf16[2,2,64,256]{3,2,1,0:T(8,128)(2,1)S(1)}, bf16[2,2,64,256]{3,2,1,0:T(8,128)(2,1)S(1)}, u32[]{:S(2)}, u32[]{:S(2)}) collective-permute-start(bf16[2,2,64,256]{3,2,1,0:T(8,128)(2,1)S(1)} %get-tuple-element.59), channel_id=1, source_target_pairs={{0,8},{4,12},{8,0},{12,4},{1,9},{5,13},{9,1},{13,5},{2,10},{6,14},... | collective-permute-start | bytes 393224 | tf_op jit(solution)/shard_map/ppermute | solution.py:486
  13.3 8.2 %collective-permute-done.3.refs_1_ = bf16[2,2,64,256]{3,2,1,0:T(8,128)(2,1)S(1)} collective-permute-done((bf16[2,2,64,256]{3,2,1,0:T(8,128)(2,1)S(1)}, bf16[2,2,64,256]{3,2,1,0:T(8,128)(2,1)S(1)}, u32[]{:S(2)}, u32[]{:S(2)}) %collective-permute-start.3) | collective-permute-done | bytes 131104 | tf_op jit(solution)/shard_map/ppermute | solution.py:486
  21.8 1.6 %collective-permute-start.8 = (bf16[2,2,64,256]{3,2,1,0:T(8,128)(2,1)S(1)}, bf16[2,2,64,256]{3,2,1,0:T(8,128)(2,1)S(1)}, u32[]{:S(2)}, u32[]{:S(2)}) collective-permute-start(bf16[2,2,64,256]{3,2,1,0:T(8,128)(2,1)S(1)} %get-tuple-element.68.rest_0_), channel_id=1, source_target_pairs={{0,2},{2,0},{1,3},{3,1},{4,6},{6,4},{5,7},{7,5},{8,10},{10,8},{9,1... | collective-permute-start | bytes 393224 | tf_op jit(solution)/shard_map/ppermute | solution.py:486
  23.9 7.7 %collective-permute-done.8.rest_1_ = bf16[2,2,64,256]{3,2,1,0:T(8,128)(2,1)S(1)} collective-permute-done((bf16[2,2,64,256]{3,2,1,0:T(8,128)(2,1)S(1)}, bf16[2,2,64,256]{3,2,1,0:T(8,128)(2,1)S(1)}, u32[]{:S(2)}, u32[]{:S(2)}) %collective-permute-start.8) | collective-permute-done | bytes 131104 | tf_op jit(solution)/shard_map/ppermute | solution.py:486
  31.6 1.9 %collective-permute-done.10.rest_9_.rest_3_.rest_11_ = bf16[2,256,512]{2,1,0:T(8,128)(2,1)S(1)} collective-permute-done((bf16[2,256,512]{2,1,0:T(8,128)(2,1)S(1)}, bf16[2,256,512]{2,1,0:T(8,128)(2,1)S(1)}, u32[]{:S(2)}, u32[]{:S(2)}) %collective-permute-start.10) | collective-permute-done | bytes 524320 | tf_op jit(solution)/shard_map/ppermute | solution.py:486
  35.0 2.9 %collective-permute-start.11 = (bf16[64,1024]{1,0:T(8,128)(2,1)S(1)}, bf16[64,1024]{1,0:T(8,128)(2,1)S(1)}, u32[]{:S(2)}, u32[]{:S(2)}) collective-permute-start(bf16[64,1024]{1,0:T(8,128)(2,1)S(1)} %get-tuple-element.74), channel_id=1, source_target_pairs={{0,8},{4,12},{8,0},{12,4},{1,9},{5,13},{9,1},{13,5},{2,10},{6,14},... | collective-permute-start | bytes 393224 | tf_op jit(solution)/shard_map/ppermute | solution.py:486
  41.4 6.5 %collective-permute-done.11.rest_1_ = bf16[64,1024]{1,0:T(8,128)(2,1)S(1)} collective-permute-done((bf16[64,1024]{1,0:T(8,128)(2,1)S(1)}, bf16[64,1024]{1,0:T(8,128)(2,1)S(1)}, u32[]{:S(2)}, u32[]{:S(2)}) %collective-permute-start.11) | collective-permute-done | bytes 131104 | tf_op jit(solution)/shard_map/ppermute | solution.py:486
  49.7 4.2 %collective-permute-start.14 = (bf16[64,1024]{1,0:T(8,128)(2,1)S(1)}, bf16[64,1024]{1,0:T(8,128)(2,1)S(1)}, u32[]{:S(2)}, u32[]{:S(2)}) collective-permute-start(bf16[64,1024]{1,0:T(8,128)(2,1)S(1)} %get-tuple-element.78), channel_id=1, source_target_pairs={{0,8},{4,12},{8,0},{12,4},{1,9},{5,13},{9,1},{13,5},{2,10},{6,14},... | collective-permute-start | bytes 393224 | tf_op jit(solution)/shard_map/ppermute | solution.py:486
  54.5 9.0 %collective-permute-done.14.rest_5_ = bf16[64,1024]{1,0:T(8,128)(2,1)S(1)} collective-permute-done((bf16[64,1024]{1,0:T(8,128)(2,1)S(1)}, bf16[64,1024]{1,0:T(8,128)(2,1)S(1)}, u32[]{:S(2)}, u32[]{:S(2)}) %collective-permute-start.14) | collective-permute-done | bytes 131104 | tf_op jit(solution)/shard_map/ppermute | solution.py:486
  67.7 1.8 %collective-permute-done.17.r_ref = bf16[2,2,32,256]{3,2,1,0:T(8,128)(2,1)S(1)} collective-permute-done((bf16[2,2,32,256]{3,2,1,0:T(8,128)(2,1)S(1)}, bf16[2,2,32,256]{3,2,1,0:T(8,128)(2,1)S(1)}, u32[]{:S(2)}, u32[]{:S(2)}) %collective-permute-start.17) | collective-permute-done | bytes 65568 | tf_op jit(solution)/shard_map/ppermute | solution.py:486
  69.4 1.9 %collective-permute-start.18 = (bf16[2,2,32,256]{3,2,1,0:T(8,128)(2,1)S(1)}, bf16[2,2,32,256]{3,2,1,0:T(8,128)(2,1)S(1)}, u32[]{:S(2)}, u32[]{:S(2)}) collective-permute-start(bf16[2,2,32,256]{3,2,1,0:T(8,128)(2,1)S(1)} %shard_map.83.rest_0_), channel_id=1, source_target_pairs={{0,8},{4,12},{8,0},{12,4},{1,9},{5,13},{9,1},{13,5},{2,10},{6,14},... | collective-permute-start | bytes 196616 | tf_op jit(solution)/shard_map/ppermute | solution.py:486
  72.9 2.2 %collective-permute-start.20 = (bf16[2,2,32,256]{3,2,1,0:T(8,128)(2,1)S(1)}, bf16[2,2,32,256]{3,2,1,0:T(8,128)(2,1)S(1)}, u32[]{:S(2)}, u32[]{:S(2)}) collective-permute-start(bf16[2,2,32,256]{3,2,1,0:T(8,128)(2,1)S(1)} %shard_map.83.rest_0_), channel_id=1, source_target_pairs={{0,4},{4,0},{8,12},{12,8},{1,5},{5,1},{9,13},{13,9},{2,6},{6,2},{1... | collective-permute-start | bytes 196616 | tf_op jit(solution)/shard_map/ppermute | solution.py:486
  75.1 2.8 %collective-permute-start.19 = (bf16[2,2,32,256]{3,2,1,0:T(8,128)(2,1)S(1)}, bf16[2,2,32,256]{3,2,1,0:T(8,128)(2,1)S(1)}, u32[]{:S(2)}, u32[]{:S(2)}) collective-permute-start(bf16[2,2,32,256]{3,2,1,0:T(8,128)(2,1)S(1)} %collective-permute-done.18.rest_1_), channel_id=1, source_target_pairs={{0,4},{4,0},{8,12},{12,8},{1,5},{5,1},{9,13},{13,9},{2,6},{6,2},{1... | collective-permute-start | bytes 196616 | tf_op jit(solution)/shard_map/ppermute | solution.py:486
  78.0 2.0 %collective-permute-start.23 = (bf16[2,2,32,256]{3,2,1,0:T(8,128)(2,1)S(1)}, bf16[2,2,32,256]{3,2,1,0:T(8,128)(2,1)S(1)}, u32[]{:S(2)}, u32[]{:S(2)}) collective-permute-start(bf16[2,2,32,256]{3,2,1,0:T(8,128)(2,1)S(1)} %collective-permute-done.22.rest_1_), channel_id=1, source_target_pairs={{0,4},{4,0},{8,12},{12,8},{1,5},{5,1},{9,13},{13,9},{2,6},{6,2},{1... | collective-permute-start | bytes 196616 | tf_op jit(solution)/shard_map/ppermute | solution.py:486
  85.3 2.2 %collective-permute-done.26.rest_3_ = bf16[2,2,32,256]{3,2,1,0:T(8,128)(2,1)S(1)} collective-permute-done((bf16[2,2,32,256]{3,2,1,0:T(8,128)(2,1)S(1)}, bf16[2,2,32,256]{3,2,1,0:T(8,128)(2,1)S(1)}, u32[]{:S(2)}, u32[]{:S(2)}) %collective-permute-start.26) | collective-permute-done | bytes 65568 | tf_op jit(solution)/shard_map/ppermute | solution.py:486
  89.8 3.0 %collective-permute-start.28 = (bf16[64,1024]{1,0:T(8,128)(2,1)S(1)}, bf16[64,1024]{1,0:T(8,128)(2,1)S(1)}, u32[]{:S(2)}, u32[]{:S(2)}) collective-permute-start(bf16[64,1024]{1,0:T(8,128)(2,1)S(1)} %get-tuple-element.87), channel_id=1, source_target_pairs={{0,12},{4,8},{8,4},{12,0},{1,13},{5,9},{9,5},{13,1},{2,14},{6,10},... | collective-permute-start | bytes 393224 | tf_op jit(solution)/shard_map/ppermute | solution.py:486
  92.8 5.1 %collective-permute-done.27.rest_1_ = bf16[64,1024]{1,0:T(8,128)(2,1)S(1)} collective-permute-done((bf16[64,1024]{1,0:T(8,128)(2,1)S(1)}, bf16[64,1024]{1,0:T(8,128)(2,1)S(1)}, u32[]{:S(2)}, u32[]{:S(2)}) %collective-permute-start.27) | collective-permute-done | bytes 131104 | tf_op jit(solution)/shard_map/ppermute | solution.py:486
  100.4 1.7 %collective-permute-start.30 = (bf16[64,1024]{1,0:T(8,128)(2,1)S(1)}, bf16[64,1024]{1,0:T(8,128)(2,1)S(1)}, u32[]{:S(2)}, u32[]{:S(2)}) collective-permute-start(bf16[64,1024]{1,0:T(8,128)(2,1)S(1)} %get-tuple-element.90), channel_id=1, source_target_pairs={{0,8},{4,12},{8,0},{12,4},{1,9},{5,13},{9,1},{13,5},{2,10},{6,14},... | collective-permute-start | bytes 393224 | tf_op jit(solution)/shard_map/ppermute | solution.py:486
  102.1 3.4 %collective-permute-start.31 = (bf16[64,1024]{1,0:T(8,128)(2,1)S(1)}, bf16[64,1024]{1,0:T(8,128)(2,1)S(1)}, u32[]{:S(2)}, u32[]{:S(2)}) collective-permute-start(bf16[64,1024]{1,0:T(8,128)(2,1)S(1)} %get-tuple-element.91), channel_id=1, source_target_pairs={{0,12},{4,8},{8,4},{12,0},{1,13},{5,9},{9,5},{13,1},{2,14},{6,10},... | collective-permute-start | bytes 393224 | tf_op jit(solution)/shard_map/ppermute | solution.py:486
  106.3 3.7 %collective-permute-done.31.rest_6_ = bf16[64,1024]{1,0:T(8,128)(2,1)S(1)} collective-permute-done((bf16[64,1024]{1,0:T(8,128)(2,1)S(1)}, bf16[64,1024]{1,0:T(8,128)(2,1)S(1)}, u32[]{:S(2)}, u32[]{:S(2)}) %collective-permute-start.31) | collective-permute-done | bytes 131104 | tf_op jit(solution)/shard_map/ppermute | solution.py:486
  110.0 2.0 %collective-permute-done.32.rest_7_ = bf16[64,1024]{1,0:T(8,128)(2,1)S(1)} collective-permute-done((bf16[64,1024]{1,0:T(8,128)(2,1)S(1)}, bf16[64,1024]{1,0:T(8,128)(2,1)S(1)}, u32[]{:S(2)}, u32[]{:S(2)}) %collective-permute-start.32) | collective-permute-done | bytes 131104 | tf_op jit(solution)/shard_map/ppermute | solution.py:486
  112.5 1.8 %collective-permute-start.37 = (bf16[2,2,32,256]{3,2,1,0:T(8,128)(2,1)S(1)}, bf16[2,2,32,256]{3,2,1,0:T(8,128)(2,1)S(1)}, u32[]{:S(2)}, u32[]{:S(2)}) collective-permute-start(bf16[2,2,32,256]{3,2,1,0:T(8,128)(2,1)S(1)} %get-tuple-element.96), channel_id=1, source_target_pairs={{0,2},{2,0},{1,3},{3,1},{4,6},{6,4},{5,7},{7,5},{8,10},{10,8},{9,1... | collective-permute-start | bytes 196616 | tf_op jit(solution)/shard_map/ppermute | solution.py:486
  115.1 1.8 %collective-permute-done.37.r_ref = bf16[2,2,32,256]{3,2,1,0:T(8,128)(2,1)S(1)} collective-permute-done((bf16[2,2,32,256]{3,2,1,0:T(8,128)(2,1)S(1)}, bf16[2,2,32,256]{3,2,1,0:T(8,128)(2,1)S(1)}, u32[]{:S(2)}, u32[]{:S(2)}) %collective-permute-start.37) | collective-permute-done | bytes 65568 | tf_op jit(solution)/shard_map/ppermute | solution.py:486
  116.8 2.5 %collective-permute-start.38 = (bf16[2,2,32,256]{3,2,1,0:T(8,128)(2,1)S(1)}, bf16[2,2,32,256]{3,2,1,0:T(8,128)(2,1)S(1)}, u32[]{:S(2)}, u32[]{:S(2)}) collective-permute-start(bf16[2,2,32,256]{3,2,1,0:T(8,128)(2,1)S(1)} %shard_map.92.rest_0_), channel_id=1, source_target_pairs={{0,8},{4,12},{8,0},{12,4},{1,9},{5,13},{9,1},{13,5},{2,10},{6,14},... | collective-permute-start | bytes 196616 | tf_op jit(solution)/shard_map/ppermute | solution.py:486
  119.4 2.0 %collective-permute-start.34 = (bf16[2,2,32,256]{3,2,1,0:T(8,128)(2,1)S(1)}, bf16[2,2,32,256]{3,2,1,0:T(8,128)(2,1)S(1)}, u32[]{:S(2)}, u32[]{:S(2)}) collective-permute-start(bf16[2,2,32,256]{3,2,1,0:T(8,128)(2,1)S(1)} %shard_map.91.rest_0_), channel_id=1, source_target_pairs={{0,8},{4,12},{8,0},{12,4},{1,9},{5,13},{9,1},{13,5},{2,10},{6,14},... | collective-permute-start | bytes 196616 | tf_op jit(solution)/shard_map/ppermute | solution.py:486
  121.4 1.7 %collective-permute-start.40 = (bf16[2,2,32,256]{3,2,1,0:T(8,128)(2,1)S(1)}, bf16[2,2,32,256]{3,2,1,0:T(8,128)(2,1)S(1)}, u32[]{:S(2)}, u32[]{:S(2)}) collective-permute-start(bf16[2,2,32,256]{3,2,1,0:T(8,128)(2,1)S(1)} %shard_map.92.rest_0_), channel_id=1, source_target_pairs={{0,4},{4,0},{8,12},{12,8},{1,5},{5,1},{9,13},{13,9},{2,6},{6,2},{1... | collective-permute-start | bytes 196616 | tf_op jit(solution)/shard_map/ppermute | solution.py:486
  123.4 1.7 %collective-permute-start.36 = (bf16[2,2,32,256]{3,2,1,0:T(8,128)(2,1)S(1)}, bf16[2,2,32,256]{3,2,1,0:T(8,128)(2,1)S(1)}, u32[]{:S(2)}, u32[]{:S(2)}) collective-permute-start(bf16[2,2,32,256]{3,2,1,0:T(8,128)(2,1)S(1)} %shard_map.91.rest_0_), channel_id=1, source_target_pairs={{0,4},{4,0},{8,12},{12,8},{1,5},{5,1},{9,13},{13,9},{2,6},{6,2},{1... | collective-permute-start | bytes 196616 | tf_op jit(solution)/shard_map/ppermute | solution.py:486
  127.3 1.9 %shard_map.93.rest_4_ = bf16[64,128,256]{2,1,0:T(8,128)(2,1)} custom-call(s32[1]{0:T(128)} %bitcast._.freq.place_ref, s32[1]{0:T(128)} %bitcast.1.rblk._, s32[1]{0:T(128)} %bitcast.2.__.sblk, bf16[64,128,256]{2,1,0:T(8,128)(2,1)S(1)} %copy-done.1, s32[128,256]{1,0:T(8,128)S(1)} %copy-done.4, bf16[4,128,128]{2,1,0:T(8,128)(2,1)S(1)} %copy-done.5, ...), custom_call_target="tpu_custom_call" | custom-call | flops 33554432 | bytes 8912896 | tf_op jit(solution)/shard_map/pallas_call | solution.py:78
  129.4 1.9 %shard_map.94 = bf16[64,128,256]{2,1,0:T(8,128)(2,1)} custom-call(s32[1]{0:T(128)} %bitcast._.freq.place_ref, s32[1]{0:T(128)} %bitcast.1.rblk._, s32[1]{0:T(128)} %bitcast.2.__.sblk, bf16[64,128,256]{2,1,0:T(8,128)(2,1)S(1)} %copy-done.1, s32[128,256]{1,0:T(8,128)S(1)} %copy-done.4, ...), custom_call_target="tpu_custom_call", output_to_operand_aliasing={{}: (10, {})} | custom-call | flops 33554432 | bytes 13107200 | tf_op jit(solution)/shard_map/pallas_call | solution.py:78
  (87 shorter events, 32.2 us)
Async XLA Ops:
  2.6 21.3 %collective-permute-start.6 = (bf16[2,256,512]{2,1,0:T(8,128)(2,1)S(1)}, bf16[2,256,512]{2,1,0:T(8,128)(2,1)S(1)}, u32[]{:S(2)}, u32[]{:S(2)}) collective-permute-start(bf16[2,256,512]{2,1,0:T(8,128)(2,1)S(1)} %get-tuple-element.66), channel_id=1, source_target_pairs={{0,2},{2,0},{1,3},{3,1},{4,6},{6,4},{5,7},{7,5},{8,10},{10,8},{9,1... | collective-permute-start | bytes 1572872 | tf_op jit(solution)/shard_map/ppermute | solution.py:486
  5.6 26.0 %collective-permute-start.7 = (bf16[2,256,512]{2,1,0:T(8,128)(2,1)S(1)}, bf16[2,256,512]{2,1,0:T(8,128)(2,1)S(1)}, u32[]{:S(2)}, u32[]{:S(2)}) collective-permute-start(bf16[2,256,512]{2,1,0:T(8,128)(2,1)S(1)} %get-tuple-element.69), channel_id=1, source_target_pairs={{0,2},{2,0},{1,3},{3,1},{4,6},{6,4},{5,7},{7,5},{8,10},{10,8},{9,1... | collective-permute-start | bytes 1572872 | tf_op jit(solution)/shard_map/ppermute | solution.py:486
  8.6 12.9 %collective-permute-start.3 = (bf16[2,2,64,256]{3,2,1,0:T(8,128)(2,1)S(1)}, bf16[2,2,64,256]{3,2,1,0:T(8,128)(2,1)S(1)}, u32[]{:S(2)}, u32[]{:S(2)}) collective-permute-start(bf16[2,2,64,256]{3,2,1,0:T(8,128)(2,1)S(1)} %get-tuple-element.59), channel_id=1, source_target_pairs={{0,8},{4,12},{8,0},{12,4},{1,9},{5,13},{9,1},{13,5},{2,10},{6,14},... | collective-permute-start | bytes 393224 | tf_op jit(solution)/shard_map/ppermute | solution.py:486
  11.7 9.8 %collective-permute-start.4 = (bf16[2,2,64,256]{3,2,1,0:T(8,128)(2,1)S(1)}, bf16[2,2,64,256]{3,2,1,0:T(8,128)(2,1)S(1)}, u32[]{:S(2)}, u32[]{:S(2)}) collective-permute-start(bf16[2,2,64,256]{3,2,1,0:T(8,128)(2,1)S(1)} %get-tuple-element.60), channel_id=1, source_target_pairs={{0,12},{4,8},{8,4},{12,0},{1,13},{5,9},{9,5},{13,1},{2,14},{6,10},... | collective-permute-start | bytes 393224 | tf_op jit(solution)/shard_map/ppermute | solution.py:486
  13.1 8.6 %collective-permute-start.5 = (bf16[2,2,64,256]{3,2,1,0:T(8,128)(2,1)S(1)}, bf16[2,2,64,256]{3,2,1,0:T(8,128)(2,1)S(1)}, u32[]{:S(2)}, u32[]{:S(2)}) collective-permute-start(bf16[2,2,64,256]{3,2,1,0:T(8,128)(2,1)S(1)} %get-tuple-element.61), channel_id=1, source_target_pairs={{0,4},{4,0},{8,12},{12,8},{1,5},{5,1},{9,13},{13,9},{2,6},{6,2},{1... | collective-permute-start | bytes 393224 | tf_op jit(solution)/shard_map/ppermute | solution.py:486
  21.8 9.8 %collective-permute-start.8 = (bf16[2,2,64,256]{3,2,1,0:T(8,128)(2,1)S(1)}, bf16[2,2,64,256]{3,2,1,0:T(8,128)(2,1)S(1)}, u32[]{:S(2)}, u32[]{:S(2)}) collective-permute-start(bf16[2,2,64,256]{3,2,1,0:T(8,128)(2,1)S(1)} %get-tuple-element.68.rest_0_), channel_id=1, source_target_pairs={{0,2},{2,0},{1,3},{3,1},{4,6},{6,4},{5,7},{7,5},{8,10},{10,8},{9,1... | collective-permute-start | bytes 393224 | tf_op jit(solution)/shard_map/ppermute | solution.py:486
  23.4 8.2 %collective-permute-start = (bf16[2,256,512]{2,1,0:T(8,128)(2,1)S(1)}, bf16[2,256,512]{2,1,0:T(8,128)(2,1)S(1)}, u32[]{:S(2)}, u32[]{:S(2)}) collective-permute-start(bf16[2,256,512]{2,1,0:T(8,128)(2,1)S(1)} %get-tuple-element.51.rest_2_.rest_0_.rest_4_), channel_id=1, source_target_pairs={{0,1},{1,0},{2,3},{3,2},{4,5},{5,4},{6,7},{7,6},{8,9},{9,8},{10,11... | collective-permute-start | bytes 1572872 | tf_op jit(solution)/shard_map/ppermute | solution.py:486
  23.4 8.2 %collective-permute-start.1 = (bf16[2,256,512]{2,1,0:T(8,128)(2,1)S(1)}, bf16[2,256,512]{2,1,0:T(8,128)(2,1)S(1)}, u32[]{:S(2)}, u32[]{:S(2)}) collective-permute-start(bf16[2,256,512]{2,1,0:T(8,128)(2,1)S(1)} %get-tuple-element.52.rest_6_.rest_2_.rest_8_), channel_id=1, source_target_pairs={{0,1},{1,0},{2,3},{3,2},{4,5},{5,4},{6,7},{7,6},{8,9},{9,8},{10,11... | collective-permute-start | bytes 1572872 | tf_op jit(solution)/shard_map/ppermute | solution.py:486
  23.9 7.7 %collective-permute-start.9 = (bf16[2,256,512]{2,1,0:T(8,128)(2,1)S(1)}, bf16[2,256,512]{2,1,0:T(8,128)(2,1)S(1)}, u32[]{:S(2)}, u32[]{:S(2)}) collective-permute-start(bf16[2,256,512]{2,1,0:T(8,128)(2,1)S(1)} %collective-permute-done.6.rest_3_.rest_0_.rest_5_), channel_id=1, source_target_pairs={{0,1},{1,0},{2,3},{3,2},{4,5},{5,4},{6,7},{7,6},{8,9},{9,8},{10,11... | collective-permute-start | bytes 1572872 | tf_op jit(solution)/shard_map/ppermute | solution.py:486
  35.0 12.9 %collective-permute-start.11 = (bf16[64,1024]{1,0:T(8,128)(2,1)S(1)}, bf16[64,1024]{1,0:T(8,128)(2,1)S(1)}, u32[]{:S(2)}, u32[]{:S(2)}) collective-permute-start(bf16[64,1024]{1,0:T(8,128)(2,1)S(1)} %get-tuple-element.74), channel_id=1, source_target_pairs={{0,8},{4,12},{8,0},{12,4},{1,9},{5,13},{9,1},{13,5},{2,10},{6,14},... | collective-permute-start | bytes 393224 | tf_op jit(solution)/shard_map/ppermute | solution.py:486
  37.9 10.0 %collective-permute-start.12 = (bf16[64,1024]{1,0:T(8,128)(2,1)S(1)}, bf16[64,1024]{1,0:T(8,128)(2,1)S(1)}, u32[]{:S(2)}, u32[]{:S(2)}) collective-permute-start(bf16[64,1024]{1,0:T(8,128)(2,1)S(1)} %get-tuple-element.75), channel_id=1, source_target_pairs={{0,12},{4,8},{8,4},{12,0},{1,13},{5,9},{9,5},{13,1},{2,14},{6,10},... | collective-permute-start | bytes 393224 | tf_op jit(solution)/shard_map/ppermute | solution.py:486
  39.2 9.5 %collective-permute-start.13 = (bf16[64,1024]{1,0:T(8,128)(2,1)S(1)}, bf16[64,1024]{1,0:T(8,128)(2,1)S(1)}, u32[]{:S(2)}, u32[]{:S(2)}) collective-permute-start(bf16[64,1024]{1,0:T(8,128)(2,1)S(1)} %get-tuple-element.76), channel_id=1, source_target_pairs={{0,4},{4,0},{8,12},{12,8},{1,5},{5,1},{9,13},{13,9},{2,6},{6,2},{1... | collective-permute-start | bytes 393224 | tf_op jit(solution)/shard_map/ppermute | solution.py:486
  49.7 13.8 %collective-permute-start.14 = (bf16[64,1024]{1,0:T(8,128)(2,1)S(1)}, bf16[64,1024]{1,0:T(8,128)(2,1)S(1)}, u32[]{:S(2)}, u32[]{:S(2)}) collective-permute-start(bf16[64,1024]{1,0:T(8,128)(2,1)S(1)} %get-tuple-element.78), channel_id=1, source_target_pairs={{0,8},{4,12},{8,0},{12,4},{1,9},{5,13},{9,1},{13,5},{2,10},{6,14},... | collective-permute-start | bytes 393224 | tf_op jit(solution)/shard_map/ppermute | solution.py:486
  53.9 9.6 %collective-permute-start.15 = (bf16[64,1024]{1,0:T(8,128)(2,1)S(1)}, bf16[64,1024]{1,0:T(8,128)(2,1)S(1)}, u32[]{:S(2)}, u32[]{:S(2)}) collective-permute-start(bf16[64,1024]{1,0:T(8,128)(2,1)S(1)} %get-tuple-element.79), channel_id=1, source_target_pairs={{0,12},{4,8},{8,4},{12,0},{1,13},{5,9},{9,5},{13,1},{2,14},{6,10},... | collective-permute-start | bytes 393224 | tf_op jit(solution)/shard_map/ppermute | solution.py:486
  54.3 10.3 %collective-permute-start.16 = (bf16[64,1024]{1,0:T(8,128)(2,1)S(1)}, bf16[64,1024]{1,0:T(8,128)(2,1)S(1)}, u32[]{:S(2)}, u32[]{:S(2)}) collective-permute-start(bf16[64,1024]{1,0:T(8,128)(2,1)S(1)} %get-tuple-element.80), channel_id=1, source_target_pairs={{0,4},{4,0},{8,12},{12,8},{1,5},{5,1},{9,13},{13,9},{2,6},{6,2},{1... | collective-permute-start | bytes 393224 | tf_op jit(solution)/shard_map/ppermute | solution.py:486
  66.7 4.7 %collective-permute-start.21 = (bf16[2,2,32,256]{3,2,1,0:T(8,128)(2,1)S(1)}, bf16[2,2,32,256]{3,2,1,0:T(8,128)(2,1)S(1)}, u32[]{:S(2)}, u32[]{:S(2)}) collective-permute-start(bf16[2,2,32,256]{3,2,1,0:T(8,128)(2,1)S(1)} %get-tuple-element.84), channel_id=1, source_target_pairs={{0,2},{2,0},{1,3},{3,1},{4,6},{6,4},{5,7},{7,5},{8,10},{10,8},{9,1... | collective-permute-start | bytes 196616 | tf_op jit(solution)/shard_map/ppermute | solution.py:486
  69.4 5.7 %collective-permute-start.18 = (bf16[2,2,32,256]{3,2,1,0:T(8,128)(2,1)S(1)}, bf16[2,2,32,256]{3,2,1,0:T(8,128)(2,1)S(1)}, u32[]{:S(2)}, u32[]{:S(2)}) collective-permute-start(bf16[2,2,32,256]{3,2,1,0:T(8,128)(2,1)S(1)} %shard_map.83.rest_0_), channel_id=1, source_target_pairs={{0,8},{4,12},{8,0},{12,4},{1,9},{5,13},{9,1},{13,5},{2,10},{6,14},... | collective-permute-start | bytes 196616 | tf_op jit(solution)/shard_map/ppermute | solution.py:486
  71.4 6.6 %collective-permute-start.22 = (bf16[2,2,32,256]{3,2,1,0:T(8,128)(2,1)S(1)}, bf16[2,2,32,256]{3,2,1,0:T(8,128)(2,1)S(1)}, u32[]{:S(2)}, u32[]{:S(2)}) collective-permute-start(bf16[2,2,32,256]{3,2,1,0:T(8,128)(2,1)S(1)} %shard_map.85.rest_0_), channel_id=1, source_target_pairs={{0,8},{4,12},{8,0},{12,4},{1,9},{5,13},{9,1},{13,5},{2,10},{6,14},... | collective-permute-start | bytes 196616 | tf_op jit(solution)/shard_map/ppermute | solution.py:486
  72.9 7.8 %collective-permute-start.20 = (bf16[2,2,32,256]{3,2,1,0:T(8,128)(2,1)S(1)}, bf16[2,2,32,256]{3,2,1,0:T(8,128)(2,1)S(1)}, u32[]{:S(2)}, u32[]{:S(2)}) collective-permute-start(bf16[2,2,32,256]{3,2,1,0:T(8,128)(2,1)S(1)} %shard_map.83.rest_0_), channel_id=1, source_target_pairs={{0,4},{4,0},{8,12},{12,8},{1,5},{5,1},{9,13},{13,9},{2,6},{6,2},{1... | collective-permute-start | bytes 196616 | tf_op jit(solution)/shard_map/ppermute | solution.py:486
  75.1 5.6 %collective-permute-start.19 = (bf16[2,2,32,256]{3,2,1,0:T(8,128)(2,1)S(1)}, bf16[2,2,32,256]{3,2,1,0:T(8,128)(2,1)S(1)}, u32[]{:S(2)}, u32[]{:S(2)}) collective-permute-start(bf16[2,2,32,256]{3,2,1,0:T(8,128)(2,1)S(1)} %collective-permute-done.18.rest_1_), channel_id=1, source_target_pairs={{0,4},{4,0},{8,12},{12,8},{1,5},{5,1},{9,13},{13,9},{2,6},{6,2},{1... | collective-permute-start | bytes 196616 | tf_op jit(solution)/shard_map/ppermute | solution.py:486
  78.0 4.9 %collective-permute-start.23 = (bf16[2,2,32,256]{3,2,1,0:T(8,128)(2,1)S(1)}, bf16[2,2,32,256]{3,2,1,0:T(8,128)(2,1)S(1)}, u32[]{:S(2)}, u32[]{:S(2)}) collective-permute-start(bf16[2,2,32,256]{3,2,1,0:T(8,128)(2,1)S(1)} %collective-permute-done.22.rest_1_), channel_id=1, source_target_pairs={{0,4},{4,0},{8,12},{12,8},{1,5},{5,1},{9,13},{13,9},{2,6},{6,2},{1... | collective-permute-start | bytes 196616 | tf_op jit(solution)/shard_map/ppermute | solution.py:486
  89.0 8.8 %collective-permute-start.27 = (bf16[64,1024]{1,0:T(8,128)(2,1)S(1)}, bf16[64,1024]{1,0:T(8,128)(2,1)S(1)}, u32[]{:S(2)}, u32[]{:S(2)}) collective-permute-start(bf16[64,1024]{1,0:T(8,128)(2,1)S(1)} %get-tuple-element.86), channel_id=1, source_target_pairs={{0,8},{4,12},{8,0},{12,4},{1,9},{5,13},{9,1},{13,5},{2,10},{6,14},... | collective-permute-start | bytes 393224 | tf_op jit(solution)/shard_map/ppermute | solution.py:486
  89.8 8.1 %collective-permute-start.28 = (bf16[64,1024]{1,0:T(8,128)(2,1)S(1)}, bf16[64,1024]{1,0:T(8,128)(2,1)S(1)}, u32[]{:S(2)}, u32[]{:S(2)}) collective-permute-start(bf16[64,1024]{1,0:T(8,128)(2,1)S(1)} %get-tuple-element.87), channel_id=1, source_target_pairs={{0,12},{4,8},{8,4},{12,0},{1,13},{5,9},{9,5},{13,1},{2,14},{6,10},... | collective-permute-start | bytes 393224 | tf_op jit(solution)/shard_map/ppermute | solution.py:486
  92.8 6.6 %collective-permute-start.29 = (bf16[64,1024]{1,0:T(8,128)(2,1)S(1)}, bf16[64,1024]{1,0:T(8,128)(2,1)S(1)}, u32[]{:S(2)}, u32[]{:S(2)}) collective-permute-start(bf16[64,1024]{1,0:T(8,128)(2,1)S(1)} %get-tuple-element.88), channel_id=1, source_target_pairs={{0,4},{4,0},{8,12},{12,8},{1,5},{5,1},{9,13},{13,9},{2,6},{6,2},{1... | collective-permute-start | bytes 393224 | tf_op jit(solution)/shard_map/ppermute | solution.py:486
  100.4 5.9 %collective-permute-start.30 = (bf16[64,1024]{1,0:T(8,128)(2,1)S(1)}, bf16[64,1024]{1,0:T(8,128)(2,1)S(1)}, u32[]{:S(2)}, u32[]{:S(2)}) collective-permute-start(bf16[64,1024]{1,0:T(8,128)(2,1)S(1)} %get-tuple-element.90), channel_id=1, source_target_pairs={{0,8},{4,12},{8,0},{12,4},{1,9},{5,13},{9,1},{13,5},{2,10},{6,14},... | collective-permute-start | bytes 393224 | tf_op jit(solution)/shard_map/ppermute | solution.py:486
  102.1 7.9 %collective-permute-start.31 = (bf16[64,1024]{1,0:T(8,128)(2,1)S(1)}, bf16[64,1024]{1,0:T(8,128)(2,1)S(1)}, u32[]{:S(2)}, u32[]{:S(2)}) collective-permute-start(bf16[64,1024]{1,0:T(8,128)(2,1)S(1)} %get-tuple-element.91), channel_id=1, source_target_pairs={{0,12},{4,8},{8,4},{12,0},{1,13},{5,9},{9,5},{13,1},{2,14},{6,10},... | collective-permute-start | bytes 393224 | tf_op jit(solution)/shard_map/ppermute | solution.py:486
  105.5 6.6 %collective-permute-start.32 = (bf16[64,1024]{1,0:T(8,128)(2,1)S(1)}, bf16[64,1024]{1,0:T(8,128)(2,1)S(1)}, u32[]{:S(2)}, u32[]{:S(2)}) collective-permute-start(bf16[64,1024]{1,0:T(8,128)(2,1)S(1)} %get-tuple-element.92), channel_id=1, source_target_pairs={{0,4},{4,0},{8,12},{12,8},{1,5},{5,1},{9,13},{13,9},{2,6},{6,2},{1... | collective-permute-start | bytes 393224 | tf_op jit(solution)/shard_map/ppermute | solution.py:486
  114.2 5.1 %collective-permute-start.33 = (bf16[2,2,32,256]{3,2,1,0:T(8,128)(2,1)S(1)}, bf16[2,2,32,256]{3,2,1,0:T(8,128)(2,1)S(1)}, u32[]{:S(2)}, u32[]{:S(2)}) collective-permute-start(bf16[2,2,32,256]{3,2,1,0:T(8,128)(2,1)S(1)} %get-tuple-element.94), channel_id=1, source_target_pairs={{0,2},{2,0},{1,3},{3,1},{4,6},{6,4},{5,7},{7,5},{8,10},{10,8},{9,1... | collective-permute-start | bytes 196616 | tf_op jit(solution)/shard_map/ppermute | solution.py:486
  116.8 6.2 %collective-permute-start.38 = (bf16[2,2,32,256]{3,2,1,0:T(8,128)(2,1)S(1)}, bf16[2,2,32,256]{3,2,1,0:T(8,128)(2,1)S(1)}, u32[]{:S(2)}, u32[]{:S(2)}) collective-permute-start(bf16[2,2,32,256]{3,2,1,0:T(8,128)(2,1)S(1)} %shard_map.92.rest_0_), channel_id=1, source_target_pairs={{0,8},{4,12},{8,0},{12,4},{1,9},{5,13},{9,1},{13,5},{2,10},{6,14},... | collective-permute-start | bytes 196616 | tf_op jit(solution)/shard_map/ppermute | solution.py:486
  119.4 5.7 %collective-permute-start.34 = (bf16[2,2,32,256]{3,2,1,0:T(8,128)(2,1)S(1)}, bf16[2,2,32,256]{3,2,1,0:T(8,128)(2,1)S(1)}, u32[]{:S(2)}, u32[]{:S(2)}) collective-permute-start(bf16[2,2,32,256]{3,2,1,0:T(8,128)(2,1)S(1)} %shard_map.91.rest_0_), channel_id=1, source_target_pairs={{0,8},{4,12},{8,0},{12,4},{1,9},{5,13},{9,1},{13,5},{2,10},{6,14},... | collective-permute-start | bytes 196616 | tf_op jit(solution)/shard_map/ppermute | solution.py:486
  121.4 4.9 %collective-permute-start.40 = (bf16[2,2,32,256]{3,2,1,0:T(8,128)(2,1)S(1)}, bf16[2,2,32,256]{3,2,1,0:T(8,128)(2,1)S(1)}, u32[]{:S(2)}, u32[]{:S(2)}) collective-permute-start(bf16[2,2,32,256]{3,2,1,0:T(8,128)(2,1)S(1)} %shard_map.92.rest_0_), channel_id=1, source_target_pairs={{0,4},{4,0},{8,12},{12,8},{1,5},{5,1},{9,13},{13,9},{2,6},{6,2},{1... | collective-permute-start | bytes 196616 | tf_op jit(solution)/shard_map/ppermute | solution.py:486
  123.4 5.9 %collective-permute-start.36 = (bf16[2,2,32,256]{3,2,1,0:T(8,128)(2,1)S(1)}, bf16[2,2,32,256]{3,2,1,0:T(8,128)(2,1)S(1)}, u32[]{:S(2)}, u32[]{:S(2)}) collective-permute-start(bf16[2,2,32,256]{3,2,1,0:T(8,128)(2,1)S(1)} %shard_map.91.rest_0_), channel_id=1, source_target_pairs={{0,4},{4,0},{8,12},{12,8},{1,5},{5,1},{9,13},{13,9},{2,6},{6,2},{1... | collective-permute-start | bytes 196616 | tf_op jit(solution)/shard_map/ppermute | solution.py:486
  (16 other events, 231.2 us)

commit v14 on v13

--- a/solution.py
+++ b/solution.py
@@ -216,72 +216,81 @@
     return call(body, places, [(onset, whole(onset))], [(shape, whole(shape))] * 2, (1,))
 
 
-def phase_tables(onsets, places, freq_devs, per_dev, samples, parts=1, rows=None):
-    count = rows or onsets[0].shape[0]
-    width = onsets[0].shape[1] // parts
-
-    def body(freq, _, sblk, *refs):
-        cosines, sines, fraction = refs[-3:]
+def phase_tables(src, rcv, places, freq_devs, per_dev, samples, parts, rows):
+    width = src[0].shape[1] // parts
+
+    def fill(outs, value, to, freq):
+        cosines, sines, fraction = outs
+        value = value.astype(F32) * (1.0 / samples)
+        fraction[:, to] = value
+        for step, way in enumerate(ways(freq_devs)):
+            for j in range(per_dev):
+                order = ((freq[0] ^ way) * per_dev + j + 1).astype(F32)
+                cosines[step, j, :, to], sines[step, j, :, to] = turned(value * order)
+
+    def body(freq, _, sblk, own, other, r_ref, *outs):
         for part in range(parts):
-            for spot, ref in enumerate(refs[: len(onsets)]):
-                here = slice(part * width, (part + 1) * width)
-                if rows:
-                    value = ref[pl.ds(pl.multiple_of(sblk[0] * rows, ROWS), rows), here]
-                else:
-                    value = ref[:, here]
-                value = value.astype(F32) * (1.0 / samples)
-                at = (part * len(onsets) + spot) * width
-                to = slice(at, at + width)
-                fraction[:, to] = value
-                for step, way in enumerate(ways(freq_devs)):
-                    for j in range(per_dev):
-                        order = ((freq[0] ^ way) * per_dev + j + 1).astype(F32)
-                        cosines[step, j, :, to], sines[step, j, :, to] = turned(value * order)
-
-    table = jax.ShapeDtypeStruct((freq_devs, per_dev, count, width * parts * len(onsets)), F32)
-    shapes = [table, table, jax.ShapeDtypeStruct(table.shape[2:], F32)]
-    return call(body, places, [(v, whole(v)) for v in onsets], [(v, whole(v)) for v in shapes], (1,))
-
-
-def down_products(near, far, parts, freq_place, freq_devs):
-    _, per_dev, _, rcv = near[0].shape
-    rows = sum(v.shape[2] for v in near)
-    flat = [v for part in parts for pair in part for v in pair]
+            for spot, ref in enumerate((own, other)):
+                at = (part * 2 + spot) * width
+                fill(outs[:3], ref[:, part * width : (part + 1) * width], slice(at, at + width), freq)
+        value = r_ref[pl.ds(pl.multiple_of(sblk[0] * rows, ROWS), rows), :]
+        fill(outs[3:], value, slice(0, value.shape[1]), freq)
+
+    shapes = []
+    for count, total in ((src[0].shape[0], 2 * src[0].shape[1]), (rows, rcv.shape[1])):
+        table = jax.ShapeDtypeStruct((freq_devs, per_dev, count, total), F32)
+        shapes += [table, table, jax.ShapeDtypeStruct(table.shape[2:], F32)]
+    outs = call(body, places, [(v, whole(v)) for v in (*src, rcv)], [(v, whole(v)) for v in shapes], (1,))
+    return tuple(outs[:3]), tuple(outs[3:])
+
+
+def down_products(before, spectra, parts, side, first, freq_place, freq_devs=0):
+    _, per_dev, _, rcv = spectra[0].shape
+    rows = sum(v.shape[2] for v in spectra)
+    flat = [pair[side] for part in parts for pair in part]
     width = flat[0].shape[1]
-    total_width = width * len(flat) // 2
-    share = rows // freq_devs
+    total_width = before.shape[-1] if before is not None else first + width * len(flat)
+    share = rows // freq_devs if freq_devs else 0
+    old = [] if before is None else [before]
 
     def body(place_ref, *rest):
-        spectra, rest = rest[: 2 * len(near)], rest[2 * len(near) :]
-        resp, outs, held = rest[: len(flat)], rest[len(flat) : -1], rest[-1]
+        held_ref, rest = (rest[0], rest[1:]) if old else (None, rest)
+        refs, resp, outs = rest[: len(spectra)], rest[len(spectra) : len(spectra) + len(flat)], rest[len(spectra) + len(flat) :]
+        held = outs[-1]
         for j in range(per_dev):
-            sides = []
-            for refs in (spectra[: len(near)], spectra[len(near) :]):
-                real = jnp.concatenate([ref[0, j] for ref in refs], 0)
-                imag = jnp.concatenate([ref[1, j] for ref in refs], 0)
-                sides.append(jnp.concatenate([jnp.concatenate([real, -imag], 1), jnp.concatenate([imag, real], 1)], 0))
-            for at in range(len(flat) // 2):
-                total = sum(
-                    lax.dot_general(lhs, ref[j], (((1,), (1,)), ((), ())), preferred_element_type=F32)
-                    for lhs, ref in zip(sides, resp[2 * at : 2 * at + 2])
-                )
-                to = slice(at * width, (at + 1) * width)
-                held[0, j, :, to] = total[:rows]
-                held[1, j, :, to] = total[rows:]
-        for way, out in zip(ways(freq_devs), outs):
-            start = pl.multiple_of((place_ref[0] ^ way) * share, share)
-            out[...] = held[:, :, pl.ds(start, share), :].reshape(out.shape).astype(BF16)
-
-    shape = jax.ShapeDtypeStruct((2 * per_dev * share, total_width), BF16)
-    return call(
+            real = jnp.concatenate([ref[0, j] for ref in refs], 0)
+            imag = jnp.concatenate([ref[1, j] for ref in refs], 0)
+            lhs = jnp.concatenate([jnp.concatenate([real, -imag], 1), jnp.concatenate([imag, real], 1)], 0)
+            for at, ref in enumerate(resp):
+                total = lax.dot_general(lhs, ref[j], (((1,), (1,)), ((), ())), preferred_element_type=F32)
+                to = slice(first + at * width, first + (at + 1) * width)
+                for part in range(2):
+                    value = total[part * rows : (part + 1) * rows]
+                    held[part, j, :, to] = value + held_ref[part, j, :, to] if old else value
+        if old:
+            for to in (slice(0, first), slice(first + len(flat) * width, total_width)):
+                if to.start < to.stop:
+                    held[:, :, :, to] = held_ref[:, :, :, to]
+        if freq_devs:
+            for way, out in zip(ways(freq_devs), outs):
+                start = pl.multiple_of((place_ref[0] ^ way) * share, share)
+                out[...] = held[:, :, pl.ds(start, share), :].reshape(out.shape).astype(BF16)
+
+    sums = (2, per_dev, rows, total_width)
+    if freq_devs:
+        shapes = [jax.ShapeDtypeStruct((2 * per_dev * share, total_width), BF16)] * freq_devs
+    else:
+        shapes = [jax.ShapeDtypeStruct(sums, F32)]
+    outs = call(
         body,
         (freq_place,),
-        [(v, whole(v)) for v in (*near, *far, *flat)],
-        [(shape, whole(shape))] * freq_devs,
+        [(v, whole(v)) for v in (*old, *spectra, *flat)],
+        [(v, whole(v)) for v in shapes],
         (1,),
-        scratch=[pltpu.VMEM((2, per_dev, rows, total_width), F32)],
-        flops=2 * 8 * per_dev * rows * total_width * rcv,
-    )
+        scratch=[pltpu.VMEM(sums, F32)] if freq_devs else [],
+        flops=2 * 4 * per_dev * rows * len(flat) * width * rcv,
+    )
+    return outs if freq_devs else outs[0]
 
 
 def mixed_fields(plain, cos, sin, matrix):
@@ -527,12 +536,17 @@
     parts = [((kept[i], moved[i]), (kept_pair[i], moved_pair[i])) for i in range(PARTS)]
 
     own, other = src_onsets(onset_src, places, half_rows, share, src_width)
-    src_tables = phase_tables((own, exchanged(other, "sblk", 1)), places, freq_devs, per_dev, samples, PARTS)
-    rcv_tables = phase_tables((onset_rcv,), places, freq_devs, per_dev, samples, rows=half_rows)
+    onsets = (own, exchanged(other, "sblk", 1))
+    src_tables, rcv_tables = phase_tables(onsets, onset_rcv, places, freq_devs, per_dev, samples, PARTS, half_rows)
 
     near, far, result = [spectra], [far], None
     for step in range(ITERS):
-        messages = dealt_out(down_products(near, far, parts, freq_place, freq_devs))
+        held = down_products(None, near, parts, 0, 0, freq_place)
+        at = 0 if step else PARTS - 1
+        if at:
+            held = down_products(held, far, parts[:at], 1, 0, freq_place)
+        first = at * 2 * kept[0].shape[1]
+        messages = dealt_out(down_products(held, far, parts[at:], 1, first, freq_place, freq_devs))
         messages = dealt_out(windowed(messages, src_tables, matrix, freq_place, per_dev, share))
         received = [exchanged(v, "rblk", 1) for v in up_products(messages, parts, freq_place, half_rows, 1)]
         keep = up_products(messages, parts, freq_place, half_rows, 0)

time: 132 us -> 130 us (0.985)
  waiting for transfers between devices: 58.3 us -> 56.2 us
    ppermute x41, waiting for transfers between devices: 58.3 us -> 56.2 us  [exchanged(): lax.ppermute(value, axis, [(i, i ^ step) for i in range(lax.axis_size(axi...]
    pallas_call x22 -> x24, Pallas kernels: 13.8 us -> 14.2 us  [call(): pl.pallas_call(body, grid_spec=pltpu.PrefetchScalarGridSpec(num_scalar_pr...]
  transfers between devices with their start and end apart: 41 -> 41, of which waited for: 22 -> 22; matrix products, arithmetic and copies ran while one was open for 0% -> 0% of each run, Pallas kernels for 4% -> 6%
where the time goes in v14:
time: 130 us
  waiting for transfers between devices  56.2 us (43%)
  starting transfers between devices  54.5 us (42%)
  Pallas kernels  14.2 us (11%)
  local copies, waits for them, and re-layouts  4.56 us (4%)
    ppermute x41, waiting for transfers between devices, exchanged(): lax.ppermute(value, axis, [(i, i ^ step) for i in range(lax.axis_size(axi...  56.2 us
    ppermute x41, starting transfers between devices, exchanged(): lax.ppermute(value, axis, [(i, i ^ step) for i in range(lax.axis_size(axi...  54.5 us
    pallas_call x24, Pallas kernels, call(): pl.pallas_call(body, grid_spec=pltpu.PrefetchScalarGridSpec(num_scalar_pr...  14.2 us
    unnamed x15, local copies, waits for them, and re-layouts  4.56 us
  transfers between devices with their start and end apart: 41, of which 22 were waited for; matrix products, arithmetic and copies ran while one was open for 0% of the time, Pallas kernels for 6%

profile of v14, /device:TPU:0, one launch (start us, length us, event | category | flops | bytes accessed | tf_op | source)
XLA Modules:
  0.0 129.7 jit_solution(6480837994808656615)
XLA Ops:
  0.8 1.6 %copy-done.2 = bf16[2,2,1024,256]{3,2,1,0:T(8,128)(2,1)S(1)} copy-done((bf16[2,2,1024,256]{3,2,1,0:T(8,128)(2,1)S(1)}, bf16[2,2,1024,256]{3,2,1,0:T(8,128)(2,1)}, u32[]{:S(2)}) %copy-start.2) | copy-done | bytes 2097176
  2.6 3.0 %collective-permute-start.6 = (bf16[2,256,512]{2,1,0:T(8,128)(2,1)S(1)}, bf16[2,256,512]{2,1,0:T(8,128)(2,1)S(1)}, u32[]{:S(2)}, u32[]{:S(2)}) collective-permute-start(bf16[2,256,512]{2,1,0:T(8,128)(2,1)S(1)} %get-tuple-element.66), channel_id=1, source_target_pairs={{0,2},{2,0},{1,3},{3,1},{4,6},{6,4},{5,7},{7,5},{8,10},{10,8},{9,1... | collective-permute-start | bytes 1572872 | tf_op jit(solution)/shard_map/ppermute | solution.py:495
  5.7 2.2 %copy-done = bf16[64,128,256]{2,1,0:T(8,128)(2,1)S(1)} copy-done((bf16[64,128,256]{2,1,0:T(8,128)(2,1)S(1)}, bf16[64,128,256]{2,1,0:T(8,128)(2,1)}, u32[]{:S(2)}) %copy-start) | copy-done | bytes 4194328
  8.6 3.1 %collective-permute-start.3 = (bf16[2,2,64,256]{3,2,1,0:T(8,128)(2,1)S(1)}, bf16[2,2,64,256]{3,2,1,0:T(8,128)(2,1)S(1)}, u32[]{:S(2)}, u32[]{:S(2)}) collective-permute-start(bf16[2,2,64,256]{3,2,1,0:T(8,128)(2,1)S(1)} %get-tuple-element.59), channel_id=1, source_target_pairs={{0,8},{4,12},{8,0},{12,4},{1,9},{5,13},{9,1},{13,5},{2,10},{6,14},... | collective-permute-start | bytes 393224 | tf_op jit(solution)/shard_map/ppermute | solution.py:495
  13.3 8.2 %collective-permute-done.3.refs_1_ = bf16[2,2,64,256]{3,2,1,0:T(8,128)(2,1)S(1)} collective-permute-done((bf16[2,2,64,256]{3,2,1,0:T(8,128)(2,1)S(1)}, bf16[2,2,64,256]{3,2,1,0:T(8,128)(2,1)S(1)}, u32[]{:S(2)}, u32[]{:S(2)}) %collective-permute-start.3) | collective-permute-done | bytes 131104 | tf_op jit(solution)/shard_map/ppermute | solution.py:495
  21.8 1.6 %collective-permute-start.8 = (bf16[2,2,64,256]{3,2,1,0:T(8,128)(2,1)S(1)}, bf16[2,2,64,256]{3,2,1,0:T(8,128)(2,1)S(1)}, u32[]{:S(2)}, u32[]{:S(2)}) collective-permute-start(bf16[2,2,64,256]{3,2,1,0:T(8,128)(2,1)S(1)} %get-tuple-element.68.rest_0_), channel_id=1, source_target_pairs={{0,2},{2,0},{1,3},{3,1},{4,6},{6,4},{5,7},{7,5},{8,10},{10,8},{9,1... | collective-permute-start | bytes 393224 | tf_op jit(solution)/shard_map/ppermute | solution.py:495
  24.0 7.6 %collective-permute-done.8.rest_1_ = bf16[2,2,64,256]{3,2,1,0:T(8,128)(2,1)S(1)} collective-permute-done((bf16[2,2,64,256]{3,2,1,0:T(8,128)(2,1)S(1)}, bf16[2,2,64,256]{3,2,1,0:T(8,128)(2,1)S(1)}, u32[]{:S(2)}, u32[]{:S(2)}) %collective-permute-start.8) | collective-permute-done | bytes 131104 | tf_op jit(solution)/shard_map/ppermute | solution.py:495
  34.0 2.9 %collective-permute-start.11 = (bf16[64,1024]{1,0:T(8,128)(2,1)S(1)}, bf16[64,1024]{1,0:T(8,128)(2,1)S(1)}, u32[]{:S(2)}, u32[]{:S(2)}) collective-permute-start(bf16[64,1024]{1,0:T(8,128)(2,1)S(1)} %get-tuple-element.74), channel_id=1, source_target_pairs={{0,8},{4,12},{8,0},{12,4},{1,9},{5,13},{9,1},{13,5},{2,10},{6,14},... | collective-permute-start | bytes 393224 | tf_op jit(solution)/shard_map/ppermute | solution.py:495
  41.1 5.8 %collective-permute-done.11.rest_1_ = bf16[64,1024]{1,0:T(8,128)(2,1)S(1)} collective-permute-done((bf16[64,1024]{1,0:T(8,128)(2,1)S(1)}, bf16[64,1024]{1,0:T(8,128)(2,1)S(1)}, u32[]{:S(2)}, u32[]{:S(2)}) %collective-permute-start.11) | collective-permute-done | bytes 131104 | tf_op jit(solution)/shard_map/ppermute | solution.py:495
  48.7 4.2 %collective-permute-start.14 = (bf16[64,1024]{1,0:T(8,128)(2,1)S(1)}, bf16[64,1024]{1,0:T(8,128)(2,1)S(1)}, u32[]{:S(2)}, u32[]{:S(2)}) collective-permute-start(bf16[64,1024]{1,0:T(8,128)(2,1)S(1)} %get-tuple-element.78), channel_id=1, source_target_pairs={{0,8},{4,12},{8,0},{12,4},{1,9},{5,13},{9,1},{13,5},{2,10},{6,14},... | collective-permute-start | bytes 393224 | tf_op jit(solution)/shard_map/ppermute | solution.py:495
  53.5 9.0 %collective-permute-done.14.rest_5_ = bf16[64,1024]{1,0:T(8,128)(2,1)S(1)} collective-permute-done((bf16[64,1024]{1,0:T(8,128)(2,1)S(1)}, bf16[64,1024]{1,0:T(8,128)(2,1)S(1)}, u32[]{:S(2)}, u32[]{:S(2)}) %collective-permute-start.14) | collective-permute-done | bytes 131104 | tf_op jit(solution)/shard_map/ppermute | solution.py:495
  64.1 1.6 %collective-permute-start.17 = (bf16[2,2,32,256]{3,2,1,0:T(8,128)(2,1)S(1)}, bf16[2,2,32,256]{3,2,1,0:T(8,128)(2,1)S(1)}, u32[]{:S(2)}, u32[]{:S(2)}) collective-permute-start(bf16[2,2,32,256]{3,2,1,0:T(8,128)(2,1)S(1)} %get-tuple-element.82), channel_id=1, source_target_pairs={{0,2},{2,0},{1,3},{3,1},{4,6},{6,4},{5,7},{7,5},{8,10},{10,8},{9,1... | collective-permute-start | bytes 196616 | tf_op jit(solution)/shard_map/ppermute | solution.py:495
  66.7 1.8 %collective-permute-done.17.r_ref = bf16[2,2,32,256]{3,2,1,0:T(8,128)(2,1)S(1)} collective-permute-done((bf16[2,2,32,256]{3,2,1,0:T(8,128)(2,1)S(1)}, bf16[2,2,32,256]{3,2,1,0:T(8,128)(2,1)S(1)}, u32[]{:S(2)}, u32[]{:S(2)}) %collective-permute-start.17) | collective-permute-done | bytes 65568 | tf_op jit(solution)/shard_map/ppermute | solution.py:495
  68.4 1.9 %collective-permute-start.18 = (bf16[2,2,32,256]{3,2,1,0:T(8,128)(2,1)S(1)}, bf16[2,2,32,256]{3,2,1,0:T(8,128)(2,1)S(1)}, u32[]{:S(2)}, u32[]{:S(2)}) collective-permute-start(bf16[2,2,32,256]{3,2,1,0:T(8,128)(2,1)S(1)} %shard_map.84.rest_0_), channel_id=1, source_target_pairs={{0,8},{4,12},{8,0},{12,4},{1,9},{5,13},{9,1},{13,5},{2,10},{6,14},... | collective-permute-start | bytes 196616 | tf_op jit(solution)/shard_map/ppermute | solution.py:495
  71.9 2.3 %collective-permute-start.20 = (bf16[2,2,32,256]{3,2,1,0:T(8,128)(2,1)S(1)}, bf16[2,2,32,256]{3,2,1,0:T(8,128)(2,1)S(1)}, u32[]{:S(2)}, u32[]{:S(2)}) collective-permute-start(bf16[2,2,32,256]{3,2,1,0:T(8,128)(2,1)S(1)} %shard_map.84.rest_0_), channel_id=1, source_target_pairs={{0,4},{4,0},{8,12},{12,8},{1,5},{5,1},{9,13},{13,9},{2,6},{6,2},{1... | collective-permute-start | bytes 196616 | tf_op jit(solution)/shard_map/ppermute | solution.py:495
  74.1 2.8 %collective-permute-start.19 = (bf16[2,2,32,256]{3,2,1,0:T(8,128)(2,1)S(1)}, bf16[2,2,32,256]{3,2,1,0:T(8,128)(2,1)S(1)}, u32[]{:S(2)}, u32[]{:S(2)}) collective-permute-start(bf16[2,2,32,256]{3,2,1,0:T(8,128)(2,1)S(1)} %collective-permute-done.18.rest_1_), channel_id=1, source_target_pairs={{0,4},{4,0},{8,12},{12,8},{1,5},{5,1},{9,13},{13,9},{2,6},{6,2},{1... | collective-permute-start | bytes 196616 | tf_op jit(solution)/shard_map/ppermute | solution.py:495
  77.0 2.0 %collective-permute-start.23 = (bf16[2,2,32,256]{3,2,1,0:T(8,128)(2,1)S(1)}, bf16[2,2,32,256]{3,2,1,0:T(8,128)(2,1)S(1)}, u32[]{:S(2)}, u32[]{:S(2)}) collective-permute-start(bf16[2,2,32,256]{3,2,1,0:T(8,128)(2,1)S(1)} %collective-permute-done.22.rest_1_), channel_id=1, source_target_pairs={{0,4},{4,0},{8,12},{12,8},{1,5},{5,1},{9,13},{13,9},{2,6},{6,2},{1... | collective-permute-start | bytes 196616 | tf_op jit(solution)/shard_map/ppermute | solution.py:495
  84.1 2.4 %collective-permute-done.26.rest_2_ = bf16[2,2,32,256]{3,2,1,0:T(8,128)(2,1)S(1)} collective-permute-done((bf16[2,2,32,256]{3,2,1,0:T(8,128)(2,1)S(1)}, bf16[2,2,32,256]{3,2,1,0:T(8,128)(2,1)S(1)}, u32[]{:S(2)}, u32[]{:S(2)}) %collective-permute-start.26) | collective-permute-done | bytes 65568 | tf_op jit(solution)/shard_map/ppermute | solution.py:495
  88.2 3.0 %collective-permute-start.28 = (bf16[64,1024]{1,0:T(8,128)(2,1)S(1)}, bf16[64,1024]{1,0:T(8,128)(2,1)S(1)}, u32[]{:S(2)}, u32[]{:S(2)}) collective-permute-start(bf16[64,1024]{1,0:T(8,128)(2,1)S(1)} %get-tuple-element.87), channel_id=1, source_target_pairs={{0,12},{4,8},{8,4},{12,0},{1,13},{5,9},{9,5},{13,1},{2,14},{6,10},... | collective-permute-start | bytes 393224 | tf_op jit(solution)/shard_map/ppermute | solution.py:495
  91.2 5.1 %collective-permute-done.27.rest_1_ = bf16[64,1024]{1,0:T(8,128)(2,1)S(1)} collective-permute-done((bf16[64,1024]{1,0:T(8,128)(2,1)S(1)}, bf16[64,1024]{1,0:T(8,128)(2,1)S(1)}, u32[]{:S(2)}, u32[]{:S(2)}) %collective-permute-start.27) | collective-permute-done | bytes 131104 | tf_op jit(solution)/shard_map/ppermute | solution.py:495
  98.8 1.7 %collective-permute-start.30 = (bf16[64,1024]{1,0:T(8,128)(2,1)S(1)}, bf16[64,1024]{1,0:T(8,128)(2,1)S(1)}, u32[]{:S(2)}, u32[]{:S(2)}) collective-permute-start(bf16[64,1024]{1,0:T(8,128)(2,1)S(1)} %get-tuple-element.90), channel_id=1, source_target_pairs={{0,8},{4,12},{8,0},{12,4},{1,9},{5,13},{9,1},{13,5},{2,10},{6,14},... | collective-permute-start | bytes 393224 | tf_op jit(solution)/shard_map/ppermute | solution.py:495
  100.4 3.4 %collective-permute-start.31 = (bf16[64,1024]{1,0:T(8,128)(2,1)S(1)}, bf16[64,1024]{1,0:T(8,128)(2,1)S(1)}, u32[]{:S(2)}, u32[]{:S(2)}) collective-permute-start(bf16[64,1024]{1,0:T(8,128)(2,1)S(1)} %get-tuple-element.91), channel_id=1, source_target_pairs={{0,12},{4,8},{8,4},{12,0},{1,13},{5,9},{9,5},{13,1},{2,14},{6,10},... | collective-permute-start | bytes 393224 | tf_op jit(solution)/shard_map/ppermute | solution.py:495
  104.7 3.7 %collective-permute-done.31.rest_6_ = bf16[64,1024]{1,0:T(8,128)(2,1)S(1)} collective-permute-done((bf16[64,1024]{1,0:T(8,128)(2,1)S(1)}, bf16[64,1024]{1,0:T(8,128)(2,1)S(1)}, u32[]{:S(2)}, u32[]{:S(2)}) %collective-permute-start.31) | collective-permute-done | bytes 131104 | tf_op jit(solution)/shard_map/ppermute | solution.py:495
  108.4 2.0 %collective-permute-done.32.rest_7_ = bf16[64,1024]{1,0:T(8,128)(2,1)S(1)} collective-permute-done((bf16[64,1024]{1,0:T(8,128)(2,1)S(1)}, bf16[64,1024]{1,0:T(8,128)(2,1)S(1)}, u32[]{:S(2)}, u32[]{:S(2)}) %collective-permute-start.32) | collective-permute-done | bytes 131104 | tf_op jit(solution)/shard_map/ppermute | solution.py:495
  110.9 1.8 %collective-permute-start.37 = (bf16[2,2,32,256]{3,2,1,0:T(8,128)(2,1)S(1)}, bf16[2,2,32,256]{3,2,1,0:T(8,128)(2,1)S(1)}, u32[]{:S(2)}, u32[]{:S(2)}) collective-permute-start(bf16[2,2,32,256]{3,2,1,0:T(8,128)(2,1)S(1)} %get-tuple-element.96), channel_id=1, source_target_pairs={{0,2},{2,0},{1,3},{3,1},{4,6},{6,4},{5,7},{7,5},{8,10},{10,8},{9,1... | collective-permute-start | bytes 196616 | tf_op jit(solution)/shard_map/ppermute | solution.py:495
  113.4 1.8 %collective-permute-done.37.r_ref = bf16[2,2,32,256]{3,2,1,0:T(8,128)(2,1)S(1)} collective-permute-done((bf16[2,2,32,256]{3,2,1,0:T(8,128)(2,1)S(1)}, bf16[2,2,32,256]{3,2,1,0:T(8,128)(2,1)S(1)}, u32[]{:S(2)}, u32[]{:S(2)}) %collective-permute-start.37) | collective-permute-done | bytes 65568 | tf_op jit(solution)/shard_map/ppermute | solution.py:495
  115.2 2.5 %collective-permute-start.38 = (bf16[2,2,32,256]{3,2,1,0:T(8,128)(2,1)S(1)}, bf16[2,2,32,256]{3,2,1,0:T(8,128)(2,1)S(1)}, u32[]{:S(2)}, u32[]{:S(2)}) collective-permute-start(bf16[2,2,32,256]{3,2,1,0:T(8,128)(2,1)S(1)} %shard_map.94.rest_0_), channel_id=1, source_target_pairs={{0,8},{4,12},{8,0},{12,4},{1,9},{5,13},{9,1},{13,5},{2,10},{6,14},... | collective-permute-start | bytes 196616 | tf_op jit(solution)/shard_map/ppermute | solution.py:495
  117.7 2.0 %collective-permute-start.34 = (bf16[2,2,32,256]{3,2,1,0:T(8,128)(2,1)S(1)}, bf16[2,2,32,256]{3,2,1,0:T(8,128)(2,1)S(1)}, u32[]{:S(2)}, u32[]{:S(2)}) collective-permute-start(bf16[2,2,32,256]{3,2,1,0:T(8,128)(2,1)S(1)} %shard_map.93.rest_0_), channel_id=1, source_target_pairs={{0,8},{4,12},{8,0},{12,4},{1,9},{5,13},{9,1},{13,5},{2,10},{6,14},... | collective-permute-start | bytes 196616 | tf_op jit(solution)/shard_map/ppermute | solution.py:495
  119.7 1.7 %collective-permute-start.40 = (bf16[2,2,32,256]{3,2,1,0:T(8,128)(2,1)S(1)}, bf16[2,2,32,256]{3,2,1,0:T(8,128)(2,1)S(1)}, u32[]{:S(2)}, u32[]{:S(2)}) collective-permute-start(bf16[2,2,32,256]{3,2,1,0:T(8,128)(2,1)S(1)} %shard_map.94.rest_0_), channel_id=1, source_target_pairs={{0,4},{4,0},{8,12},{12,8},{1,5},{5,1},{9,13},{13,9},{2,6},{6,2},{1... | collective-permute-start | bytes 196616 | tf_op jit(solution)/shard_map/ppermute | solution.py:495
  121.8 1.7 %collective-permute-start.36 = (bf16[2,2,32,256]{3,2,1,0:T(8,128)(2,1)S(1)}, bf16[2,2,32,256]{3,2,1,0:T(8,128)(2,1)S(1)}, u32[]{:S(2)}, u32[]{:S(2)}) collective-permute-start(bf16[2,2,32,256]{3,2,1,0:T(8,128)(2,1)S(1)} %shard_map.93.rest_0_), channel_id=1, source_target_pairs={{0,4},{4,0},{8,12},{12,8},{1,5},{5,1},{9,13},{13,9},{2,6},{6,2},{1... | collective-permute-start | bytes 196616 | tf_op jit(solution)/shard_map/ppermute | solution.py:495
  125.7 1.9 %shard_map.95.rest_4_ = bf16[64,128,256]{2,1,0:T(8,128)(2,1)} custom-call(s32[1]{0:T(128)} %bitcast._.freq.place_ref, s32[1]{0:T(128)} %bitcast.1.rblk._, s32[1]{0:T(128)} %bitcast.2.__.sblk, bf16[64,128,256]{2,1,0:T(8,128)(2,1)S(1)} %copy-done.1, s32[128,256]{1,0:T(8,128)S(1)} %copy-done.4, bf16[4,128,128]{2,1,0:T(8,128)(2,1)S(1)} %copy-done.5, ...), custom_call_target="tpu_custom_call" | custom-call | flops 33554432 | bytes 8912896 | tf_op jit(solution)/shard_map/pallas_call | solution.py:78
  127.7 1.9 %shard_map.96 = bf16[64,128,256]{2,1,0:T(8,128)(2,1)} custom-call(s32[1]{0:T(128)} %bitcast._.freq.place_ref, s32[1]{0:T(128)} %bitcast.1.rblk._, s32[1]{0:T(128)} %bitcast.2.__.sblk, bf16[64,128,256]{2,1,0:T(8,128)(2,1)S(1)} %copy-done.1, s32[128,256]{1,0:T(8,128)S(1)} %copy-done.4, ...), custom_call_target="tpu_custom_call", output_to_operand_aliasing={{}: (10, {})} | custom-call | flops 33554432 | bytes 13107200 | tf_op jit(solution)/shard_map/pallas_call | solution.py:78
  (89 shorter events, 31.4 us)
Async XLA Ops:
  2.6 21.3 %collective-permute-start.6 = (bf16[2,256,512]{2,1,0:T(8,128)(2,1)S(1)}, bf16[2,256,512]{2,1,0:T(8,128)(2,1)S(1)}, u32[]{:S(2)}, u32[]{:S(2)}) collective-permute-start(bf16[2,256,512]{2,1,0:T(8,128)(2,1)S(1)} %get-tuple-element.66), channel_id=1, source_target_pairs={{0,2},{2,0},{1,3},{3,1},{4,6},{6,4},{5,7},{7,5},{8,10},{10,8},{9,1... | collective-permute-start | bytes 1572872 | tf_op jit(solution)/shard_map/ppermute | solution.py:495
  5.6 26.0 %collective-permute-start.7 = (bf16[2,256,512]{2,1,0:T(8,128)(2,1)S(1)}, bf16[2,256,512]{2,1,0:T(8,128)(2,1)S(1)}, u32[]{:S(2)}, u32[]{:S(2)}) collective-permute-start(bf16[2,256,512]{2,1,0:T(8,128)(2,1)S(1)} %get-tuple-element.69), channel_id=1, source_target_pairs={{0,2},{2,0},{1,3},{3,1},{4,6},{6,4},{5,7},{7,5},{8,10},{10,8},{9,1... | collective-permute-start | bytes 1572872 | tf_op jit(solution)/shard_map/ppermute | solution.py:495
  8.6 12.9 %collective-permute-start.3 = (bf16[2,2,64,256]{3,2,1,0:T(8,128)(2,1)S(1)}, bf16[2,2,64,256]{3,2,1,0:T(8,128)(2,1)S(1)}, u32[]{:S(2)}, u32[]{:S(2)}) collective-permute-start(bf16[2,2,64,256]{3,2,1,0:T(8,128)(2,1)S(1)} %get-tuple-element.59), channel_id=1, source_target_pairs={{0,8},{4,12},{8,0},{12,4},{1,9},{5,13},{9,1},{13,5},{2,10},{6,14},... | collective-permute-start | bytes 393224 | tf_op jit(solution)/shard_map/ppermute | solution.py:495
  11.7 9.8 %collective-permute-start.4 = (bf16[2,2,64,256]{3,2,1,0:T(8,128)(2,1)S(1)}, bf16[2,2,64,256]{3,2,1,0:T(8,128)(2,1)S(1)}, u32[]{:S(2)}, u32[]{:S(2)}) collective-permute-start(bf16[2,2,64,256]{3,2,1,0:T(8,128)(2,1)S(1)} %get-tuple-element.60), channel_id=1, source_target_pairs={{0,12},{4,8},{8,4},{12,0},{1,13},{5,9},{9,5},{13,1},{2,14},{6,10},... | collective-permute-start | bytes 393224 | tf_op jit(solution)/shard_map/ppermute | solution.py:495
  13.1 8.6 %collective-permute-start.5 = (bf16[2,2,64,256]{3,2,1,0:T(8,128)(2,1)S(1)}, bf16[2,2,64,256]{3,2,1,0:T(8,128)(2,1)S(1)}, u32[]{:S(2)}, u32[]{:S(2)}) collective-permute-start(bf16[2,2,64,256]{3,2,1,0:T(8,128)(2,1)S(1)} %get-tuple-element.61), channel_id=1, source_target_pairs={{0,4},{4,0},{8,12},{12,8},{1,5},{5,1},{9,13},{13,9},{2,6},{6,2},{1... | collective-permute-start | bytes 393224 | tf_op jit(solution)/shard_map/ppermute | solution.py:495
  21.8 9.8 %collective-permute-start.8 = (bf16[2,2,64,256]{3,2,1,0:T(8,128)(2,1)S(1)}, bf16[2,2,64,256]{3,2,1,0:T(8,128)(2,1)S(1)}, u32[]{:S(2)}, u32[]{:S(2)}) collective-permute-start(bf16[2,2,64,256]{3,2,1,0:T(8,128)(2,1)S(1)} %get-tuple-element.68.rest_0_), channel_id=1, source_target_pairs={{0,2},{2,0},{1,3},{3,1},{4,6},{6,4},{5,7},{7,5},{8,10},{10,8},{9,1... | collective-permute-start | bytes 393224 | tf_op jit(solution)/shard_map/ppermute | solution.py:495
  23.4 8.2 %collective-permute-start = (bf16[2,256,512]{2,1,0:T(8,128)(2,1)S(1)}, bf16[2,256,512]{2,1,0:T(8,128)(2,1)S(1)}, u32[]{:S(2)}, u32[]{:S(2)}) collective-permute-start(bf16[2,256,512]{2,1,0:T(8,128)(2,1)S(1)} %get-tuple-element.51.rest_1_.rest_0_.rest_2_), channel_id=1, source_target_pairs={{0,1},{1,0},{2,3},{3,2},{4,5},{5,4},{6,7},{7,6},{8,9},{9,8},{10,11... | collective-permute-start | bytes 1572872 | tf_op jit(solution)/shard_map/ppermute | solution.py:495
  23.4 8.2 %collective-permute-start.1 = (bf16[2,256,512]{2,1,0:T(8,128)(2,1)S(1)}, bf16[2,256,512]{2,1,0:T(8,128)(2,1)S(1)}, u32[]{:S(2)}, u32[]{:S(2)}) collective-permute-start(bf16[2,256,512]{2,1,0:T(8,128)(2,1)S(1)} %get-tuple-element.52.rest_3_.rest_2_.rest_4_), channel_id=1, source_target_pairs={{0,1},{1,0},{2,3},{3,2},{4,5},{5,4},{6,7},{7,6},{8,9},{9,8},{10,11... | collective-permute-start | bytes 1572872 | tf_op jit(solution)/shard_map/ppermute | solution.py:495
  23.9 8.5 %collective-permute-start.9 = (bf16[2,256,512]{2,1,0:T(8,128)(2,1)S(1)}, bf16[2,256,512]{2,1,0:T(8,128)(2,1)S(1)}, u32[]{:S(2)}, u32[]{:S(2)}) collective-permute-start(bf16[2,256,512]{2,1,0:T(8,128)(2,1)S(1)} %collective-permute-done.6.rest_2_.rest_0_.rest_3_), channel_id=1, source_target_pairs={{0,1},{1,0},{2,3},{3,2},{4,5},{5,4},{6,7},{7,6},{8,9},{9,8},{10,11... | collective-permute-start | bytes 1572872 | tf_op jit(solution)/shard_map/ppermute | solution.py:495
  34.0 12.9 %collective-permute-start.11 = (bf16[64,1024]{1,0:T(8,128)(2,1)S(1)}, bf16[64,1024]{1,0:T(8,128)(2,1)S(1)}, u32[]{:S(2)}, u32[]{:S(2)}) collective-permute-start(bf16[64,1024]{1,0:T(8,128)(2,1)S(1)} %get-tuple-element.74), channel_id=1, source_target_pairs={{0,8},{4,12},{8,0},{12,4},{1,9},{5,13},{9,1},{13,5},{2,10},{6,14},... | collective-permute-start | bytes 393224 | tf_op jit(solution)/shard_map/ppermute | solution.py:495
  36.9 10.0 %collective-permute-start.12 = (bf16[64,1024]{1,0:T(8,128)(2,1)S(1)}, bf16[64,1024]{1,0:T(8,128)(2,1)S(1)}, u32[]{:S(2)}, u32[]{:S(2)}) collective-permute-start(bf16[64,1024]{1,0:T(8,128)(2,1)S(1)} %get-tuple-element.75), channel_id=1, source_target_pairs={{0,12},{4,8},{8,4},{12,0},{1,13},{5,9},{9,5},{13,1},{2,14},{6,10},... | collective-permute-start | bytes 393224 | tf_op jit(solution)/shard_map/ppermute | solution.py:495
  38.2 9.5 %collective-permute-start.13 = (bf16[64,1024]{1,0:T(8,128)(2,1)S(1)}, bf16[64,1024]{1,0:T(8,128)(2,1)S(1)}, u32[]{:S(2)}, u32[]{:S(2)}) collective-permute-start(bf16[64,1024]{1,0:T(8,128)(2,1)S(1)} %get-tuple-element.76), channel_id=1, source_target_pairs={{0,4},{4,0},{8,12},{12,8},{1,5},{5,1},{9,13},{13,9},{2,6},{6,2},{1... | collective-permute-start | bytes 393224 | tf_op jit(solution)/shard_map/ppermute | solution.py:495
  48.7 13.8 %collective-permute-start.14 = (bf16[64,1024]{1,0:T(8,128)(2,1)S(1)}, bf16[64,1024]{1,0:T(8,128)(2,1)S(1)}, u32[]{:S(2)}, u32[]{:S(2)}) collective-permute-start(bf16[64,1024]{1,0:T(8,128)(2,1)S(1)} %get-tuple-element.78), channel_id=1, source_target_pairs={{0,8},{4,12},{8,0},{12,4},{1,9},{5,13},{9,1},{13,5},{2,10},{6,14},... | collective-permute-start | bytes 393224 | tf_op jit(solution)/shard_map/ppermute | solution.py:495
  52.9 9.6 %collective-permute-start.15 = (bf16[64,1024]{1,0:T(8,128)(2,1)S(1)}, bf16[64,1024]{1,0:T(8,128)(2,1)S(1)}, u32[]{:S(2)}, u32[]{:S(2)}) collective-permute-start(bf16[64,1024]{1,0:T(8,128)(2,1)S(1)} %get-tuple-element.79), channel_id=1, source_target_pairs={{0,12},{4,8},{8,4},{12,0},{1,13},{5,9},{9,5},{13,1},{2,14},{6,10},... | collective-permute-start | bytes 393224 | tf_op jit(solution)/shard_map/ppermute | solution.py:495
  53.3 10.3 %collective-permute-start.16 = (bf16[64,1024]{1,0:T(8,128)(2,1)S(1)}, bf16[64,1024]{1,0:T(8,128)(2,1)S(1)}, u32[]{:S(2)}, u32[]{:S(2)}) collective-permute-start(bf16[64,1024]{1,0:T(8,128)(2,1)S(1)} %get-tuple-element.80), channel_id=1, source_target_pairs={{0,4},{4,0},{8,12},{12,8},{1,5},{5,1},{9,13},{13,9},{2,6},{6,2},{1... | collective-permute-start | bytes 393224 | tf_op jit(solution)/shard_map/ppermute | solution.py:495
  65.7 4.7 %collective-permute-start.21 = (bf16[2,2,32,256]{3,2,1,0:T(8,128)(2,1)S(1)}, bf16[2,2,32,256]{3,2,1,0:T(8,128)(2,1)S(1)}, u32[]{:S(2)}, u32[]{:S(2)}) collective-permute-start(bf16[2,2,32,256]{3,2,1,0:T(8,128)(2,1)S(1)} %get-tuple-element.84), channel_id=1, source_target_pairs={{0,2},{2,0},{1,3},{3,1},{4,6},{6,4},{5,7},{7,5},{8,10},{10,8},{9,1... | collective-permute-start | bytes 196616 | tf_op jit(solution)/shard_map/ppermute | solution.py:495
  68.4 5.7 %collective-permute-start.18 = (bf16[2,2,32,256]{3,2,1,0:T(8,128)(2,1)S(1)}, bf16[2,2,32,256]{3,2,1,0:T(8,128)(2,1)S(1)}, u32[]{:S(2)}, u32[]{:S(2)}) collective-permute-start(bf16[2,2,32,256]{3,2,1,0:T(8,128)(2,1)S(1)} %shard_map.84.rest_0_), channel_id=1, source_target_pairs={{0,8},{4,12},{8,0},{12,4},{1,9},{5,13},{9,1},{13,5},{2,10},{6,14},... | collective-permute-start | bytes 196616 | tf_op jit(solution)/shard_map/ppermute | solution.py:495
  70.4 6.6 %collective-permute-start.22 = (bf16[2,2,32,256]{3,2,1,0:T(8,128)(2,1)S(1)}, bf16[2,2,32,256]{3,2,1,0:T(8,128)(2,1)S(1)}, u32[]{:S(2)}, u32[]{:S(2)}) collective-permute-start(bf16[2,2,32,256]{3,2,1,0:T(8,128)(2,1)S(1)} %shard_map.86.rest_0_), channel_id=1, source_target_pairs={{0,8},{4,12},{8,0},{12,4},{1,9},{5,13},{9,1},{13,5},{2,10},{6,14},... | collective-permute-start | bytes 196616 | tf_op jit(solution)/shard_map/ppermute | solution.py:495
  71.9 7.1 %collective-permute-start.20 = (bf16[2,2,32,256]{3,2,1,0:T(8,128)(2,1)S(1)}, bf16[2,2,32,256]{3,2,1,0:T(8,128)(2,1)S(1)}, u32[]{:S(2)}, u32[]{:S(2)}) collective-permute-start(bf16[2,2,32,256]{3,2,1,0:T(8,128)(2,1)S(1)} %shard_map.84.rest_0_), channel_id=1, source_target_pairs={{0,4},{4,0},{8,12},{12,8},{1,5},{5,1},{9,13},{13,9},{2,6},{6,2},{1... | collective-permute-start | bytes 196616 | tf_op jit(solution)/shard_map/ppermute | solution.py:495
  74.1 5.1 %collective-permute-start.19 = (bf16[2,2,32,256]{3,2,1,0:T(8,128)(2,1)S(1)}, bf16[2,2,32,256]{3,2,1,0:T(8,128)(2,1)S(1)}, u32[]{:S(2)}, u32[]{:S(2)}) collective-permute-start(bf16[2,2,32,256]{3,2,1,0:T(8,128)(2,1)S(1)} %collective-permute-done.18.rest_1_), channel_id=1, source_target_pairs={{0,4},{4,0},{8,12},{12,8},{1,5},{5,1},{9,13},{13,9},{2,6},{6,2},{1... | collective-permute-start | bytes 196616 | tf_op jit(solution)/shard_map/ppermute | solution.py:495
  77.0 4.9 %collective-permute-start.23 = (bf16[2,2,32,256]{3,2,1,0:T(8,128)(2,1)S(1)}, bf16[2,2,32,256]{3,2,1,0:T(8,128)(2,1)S(1)}, u32[]{:S(2)}, u32[]{:S(2)}) collective-permute-start(bf16[2,2,32,256]{3,2,1,0:T(8,128)(2,1)S(1)} %collective-permute-done.22.rest_1_), channel_id=1, source_target_pairs={{0,4},{4,0},{8,12},{12,8},{1,5},{5,1},{9,13},{13,9},{2,6},{6,2},{1... | collective-permute-start | bytes 196616 | tf_op jit(solution)/shard_map/ppermute | solution.py:495
  87.4 8.8 %collective-permute-start.27 = (bf16[64,1024]{1,0:T(8,128)(2,1)S(1)}, bf16[64,1024]{1,0:T(8,128)(2,1)S(1)}, u32[]{:S(2)}, u32[]{:S(2)}) collective-permute-start(bf16[64,1024]{1,0:T(8,128)(2,1)S(1)} %get-tuple-element.86), channel_id=1, source_target_pairs={{0,8},{4,12},{8,0},{12,4},{1,9},{5,13},{9,1},{13,5},{2,10},{6,14},... | collective-permute-start | bytes 393224 | tf_op jit(solution)/shard_map/ppermute | solution.py:495
  88.2 8.1 %collective-permute-start.28 = (bf16[64,1024]{1,0:T(8,128)(2,1)S(1)}, bf16[64,1024]{1,0:T(8,128)(2,1)S(1)}, u32[]{:S(2)}, u32[]{:S(2)}) collective-permute-start(bf16[64,1024]{1,0:T(8,128)(2,1)S(1)} %get-tuple-element.87), channel_id=1, source_target_pairs={{0,12},{4,8},{8,4},{12,0},{1,13},{5,9},{9,5},{13,1},{2,14},{6,10},... | collective-permute-start | bytes 393224 | tf_op jit(solution)/shard_map/ppermute | solution.py:495
  91.2 6.6 %collective-permute-start.29 = (bf16[64,1024]{1,0:T(8,128)(2,1)S(1)}, bf16[64,1024]{1,0:T(8,128)(2,1)S(1)}, u32[]{:S(2)}, u32[]{:S(2)}) collective-permute-start(bf16[64,1024]{1,0:T(8,128)(2,1)S(1)} %get-tuple-element.88), channel_id=1, source_target_pairs={{0,4},{4,0},{8,12},{12,8},{1,5},{5,1},{9,13},{13,9},{2,6},{6,2},{1... | collective-permute-start | bytes 393224 | tf_op jit(solution)/shard_map/ppermute | solution.py:495
  98.8 5.9 %collective-permute-start.30 = (bf16[64,1024]{1,0:T(8,128)(2,1)S(1)}, bf16[64,1024]{1,0:T(8,128)(2,1)S(1)}, u32[]{:S(2)}, u32[]{:S(2)}) collective-permute-start(bf16[64,1024]{1,0:T(8,128)(2,1)S(1)} %get-tuple-element.90), channel_id=1, source_target_pairs={{0,8},{4,12},{8,0},{12,4},{1,9},{5,13},{9,1},{13,5},{2,10},{6,14},... | collective-permute-start | bytes 393224 | tf_op jit(solution)/shard_map/ppermute | solution.py:495
  100.4 7.9 %collective-permute-start.31 = (bf16[64,1024]{1,0:T(8,128)(2,1)S(1)}, bf16[64,1024]{1,0:T(8,128)(2,1)S(1)}, u32[]{:S(2)}, u32[]{:S(2)}) collective-permute-start(bf16[64,1024]{1,0:T(8,128)(2,1)S(1)} %get-tuple-element.91), channel_id=1, source_target_pairs={{0,12},{4,8},{8,4},{12,0},{1,13},{5,9},{9,5},{13,1},{2,14},{6,10},... | collective-permute-start | bytes 393224 | tf_op jit(solution)/shard_map/ppermute | solution.py:495
  103.8 6.6 %collective-permute-start.32 = (bf16[64,1024]{1,0:T(8,128)(2,1)S(1)}, bf16[64,1024]{1,0:T(8,128)(2,1)S(1)}, u32[]{:S(2)}, u32[]{:S(2)}) collective-permute-start(bf16[64,1024]{1,0:T(8,128)(2,1)S(1)} %get-tuple-element.92), channel_id=1, source_target_pairs={{0,4},{4,0},{8,12},{12,8},{1,5},{5,1},{9,13},{13,9},{2,6},{6,2},{1... | collective-permute-start | bytes 393224 | tf_op jit(solution)/shard_map/ppermute | solution.py:495
  112.7 5.0 %collective-permute-start.33 = (bf16[2,2,32,256]{3,2,1,0:T(8,128)(2,1)S(1)}, bf16[2,2,32,256]{3,2,1,0:T(8,128)(2,1)S(1)}, u32[]{:S(2)}, u32[]{:S(2)}) collective-permute-start(bf16[2,2,32,256]{3,2,1,0:T(8,128)(2,1)S(1)} %get-tuple-element.94), channel_id=1, source_target_pairs={{0,2},{2,0},{1,3},{3,1},{4,6},{6,4},{5,7},{7,5},{8,10},{10,8},{9,1... | collective-permute-start | bytes 196616 | tf_op jit(solution)/shard_map/ppermute | solution.py:495
  115.2 6.2 %collective-permute-start.38 = (bf16[2,2,32,256]{3,2,1,0:T(8,128)(2,1)S(1)}, bf16[2,2,32,256]{3,2,1,0:T(8,128)(2,1)S(1)}, u32[]{:S(2)}, u32[]{:S(2)}) collective-permute-start(bf16[2,2,32,256]{3,2,1,0:T(8,128)(2,1)S(1)} %shard_map.94.rest_0_), channel_id=1, source_target_pairs={{0,8},{4,12},{8,0},{12,4},{1,9},{5,13},{9,1},{13,5},{2,10},{6,14},... | collective-permute-start | bytes 196616 | tf_op jit(solution)/shard_map/ppermute | solution.py:495
  117.7 5.7 %collective-permute-start.34 = (bf16[2,2,32,256]{3,2,1,0:T(8,128)(2,1)S(1)}, bf16[2,2,32,256]{3,2,1,0:T(8,128)(2,1)S(1)}, u32[]{:S(2)}, u32[]{:S(2)}) collective-permute-start(bf16[2,2,32,256]{3,2,1,0:T(8,128)(2,1)S(1)} %shard_map.93.rest_0_), channel_id=1, source_target_pairs={{0,8},{4,12},{8,0},{12,4},{1,9},{5,13},{9,1},{13,5},{2,10},{6,14},... | collective-permute-start | bytes 196616 | tf_op jit(solution)/shard_map/ppermute | solution.py:495
  119.7 4.9 %collective-permute-start.40 = (bf16[2,2,32,256]{3,2,1,0:T(8,128)(2,1)S(1)}, bf16[2,2,32,256]{3,2,1,0:T(8,128)(2,1)S(1)}, u32[]{:S(2)}, u32[]{:S(2)}) collective-permute-start(bf16[2,2,32,256]{3,2,1,0:T(8,128)(2,1)S(1)} %shard_map.94.rest_0_), channel_id=1, source_target_pairs={{0,4},{4,0},{8,12},{12,8},{1,5},{5,1},{9,13},{13,9},{2,6},{6,2},{1... | collective-permute-start | bytes 196616 | tf_op jit(solution)/shard_map/ppermute | solution.py:495
  121.8 5.9 %collective-permute-start.36 = (bf16[2,2,32,256]{3,2,1,0:T(8,128)(2,1)S(1)}, bf16[2,2,32,256]{3,2,1,0:T(8,128)(2,1)S(1)}, u32[]{:S(2)}, u32[]{:S(2)}) collective-permute-start(bf16[2,2,32,256]{3,2,1,0:T(8,128)(2,1)S(1)} %shard_map.93.rest_0_), channel_id=1, source_target_pairs={{0,4},{4,0},{8,12},{12,8},{1,5},{5,1},{9,13},{13,9},{2,6},{6,2},{1... | collective-permute-start | bytes 196616 | tf_op jit(solution)/shard_map/ppermute | solution.py:495
  (16 other events, 169.8 us)

commit v15 on v14

--- a/solution.py
+++ b/solution.py
@@ -12,7 +12,7 @@
 BLOCK = 128
 ITERS = 2
 ROWS = 8
-CHUNKS = 2
+CHUNKS = 1
 PARTS = 2
 VMEM_BYTES = 6 * 1024 * 1024
 

time: 130 us -> 132 us (1.015)
  waiting for transfers between devices: 56.2 us -> 73.1 us
  starting transfers between devices: 54.5 us -> 40.5 us
    ppermute x41 -> x32, waiting for transfers between devices: 56.2 us -> 73.1 us  [exchanged(): lax.ppermute(value, axis, [(i, i ^ step) for i in range(lax.axis_size(axi...]
    ppermute x41 -> x32, starting transfers between devices: 54.5 us -> 40.5 us  [exchanged(): lax.ppermute(value, axis, [(i, i ^ step) for i in range(lax.axis_size(axi...]
    pallas_call x24 -> x20, Pallas kernels: 14.2 us -> 13.6 us  [call(): pl.pallas_call(body, grid_spec=pltpu.PrefetchScalarGridSpec(num_scalar_pr...]
  transfers between devices with their start and end apart: 41 -> 32, of which waited for: 22 -> 20; matrix products, arithmetic and copies ran while one was open for 0% -> 0% of each run, Pallas kernels for 6% -> 4%
where the time goes in v15:
time: 132 us
  waiting for transfers between devices  73.1 us (55%)
  starting transfers between devices  40.5 us (31%)
  Pallas kernels  13.6 us (10%)
  local copies, waits for them, and re-layouts  4.56 us (3%)
    ppermute x32, waiting for transfers between devices, exchanged(): lax.ppermute(value, axis, [(i, i ^ step) for i in range(lax.axis_size(axi...  73.1 us
    ppermute x32, starting transfers between devices, exchanged(): lax.ppermute(value, axis, [(i, i ^ step) for i in range(lax.axis_size(axi...  40.5 us
    pallas_call x20, Pallas kernels, call(): pl.pallas_call(body, grid_spec=pltpu.PrefetchScalarGridSpec(num_scalar_pr...  13.6 us
    unnamed x15, local copies, waits for them, and re-layouts  4.56 us
  transfers between devices with their start and end apart: 32, of which 20 were waited for; matrix products, arithmetic and copies ran while one was open for 0% of the time, Pallas kernels for 4%

profile of v15, /device:TPU:0, one launch (start us, length us, event | category | flops | bytes accessed | tf_op | source)
XLA Modules:
  0.0 132.0 jit_solution(3566368845057452369)
XLA Ops:
  0.8 1.6 %copy-done.2 = bf16[2,2,1024,256]{3,2,1,0:T(8,128)(2,1)S(1)} copy-done((bf16[2,2,1024,256]{3,2,1,0:T(8,128)(2,1)S(1)}, bf16[2,2,1024,256]{3,2,1,0:T(8,128)(2,1)}, u32[]{:S(2)}) %copy-start.2) | copy-done | bytes 2097176
  2.6 3.0 %collective-permute-start.6 = (bf16[2,256,512]{2,1,0:T(8,128)(2,1)S(1)}, bf16[2,256,512]{2,1,0:T(8,128)(2,1)S(1)}, u32[]{:S(2)}, u32[]{:S(2)}) collective-permute-start(bf16[2,256,512]{2,1,0:T(8,128)(2,1)S(1)} %get-tuple-element.58), channel_id=1, source_target_pairs={{0,2},{2,0},{1,3},{3,1},{4,6},{6,4},{5,7},{7,5},{8,10},{10,8},{9,1... | collective-permute-start | bytes 1572872 | tf_op jit(solution)/shard_map/ppermute | solution.py:495
  5.7 2.2 %copy-done = bf16[64,128,256]{2,1,0:T(8,128)(2,1)S(1)} copy-done((bf16[64,128,256]{2,1,0:T(8,128)(2,1)S(1)}, bf16[64,128,256]{2,1,0:T(8,128)(2,1)}, u32[]{:S(2)}) %copy-start) | copy-done | bytes 4194328
  8.6 3.1 %collective-permute-start.3 = (bf16[2,2,64,256]{3,2,1,0:T(8,128)(2,1)S(1)}, bf16[2,2,64,256]{3,2,1,0:T(8,128)(2,1)S(1)}, u32[]{:S(2)}, u32[]{:S(2)}) collective-permute-start(bf16[2,2,64,256]{3,2,1,0:T(8,128)(2,1)S(1)} %get-tuple-element.51), channel_id=1, source_target_pairs={{0,8},{4,12},{8,0},{12,4},{1,9},{5,13},{9,1},{13,5},{2,10},{6,14},... | collective-permute-start | bytes 393224 | tf_op jit(solution)/shard_map/ppermute | solution.py:495
  11.7 1.3 %collective-permute-start.4 = (bf16[2,2,64,256]{3,2,1,0:T(8,128)(2,1)S(1)}, bf16[2,2,64,256]{3,2,1,0:T(8,128)(2,1)S(1)}, u32[]{:S(2)}, u32[]{:S(2)}) collective-permute-start(bf16[2,2,64,256]{3,2,1,0:T(8,128)(2,1)S(1)} %get-tuple-element.52), channel_id=1, source_target_pairs={{0,12},{4,8},{8,4},{12,0},{1,13},{5,9},{9,5},{13,1},{2,14},{6,10},... | collective-permute-start | bytes 393224 | tf_op jit(solution)/shard_map/ppermute | solution.py:495
  13.3 8.2 %collective-permute-done.3.refs_1_ = bf16[2,2,64,256]{3,2,1,0:T(8,128)(2,1)S(1)} collective-permute-done((bf16[2,2,64,256]{3,2,1,0:T(8,128)(2,1)S(1)}, bf16[2,2,64,256]{3,2,1,0:T(8,128)(2,1)S(1)}, u32[]{:S(2)}, u32[]{:S(2)}) %collective-permute-start.3) | collective-permute-done | bytes 131104 | tf_op jit(solution)/shard_map/ppermute | solution.py:495
  21.8 1.6 %collective-permute-start.8 = (bf16[2,2,64,256]{3,2,1,0:T(8,128)(2,1)S(1)}, bf16[2,2,64,256]{3,2,1,0:T(8,128)(2,1)S(1)}, u32[]{:S(2)}, u32[]{:S(2)}) collective-permute-start(bf16[2,2,64,256]{3,2,1,0:T(8,128)(2,1)S(1)} %get-tuple-element.60.rest_0_), channel_id=1, source_target_pairs={{0,2},{2,0},{1,3},{3,1},{4,6},{6,4},{5,7},{7,5},{8,10},{10,8},{9,1... | collective-permute-start | bytes 393224 | tf_op jit(solution)/shard_map/ppermute | solution.py:495
  24.0 7.6 %collective-permute-done.8.rest_1_ = bf16[2,2,64,256]{3,2,1,0:T(8,128)(2,1)S(1)} collective-permute-done((bf16[2,2,64,256]{3,2,1,0:T(8,128)(2,1)S(1)}, bf16[2,2,64,256]{3,2,1,0:T(8,128)(2,1)S(1)}, u32[]{:S(2)}, u32[]{:S(2)}) %collective-permute-start.8) | collective-permute-done | bytes 131104 | tf_op jit(solution)/shard_map/ppermute | solution.py:495
  34.0 2.9 %collective-permute-start.11 = (bf16[64,1024]{1,0:T(8,128)(2,1)S(1)}, bf16[64,1024]{1,0:T(8,128)(2,1)S(1)}, u32[]{:S(2)}, u32[]{:S(2)}) collective-permute-start(bf16[64,1024]{1,0:T(8,128)(2,1)S(1)} %get-tuple-element.66), channel_id=1, source_target_pairs={{0,8},{4,12},{8,0},{12,4},{1,9},{5,13},{9,1},{13,5},{2,10},{6,14},... | collective-permute-start | bytes 393224 | tf_op jit(solution)/shard_map/ppermute | solution.py:495
  36.9 1.3 %collective-permute-start.12 = (bf16[64,1024]{1,0:T(8,128)(2,1)S(1)}, bf16[64,1024]{1,0:T(8,128)(2,1)S(1)}, u32[]{:S(2)}, u32[]{:S(2)}) collective-permute-start(bf16[64,1024]{1,0:T(8,128)(2,1)S(1)} %get-tuple-element.67), channel_id=1, source_target_pairs={{0,12},{4,8},{8,4},{12,0},{1,13},{5,9},{9,5},{13,1},{2,14},{6,10},... | collective-permute-start | bytes 393224 | tf_op jit(solution)/shard_map/ppermute | solution.py:495
  39.8 1.4 %shard_map.75 = (f32[4,2,16,1024]{3,2,1,0:T(8,128)S(1)}, f32[4,2,16,1024]{3,2,1,0:T(8,128)S(1)}, f32[16,1024]{1,0:T(8,128)S(1)}, f32[4,2,64,256]{3,2,1,0:T(8,128...) custom-call(s32[1]{0:T(128)} %bitcast._.freq.place_ref, s32[1]{0:T(128)} %bitcast.1.rblk._, ...), custom_call_target="tpu_custom_call" | custom-call | bytes 2424832 | tf_op jit(solution)/shard_map/pallas_call | solution.py:78
  41.1 5.8 %collective-permute-done.11.rest_1_ = bf16[64,1024]{1,0:T(8,128)(2,1)S(1)} collective-permute-done((bf16[64,1024]{1,0:T(8,128)(2,1)S(1)}, bf16[64,1024]{1,0:T(8,128)(2,1)S(1)}, u32[]{:S(2)}, u32[]{:S(2)}) %collective-permute-start.11) | collective-permute-done | bytes 131104 | tf_op jit(solution)/shard_map/ppermute | solution.py:495
  48.7 4.2 %collective-permute-start.14 = (bf16[64,1024]{1,0:T(8,128)(2,1)S(1)}, bf16[64,1024]{1,0:T(8,128)(2,1)S(1)}, u32[]{:S(2)}, u32[]{:S(2)}) collective-permute-start(bf16[64,1024]{1,0:T(8,128)(2,1)S(1)} %get-tuple-element.70), channel_id=1, source_target_pairs={{0,8},{4,12},{8,0},{12,4},{1,9},{5,13},{9,1},{13,5},{2,10},{6,14},... | collective-permute-start | bytes 393224 | tf_op jit(solution)/shard_map/ppermute | solution.py:495
  53.5 9.0 %collective-permute-done.14.rest_5_ = bf16[64,1024]{1,0:T(8,128)(2,1)S(1)} collective-permute-done((bf16[64,1024]{1,0:T(8,128)(2,1)S(1)}, bf16[64,1024]{1,0:T(8,128)(2,1)S(1)}, u32[]{:S(2)}, u32[]{:S(2)}) %collective-permute-start.14) | collective-permute-done | bytes 131104 | tf_op jit(solution)/shard_map/ppermute | solution.py:495
  64.1 1.6 %collective-permute-start.17 = (bf16[2,2,64,256]{3,2,1,0:T(8,128)(2,1)S(1)}, bf16[2,2,64,256]{3,2,1,0:T(8,128)(2,1)S(1)}, u32[]{:S(2)}, u32[]{:S(2)}) collective-permute-start(bf16[2,2,64,256]{3,2,1,0:T(8,128)(2,1)S(1)} %shard_map.83), channel_id=1, source_target_pairs={{0,2},{2,0},{1,3},{3,1},{4,6},{6,4},{5,7},{7,5},{8,10},{10,8},{9,1... | collective-permute-start | bytes 393224 | tf_op jit(solution)/shard_map/ppermute | solution.py:495
  66.1 3.0 %collective-permute-done.17.r_ref = bf16[2,2,64,256]{3,2,1,0:T(8,128)(2,1)S(1)} collective-permute-done((bf16[2,2,64,256]{3,2,1,0:T(8,128)(2,1)S(1)}, bf16[2,2,64,256]{3,2,1,0:T(8,128)(2,1)S(1)}, u32[]{:S(2)}, u32[]{:S(2)}) %collective-permute-start.17) | collective-permute-done | bytes 131104 | tf_op jit(solution)/shard_map/ppermute | solution.py:495
  69.2 1.9 %collective-permute-start.18 = (bf16[2,2,64,256]{3,2,1,0:T(8,128)(2,1)S(1)}, bf16[2,2,64,256]{3,2,1,0:T(8,128)(2,1)S(1)}, u32[]{:S(2)}, u32[]{:S(2)}) collective-permute-start(bf16[2,2,64,256]{3,2,1,0:T(8,128)(2,1)S(1)} %shard_map.84.rest_0_), channel_id=1, source_target_pairs={{0,8},{4,12},{8,0},{12,4},{1,9},{5,13},{9,1},{13,5},{2,10},{6,14},... | collective-permute-start | bytes 393224 | tf_op jit(solution)/shard_map/ppermute | solution.py:495
  71.7 5.3 %collective-permute-done.18.rest_1_ = bf16[2,2,64,256]{3,2,1,0:T(8,128)(2,1)S(1)} collective-permute-done((bf16[2,2,64,256]{3,2,1,0:T(8,128)(2,1)S(1)}, bf16[2,2,64,256]{3,2,1,0:T(8,128)(2,1)S(1)}, u32[]{:S(2)}, u32[]{:S(2)}) %collective-permute-start.18) | collective-permute-done | bytes 131104 | tf_op jit(solution)/shard_map/ppermute | solution.py:495
  78.2 3.7 %collective-permute-done.19.rest_2_ = bf16[2,2,64,256]{3,2,1,0:T(8,128)(2,1)S(1)} collective-permute-done((bf16[2,2,64,256]{3,2,1,0:T(8,128)(2,1)S(1)}, bf16[2,2,64,256]{3,2,1,0:T(8,128)(2,1)S(1)}, u32[]{:S(2)}, u32[]{:S(2)}) %collective-permute-start.19) | collective-permute-done | bytes 131104 | tf_op jit(solution)/shard_map/ppermute | solution.py:495
  82.4 1.6 %collective-permute-start.21 = (bf16[2,2,64,256]{3,2,1,0:T(8,128)(2,1)S(1)}, bf16[2,2,64,256]{3,2,1,0:T(8,128)(2,1)S(1)}, u32[]{:S(2)}, u32[]{:S(2)}) collective-permute-start(bf16[2,2,64,256]{3,2,1,0:T(8,128)(2,1)S(1)} %shard_map.85.rest_0_), channel_id=1, source_target_pairs={{0,2},{2,0},{1,3},{3,1},{4,6},{6,4},{5,7},{7,5},{8,10},{10,8},{9,1... | collective-permute-start | bytes 393224 | tf_op jit(solution)/shard_map/ppermute | solution.py:495
  84.7 2.7 %collective-permute-done.21.rest_1_ = bf16[2,2,64,256]{3,2,1,0:T(8,128)(2,1)S(1)} collective-permute-done((bf16[2,2,64,256]{3,2,1,0:T(8,128)(2,1)S(1)}, bf16[2,2,64,256]{3,2,1,0:T(8,128)(2,1)S(1)}, u32[]{:S(2)}, u32[]{:S(2)}) %collective-permute-start.21) | collective-permute-done | bytes 131104 | tf_op jit(solution)/shard_map/ppermute | solution.py:495
  89.0 3.0 %collective-permute-start.23 = (bf16[64,1024]{1,0:T(8,128)(2,1)S(1)}, bf16[64,1024]{1,0:T(8,128)(2,1)S(1)}, u32[]{:S(2)}, u32[]{:S(2)}) collective-permute-start(bf16[64,1024]{1,0:T(8,128)(2,1)S(1)} %get-tuple-element.75), channel_id=1, source_target_pairs={{0,12},{4,8},{8,4},{12,0},{1,13},{5,9},{9,5},{13,1},{2,14},{6,10},... | collective-permute-start | bytes 393224 | tf_op jit(solution)/shard_map/ppermute | solution.py:495
  92.0 5.3 %collective-permute-done.22.rest_1_ = bf16[64,1024]{1,0:T(8,128)(2,1)S(1)} collective-permute-done((bf16[64,1024]{1,0:T(8,128)(2,1)S(1)}, bf16[64,1024]{1,0:T(8,128)(2,1)S(1)}, u32[]{:S(2)}, u32[]{:S(2)}) %collective-permute-start.22) | collective-permute-done | bytes 131104 | tf_op jit(solution)/shard_map/ppermute | solution.py:495
  99.6 2.4 %collective-permute-start.25 = (bf16[64,1024]{1,0:T(8,128)(2,1)S(1)}, bf16[64,1024]{1,0:T(8,128)(2,1)S(1)}, u32[]{:S(2)}, u32[]{:S(2)}) collective-permute-start(bf16[64,1024]{1,0:T(8,128)(2,1)S(1)} %get-tuple-element.78), channel_id=1, source_target_pairs={{0,8},{4,12},{8,0},{12,4},{1,9},{5,13},{9,1},{13,5},{2,10},{6,14},... | collective-permute-start | bytes 393224 | tf_op jit(solution)/shard_map/ppermute | solution.py:495
  103.2 8.1 %collective-permute-done.25.rest_5_ = bf16[64,1024]{1,0:T(8,128)(2,1)S(1)} collective-permute-done((bf16[64,1024]{1,0:T(8,128)(2,1)S(1)}, bf16[64,1024]{1,0:T(8,128)(2,1)S(1)}, u32[]{:S(2)}, u32[]{:S(2)}) %collective-permute-start.25) | collective-permute-done | bytes 131104 | tf_op jit(solution)/shard_map/ppermute | solution.py:495
  111.9 1.6 %collective-permute-start.28 = (bf16[2,2,64,256]{3,2,1,0:T(8,128)(2,1)S(1)}, bf16[2,2,64,256]{3,2,1,0:T(8,128)(2,1)S(1)}, u32[]{:S(2)}, u32[]{:S(2)}) collective-permute-start(bf16[2,2,64,256]{3,2,1,0:T(8,128)(2,1)S(1)} %shard_map.90), channel_id=1, source_target_pairs={{0,2},{2,0},{1,3},{3,1},{4,6},{6,4},{5,7},{7,5},{8,10},{10,8},{9,1... | collective-permute-start | bytes 393224 | tf_op jit(solution)/shard_map/ppermute | solution.py:495
  113.9 3.0 %collective-permute-done.28.r_ref = bf16[2,2,64,256]{3,2,1,0:T(8,128)(2,1)S(1)} collective-permute-done((bf16[2,2,64,256]{3,2,1,0:T(8,128)(2,1)S(1)}, bf16[2,2,64,256]{3,2,1,0:T(8,128)(2,1)S(1)}, u32[]{:S(2)}, u32[]{:S(2)}) %collective-permute-start.28) | collective-permute-done | bytes 131104 | tf_op jit(solution)/shard_map/ppermute | solution.py:495
  116.9 1.9 %collective-permute-start.29 = (bf16[2,2,64,256]{3,2,1,0:T(8,128)(2,1)S(1)}, bf16[2,2,64,256]{3,2,1,0:T(8,128)(2,1)S(1)}, u32[]{:S(2)}, u32[]{:S(2)}) collective-permute-start(bf16[2,2,64,256]{3,2,1,0:T(8,128)(2,1)S(1)} %shard_map.91.rest_0_), channel_id=1, source_target_pairs={{0,8},{4,12},{8,0},{12,4},{1,9},{5,13},{9,1},{13,5},{2,10},{6,14},... | collective-permute-start | bytes 393224 | tf_op jit(solution)/shard_map/ppermute | solution.py:495
  119.8 3.1 %collective-permute-done.29.rest_1_ = bf16[2,2,64,256]{3,2,1,0:T(8,128)(2,1)S(1)} collective-permute-done((bf16[2,2,64,256]{3,2,1,0:T(8,128)(2,1)S(1)}, bf16[2,2,64,256]{3,2,1,0:T(8,128)(2,1)S(1)}, u32[]{:S(2)}, u32[]{:S(2)}) %collective-permute-start.29) | collective-permute-done | bytes 131104 | tf_op jit(solution)/shard_map/ppermute | solution.py:495
  122.9 2.8 %collective-permute-start.30 = (bf16[2,2,64,256]{3,2,1,0:T(8,128)(2,1)S(1)}, bf16[2,2,64,256]{3,2,1,0:T(8,128)(2,1)S(1)}, u32[]{:S(2)}, u32[]{:S(2)}) collective-permute-start(bf16[2,2,64,256]{3,2,1,0:T(8,128)(2,1)S(1)} %collective-permute-done.29.rest_1_), channel_id=1, source_target_pairs={{0,4},{4,0},{8,12},{12,8},{1,5},{5,1},{9,13},{13,9},{2,6},{6,2},{1... | collective-permute-start | bytes 393224 | tf_op jit(solution)/shard_map/ppermute | solution.py:495
  125.7 2.9 %collective-permute-done.30.rest_2_ = bf16[2,2,64,256]{3,2,1,0:T(8,128)(2,1)S(1)} collective-permute-done((bf16[2,2,64,256]{3,2,1,0:T(8,128)(2,1)S(1)}, bf16[2,2,64,256]{3,2,1,0:T(8,128)(2,1)S(1)}, u32[]{:S(2)}, u32[]{:S(2)}) %collective-permute-start.30) | collective-permute-done | bytes 131104 | tf_op jit(solution)/shard_map/ppermute | solution.py:495
  128.6 3.4 %shard_map.92 = bf16[64,128,256]{2,1,0:T(8,128)(2,1)} custom-call(s32[1]{0:T(128)} %bitcast._.freq.place_ref, s32[1]{0:T(128)} %bitcast.1.rblk._, s32[1]{0:T(128)} %bitcast.2.__.sblk, bf16[64,128,256]{2,1,0:T(8,128)(2,1)S(1)} %copy-done.1, s32[128,256]{1,0:T(8,128)S(1)} %copy-done.4, bf16[4,128,128]{2,1,0:T(8,128)(2,1)S(1)} %copy-done.6, ...), custom_call_target="tpu_custom_call" | custom-call | flops 67108864 | bytes 9175040 | tf_op jit(solution)/shard_map/pallas_call | solution.py:78
  (67 shorter events, 21.4 us)
Async XLA Ops:
  2.6 21.3 %collective-permute-start.6 = (bf16[2,256,512]{2,1,0:T(8,128)(2,1)S(1)}, bf16[2,256,512]{2,1,0:T(8,128)(2,1)S(1)}, u32[]{:S(2)}, u32[]{:S(2)}) collective-permute-start(bf16[2,256,512]{2,1,0:T(8,128)(2,1)S(1)} %get-tuple-element.58), channel_id=1, source_target_pairs={{0,2},{2,0},{1,3},{3,1},{4,6},{6,4},{5,7},{7,5},{8,10},{10,8},{9,1... | collective-permute-start | bytes 1572872 | tf_op jit(solution)/shard_map/ppermute | solution.py:495
  5.6 26.0 %collective-permute-start.7 = (bf16[2,256,512]{2,1,0:T(8,128)(2,1)S(1)}, bf16[2,256,512]{2,1,0:T(8,128)(2,1)S(1)}, u32[]{:S(2)}, u32[]{:S(2)}) collective-permute-start(bf16[2,256,512]{2,1,0:T(8,128)(2,1)S(1)} %get-tuple-element.61), channel_id=1, source_target_pairs={{0,2},{2,0},{1,3},{3,1},{4,6},{6,4},{5,7},{7,5},{8,10},{10,8},{9,1... | collective-permute-start | bytes 1572872 | tf_op jit(solution)/shard_map/ppermute | solution.py:495
  8.6 12.9 %collective-permute-start.3 = (bf16[2,2,64,256]{3,2,1,0:T(8,128)(2,1)S(1)}, bf16[2,2,64,256]{3,2,1,0:T(8,128)(2,1)S(1)}, u32[]{:S(2)}, u32[]{:S(2)}) collective-permute-start(bf16[2,2,64,256]{3,2,1,0:T(8,128)(2,1)S(1)} %get-tuple-element.51), channel_id=1, source_target_pairs={{0,8},{4,12},{8,0},{12,4},{1,9},{5,13},{9,1},{13,5},{2,10},{6,14},... | collective-permute-start | bytes 393224 | tf_op jit(solution)/shard_map/ppermute | solution.py:495
  11.7 9.8 %collective-permute-start.4 = (bf16[2,2,64,256]{3,2,1,0:T(8,128)(2,1)S(1)}, bf16[2,2,64,256]{3,2,1,0:T(8,128)(2,1)S(1)}, u32[]{:S(2)}, u32[]{:S(2)}) collective-permute-start(bf16[2,2,64,256]{3,2,1,0:T(8,128)(2,1)S(1)} %get-tuple-element.52), channel_id=1, source_target_pairs={{0,12},{4,8},{8,4},{12,0},{1,13},{5,9},{9,5},{13,1},{2,14},{6,10},... | collective-permute-start | bytes 393224 | tf_op jit(solution)/shard_map/ppermute | solution.py:495
  13.1 8.6 %collective-permute-start.5 = (bf16[2,2,64,256]{3,2,1,0:T(8,128)(2,1)S(1)}, bf16[2,2,64,256]{3,2,1,0:T(8,128)(2,1)S(1)}, u32[]{:S(2)}, u32[]{:S(2)}) collective-permute-start(bf16[2,2,64,256]{3,2,1,0:T(8,128)(2,1)S(1)} %get-tuple-element.53), channel_id=1, source_target_pairs={{0,4},{4,0},{8,12},{12,8},{1,5},{5,1},{9,13},{13,9},{2,6},{6,2},{1... | collective-permute-start | bytes 393224 | tf_op jit(solution)/shard_map/ppermute | solution.py:495
  21.8 9.8 %collective-permute-start.8 = (bf16[2,2,64,256]{3,2,1,0:T(8,128)(2,1)S(1)}, bf16[2,2,64,256]{3,2,1,0:T(8,128)(2,1)S(1)}, u32[]{:S(2)}, u32[]{:S(2)}) collective-permute-start(bf16[2,2,64,256]{3,2,1,0:T(8,128)(2,1)S(1)} %get-tuple-element.60.rest_0_), channel_id=1, source_target_pairs={{0,2},{2,0},{1,3},{3,1},{4,6},{6,4},{5,7},{7,5},{8,10},{10,8},{9,1... | collective-permute-start | bytes 393224 | tf_op jit(solution)/shard_map/ppermute | solution.py:495
  23.4 8.2 %collective-permute-start = (bf16[2,256,512]{2,1,0:T(8,128)(2,1)S(1)}, bf16[2,256,512]{2,1,0:T(8,128)(2,1)S(1)}, u32[]{:S(2)}, u32[]{:S(2)}) collective-permute-start(bf16[2,256,512]{2,1,0:T(8,128)(2,1)S(1)} %get-tuple-element.43.rest_1_.rest_0_), channel_id=1, source_target_pairs={{0,1},{1,0},{2,3},{3,2},{4,5},{5,4},{6,7},{7,6},{8,9},{9,8},{10,11... | collective-permute-start | bytes 1572872 | tf_op jit(solution)/shard_map/ppermute | solution.py:495
  23.4 8.2 %collective-permute-start.1 = (bf16[2,256,512]{2,1,0:T(8,128)(2,1)S(1)}, bf16[2,256,512]{2,1,0:T(8,128)(2,1)S(1)}, u32[]{:S(2)}, u32[]{:S(2)}) collective-permute-start(bf16[2,256,512]{2,1,0:T(8,128)(2,1)S(1)} %get-tuple-element.44.rest_3_.rest_2_), channel_id=1, source_target_pairs={{0,1},{1,0},{2,3},{3,2},{4,5},{5,4},{6,7},{7,6},{8,9},{9,8},{10,11... | collective-permute-start | bytes 1572872 | tf_op jit(solution)/shard_map/ppermute | solution.py:495
  23.9 8.5 %collective-permute-start.9 = (bf16[2,256,512]{2,1,0:T(8,128)(2,1)S(1)}, bf16[2,256,512]{2,1,0:T(8,128)(2,1)S(1)}, u32[]{:S(2)}, u32[]{:S(2)}) collective-permute-start(bf16[2,256,512]{2,1,0:T(8,128)(2,1)S(1)} %collective-permute-done.6.rest_2_.rest_0_), channel_id=1, source_target_pairs={{0,1},{1,0},{2,3},{3,2},{4,5},{5,4},{6,7},{7,6},{8,9},{9,8},{10,11... | collective-permute-start | bytes 1572872 | tf_op jit(solution)/shard_map/ppermute | solution.py:495
  31.5 1.9 %collective-permute-start.10 = (bf16[2,256,512]{2,1,0:T(8,128)(2,1)S(1)}, bf16[2,256,512]{2,1,0:T(8,128)(2,1)S(1)}, u32[]{:S(2)}, u32[]{:S(2)}) collective-permute-start(bf16[2,256,512]{2,1,0:T(8,128)(2,1)S(1)} %collective-permute-done.7.rest_2_.rest_4_), channel_id=1, source_target_pairs={{0,1},{1,0},{2,3},{3,2},{4,5},{5,4},{6,7},{7,6},{8,9},{9,8},{10,11... | collective-permute-start | bytes 1572872 | tf_op jit(solution)/shard_map/ppermute | solution.py:495
  34.0 12.9 %collective-permute-start.11 = (bf16[64,1024]{1,0:T(8,128)(2,1)S(1)}, bf16[64,1024]{1,0:T(8,128)(2,1)S(1)}, u32[]{:S(2)}, u32[]{:S(2)}) collective-permute-start(bf16[64,1024]{1,0:T(8,128)(2,1)S(1)} %get-tuple-element.66), channel_id=1, source_target_pairs={{0,8},{4,12},{8,0},{12,4},{1,9},{5,13},{9,1},{13,5},{2,10},{6,14},... | collective-permute-start | bytes 393224 | tf_op jit(solution)/shard_map/ppermute | solution.py:495
  36.9 10.0 %collective-permute-start.12 = (bf16[64,1024]{1,0:T(8,128)(2,1)S(1)}, bf16[64,1024]{1,0:T(8,128)(2,1)S(1)}, u32[]{:S(2)}, u32[]{:S(2)}) collective-permute-start(bf16[64,1024]{1,0:T(8,128)(2,1)S(1)} %get-tuple-element.67), channel_id=1, source_target_pairs={{0,12},{4,8},{8,4},{12,0},{1,13},{5,9},{9,5},{13,1},{2,14},{6,10},... | collective-permute-start | bytes 393224 | tf_op jit(solution)/shard_map/ppermute | solution.py:495
  38.2 9.5 %collective-permute-start.13 = (bf16[64,1024]{1,0:T(8,128)(2,1)S(1)}, bf16[64,1024]{1,0:T(8,128)(2,1)S(1)}, u32[]{:S(2)}, u32[]{:S(2)}) collective-permute-start(bf16[64,1024]{1,0:T(8,128)(2,1)S(1)} %get-tuple-element.68), channel_id=1, source_target_pairs={{0,4},{4,0},{8,12},{12,8},{1,5},{5,1},{9,13},{13,9},{2,6},{6,2},{1... | collective-permute-start | bytes 393224 | tf_op jit(solution)/shard_map/ppermute | solution.py:495
  38.5 1.3 collective-permute-start.2
  48.7 13.8 %collective-permute-start.14 = (bf16[64,1024]{1,0:T(8,128)(2,1)S(1)}, bf16[64,1024]{1,0:T(8,128)(2,1)S(1)}, u32[]{:S(2)}, u32[]{:S(2)}) collective-permute-start(bf16[64,1024]{1,0:T(8,128)(2,1)S(1)} %get-tuple-element.70), channel_id=1, source_target_pairs={{0,8},{4,12},{8,0},{12,4},{1,9},{5,13},{9,1},{13,5},{2,10},{6,14},... | collective-permute-start | bytes 393224 | tf_op jit(solution)/shard_map/ppermute | solution.py:495
  52.9 9.6 %collective-permute-start.15 = (bf16[64,1024]{1,0:T(8,128)(2,1)S(1)}, bf16[64,1024]{1,0:T(8,128)(2,1)S(1)}, u32[]{:S(2)}, u32[]{:S(2)}) collective-permute-start(bf16[64,1024]{1,0:T(8,128)(2,1)S(1)} %get-tuple-element.71), channel_id=1, source_target_pairs={{0,12},{4,8},{8,4},{12,0},{1,13},{5,9},{9,5},{13,1},{2,14},{6,10},... | collective-permute-start | bytes 393224 | tf_op jit(solution)/shard_map/ppermute | solution.py:495
  53.3 10.3 %collective-permute-start.16 = (bf16[64,1024]{1,0:T(8,128)(2,1)S(1)}, bf16[64,1024]{1,0:T(8,128)(2,1)S(1)}, u32[]{:S(2)}, u32[]{:S(2)}) collective-permute-start(bf16[64,1024]{1,0:T(8,128)(2,1)S(1)} %get-tuple-element.72), channel_id=1, source_target_pairs={{0,4},{4,0},{8,12},{12,8},{1,5},{5,1},{9,13},{13,9},{2,6},{6,2},{1... | collective-permute-start | bytes 393224 | tf_op jit(solution)/shard_map/ppermute | solution.py:495
  64.1 5.0 %collective-permute-start.17 = (bf16[2,2,64,256]{3,2,1,0:T(8,128)(2,1)S(1)}, bf16[2,2,64,256]{3,2,1,0:T(8,128)(2,1)S(1)}, u32[]{:S(2)}, u32[]{:S(2)}) collective-permute-start(bf16[2,2,64,256]{3,2,1,0:T(8,128)(2,1)S(1)} %shard_map.83), channel_id=1, source_target_pairs={{0,2},{2,0},{1,3},{3,1},{4,6},{6,4},{5,7},{7,5},{8,10},{10,8},{9,1... | collective-permute-start | bytes 393224 | tf_op jit(solution)/shard_map/ppermute | solution.py:495
  69.2 7.8 %collective-permute-start.18 = (bf16[2,2,64,256]{3,2,1,0:T(8,128)(2,1)S(1)}, bf16[2,2,64,256]{3,2,1,0:T(8,128)(2,1)S(1)}, u32[]{:S(2)}, u32[]{:S(2)}) collective-permute-start(bf16[2,2,64,256]{3,2,1,0:T(8,128)(2,1)S(1)} %shard_map.84.rest_0_), channel_id=1, source_target_pairs={{0,8},{4,12},{8,0},{12,4},{1,9},{5,13},{9,1},{13,5},{2,10},{6,14},... | collective-permute-start | bytes 393224 | tf_op jit(solution)/shard_map/ppermute | solution.py:495
  71.1 7.1 %collective-permute-start.20 = (bf16[2,2,64,256]{3,2,1,0:T(8,128)(2,1)S(1)}, bf16[2,2,64,256]{3,2,1,0:T(8,128)(2,1)S(1)}, u32[]{:S(2)}, u32[]{:S(2)}) collective-permute-start(bf16[2,2,64,256]{3,2,1,0:T(8,128)(2,1)S(1)} %shard_map.84.rest_0_), channel_id=1, source_target_pairs={{0,4},{4,0},{8,12},{12,8},{1,5},{5,1},{9,13},{13,9},{2,6},{6,2},{1... | collective-permute-start | bytes 393224 | tf_op jit(solution)/shard_map/ppermute | solution.py:495
  77.0 5.0 %collective-permute-start.19 = (bf16[2,2,64,256]{3,2,1,0:T(8,128)(2,1)S(1)}, bf16[2,2,64,256]{3,2,1,0:T(8,128)(2,1)S(1)}, u32[]{:S(2)}, u32[]{:S(2)}) collective-permute-start(bf16[2,2,64,256]{3,2,1,0:T(8,128)(2,1)S(1)} %collective-permute-done.18.rest_1_), channel_id=1, source_target_pairs={{0,4},{4,0},{8,12},{12,8},{1,5},{5,1},{9,13},{13,9},{2,6},{6,2},{1... | collective-permute-start | bytes 393224 | tf_op jit(solution)/shard_map/ppermute | solution.py:495
  82.4 5.0 %collective-permute-start.21 = (bf16[2,2,64,256]{3,2,1,0:T(8,128)(2,1)S(1)}, bf16[2,2,64,256]{3,2,1,0:T(8,128)(2,1)S(1)}, u32[]{:S(2)}, u32[]{:S(2)}) collective-permute-start(bf16[2,2,64,256]{3,2,1,0:T(8,128)(2,1)S(1)} %shard_map.85.rest_0_), channel_id=1, source_target_pairs={{0,2},{2,0},{1,3},{3,1},{4,6},{6,4},{5,7},{7,5},{8,10},{10,8},{9,1... | collective-permute-start | bytes 393224 | tf_op jit(solution)/shard_map/ppermute | solution.py:495
  88.3 9.0 %collective-permute-start.22 = (bf16[64,1024]{1,0:T(8,128)(2,1)S(1)}, bf16[64,1024]{1,0:T(8,128)(2,1)S(1)}, u32[]{:S(2)}, u32[]{:S(2)}) collective-permute-start(bf16[64,1024]{1,0:T(8,128)(2,1)S(1)} %get-tuple-element.74), channel_id=1, source_target_pairs={{0,8},{4,12},{8,0},{12,4},{1,9},{5,13},{9,1},{13,5},{2,10},{6,14},... | collective-permute-start | bytes 393224 | tf_op jit(solution)/shard_map/ppermute | solution.py:495
  89.0 8.3 %collective-permute-start.23 = (bf16[64,1024]{1,0:T(8,128)(2,1)S(1)}, bf16[64,1024]{1,0:T(8,128)(2,1)S(1)}, u32[]{:S(2)}, u32[]{:S(2)}) collective-permute-start(bf16[64,1024]{1,0:T(8,128)(2,1)S(1)} %get-tuple-element.75), channel_id=1, source_target_pairs={{0,12},{4,8},{8,4},{12,0},{1,13},{5,9},{9,5},{13,1},{2,14},{6,10},... | collective-permute-start | bytes 393224 | tf_op jit(solution)/shard_map/ppermute | solution.py:495
  92.0 6.6 %collective-permute-start.24 = (bf16[64,1024]{1,0:T(8,128)(2,1)S(1)}, bf16[64,1024]{1,0:T(8,128)(2,1)S(1)}, u32[]{:S(2)}, u32[]{:S(2)}) collective-permute-start(bf16[64,1024]{1,0:T(8,128)(2,1)S(1)} %get-tuple-element.76), channel_id=1, source_target_pairs={{0,4},{4,0},{8,12},{12,8},{1,5},{5,1},{9,13},{13,9},{2,6},{6,2},{1... | collective-permute-start | bytes 393224 | tf_op jit(solution)/shard_map/ppermute | solution.py:495
  99.6 11.6 %collective-permute-start.25 = (bf16[64,1024]{1,0:T(8,128)(2,1)S(1)}, bf16[64,1024]{1,0:T(8,128)(2,1)S(1)}, u32[]{:S(2)}, u32[]{:S(2)}) collective-permute-start(bf16[64,1024]{1,0:T(8,128)(2,1)S(1)} %get-tuple-element.78), channel_id=1, source_target_pairs={{0,8},{4,12},{8,0},{12,4},{1,9},{5,13},{9,1},{13,5},{2,10},{6,14},... | collective-permute-start | bytes 393224 | tf_op jit(solution)/shard_map/ppermute | solution.py:495
  102.0 9.3 %collective-permute-start.26 = (bf16[64,1024]{1,0:T(8,128)(2,1)S(1)}, bf16[64,1024]{1,0:T(8,128)(2,1)S(1)}, u32[]{:S(2)}, u32[]{:S(2)}) collective-permute-start(bf16[64,1024]{1,0:T(8,128)(2,1)S(1)} %get-tuple-element.79), channel_id=1, source_target_pairs={{0,12},{4,8},{8,4},{12,0},{1,13},{5,9},{9,5},{13,1},{2,14},{6,10},... | collective-permute-start | bytes 393224 | tf_op jit(solution)/shard_map/ppermute | solution.py:495
  102.6 8.8 %collective-permute-start.27 = (bf16[64,1024]{1,0:T(8,128)(2,1)S(1)}, bf16[64,1024]{1,0:T(8,128)(2,1)S(1)}, u32[]{:S(2)}, u32[]{:S(2)}) collective-permute-start(bf16[64,1024]{1,0:T(8,128)(2,1)S(1)} %get-tuple-element.80), channel_id=1, source_target_pairs={{0,4},{4,0},{8,12},{12,8},{1,5},{5,1},{9,13},{13,9},{2,6},{6,2},{1... | collective-permute-start | bytes 393224 | tf_op jit(solution)/shard_map/ppermute | solution.py:495
  111.9 5.0 %collective-permute-start.28 = (bf16[2,2,64,256]{3,2,1,0:T(8,128)(2,1)S(1)}, bf16[2,2,64,256]{3,2,1,0:T(8,128)(2,1)S(1)}, u32[]{:S(2)}, u32[]{:S(2)}) collective-permute-start(bf16[2,2,64,256]{3,2,1,0:T(8,128)(2,1)S(1)} %shard_map.90), channel_id=1, source_target_pairs={{0,2},{2,0},{1,3},{3,1},{4,6},{6,4},{5,7},{7,5},{8,10},{10,8},{9,1... | collective-permute-start | bytes 393224 | tf_op jit(solution)/shard_map/ppermute | solution.py:495
  116.9 6.0 %collective-permute-start.29 = (bf16[2,2,64,256]{3,2,1,0:T(8,128)(2,1)S(1)}, bf16[2,2,64,256]{3,2,1,0:T(8,128)(2,1)S(1)}, u32[]{:S(2)}, u32[]{:S(2)}) collective-permute-start(bf16[2,2,64,256]{3,2,1,0:T(8,128)(2,1)S(1)} %shard_map.91.rest_0_), channel_id=1, source_target_pairs={{0,8},{4,12},{8,0},{12,4},{1,9},{5,13},{9,1},{13,5},{2,10},{6,14},... | collective-permute-start | bytes 393224 | tf_op jit(solution)/shard_map/ppermute | solution.py:495
  118.8 6.8 %collective-permute-start.31 = (bf16[2,2,64,256]{3,2,1,0:T(8,128)(2,1)S(1)}, bf16[2,2,64,256]{3,2,1,0:T(8,128)(2,1)S(1)}, u32[]{:S(2)}, u32[]{:S(2)}) collective-permute-start(bf16[2,2,64,256]{3,2,1,0:T(8,128)(2,1)S(1)} %shard_map.91.rest_0_), channel_id=1, source_target_pairs={{0,4},{4,0},{8,12},{12,8},{1,5},{5,1},{9,13},{13,9},{2,6},{6,2},{1... | collective-permute-start | bytes 393224 | tf_op jit(solution)/shard_map/ppermute | solution.py:495
  122.9 5.7 %collective-permute-start.30 = (bf16[2,2,64,256]{3,2,1,0:T(8,128)(2,1)S(1)}, bf16[2,2,64,256]{3,2,1,0:T(8,128)(2,1)S(1)}, u32[]{:S(2)}, u32[]{:S(2)}) collective-permute-start(bf16[2,2,64,256]{3,2,1,0:T(8,128)(2,1)S(1)} %collective-permute-done.29.rest_1_), channel_id=1, source_target_pairs={{0,4},{4,0},{8,12},{12,8},{1,5},{5,1},{9,13},{13,9},{2,6},{6,2},{1... | collective-permute-start | bytes 393224 | tf_op jit(solution)/shard_map/ppermute | solution.py:495
  (7 other events, 140.3 us)

commit v16 on v14

--- a/solution.py
+++ b/solution.py
@@ -196,12 +196,19 @@
 
 
 def added(keep, received):
-    def body(k_ref, r_ref, out):
-        out[...] = (k_ref[...] + r_ref[...].astype(F32)).astype(BF16)
-
-    shape = jax.ShapeDtypeStruct(keep.shape, BF16)
-    (out,) = call(body, (), [(v, whole(v)) for v in (keep, received)], [(shape, whole(shape))], (1,))
-    return out
+    lead, rows, rcv = keep.shape[:2], keep.shape[2], keep.shape[3]
+    group = rows // CHUNKS
+
+    def body(k_ref, r_ref, out, *groups):
+        total = (k_ref[...] + r_ref[...].astype(F32)).astype(BF16)
+        out[...] = total
+        for index, ref in enumerate(groups):
+            ref[...] = total[:, :, index * group : (index + 1) * group]
+
+    shapes = [jax.ShapeDtypeStruct(lead + (count, rcv), BF16) for count in [rows] + [group] * CHUNKS]
+    inputs = [(v, whole(v)) for v in (keep, received)]
+    outs = call(body, (), inputs, [(v, whole(v)) for v in shapes], (1,))
+    return outs[0], outs[1:]
 
 
 def src_onsets(onset, places, half_rows, share, width):
@@ -245,8 +252,7 @@
 
 
 def down_products(before, spectra, parts, side, first, freq_place, freq_devs=0):
-    _, per_dev, _, rcv = spectra[0].shape
-    rows = sum(v.shape[2] for v in spectra)
+    _, per_dev, rows, rcv = spectra.shape
     flat = [pair[side] for part in parts for pair in part]
     width = flat[0].shape[1]
     total_width = before.shape[-1] if before is not None else first + width * len(flat)
@@ -255,14 +261,13 @@
 
     def body(place_ref, *rest):
         held_ref, rest = (rest[0], rest[1:]) if old else (None, rest)
-        refs, resp, outs = rest[: len(spectra)], rest[len(spectra) : len(spectra) + len(flat)], rest[len(spectra) + len(flat) :]
+        ref, resp, outs = rest[0], rest[1 : 1 + len(flat)], rest[1 + len(flat) :]
         held = outs[-1]
         for j in range(per_dev):
-            real = jnp.concatenate([ref[0, j] for ref in refs], 0)
-            imag = jnp.concatenate([ref[1, j] for ref in refs], 0)
+            real, imag = ref[0, j], ref[1, j]
             lhs = jnp.concatenate([jnp.concatenate([real, -imag], 1), jnp.concatenate([imag, real], 1)], 0)
-            for at, ref in enumerate(resp):
-                total = lax.dot_general(lhs, ref[j], (((1,), (1,)), ((), ())), preferred_element_type=F32)
+            for at, block in enumerate(resp):
+                total = lax.dot_general(lhs, block[j], (((1,), (1,)), ((), ())), preferred_element_type=F32)
                 to = slice(first + at * width, first + (at + 1) * width)
                 for part in range(2):
                     value = total[part * rows : (part + 1) * rows]
@@ -284,7 +289,7 @@
     outs = call(
         body,
         (freq_place,),
-        [(v, whole(v)) for v in (*old, *spectra, *flat)],
+        [(v, whole(v)) for v in (*old, spectra, *flat)],
         [(v, whole(v)) for v in shapes],
         (1,),
         scratch=[pltpu.VMEM(sums, F32)] if freq_devs else [],
@@ -360,14 +365,13 @@
     freq_devs = len(messages)
     flat = [pair[side] for part in parts for pair in part]
     per_dev, src, rcv = flat[0].shape[0], flat[0].shape[1], flat[0].shape[2] // 2
-    group = rows // CHUNKS
     share = rows // freq_devs
     total_width = src * len(flat)
     kind = BF16 if side else F32
 
     def body(place_ref, *rest):
         resp, refs = rest[: len(flat)], rest[len(flat) : len(flat) + freq_devs]
-        outs, held = rest[len(flat) + freq_devs : -1], rest[-1]
+        out, held = rest[len(flat) + freq_devs :]
         for way, ref in zip(ways(freq_devs), refs):
             start = pl.multiple_of((place_ref[0] ^ way) * share, share)
             value = ref[...].reshape(2, per_dev, share, total_width)
@@ -380,44 +384,51 @@
                 jnp.dot(both[:, at * src : (at + 1) * src], ref[j], preferred_element_type=F32)
                 for at, ref in enumerate(resp)
             )
-            real = total[:rows, :rcv] + total[rows:, rcv:]
-            imag = total[rows:, :rcv] - total[:rows, rcv:]
-            for index, out in enumerate(outs):
-                cut = slice(index * group, (index + 1) * group)
-                out[0, j] = real[cut].astype(kind)
-                out[1, j] = imag[cut].astype(kind)
-
-    shape = jax.ShapeDtypeStruct((2, per_dev, group, rcv), kind)
-    return call(
+            out[0, j] = (total[:rows, :rcv] + total[rows:, rcv:]).astype(kind)
+            out[1, j] = (total[rows:, :rcv] - total[:rows, rcv:]).astype(kind)
+
+    shape = jax.ShapeDtypeStruct((2, per_dev, rows, rcv), kind)
+    (out,) = call(
         body,
         (freq_place,),
         [(v, whole(v)) for v in (*flat, *messages)],
-        [(shape, whole(shape))] * CHUNKS,
+        [(shape, whole(shape))],
         (1,),
         scratch=[pltpu.VMEM((2, per_dev, rows, total_width), BF16)],
         flops=2 * 4 * per_dev * rows * total_width * rcv,
     )
-
-
-def next_spectra(sums, messages, tables, matrix, freq_place, first_row):
+    return out
+
+
+def piece(ref, index, group, cut):
+    first = index * group if ref.shape[2] > group else 0
+    return slice(first + cut.start, first + cut.stop)
+
+
+def next_spectra(sums, by_group, tables, matrix, freq_place):
     cosines, sines, fraction = tables
-    freq_devs = len(messages)
-    _, per_dev, rows, rcv = messages[0].shape
+    freq_devs = len(by_group[0])
+    _, per_dev, rows, rcv = sums.shape
+    group = rows // len(by_group)
+    flat = [v for messages in by_group for v in messages]
     count = freq_devs * 2 * per_dev * ROWS
     own = 2 * per_dev * ROWS
 
     def body(place_ref, u_ref, c_ref, s_ref, f_ref, g_ref, *rest):
-        refs, out = rest[:freq_devs], rest[freq_devs]
+        out = rest[-1]
         matrix_here = g_ref[place_ref[0], :own]
 
         def one(at):
             for base in range(0, rows, 2 * ROWS):
                 pair = slice(base, base + 2 * ROWS)
-                data = [ref[:, :, pair, at].astype(F32) for ref in refs]
+                index = base // group
+                refs = rest[index * freq_devs : (index + 1) * freq_devs]
+                local = slice(base - index * group, base - index * group + 2 * ROWS)
+                data = [ref[:, :, piece(ref, index, group, local), at].astype(F32) for ref in refs]
                 made = []
                 for half in range(2):
                     plain = [value[:, :, half * ROWS : (half + 1) * ROWS] for value in data]
-                    cut = slice(first_row + base + half * ROWS, first_row + base + (half + 1) * ROWS)
+                    cut = slice(base + half * ROWS, base + (half + 1) * ROWS)
                     cos = [c_ref[step, :, cut, at] for step in range(freq_devs)]
                     sin = [s_ref[step, :, cut, at] for step in range(freq_devs)]
                     up, low = mixed_fields(plain, cos, sin, matrix_here)
@@ -427,8 +438,8 @@
 
         tiles(rcv, one)
 
-    inputs = (sums, cosines, sines, fraction, matrix, *messages)
-    shape = jax.ShapeDtypeStruct(messages[0].shape, BF16)
+    inputs = (sums, cosines, sines, fraction, matrix, *flat)
+    shape = jax.ShapeDtypeStruct(sums.shape, BF16)
     (out,) = call(
         body,
         (freq_place,),
@@ -459,8 +470,11 @@
             for row in range(ROWS):
                 spread_ref[row * own : (row + 1) * own] = jnp.where(lane == row, base, 0.0).astype(BF16)
 
-        here = pl.ds(pl.multiple_of(step * tile, tile), tile)
-        data = [ref[:, :, here, :].astype(F32) for ref in refs]
+        data = []
+        for ref in refs:
+            skip = first if ref.shape[2] > rows else 0
+            here = pl.ds(pl.multiple_of(skip + step * tile, tile), tile)
+            data.append(ref[:, :, here, :].astype(F32))
         onsets = o_ref[pl.ds(pl.multiple_of(sblk[0] * half_rows + first + step * tile, tile), tile), :]
         time = lax.broadcasted_iota(jnp.int32, (own, rcv), 0) + place_ref[0] * own
         for half in range(2):
@@ -499,13 +513,16 @@
     return [exchanged(part, "freq", step) if step else part for part, step in zip(parts, ways(len(parts)))]
 
 
-def spread(value, count):
-    held = {0: value}
-    bit = count // 2
+def spread(value, groups, count):
+    top = count // 2
+    far = [{top: exchanged(group, "freq", top)} for group in groups]
+    near = {0: value}
+    bit = top // 2
     while bit:
-        held.update({way | bit: exchanged(held[way], "freq", bit) for way in sorted(held)})
+        for held in (near, *far):
+            held.update({way | bit: exchanged(held[way], "freq", bit) for way in sorted(held)})
         bit //= 2
-    return [held[way] for way in ways(count)]
+    return [[{**near, **held}[way] for way in ways(count)] for held in far]
 
 
 def on_device(initial, response, aperture, onset_rcv, onset_src):
@@ -539,7 +556,7 @@
     onsets = (own, exchanged(other, "sblk", 1))
     src_tables, rcv_tables = phase_tables(onsets, onset_rcv, places, freq_devs, per_dev, samples, PARTS, half_rows)
 
-    near, far, result = [spectra], [far], None
+    near, result = spectra, None
     for step in range(ITERS):
         held = down_products(None, near, parts, 0, 0, freq_place)
         at = 0 if step else PARTS - 1
@@ -548,16 +565,15 @@
         first = at * 2 * kept[0].shape[1]
         messages = dealt_out(down_products(held, far, parts[at:], 1, first, freq_place, freq_devs))
         messages = dealt_out(windowed(messages, src_tables, matrix, freq_place, per_dev, share))
-        received = [exchanged(v, "rblk", 1) for v in up_products(messages, parts, freq_place, half_rows, 1)]
+        received = exchanged(up_products(messages, parts, freq_place, half_rows, 1), "rblk", 1)
         keep = up_products(messages, parts, freq_place, half_rows, 0)
-        near, far = [], []
-        for chunk in range(CHUNKS):
-            back = spread(added(keep[chunk], received[chunk]), freq_devs)
-            if step < ITERS - 1:
-                near.append(next_spectra(sums, back, rcv_tables, matrix, freq_place, chunk * rows))
-                far.append(exchanged(near[chunk], "rblk", 1))
-            else:
-                result = updated(initial, onset_rcv, back, inverse, places, chunk * rows, rows, result)
+        back = spread(*added(keep, received), freq_devs)
+        if step < ITERS - 1:
+            near = next_spectra(sums, back, rcv_tables, matrix, freq_place)
+            far = exchanged(near, "rblk", 1)
+        else:
+            for chunk, messages in enumerate(back):
+                result = updated(initial, onset_rcv, messages, inverse, places, chunk * rows, rows, result)
     return result
 
 

time: 130 us -> 132 us (1.015)
  waiting for transfers between devices: 56.2 us -> 62.5 us
  starting transfers between devices: 54.5 us -> 50.1 us
    ppermute x41 -> x36, waiting for transfers between devices: 56.2 us -> 62.5 us  [exchanged(): lax.ppermute(value, axis, [(i, i ^ step) for i in range(lax.axis_size(axi...]
    ppermute x41 -> x36, starting transfers between devices: 54.5 us -> 50.1 us  [exchanged(): lax.ppermute(value, axis, [(i, i ^ step) for i in range(lax.axis_size(axi...]
    pallas_call x24 -> x21, Pallas kernels: 14.2 us -> 14.1 us  [call(): pl.pallas_call(body, grid_spec=pltpu.PrefetchScalarGridSpec(num_scalar_pr...]
  transfers between devices with their start and end apart: 41 -> 36, of which waited for: 22 -> 23; matrix products, arithmetic and copies ran while one was open for 0% -> 0% of each run, Pallas kernels for 6% -> 5%
where the time goes in v16:
time: 132 us
  waiting for transfers between devices  62.5 us (47%)
  starting transfers between devices  50.1 us (38%)
  Pallas kernels  14.1 us (11%)
  local copies, waits for them, and re-layouts  4.56 us (3%)
    ppermute x36, waiting for transfers between devices, exchanged(): lax.ppermute(value, axis, [(i, i ^ step) for i in range(lax.axis_size(axi...  62.5 us
    ppermute x36, starting transfers between devices, exchanged(): lax.ppermute(value, axis, [(i, i ^ step) for i in range(lax.axis_size(axi...  50.1 us
    pallas_call x21, Pallas kernels, call(): pl.pallas_call(body, grid_spec=pltpu.PrefetchScalarGridSpec(num_scalar_pr...  14.1 us
    unnamed x15, local copies, waits for them, and re-layouts  4.56 us
  transfers between devices with their start and end apart: 36, of which 23 were waited for; matrix products, arithmetic and copies ran while one was open for 0% of the time, Pallas kernels for 5%

profile of v16, /device:TPU:0, one launch (start us, length us, event | category | flops | bytes accessed | tf_op | source)
XLA Modules:
  0.0 131.6 jit_solution(14292215601837399347)
XLA Ops:
  0.8 1.6 %copy-done.2 = bf16[2,2,1024,256]{3,2,1,0:T(8,128)(2,1)S(1)} copy-done((bf16[2,2,1024,256]{3,2,1,0:T(8,128)(2,1)S(1)}, bf16[2,2,1024,256]{3,2,1,0:T(8,128)(2,1)}, u32[]{:S(2)}) %copy-start.2) | copy-done | bytes 2097176
  2.6 3.0 %collective-permute-start.6 = (bf16[2,256,512]{2,1,0:T(8,128)(2,1)S(1)}, bf16[2,256,512]{2,1,0:T(8,128)(2,1)S(1)}, u32[]{:S(2)}, u32[]{:S(2)}) collective-permute-start(bf16[2,256,512]{2,1,0:T(8,128)(2,1)S(1)} %get-tuple-element.64), channel_id=1, source_target_pairs={{0,2},{2,0},{1,3},{3,1},{4,6},{6,4},{5,7},{7,5},{8,10},{10,8},{9,1... | collective-permute-start | bytes 1572872 | tf_op jit(solution)/shard_map/ppermute | solution.py:509
  5.7 2.2 %copy-done = bf16[64,128,256]{2,1,0:T(8,128)(2,1)S(1)} copy-done((bf16[64,128,256]{2,1,0:T(8,128)(2,1)S(1)}, bf16[64,128,256]{2,1,0:T(8,128)(2,1)}, u32[]{:S(2)}) %copy-start) | copy-done | bytes 4194328
  8.6 3.1 %collective-permute-start.3 = (bf16[2,2,64,256]{3,2,1,0:T(8,128)(2,1)S(1)}, bf16[2,2,64,256]{3,2,1,0:T(8,128)(2,1)S(1)}, u32[]{:S(2)}, u32[]{:S(2)}) collective-permute-start(bf16[2,2,64,256]{3,2,1,0:T(8,128)(2,1)S(1)} %get-tuple-element.57), channel_id=1, source_target_pairs={{0,8},{4,12},{8,0},{12,4},{1,9},{5,13},{9,1},{13,5},{2,10},{6,14},... | collective-permute-start | bytes 393224 | tf_op jit(solution)/shard_map/ppermute | solution.py:509
  13.3 8.2 %collective-permute-done.3.refs_1_ = bf16[2,2,64,256]{3,2,1,0:T(8,128)(2,1)S(1)} collective-permute-done((bf16[2,2,64,256]{3,2,1,0:T(8,128)(2,1)S(1)}, bf16[2,2,64,256]{3,2,1,0:T(8,128)(2,1)S(1)}, u32[]{:S(2)}, u32[]{:S(2)}) %collective-permute-start.3) | collective-permute-done | bytes 131104 | tf_op jit(solution)/shard_map/ppermute | solution.py:509
  21.8 1.6 %collective-permute-start.8 = (bf16[2,2,64,256]{3,2,1,0:T(8,128)(2,1)S(1)}, bf16[2,2,64,256]{3,2,1,0:T(8,128)(2,1)S(1)}, u32[]{:S(2)}, u32[]{:S(2)}) collective-permute-start(bf16[2,2,64,256]{3,2,1,0:T(8,128)(2,1)S(1)} %get-tuple-element.66.rest_0_), channel_id=1, source_target_pairs={{0,2},{2,0},{1,3},{3,1},{4,6},{6,4},{5,7},{7,5},{8,10},{10,8},{9,1... | collective-permute-start | bytes 393224 | tf_op jit(solution)/shard_map/ppermute | solution.py:509
  24.0 7.6 %collective-permute-done.8.rest_1_ = bf16[2,2,64,256]{3,2,1,0:T(8,128)(2,1)S(1)} collective-permute-done((bf16[2,2,64,256]{3,2,1,0:T(8,128)(2,1)S(1)}, bf16[2,2,64,256]{3,2,1,0:T(8,128)(2,1)S(1)}, u32[]{:S(2)}, u32[]{:S(2)}) %collective-permute-start.8) | collective-permute-done | bytes 131104 | tf_op jit(solution)/shard_map/ppermute | solution.py:509
  34.0 2.9 %collective-permute-start.11 = (bf16[64,1024]{1,0:T(8,128)(2,1)S(1)}, bf16[64,1024]{1,0:T(8,128)(2,1)S(1)}, u32[]{:S(2)}, u32[]{:S(2)}) collective-permute-start(bf16[64,1024]{1,0:T(8,128)(2,1)S(1)} %get-tuple-element.72), channel_id=1, source_target_pairs={{0,8},{4,12},{8,0},{12,4},{1,9},{5,13},{9,1},{13,5},{2,10},{6,14},... | collective-permute-start | bytes 393224 | tf_op jit(solution)/shard_map/ppermute | solution.py:509
  41.1 5.8 %collective-permute-done.11.rest_1_ = bf16[64,1024]{1,0:T(8,128)(2,1)S(1)} collective-permute-done((bf16[64,1024]{1,0:T(8,128)(2,1)S(1)}, bf16[64,1024]{1,0:T(8,128)(2,1)S(1)}, u32[]{:S(2)}, u32[]{:S(2)}) %collective-permute-start.11) | collective-permute-done | bytes 131104 | tf_op jit(solution)/shard_map/ppermute | solution.py:509
  48.7 4.2 %collective-permute-start.14 = (bf16[64,1024]{1,0:T(8,128)(2,1)S(1)}, bf16[64,1024]{1,0:T(8,128)(2,1)S(1)}, u32[]{:S(2)}, u32[]{:S(2)}) collective-permute-start(bf16[64,1024]{1,0:T(8,128)(2,1)S(1)} %get-tuple-element.76), channel_id=1, source_target_pairs={{0,8},{4,12},{8,0},{12,4},{1,9},{5,13},{9,1},{13,5},{2,10},{6,14},... | collective-permute-start | bytes 393224 | tf_op jit(solution)/shard_map/ppermute | solution.py:509
  53.5 9.0 %collective-permute-done.14.rest_5_ = bf16[64,1024]{1,0:T(8,128)(2,1)S(1)} collective-permute-done((bf16[64,1024]{1,0:T(8,128)(2,1)S(1)}, bf16[64,1024]{1,0:T(8,128)(2,1)S(1)}, u32[]{:S(2)}, u32[]{:S(2)}) %collective-permute-start.14) | collective-permute-done | bytes 131104 | tf_op jit(solution)/shard_map/ppermute | solution.py:509
  64.1 1.6 %collective-permute-start.17 = (bf16[2,2,64,256]{3,2,1,0:T(8,128)(2,1)S(1)}, bf16[2,2,64,256]{3,2,1,0:T(8,128)(2,1)S(1)}, u32[]{:S(2)}, u32[]{:S(2)}) collective-permute-start(bf16[2,2,64,256]{3,2,1,0:T(8,128)(2,1)S(1)} %shard_map.83), channel_id=1, source_target_pairs={{0,2},{2,0},{1,3},{3,1},{4,6},{6,4},{5,7},{7,5},{8,10},{10,8},{9,1... | collective-permute-start | bytes 393224 | tf_op jit(solution)/shard_map/ppermute | solution.py:509
  66.1 3.0 %collective-permute-done.17.r_ref = bf16[2,2,64,256]{3,2,1,0:T(8,128)(2,1)S(1)} collective-permute-done((bf16[2,2,64,256]{3,2,1,0:T(8,128)(2,1)S(1)}, bf16[2,2,64,256]{3,2,1,0:T(8,128)(2,1)S(1)}, u32[]{:S(2)}, u32[]{:S(2)}) %collective-permute-start.17) | collective-permute-done | bytes 131104 | tf_op jit(solution)/shard_map/ppermute | solution.py:509
  69.2 1.9 %collective-permute-start.18 = (bf16[2,2,32,256]{3,2,1,0:T(8,128)(2,1)S(1)}, bf16[2,2,32,256]{3,2,1,0:T(8,128)(2,1)S(1)}, u32[]{:S(2)}, u32[]{:S(2)}) collective-permute-start(bf16[2,2,32,256]{3,2,1,0:T(8,128)(2,1)S(1)} %get-tuple-element.80), channel_id=1, source_target_pairs={{0,8},{4,12},{8,0},{12,4},{1,9},{5,13},{9,1},{13,5},{2,10},{6,14},... | collective-permute-start | bytes 196616 | tf_op jit(solution)/shard_map/ppermute | solution.py:509
  71.7 2.8 %collective-permute-start.21 = (bf16[2,2,32,256]{3,2,1,0:T(8,128)(2,1)S(1)}, bf16[2,2,32,256]{3,2,1,0:T(8,128)(2,1)S(1)}, u32[]{:S(2)}, u32[]{:S(2)}) collective-permute-start(bf16[2,2,32,256]{3,2,1,0:T(8,128)(2,1)S(1)} %get-tuple-element.81), channel_id=1, source_target_pairs={{0,8},{4,12},{8,0},{12,4},{1,9},{5,13},{9,1},{13,5},{2,10},{6,14},... | collective-permute-start | bytes 196616 | tf_op jit(solution)/shard_map/ppermute | solution.py:509
  75.6 1.9 %collective-permute-start.19 = (bf16[2,2,32,256]{3,2,1,0:T(8,128)(2,1)S(1)}, bf16[2,2,32,256]{3,2,1,0:T(8,128)(2,1)S(1)}, u32[]{:S(2)}, u32[]{:S(2)}) collective-permute-start(bf16[2,2,32,256]{3,2,1,0:T(8,128)(2,1)S(1)} %collective-permute-done.18.rest_1_), channel_id=1, source_target_pairs={{0,4},{4,0},{8,12},{12,8},{1,5},{5,1},{9,13},{13,9},{2,6},{6,2},{1... | collective-permute-start | bytes 196616 | tf_op jit(solution)/shard_map/ppermute | solution.py:509
  77.8 2.7 %collective-permute-start.22 = (bf16[2,2,32,256]{3,2,1,0:T(8,128)(2,1)S(1)}, bf16[2,2,32,256]{3,2,1,0:T(8,128)(2,1)S(1)}, u32[]{:S(2)}, u32[]{:S(2)}) collective-permute-start(bf16[2,2,32,256]{3,2,1,0:T(8,128)(2,1)S(1)} %collective-permute-done.21.rest_5_), channel_id=1, source_target_pairs={{0,4},{4,0},{8,12},{12,8},{1,5},{5,1},{9,13},{13,9},{2,6},{6,2},{1... | collective-permute-start | bytes 196616 | tf_op jit(solution)/shard_map/ppermute | solution.py:509
  80.4 2.2 %collective-permute-done.22.rest_6_ = bf16[2,2,32,256]{3,2,1,0:T(8,128)(2,1)S(1)} collective-permute-done((bf16[2,2,32,256]{3,2,1,0:T(8,128)(2,1)S(1)}, bf16[2,2,32,256]{3,2,1,0:T(8,128)(2,1)S(1)}, u32[]{:S(2)}, u32[]{:S(2)}) %collective-permute-start.22) | collective-permute-done | bytes 65568 | tf_op jit(solution)/shard_map/ppermute | solution.py:509
  83.1 1.6 %collective-permute-start.23 = (bf16[2,2,64,256]{3,2,1,0:T(8,128)(2,1)S(1)}, bf16[2,2,64,256]{3,2,1,0:T(8,128)(2,1)S(1)}, u32[]{:S(2)}, u32[]{:S(2)}) collective-permute-start(bf16[2,2,64,256]{3,2,1,0:T(8,128)(2,1)S(1)} %shard_map.85.rest_0_), channel_id=1, source_target_pairs={{0,2},{2,0},{1,3},{3,1},{4,6},{6,4},{5,7},{7,5},{8,10},{10,8},{9,1... | collective-permute-start | bytes 393224 | tf_op jit(solution)/shard_map/ppermute | solution.py:509
  85.4 2.7 %collective-permute-done.23.rest_1_ = bf16[2,2,64,256]{3,2,1,0:T(8,128)(2,1)S(1)} collective-permute-done((bf16[2,2,64,256]{3,2,1,0:T(8,128)(2,1)S(1)}, bf16[2,2,64,256]{3,2,1,0:T(8,128)(2,1)S(1)}, u32[]{:S(2)}, u32[]{:S(2)}) %collective-permute-start.23) | collective-permute-done | bytes 131104 | tf_op jit(solution)/shard_map/ppermute | solution.py:509
  90.4 3.0 %collective-permute-start.25 = (bf16[64,1024]{1,0:T(8,128)(2,1)S(1)}, bf16[64,1024]{1,0:T(8,128)(2,1)S(1)}, u32[]{:S(2)}, u32[]{:S(2)}) collective-permute-start(bf16[64,1024]{1,0:T(8,128)(2,1)S(1)} %get-tuple-element.84), channel_id=1, source_target_pairs={{0,12},{4,8},{8,4},{12,0},{1,13},{5,9},{9,5},{13,1},{2,14},{6,10},... | collective-permute-start | bytes 393224 | tf_op jit(solution)/shard_map/ppermute | solution.py:509
  93.4 1.5 %collective-permute-done.24.rest_1_ = bf16[64,1024]{1,0:T(8,128)(2,1)S(1)} collective-permute-done((bf16[64,1024]{1,0:T(8,128)(2,1)S(1)}, bf16[64,1024]{1,0:T(8,128)(2,1)S(1)}, u32[]{:S(2)}, u32[]{:S(2)}) %collective-permute-start.24) | collective-permute-done | bytes 131104 | tf_op jit(solution)/shard_map/ppermute | solution.py:509
  94.9 3.1 %collective-permute-done.25.rest_2_ = bf16[64,1024]{1,0:T(8,128)(2,1)S(1)} collective-permute-done((bf16[64,1024]{1,0:T(8,128)(2,1)S(1)}, bf16[64,1024]{1,0:T(8,128)(2,1)S(1)}, u32[]{:S(2)}, u32[]{:S(2)}) %collective-permute-start.25) | collective-permute-done | bytes 131104 | tf_op jit(solution)/shard_map/ppermute | solution.py:509
  100.3 2.0 %collective-permute-start.27 = (bf16[64,1024]{1,0:T(8,128)(2,1)S(1)}, bf16[64,1024]{1,0:T(8,128)(2,1)S(1)}, u32[]{:S(2)}, u32[]{:S(2)}) collective-permute-start(bf16[64,1024]{1,0:T(8,128)(2,1)S(1)} %get-tuple-element.87), channel_id=1, source_target_pairs={{0,8},{4,12},{8,0},{12,4},{1,9},{5,13},{9,1},{13,5},{2,10},{6,14},... | collective-permute-start | bytes 393224 | tf_op jit(solution)/shard_map/ppermute | solution.py:509
  103.9 7.9 %collective-permute-done.27.rest_5_ = bf16[64,1024]{1,0:T(8,128)(2,1)S(1)} collective-permute-done((bf16[64,1024]{1,0:T(8,128)(2,1)S(1)}, bf16[64,1024]{1,0:T(8,128)(2,1)S(1)}, u32[]{:S(2)}, u32[]{:S(2)}) %collective-permute-start.27) | collective-permute-done | bytes 131104 | tf_op jit(solution)/shard_map/ppermute | solution.py:509
  112.3 1.6 %collective-permute-start.30 = (bf16[2,2,64,256]{3,2,1,0:T(8,128)(2,1)S(1)}, bf16[2,2,64,256]{3,2,1,0:T(8,128)(2,1)S(1)}, u32[]{:S(2)}, u32[]{:S(2)}) collective-permute-start(bf16[2,2,64,256]{3,2,1,0:T(8,128)(2,1)S(1)} %shard_map.90), channel_id=1, source_target_pairs={{0,2},{2,0},{1,3},{3,1},{4,6},{6,4},{5,7},{7,5},{8,10},{10,8},{9,1... | collective-permute-start | bytes 393224 | tf_op jit(solution)/shard_map/ppermute | solution.py:509
  114.3 3.0 %collective-permute-done.30.r_ref = bf16[2,2,64,256]{3,2,1,0:T(8,128)(2,1)S(1)} collective-permute-done((bf16[2,2,64,256]{3,2,1,0:T(8,128)(2,1)S(1)}, bf16[2,2,64,256]{3,2,1,0:T(8,128)(2,1)S(1)}, u32[]{:S(2)}, u32[]{:S(2)}) %collective-permute-start.30) | collective-permute-done | bytes 131104 | tf_op jit(solution)/shard_map/ppermute | solution.py:509
  117.3 1.8 %collective-permute-start.34 = (bf16[2,2,32,256]{3,2,1,0:T(8,128)(2,1)S(1)}, bf16[2,2,32,256]{3,2,1,0:T(8,128)(2,1)S(1)}, u32[]{:S(2)}, u32[]{:S(2)}) collective-permute-start(bf16[2,2,32,256]{3,2,1,0:T(8,128)(2,1)S(1)} %get-tuple-element.92), channel_id=1, source_target_pairs={{0,8},{4,12},{8,0},{12,4},{1,9},{5,13},{9,1},{13,5},{2,10},{6,14},... | collective-permute-start | bytes 196616 | tf_op jit(solution)/shard_map/ppermute | solution.py:509
  120.1 2.2 %collective-permute-start.31 = (bf16[2,2,32,256]{3,2,1,0:T(8,128)(2,1)S(1)}, bf16[2,2,32,256]{3,2,1,0:T(8,128)(2,1)S(1)}, u32[]{:S(2)}, u32[]{:S(2)}) collective-permute-start(bf16[2,2,32,256]{3,2,1,0:T(8,128)(2,1)S(1)} %get-tuple-element.91), channel_id=1, source_target_pairs={{0,8},{4,12},{8,0},{12,4},{1,9},{5,13},{9,1},{13,5},{2,10},{6,14},... | collective-permute-start | bytes 196616 | tf_op jit(solution)/shard_map/ppermute | solution.py:509
  125.4 2.0 %collective-permute-start.32 = (bf16[2,2,32,256]{3,2,1,0:T(8,128)(2,1)S(1)}, bf16[2,2,32,256]{3,2,1,0:T(8,128)(2,1)S(1)}, u32[]{:S(2)}, u32[]{:S(2)}) collective-permute-start(bf16[2,2,32,256]{3,2,1,0:T(8,128)(2,1)S(1)} %collective-permute-done.31.rest_1_), channel_id=1, source_target_pairs={{0,4},{4,0},{8,12},{12,8},{1,5},{5,1},{9,13},{13,9},{2,6},{6,2},{1... | collective-permute-start | bytes 196616 | tf_op jit(solution)/shard_map/ppermute | solution.py:509
  127.5 2.0 %shard_map.92.rest_4_ = bf16[64,128,256]{2,1,0:T(8,128)(2,1)} custom-call(s32[1]{0:T(128)} %bitcast._.freq.place_ref, s32[1]{0:T(128)} %bitcast.1.rblk._, s32[1]{0:T(128)} %bitcast.2.__.sblk, bf16[64,128,256]{2,1,0:T(8,128)(2,1)S(1)} %copy-done.1, s32[128,256]{1,0:T(8,128)S(1)} %copy-done.3, bf16[4,128,128]{2,1,0:T(8,128)(2,1)S(1)} %copy-done.5, ...), custom_call_target="tpu_custom_call" | custom-call | flops 33554432 | bytes 9043968 | tf_op jit(solution)/shard_map/pallas_call | solution.py:78
  129.6 1.9 %shard_map.93 = bf16[64,128,256]{2,1,0:T(8,128)(2,1)} custom-call(s32[1]{0:T(128)} %bitcast._.freq.place_ref, s32[1]{0:T(128)} %bitcast.1.rblk._, s32[1]{0:T(128)} %bitcast.2.__.sblk, bf16[64,128,256]{2,1,0:T(8,128)(2,1)S(1)} %copy-done.1, s32[128,256]{1,0:T(8,128)S(1)} %copy-done.3, ...), custom_call_target="tpu_custom_call", output_to_operand_aliasing={{}: (10, {})} | custom-call | flops 33554432 | bytes 13238272 | tf_op jit(solution)/shard_map/pallas_call | solution.py:78
  (76 shorter events, 30.0 us)
Async XLA Ops:
  2.6 21.3 %collective-permute-start.6 = (bf16[2,256,512]{2,1,0:T(8,128)(2,1)S(1)}, bf16[2,256,512]{2,1,0:T(8,128)(2,1)S(1)}, u32[]{:S(2)}, u32[]{:S(2)}) collective-permute-start(bf16[2,256,512]{2,1,0:T(8,128)(2,1)S(1)} %get-tuple-element.64), channel_id=1, source_target_pairs={{0,2},{2,0},{1,3},{3,1},{4,6},{6,4},{5,7},{7,5},{8,10},{10,8},{9,1... | collective-permute-start | bytes 1572872 | tf_op jit(solution)/shard_map/ppermute | solution.py:509
  5.6 26.0 %collective-permute-start.7 = (bf16[2,256,512]{2,1,0:T(8,128)(2,1)S(1)}, bf16[2,256,512]{2,1,0:T(8,128)(2,1)S(1)}, u32[]{:S(2)}, u32[]{:S(2)}) collective-permute-start(bf16[2,256,512]{2,1,0:T(8,128)(2,1)S(1)} %get-tuple-element.67), channel_id=1, source_target_pairs={{0,2},{2,0},{1,3},{3,1},{4,6},{6,4},{5,7},{7,5},{8,10},{10,8},{9,1... | collective-permute-start | bytes 1572872 | tf_op jit(solution)/shard_map/ppermute | solution.py:509
  8.6 12.9 %collective-permute-start.3 = (bf16[2,2,64,256]{3,2,1,0:T(8,128)(2,1)S(1)}, bf16[2,2,64,256]{3,2,1,0:T(8,128)(2,1)S(1)}, u32[]{:S(2)}, u32[]{:S(2)}) collective-permute-start(bf16[2,2,64,256]{3,2,1,0:T(8,128)(2,1)S(1)} %get-tuple-element.57), channel_id=1, source_target_pairs={{0,8},{4,12},{8,0},{12,4},{1,9},{5,13},{9,1},{13,5},{2,10},{6,14},... | collective-permute-start | bytes 393224 | tf_op jit(solution)/shard_map/ppermute | solution.py:509
  11.7 9.8 %collective-permute-start.4 = (bf16[2,2,64,256]{3,2,1,0:T(8,128)(2,1)S(1)}, bf16[2,2,64,256]{3,2,1,0:T(8,128)(2,1)S(1)}, u32[]{:S(2)}, u32[]{:S(2)}) collective-permute-start(bf16[2,2,64,256]{3,2,1,0:T(8,128)(2,1)S(1)} %get-tuple-element.58), channel_id=1, source_target_pairs={{0,12},{4,8},{8,4},{12,0},{1,13},{5,9},{9,5},{13,1},{2,14},{6,10},... | collective-permute-start | bytes 393224 | tf_op jit(solution)/shard_map/ppermute | solution.py:509
  13.1 8.6 %collective-permute-start.5 = (bf16[2,2,64,256]{3,2,1,0:T(8,128)(2,1)S(1)}, bf16[2,2,64,256]{3,2,1,0:T(8,128)(2,1)S(1)}, u32[]{:S(2)}, u32[]{:S(2)}) collective-permute-start(bf16[2,2,64,256]{3,2,1,0:T(8,128)(2,1)S(1)} %get-tuple-element.59), channel_id=1, source_target_pairs={{0,4},{4,0},{8,12},{12,8},{1,5},{5,1},{9,13},{13,9},{2,6},{6,2},{1... | collective-permute-start | bytes 393224 | tf_op jit(solution)/shard_map/ppermute | solution.py:509
  21.8 9.8 %collective-permute-start.8 = (bf16[2,2,64,256]{3,2,1,0:T(8,128)(2,1)S(1)}, bf16[2,2,64,256]{3,2,1,0:T(8,128)(2,1)S(1)}, u32[]{:S(2)}, u32[]{:S(2)}) collective-permute-start(bf16[2,2,64,256]{3,2,1,0:T(8,128)(2,1)S(1)} %get-tuple-element.66.rest_0_), channel_id=1, source_target_pairs={{0,2},{2,0},{1,3},{3,1},{4,6},{6,4},{5,7},{7,5},{8,10},{10,8},{9,1... | collective-permute-start | bytes 393224 | tf_op jit(solution)/shard_map/ppermute | solution.py:509
  23.4 8.2 %collective-permute-start = (bf16[2,256,512]{2,1,0:T(8,128)(2,1)S(1)}, bf16[2,256,512]{2,1,0:T(8,128)(2,1)S(1)}, u32[]{:S(2)}, u32[]{:S(2)}) collective-permute-start(bf16[2,256,512]{2,1,0:T(8,128)(2,1)S(1)} %get-tuple-element.49.rest_1_.rest_0_), channel_id=1, source_target_pairs={{0,1},{1,0},{2,3},{3,2},{4,5},{5,4},{6,7},{7,6},{8,9},{9,8},{10,11... | collective-permute-start | bytes 1572872 | tf_op jit(solution)/shard_map/ppermute | solution.py:509
  23.4 8.2 %collective-permute-start.1 = (bf16[2,256,512]{2,1,0:T(8,128)(2,1)S(1)}, bf16[2,256,512]{2,1,0:T(8,128)(2,1)S(1)}, u32[]{:S(2)}, u32[]{:S(2)}) collective-permute-start(bf16[2,256,512]{2,1,0:T(8,128)(2,1)S(1)} %get-tuple-element.50.rest_3_.rest_2_), channel_id=1, source_target_pairs={{0,1},{1,0},{2,3},{3,2},{4,5},{5,4},{6,7},{7,6},{8,9},{9,8},{10,11... | collective-permute-start | bytes 1572872 | tf_op jit(solution)/shard_map/ppermute | solution.py:509
  23.9 8.5 %collective-permute-start.9 = (bf16[2,256,512]{2,1,0:T(8,128)(2,1)S(1)}, bf16[2,256,512]{2,1,0:T(8,128)(2,1)S(1)}, u32[]{:S(2)}, u32[]{:S(2)}) collective-permute-start(bf16[2,256,512]{2,1,0:T(8,128)(2,1)S(1)} %collective-permute-done.6.rest_2_.rest_0_), channel_id=1, source_target_pairs={{0,1},{1,0},{2,3},{3,2},{4,5},{5,4},{6,7},{7,6},{8,9},{9,8},{10,11... | collective-permute-start | bytes 1572872 | tf_op jit(solution)/shard_map/ppermute | solution.py:509
  34.0 12.9 %collective-permute-start.11 = (bf16[64,1024]{1,0:T(8,128)(2,1)S(1)}, bf16[64,1024]{1,0:T(8,128)(2,1)S(1)}, u32[]{:S(2)}, u32[]{:S(2)}) collective-permute-start(bf16[64,1024]{1,0:T(8,128)(2,1)S(1)} %get-tuple-element.72), channel_id=1, source_target_pairs={{0,8},{4,12},{8,0},{12,4},{1,9},{5,13},{9,1},{13,5},{2,10},{6,14},... | collective-permute-start | bytes 393224 | tf_op jit(solution)/shard_map/ppermute | solution.py:509
  36.9 10.0 %collective-permute-start.12 = (bf16[64,1024]{1,0:T(8,128)(2,1)S(1)}, bf16[64,1024]{1,0:T(8,128)(2,1)S(1)}, u32[]{:S(2)}, u32[]{:S(2)}) collective-permute-start(bf16[64,1024]{1,0:T(8,128)(2,1)S(1)} %get-tuple-element.73), channel_id=1, source_target_pairs={{0,12},{4,8},{8,4},{12,0},{1,13},{5,9},{9,5},{13,1},{2,14},{6,10},... | collective-permute-start | bytes 393224 | tf_op jit(solution)/shard_map/ppermute | solution.py:509
  38.2 9.5 %collective-permute-start.13 = (bf16[64,1024]{1,0:T(8,128)(2,1)S(1)}, bf16[64,1024]{1,0:T(8,128)(2,1)S(1)}, u32[]{:S(2)}, u32[]{:S(2)}) collective-permute-start(bf16[64,1024]{1,0:T(8,128)(2,1)S(1)} %get-tuple-element.74), channel_id=1, source_target_pairs={{0,4},{4,0},{8,12},{12,8},{1,5},{5,1},{9,13},{13,9},{2,6},{6,2},{1... | collective-permute-start | bytes 393224 | tf_op jit(solution)/shard_map/ppermute | solution.py:509
  48.7 13.8 %collective-permute-start.14 = (bf16[64,1024]{1,0:T(8,128)(2,1)S(1)}, bf16[64,1024]{1,0:T(8,128)(2,1)S(1)}, u32[]{:S(2)}, u32[]{:S(2)}) collective-permute-start(bf16[64,1024]{1,0:T(8,128)(2,1)S(1)} %get-tuple-element.76), channel_id=1, source_target_pairs={{0,8},{4,12},{8,0},{12,4},{1,9},{5,13},{9,1},{13,5},{2,10},{6,14},... | collective-permute-start | bytes 393224 | tf_op jit(solution)/shard_map/ppermute | solution.py:509
  52.9 9.6 %collective-permute-start.15 = (bf16[64,1024]{1,0:T(8,128)(2,1)S(1)}, bf16[64,1024]{1,0:T(8,128)(2,1)S(1)}, u32[]{:S(2)}, u32[]{:S(2)}) collective-permute-start(bf16[64,1024]{1,0:T(8,128)(2,1)S(1)} %get-tuple-element.77), channel_id=1, source_target_pairs={{0,12},{4,8},{8,4},{12,0},{1,13},{5,9},{9,5},{13,1},{2,14},{6,10},... | collective-permute-start | bytes 393224 | tf_op jit(solution)/shard_map/ppermute | solution.py:509
  53.3 10.3 %collective-permute-start.16 = (bf16[64,1024]{1,0:T(8,128)(2,1)S(1)}, bf16[64,1024]{1,0:T(8,128)(2,1)S(1)}, u32[]{:S(2)}, u32[]{:S(2)}) collective-permute-start(bf16[64,1024]{1,0:T(8,128)(2,1)S(1)} %get-tuple-element.78), channel_id=1, source_target_pairs={{0,4},{4,0},{8,12},{12,8},{1,5},{5,1},{9,13},{13,9},{2,6},{6,2},{1... | collective-permute-start | bytes 393224 | tf_op jit(solution)/shard_map/ppermute | solution.py:509
  64.1 5.0 %collective-permute-start.17 = (bf16[2,2,64,256]{3,2,1,0:T(8,128)(2,1)S(1)}, bf16[2,2,64,256]{3,2,1,0:T(8,128)(2,1)S(1)}, u32[]{:S(2)}, u32[]{:S(2)}) collective-permute-start(bf16[2,2,64,256]{3,2,1,0:T(8,128)(2,1)S(1)} %shard_map.83), channel_id=1, source_target_pairs={{0,2},{2,0},{1,3},{3,1},{4,6},{6,4},{5,7},{7,5},{8,10},{10,8},{9,1... | collective-permute-start | bytes 393224 | tf_op jit(solution)/shard_map/ppermute | solution.py:509
  69.2 6.5 %collective-permute-start.18 = (bf16[2,2,32,256]{3,2,1,0:T(8,128)(2,1)S(1)}, bf16[2,2,32,256]{3,2,1,0:T(8,128)(2,1)S(1)}, u32[]{:S(2)}, u32[]{:S(2)}) collective-permute-start(bf16[2,2,32,256]{3,2,1,0:T(8,128)(2,1)S(1)} %get-tuple-element.80), channel_id=1, source_target_pairs={{0,8},{4,12},{8,0},{12,4},{1,9},{5,13},{9,1},{13,5},{2,10},{6,14},... | collective-permute-start | bytes 196616 | tf_op jit(solution)/shard_map/ppermute | solution.py:509
  71.1 9.3 %collective-permute-start.20 = (bf16[2,2,64,256]{3,2,1,0:T(8,128)(2,1)S(1)}, bf16[2,2,64,256]{3,2,1,0:T(8,128)(2,1)S(1)}, u32[]{:S(2)}, u32[]{:S(2)}) collective-permute-start(bf16[2,2,64,256]{3,2,1,0:T(8,128)(2,1)S(1)} %get-tuple-element.79.rest_0_.rest_4_), channel_id=1, source_target_pairs={{0,4},{4,0},{8,12},{12,8},{1,5},{5,1},{9,13},{13,9},{2,6},{6,2},{1... | collective-permute-start | bytes 393224 | tf_op jit(solution)/shard_map/ppermute | solution.py:509
  71.7 6.1 %collective-permute-start.21 = (bf16[2,2,32,256]{3,2,1,0:T(8,128)(2,1)S(1)}, bf16[2,2,32,256]{3,2,1,0:T(8,128)(2,1)S(1)}, u32[]{:S(2)}, u32[]{:S(2)}) collective-permute-start(bf16[2,2,32,256]{3,2,1,0:T(8,128)(2,1)S(1)} %get-tuple-element.81), channel_id=1, source_target_pairs={{0,8},{4,12},{8,0},{12,4},{1,9},{5,13},{9,1},{13,5},{2,10},{6,14},... | collective-permute-start | bytes 196616 | tf_op jit(solution)/shard_map/ppermute | solution.py:509
  75.6 4.8 %collective-permute-start.19 = (bf16[2,2,32,256]{3,2,1,0:T(8,128)(2,1)S(1)}, bf16[2,2,32,256]{3,2,1,0:T(8,128)(2,1)S(1)}, u32[]{:S(2)}, u32[]{:S(2)}) collective-permute-start(bf16[2,2,32,256]{3,2,1,0:T(8,128)(2,1)S(1)} %collective-permute-done.18.rest_1_), channel_id=1, source_target_pairs={{0,4},{4,0},{8,12},{12,8},{1,5},{5,1},{9,13},{13,9},{2,6},{6,2},{1... | collective-permute-start | bytes 196616 | tf_op jit(solution)/shard_map/ppermute | solution.py:509
  77.8 4.9 %collective-permute-start.22 = (bf16[2,2,32,256]{3,2,1,0:T(8,128)(2,1)S(1)}, bf16[2,2,32,256]{3,2,1,0:T(8,128)(2,1)S(1)}, u32[]{:S(2)}, u32[]{:S(2)}) collective-permute-start(bf16[2,2,32,256]{3,2,1,0:T(8,128)(2,1)S(1)} %collective-permute-done.21.rest_5_), channel_id=1, source_target_pairs={{0,4},{4,0},{8,12},{12,8},{1,5},{5,1},{9,13},{13,9},{2,6},{6,2},{1... | collective-permute-start | bytes 196616 | tf_op jit(solution)/shard_map/ppermute | solution.py:509
  83.1 5.0 %collective-permute-start.23 = (bf16[2,2,64,256]{3,2,1,0:T(8,128)(2,1)S(1)}, bf16[2,2,64,256]{3,2,1,0:T(8,128)(2,1)S(1)}, u32[]{:S(2)}, u32[]{:S(2)}) collective-permute-start(bf16[2,2,64,256]{3,2,1,0:T(8,128)(2,1)S(1)} %shard_map.85.rest_0_), channel_id=1, source_target_pairs={{0,2},{2,0},{1,3},{3,1},{4,6},{6,4},{5,7},{7,5},{8,10},{10,8},{9,1... | collective-permute-start | bytes 393224 | tf_op jit(solution)/shard_map/ppermute | solution.py:509
  89.0 5.9 %collective-permute-start.24 = (bf16[64,1024]{1,0:T(8,128)(2,1)S(1)}, bf16[64,1024]{1,0:T(8,128)(2,1)S(1)}, u32[]{:S(2)}, u32[]{:S(2)}) collective-permute-start(bf16[64,1024]{1,0:T(8,128)(2,1)S(1)} %get-tuple-element.83), channel_id=1, source_target_pairs={{0,8},{4,12},{8,0},{12,4},{1,9},{5,13},{9,1},{13,5},{2,10},{6,14},... | collective-permute-start | bytes 393224 | tf_op jit(solution)/shard_map/ppermute | solution.py:509
  90.4 7.5 %collective-permute-start.25 = (bf16[64,1024]{1,0:T(8,128)(2,1)S(1)}, bf16[64,1024]{1,0:T(8,128)(2,1)S(1)}, u32[]{:S(2)}, u32[]{:S(2)}) collective-permute-start(bf16[64,1024]{1,0:T(8,128)(2,1)S(1)} %get-tuple-element.84), channel_id=1, source_target_pairs={{0,12},{4,8},{8,4},{12,0},{1,13},{5,9},{9,5},{13,1},{2,14},{6,10},... | collective-permute-start | bytes 393224 | tf_op jit(solution)/shard_map/ppermute | solution.py:509
  93.4 5.9 %collective-permute-start.26 = (bf16[64,1024]{1,0:T(8,128)(2,1)S(1)}, bf16[64,1024]{1,0:T(8,128)(2,1)S(1)}, u32[]{:S(2)}, u32[]{:S(2)}) collective-permute-start(bf16[64,1024]{1,0:T(8,128)(2,1)S(1)} %get-tuple-element.85), channel_id=1, source_target_pairs={{0,4},{4,0},{8,12},{12,8},{1,5},{5,1},{9,13},{13,9},{2,6},{6,2},{1... | collective-permute-start | bytes 393224 | tf_op jit(solution)/shard_map/ppermute | solution.py:509
  100.3 11.5 %collective-permute-start.27 = (bf16[64,1024]{1,0:T(8,128)(2,1)S(1)}, bf16[64,1024]{1,0:T(8,128)(2,1)S(1)}, u32[]{:S(2)}, u32[]{:S(2)}) collective-permute-start(bf16[64,1024]{1,0:T(8,128)(2,1)S(1)} %get-tuple-element.87), channel_id=1, source_target_pairs={{0,8},{4,12},{8,0},{12,4},{1,9},{5,13},{9,1},{13,5},{2,10},{6,14},... | collective-permute-start | bytes 393224 | tf_op jit(solution)/shard_map/ppermute | solution.py:509
  102.3 9.5 %collective-permute-start.28 = (bf16[64,1024]{1,0:T(8,128)(2,1)S(1)}, bf16[64,1024]{1,0:T(8,128)(2,1)S(1)}, u32[]{:S(2)}, u32[]{:S(2)}) collective-permute-start(bf16[64,1024]{1,0:T(8,128)(2,1)S(1)} %get-tuple-element.88), channel_id=1, source_target_pairs={{0,12},{4,8},{8,4},{12,0},{1,13},{5,9},{9,5},{13,1},{2,14},{6,10},... | collective-permute-start | bytes 393224 | tf_op jit(solution)/shard_map/ppermute | solution.py:509
  103.3 8.5 %collective-permute-start.29 = (bf16[64,1024]{1,0:T(8,128)(2,1)S(1)}, bf16[64,1024]{1,0:T(8,128)(2,1)S(1)}, u32[]{:S(2)}, u32[]{:S(2)}) collective-permute-start(bf16[64,1024]{1,0:T(8,128)(2,1)S(1)} %get-tuple-element.89), channel_id=1, source_target_pairs={{0,4},{4,0},{8,12},{12,8},{1,5},{5,1},{9,13},{13,9},{2,6},{6,2},{1... | collective-permute-start | bytes 393224 | tf_op jit(solution)/shard_map/ppermute | solution.py:509
  112.3 5.0 %collective-permute-start.30 = (bf16[2,2,64,256]{3,2,1,0:T(8,128)(2,1)S(1)}, bf16[2,2,64,256]{3,2,1,0:T(8,128)(2,1)S(1)}, u32[]{:S(2)}, u32[]{:S(2)}) collective-permute-start(bf16[2,2,64,256]{3,2,1,0:T(8,128)(2,1)S(1)} %shard_map.90), channel_id=1, source_target_pairs={{0,2},{2,0},{1,3},{3,1},{4,6},{6,4},{5,7},{7,5},{8,10},{10,8},{9,1... | collective-permute-start | bytes 393224 | tf_op jit(solution)/shard_map/ppermute | solution.py:509
  117.3 5.8 %collective-permute-start.34 = (bf16[2,2,32,256]{3,2,1,0:T(8,128)(2,1)S(1)}, bf16[2,2,32,256]{3,2,1,0:T(8,128)(2,1)S(1)}, u32[]{:S(2)}, u32[]{:S(2)}) collective-permute-start(bf16[2,2,32,256]{3,2,1,0:T(8,128)(2,1)S(1)} %get-tuple-element.92), channel_id=1, source_target_pairs={{0,8},{4,12},{8,0},{12,4},{1,9},{5,13},{9,1},{13,5},{2,10},{6,14},... | collective-permute-start | bytes 196616 | tf_op jit(solution)/shard_map/ppermute | solution.py:509
  119.2 8.3 %collective-permute-start.33 = (bf16[2,2,64,256]{3,2,1,0:T(8,128)(2,1)S(1)}, bf16[2,2,64,256]{3,2,1,0:T(8,128)(2,1)S(1)}, u32[]{:S(2)}, u32[]{:S(2)}) collective-permute-start(bf16[2,2,64,256]{3,2,1,0:T(8,128)(2,1)S(1)} %get-tuple-element.90.rest_0_), channel_id=1, source_target_pairs={{0,4},{4,0},{8,12},{12,8},{1,5},{5,1},{9,13},{13,9},{2,6},{6,2},{1... | collective-permute-start | bytes 393224 | tf_op jit(solution)/shard_map/ppermute | solution.py:509
  120.1 5.3 %collective-permute-start.31 = (bf16[2,2,32,256]{3,2,1,0:T(8,128)(2,1)S(1)}, bf16[2,2,32,256]{3,2,1,0:T(8,128)(2,1)S(1)}, u32[]{:S(2)}, u32[]{:S(2)}) collective-permute-start(bf16[2,2,32,256]{3,2,1,0:T(8,128)(2,1)S(1)} %get-tuple-element.91), channel_id=1, source_target_pairs={{0,8},{4,12},{8,0},{12,4},{1,9},{5,13},{9,1},{13,5},{2,10},{6,14},... | collective-permute-start | bytes 196616 | tf_op jit(solution)/shard_map/ppermute | solution.py:509
  (11 other events, 148.3 us)

commit v17 on v14

--- a/solution.py
+++ b/solution.py
@@ -204,6 +204,23 @@
     return out
 
 
+def added_to(keep, received, before):
+    group, rcv = received.shape[2:]
+    rows = group * (len(before) + 1)
+
+    def body(k_ref, r_ref, *rest):
+        refs, (out, together) = rest[: len(before)], rest[len(before) :]
+        total = (k_ref[...] + r_ref[...].astype(F32)).astype(BF16)
+        out[...] = total
+        for at, ref in enumerate(refs):
+            together[:, :, at * group : (at + 1) * group] = ref[...]
+        together[:, :, rows - group :] = total
+
+    shapes = [jax.ShapeDtypeStruct(keep.shape[:2] + (count, rcv), BF16) for count in (group, rows)]
+    inputs = [(v, whole(v)) for v in (keep, received, *before)]
+    return call(body, (), inputs, [(v, whole(v)) for v in shapes], (1,))
+
+
 def src_onsets(onset, places, half_rows, share, width):
 
     def body(freq, rblk, sblk, o_ref, own, other):
@@ -315,7 +332,7 @@
         body(pl.ds(pl.multiple_of(step * BLOCK, BLOCK), BLOCK))
         return carry
 
-    lax.fori_loop(0, width // BLOCK, at, 0, unroll=2)
+    lax.fori_loop(0, width // BLOCK, at, 0, unroll=4)
 
 
 def windowed(messages, tables, matrix, freq_place, per_dev, share):
@@ -459,8 +476,11 @@
             for row in range(ROWS):
                 spread_ref[row * own : (row + 1) * own] = jnp.where(lane == row, base, 0.0).astype(BF16)
 
-        here = pl.ds(pl.multiple_of(step * tile, tile), tile)
-        data = [ref[:, :, here, :].astype(F32) for ref in refs]
+        data = []
+        for ref in refs:
+            skip = first if ref.shape[2] > rows else 0
+            here = pl.ds(pl.multiple_of(skip + step * tile, tile), tile)
+            data.append(ref[:, :, here, :].astype(F32))
         onsets = o_ref[pl.ds(pl.multiple_of(sblk[0] * half_rows + first + step * tile, tile), tile), :]
         time = lax.broadcasted_iota(jnp.int32, (own, rcv), 0) + place_ref[0] * own
         for half in range(2):
@@ -508,6 +528,18 @@
     return [held[way] for way in ways(count)]
 
 
+def spread_groups(value, groups, count):
+    top = count // 2
+    far = [{top: exchanged(group, "freq", top)} for group in groups]
+    near = {0: value}
+    bit = top // 2
+    while bit:
+        for held in (near, *far):
+            held.update({way | bit: exchanged(held[way], "freq", bit) for way in sorted(held)})
+        bit //= 2
+    return [[{**near, **held}[way] for way in ways(count)] for held in far]
+
+
 def on_device(initial, response, aperture, onset_rcv, onset_src):
     freq_devs = lax.axis_size("freq")
     per_dev = response.shape[0]
@@ -551,13 +583,16 @@
         received = [exchanged(v, "rblk", 1) for v in up_products(messages, parts, freq_place, half_rows, 1)]
         keep = up_products(messages, parts, freq_place, half_rows, 0)
         near, far = [], []
-        for chunk in range(CHUNKS):
-            back = spread(added(keep[chunk], received[chunk]), freq_devs)
-            if step < ITERS - 1:
+        if step < ITERS - 1:
+            for chunk in range(CHUNKS):
+                back = spread(added(keep[chunk], received[chunk]), freq_devs)
                 near.append(next_spectra(sums, back, rcv_tables, matrix, freq_place, chunk * rows))
                 far.append(exchanged(near[chunk], "rblk", 1))
-            else:
-                result = updated(initial, onset_rcv, back, inverse, places, chunk * rows, rows, result)
+            continue
+        back = [added(*pair) for pair in zip(keep[:-1], received)]
+        last, together = added_to(keep[-1], received[-1], back)
+        for chunk, messages in enumerate(spread_groups(together, back + [last], freq_devs)):
+            result = updated(initial, onset_rcv, messages, inverse, places, chunk * rows, rows, result)
     return result
 
 

time: 130 us -> 133 us (1.023)
  waiting for transfers between devices: 56.2 us -> 63.9 us
  starting transfers between devices: 54.5 us -> 50.5 us
    ppermute x41 -> x40, waiting for transfers between devices: 56.2 us -> 63.9 us  [exchanged(): lax.ppermute(value, axis, [(i, i ^ step) for i in range(lax.axis_size(axi...]
    ppermute x41 -> x40, starting transfers between devices: 54.5 us -> 50.5 us  [exchanged(): lax.ppermute(value, axis, [(i, i ^ step) for i in range(lax.axis_size(axi...]
  transfers between devices with their start and end apart: 41 -> 40, of which waited for: 22 -> 25; matrix products, arithmetic and copies ran while one was open for 0% -> 0% of each run, Pallas kernels for 6% -> 6%
where the time goes in v17:
time: 133 us
  waiting for transfers between devices  63.9 us (48%)
  starting transfers between devices  50.5 us (38%)
  Pallas kernels  13.8 us (10%)
  local copies, waits for them, and re-layouts  4.56 us (3%)
    ppermute x40, waiting for transfers between devices, exchanged(): lax.ppermute(value, axis, [(i, i ^ step) for i in range(lax.axis_size(axi...  63.9 us
    ppermute x40, starting transfers between devices, exchanged(): lax.ppermute(value, axis, [(i, i ^ step) for i in range(lax.axis_size(axi...  50.5 us
    pallas_call x24, Pallas kernels, call(): pl.pallas_call(body, grid_spec=pltpu.PrefetchScalarGridSpec(num_scalar_pr...  13.8 us
    unnamed x15, local copies, waits for them, and re-layouts  4.56 us
  transfers between devices with their start and end apart: 40, of which 25 were waited for; matrix products, arithmetic and copies ran while one was open for 0% of the time, Pallas kernels for 6%

profile of v17, /device:TPU:0, one launch (start us, length us, event | category | flops | bytes accessed | tf_op | source)
XLA Modules:
  0.0 133.0 jit_solution(860616638381035188)
XLA Ops:
  0.8 1.6 %copy-done.2 = bf16[2,2,1024,256]{3,2,1,0:T(8,128)(2,1)S(1)} copy-done((bf16[2,2,1024,256]{3,2,1,0:T(8,128)(2,1)S(1)}, bf16[2,2,1024,256]{3,2,1,0:T(8,128)(2,1)}, u32[]{:S(2)}) %copy-start.2) | copy-done | bytes 2097176
  2.6 3.0 %collective-permute-start.6 = (bf16[2,256,512]{2,1,0:T(8,128)(2,1)S(1)}, bf16[2,256,512]{2,1,0:T(8,128)(2,1)S(1)}, u32[]{:S(2)}, u32[]{:S(2)}) collective-permute-start(bf16[2,256,512]{2,1,0:T(8,128)(2,1)S(1)} %get-tuple-element.68), channel_id=1, source_target_pairs={{0,2},{2,0},{1,3},{3,1},{4,6},{6,4},{5,7},{7,5},{8,10},{10,8},{9,1... | collective-permute-start | bytes 1572872 | tf_op jit(solution)/shard_map/ppermute | solution.py:515
  5.7 2.2 %copy-done = bf16[64,128,256]{2,1,0:T(8,128)(2,1)S(1)} copy-done((bf16[64,128,256]{2,1,0:T(8,128)(2,1)S(1)}, bf16[64,128,256]{2,1,0:T(8,128)(2,1)}, u32[]{:S(2)}) %copy-start) | copy-done | bytes 4194328
  8.6 3.1 %collective-permute-start.3 = (bf16[2,2,64,256]{3,2,1,0:T(8,128)(2,1)S(1)}, bf16[2,2,64,256]{3,2,1,0:T(8,128)(2,1)S(1)}, u32[]{:S(2)}, u32[]{:S(2)}) collective-permute-start(bf16[2,2,64,256]{3,2,1,0:T(8,128)(2,1)S(1)} %get-tuple-element.61), channel_id=1, source_target_pairs={{0,8},{4,12},{8,0},{12,4},{1,9},{5,13},{9,1},{13,5},{2,10},{6,14},... | collective-permute-start | bytes 393224 | tf_op jit(solution)/shard_map/ppermute | solution.py:515
  13.3 8.2 %collective-permute-done.3.refs_1_ = bf16[2,2,64,256]{3,2,1,0:T(8,128)(2,1)S(1)} collective-permute-done((bf16[2,2,64,256]{3,2,1,0:T(8,128)(2,1)S(1)}, bf16[2,2,64,256]{3,2,1,0:T(8,128)(2,1)S(1)}, u32[]{:S(2)}, u32[]{:S(2)}) %collective-permute-start.3) | collective-permute-done | bytes 131104 | tf_op jit(solution)/shard_map/ppermute | solution.py:515
  21.8 1.6 %collective-permute-start.8 = (bf16[2,2,64,256]{3,2,1,0:T(8,128)(2,1)S(1)}, bf16[2,2,64,256]{3,2,1,0:T(8,128)(2,1)S(1)}, u32[]{:S(2)}, u32[]{:S(2)}) collective-permute-start(bf16[2,2,64,256]{3,2,1,0:T(8,128)(2,1)S(1)} %get-tuple-element.70.rest_0_), channel_id=1, source_target_pairs={{0,2},{2,0},{1,3},{3,1},{4,6},{6,4},{5,7},{7,5},{8,10},{10,8},{9,1... | collective-permute-start | bytes 393224 | tf_op jit(solution)/shard_map/ppermute | solution.py:515
  24.0 7.6 %collective-permute-done.8.rest_1_ = bf16[2,2,64,256]{3,2,1,0:T(8,128)(2,1)S(1)} collective-permute-done((bf16[2,2,64,256]{3,2,1,0:T(8,128)(2,1)S(1)}, bf16[2,2,64,256]{3,2,1,0:T(8,128)(2,1)S(1)}, u32[]{:S(2)}, u32[]{:S(2)}) %collective-permute-start.8) | collective-permute-done | bytes 131104 | tf_op jit(solution)/shard_map/ppermute | solution.py:515
  34.0 2.9 %collective-permute-start.11 = (bf16[64,1024]{1,0:T(8,128)(2,1)S(1)}, bf16[64,1024]{1,0:T(8,128)(2,1)S(1)}, u32[]{:S(2)}, u32[]{:S(2)}) collective-permute-start(bf16[64,1024]{1,0:T(8,128)(2,1)S(1)} %get-tuple-element.76), channel_id=1, source_target_pairs={{0,8},{4,12},{8,0},{12,4},{1,9},{5,13},{9,1},{13,5},{2,10},{6,14},... | collective-permute-start | bytes 393224 | tf_op jit(solution)/shard_map/ppermute | solution.py:515
  41.1 5.8 %collective-permute-done.11.rest_1_ = bf16[64,1024]{1,0:T(8,128)(2,1)S(1)} collective-permute-done((bf16[64,1024]{1,0:T(8,128)(2,1)S(1)}, bf16[64,1024]{1,0:T(8,128)(2,1)S(1)}, u32[]{:S(2)}, u32[]{:S(2)}) %collective-permute-start.11) | collective-permute-done | bytes 131104 | tf_op jit(solution)/shard_map/ppermute | solution.py:515
  48.4 4.2 %collective-permute-start.14 = (bf16[64,1024]{1,0:T(8,128)(2,1)S(1)}, bf16[64,1024]{1,0:T(8,128)(2,1)S(1)}, u32[]{:S(2)}, u32[]{:S(2)}) collective-permute-start(bf16[64,1024]{1,0:T(8,128)(2,1)S(1)} %get-tuple-element.80), channel_id=1, source_target_pairs={{0,8},{4,12},{8,0},{12,4},{1,9},{5,13},{9,1},{13,5},{2,10},{6,14},... | collective-permute-start | bytes 393224 | tf_op jit(solution)/shard_map/ppermute | solution.py:515
  53.2 9.0 %collective-permute-done.14.rest_5_ = bf16[64,1024]{1,0:T(8,128)(2,1)S(1)} collective-permute-done((bf16[64,1024]{1,0:T(8,128)(2,1)S(1)}, bf16[64,1024]{1,0:T(8,128)(2,1)S(1)}, u32[]{:S(2)}, u32[]{:S(2)}) %collective-permute-start.14) | collective-permute-done | bytes 131104 | tf_op jit(solution)/shard_map/ppermute | solution.py:515
  63.7 1.6 %collective-permute-start.17 = (bf16[2,2,32,256]{3,2,1,0:T(8,128)(2,1)S(1)}, bf16[2,2,32,256]{3,2,1,0:T(8,128)(2,1)S(1)}, u32[]{:S(2)}, u32[]{:S(2)}) collective-permute-start(bf16[2,2,32,256]{3,2,1,0:T(8,128)(2,1)S(1)} %get-tuple-element.84), channel_id=1, source_target_pairs={{0,2},{2,0},{1,3},{3,1},{4,6},{6,4},{5,7},{7,5},{8,10},{10,8},{9,1... | collective-permute-start | bytes 196616 | tf_op jit(solution)/shard_map/ppermute | solution.py:515
  66.3 1.8 %collective-permute-done.17.r_ref = bf16[2,2,32,256]{3,2,1,0:T(8,128)(2,1)S(1)} collective-permute-done((bf16[2,2,32,256]{3,2,1,0:T(8,128)(2,1)S(1)}, bf16[2,2,32,256]{3,2,1,0:T(8,128)(2,1)S(1)}, u32[]{:S(2)}, u32[]{:S(2)}) %collective-permute-start.17) | collective-permute-done | bytes 65568 | tf_op jit(solution)/shard_map/ppermute | solution.py:515
  68.1 1.9 %collective-permute-start.18 = (bf16[2,2,32,256]{3,2,1,0:T(8,128)(2,1)S(1)}, bf16[2,2,32,256]{3,2,1,0:T(8,128)(2,1)S(1)}, u32[]{:S(2)}, u32[]{:S(2)}) collective-permute-start(bf16[2,2,32,256]{3,2,1,0:T(8,128)(2,1)S(1)} %shard_map.84.rest_0_), channel_id=1, source_target_pairs={{0,8},{4,12},{8,0},{12,4},{1,9},{5,13},{9,1},{13,5},{2,10},{6,14},... | collective-permute-start | bytes 196616 | tf_op jit(solution)/shard_map/ppermute | solution.py:515
  71.5 2.3 %collective-permute-start.20 = (bf16[2,2,32,256]{3,2,1,0:T(8,128)(2,1)S(1)}, bf16[2,2,32,256]{3,2,1,0:T(8,128)(2,1)S(1)}, u32[]{:S(2)}, u32[]{:S(2)}) collective-permute-start(bf16[2,2,32,256]{3,2,1,0:T(8,128)(2,1)S(1)} %shard_map.84.rest_0_), channel_id=1, source_target_pairs={{0,4},{4,0},{8,12},{12,8},{1,5},{5,1},{9,13},{13,9},{2,6},{6,2},{1... | collective-permute-start | bytes 196616 | tf_op jit(solution)/shard_map/ppermute | solution.py:515
  73.8 2.8 %collective-permute-start.19 = (bf16[2,2,32,256]{3,2,1,0:T(8,128)(2,1)S(1)}, bf16[2,2,32,256]{3,2,1,0:T(8,128)(2,1)S(1)}, u32[]{:S(2)}, u32[]{:S(2)}) collective-permute-start(bf16[2,2,32,256]{3,2,1,0:T(8,128)(2,1)S(1)} %collective-permute-done.18.rest_1_), channel_id=1, source_target_pairs={{0,4},{4,0},{8,12},{12,8},{1,5},{5,1},{9,13},{13,9},{2,6},{6,2},{1... | collective-permute-start | bytes 196616 | tf_op jit(solution)/shard_map/ppermute | solution.py:515
  76.7 2.0 %collective-permute-start.23 = (bf16[2,2,32,256]{3,2,1,0:T(8,128)(2,1)S(1)}, bf16[2,2,32,256]{3,2,1,0:T(8,128)(2,1)S(1)}, u32[]{:S(2)}, u32[]{:S(2)}) collective-permute-start(bf16[2,2,32,256]{3,2,1,0:T(8,128)(2,1)S(1)} %collective-permute-done.22.rest_1_), channel_id=1, source_target_pairs={{0,4},{4,0},{8,12},{12,8},{1,5},{5,1},{9,13},{13,9},{2,6},{6,2},{1... | collective-permute-start | bytes 196616 | tf_op jit(solution)/shard_map/ppermute | solution.py:515
  83.9 2.4 %collective-permute-done.26.rest_2_ = bf16[2,2,32,256]{3,2,1,0:T(8,128)(2,1)S(1)} collective-permute-done((bf16[2,2,32,256]{3,2,1,0:T(8,128)(2,1)S(1)}, bf16[2,2,32,256]{3,2,1,0:T(8,128)(2,1)S(1)}, u32[]{:S(2)}, u32[]{:S(2)}) %collective-permute-start.26) | collective-permute-done | bytes 65568 | tf_op jit(solution)/shard_map/ppermute | solution.py:515
  88.0 3.0 %collective-permute-start.28 = (bf16[64,1024]{1,0:T(8,128)(2,1)S(1)}, bf16[64,1024]{1,0:T(8,128)(2,1)S(1)}, u32[]{:S(2)}, u32[]{:S(2)}) collective-permute-start(bf16[64,1024]{1,0:T(8,128)(2,1)S(1)} %get-tuple-element.89), channel_id=1, source_target_pairs={{0,12},{4,8},{8,4},{12,0},{1,13},{5,9},{9,5},{13,1},{2,14},{6,10},... | collective-permute-start | bytes 393224 | tf_op jit(solution)/shard_map/ppermute | solution.py:515
  91.0 5.1 %collective-permute-done.27.rest_1_ = bf16[64,1024]{1,0:T(8,128)(2,1)S(1)} collective-permute-done((bf16[64,1024]{1,0:T(8,128)(2,1)S(1)}, bf16[64,1024]{1,0:T(8,128)(2,1)S(1)}, u32[]{:S(2)}, u32[]{:S(2)}) %collective-permute-start.27) | collective-permute-done | bytes 131104 | tf_op jit(solution)/shard_map/ppermute | solution.py:515
  96.0 1.5 %collective-permute-done.29.rest_3_ = bf16[64,1024]{1,0:T(8,128)(2,1)S(1)} collective-permute-done((bf16[64,1024]{1,0:T(8,128)(2,1)S(1)}, bf16[64,1024]{1,0:T(8,128)(2,1)S(1)}, u32[]{:S(2)}, u32[]{:S(2)}) %collective-permute-start.29) | collective-permute-done | bytes 131104 | tf_op jit(solution)/shard_map/ppermute | solution.py:515
  98.2 4.9 %collective-permute-start.30 = (bf16[64,1024]{1,0:T(8,128)(2,1)S(1)}, bf16[64,1024]{1,0:T(8,128)(2,1)S(1)}, u32[]{:S(2)}, u32[]{:S(2)}) collective-permute-start(bf16[64,1024]{1,0:T(8,128)(2,1)S(1)} %get-tuple-element.92), channel_id=1, source_target_pairs={{0,8},{4,12},{8,0},{12,4},{1,9},{5,13},{9,1},{13,5},{2,10},{6,14},... | collective-permute-start | bytes 393224 | tf_op jit(solution)/shard_map/ppermute | solution.py:515
  103.1 1.7 %collective-permute-start.31 = (bf16[64,1024]{1,0:T(8,128)(2,1)S(1)}, bf16[64,1024]{1,0:T(8,128)(2,1)S(1)}, u32[]{:S(2)}, u32[]{:S(2)}) collective-permute-start(bf16[64,1024]{1,0:T(8,128)(2,1)S(1)} %get-tuple-element.93), channel_id=1, source_target_pairs={{0,12},{4,8},{8,4},{12,0},{1,13},{5,9},{9,5},{13,1},{2,14},{6,10},... | collective-permute-start | bytes 393224 | tf_op jit(solution)/shard_map/ppermute | solution.py:515
  106.1 4.0 %collective-permute-done.31.rest_6_ = bf16[64,1024]{1,0:T(8,128)(2,1)S(1)} collective-permute-done((bf16[64,1024]{1,0:T(8,128)(2,1)S(1)}, bf16[64,1024]{1,0:T(8,128)(2,1)S(1)}, u32[]{:S(2)}, u32[]{:S(2)}) %collective-permute-start.31) | collective-permute-done | bytes 131104 | tf_op jit(solution)/shard_map/ppermute | solution.py:515
  110.0 3.3 %collective-permute-done.32.rest_7_ = bf16[64,1024]{1,0:T(8,128)(2,1)S(1)} collective-permute-done((bf16[64,1024]{1,0:T(8,128)(2,1)S(1)}, bf16[64,1024]{1,0:T(8,128)(2,1)S(1)}, u32[]{:S(2)}, u32[]{:S(2)}) %collective-permute-start.32) | collective-permute-done | bytes 131104 | tf_op jit(solution)/shard_map/ppermute | solution.py:515
  113.9 2.0 %collective-permute-start.33 = (bf16[2,2,32,256]{3,2,1,0:T(8,128)(2,1)S(1)}, bf16[2,2,32,256]{3,2,1,0:T(8,128)(2,1)S(1)}, u32[]{:S(2)}, u32[]{:S(2)}) collective-permute-start(bf16[2,2,32,256]{3,2,1,0:T(8,128)(2,1)S(1)} %get-tuple-element.96), channel_id=1, source_target_pairs={{0,2},{2,0},{1,3},{3,1},{4,6},{6,4},{5,7},{7,5},{8,10},{10,8},{9,1... | collective-permute-start | bytes 196616 | tf_op jit(solution)/shard_map/ppermute | solution.py:515
  116.4 1.8 %collective-permute-done.34.r_ref = bf16[2,2,32,256]{3,2,1,0:T(8,128)(2,1)S(1)} collective-permute-done((bf16[2,2,32,256]{3,2,1,0:T(8,128)(2,1)S(1)}, bf16[2,2,32,256]{3,2,1,0:T(8,128)(2,1)S(1)}, u32[]{:S(2)}, u32[]{:S(2)}) %collective-permute-start.34) | collective-permute-done | bytes 65568 | tf_op jit(solution)/shard_map/ppermute | solution.py:515
  118.9 2.1 %collective-permute-start.37 = (bf16[2,2,64,256]{3,2,1,0:T(8,128)(2,1)S(1)}, bf16[2,2,64,256]{3,2,1,0:T(8,128)(2,1)S(1)}, u32[]{:S(2)}, u32[]{:S(2)}) collective-permute-start(bf16[2,2,64,256]{3,2,1,0:T(8,128)(2,1)S(1)} %get-tuple-element.99.rest_0_), channel_id=1, source_target_pairs={{0,4},{4,0},{8,12},{12,8},{1,5},{5,1},{9,13},{13,9},{2,6},{6,2},{1... | collective-permute-start | bytes 393224 | tf_op jit(solution)/shard_map/ppermute | solution.py:515
  120.9 1.6 %collective-permute-start.35 = (bf16[2,2,32,256]{3,2,1,0:T(8,128)(2,1)S(1)}, bf16[2,2,32,256]{3,2,1,0:T(8,128)(2,1)S(1)}, u32[]{:S(2)}, u32[]{:S(2)}) collective-permute-start(bf16[2,2,32,256]{3,2,1,0:T(8,128)(2,1)S(1)} %get-tuple-element.100), channel_id=1, source_target_pairs={{0,8},{4,12},{8,0},{12,4},{1,9},{5,13},{9,1},{13,5},{2,10},{6,14},... | collective-permute-start | bytes 196616 | tf_op jit(solution)/shard_map/ppermute | solution.py:515
  123.5 3.3 %collective-permute-done.35.rest_1_ = bf16[2,2,32,256]{3,2,1,0:T(8,128)(2,1)S(1)} collective-permute-done((bf16[2,2,32,256]{3,2,1,0:T(8,128)(2,1)S(1)}, bf16[2,2,32,256]{3,2,1,0:T(8,128)(2,1)S(1)}, u32[]{:S(2)}, u32[]{:S(2)}) %collective-permute-start.35) | collective-permute-done | bytes 65568 | tf_op jit(solution)/shard_map/ppermute | solution.py:515
  127.8 2.0 %shard_map.95.rest_4_ = bf16[64,128,256]{2,1,0:T(8,128)(2,1)} custom-call(s32[1]{0:T(128)} %bitcast._.freq.place_ref, s32[1]{0:T(128)} %bitcast.1.rblk._, s32[1]{0:T(128)} %bitcast.2.__.sblk, bf16[64,128,256]{2,1,0:T(8,128)(2,1)S(1)} %copy-done.1, s32[128,256]{1,0:T(8,128)S(1)} %copy-done.4, bf16[4,128,128]{2,1,0:T(8,128)(2,1)S(1)} %copy-done.5, ...), custom_call_target="tpu_custom_call" | custom-call | flops 33554432 | bytes 9043968 | tf_op jit(solution)/shard_map/pallas_call | solution.py:78
  131.0 1.9 %shard_map.96 = bf16[64,128,256]{2,1,0:T(8,128)(2,1)} custom-call(s32[1]{0:T(128)} %bitcast._.freq.place_ref, s32[1]{0:T(128)} %bitcast.1.rblk._, s32[1]{0:T(128)} %bitcast.2.__.sblk, bf16[64,128,256]{2,1,0:T(8,128)(2,1)S(1)} %copy-done.1, s32[128,256]{1,0:T(8,128)S(1)} %copy-done.4, ...), custom_call_target="tpu_custom_call", output_to_operand_aliasing={{}: (10, {})} | custom-call | flops 33554432 | bytes 13238272 | tf_op jit(solution)/shard_map/pallas_call | solution.py:78
  (87 shorter events, 30.8 us)
Async XLA Ops:
  2.6 21.3 %collective-permute-start.6 = (bf16[2,256,512]{2,1,0:T(8,128)(2,1)S(1)}, bf16[2,256,512]{2,1,0:T(8,128)(2,1)S(1)}, u32[]{:S(2)}, u32[]{:S(2)}) collective-permute-start(bf16[2,256,512]{2,1,0:T(8,128)(2,1)S(1)} %get-tuple-element.68), channel_id=1, source_target_pairs={{0,2},{2,0},{1,3},{3,1},{4,6},{6,4},{5,7},{7,5},{8,10},{10,8},{9,1... | collective-permute-start | bytes 1572872 | tf_op jit(solution)/shard_map/ppermute | solution.py:515
  5.6 26.0 %collective-permute-start.7 = (bf16[2,256,512]{2,1,0:T(8,128)(2,1)S(1)}, bf16[2,256,512]{2,1,0:T(8,128)(2,1)S(1)}, u32[]{:S(2)}, u32[]{:S(2)}) collective-permute-start(bf16[2,256,512]{2,1,0:T(8,128)(2,1)S(1)} %get-tuple-element.71), channel_id=1, source_target_pairs={{0,2},{2,0},{1,3},{3,1},{4,6},{6,4},{5,7},{7,5},{8,10},{10,8},{9,1... | collective-permute-start | bytes 1572872 | tf_op jit(solution)/shard_map/ppermute | solution.py:515
  8.6 12.9 %collective-permute-start.3 = (bf16[2,2,64,256]{3,2,1,0:T(8,128)(2,1)S(1)}, bf16[2,2,64,256]{3,2,1,0:T(8,128)(2,1)S(1)}, u32[]{:S(2)}, u32[]{:S(2)}) collective-permute-start(bf16[2,2,64,256]{3,2,1,0:T(8,128)(2,1)S(1)} %get-tuple-element.61), channel_id=1, source_target_pairs={{0,8},{4,12},{8,0},{12,4},{1,9},{5,13},{9,1},{13,5},{2,10},{6,14},... | collective-permute-start | bytes 393224 | tf_op jit(solution)/shard_map/ppermute | solution.py:515
  11.7 9.8 %collective-permute-start.4 = (bf16[2,2,64,256]{3,2,1,0:T(8,128)(2,1)S(1)}, bf16[2,2,64,256]{3,2,1,0:T(8,128)(2,1)S(1)}, u32[]{:S(2)}, u32[]{:S(2)}) collective-permute-start(bf16[2,2,64,256]{3,2,1,0:T(8,128)(2,1)S(1)} %get-tuple-element.62), channel_id=1, source_target_pairs={{0,12},{4,8},{8,4},{12,0},{1,13},{5,9},{9,5},{13,1},{2,14},{6,10},... | collective-permute-start | bytes 393224 | tf_op jit(solution)/shard_map/ppermute | solution.py:515
  13.1 8.6 %collective-permute-start.5 = (bf16[2,2,64,256]{3,2,1,0:T(8,128)(2,1)S(1)}, bf16[2,2,64,256]{3,2,1,0:T(8,128)(2,1)S(1)}, u32[]{:S(2)}, u32[]{:S(2)}) collective-permute-start(bf16[2,2,64,256]{3,2,1,0:T(8,128)(2,1)S(1)} %get-tuple-element.63), channel_id=1, source_target_pairs={{0,4},{4,0},{8,12},{12,8},{1,5},{5,1},{9,13},{13,9},{2,6},{6,2},{1... | collective-permute-start | bytes 393224 | tf_op jit(solution)/shard_map/ppermute | solution.py:515
  21.8 9.8 %collective-permute-start.8 = (bf16[2,2,64,256]{3,2,1,0:T(8,128)(2,1)S(1)}, bf16[2,2,64,256]{3,2,1,0:T(8,128)(2,1)S(1)}, u32[]{:S(2)}, u32[]{:S(2)}) collective-permute-start(bf16[2,2,64,256]{3,2,1,0:T(8,128)(2,1)S(1)} %get-tuple-element.70.rest_0_), channel_id=1, source_target_pairs={{0,2},{2,0},{1,3},{3,1},{4,6},{6,4},{5,7},{7,5},{8,10},{10,8},{9,1... | collective-permute-start | bytes 393224 | tf_op jit(solution)/shard_map/ppermute | solution.py:515
  23.4 8.2 %collective-permute-start = (bf16[2,256,512]{2,1,0:T(8,128)(2,1)S(1)}, bf16[2,256,512]{2,1,0:T(8,128)(2,1)S(1)}, u32[]{:S(2)}, u32[]{:S(2)}) collective-permute-start(bf16[2,256,512]{2,1,0:T(8,128)(2,1)S(1)} %get-tuple-element.53.rest_1_.rest_0_.rest_2_), channel_id=1, source_target_pairs={{0,1},{1,0},{2,3},{3,2},{4,5},{5,4},{6,7},{7,6},{8,9},{9,8},{10,11... | collective-permute-start | bytes 1572872 | tf_op jit(solution)/shard_map/ppermute | solution.py:515
  23.4 8.2 %collective-permute-start.1 = (bf16[2,256,512]{2,1,0:T(8,128)(2,1)S(1)}, bf16[2,256,512]{2,1,0:T(8,128)(2,1)S(1)}, u32[]{:S(2)}, u32[]{:S(2)}) collective-permute-start(bf16[2,256,512]{2,1,0:T(8,128)(2,1)S(1)} %get-tuple-element.54.rest_3_.rest_2_.rest_4_), channel_id=1, source_target_pairs={{0,1},{1,0},{2,3},{3,2},{4,5},{5,4},{6,7},{7,6},{8,9},{9,8},{10,11... | collective-permute-start | bytes 1572872 | tf_op jit(solution)/shard_map/ppermute | solution.py:515
  23.9 8.5 %collective-permute-start.9 = (bf16[2,256,512]{2,1,0:T(8,128)(2,1)S(1)}, bf16[2,256,512]{2,1,0:T(8,128)(2,1)S(1)}, u32[]{:S(2)}, u32[]{:S(2)}) collective-permute-start(bf16[2,256,512]{2,1,0:T(8,128)(2,1)S(1)} %collective-permute-done.6.rest_2_.rest_0_.rest_3_), channel_id=1, source_target_pairs={{0,1},{1,0},{2,3},{3,2},{4,5},{5,4},{6,7},{7,6},{8,9},{9,8},{10,11... | collective-permute-start | bytes 1572872 | tf_op jit(solution)/shard_map/ppermute | solution.py:515
  34.0 12.9 %collective-permute-start.11 = (bf16[64,1024]{1,0:T(8,128)(2,1)S(1)}, bf16[64,1024]{1,0:T(8,128)(2,1)S(1)}, u32[]{:S(2)}, u32[]{:S(2)}) collective-permute-start(bf16[64,1024]{1,0:T(8,128)(2,1)S(1)} %get-tuple-element.76), channel_id=1, source_target_pairs={{0,8},{4,12},{8,0},{12,4},{1,9},{5,13},{9,1},{13,5},{2,10},{6,14},... | collective-permute-start | bytes 393224 | tf_op jit(solution)/shard_map/ppermute | solution.py:515
  36.9 10.0 %collective-permute-start.12 = (bf16[64,1024]{1,0:T(8,128)(2,1)S(1)}, bf16[64,1024]{1,0:T(8,128)(2,1)S(1)}, u32[]{:S(2)}, u32[]{:S(2)}) collective-permute-start(bf16[64,1024]{1,0:T(8,128)(2,1)S(1)} %get-tuple-element.77), channel_id=1, source_target_pairs={{0,12},{4,8},{8,4},{12,0},{1,13},{5,9},{9,5},{13,1},{2,14},{6,10},... | collective-permute-start | bytes 393224 | tf_op jit(solution)/shard_map/ppermute | solution.py:515
  38.2 9.5 %collective-permute-start.13 = (bf16[64,1024]{1,0:T(8,128)(2,1)S(1)}, bf16[64,1024]{1,0:T(8,128)(2,1)S(1)}, u32[]{:S(2)}, u32[]{:S(2)}) collective-permute-start(bf16[64,1024]{1,0:T(8,128)(2,1)S(1)} %get-tuple-element.78), channel_id=1, source_target_pairs={{0,4},{4,0},{8,12},{12,8},{1,5},{5,1},{9,13},{13,9},{2,6},{6,2},{1... | collective-permute-start | bytes 393224 | tf_op jit(solution)/shard_map/ppermute | solution.py:515
  48.4 13.8 %collective-permute-start.14 = (bf16[64,1024]{1,0:T(8,128)(2,1)S(1)}, bf16[64,1024]{1,0:T(8,128)(2,1)S(1)}, u32[]{:S(2)}, u32[]{:S(2)}) collective-permute-start(bf16[64,1024]{1,0:T(8,128)(2,1)S(1)} %get-tuple-element.80), channel_id=1, source_target_pairs={{0,8},{4,12},{8,0},{12,4},{1,9},{5,13},{9,1},{13,5},{2,10},{6,14},... | collective-permute-start | bytes 393224 | tf_op jit(solution)/shard_map/ppermute | solution.py:515
  52.6 9.6 %collective-permute-start.15 = (bf16[64,1024]{1,0:T(8,128)(2,1)S(1)}, bf16[64,1024]{1,0:T(8,128)(2,1)S(1)}, u32[]{:S(2)}, u32[]{:S(2)}) collective-permute-start(bf16[64,1024]{1,0:T(8,128)(2,1)S(1)} %get-tuple-element.81), channel_id=1, source_target_pairs={{0,12},{4,8},{8,4},{12,0},{1,13},{5,9},{9,5},{13,1},{2,14},{6,10},... | collective-permute-start | bytes 393224 | tf_op jit(solution)/shard_map/ppermute | solution.py:515
  53.0 10.3 %collective-permute-start.16 = (bf16[64,1024]{1,0:T(8,128)(2,1)S(1)}, bf16[64,1024]{1,0:T(8,128)(2,1)S(1)}, u32[]{:S(2)}, u32[]{:S(2)}) collective-permute-start(bf16[64,1024]{1,0:T(8,128)(2,1)S(1)} %get-tuple-element.82), channel_id=1, source_target_pairs={{0,4},{4,0},{8,12},{12,8},{1,5},{5,1},{9,13},{13,9},{2,6},{6,2},{1... | collective-permute-start | bytes 393224 | tf_op jit(solution)/shard_map/ppermute | solution.py:515
  65.3 4.7 %collective-permute-start.21 = (bf16[2,2,32,256]{3,2,1,0:T(8,128)(2,1)S(1)}, bf16[2,2,32,256]{3,2,1,0:T(8,128)(2,1)S(1)}, u32[]{:S(2)}, u32[]{:S(2)}) collective-permute-start(bf16[2,2,32,256]{3,2,1,0:T(8,128)(2,1)S(1)} %get-tuple-element.86), channel_id=1, source_target_pairs={{0,2},{2,0},{1,3},{3,1},{4,6},{6,4},{5,7},{7,5},{8,10},{10,8},{9,1... | collective-permute-start | bytes 196616 | tf_op jit(solution)/shard_map/ppermute | solution.py:515
  68.1 5.7 %collective-permute-start.18 = (bf16[2,2,32,256]{3,2,1,0:T(8,128)(2,1)S(1)}, bf16[2,2,32,256]{3,2,1,0:T(8,128)(2,1)S(1)}, u32[]{:S(2)}, u32[]{:S(2)}) collective-permute-start(bf16[2,2,32,256]{3,2,1,0:T(8,128)(2,1)S(1)} %shard_map.84.rest_0_), channel_id=1, source_target_pairs={{0,8},{4,12},{8,0},{12,4},{1,9},{5,13},{9,1},{13,5},{2,10},{6,14},... | collective-permute-start | bytes 196616 | tf_op jit(solution)/shard_map/ppermute | solution.py:515
  70.1 6.6 %collective-permute-start.22 = (bf16[2,2,32,256]{3,2,1,0:T(8,128)(2,1)S(1)}, bf16[2,2,32,256]{3,2,1,0:T(8,128)(2,1)S(1)}, u32[]{:S(2)}, u32[]{:S(2)}) collective-permute-start(bf16[2,2,32,256]{3,2,1,0:T(8,128)(2,1)S(1)} %shard_map.86.rest_0_), channel_id=1, source_target_pairs={{0,8},{4,12},{8,0},{12,4},{1,9},{5,13},{9,1},{13,5},{2,10},{6,14},... | collective-permute-start | bytes 196616 | tf_op jit(solution)/shard_map/ppermute | solution.py:515
  71.5 7.1 %collective-permute-start.20 = (bf16[2,2,32,256]{3,2,1,0:T(8,128)(2,1)S(1)}, bf16[2,2,32,256]{3,2,1,0:T(8,128)(2,1)S(1)}, u32[]{:S(2)}, u32[]{:S(2)}) collective-permute-start(bf16[2,2,32,256]{3,2,1,0:T(8,128)(2,1)S(1)} %shard_map.84.rest_0_), channel_id=1, source_target_pairs={{0,4},{4,0},{8,12},{12,8},{1,5},{5,1},{9,13},{13,9},{2,6},{6,2},{1... | collective-permute-start | bytes 196616 | tf_op jit(solution)/shard_map/ppermute | solution.py:515
  73.8 5.1 %collective-permute-start.19 = (bf16[2,2,32,256]{3,2,1,0:T(8,128)(2,1)S(1)}, bf16[2,2,32,256]{3,2,1,0:T(8,128)(2,1)S(1)}, u32[]{:S(2)}, u32[]{:S(2)}) collective-permute-start(bf16[2,2,32,256]{3,2,1,0:T(8,128)(2,1)S(1)} %collective-permute-done.18.rest_1_), channel_id=1, source_target_pairs={{0,4},{4,0},{8,12},{12,8},{1,5},{5,1},{9,13},{13,9},{2,6},{6,2},{1... | collective-permute-start | bytes 196616 | tf_op jit(solution)/shard_map/ppermute | solution.py:515
  76.7 4.9 %collective-permute-start.23 = (bf16[2,2,32,256]{3,2,1,0:T(8,128)(2,1)S(1)}, bf16[2,2,32,256]{3,2,1,0:T(8,128)(2,1)S(1)}, u32[]{:S(2)}, u32[]{:S(2)}) collective-permute-start(bf16[2,2,32,256]{3,2,1,0:T(8,128)(2,1)S(1)} %collective-permute-done.22.rest_1_), channel_id=1, source_target_pairs={{0,4},{4,0},{8,12},{12,8},{1,5},{5,1},{9,13},{13,9},{2,6},{6,2},{1... | collective-permute-start | bytes 196616 | tf_op jit(solution)/shard_map/ppermute | solution.py:515
  79.3 4.6 %collective-permute-start.25 = (bf16[2,2,32,256]{3,2,1,0:T(8,128)(2,1)S(1)}, bf16[2,2,32,256]{3,2,1,0:T(8,128)(2,1)S(1)}, u32[]{:S(2)}, u32[]{:S(2)}) collective-permute-start(bf16[2,2,32,256]{3,2,1,0:T(8,128)(2,1)S(1)} %shard_map.85.rest_0_), channel_id=1, source_target_pairs={{0,2},{2,0},{1,3},{3,1},{4,6},{6,4},{5,7},{7,5},{8,10},{10,8},{9,1... | collective-permute-start | bytes 196616 | tf_op jit(solution)/shard_map/ppermute | solution.py:515
  87.2 8.8 %collective-permute-start.27 = (bf16[64,1024]{1,0:T(8,128)(2,1)S(1)}, bf16[64,1024]{1,0:T(8,128)(2,1)S(1)}, u32[]{:S(2)}, u32[]{:S(2)}) collective-permute-start(bf16[64,1024]{1,0:T(8,128)(2,1)S(1)} %get-tuple-element.88), channel_id=1, source_target_pairs={{0,8},{4,12},{8,0},{12,4},{1,9},{5,13},{9,1},{13,5},{2,10},{6,14},... | collective-permute-start | bytes 393224 | tf_op jit(solution)/shard_map/ppermute | solution.py:515
  88.0 8.1 %collective-permute-start.28 = (bf16[64,1024]{1,0:T(8,128)(2,1)S(1)}, bf16[64,1024]{1,0:T(8,128)(2,1)S(1)}, u32[]{:S(2)}, u32[]{:S(2)}) collective-permute-start(bf16[64,1024]{1,0:T(8,128)(2,1)S(1)} %get-tuple-element.89), channel_id=1, source_target_pairs={{0,12},{4,8},{8,4},{12,0},{1,13},{5,9},{9,5},{13,1},{2,14},{6,10},... | collective-permute-start | bytes 393224 | tf_op jit(solution)/shard_map/ppermute | solution.py:515
  91.0 6.6 %collective-permute-start.29 = (bf16[64,1024]{1,0:T(8,128)(2,1)S(1)}, bf16[64,1024]{1,0:T(8,128)(2,1)S(1)}, u32[]{:S(2)}, u32[]{:S(2)}) collective-permute-start(bf16[64,1024]{1,0:T(8,128)(2,1)S(1)} %get-tuple-element.90), channel_id=1, source_target_pairs={{0,4},{4,0},{8,12},{12,8},{1,5},{5,1},{9,13},{13,9},{2,6},{6,2},{1... | collective-permute-start | bytes 393224 | tf_op jit(solution)/shard_map/ppermute | solution.py:515
  98.2 7.8 %collective-permute-start.30 = (bf16[64,1024]{1,0:T(8,128)(2,1)S(1)}, bf16[64,1024]{1,0:T(8,128)(2,1)S(1)}, u32[]{:S(2)}, u32[]{:S(2)}) collective-permute-start(bf16[64,1024]{1,0:T(8,128)(2,1)S(1)} %get-tuple-element.92), channel_id=1, source_target_pairs={{0,8},{4,12},{8,0},{12,4},{1,9},{5,13},{9,1},{13,5},{2,10},{6,14},... | collective-permute-start | bytes 393224 | tf_op jit(solution)/shard_map/ppermute | solution.py:515
  103.1 6.9 %collective-permute-start.31 = (bf16[64,1024]{1,0:T(8,128)(2,1)S(1)}, bf16[64,1024]{1,0:T(8,128)(2,1)S(1)}, u32[]{:S(2)}, u32[]{:S(2)}) collective-permute-start(bf16[64,1024]{1,0:T(8,128)(2,1)S(1)} %get-tuple-element.93), channel_id=1, source_target_pairs={{0,12},{4,8},{8,4},{12,0},{1,13},{5,9},{9,5},{13,1},{2,14},{6,10},... | collective-permute-start | bytes 393224 | tf_op jit(solution)/shard_map/ppermute | solution.py:515
  104.8 8.5 %collective-permute-start.32 = (bf16[64,1024]{1,0:T(8,128)(2,1)S(1)}, bf16[64,1024]{1,0:T(8,128)(2,1)S(1)}, u32[]{:S(2)}, u32[]{:S(2)}) collective-permute-start(bf16[64,1024]{1,0:T(8,128)(2,1)S(1)} %get-tuple-element.94), channel_id=1, source_target_pairs={{0,4},{4,0},{8,12},{12,8},{1,5},{5,1},{9,13},{13,9},{2,6},{6,2},{1... | collective-permute-start | bytes 393224 | tf_op jit(solution)/shard_map/ppermute | solution.py:515
  113.9 5.0 %collective-permute-start.33 = (bf16[2,2,32,256]{3,2,1,0:T(8,128)(2,1)S(1)}, bf16[2,2,32,256]{3,2,1,0:T(8,128)(2,1)S(1)}, u32[]{:S(2)}, u32[]{:S(2)}) collective-permute-start(bf16[2,2,32,256]{3,2,1,0:T(8,128)(2,1)S(1)} %get-tuple-element.96), channel_id=1, source_target_pairs={{0,2},{2,0},{1,3},{3,1},{4,6},{6,4},{5,7},{7,5},{8,10},{10,8},{9,1... | collective-permute-start | bytes 196616 | tf_op jit(solution)/shard_map/ppermute | solution.py:515
  118.1 5.3 %collective-permute-start.38 = (bf16[2,2,32,256]{3,2,1,0:T(8,128)(2,1)S(1)}, bf16[2,2,32,256]{3,2,1,0:T(8,128)(2,1)S(1)}, u32[]{:S(2)}, u32[]{:S(2)}) collective-permute-start(bf16[2,2,32,256]{3,2,1,0:T(8,128)(2,1)S(1)} %shard_map.93.rest_0_), channel_id=1, source_target_pairs={{0,8},{4,12},{8,0},{12,4},{1,9},{5,13},{9,1},{13,5},{2,10},{6,14},... | collective-permute-start | bytes 196616 | tf_op jit(solution)/shard_map/ppermute | solution.py:515
  118.9 8.9 %collective-permute-start.37 = (bf16[2,2,64,256]{3,2,1,0:T(8,128)(2,1)S(1)}, bf16[2,2,64,256]{3,2,1,0:T(8,128)(2,1)S(1)}, u32[]{:S(2)}, u32[]{:S(2)}) collective-permute-start(bf16[2,2,64,256]{3,2,1,0:T(8,128)(2,1)S(1)} %get-tuple-element.99.rest_0_), channel_id=1, source_target_pairs={{0,4},{4,0},{8,12},{12,8},{1,5},{5,1},{9,13},{13,9},{2,6},{6,2},{1... | collective-permute-start | bytes 393224 | tf_op jit(solution)/shard_map/ppermute | solution.py:515
  120.9 5.9 %collective-permute-start.35 = (bf16[2,2,32,256]{3,2,1,0:T(8,128)(2,1)S(1)}, bf16[2,2,32,256]{3,2,1,0:T(8,128)(2,1)S(1)}, u32[]{:S(2)}, u32[]{:S(2)}) collective-permute-start(bf16[2,2,32,256]{3,2,1,0:T(8,128)(2,1)S(1)} %get-tuple-element.100), channel_id=1, source_target_pairs={{0,8},{4,12},{8,0},{12,4},{1,9},{5,13},{9,1},{13,5},{2,10},{6,14},... | collective-permute-start | bytes 196616 | tf_op jit(solution)/shard_map/ppermute | solution.py:515
  (15 other events, 169.7 us)

commit v18 on v14

--- a/solution.py
+++ b/solution.py
@@ -310,12 +310,12 @@
     return jnp.stack([real, imag])
 
 
-def tiles(width, body):
+def tiles(width, body, unroll):
     def at(step, carry):
         body(pl.ds(pl.multiple_of(step * BLOCK, BLOCK), BLOCK))
         return carry
 
-    lax.fori_loop(0, width // BLOCK, at, 0, unroll=2)
+    lax.fori_loop(0, width // BLOCK, at, 0, unroll=unroll)
 
 
 def windowed(messages, tables, matrix, freq_place, per_dev, share):
@@ -343,7 +343,7 @@
             for out, value in zip(outs, made):
                 out[:, at] = jnp.concatenate(value, 2).reshape(out.shape[0], BLOCK).astype(BF16)
 
-        tiles(width, one)
+        tiles(width, one, 4)
 
     inputs = (cosines, sines, fraction, matrix, *messages)
     return call(
@@ -425,7 +425,7 @@
                     made.append(u_ref[:, :, cut, at] - change)
                 out[:, :, pair, at] = jnp.concatenate(made, 2).astype(BF16)
 
-        tiles(rcv, one)
+        tiles(rcv, one, 2)
 
     inputs = (sums, cosines, sines, fraction, matrix, *messages)
     shape = jax.ShapeDtypeStruct(messages[0].shape, BF16)

time: 130 us -> 131 us (level)
  waiting for transfers between devices: 56.2 us -> 58.9 us
    ppermute x41, waiting for transfers between devices: 56.2 us -> 58.9 us  [exchanged(): lax.ppermute(value, axis, [(i, i ^ step) for i in range(lax.axis_size(axi...]
  transfers between devices with their start and end apart: 41 -> 41, of which waited for: 22 -> 24; matrix products, arithmetic and copies ran while one was open for 0% -> 0% of each run, Pallas kernels for 6% -> 6%
where the time goes in v18:
time: 131 us
  waiting for transfers between devices  58.9 us (45%)
  starting transfers between devices  53.3 us (41%)
  Pallas kernels  13.5 us (10%)
  local copies, waits for them, and re-layouts  4.56 us (3%)
    ppermute x41, waiting for transfers between devices, exchanged(): lax.ppermute(value, axis, [(i, i ^ step) for i in range(lax.axis_size(axi...  58.9 us
    ppermute x41, starting transfers between devices, exchanged(): lax.ppermute(value, axis, [(i, i ^ step) for i in range(lax.axis_size(axi...  53.3 us
    pallas_call x24, Pallas kernels, call(): pl.pallas_call(body, grid_spec=pltpu.PrefetchScalarGridSpec(num_scalar_pr...  13.5 us
    unnamed x15, local copies, waits for them, and re-layouts  4.56 us
  transfers between devices with their start and end apart: 41, of which 24 were waited for; matrix products, arithmetic and copies ran while one was open for 0% of the time, Pallas kernels for 6%

profile of v18, /device:TPU:0, one launch (start us, length us, event | category | flops | bytes accessed | tf_op | source)
XLA Modules:
  0.0 130.6 jit_solution(17941931122856187137)
XLA Ops:
  0.8 1.6 %copy-done.2 = bf16[2,2,1024,256]{3,2,1,0:T(8,128)(2,1)S(1)} copy-done((bf16[2,2,1024,256]{3,2,1,0:T(8,128)(2,1)S(1)}, bf16[2,2,1024,256]{3,2,1,0:T(8,128)(2,1)}, u32[]{:S(2)}) %copy-start.2) | copy-done | bytes 2097176
  2.6 3.0 %collective-permute-start.6 = (bf16[2,256,512]{2,1,0:T(8,128)(2,1)S(1)}, bf16[2,256,512]{2,1,0:T(8,128)(2,1)S(1)}, u32[]{:S(2)}, u32[]{:S(2)}) collective-permute-start(bf16[2,256,512]{2,1,0:T(8,128)(2,1)S(1)} %get-tuple-element.66), channel_id=1, source_target_pairs={{0,2},{2,0},{1,3},{3,1},{4,6},{6,4},{5,7},{7,5},{8,10},{10,8},{9,1... | collective-permute-start | bytes 1572872 | tf_op jit(solution)/shard_map/ppermute | solution.py:495
  5.7 2.2 %copy-done = bf16[64,128,256]{2,1,0:T(8,128)(2,1)S(1)} copy-done((bf16[64,128,256]{2,1,0:T(8,128)(2,1)S(1)}, bf16[64,128,256]{2,1,0:T(8,128)(2,1)}, u32[]{:S(2)}) %copy-start) | copy-done | bytes 4194328
  8.6 3.1 %collective-permute-start.3 = (bf16[2,2,64,256]{3,2,1,0:T(8,128)(2,1)S(1)}, bf16[2,2,64,256]{3,2,1,0:T(8,128)(2,1)S(1)}, u32[]{:S(2)}, u32[]{:S(2)}) collective-permute-start(bf16[2,2,64,256]{3,2,1,0:T(8,128)(2,1)S(1)} %get-tuple-element.59), channel_id=1, source_target_pairs={{0,8},{4,12},{8,0},{12,4},{1,9},{5,13},{9,1},{13,5},{2,10},{6,14},... | collective-permute-start | bytes 393224 | tf_op jit(solution)/shard_map/ppermute | solution.py:495
  13.3 8.2 %collective-permute-done.3.refs_1_ = bf16[2,2,64,256]{3,2,1,0:T(8,128)(2,1)S(1)} collective-permute-done((bf16[2,2,64,256]{3,2,1,0:T(8,128)(2,1)S(1)}, bf16[2,2,64,256]{3,2,1,0:T(8,128)(2,1)S(1)}, u32[]{:S(2)}, u32[]{:S(2)}) %collective-permute-start.3) | collective-permute-done | bytes 131104 | tf_op jit(solution)/shard_map/ppermute | solution.py:495
  21.8 1.6 %collective-permute-start.8 = (bf16[2,2,64,256]{3,2,1,0:T(8,128)(2,1)S(1)}, bf16[2,2,64,256]{3,2,1,0:T(8,128)(2,1)S(1)}, u32[]{:S(2)}, u32[]{:S(2)}) collective-permute-start(bf16[2,2,64,256]{3,2,1,0:T(8,128)(2,1)S(1)} %get-tuple-element.68.rest_0_), channel_id=1, source_target_pairs={{0,2},{2,0},{1,3},{3,1},{4,6},{6,4},{5,7},{7,5},{8,10},{10,8},{9,1... | collective-permute-start | bytes 393224 | tf_op jit(solution)/shard_map/ppermute | solution.py:495
  24.0 7.6 %collective-permute-done.8.rest_1_ = bf16[2,2,64,256]{3,2,1,0:T(8,128)(2,1)S(1)} collective-permute-done((bf16[2,2,64,256]{3,2,1,0:T(8,128)(2,1)S(1)}, bf16[2,2,64,256]{3,2,1,0:T(8,128)(2,1)S(1)}, u32[]{:S(2)}, u32[]{:S(2)}) %collective-permute-start.8) | collective-permute-done | bytes 131104 | tf_op jit(solution)/shard_map/ppermute | solution.py:495
  34.0 2.9 %collective-permute-start.11 = (bf16[64,1024]{1,0:T(8,128)(2,1)S(1)}, bf16[64,1024]{1,0:T(8,128)(2,1)S(1)}, u32[]{:S(2)}, u32[]{:S(2)}) collective-permute-start(bf16[64,1024]{1,0:T(8,128)(2,1)S(1)} %get-tuple-element.74), channel_id=1, source_target_pairs={{0,8},{4,12},{8,0},{12,4},{1,9},{5,13},{9,1},{13,5},{2,10},{6,14},... | collective-permute-start | bytes 393224 | tf_op jit(solution)/shard_map/ppermute | solution.py:495
  41.1 5.8 %collective-permute-done.11.rest_1_ = bf16[64,1024]{1,0:T(8,128)(2,1)S(1)} collective-permute-done((bf16[64,1024]{1,0:T(8,128)(2,1)S(1)}, bf16[64,1024]{1,0:T(8,128)(2,1)S(1)}, u32[]{:S(2)}, u32[]{:S(2)}) %collective-permute-start.11) | collective-permute-done | bytes 131104 | tf_op jit(solution)/shard_map/ppermute | solution.py:495
  48.4 4.2 %collective-permute-start.14 = (bf16[64,1024]{1,0:T(8,128)(2,1)S(1)}, bf16[64,1024]{1,0:T(8,128)(2,1)S(1)}, u32[]{:S(2)}, u32[]{:S(2)}) collective-permute-start(bf16[64,1024]{1,0:T(8,128)(2,1)S(1)} %get-tuple-element.78), channel_id=1, source_target_pairs={{0,8},{4,12},{8,0},{12,4},{1,9},{5,13},{9,1},{13,5},{2,10},{6,14},... | collective-permute-start | bytes 393224 | tf_op jit(solution)/shard_map/ppermute | solution.py:495
  53.2 9.0 %collective-permute-done.14.rest_5_ = bf16[64,1024]{1,0:T(8,128)(2,1)S(1)} collective-permute-done((bf16[64,1024]{1,0:T(8,128)(2,1)S(1)}, bf16[64,1024]{1,0:T(8,128)(2,1)S(1)}, u32[]{:S(2)}, u32[]{:S(2)}) %collective-permute-start.14) | collective-permute-done | bytes 131104 | tf_op jit(solution)/shard_map/ppermute | solution.py:495
  63.7 1.6 %collective-permute-start.17 = (bf16[2,2,32,256]{3,2,1,0:T(8,128)(2,1)S(1)}, bf16[2,2,32,256]{3,2,1,0:T(8,128)(2,1)S(1)}, u32[]{:S(2)}, u32[]{:S(2)}) collective-permute-start(bf16[2,2,32,256]{3,2,1,0:T(8,128)(2,1)S(1)} %get-tuple-element.82), channel_id=1, source_target_pairs={{0,2},{2,0},{1,3},{3,1},{4,6},{6,4},{5,7},{7,5},{8,10},{10,8},{9,1... | collective-permute-start | bytes 196616 | tf_op jit(solution)/shard_map/ppermute | solution.py:495
  66.3 1.8 %collective-permute-done.17.r_ref = bf16[2,2,32,256]{3,2,1,0:T(8,128)(2,1)S(1)} collective-permute-done((bf16[2,2,32,256]{3,2,1,0:T(8,128)(2,1)S(1)}, bf16[2,2,32,256]{3,2,1,0:T(8,128)(2,1)S(1)}, u32[]{:S(2)}, u32[]{:S(2)}) %collective-permute-start.17) | collective-permute-done | bytes 65568 | tf_op jit(solution)/shard_map/ppermute | solution.py:495
  68.1 1.9 %collective-permute-start.18 = (bf16[2,2,32,256]{3,2,1,0:T(8,128)(2,1)S(1)}, bf16[2,2,32,256]{3,2,1,0:T(8,128)(2,1)S(1)}, u32[]{:S(2)}, u32[]{:S(2)}) collective-permute-start(bf16[2,2,32,256]{3,2,1,0:T(8,128)(2,1)S(1)} %shard_map.84.rest_0_), channel_id=1, source_target_pairs={{0,8},{4,12},{8,0},{12,4},{1,9},{5,13},{9,1},{13,5},{2,10},{6,14},... | collective-permute-start | bytes 196616 | tf_op jit(solution)/shard_map/ppermute | solution.py:495
  70.1 1.5 %collective-permute-start.22 = (bf16[2,2,32,256]{3,2,1,0:T(8,128)(2,1)S(1)}, bf16[2,2,32,256]{3,2,1,0:T(8,128)(2,1)S(1)}, u32[]{:S(2)}, u32[]{:S(2)}) collective-permute-start(bf16[2,2,32,256]{3,2,1,0:T(8,128)(2,1)S(1)} %shard_map.86.rest_0_), channel_id=1, source_target_pairs={{0,8},{4,12},{8,0},{12,4},{1,9},{5,13},{9,1},{13,5},{2,10},{6,14},... | collective-permute-start | bytes 196616 | tf_op jit(solution)/shard_map/ppermute | solution.py:495
  71.5 2.3 %collective-permute-start.20 = (bf16[2,2,32,256]{3,2,1,0:T(8,128)(2,1)S(1)}, bf16[2,2,32,256]{3,2,1,0:T(8,128)(2,1)S(1)}, u32[]{:S(2)}, u32[]{:S(2)}) collective-permute-start(bf16[2,2,32,256]{3,2,1,0:T(8,128)(2,1)S(1)} %shard_map.84.rest_0_), channel_id=1, source_target_pairs={{0,4},{4,0},{8,12},{12,8},{1,5},{5,1},{9,13},{13,9},{2,6},{6,2},{1... | collective-permute-start | bytes 196616 | tf_op jit(solution)/shard_map/ppermute | solution.py:495
  73.8 2.8 %collective-permute-start.19 = (bf16[2,2,32,256]{3,2,1,0:T(8,128)(2,1)S(1)}, bf16[2,2,32,256]{3,2,1,0:T(8,128)(2,1)S(1)}, u32[]{:S(2)}, u32[]{:S(2)}) collective-permute-start(bf16[2,2,32,256]{3,2,1,0:T(8,128)(2,1)S(1)} %collective-permute-done.18.rest_1_), channel_id=1, source_target_pairs={{0,4},{4,0},{8,12},{12,8},{1,5},{5,1},{9,13},{13,9},{2,6},{6,2},{1... | collective-permute-start | bytes 196616 | tf_op jit(solution)/shard_map/ppermute | solution.py:495
  76.7 2.0 %collective-permute-start.23 = (bf16[2,2,32,256]{3,2,1,0:T(8,128)(2,1)S(1)}, bf16[2,2,32,256]{3,2,1,0:T(8,128)(2,1)S(1)}, u32[]{:S(2)}, u32[]{:S(2)}) collective-permute-start(bf16[2,2,32,256]{3,2,1,0:T(8,128)(2,1)S(1)} %collective-permute-done.22.rest_1_), channel_id=1, source_target_pairs={{0,4},{4,0},{8,12},{12,8},{1,5},{5,1},{9,13},{13,9},{2,6},{6,2},{1... | collective-permute-start | bytes 196616 | tf_op jit(solution)/shard_map/ppermute | solution.py:495
  83.7 2.4 %collective-permute-done.26.rest_2_ = bf16[2,2,32,256]{3,2,1,0:T(8,128)(2,1)S(1)} collective-permute-done((bf16[2,2,32,256]{3,2,1,0:T(8,128)(2,1)S(1)}, bf16[2,2,32,256]{3,2,1,0:T(8,128)(2,1)S(1)}, u32[]{:S(2)}, u32[]{:S(2)}) %collective-permute-start.26) | collective-permute-done | bytes 65568 | tf_op jit(solution)/shard_map/ppermute | solution.py:495
  87.8 3.0 %collective-permute-start.28 = (bf16[64,1024]{1,0:T(8,128)(2,1)S(1)}, bf16[64,1024]{1,0:T(8,128)(2,1)S(1)}, u32[]{:S(2)}, u32[]{:S(2)}) collective-permute-start(bf16[64,1024]{1,0:T(8,128)(2,1)S(1)} %get-tuple-element.87), channel_id=1, source_target_pairs={{0,12},{4,8},{8,4},{12,0},{1,13},{5,9},{9,5},{13,1},{2,14},{6,10},... | collective-permute-start | bytes 393224 | tf_op jit(solution)/shard_map/ppermute | solution.py:495
  90.8 5.1 %collective-permute-done.27.rest_1_ = bf16[64,1024]{1,0:T(8,128)(2,1)S(1)} collective-permute-done((bf16[64,1024]{1,0:T(8,128)(2,1)S(1)}, bf16[64,1024]{1,0:T(8,128)(2,1)S(1)}, u32[]{:S(2)}, u32[]{:S(2)}) %collective-permute-start.27) | collective-permute-done | bytes 131104 | tf_op jit(solution)/shard_map/ppermute | solution.py:495
  95.9 1.7 %collective-permute-done.29.rest_3_ = bf16[64,1024]{1,0:T(8,128)(2,1)S(1)} collective-permute-done((bf16[64,1024]{1,0:T(8,128)(2,1)S(1)}, bf16[64,1024]{1,0:T(8,128)(2,1)S(1)}, u32[]{:S(2)}, u32[]{:S(2)}) %collective-permute-start.29) | collective-permute-done | bytes 131104 | tf_op jit(solution)/shard_map/ppermute | solution.py:495
  98.3 4.4 %collective-permute-start.30 = (bf16[64,1024]{1,0:T(8,128)(2,1)S(1)}, bf16[64,1024]{1,0:T(8,128)(2,1)S(1)}, u32[]{:S(2)}, u32[]{:S(2)}) collective-permute-start(bf16[64,1024]{1,0:T(8,128)(2,1)S(1)} %get-tuple-element.90), channel_id=1, source_target_pairs={{0,8},{4,12},{8,0},{12,4},{1,9},{5,13},{9,1},{13,5},{2,10},{6,14},... | collective-permute-start | bytes 393224 | tf_op jit(solution)/shard_map/ppermute | solution.py:495
  102.7 2.1 %collective-permute-start.31 = (bf16[64,1024]{1,0:T(8,128)(2,1)S(1)}, bf16[64,1024]{1,0:T(8,128)(2,1)S(1)}, u32[]{:S(2)}, u32[]{:S(2)}) collective-permute-start(bf16[64,1024]{1,0:T(8,128)(2,1)S(1)} %get-tuple-element.91), channel_id=1, source_target_pairs={{0,12},{4,8},{8,4},{12,0},{1,13},{5,9},{9,5},{13,1},{2,14},{6,10},... | collective-permute-start | bytes 393224 | tf_op jit(solution)/shard_map/ppermute | solution.py:495
  105.7 4.0 %collective-permute-done.31.rest_6_ = bf16[64,1024]{1,0:T(8,128)(2,1)S(1)} collective-permute-done((bf16[64,1024]{1,0:T(8,128)(2,1)S(1)}, bf16[64,1024]{1,0:T(8,128)(2,1)S(1)}, u32[]{:S(2)}, u32[]{:S(2)}) %collective-permute-start.31) | collective-permute-done | bytes 131104 | tf_op jit(solution)/shard_map/ppermute | solution.py:495
  109.6 2.6 %collective-permute-done.32.rest_7_ = bf16[64,1024]{1,0:T(8,128)(2,1)S(1)} collective-permute-done((bf16[64,1024]{1,0:T(8,128)(2,1)S(1)}, bf16[64,1024]{1,0:T(8,128)(2,1)S(1)}, u32[]{:S(2)}, u32[]{:S(2)}) %collective-permute-start.32) | collective-permute-done | bytes 131104 | tf_op jit(solution)/shard_map/ppermute | solution.py:495
  112.8 2.0 %collective-permute-start.33 = (bf16[2,2,32,256]{3,2,1,0:T(8,128)(2,1)S(1)}, bf16[2,2,32,256]{3,2,1,0:T(8,128)(2,1)S(1)}, u32[]{:S(2)}, u32[]{:S(2)}) collective-permute-start(bf16[2,2,32,256]{3,2,1,0:T(8,128)(2,1)S(1)} %get-tuple-element.94), channel_id=1, source_target_pairs={{0,2},{2,0},{1,3},{3,1},{4,6},{6,4},{5,7},{7,5},{8,10},{10,8},{9,1... | collective-permute-start | bytes 196616 | tf_op jit(solution)/shard_map/ppermute | solution.py:495
  115.3 1.8 %collective-permute-done.37.r_ref = bf16[2,2,32,256]{3,2,1,0:T(8,128)(2,1)S(1)} collective-permute-done((bf16[2,2,32,256]{3,2,1,0:T(8,128)(2,1)S(1)}, bf16[2,2,32,256]{3,2,1,0:T(8,128)(2,1)S(1)}, u32[]{:S(2)}, u32[]{:S(2)}) %collective-permute-start.37) | collective-permute-done | bytes 65568 | tf_op jit(solution)/shard_map/ppermute | solution.py:495
  117.8 2.4 %collective-permute-start.34 = (bf16[2,2,32,256]{3,2,1,0:T(8,128)(2,1)S(1)}, bf16[2,2,32,256]{3,2,1,0:T(8,128)(2,1)S(1)}, u32[]{:S(2)}, u32[]{:S(2)}) collective-permute-start(bf16[2,2,32,256]{3,2,1,0:T(8,128)(2,1)S(1)} %shard_map.93.rest_0_), channel_id=1, source_target_pairs={{0,8},{4,12},{8,0},{12,4},{1,9},{5,13},{9,1},{13,5},{2,10},{6,14},... | collective-permute-start | bytes 196616 | tf_op jit(solution)/shard_map/ppermute | solution.py:495
  122.3 2.0 %collective-permute-start.36 = (bf16[2,2,32,256]{3,2,1,0:T(8,128)(2,1)S(1)}, bf16[2,2,32,256]{3,2,1,0:T(8,128)(2,1)S(1)}, u32[]{:S(2)}, u32[]{:S(2)}) collective-permute-start(bf16[2,2,32,256]{3,2,1,0:T(8,128)(2,1)S(1)} %shard_map.93.rest_0_), channel_id=1, source_target_pairs={{0,4},{4,0},{8,12},{12,8},{1,5},{5,1},{9,13},{13,9},{2,6},{6,2},{1... | collective-permute-start | bytes 196616 | tf_op jit(solution)/shard_map/ppermute | solution.py:495
  126.6 1.9 %shard_map.95.rest_4_ = bf16[64,128,256]{2,1,0:T(8,128)(2,1)} custom-call(s32[1]{0:T(128)} %bitcast._.freq.place_ref, s32[1]{0:T(128)} %bitcast.1.rblk._, s32[1]{0:T(128)} %bitcast.2.__.sblk, bf16[64,128,256]{2,1,0:T(8,128)(2,1)S(1)} %copy-done.1, s32[128,256]{1,0:T(8,128)S(1)} %copy-done.4, bf16[4,128,128]{2,1,0:T(8,128)(2,1)S(1)} %copy-done.5, ...), custom_call_target="tpu_custom_call" | custom-call | flops 33554432 | bytes 8912896 | tf_op jit(solution)/shard_map/pallas_call | solution.py:78
  128.6 1.9 %shard_map.96 = bf16[64,128,256]{2,1,0:T(8,128)(2,1)} custom-call(s32[1]{0:T(128)} %bitcast._.freq.place_ref, s32[1]{0:T(128)} %bitcast.1.rblk._, s32[1]{0:T(128)} %bitcast.2.__.sblk, bf16[64,128,256]{2,1,0:T(8,128)(2,1)S(1)} %copy-done.1, s32[128,256]{1,0:T(8,128)S(1)} %copy-done.4, ...), custom_call_target="tpu_custom_call", output_to_operand_aliasing={{}: (10, {})} | custom-call | flops 33554432 | bytes 13107200 | tf_op jit(solution)/shard_map/pallas_call | solution.py:78
  (89 shorter events, 30.0 us)
Async XLA Ops:
  2.6 21.3 %collective-permute-start.6 = (bf16[2,256,512]{2,1,0:T(8,128)(2,1)S(1)}, bf16[2,256,512]{2,1,0:T(8,128)(2,1)S(1)}, u32[]{:S(2)}, u32[]{:S(2)}) collective-permute-start(bf16[2,256,512]{2,1,0:T(8,128)(2,1)S(1)} %get-tuple-element.66), channel_id=1, source_target_pairs={{0,2},{2,0},{1,3},{3,1},{4,6},{6,4},{5,7},{7,5},{8,10},{10,8},{9,1... | collective-permute-start | bytes 1572872 | tf_op jit(solution)/shard_map/ppermute | solution.py:495
  5.6 26.0 %collective-permute-start.7 = (bf16[2,256,512]{2,1,0:T(8,128)(2,1)S(1)}, bf16[2,256,512]{2,1,0:T(8,128)(2,1)S(1)}, u32[]{:S(2)}, u32[]{:S(2)}) collective-permute-start(bf16[2,256,512]{2,1,0:T(8,128)(2,1)S(1)} %get-tuple-element.69), channel_id=1, source_target_pairs={{0,2},{2,0},{1,3},{3,1},{4,6},{6,4},{5,7},{7,5},{8,10},{10,8},{9,1... | collective-permute-start | bytes 1572872 | tf_op jit(solution)/shard_map/ppermute | solution.py:495
  8.6 12.9 %collective-permute-start.3 = (bf16[2,2,64,256]{3,2,1,0:T(8,128)(2,1)S(1)}, bf16[2,2,64,256]{3,2,1,0:T(8,128)(2,1)S(1)}, u32[]{:S(2)}, u32[]{:S(2)}) collective-permute-start(bf16[2,2,64,256]{3,2,1,0:T(8,128)(2,1)S(1)} %get-tuple-element.59), channel_id=1, source_target_pairs={{0,8},{4,12},{8,0},{12,4},{1,9},{5,13},{9,1},{13,5},{2,10},{6,14},... | collective-permute-start | bytes 393224 | tf_op jit(solution)/shard_map/ppermute | solution.py:495
  11.7 9.8 %collective-permute-start.4 = (bf16[2,2,64,256]{3,2,1,0:T(8,128)(2,1)S(1)}, bf16[2,2,64,256]{3,2,1,0:T(8,128)(2,1)S(1)}, u32[]{:S(2)}, u32[]{:S(2)}) collective-permute-start(bf16[2,2,64,256]{3,2,1,0:T(8,128)(2,1)S(1)} %get-tuple-element.60), channel_id=1, source_target_pairs={{0,12},{4,8},{8,4},{12,0},{1,13},{5,9},{9,5},{13,1},{2,14},{6,10},... | collective-permute-start | bytes 393224 | tf_op jit(solution)/shard_map/ppermute | solution.py:495
  13.1 8.6 %collective-permute-start.5 = (bf16[2,2,64,256]{3,2,1,0:T(8,128)(2,1)S(1)}, bf16[2,2,64,256]{3,2,1,0:T(8,128)(2,1)S(1)}, u32[]{:S(2)}, u32[]{:S(2)}) collective-permute-start(bf16[2,2,64,256]{3,2,1,0:T(8,128)(2,1)S(1)} %get-tuple-element.61), channel_id=1, source_target_pairs={{0,4},{4,0},{8,12},{12,8},{1,5},{5,1},{9,13},{13,9},{2,6},{6,2},{1... | collective-permute-start | bytes 393224 | tf_op jit(solution)/shard_map/ppermute | solution.py:495
  21.8 9.8 %collective-permute-start.8 = (bf16[2,2,64,256]{3,2,1,0:T(8,128)(2,1)S(1)}, bf16[2,2,64,256]{3,2,1,0:T(8,128)(2,1)S(1)}, u32[]{:S(2)}, u32[]{:S(2)}) collective-permute-start(bf16[2,2,64,256]{3,2,1,0:T(8,128)(2,1)S(1)} %get-tuple-element.68.rest_0_), channel_id=1, source_target_pairs={{0,2},{2,0},{1,3},{3,1},{4,6},{6,4},{5,7},{7,5},{8,10},{10,8},{9,1... | collective-permute-start | bytes 393224 | tf_op jit(solution)/shard_map/ppermute | solution.py:495
  23.4 8.2 %collective-permute-start = (bf16[2,256,512]{2,1,0:T(8,128)(2,1)S(1)}, bf16[2,256,512]{2,1,0:T(8,128)(2,1)S(1)}, u32[]{:S(2)}, u32[]{:S(2)}) collective-permute-start(bf16[2,256,512]{2,1,0:T(8,128)(2,1)S(1)} %get-tuple-element.51.rest_1_.rest_0_.rest_2_), channel_id=1, source_target_pairs={{0,1},{1,0},{2,3},{3,2},{4,5},{5,4},{6,7},{7,6},{8,9},{9,8},{10,11... | collective-permute-start | bytes 1572872 | tf_op jit(solution)/shard_map/ppermute | solution.py:495
  23.4 8.2 %collective-permute-start.1 = (bf16[2,256,512]{2,1,0:T(8,128)(2,1)S(1)}, bf16[2,256,512]{2,1,0:T(8,128)(2,1)S(1)}, u32[]{:S(2)}, u32[]{:S(2)}) collective-permute-start(bf16[2,256,512]{2,1,0:T(8,128)(2,1)S(1)} %get-tuple-element.52.rest_3_.rest_2_.rest_4_), channel_id=1, source_target_pairs={{0,1},{1,0},{2,3},{3,2},{4,5},{5,4},{6,7},{7,6},{8,9},{9,8},{10,11... | collective-permute-start | bytes 1572872 | tf_op jit(solution)/shard_map/ppermute | solution.py:495
  23.9 8.5 %collective-permute-start.9 = (bf16[2,256,512]{2,1,0:T(8,128)(2,1)S(1)}, bf16[2,256,512]{2,1,0:T(8,128)(2,1)S(1)}, u32[]{:S(2)}, u32[]{:S(2)}) collective-permute-start(bf16[2,256,512]{2,1,0:T(8,128)(2,1)S(1)} %collective-permute-done.6.rest_2_.rest_0_.rest_3_), channel_id=1, source_target_pairs={{0,1},{1,0},{2,3},{3,2},{4,5},{5,4},{6,7},{7,6},{8,9},{9,8},{10,11... | collective-permute-start | bytes 1572872 | tf_op jit(solution)/shard_map/ppermute | solution.py:495
  34.0 12.9 %collective-permute-start.11 = (bf16[64,1024]{1,0:T(8,128)(2,1)S(1)}, bf16[64,1024]{1,0:T(8,128)(2,1)S(1)}, u32[]{:S(2)}, u32[]{:S(2)}) collective-permute-start(bf16[64,1024]{1,0:T(8,128)(2,1)S(1)} %get-tuple-element.74), channel_id=1, source_target_pairs={{0,8},{4,12},{8,0},{12,4},{1,9},{5,13},{9,1},{13,5},{2,10},{6,14},... | collective-permute-start | bytes 393224 | tf_op jit(solution)/shard_map/ppermute | solution.py:495
  36.9 10.0 %collective-permute-start.12 = (bf16[64,1024]{1,0:T(8,128)(2,1)S(1)}, bf16[64,1024]{1,0:T(8,128)(2,1)S(1)}, u32[]{:S(2)}, u32[]{:S(2)}) collective-permute-start(bf16[64,1024]{1,0:T(8,128)(2,1)S(1)} %get-tuple-element.75), channel_id=1, source_target_pairs={{0,12},{4,8},{8,4},{12,0},{1,13},{5,9},{9,5},{13,1},{2,14},{6,10},... | collective-permute-start | bytes 393224 | tf_op jit(solution)/shard_map/ppermute | solution.py:495
  38.2 9.5 %collective-permute-start.13 = (bf16[64,1024]{1,0:T(8,128)(2,1)S(1)}, bf16[64,1024]{1,0:T(8,128)(2,1)S(1)}, u32[]{:S(2)}, u32[]{:S(2)}) collective-permute-start(bf16[64,1024]{1,0:T(8,128)(2,1)S(1)} %get-tuple-element.76), channel_id=1, source_target_pairs={{0,4},{4,0},{8,12},{12,8},{1,5},{5,1},{9,13},{13,9},{2,6},{6,2},{1... | collective-permute-start | bytes 393224 | tf_op jit(solution)/shard_map/ppermute | solution.py:495
  48.4 13.8 %collective-permute-start.14 = (bf16[64,1024]{1,0:T(8,128)(2,1)S(1)}, bf16[64,1024]{1,0:T(8,128)(2,1)S(1)}, u32[]{:S(2)}, u32[]{:S(2)}) collective-permute-start(bf16[64,1024]{1,0:T(8,128)(2,1)S(1)} %get-tuple-element.78), channel_id=1, source_target_pairs={{0,8},{4,12},{8,0},{12,4},{1,9},{5,13},{9,1},{13,5},{2,10},{6,14},... | collective-permute-start | bytes 393224 | tf_op jit(solution)/shard_map/ppermute | solution.py:495
  52.6 9.6 %collective-permute-start.15 = (bf16[64,1024]{1,0:T(8,128)(2,1)S(1)}, bf16[64,1024]{1,0:T(8,128)(2,1)S(1)}, u32[]{:S(2)}, u32[]{:S(2)}) collective-permute-start(bf16[64,1024]{1,0:T(8,128)(2,1)S(1)} %get-tuple-element.79), channel_id=1, source_target_pairs={{0,12},{4,8},{8,4},{12,0},{1,13},{5,9},{9,5},{13,1},{2,14},{6,10},... | collective-permute-start | bytes 393224 | tf_op jit(solution)/shard_map/ppermute | solution.py:495
  53.0 10.3 %collective-permute-start.16 = (bf16[64,1024]{1,0:T(8,128)(2,1)S(1)}, bf16[64,1024]{1,0:T(8,128)(2,1)S(1)}, u32[]{:S(2)}, u32[]{:S(2)}) collective-permute-start(bf16[64,1024]{1,0:T(8,128)(2,1)S(1)} %get-tuple-element.80), channel_id=1, source_target_pairs={{0,4},{4,0},{8,12},{12,8},{1,5},{5,1},{9,13},{13,9},{2,6},{6,2},{1... | collective-permute-start | bytes 393224 | tf_op jit(solution)/shard_map/ppermute | solution.py:495
  65.3 4.7 %collective-permute-start.21 = (bf16[2,2,32,256]{3,2,1,0:T(8,128)(2,1)S(1)}, bf16[2,2,32,256]{3,2,1,0:T(8,128)(2,1)S(1)}, u32[]{:S(2)}, u32[]{:S(2)}) collective-permute-start(bf16[2,2,32,256]{3,2,1,0:T(8,128)(2,1)S(1)} %get-tuple-element.84), channel_id=1, source_target_pairs={{0,2},{2,0},{1,3},{3,1},{4,6},{6,4},{5,7},{7,5},{8,10},{10,8},{9,1... | collective-permute-start | bytes 196616 | tf_op jit(solution)/shard_map/ppermute | solution.py:495
  68.1 5.7 %collective-permute-start.18 = (bf16[2,2,32,256]{3,2,1,0:T(8,128)(2,1)S(1)}, bf16[2,2,32,256]{3,2,1,0:T(8,128)(2,1)S(1)}, u32[]{:S(2)}, u32[]{:S(2)}) collective-permute-start(bf16[2,2,32,256]{3,2,1,0:T(8,128)(2,1)S(1)} %shard_map.84.rest_0_), channel_id=1, source_target_pairs={{0,8},{4,12},{8,0},{12,4},{1,9},{5,13},{9,1},{13,5},{2,10},{6,14},... | collective-permute-start | bytes 196616 | tf_op jit(solution)/shard_map/ppermute | solution.py:495
  70.1 6.6 %collective-permute-start.22 = (bf16[2,2,32,256]{3,2,1,0:T(8,128)(2,1)S(1)}, bf16[2,2,32,256]{3,2,1,0:T(8,128)(2,1)S(1)}, u32[]{:S(2)}, u32[]{:S(2)}) collective-permute-start(bf16[2,2,32,256]{3,2,1,0:T(8,128)(2,1)S(1)} %shard_map.86.rest_0_), channel_id=1, source_target_pairs={{0,8},{4,12},{8,0},{12,4},{1,9},{5,13},{9,1},{13,5},{2,10},{6,14},... | collective-permute-start | bytes 196616 | tf_op jit(solution)/shard_map/ppermute | solution.py:495
  71.5 7.1 %collective-permute-start.20 = (bf16[2,2,32,256]{3,2,1,0:T(8,128)(2,1)S(1)}, bf16[2,2,32,256]{3,2,1,0:T(8,128)(2,1)S(1)}, u32[]{:S(2)}, u32[]{:S(2)}) collective-permute-start(bf16[2,2,32,256]{3,2,1,0:T(8,128)(2,1)S(1)} %shard_map.84.rest_0_), channel_id=1, source_target_pairs={{0,4},{4,0},{8,12},{12,8},{1,5},{5,1},{9,13},{13,9},{2,6},{6,2},{1... | collective-permute-start | bytes 196616 | tf_op jit(solution)/shard_map/ppermute | solution.py:495
  73.8 5.1 %collective-permute-start.19 = (bf16[2,2,32,256]{3,2,1,0:T(8,128)(2,1)S(1)}, bf16[2,2,32,256]{3,2,1,0:T(8,128)(2,1)S(1)}, u32[]{:S(2)}, u32[]{:S(2)}) collective-permute-start(bf16[2,2,32,256]{3,2,1,0:T(8,128)(2,1)S(1)} %collective-permute-done.18.rest_1_), channel_id=1, source_target_pairs={{0,4},{4,0},{8,12},{12,8},{1,5},{5,1},{9,13},{13,9},{2,6},{6,2},{1... | collective-permute-start | bytes 196616 | tf_op jit(solution)/shard_map/ppermute | solution.py:495
  76.7 4.9 %collective-permute-start.23 = (bf16[2,2,32,256]{3,2,1,0:T(8,128)(2,1)S(1)}, bf16[2,2,32,256]{3,2,1,0:T(8,128)(2,1)S(1)}, u32[]{:S(2)}, u32[]{:S(2)}) collective-permute-start(bf16[2,2,32,256]{3,2,1,0:T(8,128)(2,1)S(1)} %collective-permute-done.22.rest_1_), channel_id=1, source_target_pairs={{0,4},{4,0},{8,12},{12,8},{1,5},{5,1},{9,13},{13,9},{2,6},{6,2},{1... | collective-permute-start | bytes 196616 | tf_op jit(solution)/shard_map/ppermute | solution.py:495
  87.1 8.8 %collective-permute-start.27 = (bf16[64,1024]{1,0:T(8,128)(2,1)S(1)}, bf16[64,1024]{1,0:T(8,128)(2,1)S(1)}, u32[]{:S(2)}, u32[]{:S(2)}) collective-permute-start(bf16[64,1024]{1,0:T(8,128)(2,1)S(1)} %get-tuple-element.86), channel_id=1, source_target_pairs={{0,8},{4,12},{8,0},{12,4},{1,9},{5,13},{9,1},{13,5},{2,10},{6,14},... | collective-permute-start | bytes 393224 | tf_op jit(solution)/shard_map/ppermute | solution.py:495
  87.8 8.1 %collective-permute-start.28 = (bf16[64,1024]{1,0:T(8,128)(2,1)S(1)}, bf16[64,1024]{1,0:T(8,128)(2,1)S(1)}, u32[]{:S(2)}, u32[]{:S(2)}) collective-permute-start(bf16[64,1024]{1,0:T(8,128)(2,1)S(1)} %get-tuple-element.87), channel_id=1, source_target_pairs={{0,12},{4,8},{8,4},{12,0},{1,13},{5,9},{9,5},{13,1},{2,14},{6,10},... | collective-permute-start | bytes 393224 | tf_op jit(solution)/shard_map/ppermute | solution.py:495
  90.8 6.8 %collective-permute-start.29 = (bf16[64,1024]{1,0:T(8,128)(2,1)S(1)}, bf16[64,1024]{1,0:T(8,128)(2,1)S(1)}, u32[]{:S(2)}, u32[]{:S(2)}) collective-permute-start(bf16[64,1024]{1,0:T(8,128)(2,1)S(1)} %get-tuple-element.88), channel_id=1, source_target_pairs={{0,4},{4,0},{8,12},{12,8},{1,5},{5,1},{9,13},{13,9},{2,6},{6,2},{1... | collective-permute-start | bytes 393224 | tf_op jit(solution)/shard_map/ppermute | solution.py:495
  98.3 7.4 %collective-permute-start.30 = (bf16[64,1024]{1,0:T(8,128)(2,1)S(1)}, bf16[64,1024]{1,0:T(8,128)(2,1)S(1)}, u32[]{:S(2)}, u32[]{:S(2)}) collective-permute-start(bf16[64,1024]{1,0:T(8,128)(2,1)S(1)} %get-tuple-element.90), channel_id=1, source_target_pairs={{0,8},{4,12},{8,0},{12,4},{1,9},{5,13},{9,1},{13,5},{2,10},{6,14},... | collective-permute-start | bytes 393224 | tf_op jit(solution)/shard_map/ppermute | solution.py:495
  102.7 6.9 %collective-permute-start.31 = (bf16[64,1024]{1,0:T(8,128)(2,1)S(1)}, bf16[64,1024]{1,0:T(8,128)(2,1)S(1)}, u32[]{:S(2)}, u32[]{:S(2)}) collective-permute-start(bf16[64,1024]{1,0:T(8,128)(2,1)S(1)} %get-tuple-element.91), channel_id=1, source_target_pairs={{0,12},{4,8},{8,4},{12,0},{1,13},{5,9},{9,5},{13,1},{2,14},{6,10},... | collective-permute-start | bytes 393224 | tf_op jit(solution)/shard_map/ppermute | solution.py:495
  104.9 7.4 %collective-permute-start.32 = (bf16[64,1024]{1,0:T(8,128)(2,1)S(1)}, bf16[64,1024]{1,0:T(8,128)(2,1)S(1)}, u32[]{:S(2)}, u32[]{:S(2)}) collective-permute-start(bf16[64,1024]{1,0:T(8,128)(2,1)S(1)} %get-tuple-element.92), channel_id=1, source_target_pairs={{0,4},{4,0},{8,12},{12,8},{1,5},{5,1},{9,13},{13,9},{2,6},{6,2},{1... | collective-permute-start | bytes 393224 | tf_op jit(solution)/shard_map/ppermute | solution.py:495
  112.8 5.0 %collective-permute-start.33 = (bf16[2,2,32,256]{3,2,1,0:T(8,128)(2,1)S(1)}, bf16[2,2,32,256]{3,2,1,0:T(8,128)(2,1)S(1)}, u32[]{:S(2)}, u32[]{:S(2)}) collective-permute-start(bf16[2,2,32,256]{3,2,1,0:T(8,128)(2,1)S(1)} %get-tuple-element.94), channel_id=1, source_target_pairs={{0,2},{2,0},{1,3},{3,1},{4,6},{6,4},{5,7},{7,5},{8,10},{10,8},{9,1... | collective-permute-start | bytes 196616 | tf_op jit(solution)/shard_map/ppermute | solution.py:495
  117.1 5.2 %collective-permute-start.38 = (bf16[2,2,32,256]{3,2,1,0:T(8,128)(2,1)S(1)}, bf16[2,2,32,256]{3,2,1,0:T(8,128)(2,1)S(1)}, u32[]{:S(2)}, u32[]{:S(2)}) collective-permute-start(bf16[2,2,32,256]{3,2,1,0:T(8,128)(2,1)S(1)} %shard_map.94.rest_0_), channel_id=1, source_target_pairs={{0,8},{4,12},{8,0},{12,4},{1,9},{5,13},{9,1},{13,5},{2,10},{6,14},... | collective-permute-start | bytes 196616 | tf_op jit(solution)/shard_map/ppermute | solution.py:495
  117.8 6.6 %collective-permute-start.34 = (bf16[2,2,32,256]{3,2,1,0:T(8,128)(2,1)S(1)}, bf16[2,2,32,256]{3,2,1,0:T(8,128)(2,1)S(1)}, u32[]{:S(2)}, u32[]{:S(2)}) collective-permute-start(bf16[2,2,32,256]{3,2,1,0:T(8,128)(2,1)S(1)} %shard_map.93.rest_0_), channel_id=1, source_target_pairs={{0,8},{4,12},{8,0},{12,4},{1,9},{5,13},{9,1},{13,5},{2,10},{6,14},... | collective-permute-start | bytes 196616 | tf_op jit(solution)/shard_map/ppermute | solution.py:495
  120.2 5.0 %collective-permute-start.40 = (bf16[2,2,32,256]{3,2,1,0:T(8,128)(2,1)S(1)}, bf16[2,2,32,256]{3,2,1,0:T(8,128)(2,1)S(1)}, u32[]{:S(2)}, u32[]{:S(2)}) collective-permute-start(bf16[2,2,32,256]{3,2,1,0:T(8,128)(2,1)S(1)} %shard_map.94.rest_0_), channel_id=1, source_target_pairs={{0,4},{4,0},{8,12},{12,8},{1,5},{5,1},{9,13},{13,9},{2,6},{6,2},{1... | collective-permute-start | bytes 196616 | tf_op jit(solution)/shard_map/ppermute | solution.py:495
  122.3 6.2 %collective-permute-start.36 = (bf16[2,2,32,256]{3,2,1,0:T(8,128)(2,1)S(1)}, bf16[2,2,32,256]{3,2,1,0:T(8,128)(2,1)S(1)}, u32[]{:S(2)}, u32[]{:S(2)}) collective-permute-start(bf16[2,2,32,256]{3,2,1,0:T(8,128)(2,1)S(1)} %shard_map.93.rest_0_), channel_id=1, source_target_pairs={{0,4},{4,0},{8,12},{12,8},{1,5},{5,1},{9,13},{13,9},{2,6},{6,2},{1... | collective-permute-start | bytes 196616 | tf_op jit(solution)/shard_map/ppermute | solution.py:495
  (16 other events, 172.3 us)

commit v19 on v14

--- a/solution.py
+++ b/solution.py
@@ -1,4 +1,5 @@
 import functools
+import itertools
 import math
 
 import jax
@@ -25,9 +26,19 @@
     return [0] + far
 
 
-def field_rows(place, freq_devs, per_dev):
+def slot_ways(count):
+    lead = ways(count)
+    return [[0] + lead[:0:-1], lead]
+
+
+def way_of(slot, core, count):
+    first, second = (order[slot] for order in slot_ways(count))
+    return first + core * (second - first) if first != second else first
+
+
+def field_rows(place, freq_devs, per_dev, order=None):
     rows = []
-    for step in ways(freq_devs):
+    for step in order or ways(freq_devs):
         first = (place ^ step) * per_dev
         for part in range(2):
             rows.extend((part, first + local) for local in range(per_dev))
@@ -64,8 +75,8 @@
     full[1, :, 0, :] = same.imag + mixed.imag
     full[1, :, 1, :] = same.real - mixed.real
     out = []
-    for place in range(freq_devs):
-        rows = [c * freq_total + j for c, j in field_rows(place, freq_devs, per_dev)]
+    for place, order in itertools.product(range(freq_devs), slot_ways(freq_devs)):
+        rows = [c * freq_total + j for c, j in field_rows(place, freq_devs, per_dev, order)]
         flat = full.reshape(2 * freq_total, 2 * freq_total)[np.ix_(rows, rows)]
         out.append(np.kron(flat, np.eye(ROWS)))
     return np.stack(out).astype(np.float32).astype(BF16)
@@ -219,22 +230,23 @@
 def phase_tables(src, rcv, places, freq_devs, per_dev, samples, parts, rows):
     width = src[0].shape[1] // parts
 
-    def fill(outs, value, to, freq):
+    def fill(outs, value, to, freq, order_of):
         cosines, sines, fraction = outs
         value = value.astype(F32) * (1.0 / samples)
         fraction[:, to] = value
-        for step, way in enumerate(ways(freq_devs)):
+        for step, way in enumerate(order_of):
             for j in range(per_dev):
                 order = ((freq[0] ^ way) * per_dev + j + 1).astype(F32)
                 cosines[step, j, :, to], sines[step, j, :, to] = turned(value * order)
 
     def body(freq, _, sblk, own, other, r_ref, *outs):
+        slots = [way_of(slot, sblk[0], freq_devs) for slot in range(freq_devs)]
         for part in range(parts):
             for spot, ref in enumerate((own, other)):
                 at = (part * 2 + spot) * width
-                fill(outs[:3], ref[:, part * width : (part + 1) * width], slice(at, at + width), freq)
+                fill(outs[:3], ref[:, part * width : (part + 1) * width], slice(at, at + width), freq, slots)
         value = r_ref[pl.ds(pl.multiple_of(sblk[0] * rows, ROWS), rows), :]
-        fill(outs[3:], value, slice(0, value.shape[1]), freq)
+        fill(outs[3:], value, slice(0, value.shape[1]), freq, ways(freq_devs))
 
     shapes = []
     for count, total in ((src[0].shape[0], 2 * src[0].shape[1]), (rows, rcv.shape[1])):
@@ -244,7 +256,7 @@
     return tuple(outs[:3]), tuple(outs[3:])
 
 
-def down_products(before, spectra, parts, side, first, freq_place, freq_devs=0):
+def down_products(before, spectra, parts, side, first, places, freq_devs=0):
     _, per_dev, _, rcv = spectra[0].shape
     rows = sum(v.shape[2] for v in spectra)
     flat = [pair[side] for part in parts for pair in part]
@@ -253,7 +265,7 @@
     share = rows // freq_devs if freq_devs else 0
     old = [] if before is None else [before]
 
-    def body(place_ref, *rest):
+    def body(freq, _, sblk, *rest):
         held_ref, rest = (rest[0], rest[1:]) if old else (None, rest)
         refs, resp, outs = rest[: len(spectra)], rest[len(spectra) : len(spectra) + len(flat)], rest[len(spectra) + len(flat) :]
         held = outs[-1]
@@ -272,8 +284,8 @@
                 if to.start < to.stop:
                     held[:, :, :, to] = held_ref[:, :, :, to]
         if freq_devs:
-            for way, out in zip(ways(freq_devs), outs):
-                start = pl.multiple_of((place_ref[0] ^ way) * share, share)
+            for slot, out in enumerate(outs[:freq_devs]):
+                start = pl.multiple_of((freq[0] ^ way_of(slot, sblk[0], freq_devs)) * share, share)
                 out[...] = held[:, :, pl.ds(start, share), :].reshape(out.shape).astype(BF16)
 
     sums = (2, per_dev, rows, total_width)
@@ -283,7 +295,7 @@
         shapes = [jax.ShapeDtypeStruct(sums, F32)]
     outs = call(
         body,
-        (freq_place,),
+        places,
         [(v, whole(v)) for v in (*old, *spectra, *flat)],
         [(v, whole(v)) for v in shapes],
         (1,),
@@ -318,15 +330,15 @@
     lax.fori_loop(0, width // BLOCK, at, 0, unroll=2)
 
 
-def windowed(messages, tables, matrix, freq_place, per_dev, share):
+def windowed(messages, tables, matrix, places, per_dev, share):
     cosines, sines, fraction = tables
     freq_devs = len(messages)
     width = messages[0].shape[-1]
     count = freq_devs * 2 * per_dev * ROWS
 
-    def body(place_ref, c_ref, s_ref, f_ref, g_ref, *rest):
+    def body(freq, _, sblk, c_ref, s_ref, f_ref, g_ref, *rest):
         refs, outs = rest[:freq_devs], rest[freq_devs:]
-        matrix_here = g_ref[place_ref[0]]
+        matrix_here = g_ref[freq[0] * 2 + sblk[0]]
 
         def one(at):
             data = [ref[:, at].astype(F32).reshape(2, per_dev, share, BLOCK) for ref in refs]
@@ -348,7 +360,7 @@
     inputs = (cosines, sines, fraction, matrix, *messages)
     return call(
         body,
-        (freq_place,),
+        places,
         [(v, whole(v)) for v in inputs],
         [(jax.ShapeDtypeStruct(v.shape, BF16), whole(v)) for v in messages],
         (1,),
@@ -356,7 +368,7 @@
     )
 
 
-def up_products(messages, parts, freq_place, rows, side):
+def up_products(messages, parts, places, rows, side):
     freq_devs = len(messages)
     flat = [pair[side] for part in parts for pair in part]
     per_dev, src, rcv = flat[0].shape[0], flat[0].shape[1], flat[0].shape[2] // 2
@@ -365,11 +377,11 @@
     total_width = src * len(flat)
     kind = BF16 if side else F32
 
-    def body(place_ref, *rest):
+    def body(freq, _, sblk, *rest):
         resp, refs = rest[: len(flat)], rest[len(flat) : len(flat) + freq_devs]
         outs, held = rest[len(flat) + freq_devs : -1], rest[-1]
-        for way, ref in zip(ways(freq_devs), refs):
-            start = pl.multiple_of((place_ref[0] ^ way) * share, share)
+        for slot, ref in enumerate(refs):
+            start = pl.multiple_of((freq[0] ^ way_of(slot, sblk[0], freq_devs)) * share, share)
             value = ref[...].reshape(2, per_dev, share, total_width)
             for part in range(2):
                 for j in range(per_dev):
@@ -390,7 +402,7 @@
     shape = jax.ShapeDtypeStruct((2, per_dev, group, rcv), kind)
     return call(
         body,
-        (freq_place,),
+        places,
         [(v, whole(v)) for v in (*flat, *messages)],
         [(shape, whole(shape))] * CHUNKS,
         (1,),
@@ -408,7 +420,7 @@
 
     def body(place_ref, u_ref, c_ref, s_ref, f_ref, g_ref, *rest):
         refs, out = rest[:freq_devs], rest[freq_devs]
-        matrix_here = g_ref[place_ref[0], :own]
+        matrix_here = g_ref[place_ref[0] * 2 + 1, :own]
 
         def one(at):
             for base in range(0, rows, 2 * ROWS):
@@ -499,6 +511,16 @@
     return [exchanged(part, "freq", step) if step else part for part, step in zip(parts, ways(len(parts)))]
 
 
+def dealt_by_core(parts):
+    count = len(parts)
+    out = [parts[0]]
+    for slot in range(1, count):
+        steps = [order[slot] for order in slot_ways(count)]
+        pairs = [(f * 2 + core, (f ^ steps[core]) * 2 + core) for f in range(count) for core in range(2)]
+        out.append(lax.ppermute(parts[slot], ("freq", "sblk"), pairs))
+    return out
+
+
 def spread(value, count):
     held = {0: value}
     bit = count // 2
@@ -541,15 +563,15 @@
 
     near, far, result = [spectra], [far], None
     for step in range(ITERS):
-        held = down_products(None, near, parts, 0, 0, freq_place)
+        held = down_products(None, near, parts, 0, 0, places)
         at = 0 if step else PARTS - 1
         if at:
-            held = down_products(held, far, parts[:at], 1, 0, freq_place)
+            held = down_products(held, far, parts[:at], 1, 0, places)
         first = at * 2 * kept[0].shape[1]
-        messages = dealt_out(down_products(held, far, parts[at:], 1, first, freq_place, freq_devs))
-        messages = dealt_out(windowed(messages, src_tables, matrix, freq_place, per_dev, share))
-        received = [exchanged(v, "rblk", 1) for v in up_products(messages, parts, freq_place, half_rows, 1)]
-        keep = up_products(messages, parts, freq_place, half_rows, 0)
+        messages = dealt_by_core(down_products(held, far, parts[at:], 1, first, places, freq_devs))
+        messages = dealt_by_core(windowed(messages, src_tables, matrix, places, per_dev, share))
+        received = [exchanged(v, "rblk", 1) for v in up_products(messages, parts, places, half_rows, 1)]
+        keep = up_products(messages, parts, places, half_rows, 0)
         near, far = [], []
         for chunk in range(CHUNKS):
             back = spread(added(keep[chunk], received[chunk]), freq_devs)

time: 130 us -> 135 us (1.038)
  waiting for transfers between devices: 56.2 us -> 72.5 us
  starting transfers between devices: 54.5 us -> 42.8 us
    ppermute x0 -> x12, waiting for transfers between devices: none -> 39.3 us  [dealt_by_core(): out.append(lax.ppermute(parts[slot], ('freq', 'sblk'), pairs))]
    ppermute x41 -> x29, starting transfers between devices: 54.5 us -> 27 us  [exchanged(): lax.ppermute(value, axis, [(i, i ^ step) for i in range(lax.axis_size(axi...]
    ppermute x41 -> x29, waiting for transfers between devices: 56.2 us -> 33.3 us  [exchanged(): lax.ppermute(value, axis, [(i, i ^ step) for i in range(lax.axis_size(axi...]
    ppermute x0 -> x12, starting transfers between devices: none -> 15.8 us  [dealt_by_core(): out.append(lax.ppermute(parts[slot], ('freq', 'sblk'), pairs))]
  transfers between devices with their start and end apart: 41 -> 41, of which waited for: 22 -> 30; matrix products, arithmetic and copies ran while one was open for 0% -> 0% of each run, Pallas kernels for 6% -> 6%
where the time goes in v19:
time: 135 us; the launch traced here: 134 us
  waiting for transfers between devices  72.5 us (54%)
  starting transfers between devices  42.8 us (32%)
  Pallas kernels  14.2 us (11%)
  local copies, waits for them, and re-layouts  4.56 us (3%)
    ppermute x12, waiting for transfers between devices, dealt_by_core(): out.append(lax.ppermute(parts[slot], ('freq', 'sblk'), pairs))  39.3 us
    ppermute x29, waiting for transfers between devices, exchanged(): lax.ppermute(value, axis, [(i, i ^ step) for i in range(lax.axis_size(axi...  33.3 us
    ppermute x29, starting transfers between devices, exchanged(): lax.ppermute(value, axis, [(i, i ^ step) for i in range(lax.axis_size(axi...  27 us
    ppermute x12, starting transfers between devices, dealt_by_core(): out.append(lax.ppermute(parts[slot], ('freq', 'sblk'), pairs))  15.8 us
    pallas_call x24, Pallas kernels, call(): pl.pallas_call(body, grid_spec=pltpu.PrefetchScalarGridSpec(num_scalar_pr...  14.2 us
    unnamed x15, local copies, waits for them, and re-layouts  4.56 us
  transfers between devices with their start and end apart: 41, of which 30 were waited for; matrix products, arithmetic and copies ran while one was open for 0% of the time, Pallas kernels for 6%

profile of v19, /device:TPU:0, one launch (start us, length us, event | category | flops | bytes accessed | tf_op | source)
XLA Modules:
  0.0 134.3 jit_solution(4622037725694913912)
XLA Ops:
  0.8 1.6 %copy-done.3 = bf16[2,2,1024,256]{3,2,1,0:T(8,128)(2,1)S(1)} copy-done((bf16[2,2,1024,256]{3,2,1,0:T(8,128)(2,1)S(1)}, bf16[2,2,1024,256]{3,2,1,0:T(8,128)(2,1)}, u32[]{:S(2)}) %copy-start.3) | copy-done | bytes 2097176
  2.6 3.0 %collective-permute-start.6 = (bf16[2,256,512]{2,1,0:T(8,128)(2,1)S(1)}, bf16[2,256,512]{2,1,0:T(8,128)(2,1)S(1)}, u32[]{:S(2)}, u32[]{:S(2)}) collective-permute-start(bf16[2,256,512]{2,1,0:T(8,128)(2,1)S(1)} %get-tuple-element.66), channel_id=1, source_target_pairs={{0,2},{2,0},{1,3},{3,1},{4,6},{6,4},{5,7},{7,5},{8,10},{10,8},{9,1... | collective-permute-start | bytes 1572872 | tf_op jit(solution)/shard_map/ppermute | solution.py:507
  5.7 2.2 %copy-done = bf16[64,128,256]{2,1,0:T(8,128)(2,1)S(1)} copy-done((bf16[64,128,256]{2,1,0:T(8,128)(2,1)S(1)}, bf16[64,128,256]{2,1,0:T(8,128)(2,1)}, u32[]{:S(2)}) %copy-start) | copy-done | bytes 4194328
  8.6 3.1 %collective-permute-start.3 = (bf16[2,2,64,256]{3,2,1,0:T(8,128)(2,1)S(1)}, bf16[2,2,64,256]{3,2,1,0:T(8,128)(2,1)S(1)}, u32[]{:S(2)}, u32[]{:S(2)}) collective-permute-start(bf16[2,2,64,256]{3,2,1,0:T(8,128)(2,1)S(1)} %get-tuple-element.59), channel_id=1, source_target_pairs={{0,8},{4,12},{8,0},{12,4},{1,9},{5,13},{9,1},{13,5},{2,10},{6,14},... | collective-permute-start | bytes 393224 | tf_op jit(solution)/shard_map/ppermute | solution.py:507
  13.3 8.2 %collective-permute-done.3.refs_1_ = bf16[2,2,64,256]{3,2,1,0:T(8,128)(2,1)S(1)} collective-permute-done((bf16[2,2,64,256]{3,2,1,0:T(8,128)(2,1)S(1)}, bf16[2,2,64,256]{3,2,1,0:T(8,128)(2,1)S(1)}, u32[]{:S(2)}, u32[]{:S(2)}) %collective-permute-start.3) | collective-permute-done | bytes 131104 | tf_op jit(solution)/shard_map/ppermute | solution.py:507
  21.8 1.6 %collective-permute-start.8 = (bf16[2,2,64,256]{3,2,1,0:T(8,128)(2,1)S(1)}, bf16[2,2,64,256]{3,2,1,0:T(8,128)(2,1)S(1)}, u32[]{:S(2)}, u32[]{:S(2)}) collective-permute-start(bf16[2,2,64,256]{3,2,1,0:T(8,128)(2,1)S(1)} %get-tuple-element.68.rest_0_), channel_id=1, source_target_pairs={{0,2},{2,0},{1,3},{3,1},{4,6},{6,4},{5,7},{7,5},{8,10},{10,8},{9,1... | collective-permute-start | bytes 393224 | tf_op jit(solution)/shard_map/ppermute | solution.py:507
  24.0 7.6 %collective-permute-done.8.rest_1_ = bf16[2,2,64,256]{3,2,1,0:T(8,128)(2,1)S(1)} collective-permute-done((bf16[2,2,64,256]{3,2,1,0:T(8,128)(2,1)S(1)}, bf16[2,2,64,256]{3,2,1,0:T(8,128)(2,1)S(1)}, u32[]{:S(2)}, u32[]{:S(2)}) %collective-permute-start.8) | collective-permute-done | bytes 131104 | tf_op jit(solution)/shard_map/ppermute | solution.py:507
  34.0 1.9 %collective-permute-start.11 = (bf16[64,1024]{1,0:T(8,128)(2,1)S(1)}, bf16[64,1024]{1,0:T(8,128)(2,1)S(1)}, u32[]{:S(2)}, u32[]{:S(2)}) collective-permute-start(bf16[64,1024]{1,0:T(8,128)(2,1)S(1)} %get-tuple-element.74), channel_id=1, source_target_pairs={{0,4},{1,9},{4,0},{5,13},{8,12},{9,1},{12,8},{13,5},{2,6},{3,11},{... | collective-permute-start | bytes 393224 | tf_op jit(solution)/shard_map/ppermute | solution.py:520
  35.9 2.5 %collective-permute-start.12 = (bf16[64,1024]{1,0:T(8,128)(2,1)S(1)}, bf16[64,1024]{1,0:T(8,128)(2,1)S(1)}, u32[]{:S(2)}, u32[]{:S(2)}) collective-permute-start(bf16[64,1024]{1,0:T(8,128)(2,1)S(1)} %get-tuple-element.75), channel_id=1, source_target_pairs={{0,12},{1,13},{4,8},{5,9},{8,4},{9,5},{12,0},{13,1},{2,14},{3,15},... | collective-permute-start | bytes 393224 | tf_op jit(solution)/shard_map/ppermute | solution.py:520
  41.1 4.0 %collective-permute-done.12.rest_2_ = bf16[64,1024]{1,0:T(8,128)(2,1)S(1)} collective-permute-done((bf16[64,1024]{1,0:T(8,128)(2,1)S(1)}, bf16[64,1024]{1,0:T(8,128)(2,1)S(1)}, u32[]{:S(2)}, u32[]{:S(2)}) %collective-permute-start.12) | collective-permute-done | bytes 131104 | tf_op jit(solution)/shard_map/ppermute | solution.py:520
  45.2 4.0 %collective-permute-done.13.rest_3_ = bf16[64,1024]{1,0:T(8,128)(2,1)S(1)} collective-permute-done((bf16[64,1024]{1,0:T(8,128)(2,1)S(1)}, bf16[64,1024]{1,0:T(8,128)(2,1)S(1)}, u32[]{:S(2)}, u32[]{:S(2)}) %collective-permute-start.13) | collective-permute-done | bytes 131104 | tf_op jit(solution)/shard_map/ppermute | solution.py:520
  51.0 2.9 %collective-permute-start.15 = (bf16[64,1024]{1,0:T(8,128)(2,1)S(1)}, bf16[64,1024]{1,0:T(8,128)(2,1)S(1)}, u32[]{:S(2)}, u32[]{:S(2)}) collective-permute-start(bf16[64,1024]{1,0:T(8,128)(2,1)S(1)} %get-tuple-element.79), channel_id=1, source_target_pairs={{0,12},{1,13},{4,8},{5,9},{8,4},{9,5},{12,0},{13,1},{2,14},{3,15},... | collective-permute-start | bytes 393224 | tf_op jit(solution)/shard_map/ppermute | solution.py:520
  54.4 2.7 %collective-permute-done.14.rest_5_ = bf16[64,1024]{1,0:T(8,128)(2,1)S(1)} collective-permute-done((bf16[64,1024]{1,0:T(8,128)(2,1)S(1)}, bf16[64,1024]{1,0:T(8,128)(2,1)S(1)}, u32[]{:S(2)}, u32[]{:S(2)}) %collective-permute-start.14) | collective-permute-done | bytes 131104 | tf_op jit(solution)/shard_map/ppermute | solution.py:520
  57.1 3.2 %collective-permute-done.15.rest_6_ = bf16[64,1024]{1,0:T(8,128)(2,1)S(1)} collective-permute-done((bf16[64,1024]{1,0:T(8,128)(2,1)S(1)}, bf16[64,1024]{1,0:T(8,128)(2,1)S(1)}, u32[]{:S(2)}, u32[]{:S(2)}) %collective-permute-start.15) | collective-permute-done | bytes 131104 | tf_op jit(solution)/shard_map/ppermute | solution.py:520
  60.3 3.8 %collective-permute-done.16.rest_7_ = bf16[64,1024]{1,0:T(8,128)(2,1)S(1)} collective-permute-done((bf16[64,1024]{1,0:T(8,128)(2,1)S(1)}, bf16[64,1024]{1,0:T(8,128)(2,1)S(1)}, u32[]{:S(2)}, u32[]{:S(2)}) %collective-permute-start.16) | collective-permute-done | bytes 131104 | tf_op jit(solution)/shard_map/ppermute | solution.py:520
  67.1 1.8 %collective-permute-done.17.r_ref = bf16[2,2,32,256]{3,2,1,0:T(8,128)(2,1)S(1)} collective-permute-done((bf16[2,2,32,256]{3,2,1,0:T(8,128)(2,1)S(1)}, bf16[2,2,32,256]{3,2,1,0:T(8,128)(2,1)S(1)}, u32[]{:S(2)}, u32[]{:S(2)}) %collective-permute-start.17) | collective-permute-done | bytes 65568 | tf_op jit(solution)/shard_map/ppermute | solution.py:507
  70.4 1.6 %collective-permute-start.22 = (bf16[2,2,32,256]{3,2,1,0:T(8,128)(2,1)S(1)}, bf16[2,2,32,256]{3,2,1,0:T(8,128)(2,1)S(1)}, u32[]{:S(2)}, u32[]{:S(2)}) collective-permute-start(bf16[2,2,32,256]{3,2,1,0:T(8,128)(2,1)S(1)} %shard_map.86.rest_0_), channel_id=1, source_target_pairs={{0,8},{4,12},{8,0},{12,4},{1,9},{5,13},{9,1},{13,5},{2,10},{6,14},... | collective-permute-start | bytes 196616 | tf_op jit(solution)/shard_map/ppermute | solution.py:507
  73.0 1.6 %collective-permute-done.18.rest_1_ = bf16[2,2,32,256]{3,2,1,0:T(8,128)(2,1)S(1)} collective-permute-done((bf16[2,2,32,256]{3,2,1,0:T(8,128)(2,1)S(1)}, bf16[2,2,32,256]{3,2,1,0:T(8,128)(2,1)S(1)}, u32[]{:S(2)}, u32[]{:S(2)}) %collective-permute-start.18) | collective-permute-done | bytes 65568 | tf_op jit(solution)/shard_map/ppermute | solution.py:507
  74.6 2.0 %collective-permute-start.24 = (bf16[2,2,32,256]{3,2,1,0:T(8,128)(2,1)S(1)}, bf16[2,2,32,256]{3,2,1,0:T(8,128)(2,1)S(1)}, u32[]{:S(2)}, u32[]{:S(2)}) collective-permute-start(bf16[2,2,32,256]{3,2,1,0:T(8,128)(2,1)S(1)} %shard_map.86.rest_0_), channel_id=1, source_target_pairs={{0,4},{4,0},{8,12},{12,8},{1,5},{5,1},{9,13},{13,9},{2,6},{6,2},{1... | collective-permute-start | bytes 196616 | tf_op jit(solution)/shard_map/ppermute | solution.py:507
  83.4 2.0 %collective-permute-done.26.rest_2_ = bf16[2,2,32,256]{3,2,1,0:T(8,128)(2,1)S(1)} collective-permute-done((bf16[2,2,32,256]{3,2,1,0:T(8,128)(2,1)S(1)}, bf16[2,2,32,256]{3,2,1,0:T(8,128)(2,1)S(1)}, u32[]{:S(2)}, u32[]{:S(2)}) %collective-permute-start.26) | collective-permute-done | bytes 65568 | tf_op jit(solution)/shard_map/ppermute | solution.py:507
  87.1 2.0 %collective-permute-start.28 = (bf16[64,1024]{1,0:T(8,128)(2,1)S(1)}, bf16[64,1024]{1,0:T(8,128)(2,1)S(1)}, u32[]{:S(2)}, u32[]{:S(2)}) collective-permute-start(bf16[64,1024]{1,0:T(8,128)(2,1)S(1)} %get-tuple-element.87), channel_id=1, source_target_pairs={{0,12},{1,13},{4,8},{5,9},{8,4},{9,5},{12,0},{13,1},{2,14},{3,15},... | collective-permute-start | bytes 393224 | tf_op jit(solution)/shard_map/ppermute | solution.py:520
  91.4 2.6 %collective-permute-done.28.rest_2_ = bf16[64,1024]{1,0:T(8,128)(2,1)S(1)} collective-permute-done((bf16[64,1024]{1,0:T(8,128)(2,1)S(1)}, bf16[64,1024]{1,0:T(8,128)(2,1)S(1)}, u32[]{:S(2)}, u32[]{:S(2)}) %collective-permute-start.28) | collective-permute-done | bytes 131104 | tf_op jit(solution)/shard_map/ppermute | solution.py:520
  94.0 7.4 %collective-permute-done.29.rest_3_ = bf16[64,1024]{1,0:T(8,128)(2,1)S(1)} collective-permute-done((bf16[64,1024]{1,0:T(8,128)(2,1)S(1)}, bf16[64,1024]{1,0:T(8,128)(2,1)S(1)}, u32[]{:S(2)}, u32[]{:S(2)}) %collective-permute-start.29) | collective-permute-done | bytes 131104 | tf_op jit(solution)/shard_map/ppermute | solution.py:520
  104.1 1.9 %collective-permute-start.32 = (bf16[64,1024]{1,0:T(8,128)(2,1)S(1)}, bf16[64,1024]{1,0:T(8,128)(2,1)S(1)}, u32[]{:S(2)}, u32[]{:S(2)}) collective-permute-start(bf16[64,1024]{1,0:T(8,128)(2,1)S(1)} %get-tuple-element.92), channel_id=1, source_target_pairs={{0,8},{1,5},{4,12},{5,1},{8,0},{9,13},{12,4},{13,9},{2,10},{3,7},{... | collective-permute-start | bytes 393224 | tf_op jit(solution)/shard_map/ppermute | solution.py:520
  107.5 2.0 %collective-permute-done.31.rest_6_ = bf16[64,1024]{1,0:T(8,128)(2,1)S(1)} collective-permute-done((bf16[64,1024]{1,0:T(8,128)(2,1)S(1)}, bf16[64,1024]{1,0:T(8,128)(2,1)S(1)}, u32[]{:S(2)}, u32[]{:S(2)}) %collective-permute-start.31) | collective-permute-done | bytes 131104 | tf_op jit(solution)/shard_map/ppermute | solution.py:520
  109.5 6.5 %collective-permute-done.32.rest_7_ = bf16[64,1024]{1,0:T(8,128)(2,1)S(1)} collective-permute-done((bf16[64,1024]{1,0:T(8,128)(2,1)S(1)}, bf16[64,1024]{1,0:T(8,128)(2,1)S(1)}, u32[]{:S(2)}, u32[]{:S(2)}) %collective-permute-start.32) | collective-permute-done | bytes 131104 | tf_op jit(solution)/shard_map/ppermute | solution.py:520
  119.0 1.8 %collective-permute-done.37.r_ref = bf16[2,2,32,256]{3,2,1,0:T(8,128)(2,1)S(1)} collective-permute-done((bf16[2,2,32,256]{3,2,1,0:T(8,128)(2,1)S(1)}, bf16[2,2,32,256]{3,2,1,0:T(8,128)(2,1)S(1)}, u32[]{:S(2)}, u32[]{:S(2)}) %collective-permute-start.37) | collective-permute-done | bytes 65568 | tf_op jit(solution)/shard_map/ppermute | solution.py:507
  122.1 1.8 %collective-permute-start.34 = (bf16[2,2,32,256]{3,2,1,0:T(8,128)(2,1)S(1)}, bf16[2,2,32,256]{3,2,1,0:T(8,128)(2,1)S(1)}, u32[]{:S(2)}, u32[]{:S(2)}) collective-permute-start(bf16[2,2,32,256]{3,2,1,0:T(8,128)(2,1)S(1)} %shard_map.93.rest_0_), channel_id=1, source_target_pairs={{0,8},{4,12},{8,0},{12,4},{1,9},{5,13},{9,1},{13,5},{2,10},{6,14},... | collective-permute-start | bytes 196616 | tf_op jit(solution)/shard_map/ppermute | solution.py:507
  126.0 2.0 %collective-permute-start.36 = (bf16[2,2,32,256]{3,2,1,0:T(8,128)(2,1)S(1)}, bf16[2,2,32,256]{3,2,1,0:T(8,128)(2,1)S(1)}, u32[]{:S(2)}, u32[]{:S(2)}) collective-permute-start(bf16[2,2,32,256]{3,2,1,0:T(8,128)(2,1)S(1)} %shard_map.93.rest_0_), channel_id=1, source_target_pairs={{0,4},{4,0},{8,12},{12,8},{1,5},{5,1},{9,13},{13,9},{2,6},{6,2},{1... | collective-permute-start | bytes 196616 | tf_op jit(solution)/shard_map/ppermute | solution.py:507
  128.4 1.8 %collective-permute-done.39.rest_2_ = bf16[2,2,32,256]{3,2,1,0:T(8,128)(2,1)S(1)} collective-permute-done((bf16[2,2,32,256]{3,2,1,0:T(8,128)(2,1)S(1)}, bf16[2,2,32,256]{3,2,1,0:T(8,128)(2,1)S(1)}, u32[]{:S(2)}, u32[]{:S(2)}) %collective-permute-start.39) | collective-permute-done | bytes 65568 | tf_op jit(solution)/shard_map/ppermute | solution.py:507
  130.3 1.9 %shard_map.95.rest_4_ = bf16[64,128,256]{2,1,0:T(8,128)(2,1)} custom-call(s32[1]{0:T(128)} %bitcast._.freq.place_ref, s32[1]{0:T(128)} %bitcast.1.rblk._, s32[1]{0:T(128)} %bitcast.2.__.sblk, bf16[64,128,256]{2,1,0:T(8,128)(2,1)S(1)} %copy-done.1, s32[128,256]{1,0:T(8,128)S(1)} %copy-done.4, bf16[4,128,128]{2,1,0:T(8,128)(2,1)S(1)} %copy-done.5, ...), custom_call_target="tpu_custom_call" | custom-call | flops 33554432 | bytes 8912896 | tf_op jit(solution)/shard_map/pallas_call | solution.py:89
  132.4 1.9 %shard_map.96 = bf16[64,128,256]{2,1,0:T(8,128)(2,1)} custom-call(s32[1]{0:T(128)} %bitcast._.freq.place_ref, s32[1]{0:T(128)} %bitcast.1.rblk._, s32[1]{0:T(128)} %bitcast.2.__.sblk, bf16[64,128,256]{2,1,0:T(8,128)(2,1)S(1)} %copy-done.1, s32[128,256]{1,0:T(8,128)S(1)} %copy-done.4, ...), custom_call_target="tpu_custom_call", output_to_operand_aliasing={{}: (10, {})} | custom-call | flops 33554432 | bytes 13107200 | tf_op jit(solution)/shard_map/pallas_call | solution.py:89
  (89 shorter events, 39.1 us)
Async XLA Ops:
  2.6 21.3 %collective-permute-start.6 = (bf16[2,256,512]{2,1,0:T(8,128)(2,1)S(1)}, bf16[2,256,512]{2,1,0:T(8,128)(2,1)S(1)}, u32[]{:S(2)}, u32[]{:S(2)}) collective-permute-start(bf16[2,256,512]{2,1,0:T(8,128)(2,1)S(1)} %get-tuple-element.66), channel_id=1, source_target_pairs={{0,2},{2,0},{1,3},{3,1},{4,6},{6,4},{5,7},{7,5},{8,10},{10,8},{9,1... | collective-permute-start | bytes 1572872 | tf_op jit(solution)/shard_map/ppermute | solution.py:507
  5.6 26.0 %collective-permute-start.7 = (bf16[2,256,512]{2,1,0:T(8,128)(2,1)S(1)}, bf16[2,256,512]{2,1,0:T(8,128)(2,1)S(1)}, u32[]{:S(2)}, u32[]{:S(2)}) collective-permute-start(bf16[2,256,512]{2,1,0:T(8,128)(2,1)S(1)} %get-tuple-element.69), channel_id=1, source_target_pairs={{0,2},{2,0},{1,3},{3,1},{4,6},{6,4},{5,7},{7,5},{8,10},{10,8},{9,1... | collective-permute-start | bytes 1572872 | tf_op jit(solution)/shard_map/ppermute | solution.py:507
  8.6 12.9 %collective-permute-start.3 = (bf16[2,2,64,256]{3,2,1,0:T(8,128)(2,1)S(1)}, bf16[2,2,64,256]{3,2,1,0:T(8,128)(2,1)S(1)}, u32[]{:S(2)}, u32[]{:S(2)}) collective-permute-start(bf16[2,2,64,256]{3,2,1,0:T(8,128)(2,1)S(1)} %get-tuple-element.59), channel_id=1, source_target_pairs={{0,8},{4,12},{8,0},{12,4},{1,9},{5,13},{9,1},{13,5},{2,10},{6,14},... | collective-permute-start | bytes 393224 | tf_op jit(solution)/shard_map/ppermute | solution.py:507
  11.7 9.8 %collective-permute-start.4 = (bf16[2,2,64,256]{3,2,1,0:T(8,128)(2,1)S(1)}, bf16[2,2,64,256]{3,2,1,0:T(8,128)(2,1)S(1)}, u32[]{:S(2)}, u32[]{:S(2)}) collective-permute-start(bf16[2,2,64,256]{3,2,1,0:T(8,128)(2,1)S(1)} %get-tuple-element.60), channel_id=1, source_target_pairs={{0,12},{4,8},{8,4},{12,0},{1,13},{5,9},{9,5},{13,1},{2,14},{6,10},... | collective-permute-start | bytes 393224 | tf_op jit(solution)/shard_map/ppermute | solution.py:507
  13.1 8.6 %collective-permute-start.5 = (bf16[2,2,64,256]{3,2,1,0:T(8,128)(2,1)S(1)}, bf16[2,2,64,256]{3,2,1,0:T(8,128)(2,1)S(1)}, u32[]{:S(2)}, u32[]{:S(2)}) collective-permute-start(bf16[2,2,64,256]{3,2,1,0:T(8,128)(2,1)S(1)} %get-tuple-element.61), channel_id=1, source_target_pairs={{0,4},{4,0},{8,12},{12,8},{1,5},{5,1},{9,13},{13,9},{2,6},{6,2},{1... | collective-permute-start | bytes 393224 | tf_op jit(solution)/shard_map/ppermute | solution.py:507
  21.8 9.8 %collective-permute-start.8 = (bf16[2,2,64,256]{3,2,1,0:T(8,128)(2,1)S(1)}, bf16[2,2,64,256]{3,2,1,0:T(8,128)(2,1)S(1)}, u32[]{:S(2)}, u32[]{:S(2)}) collective-permute-start(bf16[2,2,64,256]{3,2,1,0:T(8,128)(2,1)S(1)} %get-tuple-element.68.rest_0_), channel_id=1, source_target_pairs={{0,2},{2,0},{1,3},{3,1},{4,6},{6,4},{5,7},{7,5},{8,10},{10,8},{9,1... | collective-permute-start | bytes 393224 | tf_op jit(solution)/shard_map/ppermute | solution.py:507
  23.4 8.2 %collective-permute-start = (bf16[2,256,512]{2,1,0:T(8,128)(2,1)S(1)}, bf16[2,256,512]{2,1,0:T(8,128)(2,1)S(1)}, u32[]{:S(2)}, u32[]{:S(2)}) collective-permute-start(bf16[2,256,512]{2,1,0:T(8,128)(2,1)S(1)} %get-tuple-element.51.rest_1_.rest_0_.rest_2_), channel_id=1, source_target_pairs={{0,1},{1,0},{2,3},{3,2},{4,5},{5,4},{6,7},{7,6},{8,9},{9,8},{10,11... | collective-permute-start | bytes 1572872 | tf_op jit(solution)/shard_map/ppermute | solution.py:507
  23.4 8.2 %collective-permute-start.1 = (bf16[2,256,512]{2,1,0:T(8,128)(2,1)S(1)}, bf16[2,256,512]{2,1,0:T(8,128)(2,1)S(1)}, u32[]{:S(2)}, u32[]{:S(2)}) collective-permute-start(bf16[2,256,512]{2,1,0:T(8,128)(2,1)S(1)} %get-tuple-element.52.rest_3_.rest_2_.rest_4_), channel_id=1, source_target_pairs={{0,1},{1,0},{2,3},{3,2},{4,5},{5,4},{6,7},{7,6},{8,9},{9,8},{10,11... | collective-permute-start | bytes 1572872 | tf_op jit(solution)/shard_map/ppermute | solution.py:507
  23.9 8.5 %collective-permute-start.9 = (bf16[2,256,512]{2,1,0:T(8,128)(2,1)S(1)}, bf16[2,256,512]{2,1,0:T(8,128)(2,1)S(1)}, u32[]{:S(2)}, u32[]{:S(2)}) collective-permute-start(bf16[2,256,512]{2,1,0:T(8,128)(2,1)S(1)} %collective-permute-done.6.rest_2_.rest_0_.rest_3_), channel_id=1, source_target_pairs={{0,1},{1,0},{2,3},{3,2},{4,5},{5,4},{6,7},{7,6},{8,9},{9,8},{10,11... | collective-permute-start | bytes 1572872 | tf_op jit(solution)/shard_map/ppermute | solution.py:507
  34.0 7.1 %collective-permute-start.11 = (bf16[64,1024]{1,0:T(8,128)(2,1)S(1)}, bf16[64,1024]{1,0:T(8,128)(2,1)S(1)}, u32[]{:S(2)}, u32[]{:S(2)}) collective-permute-start(bf16[64,1024]{1,0:T(8,128)(2,1)S(1)} %get-tuple-element.74), channel_id=1, source_target_pairs={{0,4},{1,9},{4,0},{5,13},{8,12},{9,1},{12,8},{13,5},{2,6},{3,11},{... | collective-permute-start | bytes 393224 | tf_op jit(solution)/shard_map/ppermute | solution.py:520
  35.9 9.3 %collective-permute-start.12 = (bf16[64,1024]{1,0:T(8,128)(2,1)S(1)}, bf16[64,1024]{1,0:T(8,128)(2,1)S(1)}, u32[]{:S(2)}, u32[]{:S(2)}) collective-permute-start(bf16[64,1024]{1,0:T(8,128)(2,1)S(1)} %get-tuple-element.75), channel_id=1, source_target_pairs={{0,12},{1,13},{4,8},{5,9},{8,4},{9,5},{12,0},{13,1},{2,14},{3,15},... | collective-permute-start | bytes 393224 | tf_op jit(solution)/shard_map/ppermute | solution.py:520
  38.4 10.8 %collective-permute-start.13 = (bf16[64,1024]{1,0:T(8,128)(2,1)S(1)}, bf16[64,1024]{1,0:T(8,128)(2,1)S(1)}, u32[]{:S(2)}, u32[]{:S(2)}) collective-permute-start(bf16[64,1024]{1,0:T(8,128)(2,1)S(1)} %get-tuple-element.76), channel_id=1, source_target_pairs={{0,8},{1,5},{4,12},{5,1},{8,0},{9,13},{12,4},{13,9},{2,10},{3,7},{... | collective-permute-start | bytes 393224 | tf_op jit(solution)/shard_map/ppermute | solution.py:520
  50.2 6.9 %collective-permute-start.14 = (bf16[64,1024]{1,0:T(8,128)(2,1)S(1)}, bf16[64,1024]{1,0:T(8,128)(2,1)S(1)}, u32[]{:S(2)}, u32[]{:S(2)}) collective-permute-start(bf16[64,1024]{1,0:T(8,128)(2,1)S(1)} %get-tuple-element.78), channel_id=1, source_target_pairs={{0,4},{1,9},{4,0},{5,13},{8,12},{9,1},{12,8},{13,5},{2,6},{3,11},{... | collective-permute-start | bytes 393224 | tf_op jit(solution)/shard_map/ppermute | solution.py:520
  51.0 9.3 %collective-permute-start.15 = (bf16[64,1024]{1,0:T(8,128)(2,1)S(1)}, bf16[64,1024]{1,0:T(8,128)(2,1)S(1)}, u32[]{:S(2)}, u32[]{:S(2)}) collective-permute-start(bf16[64,1024]{1,0:T(8,128)(2,1)S(1)} %get-tuple-element.79), channel_id=1, source_target_pairs={{0,12},{1,13},{4,8},{5,9},{8,4},{9,5},{12,0},{13,1},{2,14},{3,15},... | collective-permute-start | bytes 393224 | tf_op jit(solution)/shard_map/ppermute | solution.py:520
  53.9 10.2 %collective-permute-start.16 = (bf16[64,1024]{1,0:T(8,128)(2,1)S(1)}, bf16[64,1024]{1,0:T(8,128)(2,1)S(1)}, u32[]{:S(2)}, u32[]{:S(2)}) collective-permute-start(bf16[64,1024]{1,0:T(8,128)(2,1)S(1)} %get-tuple-element.80), channel_id=1, source_target_pairs={{0,8},{1,5},{4,12},{5,1},{8,0},{9,13},{12,4},{13,9},{2,10},{3,7},{... | collective-permute-start | bytes 393224 | tf_op jit(solution)/shard_map/ppermute | solution.py:520
  64.5 4.3 %collective-permute-start.17 = (bf16[2,2,32,256]{3,2,1,0:T(8,128)(2,1)S(1)}, bf16[2,2,32,256]{3,2,1,0:T(8,128)(2,1)S(1)}, u32[]{:S(2)}, u32[]{:S(2)}) collective-permute-start(bf16[2,2,32,256]{3,2,1,0:T(8,128)(2,1)S(1)} %get-tuple-element.82), channel_id=1, source_target_pairs={{0,2},{2,0},{1,3},{3,1},{4,6},{6,4},{5,7},{7,5},{8,10},{10,8},{9,1... | collective-permute-start | bytes 196616 | tf_op jit(solution)/shard_map/ppermute | solution.py:507
  68.9 5.7 %collective-permute-start.18 = (bf16[2,2,32,256]{3,2,1,0:T(8,128)(2,1)S(1)}, bf16[2,2,32,256]{3,2,1,0:T(8,128)(2,1)S(1)}, u32[]{:S(2)}, u32[]{:S(2)}) collective-permute-start(bf16[2,2,32,256]{3,2,1,0:T(8,128)(2,1)S(1)} %shard_map.84.rest_0_), channel_id=1, source_target_pairs={{0,8},{4,12},{8,0},{12,4},{1,9},{5,13},{9,1},{13,5},{2,10},{6,14},... | collective-permute-start | bytes 196616 | tf_op jit(solution)/shard_map/ppermute | solution.py:507
  70.4 6.2 %collective-permute-start.22 = (bf16[2,2,32,256]{3,2,1,0:T(8,128)(2,1)S(1)}, bf16[2,2,32,256]{3,2,1,0:T(8,128)(2,1)S(1)}, u32[]{:S(2)}, u32[]{:S(2)}) collective-permute-start(bf16[2,2,32,256]{3,2,1,0:T(8,128)(2,1)S(1)} %shard_map.86.rest_0_), channel_id=1, source_target_pairs={{0,8},{4,12},{8,0},{12,4},{1,9},{5,13},{9,1},{13,5},{2,10},{6,14},... | collective-permute-start | bytes 196616 | tf_op jit(solution)/shard_map/ppermute | solution.py:507
  72.0 5.3 %collective-permute-start.20 = (bf16[2,2,32,256]{3,2,1,0:T(8,128)(2,1)S(1)}, bf16[2,2,32,256]{3,2,1,0:T(8,128)(2,1)S(1)}, u32[]{:S(2)}, u32[]{:S(2)}) collective-permute-start(bf16[2,2,32,256]{3,2,1,0:T(8,128)(2,1)S(1)} %shard_map.84.rest_0_), channel_id=1, source_target_pairs={{0,4},{4,0},{8,12},{12,8},{1,5},{5,1},{9,13},{13,9},{2,6},{6,2},{1... | collective-permute-start | bytes 196616 | tf_op jit(solution)/shard_map/ppermute | solution.py:507
  74.6 5.8 %collective-permute-start.24 = (bf16[2,2,32,256]{3,2,1,0:T(8,128)(2,1)S(1)}, bf16[2,2,32,256]{3,2,1,0:T(8,128)(2,1)S(1)}, u32[]{:S(2)}, u32[]{:S(2)}) collective-permute-start(bf16[2,2,32,256]{3,2,1,0:T(8,128)(2,1)S(1)} %shard_map.86.rest_0_), channel_id=1, source_target_pairs={{0,4},{4,0},{8,12},{12,8},{1,5},{5,1},{9,13},{13,9},{2,6},{6,2},{1... | collective-permute-start | bytes 196616 | tf_op jit(solution)/shard_map/ppermute | solution.py:507
  79.1 4.3 %collective-permute-start.25 = (bf16[2,2,32,256]{3,2,1,0:T(8,128)(2,1)S(1)}, bf16[2,2,32,256]{3,2,1,0:T(8,128)(2,1)S(1)}, u32[]{:S(2)}, u32[]{:S(2)}) collective-permute-start(bf16[2,2,32,256]{3,2,1,0:T(8,128)(2,1)S(1)} %shard_map.85.rest_0_), channel_id=1, source_target_pairs={{0,2},{2,0},{1,3},{3,1},{4,6},{6,4},{5,7},{7,5},{8,10},{10,8},{9,1... | collective-permute-start | bytes 196616 | tf_op jit(solution)/shard_map/ppermute | solution.py:507
  81.1 4.3 %collective-permute-start.26 = (bf16[2,2,32,256]{3,2,1,0:T(8,128)(2,1)S(1)}, bf16[2,2,32,256]{3,2,1,0:T(8,128)(2,1)S(1)}, u32[]{:S(2)}, u32[]{:S(2)}) collective-permute-start(bf16[2,2,32,256]{3,2,1,0:T(8,128)(2,1)S(1)} %shard_map.87.rest_1_), channel_id=1, source_target_pairs={{0,2},{2,0},{1,3},{3,1},{4,6},{6,4},{5,7},{7,5},{8,10},{10,8},{9,1... | collective-permute-start | bytes 196616 | tf_op jit(solution)/shard_map/ppermute | solution.py:507
  86.3 5.0 %collective-permute-start.27 = (bf16[64,1024]{1,0:T(8,128)(2,1)S(1)}, bf16[64,1024]{1,0:T(8,128)(2,1)S(1)}, u32[]{:S(2)}, u32[]{:S(2)}) collective-permute-start(bf16[64,1024]{1,0:T(8,128)(2,1)S(1)} %get-tuple-element.86), channel_id=1, source_target_pairs={{0,4},{1,9},{4,0},{5,13},{8,12},{9,1},{12,8},{13,5},{2,6},{3,11},{... | collective-permute-start | bytes 393224 | tf_op jit(solution)/shard_map/ppermute | solution.py:520
  87.1 6.9 %collective-permute-start.28 = (bf16[64,1024]{1,0:T(8,128)(2,1)S(1)}, bf16[64,1024]{1,0:T(8,128)(2,1)S(1)}, u32[]{:S(2)}, u32[]{:S(2)}) collective-permute-start(bf16[64,1024]{1,0:T(8,128)(2,1)S(1)} %get-tuple-element.87), channel_id=1, source_target_pairs={{0,12},{1,13},{4,8},{5,9},{8,4},{9,5},{12,0},{13,1},{2,14},{3,15},... | collective-permute-start | bytes 393224 | tf_op jit(solution)/shard_map/ppermute | solution.py:520
  89.1 12.3 %collective-permute-start.29 = (bf16[64,1024]{1,0:T(8,128)(2,1)S(1)}, bf16[64,1024]{1,0:T(8,128)(2,1)S(1)}, u32[]{:S(2)}, u32[]{:S(2)}) collective-permute-start(bf16[64,1024]{1,0:T(8,128)(2,1)S(1)} %get-tuple-element.88), channel_id=1, source_target_pairs={{0,8},{1,5},{4,12},{5,1},{8,0},{9,13},{12,4},{13,9},{2,10},{3,7},{... | collective-permute-start | bytes 393224 | tf_op jit(solution)/shard_map/ppermute | solution.py:520
  102.4 5.0 %collective-permute-start.30 = (bf16[64,1024]{1,0:T(8,128)(2,1)S(1)}, bf16[64,1024]{1,0:T(8,128)(2,1)S(1)}, u32[]{:S(2)}, u32[]{:S(2)}) collective-permute-start(bf16[64,1024]{1,0:T(8,128)(2,1)S(1)} %get-tuple-element.90), channel_id=1, source_target_pairs={{0,4},{1,9},{4,0},{5,13},{8,12},{9,1},{12,8},{13,5},{2,6},{3,11},{... | collective-permute-start | bytes 393224 | tf_op jit(solution)/shard_map/ppermute | solution.py:520
  102.5 6.9 %collective-permute-start.31 = (bf16[64,1024]{1,0:T(8,128)(2,1)S(1)}, bf16[64,1024]{1,0:T(8,128)(2,1)S(1)}, u32[]{:S(2)}, u32[]{:S(2)}) collective-permute-start(bf16[64,1024]{1,0:T(8,128)(2,1)S(1)} %get-tuple-element.91), channel_id=1, source_target_pairs={{0,12},{1,13},{4,8},{5,9},{8,4},{9,5},{12,0},{13,1},{2,14},{3,15},... | collective-permute-start | bytes 393224 | tf_op jit(solution)/shard_map/ppermute | solution.py:520
  104.1 11.9 %collective-permute-start.32 = (bf16[64,1024]{1,0:T(8,128)(2,1)S(1)}, bf16[64,1024]{1,0:T(8,128)(2,1)S(1)}, u32[]{:S(2)}, u32[]{:S(2)}) collective-permute-start(bf16[64,1024]{1,0:T(8,128)(2,1)S(1)} %get-tuple-element.92), channel_id=1, source_target_pairs={{0,8},{1,5},{4,12},{5,1},{8,0},{9,13},{12,4},{13,9},{2,10},{3,7},{... | collective-permute-start | bytes 393224 | tf_op jit(solution)/shard_map/ppermute | solution.py:520
  120.8 5.2 %collective-permute-start.38 = (bf16[2,2,32,256]{3,2,1,0:T(8,128)(2,1)S(1)}, bf16[2,2,32,256]{3,2,1,0:T(8,128)(2,1)S(1)}, u32[]{:S(2)}, u32[]{:S(2)}) collective-permute-start(bf16[2,2,32,256]{3,2,1,0:T(8,128)(2,1)S(1)} %shard_map.94.rest_0_), channel_id=1, source_target_pairs={{0,8},{4,12},{8,0},{12,4},{1,9},{5,13},{9,1},{13,5},{2,10},{6,14},... | collective-permute-start | bytes 196616 | tf_op jit(solution)/shard_map/ppermute | solution.py:507
  122.1 6.0 %collective-permute-start.34 = (bf16[2,2,32,256]{3,2,1,0:T(8,128)(2,1)S(1)}, bf16[2,2,32,256]{3,2,1,0:T(8,128)(2,1)S(1)}, u32[]{:S(2)}, u32[]{:S(2)}) collective-permute-start(bf16[2,2,32,256]{3,2,1,0:T(8,128)(2,1)S(1)} %shard_map.93.rest_0_), channel_id=1, source_target_pairs={{0,8},{4,12},{8,0},{12,4},{1,9},{5,13},{9,1},{13,5},{2,10},{6,14},... | collective-permute-start | bytes 196616 | tf_op jit(solution)/shard_map/ppermute | solution.py:507
  123.9 4.6 %collective-permute-start.40 = (bf16[2,2,32,256]{3,2,1,0:T(8,128)(2,1)S(1)}, bf16[2,2,32,256]{3,2,1,0:T(8,128)(2,1)S(1)}, u32[]{:S(2)}, u32[]{:S(2)}) collective-permute-start(bf16[2,2,32,256]{3,2,1,0:T(8,128)(2,1)S(1)} %shard_map.94.rest_0_), channel_id=1, source_target_pairs={{0,4},{4,0},{8,12},{12,8},{1,5},{5,1},{9,13},{13,9},{2,6},{6,2},{1... | collective-permute-start | bytes 196616 | tf_op jit(solution)/shard_map/ppermute | solution.py:507
  126.0 6.2 %collective-permute-start.36 = (bf16[2,2,32,256]{3,2,1,0:T(8,128)(2,1)S(1)}, bf16[2,2,32,256]{3,2,1,0:T(8,128)(2,1)S(1)}, u32[]{:S(2)}, u32[]{:S(2)}) collective-permute-start(bf16[2,2,32,256]{3,2,1,0:T(8,128)(2,1)S(1)} %shard_map.93.rest_0_), channel_id=1, source_target_pairs={{0,4},{4,0},{8,12},{12,8},{1,5},{5,1},{9,13},{13,9},{2,6},{6,2},{1... | collective-permute-start | bytes 196616 | tf_op jit(solution)/shard_map/ppermute | solution.py:507
  (16 other events, 182.2 us)

commit v20 on v19

--- a/solution.py
+++ b/solution.py
@@ -256,7 +256,7 @@
     return tuple(outs[:3]), tuple(outs[3:])
 
 
-def down_products(before, spectra, parts, side, first, places, freq_devs=0):
+def down_products(before, spectra, parts, side, first, places, freq_devs=0, by_core=False):
     _, per_dev, _, rcv = spectra[0].shape
     rows = sum(v.shape[2] for v in spectra)
     flat = [pair[side] for part in parts for pair in part]
@@ -285,7 +285,8 @@
                     held[:, :, :, to] = held_ref[:, :, :, to]
         if freq_devs:
             for slot, out in enumerate(outs[:freq_devs]):
-                start = pl.multiple_of((freq[0] ^ way_of(slot, sblk[0], freq_devs)) * share, share)
+                way = way_of(slot, sblk[0] if by_core else 1, freq_devs)
+                start = pl.multiple_of((freq[0] ^ way) * share, share)
                 out[...] = held[:, :, pl.ds(start, share), :].reshape(out.shape).astype(BF16)
 
     sums = (2, per_dev, rows, total_width)
@@ -330,7 +331,7 @@
     lax.fori_loop(0, width // BLOCK, at, 0, unroll=2)
 
 
-def windowed(messages, tables, matrix, places, per_dev, share):
+def windowed(messages, tables, matrix, places, per_dev, share, by_core):
     cosines, sines, fraction = tables
     freq_devs = len(messages)
     width = messages[0].shape[-1]
@@ -338,7 +339,11 @@
 
     def body(freq, _, sblk, c_ref, s_ref, f_ref, g_ref, *rest):
         refs, outs = rest[:freq_devs], rest[freq_devs:]
-        matrix_here = g_ref[freq[0] * 2 + sblk[0]]
+        matrix_here = g_ref[freq[0] * 2 + (sblk[0] if by_core else 1)]
+        spots = list(range(freq_devs))
+        if not by_core:
+            first, second = slot_ways(freq_devs)
+            spots = [first.index(way) + sblk[0] * (slot - first.index(way)) for slot, way in enumerate(second)]
 
         def one(at):
             data = [ref[:, at].astype(F32).reshape(2, per_dev, share, BLOCK) for ref in refs]
@@ -346,8 +351,8 @@
             for first in range(0, share, ROWS):
                 cut = slice(first, first + ROWS)
                 plain = [value[:, :, cut] for value in data]
-                cos = [c_ref[step, :, cut, at] for step in range(freq_devs)]
-                sin = [s_ref[step, :, cut, at] for step in range(freq_devs)]
+                cos = [c_ref[spot, :, cut, at] for spot in spots]
+                sin = [s_ref[spot, :, cut, at] for spot in spots]
                 up, low = mixed_fields(plain, cos, sin, matrix_here)
                 part = f_ref[cut, at]
                 for step in range(freq_devs):
@@ -368,7 +373,7 @@
     )
 
 
-def up_products(messages, parts, places, rows, side):
+def up_products(messages, parts, places, rows, side, by_core):
     freq_devs = len(messages)
     flat = [pair[side] for part in parts for pair in part]
     per_dev, src, rcv = flat[0].shape[0], flat[0].shape[1], flat[0].shape[2] // 2
@@ -381,7 +386,8 @@
         resp, refs = rest[: len(flat)], rest[len(flat) : len(flat) + freq_devs]
         outs, held = rest[len(flat) + freq_devs : -1], rest[-1]
         for slot, ref in enumerate(refs):
-            start = pl.multiple_of((freq[0] ^ way_of(slot, sblk[0], freq_devs)) * share, share)
+            way = way_of(slot, sblk[0] if by_core else 1, freq_devs)
+            start = pl.multiple_of((freq[0] ^ way) * share, share)
             value = ref[...].reshape(2, per_dev, share, total_width)
             for part in range(2):
                 for j in range(per_dev):
@@ -568,10 +574,12 @@
         if at:
             held = down_products(held, far, parts[:at], 1, 0, places)
         first = at * 2 * kept[0].shape[1]
-        messages = dealt_by_core(down_products(held, far, parts[at:], 1, first, places, freq_devs))
-        messages = dealt_by_core(windowed(messages, src_tables, matrix, places, per_dev, share))
-        received = [exchanged(v, "rblk", 1) for v in up_products(messages, parts, places, half_rows, 1)]
-        keep = up_products(messages, parts, places, half_rows, 0)
+        by_core = step == 0
+        deal = dealt_by_core if by_core else dealt_out
+        messages = deal(down_products(held, far, parts[at:], 1, first, places, freq_devs, by_core))
+        messages = deal(windowed(messages, src_tables, matrix, places, per_dev, share, by_core))
+        received = [exchanged(v, "rblk", 1) for v in up_products(messages, parts, places, half_rows, 1, by_core)]
+        keep = up_products(messages, parts, places, half_rows, 0, by_core)
         near, far = [], []
         for chunk in range(CHUNKS):
             back = spread(added(keep[chunk], received[chunk]), freq_devs)

time: 135 us -> 131 us (0.970)
  waiting for transfers between devices: 72.5 us -> 65.6 us
  starting transfers between devices: 42.8 us -> 46.5 us
    ppermute x12 -> x6, waiting for transfers between devices: 39.3 us -> 17.7 us  [dealt_by_core(): out.append(lax.ppermute(parts[slot], ('freq', 'sblk'), pairs))]
    ppermute x29 -> x35, waiting for transfers between devices: 33.3 us -> 47.9 us  [exchanged(): lax.ppermute(value, axis, [(i, i ^ step) for i in range(lax.axis_size(axi...]
    ppermute x29 -> x35, starting transfers between devices: 27 us -> 37.8 us  [exchanged(): lax.ppermute(value, axis, [(i, i ^ step) for i in range(lax.axis_size(axi...]
    ppermute x12 -> x6, starting transfers between devices: 15.8 us -> 8.66 us  [dealt_by_core(): out.append(lax.ppermute(parts[slot], ('freq', 'sblk'), pairs))]
  transfers between devices with their start and end apart: 41 -> 41, of which waited for: 30 -> 27; matrix products, arithmetic and copies ran while one was open for 0% -> 0% of each run, Pallas kernels for 6% -> 6%
where the time goes in v20:
time: 131 us
  waiting for transfers between devices  65.6 us (50%)
  starting transfers between devices  46.5 us (35%)
  Pallas kernels  14.2 us (11%)
  local copies, waits for them, and re-layouts  4.56 us (3%)
    ppermute x35, waiting for transfers between devices, exchanged(): lax.ppermute(value, axis, [(i, i ^ step) for i in range(lax.axis_size(axi...  47.9 us
    ppermute x35, starting transfers between devices, exchanged(): lax.ppermute(value, axis, [(i, i ^ step) for i in range(lax.axis_size(axi...  37.8 us
    ppermute x6, waiting for transfers between devices, dealt_by_core(): out.append(lax.ppermute(parts[slot], ('freq', 'sblk'), pairs))  17.7 us
    pallas_call x24, Pallas kernels, call(): pl.pallas_call(body, grid_spec=pltpu.PrefetchScalarGridSpec(num_scalar_pr...  14.2 us
    ppermute x6, starting transfers between devices, dealt_by_core(): out.append(lax.ppermute(parts[slot], ('freq', 'sblk'), pairs))  8.66 us
    unnamed x15, local copies, waits for them, and re-layouts  4.56 us
  transfers between devices with their start and end apart: 41, of which 27 were waited for; matrix products, arithmetic and copies ran while one was open for 0% of the time, Pallas kernels for 6%

profile of v20, /device:TPU:0, one launch (start us, length us, event | category | flops | bytes accessed | tf_op | source)
XLA Modules:
  0.0 131.1 jit_solution(12485866377242358135)
XLA Ops:
  0.8 1.6 %copy-done.3 = bf16[2,2,1024,256]{3,2,1,0:T(8,128)(2,1)S(1)} copy-done((bf16[2,2,1024,256]{3,2,1,0:T(8,128)(2,1)S(1)}, bf16[2,2,1024,256]{3,2,1,0:T(8,128)(2,1)}, u32[]{:S(2)}) %copy-start.3) | copy-done | bytes 2097176
  2.6 3.0 %collective-permute-start.6 = (bf16[2,256,512]{2,1,0:T(8,128)(2,1)S(1)}, bf16[2,256,512]{2,1,0:T(8,128)(2,1)S(1)}, u32[]{:S(2)}, u32[]{:S(2)}) collective-permute-start(bf16[2,256,512]{2,1,0:T(8,128)(2,1)S(1)} %get-tuple-element.66), channel_id=1, source_target_pairs={{0,2},{2,0},{1,3},{3,1},{4,6},{6,4},{5,7},{7,5},{8,10},{10,8},{9,1... | collective-permute-start | bytes 1572872 | tf_op jit(solution)/shard_map/ppermute | solution.py:513
  5.7 2.2 %copy-done = bf16[64,128,256]{2,1,0:T(8,128)(2,1)S(1)} copy-done((bf16[64,128,256]{2,1,0:T(8,128)(2,1)S(1)}, bf16[64,128,256]{2,1,0:T(8,128)(2,1)}, u32[]{:S(2)}) %copy-start) | copy-done | bytes 4194328
  8.6 3.1 %collective-permute-start.3 = (bf16[2,2,64,256]{3,2,1,0:T(8,128)(2,1)S(1)}, bf16[2,2,64,256]{3,2,1,0:T(8,128)(2,1)S(1)}, u32[]{:S(2)}, u32[]{:S(2)}) collective-permute-start(bf16[2,2,64,256]{3,2,1,0:T(8,128)(2,1)S(1)} %get-tuple-element.59), channel_id=1, source_target_pairs={{0,8},{4,12},{8,0},{12,4},{1,9},{5,13},{9,1},{13,5},{2,10},{6,14},... | collective-permute-start | bytes 393224 | tf_op jit(solution)/shard_map/ppermute | solution.py:513
  13.3 8.2 %collective-permute-done.3.refs_1_ = bf16[2,2,64,256]{3,2,1,0:T(8,128)(2,1)S(1)} collective-permute-done((bf16[2,2,64,256]{3,2,1,0:T(8,128)(2,1)S(1)}, bf16[2,2,64,256]{3,2,1,0:T(8,128)(2,1)S(1)}, u32[]{:S(2)}, u32[]{:S(2)}) %collective-permute-start.3) | collective-permute-done | bytes 131104 | tf_op jit(solution)/shard_map/ppermute | solution.py:513
  21.8 1.6 %collective-permute-start.8 = (bf16[2,2,64,256]{3,2,1,0:T(8,128)(2,1)S(1)}, bf16[2,2,64,256]{3,2,1,0:T(8,128)(2,1)S(1)}, u32[]{:S(2)}, u32[]{:S(2)}) collective-permute-start(bf16[2,2,64,256]{3,2,1,0:T(8,128)(2,1)S(1)} %get-tuple-element.68.rest_0_), channel_id=1, source_target_pairs={{0,2},{2,0},{1,3},{3,1},{4,6},{6,4},{5,7},{7,5},{8,10},{10,8},{9,1... | collective-permute-start | bytes 393224 | tf_op jit(solution)/shard_map/ppermute | solution.py:513
  24.0 7.6 %collective-permute-done.8.rest_1_ = bf16[2,2,64,256]{3,2,1,0:T(8,128)(2,1)S(1)} collective-permute-done((bf16[2,2,64,256]{3,2,1,0:T(8,128)(2,1)S(1)}, bf16[2,2,64,256]{3,2,1,0:T(8,128)(2,1)S(1)}, u32[]{:S(2)}, u32[]{:S(2)}) %collective-permute-start.8) | collective-permute-done | bytes 131104 | tf_op jit(solution)/shard_map/ppermute | solution.py:513
  34.0 1.9 %collective-permute-start.11 = (bf16[64,1024]{1,0:T(8,128)(2,1)S(1)}, bf16[64,1024]{1,0:T(8,128)(2,1)S(1)}, u32[]{:S(2)}, u32[]{:S(2)}) collective-permute-start(bf16[64,1024]{1,0:T(8,128)(2,1)S(1)} %get-tuple-element.74), channel_id=1, source_target_pairs={{0,4},{1,9},{4,0},{5,13},{8,12},{9,1},{12,8},{13,5},{2,6},{3,11},{... | collective-permute-start | bytes 393224 | tf_op jit(solution)/shard_map/ppermute | solution.py:526
  35.9 2.5 %collective-permute-start.12 = (bf16[64,1024]{1,0:T(8,128)(2,1)S(1)}, bf16[64,1024]{1,0:T(8,128)(2,1)S(1)}, u32[]{:S(2)}, u32[]{:S(2)}) collective-permute-start(bf16[64,1024]{1,0:T(8,128)(2,1)S(1)} %get-tuple-element.75), channel_id=1, source_target_pairs={{0,12},{1,13},{4,8},{5,9},{8,4},{9,5},{12,0},{13,1},{2,14},{3,15},... | collective-permute-start | bytes 393224 | tf_op jit(solution)/shard_map/ppermute | solution.py:526
  41.1 4.0 %collective-permute-done.12.rest_2_ = bf16[64,1024]{1,0:T(8,128)(2,1)S(1)} collective-permute-done((bf16[64,1024]{1,0:T(8,128)(2,1)S(1)}, bf16[64,1024]{1,0:T(8,128)(2,1)S(1)}, u32[]{:S(2)}, u32[]{:S(2)}) %collective-permute-start.12) | collective-permute-done | bytes 131104 | tf_op jit(solution)/shard_map/ppermute | solution.py:526
  45.2 4.0 %collective-permute-done.13.rest_3_ = bf16[64,1024]{1,0:T(8,128)(2,1)S(1)} collective-permute-done((bf16[64,1024]{1,0:T(8,128)(2,1)S(1)}, bf16[64,1024]{1,0:T(8,128)(2,1)S(1)}, u32[]{:S(2)}, u32[]{:S(2)}) %collective-permute-start.13) | collective-permute-done | bytes 131104 | tf_op jit(solution)/shard_map/ppermute | solution.py:526
  51.0 2.9 %collective-permute-start.15 = (bf16[64,1024]{1,0:T(8,128)(2,1)S(1)}, bf16[64,1024]{1,0:T(8,128)(2,1)S(1)}, u32[]{:S(2)}, u32[]{:S(2)}) collective-permute-start(bf16[64,1024]{1,0:T(8,128)(2,1)S(1)} %get-tuple-element.79), channel_id=1, source_target_pairs={{0,12},{1,13},{4,8},{5,9},{8,4},{9,5},{12,0},{13,1},{2,14},{3,15},... | collective-permute-start | bytes 393224 | tf_op jit(solution)/shard_map/ppermute | solution.py:526
  54.4 2.7 %collective-permute-done.14.rest_5_ = bf16[64,1024]{1,0:T(8,128)(2,1)S(1)} collective-permute-done((bf16[64,1024]{1,0:T(8,128)(2,1)S(1)}, bf16[64,1024]{1,0:T(8,128)(2,1)S(1)}, u32[]{:S(2)}, u32[]{:S(2)}) %collective-permute-start.14) | collective-permute-done | bytes 131104 | tf_op jit(solution)/shard_map/ppermute | solution.py:526
  57.1 3.2 %collective-permute-done.15.rest_6_ = bf16[64,1024]{1,0:T(8,128)(2,1)S(1)} collective-permute-done((bf16[64,1024]{1,0:T(8,128)(2,1)S(1)}, bf16[64,1024]{1,0:T(8,128)(2,1)S(1)}, u32[]{:S(2)}, u32[]{:S(2)}) %collective-permute-start.15) | collective-permute-done | bytes 131104 | tf_op jit(solution)/shard_map/ppermute | solution.py:526
  60.3 3.8 %collective-permute-done.16.rest_7_ = bf16[64,1024]{1,0:T(8,128)(2,1)S(1)} collective-permute-done((bf16[64,1024]{1,0:T(8,128)(2,1)S(1)}, bf16[64,1024]{1,0:T(8,128)(2,1)S(1)}, u32[]{:S(2)}, u32[]{:S(2)}) %collective-permute-start.16) | collective-permute-done | bytes 131104 | tf_op jit(solution)/shard_map/ppermute | solution.py:526
  67.1 1.8 %collective-permute-done.17.r_ref = bf16[2,2,32,256]{3,2,1,0:T(8,128)(2,1)S(1)} collective-permute-done((bf16[2,2,32,256]{3,2,1,0:T(8,128)(2,1)S(1)}, bf16[2,2,32,256]{3,2,1,0:T(8,128)(2,1)S(1)}, u32[]{:S(2)}, u32[]{:S(2)}) %collective-permute-start.17) | collective-permute-done | bytes 65568 | tf_op jit(solution)/shard_map/ppermute | solution.py:513
  70.4 1.6 %collective-permute-start.22 = (bf16[2,2,32,256]{3,2,1,0:T(8,128)(2,1)S(1)}, bf16[2,2,32,256]{3,2,1,0:T(8,128)(2,1)S(1)}, u32[]{:S(2)}, u32[]{:S(2)}) collective-permute-start(bf16[2,2,32,256]{3,2,1,0:T(8,128)(2,1)S(1)} %shard_map.86.rest_0_), channel_id=1, source_target_pairs={{0,8},{4,12},{8,0},{12,4},{1,9},{5,13},{9,1},{13,5},{2,10},{6,14},... | collective-permute-start | bytes 196616 | tf_op jit(solution)/shard_map/ppermute | solution.py:513
  73.0 1.6 %collective-permute-done.18.rest_1_ = bf16[2,2,32,256]{3,2,1,0:T(8,128)(2,1)S(1)} collective-permute-done((bf16[2,2,32,256]{3,2,1,0:T(8,128)(2,1)S(1)}, bf16[2,2,32,256]{3,2,1,0:T(8,128)(2,1)S(1)}, u32[]{:S(2)}, u32[]{:S(2)}) %collective-permute-start.18) | collective-permute-done | bytes 65568 | tf_op jit(solution)/shard_map/ppermute | solution.py:513
  74.6 2.0 %collective-permute-start.24 = (bf16[2,2,32,256]{3,2,1,0:T(8,128)(2,1)S(1)}, bf16[2,2,32,256]{3,2,1,0:T(8,128)(2,1)S(1)}, u32[]{:S(2)}, u32[]{:S(2)}) collective-permute-start(bf16[2,2,32,256]{3,2,1,0:T(8,128)(2,1)S(1)} %shard_map.86.rest_0_), channel_id=1, source_target_pairs={{0,4},{4,0},{8,12},{12,8},{1,5},{5,1},{9,13},{13,9},{2,6},{6,2},{1... | collective-permute-start | bytes 196616 | tf_op jit(solution)/shard_map/ppermute | solution.py:513
  83.4 2.0 %collective-permute-done.26.rest_2_ = bf16[2,2,32,256]{3,2,1,0:T(8,128)(2,1)S(1)} collective-permute-done((bf16[2,2,32,256]{3,2,1,0:T(8,128)(2,1)S(1)}, bf16[2,2,32,256]{3,2,1,0:T(8,128)(2,1)S(1)}, u32[]{:S(2)}, u32[]{:S(2)}) %collective-permute-start.26) | collective-permute-done | bytes 65568 | tf_op jit(solution)/shard_map/ppermute | solution.py:513
  87.6 1.9 %collective-permute-start.28 = (bf16[64,1024]{1,0:T(8,128)(2,1)S(1)}, bf16[64,1024]{1,0:T(8,128)(2,1)S(1)}, u32[]{:S(2)}, u32[]{:S(2)}) collective-permute-start(bf16[64,1024]{1,0:T(8,128)(2,1)S(1)} %get-tuple-element.87), channel_id=1, source_target_pairs={{0,12},{4,8},{8,4},{12,0},{1,13},{5,9},{9,5},{13,1},{2,14},{6,10},... | collective-permute-start | bytes 393224 | tf_op jit(solution)/shard_map/ppermute | solution.py:513
  89.9 6.8 %collective-permute-done.27.rest_1_ = bf16[64,1024]{1,0:T(8,128)(2,1)S(1)} collective-permute-done((bf16[64,1024]{1,0:T(8,128)(2,1)S(1)}, bf16[64,1024]{1,0:T(8,128)(2,1)S(1)}, u32[]{:S(2)}, u32[]{:S(2)}) %collective-permute-start.27) | collective-permute-done | bytes 131104 | tf_op jit(solution)/shard_map/ppermute | solution.py:513
  96.7 2.9 %collective-permute-done.29.rest_3_ = bf16[64,1024]{1,0:T(8,128)(2,1)S(1)} collective-permute-done((bf16[64,1024]{1,0:T(8,128)(2,1)S(1)}, bf16[64,1024]{1,0:T(8,128)(2,1)S(1)}, u32[]{:S(2)}, u32[]{:S(2)}) %collective-permute-start.29) | collective-permute-done | bytes 131104 | tf_op jit(solution)/shard_map/ppermute | solution.py:513
  100.6 2.3 %collective-permute-start.30 = (bf16[64,1024]{1,0:T(8,128)(2,1)S(1)}, bf16[64,1024]{1,0:T(8,128)(2,1)S(1)}, u32[]{:S(2)}, u32[]{:S(2)}) collective-permute-start(bf16[64,1024]{1,0:T(8,128)(2,1)S(1)} %get-tuple-element.90), channel_id=1, source_target_pairs={{0,8},{4,12},{8,0},{12,4},{1,9},{5,13},{9,1},{13,5},{2,10},{6,14},... | collective-permute-start | bytes 393224 | tf_op jit(solution)/shard_map/ppermute | solution.py:513
  102.9 2.3 %collective-permute-start.31 = (bf16[64,1024]{1,0:T(8,128)(2,1)S(1)}, bf16[64,1024]{1,0:T(8,128)(2,1)S(1)}, u32[]{:S(2)}, u32[]{:S(2)}) collective-permute-start(bf16[64,1024]{1,0:T(8,128)(2,1)S(1)} %get-tuple-element.91), channel_id=1, source_target_pairs={{0,12},{4,8},{8,4},{12,0},{1,13},{5,9},{9,5},{13,1},{2,14},{6,10},... | collective-permute-start | bytes 393224 | tf_op jit(solution)/shard_map/ppermute | solution.py:513
  106.6 3.6 %collective-permute-done.31.rest_6_ = bf16[64,1024]{1,0:T(8,128)(2,1)S(1)} collective-permute-done((bf16[64,1024]{1,0:T(8,128)(2,1)S(1)}, bf16[64,1024]{1,0:T(8,128)(2,1)S(1)}, u32[]{:S(2)}, u32[]{:S(2)}) %collective-permute-start.31) | collective-permute-done | bytes 131104 | tf_op jit(solution)/shard_map/ppermute | solution.py:513
  110.2 2.2 %collective-permute-done.32.rest_7_ = bf16[64,1024]{1,0:T(8,128)(2,1)S(1)} collective-permute-done((bf16[64,1024]{1,0:T(8,128)(2,1)S(1)}, bf16[64,1024]{1,0:T(8,128)(2,1)S(1)}, u32[]{:S(2)}, u32[]{:S(2)}) %collective-permute-start.32) | collective-permute-done | bytes 131104 | tf_op jit(solution)/shard_map/ppermute | solution.py:513
  112.9 1.7 %collective-permute-start.37 = (bf16[2,2,32,256]{3,2,1,0:T(8,128)(2,1)S(1)}, bf16[2,2,32,256]{3,2,1,0:T(8,128)(2,1)S(1)}, u32[]{:S(2)}, u32[]{:S(2)}) collective-permute-start(bf16[2,2,32,256]{3,2,1,0:T(8,128)(2,1)S(1)} %get-tuple-element.96), channel_id=1, source_target_pairs={{0,2},{2,0},{1,3},{3,1},{4,6},{6,4},{5,7},{7,5},{8,10},{10,8},{9,1... | collective-permute-start | bytes 196616 | tf_op jit(solution)/shard_map/ppermute | solution.py:513
  115.5 1.8 %collective-permute-done.37.r_ref = bf16[2,2,32,256]{3,2,1,0:T(8,128)(2,1)S(1)} collective-permute-done((bf16[2,2,32,256]{3,2,1,0:T(8,128)(2,1)S(1)}, bf16[2,2,32,256]{3,2,1,0:T(8,128)(2,1)S(1)}, u32[]{:S(2)}, u32[]{:S(2)}) %collective-permute-start.37) | collective-permute-done | bytes 65568 | tf_op jit(solution)/shard_map/ppermute | solution.py:513
  117.3 1.6 %collective-permute-start.38 = (bf16[2,2,32,256]{3,2,1,0:T(8,128)(2,1)S(1)}, bf16[2,2,32,256]{3,2,1,0:T(8,128)(2,1)S(1)}, u32[]{:S(2)}, u32[]{:S(2)}) collective-permute-start(bf16[2,2,32,256]{3,2,1,0:T(8,128)(2,1)S(1)} %shard_map.94.rest_0_), channel_id=1, source_target_pairs={{0,8},{4,12},{8,0},{12,4},{1,9},{5,13},{9,1},{13,5},{2,10},{6,14},... | collective-permute-start | bytes 196616 | tf_op jit(solution)/shard_map/ppermute | solution.py:513
  126.8 1.9 %shard_map.95.rest_4_ = bf16[64,128,256]{2,1,0:T(8,128)(2,1)} custom-call(s32[1]{0:T(128)} %bitcast._.freq.place_ref, s32[1]{0:T(128)} %bitcast.1.rblk._, s32[1]{0:T(128)} %bitcast.2.__.sblk, bf16[64,128,256]{2,1,0:T(8,128)(2,1)S(1)} %copy-done.1, s32[128,256]{1,0:T(8,128)S(1)} %copy-done.4, bf16[4,128,128]{2,1,0:T(8,128)(2,1)S(1)} %copy-done.5, ...), custom_call_target="tpu_custom_call" | custom-call | flops 33554432 | bytes 8912896 | tf_op jit(solution)/shard_map/pallas_call | solution.py:89
  129.2 1.9 %shard_map.96 = bf16[64,128,256]{2,1,0:T(8,128)(2,1)} custom-call(s32[1]{0:T(128)} %bitcast._.freq.place_ref, s32[1]{0:T(128)} %bitcast.1.rblk._, s32[1]{0:T(128)} %bitcast.2.__.sblk, bf16[64,128,256]{2,1,0:T(8,128)(2,1)S(1)} %copy-done.1, s32[128,256]{1,0:T(8,128)S(1)} %copy-done.4, ...), custom_call_target="tpu_custom_call", output_to_operand_aliasing={{}: (10, {})} | custom-call | flops 33554432 | bytes 13107200 | tf_op jit(solution)/shard_map/pallas_call | solution.py:89
  (89 shorter events, 38.7 us)
Async XLA Ops:
  2.6 21.3 %collective-permute-start.6 = (bf16[2,256,512]{2,1,0:T(8,128)(2,1)S(1)}, bf16[2,256,512]{2,1,0:T(8,128)(2,1)S(1)}, u32[]{:S(2)}, u32[]{:S(2)}) collective-permute-start(bf16[2,256,512]{2,1,0:T(8,128)(2,1)S(1)} %get-tuple-element.66), channel_id=1, source_target_pairs={{0,2},{2,0},{1,3},{3,1},{4,6},{6,4},{5,7},{7,5},{8,10},{10,8},{9,1... | collective-permute-start | bytes 1572872 | tf_op jit(solution)/shard_map/ppermute | solution.py:513
  5.6 26.0 %collective-permute-start.7 = (bf16[2,256,512]{2,1,0:T(8,128)(2,1)S(1)}, bf16[2,256,512]{2,1,0:T(8,128)(2,1)S(1)}, u32[]{:S(2)}, u32[]{:S(2)}) collective-permute-start(bf16[2,256,512]{2,1,0:T(8,128)(2,1)S(1)} %get-tuple-element.69), channel_id=1, source_target_pairs={{0,2},{2,0},{1,3},{3,1},{4,6},{6,4},{5,7},{7,5},{8,10},{10,8},{9,1... | collective-permute-start | bytes 1572872 | tf_op jit(solution)/shard_map/ppermute | solution.py:513
  8.6 12.9 %collective-permute-start.3 = (bf16[2,2,64,256]{3,2,1,0:T(8,128)(2,1)S(1)}, bf16[2,2,64,256]{3,2,1,0:T(8,128)(2,1)S(1)}, u32[]{:S(2)}, u32[]{:S(2)}) collective-permute-start(bf16[2,2,64,256]{3,2,1,0:T(8,128)(2,1)S(1)} %get-tuple-element.59), channel_id=1, source_target_pairs={{0,8},{4,12},{8,0},{12,4},{1,9},{5,13},{9,1},{13,5},{2,10},{6,14},... | collective-permute-start | bytes 393224 | tf_op jit(solution)/shard_map/ppermute | solution.py:513
  11.7 9.8 %collective-permute-start.4 = (bf16[2,2,64,256]{3,2,1,0:T(8,128)(2,1)S(1)}, bf16[2,2,64,256]{3,2,1,0:T(8,128)(2,1)S(1)}, u32[]{:S(2)}, u32[]{:S(2)}) collective-permute-start(bf16[2,2,64,256]{3,2,1,0:T(8,128)(2,1)S(1)} %get-tuple-element.60), channel_id=1, source_target_pairs={{0,12},{4,8},{8,4},{12,0},{1,13},{5,9},{9,5},{13,1},{2,14},{6,10},... | collective-permute-start | bytes 393224 | tf_op jit(solution)/shard_map/ppermute | solution.py:513
  13.1 8.6 %collective-permute-start.5 = (bf16[2,2,64,256]{3,2,1,0:T(8,128)(2,1)S(1)}, bf16[2,2,64,256]{3,2,1,0:T(8,128)(2,1)S(1)}, u32[]{:S(2)}, u32[]{:S(2)}) collective-permute-start(bf16[2,2,64,256]{3,2,1,0:T(8,128)(2,1)S(1)} %get-tuple-element.61), channel_id=1, source_target_pairs={{0,4},{4,0},{8,12},{12,8},{1,5},{5,1},{9,13},{13,9},{2,6},{6,2},{1... | collective-permute-start | bytes 393224 | tf_op jit(solution)/shard_map/ppermute | solution.py:513
  21.8 9.8 %collective-permute-start.8 = (bf16[2,2,64,256]{3,2,1,0:T(8,128)(2,1)S(1)}, bf16[2,2,64,256]{3,2,1,0:T(8,128)(2,1)S(1)}, u32[]{:S(2)}, u32[]{:S(2)}) collective-permute-start(bf16[2,2,64,256]{3,2,1,0:T(8,128)(2,1)S(1)} %get-tuple-element.68.rest_0_), channel_id=1, source_target_pairs={{0,2},{2,0},{1,3},{3,1},{4,6},{6,4},{5,7},{7,5},{8,10},{10,8},{9,1... | collective-permute-start | bytes 393224 | tf_op jit(solution)/shard_map/ppermute | solution.py:513
  23.4 8.2 %collective-permute-start = (bf16[2,256,512]{2,1,0:T(8,128)(2,1)S(1)}, bf16[2,256,512]{2,1,0:T(8,128)(2,1)S(1)}, u32[]{:S(2)}, u32[]{:S(2)}) collective-permute-start(bf16[2,256,512]{2,1,0:T(8,128)(2,1)S(1)} %get-tuple-element.51.rest_1_.rest_0_.rest_2_), channel_id=1, source_target_pairs={{0,1},{1,0},{2,3},{3,2},{4,5},{5,4},{6,7},{7,6},{8,9},{9,8},{10,11... | collective-permute-start | bytes 1572872 | tf_op jit(solution)/shard_map/ppermute | solution.py:513
  23.4 8.2 %collective-permute-start.1 = (bf16[2,256,512]{2,1,0:T(8,128)(2,1)S(1)}, bf16[2,256,512]{2,1,0:T(8,128)(2,1)S(1)}, u32[]{:S(2)}, u32[]{:S(2)}) collective-permute-start(bf16[2,256,512]{2,1,0:T(8,128)(2,1)S(1)} %get-tuple-element.52.rest_3_.rest_2_.rest_4_), channel_id=1, source_target_pairs={{0,1},{1,0},{2,3},{3,2},{4,5},{5,4},{6,7},{7,6},{8,9},{9,8},{10,11... | collective-permute-start | bytes 1572872 | tf_op jit(solution)/shard_map/ppermute | solution.py:513
  23.9 8.5 %collective-permute-start.9 = (bf16[2,256,512]{2,1,0:T(8,128)(2,1)S(1)}, bf16[2,256,512]{2,1,0:T(8,128)(2,1)S(1)}, u32[]{:S(2)}, u32[]{:S(2)}) collective-permute-start(bf16[2,256,512]{2,1,0:T(8,128)(2,1)S(1)} %collective-permute-done.6.rest_2_.rest_0_.rest_3_), channel_id=1, source_target_pairs={{0,1},{1,0},{2,3},{3,2},{4,5},{5,4},{6,7},{7,6},{8,9},{9,8},{10,11... | collective-permute-start | bytes 1572872 | tf_op jit(solution)/shard_map/ppermute | solution.py:513
  34.0 7.1 %collective-permute-start.11 = (bf16[64,1024]{1,0:T(8,128)(2,1)S(1)}, bf16[64,1024]{1,0:T(8,128)(2,1)S(1)}, u32[]{:S(2)}, u32[]{:S(2)}) collective-permute-start(bf16[64,1024]{1,0:T(8,128)(2,1)S(1)} %get-tuple-element.74), channel_id=1, source_target_pairs={{0,4},{1,9},{4,0},{5,13},{8,12},{9,1},{12,8},{13,5},{2,6},{3,11},{... | collective-permute-start | bytes 393224 | tf_op jit(solution)/shard_map/ppermute | solution.py:526
  35.9 9.3 %collective-permute-start.12 = (bf16[64,1024]{1,0:T(8,128)(2,1)S(1)}, bf16[64,1024]{1,0:T(8,128)(2,1)S(1)}, u32[]{:S(2)}, u32[]{:S(2)}) collective-permute-start(bf16[64,1024]{1,0:T(8,128)(2,1)S(1)} %get-tuple-element.75), channel_id=1, source_target_pairs={{0,12},{1,13},{4,8},{5,9},{8,4},{9,5},{12,0},{13,1},{2,14},{3,15},... | collective-permute-start | bytes 393224 | tf_op jit(solution)/shard_map/ppermute | solution.py:526
  38.4 10.8 %collective-permute-start.13 = (bf16[64,1024]{1,0:T(8,128)(2,1)S(1)}, bf16[64,1024]{1,0:T(8,128)(2,1)S(1)}, u32[]{:S(2)}, u32[]{:S(2)}) collective-permute-start(bf16[64,1024]{1,0:T(8,128)(2,1)S(1)} %get-tuple-element.76), channel_id=1, source_target_pairs={{0,8},{1,5},{4,12},{5,1},{8,0},{9,13},{12,4},{13,9},{2,10},{3,7},{... | collective-permute-start | bytes 393224 | tf_op jit(solution)/shard_map/ppermute | solution.py:526
  50.2 6.9 %collective-permute-start.14 = (bf16[64,1024]{1,0:T(8,128)(2,1)S(1)}, bf16[64,1024]{1,0:T(8,128)(2,1)S(1)}, u32[]{:S(2)}, u32[]{:S(2)}) collective-permute-start(bf16[64,1024]{1,0:T(8,128)(2,1)S(1)} %get-tuple-element.78), channel_id=1, source_target_pairs={{0,4},{1,9},{4,0},{5,13},{8,12},{9,1},{12,8},{13,5},{2,6},{3,11},{... | collective-permute-start | bytes 393224 | tf_op jit(solution)/shard_map/ppermute | solution.py:526
  51.0 9.3 %collective-permute-start.15 = (bf16[64,1024]{1,0:T(8,128)(2,1)S(1)}, bf16[64,1024]{1,0:T(8,128)(2,1)S(1)}, u32[]{:S(2)}, u32[]{:S(2)}) collective-permute-start(bf16[64,1024]{1,0:T(8,128)(2,1)S(1)} %get-tuple-element.79), channel_id=1, source_target_pairs={{0,12},{1,13},{4,8},{5,9},{8,4},{9,5},{12,0},{13,1},{2,14},{3,15},... | collective-permute-start | bytes 393224 | tf_op jit(solution)/shard_map/ppermute | solution.py:526
  53.9 10.2 %collective-permute-start.16 = (bf16[64,1024]{1,0:T(8,128)(2,1)S(1)}, bf16[64,1024]{1,0:T(8,128)(2,1)S(1)}, u32[]{:S(2)}, u32[]{:S(2)}) collective-permute-start(bf16[64,1024]{1,0:T(8,128)(2,1)S(1)} %get-tuple-element.80), channel_id=1, source_target_pairs={{0,8},{1,5},{4,12},{5,1},{8,0},{9,13},{12,4},{13,9},{2,10},{3,7},{... | collective-permute-start | bytes 393224 | tf_op jit(solution)/shard_map/ppermute | solution.py:526
  64.5 4.3 %collective-permute-start.17 = (bf16[2,2,32,256]{3,2,1,0:T(8,128)(2,1)S(1)}, bf16[2,2,32,256]{3,2,1,0:T(8,128)(2,1)S(1)}, u32[]{:S(2)}, u32[]{:S(2)}) collective-permute-start(bf16[2,2,32,256]{3,2,1,0:T(8,128)(2,1)S(1)} %get-tuple-element.82), channel_id=1, source_target_pairs={{0,2},{2,0},{1,3},{3,1},{4,6},{6,4},{5,7},{7,5},{8,10},{10,8},{9,1... | collective-permute-start | bytes 196616 | tf_op jit(solution)/shard_map/ppermute | solution.py:513
  68.9 5.7 %collective-permute-start.18 = (bf16[2,2,32,256]{3,2,1,0:T(8,128)(2,1)S(1)}, bf16[2,2,32,256]{3,2,1,0:T(8,128)(2,1)S(1)}, u32[]{:S(2)}, u32[]{:S(2)}) collective-permute-start(bf16[2,2,32,256]{3,2,1,0:T(8,128)(2,1)S(1)} %shard_map.84.rest_0_), channel_id=1, source_target_pairs={{0,8},{4,12},{8,0},{12,4},{1,9},{5,13},{9,1},{13,5},{2,10},{6,14},... | collective-permute-start | bytes 196616 | tf_op jit(solution)/shard_map/ppermute | solution.py:513
  70.4 6.2 %collective-permute-start.22 = (bf16[2,2,32,256]{3,2,1,0:T(8,128)(2,1)S(1)}, bf16[2,2,32,256]{3,2,1,0:T(8,128)(2,1)S(1)}, u32[]{:S(2)}, u32[]{:S(2)}) collective-permute-start(bf16[2,2,32,256]{3,2,1,0:T(8,128)(2,1)S(1)} %shard_map.86.rest_0_), channel_id=1, source_target_pairs={{0,8},{4,12},{8,0},{12,4},{1,9},{5,13},{9,1},{13,5},{2,10},{6,14},... | collective-permute-start | bytes 196616 | tf_op jit(solution)/shard_map/ppermute | solution.py:513
  72.0 5.3 %collective-permute-start.20 = (bf16[2,2,32,256]{3,2,1,0:T(8,128)(2,1)S(1)}, bf16[2,2,32,256]{3,2,1,0:T(8,128)(2,1)S(1)}, u32[]{:S(2)}, u32[]{:S(2)}) collective-permute-start(bf16[2,2,32,256]{3,2,1,0:T(8,128)(2,1)S(1)} %shard_map.84.rest_0_), channel_id=1, source_target_pairs={{0,4},{4,0},{8,12},{12,8},{1,5},{5,1},{9,13},{13,9},{2,6},{6,2},{1... | collective-permute-start | bytes 196616 | tf_op jit(solution)/shard_map/ppermute | solution.py:513
  74.6 5.8 %collective-permute-start.24 = (bf16[2,2,32,256]{3,2,1,0:T(8,128)(2,1)S(1)}, bf16[2,2,32,256]{3,2,1,0:T(8,128)(2,1)S(1)}, u32[]{:S(2)}, u32[]{:S(2)}) collective-permute-start(bf16[2,2,32,256]{3,2,1,0:T(8,128)(2,1)S(1)} %shard_map.86.rest_0_), channel_id=1, source_target_pairs={{0,4},{4,0},{8,12},{12,8},{1,5},{5,1},{9,13},{13,9},{2,6},{6,2},{1... | collective-permute-start | bytes 196616 | tf_op jit(solution)/shard_map/ppermute | solution.py:513
  79.1 4.3 %collective-permute-start.25 = (bf16[2,2,32,256]{3,2,1,0:T(8,128)(2,1)S(1)}, bf16[2,2,32,256]{3,2,1,0:T(8,128)(2,1)S(1)}, u32[]{:S(2)}, u32[]{:S(2)}) collective-permute-start(bf16[2,2,32,256]{3,2,1,0:T(8,128)(2,1)S(1)} %shard_map.85.rest_0_), channel_id=1, source_target_pairs={{0,2},{2,0},{1,3},{3,1},{4,6},{6,4},{5,7},{7,5},{8,10},{10,8},{9,1... | collective-permute-start | bytes 196616 | tf_op jit(solution)/shard_map/ppermute | solution.py:513
  86.3 10.4 %collective-permute-start.27 = (bf16[64,1024]{1,0:T(8,128)(2,1)S(1)}, bf16[64,1024]{1,0:T(8,128)(2,1)S(1)}, u32[]{:S(2)}, u32[]{:S(2)}) collective-permute-start(bf16[64,1024]{1,0:T(8,128)(2,1)S(1)} %get-tuple-element.86), channel_id=1, source_target_pairs={{0,8},{4,12},{8,0},{12,4},{1,9},{5,13},{9,1},{13,5},{2,10},{6,14},... | collective-permute-start | bytes 393224 | tf_op jit(solution)/shard_map/ppermute | solution.py:513
  87.6 9.1 %collective-permute-start.28 = (bf16[64,1024]{1,0:T(8,128)(2,1)S(1)}, bf16[64,1024]{1,0:T(8,128)(2,1)S(1)}, u32[]{:S(2)}, u32[]{:S(2)}) collective-permute-start(bf16[64,1024]{1,0:T(8,128)(2,1)S(1)} %get-tuple-element.87), channel_id=1, source_target_pairs={{0,12},{4,8},{8,4},{12,0},{1,13},{5,9},{9,5},{13,1},{2,14},{6,10},... | collective-permute-start | bytes 393224 | tf_op jit(solution)/shard_map/ppermute | solution.py:513
  89.5 10.2 %collective-permute-start.29 = (bf16[64,1024]{1,0:T(8,128)(2,1)S(1)}, bf16[64,1024]{1,0:T(8,128)(2,1)S(1)}, u32[]{:S(2)}, u32[]{:S(2)}) collective-permute-start(bf16[64,1024]{1,0:T(8,128)(2,1)S(1)} %get-tuple-element.88), channel_id=1, source_target_pairs={{0,4},{4,0},{8,12},{12,8},{1,5},{5,1},{9,13},{13,9},{2,6},{6,2},{1... | collective-permute-start | bytes 393224 | tf_op jit(solution)/shard_map/ppermute | solution.py:513
  100.6 5.9 %collective-permute-start.30 = (bf16[64,1024]{1,0:T(8,128)(2,1)S(1)}, bf16[64,1024]{1,0:T(8,128)(2,1)S(1)}, u32[]{:S(2)}, u32[]{:S(2)}) collective-permute-start(bf16[64,1024]{1,0:T(8,128)(2,1)S(1)} %get-tuple-element.90), channel_id=1, source_target_pairs={{0,8},{4,12},{8,0},{12,4},{1,9},{5,13},{9,1},{13,5},{2,10},{6,14},... | collective-permute-start | bytes 393224 | tf_op jit(solution)/shard_map/ppermute | solution.py:513
  102.9 7.3 %collective-permute-start.31 = (bf16[64,1024]{1,0:T(8,128)(2,1)S(1)}, bf16[64,1024]{1,0:T(8,128)(2,1)S(1)}, u32[]{:S(2)}, u32[]{:S(2)}) collective-permute-start(bf16[64,1024]{1,0:T(8,128)(2,1)S(1)} %get-tuple-element.91), channel_id=1, source_target_pairs={{0,12},{4,8},{8,4},{12,0},{1,13},{5,9},{9,5},{13,1},{2,14},{6,10},... | collective-permute-start | bytes 393224 | tf_op jit(solution)/shard_map/ppermute | solution.py:513
  105.2 7.3 %collective-permute-start.32 = (bf16[64,1024]{1,0:T(8,128)(2,1)S(1)}, bf16[64,1024]{1,0:T(8,128)(2,1)S(1)}, u32[]{:S(2)}, u32[]{:S(2)}) collective-permute-start(bf16[64,1024]{1,0:T(8,128)(2,1)S(1)} %get-tuple-element.92), channel_id=1, source_target_pairs={{0,4},{4,0},{8,12},{12,8},{1,5},{5,1},{9,13},{13,9},{2,6},{6,2},{1... | collective-permute-start | bytes 393224 | tf_op jit(solution)/shard_map/ppermute | solution.py:513
  112.9 4.3 %collective-permute-start.37 = (bf16[2,2,32,256]{3,2,1,0:T(8,128)(2,1)S(1)}, bf16[2,2,32,256]{3,2,1,0:T(8,128)(2,1)S(1)}, u32[]{:S(2)}, u32[]{:S(2)}) collective-permute-start(bf16[2,2,32,256]{3,2,1,0:T(8,128)(2,1)S(1)} %get-tuple-element.96), channel_id=1, source_target_pairs={{0,2},{2,0},{1,3},{3,1},{4,6},{6,4},{5,7},{7,5},{8,10},{10,8},{9,1... | collective-permute-start | bytes 196616 | tf_op jit(solution)/shard_map/ppermute | solution.py:513
  117.3 5.2 %collective-permute-start.38 = (bf16[2,2,32,256]{3,2,1,0:T(8,128)(2,1)S(1)}, bf16[2,2,32,256]{3,2,1,0:T(8,128)(2,1)S(1)}, u32[]{:S(2)}, u32[]{:S(2)}) collective-permute-start(bf16[2,2,32,256]{3,2,1,0:T(8,128)(2,1)S(1)} %shard_map.94.rest_0_), channel_id=1, source_target_pairs={{0,8},{4,12},{8,0},{12,4},{1,9},{5,13},{9,1},{13,5},{2,10},{6,14},... | collective-permute-start | bytes 196616 | tf_op jit(solution)/shard_map/ppermute | solution.py:513
  118.9 6.0 %collective-permute-start.34 = (bf16[2,2,32,256]{3,2,1,0:T(8,128)(2,1)S(1)}, bf16[2,2,32,256]{3,2,1,0:T(8,128)(2,1)S(1)}, u32[]{:S(2)}, u32[]{:S(2)}) collective-permute-start(bf16[2,2,32,256]{3,2,1,0:T(8,128)(2,1)S(1)} %shard_map.93.rest_0_), channel_id=1, source_target_pairs={{0,8},{4,12},{8,0},{12,4},{1,9},{5,13},{9,1},{13,5},{2,10},{6,14},... | collective-permute-start | bytes 196616 | tf_op jit(solution)/shard_map/ppermute | solution.py:513
  120.5 5.5 %collective-permute-start.40 = (bf16[2,2,32,256]{3,2,1,0:T(8,128)(2,1)S(1)}, bf16[2,2,32,256]{3,2,1,0:T(8,128)(2,1)S(1)}, u32[]{:S(2)}, u32[]{:S(2)}) collective-permute-start(bf16[2,2,32,256]{3,2,1,0:T(8,128)(2,1)S(1)} %shard_map.94.rest_0_), channel_id=1, source_target_pairs={{0,4},{4,0},{8,12},{12,8},{1,5},{5,1},{9,13},{13,9},{2,6},{6,2},{1... | collective-permute-start | bytes 196616 | tf_op jit(solution)/shard_map/ppermute | solution.py:513
  123.9 4.8 %collective-permute-start.36 = (bf16[2,2,32,256]{3,2,1,0:T(8,128)(2,1)S(1)}, bf16[2,2,32,256]{3,2,1,0:T(8,128)(2,1)S(1)}, u32[]{:S(2)}, u32[]{:S(2)}) collective-permute-start(bf16[2,2,32,256]{3,2,1,0:T(8,128)(2,1)S(1)} %shard_map.93.rest_0_), channel_id=1, source_target_pairs={{0,4},{4,0},{8,12},{12,8},{1,5},{5,1},{9,13},{13,9},{2,6},{6,2},{1... | collective-permute-start | bytes 196616 | tf_op jit(solution)/shard_map/ppermute | solution.py:513
  (16 other events, 175.1 us)

commit v21 on v20

--- a/solution.py
+++ b/solution.py
@@ -28,7 +28,7 @@
 
 def slot_ways(count):
     lead = ways(count)
-    return [[0] + lead[:0:-1], lead]
+    return [lead, [0] + lead[:0:-1]]
 
 
 def way_of(slot, core, count):
@@ -285,7 +285,7 @@
                     held[:, :, :, to] = held_ref[:, :, :, to]
         if freq_devs:
             for slot, out in enumerate(outs[:freq_devs]):
-                way = way_of(slot, sblk[0] if by_core else 1, freq_devs)
+                way = way_of(slot, sblk[0] if by_core else 0, freq_devs)
                 start = pl.multiple_of((freq[0] ^ way) * share, share)
                 out[...] = held[:, :, pl.ds(start, share), :].reshape(out.shape).astype(BF16)
 
@@ -339,11 +339,11 @@
 
     def body(freq, _, sblk, c_ref, s_ref, f_ref, g_ref, *rest):
         refs, outs = rest[:freq_devs], rest[freq_devs:]
-        matrix_here = g_ref[freq[0] * 2 + (sblk[0] if by_core else 1)]
+        matrix_here = g_ref[freq[0] * 2 + (sblk[0] if by_core else 0)]
         spots = list(range(freq_devs))
         if not by_core:
             first, second = slot_ways(freq_devs)
-            spots = [first.index(way) + sblk[0] * (slot - first.index(way)) for slot, way in enumerate(second)]
+            spots = [slot + sblk[0] * (second.index(way) - slot) for slot, way in enumerate(first)]
 
         def one(at):
             data = [ref[:, at].astype(F32).reshape(2, per_dev, share, BLOCK) for ref in refs]
@@ -386,7 +386,7 @@
         resp, refs = rest[: len(flat)], rest[len(flat) : len(flat) + freq_devs]
         outs, held = rest[len(flat) + freq_devs : -1], rest[-1]
         for slot, ref in enumerate(refs):
-            way = way_of(slot, sblk[0] if by_core else 1, freq_devs)
+            way = way_of(slot, sblk[0] if by_core else 0, freq_devs)
             start = pl.multiple_of((freq[0] ^ way) * share, share)
             value = ref[...].reshape(2, per_dev, share, total_width)
             for part in range(2):
@@ -426,7 +426,7 @@
 
     def body(place_ref, u_ref, c_ref, s_ref, f_ref, g_ref, *rest):
         refs, out = rest[:freq_devs], rest[freq_devs]
-        matrix_here = g_ref[place_ref[0] * 2 + 1, :own]
+        matrix_here = g_ref[place_ref[0] * 2, :own]
 
         def one(at):
             for base in range(0, rows, 2 * ROWS):
@@ -574,7 +574,7 @@
         if at:
             held = down_products(held, far, parts[:at], 1, 0, places)
         first = at * 2 * kept[0].shape[1]
-        by_core = step == 0
+        by_core = step > 0
         deal = dealt_by_core if by_core else dealt_out
         messages = deal(down_products(held, far, parts[at:], 1, first, places, freq_devs, by_core))
         messages = deal(windowed(messages, src_tables, matrix, places, per_dev, share, by_core))

time: 131 us -> 132 us (level)
  starting transfers between devices: 46.5 us -> 51.2 us
  waiting for transfers between devices: 65.6 us -> 61.7 us
    ppermute x35, starting transfers between devices: 37.8 us -> 43.9 us  [exchanged(): lax.ppermute(value, axis, [(i, i ^ step) for i in range(lax.axis_size(axi...]
    ppermute x6, waiting for transfers between devices: 17.7 us -> 15.7 us  [dealt_by_core(): out.append(lax.ppermute(parts[slot], ('freq', 'sblk'), pairs))]
    ppermute x35, waiting for transfers between devices: 47.9 us -> 46 us  [exchanged(): lax.ppermute(value, axis, [(i, i ^ step) for i in range(lax.axis_size(axi...]
    ppermute x6, starting transfers between devices: 8.66 us -> 7.31 us  [dealt_by_core(): out.append(lax.ppermute(parts[slot], ('freq', 'sblk'), pairs))]
  transfers between devices with their start and end apart: 41 -> 41, of which waited for: 27 -> 21; matrix products, arithmetic and copies ran while one was open for 0% -> 0% of each run, Pallas kernels for 6% -> 6%
where the time goes in v21:
time: 132 us
  waiting for transfers between devices  61.7 us (47%)
  starting transfers between devices  51.2 us (39%)
  Pallas kernels  14.2 us (11%)
  local copies, waits for them, and re-layouts  4.56 us (3%)
    ppermute x35, waiting for transfers between devices, exchanged(): lax.ppermute(value, axis, [(i, i ^ step) for i in range(lax.axis_size(axi...  46 us
    ppermute x35, starting transfers between devices, exchanged(): lax.ppermute(value, axis, [(i, i ^ step) for i in range(lax.axis_size(axi...  43.9 us
    ppermute x6, waiting for transfers between devices, dealt_by_core(): out.append(lax.ppermute(parts[slot], ('freq', 'sblk'), pairs))  15.7 us
    pallas_call x24, Pallas kernels, call(): pl.pallas_call(body, grid_spec=pltpu.PrefetchScalarGridSpec(num_scalar_pr...  14.2 us
    ppermute x6, starting transfers between devices, dealt_by_core(): out.append(lax.ppermute(parts[slot], ('freq', 'sblk'), pairs))  7.31 us
    unnamed x15, local copies, waits for them, and re-layouts  4.56 us
  transfers between devices with their start and end apart: 41, of which 21 were waited for; matrix products, arithmetic and copies ran while one was open for 0% of the time, Pallas kernels for 6%

profile of v21, /device:TPU:0, one launch (start us, length us, event | category | flops | bytes accessed | tf_op | source)
XLA Modules:
  0.0 131.9 jit_solution(350003570641446734)
XLA Ops:
  0.8 1.6 %copy-done.3 = bf16[2,2,1024,256]{3,2,1,0:T(8,128)(2,1)S(1)} copy-done((bf16[2,2,1024,256]{3,2,1,0:T(8,128)(2,1)S(1)}, bf16[2,2,1024,256]{3,2,1,0:T(8,128)(2,1)}, u32[]{:S(2)}) %copy-start.3) | copy-done | bytes 2097176
  2.6 3.0 %collective-permute-start.6 = (bf16[2,256,512]{2,1,0:T(8,128)(2,1)S(1)}, bf16[2,256,512]{2,1,0:T(8,128)(2,1)S(1)}, u32[]{:S(2)}, u32[]{:S(2)}) collective-permute-start(bf16[2,256,512]{2,1,0:T(8,128)(2,1)S(1)} %get-tuple-element.66), channel_id=1, source_target_pairs={{0,2},{2,0},{1,3},{3,1},{4,6},{6,4},{5,7},{7,5},{8,10},{10,8},{9,1... | collective-permute-start | bytes 1572872 | tf_op jit(solution)/shard_map/ppermute | solution.py:513
  5.7 2.2 %copy-done = bf16[64,128,256]{2,1,0:T(8,128)(2,1)S(1)} copy-done((bf16[64,128,256]{2,1,0:T(8,128)(2,1)S(1)}, bf16[64,128,256]{2,1,0:T(8,128)(2,1)}, u32[]{:S(2)}) %copy-start) | copy-done | bytes 4194328
  8.6 3.1 %collective-permute-start.3 = (bf16[2,2,64,256]{3,2,1,0:T(8,128)(2,1)S(1)}, bf16[2,2,64,256]{3,2,1,0:T(8,128)(2,1)S(1)}, u32[]{:S(2)}, u32[]{:S(2)}) collective-permute-start(bf16[2,2,64,256]{3,2,1,0:T(8,128)(2,1)S(1)} %get-tuple-element.59), channel_id=1, source_target_pairs={{0,8},{4,12},{8,0},{12,4},{1,9},{5,13},{9,1},{13,5},{2,10},{6,14},... | collective-permute-start | bytes 393224 | tf_op jit(solution)/shard_map/ppermute | solution.py:513
  13.3 8.2 %collective-permute-done.3.refs_1_ = bf16[2,2,64,256]{3,2,1,0:T(8,128)(2,1)S(1)} collective-permute-done((bf16[2,2,64,256]{3,2,1,0:T(8,128)(2,1)S(1)}, bf16[2,2,64,256]{3,2,1,0:T(8,128)(2,1)S(1)}, u32[]{:S(2)}, u32[]{:S(2)}) %collective-permute-start.3) | collective-permute-done | bytes 131104 | tf_op jit(solution)/shard_map/ppermute | solution.py:513
  21.8 1.6 %collective-permute-start.8 = (bf16[2,2,64,256]{3,2,1,0:T(8,128)(2,1)S(1)}, bf16[2,2,64,256]{3,2,1,0:T(8,128)(2,1)S(1)}, u32[]{:S(2)}, u32[]{:S(2)}) collective-permute-start(bf16[2,2,64,256]{3,2,1,0:T(8,128)(2,1)S(1)} %get-tuple-element.68.rest_0_), channel_id=1, source_target_pairs={{0,2},{2,0},{1,3},{3,1},{4,6},{6,4},{5,7},{7,5},{8,10},{10,8},{9,1... | collective-permute-start | bytes 393224 | tf_op jit(solution)/shard_map/ppermute | solution.py:513
  24.0 7.6 %collective-permute-done.8.rest_1_ = bf16[2,2,64,256]{3,2,1,0:T(8,128)(2,1)S(1)} collective-permute-done((bf16[2,2,64,256]{3,2,1,0:T(8,128)(2,1)S(1)}, bf16[2,2,64,256]{3,2,1,0:T(8,128)(2,1)S(1)}, u32[]{:S(2)}, u32[]{:S(2)}) %collective-permute-start.8) | collective-permute-done | bytes 131104 | tf_op jit(solution)/shard_map/ppermute | solution.py:513
  34.0 2.9 %collective-permute-start.11 = (bf16[64,1024]{1,0:T(8,128)(2,1)S(1)}, bf16[64,1024]{1,0:T(8,128)(2,1)S(1)}, u32[]{:S(2)}, u32[]{:S(2)}) collective-permute-start(bf16[64,1024]{1,0:T(8,128)(2,1)S(1)} %get-tuple-element.74), channel_id=1, source_target_pairs={{0,8},{4,12},{8,0},{12,4},{1,9},{5,13},{9,1},{13,5},{2,10},{6,14},... | collective-permute-start | bytes 393224 | tf_op jit(solution)/shard_map/ppermute | solution.py:513
  36.9 1.3 %collective-permute-start.12 = (bf16[64,1024]{1,0:T(8,128)(2,1)S(1)}, bf16[64,1024]{1,0:T(8,128)(2,1)S(1)}, u32[]{:S(2)}, u32[]{:S(2)}) collective-permute-start(bf16[64,1024]{1,0:T(8,128)(2,1)S(1)} %get-tuple-element.75), channel_id=1, source_target_pairs={{0,12},{4,8},{8,4},{12,0},{1,13},{5,9},{9,5},{13,1},{2,14},{6,10},... | collective-permute-start | bytes 393224 | tf_op jit(solution)/shard_map/ppermute | solution.py:513
  41.1 5.8 %collective-permute-done.11.rest_1_ = bf16[64,1024]{1,0:T(8,128)(2,1)S(1)} collective-permute-done((bf16[64,1024]{1,0:T(8,128)(2,1)S(1)}, bf16[64,1024]{1,0:T(8,128)(2,1)S(1)}, u32[]{:S(2)}, u32[]{:S(2)}) %collective-permute-start.11) | collective-permute-done | bytes 131104 | tf_op jit(solution)/shard_map/ppermute | solution.py:513
  48.7 4.2 %collective-permute-start.14 = (bf16[64,1024]{1,0:T(8,128)(2,1)S(1)}, bf16[64,1024]{1,0:T(8,128)(2,1)S(1)}, u32[]{:S(2)}, u32[]{:S(2)}) collective-permute-start(bf16[64,1024]{1,0:T(8,128)(2,1)S(1)} %get-tuple-element.78), channel_id=1, source_target_pairs={{0,8},{4,12},{8,0},{12,4},{1,9},{5,13},{9,1},{13,5},{2,10},{6,14},... | collective-permute-start | bytes 393224 | tf_op jit(solution)/shard_map/ppermute | solution.py:513
  53.5 9.0 %collective-permute-done.14.rest_5_ = bf16[64,1024]{1,0:T(8,128)(2,1)S(1)} collective-permute-done((bf16[64,1024]{1,0:T(8,128)(2,1)S(1)}, bf16[64,1024]{1,0:T(8,128)(2,1)S(1)}, u32[]{:S(2)}, u32[]{:S(2)}) %collective-permute-start.14) | collective-permute-done | bytes 131104 | tf_op jit(solution)/shard_map/ppermute | solution.py:513
  64.1 1.6 %collective-permute-start.17 = (bf16[2,2,32,256]{3,2,1,0:T(8,128)(2,1)S(1)}, bf16[2,2,32,256]{3,2,1,0:T(8,128)(2,1)S(1)}, u32[]{:S(2)}, u32[]{:S(2)}) collective-permute-start(bf16[2,2,32,256]{3,2,1,0:T(8,128)(2,1)S(1)} %get-tuple-element.82), channel_id=1, source_target_pairs={{0,2},{2,0},{1,3},{3,1},{4,6},{6,4},{5,7},{7,5},{8,10},{10,8},{9,1... | collective-permute-start | bytes 196616 | tf_op jit(solution)/shard_map/ppermute | solution.py:513
  66.7 1.8 %collective-permute-done.17.r_ref = bf16[2,2,32,256]{3,2,1,0:T(8,128)(2,1)S(1)} collective-permute-done((bf16[2,2,32,256]{3,2,1,0:T(8,128)(2,1)S(1)}, bf16[2,2,32,256]{3,2,1,0:T(8,128)(2,1)S(1)}, u32[]{:S(2)}, u32[]{:S(2)}) %collective-permute-start.17) | collective-permute-done | bytes 65568 | tf_op jit(solution)/shard_map/ppermute | solution.py:513
  68.4 1.9 %collective-permute-start.18 = (bf16[2,2,32,256]{3,2,1,0:T(8,128)(2,1)S(1)}, bf16[2,2,32,256]{3,2,1,0:T(8,128)(2,1)S(1)}, u32[]{:S(2)}, u32[]{:S(2)}) collective-permute-start(bf16[2,2,32,256]{3,2,1,0:T(8,128)(2,1)S(1)} %shard_map.84.rest_0_), channel_id=1, source_target_pairs={{0,8},{4,12},{8,0},{12,4},{1,9},{5,13},{9,1},{13,5},{2,10},{6,14},... | collective-permute-start | bytes 196616 | tf_op jit(solution)/shard_map/ppermute | solution.py:513
  70.4 1.5 %collective-permute-start.22 = (bf16[2,2,32,256]{3,2,1,0:T(8,128)(2,1)S(1)}, bf16[2,2,32,256]{3,2,1,0:T(8,128)(2,1)S(1)}, u32[]{:S(2)}, u32[]{:S(2)}) collective-permute-start(bf16[2,2,32,256]{3,2,1,0:T(8,128)(2,1)S(1)} %shard_map.86.rest_0_), channel_id=1, source_target_pairs={{0,8},{4,12},{8,0},{12,4},{1,9},{5,13},{9,1},{13,5},{2,10},{6,14},... | collective-permute-start | bytes 196616 | tf_op jit(solution)/shard_map/ppermute | solution.py:513
  71.9 2.3 %collective-permute-start.20 = (bf16[2,2,32,256]{3,2,1,0:T(8,128)(2,1)S(1)}, bf16[2,2,32,256]{3,2,1,0:T(8,128)(2,1)S(1)}, u32[]{:S(2)}, u32[]{:S(2)}) collective-permute-start(bf16[2,2,32,256]{3,2,1,0:T(8,128)(2,1)S(1)} %shard_map.84.rest_0_), channel_id=1, source_target_pairs={{0,4},{4,0},{8,12},{12,8},{1,5},{5,1},{9,13},{13,9},{2,6},{6,2},{1... | collective-permute-start | bytes 196616 | tf_op jit(solution)/shard_map/ppermute | solution.py:513
  74.1 2.8 %collective-permute-start.19 = (bf16[2,2,32,256]{3,2,1,0:T(8,128)(2,1)S(1)}, bf16[2,2,32,256]{3,2,1,0:T(8,128)(2,1)S(1)}, u32[]{:S(2)}, u32[]{:S(2)}) collective-permute-start(bf16[2,2,32,256]{3,2,1,0:T(8,128)(2,1)S(1)} %collective-permute-done.18.rest_1_), channel_id=1, source_target_pairs={{0,4},{4,0},{8,12},{12,8},{1,5},{5,1},{9,13},{13,9},{2,6},{6,2},{1... | collective-permute-start | bytes 196616 | tf_op jit(solution)/shard_map/ppermute | solution.py:513
  77.0 2.0 %collective-permute-start.23 = (bf16[2,2,32,256]{3,2,1,0:T(8,128)(2,1)S(1)}, bf16[2,2,32,256]{3,2,1,0:T(8,128)(2,1)S(1)}, u32[]{:S(2)}, u32[]{:S(2)}) collective-permute-start(bf16[2,2,32,256]{3,2,1,0:T(8,128)(2,1)S(1)} %collective-permute-done.22.rest_1_), channel_id=1, source_target_pairs={{0,4},{4,0},{8,12},{12,8},{1,5},{5,1},{9,13},{13,9},{2,6},{6,2},{1... | collective-permute-start | bytes 196616 | tf_op jit(solution)/shard_map/ppermute | solution.py:513
  84.1 2.5 %collective-permute-done.26.rest_2_ = bf16[2,2,32,256]{3,2,1,0:T(8,128)(2,1)S(1)} collective-permute-done((bf16[2,2,32,256]{3,2,1,0:T(8,128)(2,1)S(1)}, bf16[2,2,32,256]{3,2,1,0:T(8,128)(2,1)S(1)}, u32[]{:S(2)}, u32[]{:S(2)}) %collective-permute-start.26) | collective-permute-done | bytes 65568 | tf_op jit(solution)/shard_map/ppermute | solution.py:513
  88.2 3.0 %collective-permute-start.28 = (bf16[64,1024]{1,0:T(8,128)(2,1)S(1)}, bf16[64,1024]{1,0:T(8,128)(2,1)S(1)}, u32[]{:S(2)}, u32[]{:S(2)}) collective-permute-start(bf16[64,1024]{1,0:T(8,128)(2,1)S(1)} %get-tuple-element.87), channel_id=1, source_target_pairs={{0,12},{1,13},{4,8},{5,9},{8,4},{9,5},{12,0},{13,1},{2,14},{3,15},... | collective-permute-start | bytes 393224 | tf_op jit(solution)/shard_map/ppermute | solution.py:526
  91.2 6.2 %collective-permute-done.27.rest_1_ = bf16[64,1024]{1,0:T(8,128)(2,1)S(1)} collective-permute-done((bf16[64,1024]{1,0:T(8,128)(2,1)S(1)}, bf16[64,1024]{1,0:T(8,128)(2,1)S(1)}, u32[]{:S(2)}, u32[]{:S(2)}) %collective-permute-start.27) | collective-permute-done | bytes 131104 | tf_op jit(solution)/shard_map/ppermute | solution.py:526
  100.6 2.2 %collective-permute-start.31 = (bf16[64,1024]{1,0:T(8,128)(2,1)S(1)}, bf16[64,1024]{1,0:T(8,128)(2,1)S(1)}, u32[]{:S(2)}, u32[]{:S(2)}) collective-permute-start(bf16[64,1024]{1,0:T(8,128)(2,1)S(1)} %get-tuple-element.91), channel_id=1, source_target_pairs={{0,12},{1,13},{4,8},{5,9},{8,4},{9,5},{12,0},{13,1},{2,14},{3,15},... | collective-permute-start | bytes 393224 | tf_op jit(solution)/shard_map/ppermute | solution.py:526
  103.3 8.1 %collective-permute-done.30.rest_5_ = bf16[64,1024]{1,0:T(8,128)(2,1)S(1)} collective-permute-done((bf16[64,1024]{1,0:T(8,128)(2,1)S(1)}, bf16[64,1024]{1,0:T(8,128)(2,1)S(1)}, u32[]{:S(2)}, u32[]{:S(2)}) %collective-permute-start.30) | collective-permute-done | bytes 131104 | tf_op jit(solution)/shard_map/ppermute | solution.py:526
  114.5 2.5 %collective-permute-done.37.r_ref = bf16[2,2,32,256]{3,2,1,0:T(8,128)(2,1)S(1)} collective-permute-done((bf16[2,2,32,256]{3,2,1,0:T(8,128)(2,1)S(1)}, bf16[2,2,32,256]{3,2,1,0:T(8,128)(2,1)S(1)}, u32[]{:S(2)}, u32[]{:S(2)}) %collective-permute-start.37) | collective-permute-done | bytes 65568 | tf_op jit(solution)/shard_map/ppermute | solution.py:513
  117.0 1.6 %collective-permute-start.38 = (bf16[2,2,32,256]{3,2,1,0:T(8,128)(2,1)S(1)}, bf16[2,2,32,256]{3,2,1,0:T(8,128)(2,1)S(1)}, u32[]{:S(2)}, u32[]{:S(2)}) collective-permute-start(bf16[2,2,32,256]{3,2,1,0:T(8,128)(2,1)S(1)} %shard_map.94.rest_0_), channel_id=1, source_target_pairs={{0,8},{4,12},{8,0},{12,4},{1,9},{5,13},{9,1},{13,5},{2,10},{6,14},... | collective-permute-start | bytes 196616 | tf_op jit(solution)/shard_map/ppermute | solution.py:513
  118.6 1.5 %collective-permute-start.34 = (bf16[2,2,32,256]{3,2,1,0:T(8,128)(2,1)S(1)}, bf16[2,2,32,256]{3,2,1,0:T(8,128)(2,1)S(1)}, u32[]{:S(2)}, u32[]{:S(2)}) collective-permute-start(bf16[2,2,32,256]{3,2,1,0:T(8,128)(2,1)S(1)} %shard_map.93.rest_0_), channel_id=1, source_target_pairs={{0,8},{4,12},{8,0},{12,4},{1,9},{5,13},{9,1},{13,5},{2,10},{6,14},... | collective-permute-start | bytes 196616 | tf_op jit(solution)/shard_map/ppermute | solution.py:513
  120.1 1.7 %collective-permute-start.40 = (bf16[2,2,32,256]{3,2,1,0:T(8,128)(2,1)S(1)}, bf16[2,2,32,256]{3,2,1,0:T(8,128)(2,1)S(1)}, u32[]{:S(2)}, u32[]{:S(2)}) collective-permute-start(bf16[2,2,32,256]{3,2,1,0:T(8,128)(2,1)S(1)} %shard_map.94.rest_0_), channel_id=1, source_target_pairs={{0,4},{4,0},{8,12},{12,8},{1,5},{5,1},{9,13},{13,9},{2,6},{6,2},{1... | collective-permute-start | bytes 196616 | tf_op jit(solution)/shard_map/ppermute | solution.py:513
  121.7 1.7 %collective-permute-done.38.rest_1_ = bf16[2,2,32,256]{3,2,1,0:T(8,128)(2,1)S(1)} collective-permute-done((bf16[2,2,32,256]{3,2,1,0:T(8,128)(2,1)S(1)}, bf16[2,2,32,256]{3,2,1,0:T(8,128)(2,1)S(1)}, u32[]{:S(2)}, u32[]{:S(2)}) %collective-permute-start.38) | collective-permute-done | bytes 65568 | tf_op jit(solution)/shard_map/ppermute | solution.py:513
  126.4 1.6 %collective-permute-done.39.rest_2_ = bf16[2,2,32,256]{3,2,1,0:T(8,128)(2,1)S(1)} collective-permute-done((bf16[2,2,32,256]{3,2,1,0:T(8,128)(2,1)S(1)}, bf16[2,2,32,256]{3,2,1,0:T(8,128)(2,1)S(1)}, u32[]{:S(2)}, u32[]{:S(2)}) %collective-permute-start.39) | collective-permute-done | bytes 65568 | tf_op jit(solution)/shard_map/ppermute | solution.py:513
  128.0 1.9 %shard_map.95.rest_4_ = bf16[64,128,256]{2,1,0:T(8,128)(2,1)} custom-call(s32[1]{0:T(128)} %bitcast._.freq.place_ref, s32[1]{0:T(128)} %bitcast.1.rblk._, s32[1]{0:T(128)} %bitcast.2.__.sblk, bf16[64,128,256]{2,1,0:T(8,128)(2,1)S(1)} %copy-done.1, s32[128,256]{1,0:T(8,128)S(1)} %copy-done.4, bf16[4,128,128]{2,1,0:T(8,128)(2,1)S(1)} %copy-done.5, ...), custom_call_target="tpu_custom_call" | custom-call | flops 33554432 | bytes 8912896 | tf_op jit(solution)/shard_map/pallas_call | solution.py:89
  129.9 1.9 %shard_map.96 = bf16[64,128,256]{2,1,0:T(8,128)(2,1)} custom-call(s32[1]{0:T(128)} %bitcast._.freq.place_ref, s32[1]{0:T(128)} %bitcast.1.rblk._, s32[1]{0:T(128)} %bitcast.2.__.sblk, bf16[64,128,256]{2,1,0:T(8,128)(2,1)S(1)} %copy-done.1, s32[128,256]{1,0:T(8,128)S(1)} %copy-done.4, ...), custom_call_target="tpu_custom_call", output_to_operand_aliasing={{}: (10, {})} | custom-call | flops 33554432 | bytes 13107200 | tf_op jit(solution)/shard_map/pallas_call | solution.py:89
  (89 shorter events, 31.0 us)
Async XLA Ops:
  2.6 21.3 %collective-permute-start.6 = (bf16[2,256,512]{2,1,0:T(8,128)(2,1)S(1)}, bf16[2,256,512]{2,1,0:T(8,128)(2,1)S(1)}, u32[]{:S(2)}, u32[]{:S(2)}) collective-permute-start(bf16[2,256,512]{2,1,0:T(8,128)(2,1)S(1)} %get-tuple-element.66), channel_id=1, source_target_pairs={{0,2},{2,0},{1,3},{3,1},{4,6},{6,4},{5,7},{7,5},{8,10},{10,8},{9,1... | collective-permute-start | bytes 1572872 | tf_op jit(solution)/shard_map/ppermute | solution.py:513
  5.6 26.0 %collective-permute-start.7 = (bf16[2,256,512]{2,1,0:T(8,128)(2,1)S(1)}, bf16[2,256,512]{2,1,0:T(8,128)(2,1)S(1)}, u32[]{:S(2)}, u32[]{:S(2)}) collective-permute-start(bf16[2,256,512]{2,1,0:T(8,128)(2,1)S(1)} %get-tuple-element.69), channel_id=1, source_target_pairs={{0,2},{2,0},{1,3},{3,1},{4,6},{6,4},{5,7},{7,5},{8,10},{10,8},{9,1... | collective-permute-start | bytes 1572872 | tf_op jit(solution)/shard_map/ppermute | solution.py:513
  8.6 12.9 %collective-permute-start.3 = (bf16[2,2,64,256]{3,2,1,0:T(8,128)(2,1)S(1)}, bf16[2,2,64,256]{3,2,1,0:T(8,128)(2,1)S(1)}, u32[]{:S(2)}, u32[]{:S(2)}) collective-permute-start(bf16[2,2,64,256]{3,2,1,0:T(8,128)(2,1)S(1)} %get-tuple-element.59), channel_id=1, source_target_pairs={{0,8},{4,12},{8,0},{12,4},{1,9},{5,13},{9,1},{13,5},{2,10},{6,14},... | collective-permute-start | bytes 393224 | tf_op jit(solution)/shard_map/ppermute | solution.py:513
  11.7 9.8 %collective-permute-start.4 = (bf16[2,2,64,256]{3,2,1,0:T(8,128)(2,1)S(1)}, bf16[2,2,64,256]{3,2,1,0:T(8,128)(2,1)S(1)}, u32[]{:S(2)}, u32[]{:S(2)}) collective-permute-start(bf16[2,2,64,256]{3,2,1,0:T(8,128)(2,1)S(1)} %get-tuple-element.60), channel_id=1, source_target_pairs={{0,12},{4,8},{8,4},{12,0},{1,13},{5,9},{9,5},{13,1},{2,14},{6,10},... | collective-permute-start | bytes 393224 | tf_op jit(solution)/shard_map/ppermute | solution.py:513
  13.1 8.6 %collective-permute-start.5 = (bf16[2,2,64,256]{3,2,1,0:T(8,128)(2,1)S(1)}, bf16[2,2,64,256]{3,2,1,0:T(8,128)(2,1)S(1)}, u32[]{:S(2)}, u32[]{:S(2)}) collective-permute-start(bf16[2,2,64,256]{3,2,1,0:T(8,128)(2,1)S(1)} %get-tuple-element.61), channel_id=1, source_target_pairs={{0,4},{4,0},{8,12},{12,8},{1,5},{5,1},{9,13},{13,9},{2,6},{6,2},{1... | collective-permute-start | bytes 393224 | tf_op jit(solution)/shard_map/ppermute | solution.py:513
  21.8 9.8 %collective-permute-start.8 = (bf16[2,2,64,256]{3,2,1,0:T(8,128)(2,1)S(1)}, bf16[2,2,64,256]{3,2,1,0:T(8,128)(2,1)S(1)}, u32[]{:S(2)}, u32[]{:S(2)}) collective-permute-start(bf16[2,2,64,256]{3,2,1,0:T(8,128)(2,1)S(1)} %get-tuple-element.68.rest_0_), channel_id=1, source_target_pairs={{0,2},{2,0},{1,3},{3,1},{4,6},{6,4},{5,7},{7,5},{8,10},{10,8},{9,1... | collective-permute-start | bytes 393224 | tf_op jit(solution)/shard_map/ppermute | solution.py:513
  23.4 8.2 %collective-permute-start = (bf16[2,256,512]{2,1,0:T(8,128)(2,1)S(1)}, bf16[2,256,512]{2,1,0:T(8,128)(2,1)S(1)}, u32[]{:S(2)}, u32[]{:S(2)}) collective-permute-start(bf16[2,256,512]{2,1,0:T(8,128)(2,1)S(1)} %get-tuple-element.51.rest_1_.rest_0_.rest_2_), channel_id=1, source_target_pairs={{0,1},{1,0},{2,3},{3,2},{4,5},{5,4},{6,7},{7,6},{8,9},{9,8},{10,11... | collective-permute-start | bytes 1572872 | tf_op jit(solution)/shard_map/ppermute | solution.py:513
  23.4 8.2 %collective-permute-start.1 = (bf16[2,256,512]{2,1,0:T(8,128)(2,1)S(1)}, bf16[2,256,512]{2,1,0:T(8,128)(2,1)S(1)}, u32[]{:S(2)}, u32[]{:S(2)}) collective-permute-start(bf16[2,256,512]{2,1,0:T(8,128)(2,1)S(1)} %get-tuple-element.52.rest_3_.rest_2_.rest_4_), channel_id=1, source_target_pairs={{0,1},{1,0},{2,3},{3,2},{4,5},{5,4},{6,7},{7,6},{8,9},{9,8},{10,11... | collective-permute-start | bytes 1572872 | tf_op jit(solution)/shard_map/ppermute | solution.py:513
  23.9 8.5 %collective-permute-start.9 = (bf16[2,256,512]{2,1,0:T(8,128)(2,1)S(1)}, bf16[2,256,512]{2,1,0:T(8,128)(2,1)S(1)}, u32[]{:S(2)}, u32[]{:S(2)}) collective-permute-start(bf16[2,256,512]{2,1,0:T(8,128)(2,1)S(1)} %collective-permute-done.6.rest_2_.rest_0_.rest_3_), channel_id=1, source_target_pairs={{0,1},{1,0},{2,3},{3,2},{4,5},{5,4},{6,7},{7,6},{8,9},{9,8},{10,11... | collective-permute-start | bytes 1572872 | tf_op jit(solution)/shard_map/ppermute | solution.py:513
  34.0 12.9 %collective-permute-start.11 = (bf16[64,1024]{1,0:T(8,128)(2,1)S(1)}, bf16[64,1024]{1,0:T(8,128)(2,1)S(1)}, u32[]{:S(2)}, u32[]{:S(2)}) collective-permute-start(bf16[64,1024]{1,0:T(8,128)(2,1)S(1)} %get-tuple-element.74), channel_id=1, source_target_pairs={{0,8},{4,12},{8,0},{12,4},{1,9},{5,13},{9,1},{13,5},{2,10},{6,14},... | collective-permute-start | bytes 393224 | tf_op jit(solution)/shard_map/ppermute | solution.py:513
  36.9 10.0 %collective-permute-start.12 = (bf16[64,1024]{1,0:T(8,128)(2,1)S(1)}, bf16[64,1024]{1,0:T(8,128)(2,1)S(1)}, u32[]{:S(2)}, u32[]{:S(2)}) collective-permute-start(bf16[64,1024]{1,0:T(8,128)(2,1)S(1)} %get-tuple-element.75), channel_id=1, source_target_pairs={{0,12},{4,8},{8,4},{12,0},{1,13},{5,9},{9,5},{13,1},{2,14},{6,10},... | collective-permute-start | bytes 393224 | tf_op jit(solution)/shard_map/ppermute | solution.py:513
  38.2 9.5 %collective-permute-start.13 = (bf16[64,1024]{1,0:T(8,128)(2,1)S(1)}, bf16[64,1024]{1,0:T(8,128)(2,1)S(1)}, u32[]{:S(2)}, u32[]{:S(2)}) collective-permute-start(bf16[64,1024]{1,0:T(8,128)(2,1)S(1)} %get-tuple-element.76), channel_id=1, source_target_pairs={{0,4},{4,0},{8,12},{12,8},{1,5},{5,1},{9,13},{13,9},{2,6},{6,2},{1... | collective-permute-start | bytes 393224 | tf_op jit(solution)/shard_map/ppermute | solution.py:513
  48.7 13.8 %collective-permute-start.14 = (bf16[64,1024]{1,0:T(8,128)(2,1)S(1)}, bf16[64,1024]{1,0:T(8,128)(2,1)S(1)}, u32[]{:S(2)}, u32[]{:S(2)}) collective-permute-start(bf16[64,1024]{1,0:T(8,128)(2,1)S(1)} %get-tuple-element.78), channel_id=1, source_target_pairs={{0,8},{4,12},{8,0},{12,4},{1,9},{5,13},{9,1},{13,5},{2,10},{6,14},... | collective-permute-start | bytes 393224 | tf_op jit(solution)/shard_map/ppermute | solution.py:513
  52.9 9.6 %collective-permute-start.15 = (bf16[64,1024]{1,0:T(8,128)(2,1)S(1)}, bf16[64,1024]{1,0:T(8,128)(2,1)S(1)}, u32[]{:S(2)}, u32[]{:S(2)}) collective-permute-start(bf16[64,1024]{1,0:T(8,128)(2,1)S(1)} %get-tuple-element.79), channel_id=1, source_target_pairs={{0,12},{4,8},{8,4},{12,0},{1,13},{5,9},{9,5},{13,1},{2,14},{6,10},... | collective-permute-start | bytes 393224 | tf_op jit(solution)/shard_map/ppermute | solution.py:513
  53.3 10.3 %collective-permute-start.16 = (bf16[64,1024]{1,0:T(8,128)(2,1)S(1)}, bf16[64,1024]{1,0:T(8,128)(2,1)S(1)}, u32[]{:S(2)}, u32[]{:S(2)}) collective-permute-start(bf16[64,1024]{1,0:T(8,128)(2,1)S(1)} %get-tuple-element.80), channel_id=1, source_target_pairs={{0,4},{4,0},{8,12},{12,8},{1,5},{5,1},{9,13},{13,9},{2,6},{6,2},{1... | collective-permute-start | bytes 393224 | tf_op jit(solution)/shard_map/ppermute | solution.py:513
  68.4 5.7 %collective-permute-start.18 = (bf16[2,2,32,256]{3,2,1,0:T(8,128)(2,1)S(1)}, bf16[2,2,32,256]{3,2,1,0:T(8,128)(2,1)S(1)}, u32[]{:S(2)}, u32[]{:S(2)}) collective-permute-start(bf16[2,2,32,256]{3,2,1,0:T(8,128)(2,1)S(1)} %shard_map.84.rest_0_), channel_id=1, source_target_pairs={{0,8},{4,12},{8,0},{12,4},{1,9},{5,13},{9,1},{13,5},{2,10},{6,14},... | collective-permute-start | bytes 196616 | tf_op jit(solution)/shard_map/ppermute | solution.py:513
  70.4 6.6 %collective-permute-start.22 = (bf16[2,2,32,256]{3,2,1,0:T(8,128)(2,1)S(1)}, bf16[2,2,32,256]{3,2,1,0:T(8,128)(2,1)S(1)}, u32[]{:S(2)}, u32[]{:S(2)}) collective-permute-start(bf16[2,2,32,256]{3,2,1,0:T(8,128)(2,1)S(1)} %shard_map.86.rest_0_), channel_id=1, source_target_pairs={{0,8},{4,12},{8,0},{12,4},{1,9},{5,13},{9,1},{13,5},{2,10},{6,14},... | collective-permute-start | bytes 196616 | tf_op jit(solution)/shard_map/ppermute | solution.py:513
  71.9 7.1 %collective-permute-start.20 = (bf16[2,2,32,256]{3,2,1,0:T(8,128)(2,1)S(1)}, bf16[2,2,32,256]{3,2,1,0:T(8,128)(2,1)S(1)}, u32[]{:S(2)}, u32[]{:S(2)}) collective-permute-start(bf16[2,2,32,256]{3,2,1,0:T(8,128)(2,1)S(1)} %shard_map.84.rest_0_), channel_id=1, source_target_pairs={{0,4},{4,0},{8,12},{12,8},{1,5},{5,1},{9,13},{13,9},{2,6},{6,2},{1... | collective-permute-start | bytes 196616 | tf_op jit(solution)/shard_map/ppermute | solution.py:513
  74.1 5.1 %collective-permute-start.19 = (bf16[2,2,32,256]{3,2,1,0:T(8,128)(2,1)S(1)}, bf16[2,2,32,256]{3,2,1,0:T(8,128)(2,1)S(1)}, u32[]{:S(2)}, u32[]{:S(2)}) collective-permute-start(bf16[2,2,32,256]{3,2,1,0:T(8,128)(2,1)S(1)} %collective-permute-done.18.rest_1_), channel_id=1, source_target_pairs={{0,4},{4,0},{8,12},{12,8},{1,5},{5,1},{9,13},{13,9},{2,6},{6,2},{1... | collective-permute-start | bytes 196616 | tf_op jit(solution)/shard_map/ppermute | solution.py:513
  77.0 4.9 %collective-permute-start.23 = (bf16[2,2,32,256]{3,2,1,0:T(8,128)(2,1)S(1)}, bf16[2,2,32,256]{3,2,1,0:T(8,128)(2,1)S(1)}, u32[]{:S(2)}, u32[]{:S(2)}) collective-permute-start(bf16[2,2,32,256]{3,2,1,0:T(8,128)(2,1)S(1)} %collective-permute-done.22.rest_1_), channel_id=1, source_target_pairs={{0,4},{4,0},{8,12},{12,8},{1,5},{5,1},{9,13},{13,9},{2,6},{6,2},{1... | collective-permute-start | bytes 196616 | tf_op jit(solution)/shard_map/ppermute | solution.py:513
  87.4 10.0 %collective-permute-start.27 = (bf16[64,1024]{1,0:T(8,128)(2,1)S(1)}, bf16[64,1024]{1,0:T(8,128)(2,1)S(1)}, u32[]{:S(2)}, u32[]{:S(2)}) collective-permute-start(bf16[64,1024]{1,0:T(8,128)(2,1)S(1)} %get-tuple-element.86), channel_id=1, source_target_pairs={{0,8},{1,5},{4,12},{5,1},{8,0},{9,13},{12,4},{13,9},{2,10},{3,7},{... | collective-permute-start | bytes 393224 | tf_op jit(solution)/shard_map/ppermute | solution.py:526
  88.2 9.2 %collective-permute-start.28 = (bf16[64,1024]{1,0:T(8,128)(2,1)S(1)}, bf16[64,1024]{1,0:T(8,128)(2,1)S(1)}, u32[]{:S(2)}, u32[]{:S(2)}) collective-permute-start(bf16[64,1024]{1,0:T(8,128)(2,1)S(1)} %get-tuple-element.87), channel_id=1, source_target_pairs={{0,12},{1,13},{4,8},{5,9},{8,4},{9,5},{12,0},{13,1},{2,14},{3,15},... | collective-permute-start | bytes 393224 | tf_op jit(solution)/shard_map/ppermute | solution.py:526
  91.2 7.5 %collective-permute-start.29 = (bf16[64,1024]{1,0:T(8,128)(2,1)S(1)}, bf16[64,1024]{1,0:T(8,128)(2,1)S(1)}, u32[]{:S(2)}, u32[]{:S(2)}) collective-permute-start(bf16[64,1024]{1,0:T(8,128)(2,1)S(1)} %get-tuple-element.88), channel_id=1, source_target_pairs={{0,4},{1,9},{4,0},{5,13},{8,12},{9,1},{12,8},{13,5},{2,6},{3,11},{... | collective-permute-start | bytes 393224 | tf_op jit(solution)/shard_map/ppermute | solution.py:526
  99.7 11.6 %collective-permute-start.30 = (bf16[64,1024]{1,0:T(8,128)(2,1)S(1)}, bf16[64,1024]{1,0:T(8,128)(2,1)S(1)}, u32[]{:S(2)}, u32[]{:S(2)}) collective-permute-start(bf16[64,1024]{1,0:T(8,128)(2,1)S(1)} %get-tuple-element.90), channel_id=1, source_target_pairs={{0,8},{1,5},{4,12},{5,1},{8,0},{9,13},{12,4},{13,9},{2,10},{3,7},{... | collective-permute-start | bytes 393224 | tf_op jit(solution)/shard_map/ppermute | solution.py:526
  100.6 10.8 %collective-permute-start.31 = (bf16[64,1024]{1,0:T(8,128)(2,1)S(1)}, bf16[64,1024]{1,0:T(8,128)(2,1)S(1)}, u32[]{:S(2)}, u32[]{:S(2)}) collective-permute-start(bf16[64,1024]{1,0:T(8,128)(2,1)S(1)} %get-tuple-element.91), channel_id=1, source_target_pairs={{0,12},{1,13},{4,8},{5,9},{8,4},{9,5},{12,0},{13,1},{2,14},{3,15},... | collective-permute-start | bytes 393224 | tf_op jit(solution)/shard_map/ppermute | solution.py:526
  102.8 8.7 %collective-permute-start.32 = (bf16[64,1024]{1,0:T(8,128)(2,1)S(1)}, bf16[64,1024]{1,0:T(8,128)(2,1)S(1)}, u32[]{:S(2)}, u32[]{:S(2)}) collective-permute-start(bf16[64,1024]{1,0:T(8,128)(2,1)S(1)} %get-tuple-element.92), channel_id=1, source_target_pairs={{0,4},{1,9},{4,0},{5,13},{8,12},{9,1},{12,8},{13,5},{2,6},{3,11},{... | collective-permute-start | bytes 393224 | tf_op jit(solution)/shard_map/ppermute | solution.py:526
  111.9 5.0 %collective-permute-start.37 = (bf16[2,2,32,256]{3,2,1,0:T(8,128)(2,1)S(1)}, bf16[2,2,32,256]{3,2,1,0:T(8,128)(2,1)S(1)}, u32[]{:S(2)}, u32[]{:S(2)}) collective-permute-start(bf16[2,2,32,256]{3,2,1,0:T(8,128)(2,1)S(1)} %get-tuple-element.96), channel_id=1, source_target_pairs={{0,2},{2,0},{1,3},{3,1},{4,6},{6,4},{5,7},{7,5},{8,10},{10,8},{9,1... | collective-permute-start | bytes 196616 | tf_op jit(solution)/shard_map/ppermute | solution.py:513
  112.8 5.7 %collective-permute-start.33 = (bf16[2,2,32,256]{3,2,1,0:T(8,128)(2,1)S(1)}, bf16[2,2,32,256]{3,2,1,0:T(8,128)(2,1)S(1)}, u32[]{:S(2)}, u32[]{:S(2)}) collective-permute-start(bf16[2,2,32,256]{3,2,1,0:T(8,128)(2,1)S(1)} %get-tuple-element.94), channel_id=1, source_target_pairs={{0,2},{2,0},{1,3},{3,1},{4,6},{6,4},{5,7},{7,5},{8,10},{10,8},{9,1... | collective-permute-start | bytes 196616 | tf_op jit(solution)/shard_map/ppermute | solution.py:513
  117.0 6.5 %collective-permute-start.38 = (bf16[2,2,32,256]{3,2,1,0:T(8,128)(2,1)S(1)}, bf16[2,2,32,256]{3,2,1,0:T(8,128)(2,1)S(1)}, u32[]{:S(2)}, u32[]{:S(2)}) collective-permute-start(bf16[2,2,32,256]{3,2,1,0:T(8,128)(2,1)S(1)} %shard_map.94.rest_0_), channel_id=1, source_target_pairs={{0,8},{4,12},{8,0},{12,4},{1,9},{5,13},{9,1},{13,5},{2,10},{6,14},... | collective-permute-start | bytes 196616 | tf_op jit(solution)/shard_map/ppermute | solution.py:513
  118.6 6.9 %collective-permute-start.34 = (bf16[2,2,32,256]{3,2,1,0:T(8,128)(2,1)S(1)}, bf16[2,2,32,256]{3,2,1,0:T(8,128)(2,1)S(1)}, u32[]{:S(2)}, u32[]{:S(2)}) collective-permute-start(bf16[2,2,32,256]{3,2,1,0:T(8,128)(2,1)S(1)} %shard_map.93.rest_0_), channel_id=1, source_target_pairs={{0,8},{4,12},{8,0},{12,4},{1,9},{5,13},{9,1},{13,5},{2,10},{6,14},... | collective-permute-start | bytes 196616 | tf_op jit(solution)/shard_map/ppermute | solution.py:513
  120.1 6.4 %collective-permute-start.40 = (bf16[2,2,32,256]{3,2,1,0:T(8,128)(2,1)S(1)}, bf16[2,2,32,256]{3,2,1,0:T(8,128)(2,1)S(1)}, u32[]{:S(2)}, u32[]{:S(2)}) collective-permute-start(bf16[2,2,32,256]{3,2,1,0:T(8,128)(2,1)S(1)} %shard_map.94.rest_0_), channel_id=1, source_target_pairs={{0,4},{4,0},{8,12},{12,8},{1,5},{5,1},{9,13},{13,9},{2,6},{6,2},{1... | collective-permute-start | bytes 196616 | tf_op jit(solution)/shard_map/ppermute | solution.py:513
  124.4 5.5 %collective-permute-start.36 = (bf16[2,2,32,256]{3,2,1,0:T(8,128)(2,1)S(1)}, bf16[2,2,32,256]{3,2,1,0:T(8,128)(2,1)S(1)}, u32[]{:S(2)}, u32[]{:S(2)}) collective-permute-start(bf16[2,2,32,256]{3,2,1,0:T(8,128)(2,1)S(1)} %shard_map.93.rest_0_), channel_id=1, source_target_pairs={{0,4},{4,0},{8,12},{12,8},{1,5},{5,1},{9,13},{13,9},{2,6},{6,2},{1... | collective-permute-start | bytes 196616 | tf_op jit(solution)/shard_map/ppermute | solution.py:513
  (16 other events, 175.1 us)

commit v22 on v14

--- a/solution.py
+++ b/solution.py
@@ -448,7 +448,7 @@
     count = table.shape[2]
 
     def body(place_ref, _, sblk, x_ref, o_ref, t_ref, *rest):
-        refs = rest[:freq_devs]
+        refs = rest[:freq_devs][::-1]
         out, spread_ref = rest[-2:]
         step = pl.program_id(0)
 
@@ -473,7 +473,7 @@
                 moved = jnp.where(on, change[row * own : (row + 1) * own], 0.0)
                 out[spot] = (x_ref[first + step * tile + spot].astype(F32) - moved).astype(BF16)
 
-    inputs = [(v, whole(v)) for v in (initial, onset, table, *messages)]
+    inputs = [(v, whole(v)) for v in (initial, onset, table, *messages[::-1])]
     aliases = {}
     if target is not None:
         inputs.append((target, pl.BlockSpec(memory_space=pl.ANY)))
@@ -552,7 +552,8 @@
         keep = up_products(messages, parts, freq_place, half_rows, 0)
         near, far = [], []
         for chunk in range(CHUNKS):
-            back = spread(added(keep[chunk], received[chunk]), freq_devs)
+            back = added(keep[chunk], received[chunk])
+            back = spread(back, freq_devs) if step < ITERS - 1 else dealt_out([back] * freq_devs)
             if step < ITERS - 1:
                 near.append(next_spectra(sums, back, rcv_tables, matrix, freq_place, chunk * rows))
                 far.append(exchanged(near[chunk], "rblk", 1))

time: 130 us -> 130 us (level)
  waiting for transfers between devices: 56.2 us -> 58 us
  starting transfers between devices: 54.5 us -> 52.8 us
    ppermute x41, waiting for transfers between devices: 56.2 us -> 58 us  [exchanged(): lax.ppermute(value, axis, [(i, i ^ step) for i in range(lax.axis_size(axi...]
    ppermute x41, starting transfers between devices: 54.5 us -> 52.8 us  [exchanged(): lax.ppermute(value, axis, [(i, i ^ step) for i in range(lax.axis_size(axi...]
where the time goes in v22:
time: 130 us
  waiting for transfers between devices  58 us (45%)
  starting transfers between devices  52.8 us (41%)
  Pallas kernels  14.3 us (11%)
  local copies, waits for them, and re-layouts  4.56 us (4%)
    ppermute x41, waiting for transfers between devices, exchanged(): lax.ppermute(value, axis, [(i, i ^ step) for i in range(lax.axis_size(axi...  58 us
    ppermute x41, starting transfers between devices, exchanged(): lax.ppermute(value, axis, [(i, i ^ step) for i in range(lax.axis_size(axi...  52.8 us
    pallas_call x24, Pallas kernels, call(): pl.pallas_call(body, grid_spec=pltpu.PrefetchScalarGridSpec(num_scalar_pr...  14.3 us
    unnamed x15, local copies, waits for them, and re-layouts  4.56 us
  transfers between devices with their start and end apart: 41, of which 22 were waited for; matrix products, arithmetic and copies ran while one was open for 0% of the time, Pallas kernels for 6%

profile of v22, /device:TPU:0, one launch (start us, length us, event | category | flops | bytes accessed | tf_op | source)
XLA Modules:
  0.0 129.9 jit_solution(14596744756819185506)
XLA Ops:
  0.8 1.6 %copy-done.2 = bf16[2,2,1024,256]{3,2,1,0:T(8,128)(2,1)S(1)} copy-done((bf16[2,2,1024,256]{3,2,1,0:T(8,128)(2,1)S(1)}, bf16[2,2,1024,256]{3,2,1,0:T(8,128)(2,1)}, u32[]{:S(2)}) %copy-start.2) | copy-done | bytes 2097176
  2.6 3.0 %collective-permute-start.6 = (bf16[2,256,512]{2,1,0:T(8,128)(2,1)S(1)}, bf16[2,256,512]{2,1,0:T(8,128)(2,1)S(1)}, u32[]{:S(2)}, u32[]{:S(2)}) collective-permute-start(bf16[2,256,512]{2,1,0:T(8,128)(2,1)S(1)} %get-tuple-element.66), channel_id=1, source_target_pairs={{0,2},{2,0},{1,3},{3,1},{4,6},{6,4},{5,7},{7,5},{8,10},{10,8},{9,1... | collective-permute-start | bytes 1572872 | tf_op jit(solution)/shard_map/ppermute | solution.py:495
  5.7 2.2 %copy-done = bf16[64,128,256]{2,1,0:T(8,128)(2,1)S(1)} copy-done((bf16[64,128,256]{2,1,0:T(8,128)(2,1)S(1)}, bf16[64,128,256]{2,1,0:T(8,128)(2,1)}, u32[]{:S(2)}) %copy-start) | copy-done | bytes 4194328
  8.6 3.1 %collective-permute-start.3 = (bf16[2,2,64,256]{3,2,1,0:T(8,128)(2,1)S(1)}, bf16[2,2,64,256]{3,2,1,0:T(8,128)(2,1)S(1)}, u32[]{:S(2)}, u32[]{:S(2)}) collective-permute-start(bf16[2,2,64,256]{3,2,1,0:T(8,128)(2,1)S(1)} %get-tuple-element.59), channel_id=1, source_target_pairs={{0,8},{4,12},{8,0},{12,4},{1,9},{5,13},{9,1},{13,5},{2,10},{6,14},... | collective-permute-start | bytes 393224 | tf_op jit(solution)/shard_map/ppermute | solution.py:495
  13.3 8.2 %collective-permute-done.3.refs_1_ = bf16[2,2,64,256]{3,2,1,0:T(8,128)(2,1)S(1)} collective-permute-done((bf16[2,2,64,256]{3,2,1,0:T(8,128)(2,1)S(1)}, bf16[2,2,64,256]{3,2,1,0:T(8,128)(2,1)S(1)}, u32[]{:S(2)}, u32[]{:S(2)}) %collective-permute-start.3) | collective-permute-done | bytes 131104 | tf_op jit(solution)/shard_map/ppermute | solution.py:495
  21.8 1.6 %collective-permute-start.8 = (bf16[2,2,64,256]{3,2,1,0:T(8,128)(2,1)S(1)}, bf16[2,2,64,256]{3,2,1,0:T(8,128)(2,1)S(1)}, u32[]{:S(2)}, u32[]{:S(2)}) collective-permute-start(bf16[2,2,64,256]{3,2,1,0:T(8,128)(2,1)S(1)} %get-tuple-element.68.rest_0_), channel_id=1, source_target_pairs={{0,2},{2,0},{1,3},{3,1},{4,6},{6,4},{5,7},{7,5},{8,10},{10,8},{9,1... | collective-permute-start | bytes 393224 | tf_op jit(solution)/shard_map/ppermute | solution.py:495
  24.0 7.6 %collective-permute-done.8.rest_1_ = bf16[2,2,64,256]{3,2,1,0:T(8,128)(2,1)S(1)} collective-permute-done((bf16[2,2,64,256]{3,2,1,0:T(8,128)(2,1)S(1)}, bf16[2,2,64,256]{3,2,1,0:T(8,128)(2,1)S(1)}, u32[]{:S(2)}, u32[]{:S(2)}) %collective-permute-start.8) | collective-permute-done | bytes 131104 | tf_op jit(solution)/shard_map/ppermute | solution.py:495
  34.0 2.9 %collective-permute-start.11 = (bf16[64,1024]{1,0:T(8,128)(2,1)S(1)}, bf16[64,1024]{1,0:T(8,128)(2,1)S(1)}, u32[]{:S(2)}, u32[]{:S(2)}) collective-permute-start(bf16[64,1024]{1,0:T(8,128)(2,1)S(1)} %get-tuple-element.74), channel_id=1, source_target_pairs={{0,8},{4,12},{8,0},{12,4},{1,9},{5,13},{9,1},{13,5},{2,10},{6,14},... | collective-permute-start | bytes 393224 | tf_op jit(solution)/shard_map/ppermute | solution.py:495
  41.1 5.8 %collective-permute-done.11.rest_1_ = bf16[64,1024]{1,0:T(8,128)(2,1)S(1)} collective-permute-done((bf16[64,1024]{1,0:T(8,128)(2,1)S(1)}, bf16[64,1024]{1,0:T(8,128)(2,1)S(1)}, u32[]{:S(2)}, u32[]{:S(2)}) %collective-permute-start.11) | collective-permute-done | bytes 131104 | tf_op jit(solution)/shard_map/ppermute | solution.py:495
  48.7 4.2 %collective-permute-start.14 = (bf16[64,1024]{1,0:T(8,128)(2,1)S(1)}, bf16[64,1024]{1,0:T(8,128)(2,1)S(1)}, u32[]{:S(2)}, u32[]{:S(2)}) collective-permute-start(bf16[64,1024]{1,0:T(8,128)(2,1)S(1)} %get-tuple-element.78), channel_id=1, source_target_pairs={{0,8},{4,12},{8,0},{12,4},{1,9},{5,13},{9,1},{13,5},{2,10},{6,14},... | collective-permute-start | bytes 393224 | tf_op jit(solution)/shard_map/ppermute | solution.py:495
  53.5 9.0 %collective-permute-done.14.rest_5_ = bf16[64,1024]{1,0:T(8,128)(2,1)S(1)} collective-permute-done((bf16[64,1024]{1,0:T(8,128)(2,1)S(1)}, bf16[64,1024]{1,0:T(8,128)(2,1)S(1)}, u32[]{:S(2)}, u32[]{:S(2)}) %collective-permute-start.14) | collective-permute-done | bytes 131104 | tf_op jit(solution)/shard_map/ppermute | solution.py:495
  64.1 1.6 %collective-permute-start.17 = (bf16[2,2,32,256]{3,2,1,0:T(8,128)(2,1)S(1)}, bf16[2,2,32,256]{3,2,1,0:T(8,128)(2,1)S(1)}, u32[]{:S(2)}, u32[]{:S(2)}) collective-permute-start(bf16[2,2,32,256]{3,2,1,0:T(8,128)(2,1)S(1)} %get-tuple-element.82), channel_id=1, source_target_pairs={{0,2},{2,0},{1,3},{3,1},{4,6},{6,4},{5,7},{7,5},{8,10},{10,8},{9,1... | collective-permute-start | bytes 196616 | tf_op jit(solution)/shard_map/ppermute | solution.py:495
  66.7 1.8 %collective-permute-done.17.r_ref = bf16[2,2,32,256]{3,2,1,0:T(8,128)(2,1)S(1)} collective-permute-done((bf16[2,2,32,256]{3,2,1,0:T(8,128)(2,1)S(1)}, bf16[2,2,32,256]{3,2,1,0:T(8,128)(2,1)S(1)}, u32[]{:S(2)}, u32[]{:S(2)}) %collective-permute-start.17) | collective-permute-done | bytes 65568 | tf_op jit(solution)/shard_map/ppermute | solution.py:495
  68.4 1.9 %collective-permute-start.18 = (bf16[2,2,32,256]{3,2,1,0:T(8,128)(2,1)S(1)}, bf16[2,2,32,256]{3,2,1,0:T(8,128)(2,1)S(1)}, u32[]{:S(2)}, u32[]{:S(2)}) collective-permute-start(bf16[2,2,32,256]{3,2,1,0:T(8,128)(2,1)S(1)} %shard_map.84.rest_0_), channel_id=1, source_target_pairs={{0,8},{4,12},{8,0},{12,4},{1,9},{5,13},{9,1},{13,5},{2,10},{6,14},... | collective-permute-start | bytes 196616 | tf_op jit(solution)/shard_map/ppermute | solution.py:495
  71.9 2.3 %collective-permute-start.20 = (bf16[2,2,32,256]{3,2,1,0:T(8,128)(2,1)S(1)}, bf16[2,2,32,256]{3,2,1,0:T(8,128)(2,1)S(1)}, u32[]{:S(2)}, u32[]{:S(2)}) collective-permute-start(bf16[2,2,32,256]{3,2,1,0:T(8,128)(2,1)S(1)} %shard_map.84.rest_0_), channel_id=1, source_target_pairs={{0,4},{4,0},{8,12},{12,8},{1,5},{5,1},{9,13},{13,9},{2,6},{6,2},{1... | collective-permute-start | bytes 196616 | tf_op jit(solution)/shard_map/ppermute | solution.py:495
  74.1 2.8 %collective-permute-start.19 = (bf16[2,2,32,256]{3,2,1,0:T(8,128)(2,1)S(1)}, bf16[2,2,32,256]{3,2,1,0:T(8,128)(2,1)S(1)}, u32[]{:S(2)}, u32[]{:S(2)}) collective-permute-start(bf16[2,2,32,256]{3,2,1,0:T(8,128)(2,1)S(1)} %collective-permute-done.18.rest_1_), channel_id=1, source_target_pairs={{0,4},{4,0},{8,12},{12,8},{1,5},{5,1},{9,13},{13,9},{2,6},{6,2},{1... | collective-permute-start | bytes 196616 | tf_op jit(solution)/shard_map/ppermute | solution.py:495
  77.0 2.0 %collective-permute-start.23 = (bf16[2,2,32,256]{3,2,1,0:T(8,128)(2,1)S(1)}, bf16[2,2,32,256]{3,2,1,0:T(8,128)(2,1)S(1)}, u32[]{:S(2)}, u32[]{:S(2)}) collective-permute-start(bf16[2,2,32,256]{3,2,1,0:T(8,128)(2,1)S(1)} %collective-permute-done.22.rest_1_), channel_id=1, source_target_pairs={{0,4},{4,0},{8,12},{12,8},{1,5},{5,1},{9,13},{13,9},{2,6},{6,2},{1... | collective-permute-start | bytes 196616 | tf_op jit(solution)/shard_map/ppermute | solution.py:495
  84.1 2.4 %collective-permute-done.26.rest_2_ = bf16[2,2,32,256]{3,2,1,0:T(8,128)(2,1)S(1)} collective-permute-done((bf16[2,2,32,256]{3,2,1,0:T(8,128)(2,1)S(1)}, bf16[2,2,32,256]{3,2,1,0:T(8,128)(2,1)S(1)}, u32[]{:S(2)}, u32[]{:S(2)}) %collective-permute-start.26) | collective-permute-done | bytes 65568 | tf_op jit(solution)/shard_map/ppermute | solution.py:495
  88.2 3.0 %collective-permute-start.28 = (bf16[64,1024]{1,0:T(8,128)(2,1)S(1)}, bf16[64,1024]{1,0:T(8,128)(2,1)S(1)}, u32[]{:S(2)}, u32[]{:S(2)}) collective-permute-start(bf16[64,1024]{1,0:T(8,128)(2,1)S(1)} %get-tuple-element.87), channel_id=1, source_target_pairs={{0,12},{4,8},{8,4},{12,0},{1,13},{5,9},{9,5},{13,1},{2,14},{6,10},... | collective-permute-start | bytes 393224 | tf_op jit(solution)/shard_map/ppermute | solution.py:495
  91.2 5.1 %collective-permute-done.27.rest_1_ = bf16[64,1024]{1,0:T(8,128)(2,1)S(1)} collective-permute-done((bf16[64,1024]{1,0:T(8,128)(2,1)S(1)}, bf16[64,1024]{1,0:T(8,128)(2,1)S(1)}, u32[]{:S(2)}, u32[]{:S(2)}) %collective-permute-start.27) | collective-permute-done | bytes 131104 | tf_op jit(solution)/shard_map/ppermute | solution.py:495
  96.3 1.5 %collective-permute-done.29.rest_3_ = bf16[64,1024]{1,0:T(8,128)(2,1)S(1)} collective-permute-done((bf16[64,1024]{1,0:T(8,128)(2,1)S(1)}, bf16[64,1024]{1,0:T(8,128)(2,1)S(1)}, u32[]{:S(2)}, u32[]{:S(2)}) %collective-permute-start.29) | collective-permute-done | bytes 131104 | tf_op jit(solution)/shard_map/ppermute | solution.py:495
  98.8 1.7 %collective-permute-start.30 = (bf16[64,1024]{1,0:T(8,128)(2,1)S(1)}, bf16[64,1024]{1,0:T(8,128)(2,1)S(1)}, u32[]{:S(2)}, u32[]{:S(2)}) collective-permute-start(bf16[64,1024]{1,0:T(8,128)(2,1)S(1)} %get-tuple-element.90), channel_id=1, source_target_pairs={{0,8},{4,12},{8,0},{12,4},{1,9},{5,13},{9,1},{13,5},{2,10},{6,14},... | collective-permute-start | bytes 393224 | tf_op jit(solution)/shard_map/ppermute | solution.py:495
  100.4 3.4 %collective-permute-start.31 = (bf16[64,1024]{1,0:T(8,128)(2,1)S(1)}, bf16[64,1024]{1,0:T(8,128)(2,1)S(1)}, u32[]{:S(2)}, u32[]{:S(2)}) collective-permute-start(bf16[64,1024]{1,0:T(8,128)(2,1)S(1)} %get-tuple-element.91), channel_id=1, source_target_pairs={{0,12},{4,8},{8,4},{12,0},{1,13},{5,9},{9,5},{13,1},{2,14},{6,10},... | collective-permute-start | bytes 393224 | tf_op jit(solution)/shard_map/ppermute | solution.py:495
  104.7 3.7 %collective-permute-done.31.rest_6_ = bf16[64,1024]{1,0:T(8,128)(2,1)S(1)} collective-permute-done((bf16[64,1024]{1,0:T(8,128)(2,1)S(1)}, bf16[64,1024]{1,0:T(8,128)(2,1)S(1)}, u32[]{:S(2)}, u32[]{:S(2)}) %collective-permute-start.31) | collective-permute-done | bytes 131104 | tf_op jit(solution)/shard_map/ppermute | solution.py:495
  108.4 2.0 %collective-permute-done.32.rest_7_ = bf16[64,1024]{1,0:T(8,128)(2,1)S(1)} collective-permute-done((bf16[64,1024]{1,0:T(8,128)(2,1)S(1)}, bf16[64,1024]{1,0:T(8,128)(2,1)S(1)}, u32[]{:S(2)}, u32[]{:S(2)}) %collective-permute-start.32) | collective-permute-done | bytes 131104 | tf_op jit(solution)/shard_map/ppermute | solution.py:495
  110.9 1.8 %collective-permute-start.37 = (bf16[2,2,32,256]{3,2,1,0:T(8,128)(2,1)S(1)}, bf16[2,2,32,256]{3,2,1,0:T(8,128)(2,1)S(1)}, u32[]{:S(2)}, u32[]{:S(2)}) collective-permute-start(bf16[2,2,32,256]{3,2,1,0:T(8,128)(2,1)S(1)} %get-tuple-element.96), channel_id=1, source_target_pairs={{0,2},{2,0},{1,3},{3,1},{4,6},{6,4},{5,7},{7,5},{8,10},{10,8},{9,1... | collective-permute-start | bytes 196616 | tf_op jit(solution)/shard_map/ppermute | solution.py:495
  113.4 1.8 %collective-permute-done.37.r_ref = bf16[2,2,32,256]{3,2,1,0:T(8,128)(2,1)S(1)} collective-permute-done((bf16[2,2,32,256]{3,2,1,0:T(8,128)(2,1)S(1)}, bf16[2,2,32,256]{3,2,1,0:T(8,128)(2,1)S(1)}, u32[]{:S(2)}, u32[]{:S(2)}) %collective-permute-start.37) | collective-permute-done | bytes 65568 | tf_op jit(solution)/shard_map/ppermute | solution.py:495
  115.2 2.2 %collective-permute-start.40 = (bf16[2,2,32,256]{3,2,1,0:T(8,128)(2,1)S(1)}, bf16[2,2,32,256]{3,2,1,0:T(8,128)(2,1)S(1)}, u32[]{:S(2)}, u32[]{:S(2)}) collective-permute-start(bf16[2,2,32,256]{3,2,1,0:T(8,128)(2,1)S(1)} %shard_map.94.rest_3_), channel_id=1, source_target_pairs={{0,8},{4,12},{8,0},{12,4},{1,9},{5,13},{9,1},{13,5},{2,10},{6,14},... | collective-permute-start | bytes 196616 | tf_op jit(solution)/shard_map/ppermute | solution.py:495
  118.8 3.0 %collective-permute-start.36 = (bf16[2,2,32,256]{3,2,1,0:T(8,128)(2,1)S(1)}, bf16[2,2,32,256]{3,2,1,0:T(8,128)(2,1)S(1)}, u32[]{:S(2)}, u32[]{:S(2)}) collective-permute-start(bf16[2,2,32,256]{3,2,1,0:T(8,128)(2,1)S(1)} %shard_map.93.rest_3_), channel_id=1, source_target_pairs={{0,8},{4,12},{8,0},{12,4},{1,9},{5,13},{9,1},{13,5},{2,10},{6,14},... | collective-permute-start | bytes 196616 | tf_op jit(solution)/shard_map/ppermute | solution.py:495
  123.5 2.0 %shard_map.95.rest_4_ = bf16[64,128,256]{2,1,0:T(8,128)(2,1)} custom-call(s32[1]{0:T(128)} %bitcast._.freq.place_ref, s32[1]{0:T(128)} %bitcast.1.rblk._, s32[1]{0:T(128)} %bitcast.2.__.sblk, bf16[64,128,256]{2,1,0:T(8,128)(2,1)S(1)} %copy-done.1, s32[128,256]{1,0:T(8,128)S(1)} %copy-done.4, bf16[4,128,128]{2,1,0:T(8,128)(2,1)S(1)} %copy-done.5, ...), custom_call_target="tpu_custom_call" | custom-call | flops 33554432 | bytes 8912896 | tf_op jit(solution)/shard_map/pallas_call | solution.py:78
  125.5 2.5 %collective-permute-done.35.rest_1_ = bf16[2,2,32,256]{3,2,1,0:T(8,128)(2,1)S(1)} collective-permute-done((bf16[2,2,32,256]{3,2,1,0:T(8,128)(2,1)S(1)}, bf16[2,2,32,256]{3,2,1,0:T(8,128)(2,1)S(1)}, u32[]{:S(2)}, u32[]{:S(2)}) %collective-permute-start.35) | collective-permute-done | bytes 65568 | tf_op jit(solution)/shard_map/ppermute | solution.py:495
  128.0 1.9 %shard_map.96 = bf16[64,128,256]{2,1,0:T(8,128)(2,1)} custom-call(s32[1]{0:T(128)} %bitcast._.freq.place_ref, s32[1]{0:T(128)} %bitcast.1.rblk._, s32[1]{0:T(128)} %bitcast.2.__.sblk, bf16[64,128,256]{2,1,0:T(8,128)(2,1)S(1)} %copy-done.1, s32[128,256]{1,0:T(8,128)S(1)} %copy-done.4, ...), custom_call_target="tpu_custom_call", output_to_operand_aliasing={{}: (10, {})} | custom-call | flops 33554432 | bytes 13107200 | tf_op jit(solution)/shard_map/pallas_call | solution.py:78
  (89 shorter events, 30.3 us)
Async XLA Ops:
  2.6 21.3 %collective-permute-start.6 = (bf16[2,256,512]{2,1,0:T(8,128)(2,1)S(1)}, bf16[2,256,512]{2,1,0:T(8,128)(2,1)S(1)}, u32[]{:S(2)}, u32[]{:S(2)}) collective-permute-start(bf16[2,256,512]{2,1,0:T(8,128)(2,1)S(1)} %get-tuple-element.66), channel_id=1, source_target_pairs={{0,2},{2,0},{1,3},{3,1},{4,6},{6,4},{5,7},{7,5},{8,10},{10,8},{9,1... | collective-permute-start | bytes 1572872 | tf_op jit(solution)/shard_map/ppermute | solution.py:495
  5.6 26.0 %collective-permute-start.7 = (bf16[2,256,512]{2,1,0:T(8,128)(2,1)S(1)}, bf16[2,256,512]{2,1,0:T(8,128)(2,1)S(1)}, u32[]{:S(2)}, u32[]{:S(2)}) collective-permute-start(bf16[2,256,512]{2,1,0:T(8,128)(2,1)S(1)} %get-tuple-element.69), channel_id=1, source_target_pairs={{0,2},{2,0},{1,3},{3,1},{4,6},{6,4},{5,7},{7,5},{8,10},{10,8},{9,1... | collective-permute-start | bytes 1572872 | tf_op jit(solution)/shard_map/ppermute | solution.py:495
  8.6 12.9 %collective-permute-start.3 = (bf16[2,2,64,256]{3,2,1,0:T(8,128)(2,1)S(1)}, bf16[2,2,64,256]{3,2,1,0:T(8,128)(2,1)S(1)}, u32[]{:S(2)}, u32[]{:S(2)}) collective-permute-start(bf16[2,2,64,256]{3,2,1,0:T(8,128)(2,1)S(1)} %get-tuple-element.59), channel_id=1, source_target_pairs={{0,8},{4,12},{8,0},{12,4},{1,9},{5,13},{9,1},{13,5},{2,10},{6,14},... | collective-permute-start | bytes 393224 | tf_op jit(solution)/shard_map/ppermute | solution.py:495
  11.7 9.8 %collective-permute-start.4 = (bf16[2,2,64,256]{3,2,1,0:T(8,128)(2,1)S(1)}, bf16[2,2,64,256]{3,2,1,0:T(8,128)(2,1)S(1)}, u32[]{:S(2)}, u32[]{:S(2)}) collective-permute-start(bf16[2,2,64,256]{3,2,1,0:T(8,128)(2,1)S(1)} %get-tuple-element.60), channel_id=1, source_target_pairs={{0,12},{4,8},{8,4},{12,0},{1,13},{5,9},{9,5},{13,1},{2,14},{6,10},... | collective-permute-start | bytes 393224 | tf_op jit(solution)/shard_map/ppermute | solution.py:495
  13.1 8.6 %collective-permute-start.5 = (bf16[2,2,64,256]{3,2,1,0:T(8,128)(2,1)S(1)}, bf16[2,2,64,256]{3,2,1,0:T(8,128)(2,1)S(1)}, u32[]{:S(2)}, u32[]{:S(2)}) collective-permute-start(bf16[2,2,64,256]{3,2,1,0:T(8,128)(2,1)S(1)} %get-tuple-element.61), channel_id=1, source_target_pairs={{0,4},{4,0},{8,12},{12,8},{1,5},{5,1},{9,13},{13,9},{2,6},{6,2},{1... | collective-permute-start | bytes 393224 | tf_op jit(solution)/shard_map/ppermute | solution.py:495
  21.8 9.8 %collective-permute-start.8 = (bf16[2,2,64,256]{3,2,1,0:T(8,128)(2,1)S(1)}, bf16[2,2,64,256]{3,2,1,0:T(8,128)(2,1)S(1)}, u32[]{:S(2)}, u32[]{:S(2)}) collective-permute-start(bf16[2,2,64,256]{3,2,1,0:T(8,128)(2,1)S(1)} %get-tuple-element.68.rest_0_), channel_id=1, source_target_pairs={{0,2},{2,0},{1,3},{3,1},{4,6},{6,4},{5,7},{7,5},{8,10},{10,8},{9,1... | collective-permute-start | bytes 393224 | tf_op jit(solution)/shard_map/ppermute | solution.py:495
  23.4 8.2 %collective-permute-start = (bf16[2,256,512]{2,1,0:T(8,128)(2,1)S(1)}, bf16[2,256,512]{2,1,0:T(8,128)(2,1)S(1)}, u32[]{:S(2)}, u32[]{:S(2)}) collective-permute-start(bf16[2,256,512]{2,1,0:T(8,128)(2,1)S(1)} %get-tuple-element.51.rest_1_.rest_0_.rest_2_), channel_id=1, source_target_pairs={{0,1},{1,0},{2,3},{3,2},{4,5},{5,4},{6,7},{7,6},{8,9},{9,8},{10,11... | collective-permute-start | bytes 1572872 | tf_op jit(solution)/shard_map/ppermute | solution.py:495
  23.4 8.2 %collective-permute-start.1 = (bf16[2,256,512]{2,1,0:T(8,128)(2,1)S(1)}, bf16[2,256,512]{2,1,0:T(8,128)(2,1)S(1)}, u32[]{:S(2)}, u32[]{:S(2)}) collective-permute-start(bf16[2,256,512]{2,1,0:T(8,128)(2,1)S(1)} %get-tuple-element.52.rest_3_.rest_2_.rest_4_), channel_id=1, source_target_pairs={{0,1},{1,0},{2,3},{3,2},{4,5},{5,4},{6,7},{7,6},{8,9},{9,8},{10,11... | collective-permute-start | bytes 1572872 | tf_op jit(solution)/shard_map/ppermute | solution.py:495
  23.9 8.5 %collective-permute-start.9 = (bf16[2,256,512]{2,1,0:T(8,128)(2,1)S(1)}, bf16[2,256,512]{2,1,0:T(8,128)(2,1)S(1)}, u32[]{:S(2)}, u32[]{:S(2)}) collective-permute-start(bf16[2,256,512]{2,1,0:T(8,128)(2,1)S(1)} %collective-permute-done.6.rest_2_.rest_0_.rest_3_), channel_id=1, source_target_pairs={{0,1},{1,0},{2,3},{3,2},{4,5},{5,4},{6,7},{7,6},{8,9},{9,8},{10,11... | collective-permute-start | bytes 1572872 | tf_op jit(solution)/shard_map/ppermute | solution.py:495
  34.0 12.9 %collective-permute-start.11 = (bf16[64,1024]{1,0:T(8,128)(2,1)S(1)}, bf16[64,1024]{1,0:T(8,128)(2,1)S(1)}, u32[]{:S(2)}, u32[]{:S(2)}) collective-permute-start(bf16[64,1024]{1,0:T(8,128)(2,1)S(1)} %get-tuple-element.74), channel_id=1, source_target_pairs={{0,8},{4,12},{8,0},{12,4},{1,9},{5,13},{9,1},{13,5},{2,10},{6,14},... | collective-permute-start | bytes 393224 | tf_op jit(solution)/shard_map/ppermute | solution.py:495
  36.9 10.0 %collective-permute-start.12 = (bf16[64,1024]{1,0:T(8,128)(2,1)S(1)}, bf16[64,1024]{1,0:T(8,128)(2,1)S(1)}, u32[]{:S(2)}, u32[]{:S(2)}) collective-permute-start(bf16[64,1024]{1,0:T(8,128)(2,1)S(1)} %get-tuple-element.75), channel_id=1, source_target_pairs={{0,12},{4,8},{8,4},{12,0},{1,13},{5,9},{9,5},{13,1},{2,14},{6,10},... | collective-permute-start | bytes 393224 | tf_op jit(solution)/shard_map/ppermute | solution.py:495
  38.2 9.5 %collective-permute-start.13 = (bf16[64,1024]{1,0:T(8,128)(2,1)S(1)}, bf16[64,1024]{1,0:T(8,128)(2,1)S(1)}, u32[]{:S(2)}, u32[]{:S(2)}) collective-permute-start(bf16[64,1024]{1,0:T(8,128)(2,1)S(1)} %get-tuple-element.76), channel_id=1, source_target_pairs={{0,4},{4,0},{8,12},{12,8},{1,5},{5,1},{9,13},{13,9},{2,6},{6,2},{1... | collective-permute-start | bytes 393224 | tf_op jit(solution)/shard_map/ppermute | solution.py:495
  48.7 13.8 %collective-permute-start.14 = (bf16[64,1024]{1,0:T(8,128)(2,1)S(1)}, bf16[64,1024]{1,0:T(8,128)(2,1)S(1)}, u32[]{:S(2)}, u32[]{:S(2)}) collective-permute-start(bf16[64,1024]{1,0:T(8,128)(2,1)S(1)} %get-tuple-element.78), channel_id=1, source_target_pairs={{0,8},{4,12},{8,0},{12,4},{1,9},{5,13},{9,1},{13,5},{2,10},{6,14},... | collective-permute-start | bytes 393224 | tf_op jit(solution)/shard_map/ppermute | solution.py:495
  52.9 9.6 %collective-permute-start.15 = (bf16[64,1024]{1,0:T(8,128)(2,1)S(1)}, bf16[64,1024]{1,0:T(8,128)(2,1)S(1)}, u32[]{:S(2)}, u32[]{:S(2)}) collective-permute-start(bf16[64,1024]{1,0:T(8,128)(2,1)S(1)} %get-tuple-element.79), channel_id=1, source_target_pairs={{0,12},{4,8},{8,4},{12,0},{1,13},{5,9},{9,5},{13,1},{2,14},{6,10},... | collective-permute-start | bytes 393224 | tf_op jit(solution)/shard_map/ppermute | solution.py:495
  53.3 10.3 %collective-permute-start.16 = (bf16[64,1024]{1,0:T(8,128)(2,1)S(1)}, bf16[64,1024]{1,0:T(8,128)(2,1)S(1)}, u32[]{:S(2)}, u32[]{:S(2)}) collective-permute-start(bf16[64,1024]{1,0:T(8,128)(2,1)S(1)} %get-tuple-element.80), channel_id=1, source_target_pairs={{0,4},{4,0},{8,12},{12,8},{1,5},{5,1},{9,13},{13,9},{2,6},{6,2},{1... | collective-permute-start | bytes 393224 | tf_op jit(solution)/shard_map/ppermute | solution.py:495
  68.4 5.7 %collective-permute-start.18 = (bf16[2,2,32,256]{3,2,1,0:T(8,128)(2,1)S(1)}, bf16[2,2,32,256]{3,2,1,0:T(8,128)(2,1)S(1)}, u32[]{:S(2)}, u32[]{:S(2)}) collective-permute-start(bf16[2,2,32,256]{3,2,1,0:T(8,128)(2,1)S(1)} %shard_map.84.rest_0_), channel_id=1, source_target_pairs={{0,8},{4,12},{8,0},{12,4},{1,9},{5,13},{9,1},{13,5},{2,10},{6,14},... | collective-permute-start | bytes 196616 | tf_op jit(solution)/shard_map/ppermute | solution.py:495
  70.4 6.6 %collective-permute-start.22 = (bf16[2,2,32,256]{3,2,1,0:T(8,128)(2,1)S(1)}, bf16[2,2,32,256]{3,2,1,0:T(8,128)(2,1)S(1)}, u32[]{:S(2)}, u32[]{:S(2)}) collective-permute-start(bf16[2,2,32,256]{3,2,1,0:T(8,128)(2,1)S(1)} %shard_map.86.rest_0_), channel_id=1, source_target_pairs={{0,8},{4,12},{8,0},{12,4},{1,9},{5,13},{9,1},{13,5},{2,10},{6,14},... | collective-permute-start | bytes 196616 | tf_op jit(solution)/shard_map/ppermute | solution.py:495
  71.9 7.1 %collective-permute-start.20 = (bf16[2,2,32,256]{3,2,1,0:T(8,128)(2,1)S(1)}, bf16[2,2,32,256]{3,2,1,0:T(8,128)(2,1)S(1)}, u32[]{:S(2)}, u32[]{:S(2)}) collective-permute-start(bf16[2,2,32,256]{3,2,1,0:T(8,128)(2,1)S(1)} %shard_map.84.rest_0_), channel_id=1, source_target_pairs={{0,4},{4,0},{8,12},{12,8},{1,5},{5,1},{9,13},{13,9},{2,6},{6,2},{1... | collective-permute-start | bytes 196616 | tf_op jit(solution)/shard_map/ppermute | solution.py:495
  74.1 5.1 %collective-permute-start.19 = (bf16[2,2,32,256]{3,2,1,0:T(8,128)(2,1)S(1)}, bf16[2,2,32,256]{3,2,1,0:T(8,128)(2,1)S(1)}, u32[]{:S(2)}, u32[]{:S(2)}) collective-permute-start(bf16[2,2,32,256]{3,2,1,0:T(8,128)(2,1)S(1)} %collective-permute-done.18.rest_1_), channel_id=1, source_target_pairs={{0,4},{4,0},{8,12},{12,8},{1,5},{5,1},{9,13},{13,9},{2,6},{6,2},{1... | collective-permute-start | bytes 196616 | tf_op jit(solution)/shard_map/ppermute | solution.py:495
  87.4 8.8 %collective-permute-start.27 = (bf16[64,1024]{1,0:T(8,128)(2,1)S(1)}, bf16[64,1024]{1,0:T(8,128)(2,1)S(1)}, u32[]{:S(2)}, u32[]{:S(2)}) collective-permute-start(bf16[64,1024]{1,0:T(8,128)(2,1)S(1)} %get-tuple-element.86), channel_id=1, source_target_pairs={{0,8},{4,12},{8,0},{12,4},{1,9},{5,13},{9,1},{13,5},{2,10},{6,14},... | collective-permute-start | bytes 393224 | tf_op jit(solution)/shard_map/ppermute | solution.py:495
  88.2 8.1 %collective-permute-start.28 = (bf16[64,1024]{1,0:T(8,128)(2,1)S(1)}, bf16[64,1024]{1,0:T(8,128)(2,1)S(1)}, u32[]{:S(2)}, u32[]{:S(2)}) collective-permute-start(bf16[64,1024]{1,0:T(8,128)(2,1)S(1)} %get-tuple-element.87), channel_id=1, source_target_pairs={{0,12},{4,8},{8,4},{12,0},{1,13},{5,9},{9,5},{13,1},{2,14},{6,10},... | collective-permute-start | bytes 393224 | tf_op jit(solution)/shard_map/ppermute | solution.py:495
  91.2 6.6 %collective-permute-start.29 = (bf16[64,1024]{1,0:T(8,128)(2,1)S(1)}, bf16[64,1024]{1,0:T(8,128)(2,1)S(1)}, u32[]{:S(2)}, u32[]{:S(2)}) collective-permute-start(bf16[64,1024]{1,0:T(8,128)(2,1)S(1)} %get-tuple-element.88), channel_id=1, source_target_pairs={{0,4},{4,0},{8,12},{12,8},{1,5},{5,1},{9,13},{13,9},{2,6},{6,2},{1... | collective-permute-start | bytes 393224 | tf_op jit(solution)/shard_map/ppermute | solution.py:495
  98.8 5.9 %collective-permute-start.30 = (bf16[64,1024]{1,0:T(8,128)(2,1)S(1)}, bf16[64,1024]{1,0:T(8,128)(2,1)S(1)}, u32[]{:S(2)}, u32[]{:S(2)}) collective-permute-start(bf16[64,1024]{1,0:T(8,128)(2,1)S(1)} %get-tuple-element.90), channel_id=1, source_target_pairs={{0,8},{4,12},{8,0},{12,4},{1,9},{5,13},{9,1},{13,5},{2,10},{6,14},... | collective-permute-start | bytes 393224 | tf_op jit(solution)/shard_map/ppermute | solution.py:495
  100.4 7.9 %collective-permute-start.31 = (bf16[64,1024]{1,0:T(8,128)(2,1)S(1)}, bf16[64,1024]{1,0:T(8,128)(2,1)S(1)}, u32[]{:S(2)}, u32[]{:S(2)}) collective-permute-start(bf16[64,1024]{1,0:T(8,128)(2,1)S(1)} %get-tuple-element.91), channel_id=1, source_target_pairs={{0,12},{4,8},{8,4},{12,0},{1,13},{5,9},{9,5},{13,1},{2,14},{6,10},... | collective-permute-start | bytes 393224 | tf_op jit(solution)/shard_map/ppermute | solution.py:495
  103.8 6.6 %collective-permute-start.32 = (bf16[64,1024]{1,0:T(8,128)(2,1)S(1)}, bf16[64,1024]{1,0:T(8,128)(2,1)S(1)}, u32[]{:S(2)}, u32[]{:S(2)}) collective-permute-start(bf16[64,1024]{1,0:T(8,128)(2,1)S(1)} %get-tuple-element.92), channel_id=1, source_target_pairs={{0,4},{4,0},{8,12},{12,8},{1,5},{5,1},{9,13},{13,9},{2,6},{6,2},{1... | collective-permute-start | bytes 393224 | tf_op jit(solution)/shard_map/ppermute | solution.py:495
  112.7 6.1 %collective-permute-start.33 = (bf16[2,2,32,256]{3,2,1,0:T(8,128)(2,1)S(1)}, bf16[2,2,32,256]{3,2,1,0:T(8,128)(2,1)S(1)}, u32[]{:S(2)}, u32[]{:S(2)}) collective-permute-start(bf16[2,2,32,256]{3,2,1,0:T(8,128)(2,1)S(1)} %get-tuple-element.94), channel_id=1, source_target_pairs={{0,2},{2,0},{1,3},{3,1},{4,6},{6,4},{5,7},{7,5},{8,10},{10,8},{9,1... | collective-permute-start | bytes 196616 | tf_op jit(solution)/shard_map/ppermute | solution.py:495
  115.2 7.8 %collective-permute-start.40 = (bf16[2,2,32,256]{3,2,1,0:T(8,128)(2,1)S(1)}, bf16[2,2,32,256]{3,2,1,0:T(8,128)(2,1)S(1)}, u32[]{:S(2)}, u32[]{:S(2)}) collective-permute-start(bf16[2,2,32,256]{3,2,1,0:T(8,128)(2,1)S(1)} %shard_map.94.rest_3_), channel_id=1, source_target_pairs={{0,8},{4,12},{8,0},{12,4},{1,9},{5,13},{9,1},{13,5},{2,10},{6,14},... | collective-permute-start | bytes 196616 | tf_op jit(solution)/shard_map/ppermute | solution.py:495
  117.4 6.1 %collective-permute-start.39 = (bf16[2,2,32,256]{3,2,1,0:T(8,128)(2,1)S(1)}, bf16[2,2,32,256]{3,2,1,0:T(8,128)(2,1)S(1)}, u32[]{:S(2)}, u32[]{:S(2)}) collective-permute-start(bf16[2,2,32,256]{3,2,1,0:T(8,128)(2,1)S(1)} %shard_map.94.rest_3_), channel_id=1, source_target_pairs={{0,12},{4,8},{8,4},{12,0},{1,13},{5,9},{9,5},{13,1},{2,14},{6,10},... | collective-permute-start | bytes 196616 | tf_op jit(solution)/shard_map/ppermute | solution.py:495
  118.5 5.0 %collective-permute-start.38 = (bf16[2,2,32,256]{3,2,1,0:T(8,128)(2,1)S(1)}, bf16[2,2,32,256]{3,2,1,0:T(8,128)(2,1)S(1)}, u32[]{:S(2)}, u32[]{:S(2)}) collective-permute-start(bf16[2,2,32,256]{3,2,1,0:T(8,128)(2,1)S(1)} %shard_map.94.rest_3_), channel_id=1, source_target_pairs={{0,4},{4,0},{8,12},{12,8},{1,5},{5,1},{9,13},{13,9},{2,6},{6,2},{1... | collective-permute-start | bytes 196616 | tf_op jit(solution)/shard_map/ppermute | solution.py:495
  118.8 6.6 %collective-permute-start.36 = (bf16[2,2,32,256]{3,2,1,0:T(8,128)(2,1)S(1)}, bf16[2,2,32,256]{3,2,1,0:T(8,128)(2,1)S(1)}, u32[]{:S(2)}, u32[]{:S(2)}) collective-permute-start(bf16[2,2,32,256]{3,2,1,0:T(8,128)(2,1)S(1)} %shard_map.93.rest_3_), channel_id=1, source_target_pairs={{0,8},{4,12},{8,0},{12,4},{1,9},{5,13},{9,1},{13,5},{2,10},{6,14},... | collective-permute-start | bytes 196616 | tf_op jit(solution)/shard_map/ppermute | solution.py:495
  121.9 6.1 %collective-permute-start.35 = (bf16[2,2,32,256]{3,2,1,0:T(8,128)(2,1)S(1)}, bf16[2,2,32,256]{3,2,1,0:T(8,128)(2,1)S(1)}, u32[]{:S(2)}, u32[]{:S(2)}) collective-permute-start(bf16[2,2,32,256]{3,2,1,0:T(8,128)(2,1)S(1)} %shard_map.93.rest_3_), channel_id=1, source_target_pairs={{0,12},{4,8},{8,4},{12,0},{1,13},{5,9},{9,5},{13,1},{2,14},{6,10},... | collective-permute-start | bytes 196616 | tf_op jit(solution)/shard_map/ppermute | solution.py:495
  123.0 5.0 %collective-permute-start.34 = (bf16[2,2,32,256]{3,2,1,0:T(8,128)(2,1)S(1)}, bf16[2,2,32,256]{3,2,1,0:T(8,128)(2,1)S(1)}, u32[]{:S(2)}, u32[]{:S(2)}) collective-permute-start(bf16[2,2,32,256]{3,2,1,0:T(8,128)(2,1)S(1)} %shard_map.93.rest_3_), channel_id=1, source_target_pairs={{0,4},{4,0},{8,12},{12,8},{1,5},{5,1},{9,13},{13,9},{2,6},{6,2},{1... | collective-permute-start | bytes 196616 | tf_op jit(solution)/shard_map/ppermute | solution.py:495
  (16 other events, 166.5 us)

commit v23 on v18

--- a/solution.py
+++ b/solution.py
@@ -163,15 +163,17 @@
     per_dev, _, src, rcv = response.shape
     half = src // 2
     width = half // PARTS
+    aperture = jnp.swapaxes(aperture, 1, 2)
 
     def body(_, rblk, __, flags, x_ref, *outs):
         lane = lax.broadcasted_iota(jnp.int32, (1, rcv), 1) // BLOCK
+        spot = lax.broadcasted_iota(jnp.int32, aperture.shape[1:], 1)
         for flip in (1, 0):
             for j in range(per_dev):
                 for step in range(half // BLOCK):
                     block = (rblk[0] ^ flip) * (half // BLOCK) + step
-                    on = flags[j, pl.ds(block, 1), :].astype(F32)
-                    row = sum(jnp.where(lane == r, on[:, r : r + 1], 0.0) for r in range(rcv // BLOCK))
+                    on = jnp.sum(jnp.where(spot == block, flags[j].astype(F32), 0.0), 1, keepdims=True)
+                    row = sum(jnp.where(lane == r, on[r : r + 1, :], 0.0) for r in range(rcv // BLOCK))
                     gate = jnp.broadcast_to(row, (BLOCK, rcv)).astype(BF16)
                     rows = pl.ds(pl.multiple_of(block * BLOCK, BLOCK), BLOCK)
                     part, at = divmod(step * BLOCK, width)

time: 131 us -> 131 us (level)
    unnamed x15 -> x16, local copies, waits for them, and re-layouts: 4.56 us -> 4.48 us
where the time goes in v23:
time: 131 us; the launch traced here: 130 us
  waiting for transfers between devices  58.9 us (45%)
  starting transfers between devices  53.3 us (41%)
  Pallas kernels  13.5 us (10%)
  local copies, waits for them, and re-layouts  4.48 us (3%)
    ppermute x41, waiting for transfers between devices, exchanged(): lax.ppermute(value, axis, [(i, i ^ step) for i in range(lax.axis_size(axi...  58.9 us
    ppermute x41, starting transfers between devices, exchanged(): lax.ppermute(value, axis, [(i, i ^ step) for i in range(lax.axis_size(axi...  53.3 us
    pallas_call x24, Pallas kernels, call(): pl.pallas_call(body, grid_spec=pltpu.PrefetchScalarGridSpec(num_scalar_pr...  13.5 us
    unnamed x16, local copies, waits for them, and re-layouts  4.48 us
  transfers between devices with their start and end apart: 41, of which 24 were waited for; matrix products, arithmetic and copies ran while one was open for 0% of the time, Pallas kernels for 6%

profile of v23, /device:TPU:0, one launch (start us, length us, event | category | flops | bytes accessed | tf_op | source)
XLA Modules:
  0.0 130.5 jit_solution(10625299981403470485)
XLA Ops:
  0.0 1.6 %copy-done.2 = bf16[2,2,1024,256]{3,2,1,0:T(8,128)(2,1)S(1)} copy-done((bf16[2,2,1024,256]{3,2,1,0:T(8,128)(2,1)S(1)}, bf16[2,2,1024,256]{3,2,1,0:T(8,128)(2,1)}, u32[]{:S(2)}) %copy-start.2) | copy-done | bytes 2097176
  2.5 3.0 %collective-permute-start.6 = (bf16[2,256,512]{2,1,0:T(8,128)(2,1)S(1)}, bf16[2,256,512]{2,1,0:T(8,128)(2,1)S(1)}, u32[]{:S(2)}, u32[]{:S(2)}) collective-permute-start(bf16[2,256,512]{2,1,0:T(8,128)(2,1)S(1)} %get-tuple-element.66), channel_id=1, source_target_pairs={{0,2},{2,0},{1,3},{3,1},{4,6},{6,4},{5,7},{7,5},{8,10},{10,8},{9,1... | collective-permute-start | bytes 1572872 | tf_op jit(solution)/shard_map/ppermute | solution.py:497
  5.6 2.2 %copy-done = bf16[64,128,256]{2,1,0:T(8,128)(2,1)S(1)} copy-done((bf16[64,128,256]{2,1,0:T(8,128)(2,1)S(1)}, bf16[64,128,256]{2,1,0:T(8,128)(2,1)}, u32[]{:S(2)}) %copy-start) | copy-done | bytes 4194328
  8.6 3.1 %collective-permute-start.3 = (bf16[2,2,64,256]{3,2,1,0:T(8,128)(2,1)S(1)}, bf16[2,2,64,256]{3,2,1,0:T(8,128)(2,1)S(1)}, u32[]{:S(2)}, u32[]{:S(2)}) collective-permute-start(bf16[2,2,64,256]{3,2,1,0:T(8,128)(2,1)S(1)} %get-tuple-element.59), channel_id=1, source_target_pairs={{0,8},{4,12},{8,0},{12,4},{1,9},{5,13},{9,1},{13,5},{2,10},{6,14},... | collective-permute-start | bytes 393224 | tf_op jit(solution)/shard_map/ppermute | solution.py:497
  13.2 8.2 %collective-permute-done.3.refs_1_ = bf16[2,2,64,256]{3,2,1,0:T(8,128)(2,1)S(1)} collective-permute-done((bf16[2,2,64,256]{3,2,1,0:T(8,128)(2,1)S(1)}, bf16[2,2,64,256]{3,2,1,0:T(8,128)(2,1)S(1)}, u32[]{:S(2)}, u32[]{:S(2)}) %collective-permute-start.3) | collective-permute-done | bytes 131104 | tf_op jit(solution)/shard_map/ppermute | solution.py:497
  21.7 1.6 %collective-permute-start.8 = (bf16[2,2,64,256]{3,2,1,0:T(8,128)(2,1)S(1)}, bf16[2,2,64,256]{3,2,1,0:T(8,128)(2,1)S(1)}, u32[]{:S(2)}, u32[]{:S(2)}) collective-permute-start(bf16[2,2,64,256]{3,2,1,0:T(8,128)(2,1)S(1)} %get-tuple-element.68.rest_0_), channel_id=1, source_target_pairs={{0,2},{2,0},{1,3},{3,1},{4,6},{6,4},{5,7},{7,5},{8,10},{10,8},{9,1... | collective-permute-start | bytes 393224 | tf_op jit(solution)/shard_map/ppermute | solution.py:497
  23.9 7.6 %collective-permute-done.8.rest_1_ = bf16[2,2,64,256]{3,2,1,0:T(8,128)(2,1)S(1)} collective-permute-done((bf16[2,2,64,256]{3,2,1,0:T(8,128)(2,1)S(1)}, bf16[2,2,64,256]{3,2,1,0:T(8,128)(2,1)S(1)}, u32[]{:S(2)}, u32[]{:S(2)}) %collective-permute-start.8) | collective-permute-done | bytes 131104 | tf_op jit(solution)/shard_map/ppermute | solution.py:497
  33.9 2.9 %collective-permute-start.11 = (bf16[64,1024]{1,0:T(8,128)(2,1)S(1)}, bf16[64,1024]{1,0:T(8,128)(2,1)S(1)}, u32[]{:S(2)}, u32[]{:S(2)}) collective-permute-start(bf16[64,1024]{1,0:T(8,128)(2,1)S(1)} %get-tuple-element.74), channel_id=1, source_target_pairs={{0,8},{4,12},{8,0},{12,4},{1,9},{5,13},{9,1},{13,5},{2,10},{6,14},... | collective-permute-start | bytes 393224 | tf_op jit(solution)/shard_map/ppermute | solution.py:497
  41.0 5.8 %collective-permute-done.11.rest_1_ = bf16[64,1024]{1,0:T(8,128)(2,1)S(1)} collective-permute-done((bf16[64,1024]{1,0:T(8,128)(2,1)S(1)}, bf16[64,1024]{1,0:T(8,128)(2,1)S(1)}, u32[]{:S(2)}, u32[]{:S(2)}) %collective-permute-start.11) | collective-permute-done | bytes 131104 | tf_op jit(solution)/shard_map/ppermute | solution.py:497
  48.3 4.2 %collective-permute-start.14 = (bf16[64,1024]{1,0:T(8,128)(2,1)S(1)}, bf16[64,1024]{1,0:T(8,128)(2,1)S(1)}, u32[]{:S(2)}, u32[]{:S(2)}) collective-permute-start(bf16[64,1024]{1,0:T(8,128)(2,1)S(1)} %get-tuple-element.78), channel_id=1, source_target_pairs={{0,8},{4,12},{8,0},{12,4},{1,9},{5,13},{9,1},{13,5},{2,10},{6,14},... | collective-permute-start | bytes 393224 | tf_op jit(solution)/shard_map/ppermute | solution.py:497
  53.1 9.0 %collective-permute-done.14.rest_5_ = bf16[64,1024]{1,0:T(8,128)(2,1)S(1)} collective-permute-done((bf16[64,1024]{1,0:T(8,128)(2,1)S(1)}, bf16[64,1024]{1,0:T(8,128)(2,1)S(1)}, u32[]{:S(2)}, u32[]{:S(2)}) %collective-permute-start.14) | collective-permute-done | bytes 131104 | tf_op jit(solution)/shard_map/ppermute | solution.py:497
  63.7 1.6 %collective-permute-start.17 = (bf16[2,2,32,256]{3,2,1,0:T(8,128)(2,1)S(1)}, bf16[2,2,32,256]{3,2,1,0:T(8,128)(2,1)S(1)}, u32[]{:S(2)}, u32[]{:S(2)}) collective-permute-start(bf16[2,2,32,256]{3,2,1,0:T(8,128)(2,1)S(1)} %get-tuple-element.82), channel_id=1, source_target_pairs={{0,2},{2,0},{1,3},{3,1},{4,6},{6,4},{5,7},{7,5},{8,10},{10,8},{9,1... | collective-permute-start | bytes 196616 | tf_op jit(solution)/shard_map/ppermute | solution.py:497
  66.2 1.8 %collective-permute-done.17.r_ref = bf16[2,2,32,256]{3,2,1,0:T(8,128)(2,1)S(1)} collective-permute-done((bf16[2,2,32,256]{3,2,1,0:T(8,128)(2,1)S(1)}, bf16[2,2,32,256]{3,2,1,0:T(8,128)(2,1)S(1)}, u32[]{:S(2)}, u32[]{:S(2)}) %collective-permute-start.17) | collective-permute-done | bytes 65568 | tf_op jit(solution)/shard_map/ppermute | solution.py:497
  68.0 1.9 %collective-permute-start.18 = (bf16[2,2,32,256]{3,2,1,0:T(8,128)(2,1)S(1)}, bf16[2,2,32,256]{3,2,1,0:T(8,128)(2,1)S(1)}, u32[]{:S(2)}, u32[]{:S(2)}) collective-permute-start(bf16[2,2,32,256]{3,2,1,0:T(8,128)(2,1)S(1)} %shard_map.84.rest_0_), channel_id=1, source_target_pairs={{0,8},{4,12},{8,0},{12,4},{1,9},{5,13},{9,1},{13,5},{2,10},{6,14},... | collective-permute-start | bytes 196616 | tf_op jit(solution)/shard_map/ppermute | solution.py:497
  70.0 1.5 %collective-permute-start.22 = (bf16[2,2,32,256]{3,2,1,0:T(8,128)(2,1)S(1)}, bf16[2,2,32,256]{3,2,1,0:T(8,128)(2,1)S(1)}, u32[]{:S(2)}, u32[]{:S(2)}) collective-permute-start(bf16[2,2,32,256]{3,2,1,0:T(8,128)(2,1)S(1)} %shard_map.86.rest_0_), channel_id=1, source_target_pairs={{0,8},{4,12},{8,0},{12,4},{1,9},{5,13},{9,1},{13,5},{2,10},{6,14},... | collective-permute-start | bytes 196616 | tf_op jit(solution)/shard_map/ppermute | solution.py:497
  71.4 2.3 %collective-permute-start.20 = (bf16[2,2,32,256]{3,2,1,0:T(8,128)(2,1)S(1)}, bf16[2,2,32,256]{3,2,1,0:T(8,128)(2,1)S(1)}, u32[]{:S(2)}, u32[]{:S(2)}) collective-permute-start(bf16[2,2,32,256]{3,2,1,0:T(8,128)(2,1)S(1)} %shard_map.84.rest_0_), channel_id=1, source_target_pairs={{0,4},{4,0},{8,12},{12,8},{1,5},{5,1},{9,13},{13,9},{2,6},{6,2},{1... | collective-permute-start | bytes 196616 | tf_op jit(solution)/shard_map/ppermute | solution.py:497
  73.7 2.8 %collective-permute-start.19 = (bf16[2,2,32,256]{3,2,1,0:T(8,128)(2,1)S(1)}, bf16[2,2,32,256]{3,2,1,0:T(8,128)(2,1)S(1)}, u32[]{:S(2)}, u32[]{:S(2)}) collective-permute-start(bf16[2,2,32,256]{3,2,1,0:T(8,128)(2,1)S(1)} %collective-permute-done.18.rest_1_), channel_id=1, source_target_pairs={{0,4},{4,0},{8,12},{12,8},{1,5},{5,1},{9,13},{13,9},{2,6},{6,2},{1... | collective-permute-start | bytes 196616 | tf_op jit(solution)/shard_map/ppermute | solution.py:497
  76.6 2.0 %collective-permute-start.23 = (bf16[2,2,32,256]{3,2,1,0:T(8,128)(2,1)S(1)}, bf16[2,2,32,256]{3,2,1,0:T(8,128)(2,1)S(1)}, u32[]{:S(2)}, u32[]{:S(2)}) collective-permute-start(bf16[2,2,32,256]{3,2,1,0:T(8,128)(2,1)S(1)} %collective-permute-done.22.rest_1_), channel_id=1, source_target_pairs={{0,4},{4,0},{8,12},{12,8},{1,5},{5,1},{9,13},{13,9},{2,6},{6,2},{1... | collective-permute-start | bytes 196616 | tf_op jit(solution)/shard_map/ppermute | solution.py:497
  83.7 2.4 %collective-permute-done.26.rest_2_ = bf16[2,2,32,256]{3,2,1,0:T(8,128)(2,1)S(1)} collective-permute-done((bf16[2,2,32,256]{3,2,1,0:T(8,128)(2,1)S(1)}, bf16[2,2,32,256]{3,2,1,0:T(8,128)(2,1)S(1)}, u32[]{:S(2)}, u32[]{:S(2)}) %collective-permute-start.26) | collective-permute-done | bytes 65568 | tf_op jit(solution)/shard_map/ppermute | solution.py:497
  87.7 3.0 %collective-permute-start.28 = (bf16[64,1024]{1,0:T(8,128)(2,1)S(1)}, bf16[64,1024]{1,0:T(8,128)(2,1)S(1)}, u32[]{:S(2)}, u32[]{:S(2)}) collective-permute-start(bf16[64,1024]{1,0:T(8,128)(2,1)S(1)} %get-tuple-element.87), channel_id=1, source_target_pairs={{0,12},{4,8},{8,4},{12,0},{1,13},{5,9},{9,5},{13,1},{2,14},{6,10},... | collective-permute-start | bytes 393224 | tf_op jit(solution)/shard_map/ppermute | solution.py:497
  90.7 5.1 %collective-permute-done.27.rest_1_ = bf16[64,1024]{1,0:T(8,128)(2,1)S(1)} collective-permute-done((bf16[64,1024]{1,0:T(8,128)(2,1)S(1)}, bf16[64,1024]{1,0:T(8,128)(2,1)S(1)}, u32[]{:S(2)}, u32[]{:S(2)}) %collective-permute-start.27) | collective-permute-done | bytes 131104 | tf_op jit(solution)/shard_map/ppermute | solution.py:497
  95.8 1.7 %collective-permute-done.29.rest_3_ = bf16[64,1024]{1,0:T(8,128)(2,1)S(1)} collective-permute-done((bf16[64,1024]{1,0:T(8,128)(2,1)S(1)}, bf16[64,1024]{1,0:T(8,128)(2,1)S(1)}, u32[]{:S(2)}, u32[]{:S(2)}) %collective-permute-start.29) | collective-permute-done | bytes 131104 | tf_op jit(solution)/shard_map/ppermute | solution.py:497
  98.2 4.4 %collective-permute-start.30 = (bf16[64,1024]{1,0:T(8,128)(2,1)S(1)}, bf16[64,1024]{1,0:T(8,128)(2,1)S(1)}, u32[]{:S(2)}, u32[]{:S(2)}) collective-permute-start(bf16[64,1024]{1,0:T(8,128)(2,1)S(1)} %get-tuple-element.90), channel_id=1, source_target_pairs={{0,8},{4,12},{8,0},{12,4},{1,9},{5,13},{9,1},{13,5},{2,10},{6,14},... | collective-permute-start | bytes 393224 | tf_op jit(solution)/shard_map/ppermute | solution.py:497
  102.7 2.1 %collective-permute-start.31 = (bf16[64,1024]{1,0:T(8,128)(2,1)S(1)}, bf16[64,1024]{1,0:T(8,128)(2,1)S(1)}, u32[]{:S(2)}, u32[]{:S(2)}) collective-permute-start(bf16[64,1024]{1,0:T(8,128)(2,1)S(1)} %get-tuple-element.91), channel_id=1, source_target_pairs={{0,12},{4,8},{8,4},{12,0},{1,13},{5,9},{9,5},{13,1},{2,14},{6,10},... | collective-permute-start | bytes 393224 | tf_op jit(solution)/shard_map/ppermute | solution.py:497
  105.6 4.0 %collective-permute-done.31.rest_6_ = bf16[64,1024]{1,0:T(8,128)(2,1)S(1)} collective-permute-done((bf16[64,1024]{1,0:T(8,128)(2,1)S(1)}, bf16[64,1024]{1,0:T(8,128)(2,1)S(1)}, u32[]{:S(2)}, u32[]{:S(2)}) %collective-permute-start.31) | collective-permute-done | bytes 131104 | tf_op jit(solution)/shard_map/ppermute | solution.py:497
  109.6 2.6 %collective-permute-done.32.rest_7_ = bf16[64,1024]{1,0:T(8,128)(2,1)S(1)} collective-permute-done((bf16[64,1024]{1,0:T(8,128)(2,1)S(1)}, bf16[64,1024]{1,0:T(8,128)(2,1)S(1)}, u32[]{:S(2)}, u32[]{:S(2)}) %collective-permute-start.32) | collective-permute-done | bytes 131104 | tf_op jit(solution)/shard_map/ppermute | solution.py:497
  112.7 2.0 %collective-permute-start.33 = (bf16[2,2,32,256]{3,2,1,0:T(8,128)(2,1)S(1)}, bf16[2,2,32,256]{3,2,1,0:T(8,128)(2,1)S(1)}, u32[]{:S(2)}, u32[]{:S(2)}) collective-permute-start(bf16[2,2,32,256]{3,2,1,0:T(8,128)(2,1)S(1)} %get-tuple-element.94), channel_id=1, source_target_pairs={{0,2},{2,0},{1,3},{3,1},{4,6},{6,4},{5,7},{7,5},{8,10},{10,8},{9,1... | collective-permute-start | bytes 196616 | tf_op jit(solution)/shard_map/ppermute | solution.py:497
  115.2 1.8 %collective-permute-done.37.r_ref = bf16[2,2,32,256]{3,2,1,0:T(8,128)(2,1)S(1)} collective-permute-done((bf16[2,2,32,256]{3,2,1,0:T(8,128)(2,1)S(1)}, bf16[2,2,32,256]{3,2,1,0:T(8,128)(2,1)S(1)}, u32[]{:S(2)}, u32[]{:S(2)}) %collective-permute-start.37) | collective-permute-done | bytes 65568 | tf_op jit(solution)/shard_map/ppermute | solution.py:497
  117.7 2.4 %collective-permute-start.34 = (bf16[2,2,32,256]{3,2,1,0:T(8,128)(2,1)S(1)}, bf16[2,2,32,256]{3,2,1,0:T(8,128)(2,1)S(1)}, u32[]{:S(2)}, u32[]{:S(2)}) collective-permute-start(bf16[2,2,32,256]{3,2,1,0:T(8,128)(2,1)S(1)} %shard_map.93.rest_0_), channel_id=1, source_target_pairs={{0,8},{4,12},{8,0},{12,4},{1,9},{5,13},{9,1},{13,5},{2,10},{6,14},... | collective-permute-start | bytes 196616 | tf_op jit(solution)/shard_map/ppermute | solution.py:497
  122.2 2.0 %collective-permute-start.36 = (bf16[2,2,32,256]{3,2,1,0:T(8,128)(2,1)S(1)}, bf16[2,2,32,256]{3,2,1,0:T(8,128)(2,1)S(1)}, u32[]{:S(2)}, u32[]{:S(2)}) collective-permute-start(bf16[2,2,32,256]{3,2,1,0:T(8,128)(2,1)S(1)} %shard_map.93.rest_0_), channel_id=1, source_target_pairs={{0,4},{4,0},{8,12},{12,8},{1,5},{5,1},{9,13},{13,9},{2,6},{6,2},{1... | collective-permute-start | bytes 196616 | tf_op jit(solution)/shard_map/ppermute | solution.py:497
  126.5 1.9 %shard_map.95.rest_4_ = bf16[64,128,256]{2,1,0:T(8,128)(2,1)} custom-call(s32[1]{0:T(128)} %bitcast._.freq.place_ref, s32[1]{0:T(128)} %bitcast.1.rblk._, s32[1]{0:T(128)} %bitcast.2.__.sblk, bf16[64,128,256]{2,1,0:T(8,128)(2,1)S(1)} %copy-done.1, s32[128,256]{1,0:T(8,128)S(1)} %copy-done.4, bf16[4,128,128]{2,1,0:T(8,128)(2,1)S(1)} %copy-done.5, ...), custom_call_target="tpu_custom_call" | custom-call | flops 33554432 | bytes 8912896 | tf_op jit(solution)/shard_map/pallas_call | solution.py:78
  128.5 1.9 %shard_map.96 = bf16[64,128,256]{2,1,0:T(8,128)(2,1)} custom-call(s32[1]{0:T(128)} %bitcast._.freq.place_ref, s32[1]{0:T(128)} %bitcast.1.rblk._, s32[1]{0:T(128)} %bitcast.2.__.sblk, bf16[64,128,256]{2,1,0:T(8,128)(2,1)S(1)} %copy-done.1, s32[128,256]{1,0:T(8,128)S(1)} %copy-done.4, ...), custom_call_target="tpu_custom_call", output_to_operand_aliasing={{}: (10, {})} | custom-call | flops 33554432 | bytes 13107200 | tf_op jit(solution)/shard_map/pallas_call | solution.py:78
  (90 shorter events, 29.9 us)
Async XLA Ops:
  2.5 21.3 %collective-permute-start.6 = (bf16[2,256,512]{2,1,0:T(8,128)(2,1)S(1)}, bf16[2,256,512]{2,1,0:T(8,128)(2,1)S(1)}, u32[]{:S(2)}, u32[]{:S(2)}) collective-permute-start(bf16[2,256,512]{2,1,0:T(8,128)(2,1)S(1)} %get-tuple-element.66), channel_id=1, source_target_pairs={{0,2},{2,0},{1,3},{3,1},{4,6},{6,4},{5,7},{7,5},{8,10},{10,8},{9,1... | collective-permute-start | bytes 1572872 | tf_op jit(solution)/shard_map/ppermute | solution.py:497
  5.5 26.0 %collective-permute-start.7 = (bf16[2,256,512]{2,1,0:T(8,128)(2,1)S(1)}, bf16[2,256,512]{2,1,0:T(8,128)(2,1)S(1)}, u32[]{:S(2)}, u32[]{:S(2)}) collective-permute-start(bf16[2,256,512]{2,1,0:T(8,128)(2,1)S(1)} %get-tuple-element.69), channel_id=1, source_target_pairs={{0,2},{2,0},{1,3},{3,1},{4,6},{6,4},{5,7},{7,5},{8,10},{10,8},{9,1... | collective-permute-start | bytes 1572872 | tf_op jit(solution)/shard_map/ppermute | solution.py:497
  8.6 12.9 %collective-permute-start.3 = (bf16[2,2,64,256]{3,2,1,0:T(8,128)(2,1)S(1)}, bf16[2,2,64,256]{3,2,1,0:T(8,128)(2,1)S(1)}, u32[]{:S(2)}, u32[]{:S(2)}) collective-permute-start(bf16[2,2,64,256]{3,2,1,0:T(8,128)(2,1)S(1)} %get-tuple-element.59), channel_id=1, source_target_pairs={{0,8},{4,12},{8,0},{12,4},{1,9},{5,13},{9,1},{13,5},{2,10},{6,14},... | collective-permute-start | bytes 393224 | tf_op jit(solution)/shard_map/ppermute | solution.py:497
  11.7 9.8 %collective-permute-start.4 = (bf16[2,2,64,256]{3,2,1,0:T(8,128)(2,1)S(1)}, bf16[2,2,64,256]{3,2,1,0:T(8,128)(2,1)S(1)}, u32[]{:S(2)}, u32[]{:S(2)}) collective-permute-start(bf16[2,2,64,256]{3,2,1,0:T(8,128)(2,1)S(1)} %get-tuple-element.60), channel_id=1, source_target_pairs={{0,12},{4,8},{8,4},{12,0},{1,13},{5,9},{9,5},{13,1},{2,14},{6,10},... | collective-permute-start | bytes 393224 | tf_op jit(solution)/shard_map/ppermute | solution.py:497
  13.0 8.6 %collective-permute-start.5 = (bf16[2,2,64,256]{3,2,1,0:T(8,128)(2,1)S(1)}, bf16[2,2,64,256]{3,2,1,0:T(8,128)(2,1)S(1)}, u32[]{:S(2)}, u32[]{:S(2)}) collective-permute-start(bf16[2,2,64,256]{3,2,1,0:T(8,128)(2,1)S(1)} %get-tuple-element.61), channel_id=1, source_target_pairs={{0,4},{4,0},{8,12},{12,8},{1,5},{5,1},{9,13},{13,9},{2,6},{6,2},{1... | collective-permute-start | bytes 393224 | tf_op jit(solution)/shard_map/ppermute | solution.py:497
  21.7 9.8 %collective-permute-start.8 = (bf16[2,2,64,256]{3,2,1,0:T(8,128)(2,1)S(1)}, bf16[2,2,64,256]{3,2,1,0:T(8,128)(2,1)S(1)}, u32[]{:S(2)}, u32[]{:S(2)}) collective-permute-start(bf16[2,2,64,256]{3,2,1,0:T(8,128)(2,1)S(1)} %get-tuple-element.68.rest_0_), channel_id=1, source_target_pairs={{0,2},{2,0},{1,3},{3,1},{4,6},{6,4},{5,7},{7,5},{8,10},{10,8},{9,1... | collective-permute-start | bytes 393224 | tf_op jit(solution)/shard_map/ppermute | solution.py:497
  23.3 8.2 %collective-permute-start = (bf16[2,256,512]{2,1,0:T(8,128)(2,1)S(1)}, bf16[2,256,512]{2,1,0:T(8,128)(2,1)S(1)}, u32[]{:S(2)}, u32[]{:S(2)}) collective-permute-start(bf16[2,256,512]{2,1,0:T(8,128)(2,1)S(1)} %get-tuple-element.51.rest_1_.rest_0_.rest_2_), channel_id=1, source_target_pairs={{0,1},{1,0},{2,3},{3,2},{4,5},{5,4},{6,7},{7,6},{8,9},{9,8},{10,11... | collective-permute-start | bytes 1572872 | tf_op jit(solution)/shard_map/ppermute | solution.py:497
  23.3 8.2 %collective-permute-start.1 = (bf16[2,256,512]{2,1,0:T(8,128)(2,1)S(1)}, bf16[2,256,512]{2,1,0:T(8,128)(2,1)S(1)}, u32[]{:S(2)}, u32[]{:S(2)}) collective-permute-start(bf16[2,256,512]{2,1,0:T(8,128)(2,1)S(1)} %get-tuple-element.52.rest_3_.rest_2_.rest_4_), channel_id=1, source_target_pairs={{0,1},{1,0},{2,3},{3,2},{4,5},{5,4},{6,7},{7,6},{8,9},{9,8},{10,11... | collective-permute-start | bytes 1572872 | tf_op jit(solution)/shard_map/ppermute | solution.py:497
  23.8 8.5 %collective-permute-start.9 = (bf16[2,256,512]{2,1,0:T(8,128)(2,1)S(1)}, bf16[2,256,512]{2,1,0:T(8,128)(2,1)S(1)}, u32[]{:S(2)}, u32[]{:S(2)}) collective-permute-start(bf16[2,256,512]{2,1,0:T(8,128)(2,1)S(1)} %collective-permute-done.6.rest_2_.rest_0_.rest_3_), channel_id=1, source_target_pairs={{0,1},{1,0},{2,3},{3,2},{4,5},{5,4},{6,7},{7,6},{8,9},{9,8},{10,11... | collective-permute-start | bytes 1572872 | tf_op jit(solution)/shard_map/ppermute | solution.py:497
  33.9 12.9 %collective-permute-start.11 = (bf16[64,1024]{1,0:T(8,128)(2,1)S(1)}, bf16[64,1024]{1,0:T(8,128)(2,1)S(1)}, u32[]{:S(2)}, u32[]{:S(2)}) collective-permute-start(bf16[64,1024]{1,0:T(8,128)(2,1)S(1)} %get-tuple-element.74), channel_id=1, source_target_pairs={{0,8},{4,12},{8,0},{12,4},{1,9},{5,13},{9,1},{13,5},{2,10},{6,14},... | collective-permute-start | bytes 393224 | tf_op jit(solution)/shard_map/ppermute | solution.py:497
  36.8 10.0 %collective-permute-start.12 = (bf16[64,1024]{1,0:T(8,128)(2,1)S(1)}, bf16[64,1024]{1,0:T(8,128)(2,1)S(1)}, u32[]{:S(2)}, u32[]{:S(2)}) collective-permute-start(bf16[64,1024]{1,0:T(8,128)(2,1)S(1)} %get-tuple-element.75), channel_id=1, source_target_pairs={{0,12},{4,8},{8,4},{12,0},{1,13},{5,9},{9,5},{13,1},{2,14},{6,10},... | collective-permute-start | bytes 393224 | tf_op jit(solution)/shard_map/ppermute | solution.py:497
  38.2 9.4 %collective-permute-start.13 = (bf16[64,1024]{1,0:T(8,128)(2,1)S(1)}, bf16[64,1024]{1,0:T(8,128)(2,1)S(1)}, u32[]{:S(2)}, u32[]{:S(2)}) collective-permute-start(bf16[64,1024]{1,0:T(8,128)(2,1)S(1)} %get-tuple-element.76), channel_id=1, source_target_pairs={{0,4},{4,0},{8,12},{12,8},{1,5},{5,1},{9,13},{13,9},{2,6},{6,2},{1... | collective-permute-start | bytes 393224 | tf_op jit(solution)/shard_map/ppermute | solution.py:497
  48.3 13.8 %collective-permute-start.14 = (bf16[64,1024]{1,0:T(8,128)(2,1)S(1)}, bf16[64,1024]{1,0:T(8,128)(2,1)S(1)}, u32[]{:S(2)}, u32[]{:S(2)}) collective-permute-start(bf16[64,1024]{1,0:T(8,128)(2,1)S(1)} %get-tuple-element.78), channel_id=1, source_target_pairs={{0,8},{4,12},{8,0},{12,4},{1,9},{5,13},{9,1},{13,5},{2,10},{6,14},... | collective-permute-start | bytes 393224 | tf_op jit(solution)/shard_map/ppermute | solution.py:497
  52.5 9.6 %collective-permute-start.15 = (bf16[64,1024]{1,0:T(8,128)(2,1)S(1)}, bf16[64,1024]{1,0:T(8,128)(2,1)S(1)}, u32[]{:S(2)}, u32[]{:S(2)}) collective-permute-start(bf16[64,1024]{1,0:T(8,128)(2,1)S(1)} %get-tuple-element.79), channel_id=1, source_target_pairs={{0,12},{4,8},{8,4},{12,0},{1,13},{5,9},{9,5},{13,1},{2,14},{6,10},... | collective-permute-start | bytes 393224 | tf_op jit(solution)/shard_map/ppermute | solution.py:497
  52.9 10.3 %collective-permute-start.16 = (bf16[64,1024]{1,0:T(8,128)(2,1)S(1)}, bf16[64,1024]{1,0:T(8,128)(2,1)S(1)}, u32[]{:S(2)}, u32[]{:S(2)}) collective-permute-start(bf16[64,1024]{1,0:T(8,128)(2,1)S(1)} %get-tuple-element.80), channel_id=1, source_target_pairs={{0,4},{4,0},{8,12},{12,8},{1,5},{5,1},{9,13},{13,9},{2,6},{6,2},{1... | collective-permute-start | bytes 393224 | tf_op jit(solution)/shard_map/ppermute | solution.py:497
  65.2 4.7 %collective-permute-start.21 = (bf16[2,2,32,256]{3,2,1,0:T(8,128)(2,1)S(1)}, bf16[2,2,32,256]{3,2,1,0:T(8,128)(2,1)S(1)}, u32[]{:S(2)}, u32[]{:S(2)}) collective-permute-start(bf16[2,2,32,256]{3,2,1,0:T(8,128)(2,1)S(1)} %get-tuple-element.84), channel_id=1, source_target_pairs={{0,2},{2,0},{1,3},{3,1},{4,6},{6,4},{5,7},{7,5},{8,10},{10,8},{9,1... | collective-permute-start | bytes 196616 | tf_op jit(solution)/shard_map/ppermute | solution.py:497
  68.0 5.7 %collective-permute-start.18 = (bf16[2,2,32,256]{3,2,1,0:T(8,128)(2,1)S(1)}, bf16[2,2,32,256]{3,2,1,0:T(8,128)(2,1)S(1)}, u32[]{:S(2)}, u32[]{:S(2)}) collective-permute-start(bf16[2,2,32,256]{3,2,1,0:T(8,128)(2,1)S(1)} %shard_map.84.rest_0_), channel_id=1, source_target_pairs={{0,8},{4,12},{8,0},{12,4},{1,9},{5,13},{9,1},{13,5},{2,10},{6,14},... | collective-permute-start | bytes 196616 | tf_op jit(solution)/shard_map/ppermute | solution.py:497
  70.0 6.6 %collective-permute-start.22 = (bf16[2,2,32,256]{3,2,1,0:T(8,128)(2,1)S(1)}, bf16[2,2,32,256]{3,2,1,0:T(8,128)(2,1)S(1)}, u32[]{:S(2)}, u32[]{:S(2)}) collective-permute-start(bf16[2,2,32,256]{3,2,1,0:T(8,128)(2,1)S(1)} %shard_map.86.rest_0_), channel_id=1, source_target_pairs={{0,8},{4,12},{8,0},{12,4},{1,9},{5,13},{9,1},{13,5},{2,10},{6,14},... | collective-permute-start | bytes 196616 | tf_op jit(solution)/shard_map/ppermute | solution.py:497
  71.4 7.1 %collective-permute-start.20 = (bf16[2,2,32,256]{3,2,1,0:T(8,128)(2,1)S(1)}, bf16[2,2,32,256]{3,2,1,0:T(8,128)(2,1)S(1)}, u32[]{:S(2)}, u32[]{:S(2)}) collective-permute-start(bf16[2,2,32,256]{3,2,1,0:T(8,128)(2,1)S(1)} %shard_map.84.rest_0_), channel_id=1, source_target_pairs={{0,4},{4,0},{8,12},{12,8},{1,5},{5,1},{9,13},{13,9},{2,6},{6,2},{1... | collective-permute-start | bytes 196616 | tf_op jit(solution)/shard_map/ppermute | solution.py:497
  73.7 5.1 %collective-permute-start.19 = (bf16[2,2,32,256]{3,2,1,0:T(8,128)(2,1)S(1)}, bf16[2,2,32,256]{3,2,1,0:T(8,128)(2,1)S(1)}, u32[]{:S(2)}, u32[]{:S(2)}) collective-permute-start(bf16[2,2,32,256]{3,2,1,0:T(8,128)(2,1)S(1)} %collective-permute-done.18.rest_1_), channel_id=1, source_target_pairs={{0,4},{4,0},{8,12},{12,8},{1,5},{5,1},{9,13},{13,9},{2,6},{6,2},{1... | collective-permute-start | bytes 196616 | tf_op jit(solution)/shard_map/ppermute | solution.py:497
  76.6 4.9 %collective-permute-start.23 = (bf16[2,2,32,256]{3,2,1,0:T(8,128)(2,1)S(1)}, bf16[2,2,32,256]{3,2,1,0:T(8,128)(2,1)S(1)}, u32[]{:S(2)}, u32[]{:S(2)}) collective-permute-start(bf16[2,2,32,256]{3,2,1,0:T(8,128)(2,1)S(1)} %collective-permute-done.22.rest_1_), channel_id=1, source_target_pairs={{0,4},{4,0},{8,12},{12,8},{1,5},{5,1},{9,13},{13,9},{2,6},{6,2},{1... | collective-permute-start | bytes 196616 | tf_op jit(solution)/shard_map/ppermute | solution.py:497
  87.0 8.8 %collective-permute-start.27 = (bf16[64,1024]{1,0:T(8,128)(2,1)S(1)}, bf16[64,1024]{1,0:T(8,128)(2,1)S(1)}, u32[]{:S(2)}, u32[]{:S(2)}) collective-permute-start(bf16[64,1024]{1,0:T(8,128)(2,1)S(1)} %get-tuple-element.86), channel_id=1, source_target_pairs={{0,8},{4,12},{8,0},{12,4},{1,9},{5,13},{9,1},{13,5},{2,10},{6,14},... | collective-permute-start | bytes 393224 | tf_op jit(solution)/shard_map/ppermute | solution.py:497
  87.7 8.1 %collective-permute-start.28 = (bf16[64,1024]{1,0:T(8,128)(2,1)S(1)}, bf16[64,1024]{1,0:T(8,128)(2,1)S(1)}, u32[]{:S(2)}, u32[]{:S(2)}) collective-permute-start(bf16[64,1024]{1,0:T(8,128)(2,1)S(1)} %get-tuple-element.87), channel_id=1, source_target_pairs={{0,12},{4,8},{8,4},{12,0},{1,13},{5,9},{9,5},{13,1},{2,14},{6,10},... | collective-permute-start | bytes 393224 | tf_op jit(solution)/shard_map/ppermute | solution.py:497
  90.7 6.8 %collective-permute-start.29 = (bf16[64,1024]{1,0:T(8,128)(2,1)S(1)}, bf16[64,1024]{1,0:T(8,128)(2,1)S(1)}, u32[]{:S(2)}, u32[]{:S(2)}) collective-permute-start(bf16[64,1024]{1,0:T(8,128)(2,1)S(1)} %get-tuple-element.88), channel_id=1, source_target_pairs={{0,4},{4,0},{8,12},{12,8},{1,5},{5,1},{9,13},{13,9},{2,6},{6,2},{1... | collective-permute-start | bytes 393224 | tf_op jit(solution)/shard_map/ppermute | solution.py:497
  98.2 7.4 %collective-permute-start.30 = (bf16[64,1024]{1,0:T(8,128)(2,1)S(1)}, bf16[64,1024]{1,0:T(8,128)(2,1)S(1)}, u32[]{:S(2)}, u32[]{:S(2)}) collective-permute-start(bf16[64,1024]{1,0:T(8,128)(2,1)S(1)} %get-tuple-element.90), channel_id=1, source_target_pairs={{0,8},{4,12},{8,0},{12,4},{1,9},{5,13},{9,1},{13,5},{2,10},{6,14},... | collective-permute-start | bytes 393224 | tf_op jit(solution)/shard_map/ppermute | solution.py:497
  102.7 6.9 %collective-permute-start.31 = (bf16[64,1024]{1,0:T(8,128)(2,1)S(1)}, bf16[64,1024]{1,0:T(8,128)(2,1)S(1)}, u32[]{:S(2)}, u32[]{:S(2)}) collective-permute-start(bf16[64,1024]{1,0:T(8,128)(2,1)S(1)} %get-tuple-element.91), channel_id=1, source_target_pairs={{0,12},{4,8},{8,4},{12,0},{1,13},{5,9},{9,5},{13,1},{2,14},{6,10},... | collective-permute-start | bytes 393224 | tf_op jit(solution)/shard_map/ppermute | solution.py:497
  104.8 7.4 %collective-permute-start.32 = (bf16[64,1024]{1,0:T(8,128)(2,1)S(1)}, bf16[64,1024]{1,0:T(8,128)(2,1)S(1)}, u32[]{:S(2)}, u32[]{:S(2)}) collective-permute-start(bf16[64,1024]{1,0:T(8,128)(2,1)S(1)} %get-tuple-element.92), channel_id=1, source_target_pairs={{0,4},{4,0},{8,12},{12,8},{1,5},{5,1},{9,13},{13,9},{2,6},{6,2},{1... | collective-permute-start | bytes 393224 | tf_op jit(solution)/shard_map/ppermute | solution.py:497
  112.7 5.0 %collective-permute-start.33 = (bf16[2,2,32,256]{3,2,1,0:T(8,128)(2,1)S(1)}, bf16[2,2,32,256]{3,2,1,0:T(8,128)(2,1)S(1)}, u32[]{:S(2)}, u32[]{:S(2)}) collective-permute-start(bf16[2,2,32,256]{3,2,1,0:T(8,128)(2,1)S(1)} %get-tuple-element.94), channel_id=1, source_target_pairs={{0,2},{2,0},{1,3},{3,1},{4,6},{6,4},{5,7},{7,5},{8,10},{10,8},{9,1... | collective-permute-start | bytes 196616 | tf_op jit(solution)/shard_map/ppermute | solution.py:497
  117.0 5.2 %collective-permute-start.38 = (bf16[2,2,32,256]{3,2,1,0:T(8,128)(2,1)S(1)}, bf16[2,2,32,256]{3,2,1,0:T(8,128)(2,1)S(1)}, u32[]{:S(2)}, u32[]{:S(2)}) collective-permute-start(bf16[2,2,32,256]{3,2,1,0:T(8,128)(2,1)S(1)} %shard_map.94.rest_0_), channel_id=1, source_target_pairs={{0,8},{4,12},{8,0},{12,4},{1,9},{5,13},{9,1},{13,5},{2,10},{6,14},... | collective-permute-start | bytes 196616 | tf_op jit(solution)/shard_map/ppermute | solution.py:497
  117.7 6.6 %collective-permute-start.34 = (bf16[2,2,32,256]{3,2,1,0:T(8,128)(2,1)S(1)}, bf16[2,2,32,256]{3,2,1,0:T(8,128)(2,1)S(1)}, u32[]{:S(2)}, u32[]{:S(2)}) collective-permute-start(bf16[2,2,32,256]{3,2,1,0:T(8,128)(2,1)S(1)} %shard_map.93.rest_0_), channel_id=1, source_target_pairs={{0,8},{4,12},{8,0},{12,4},{1,9},{5,13},{9,1},{13,5},{2,10},{6,14},... | collective-permute-start | bytes 196616 | tf_op jit(solution)/shard_map/ppermute | solution.py:497
  120.1 5.0 %collective-permute-start.40 = (bf16[2,2,32,256]{3,2,1,0:T(8,128)(2,1)S(1)}, bf16[2,2,32,256]{3,2,1,0:T(8,128)(2,1)S(1)}, u32[]{:S(2)}, u32[]{:S(2)}) collective-permute-start(bf16[2,2,32,256]{3,2,1,0:T(8,128)(2,1)S(1)} %shard_map.94.rest_0_), channel_id=1, source_target_pairs={{0,4},{4,0},{8,12},{12,8},{1,5},{5,1},{9,13},{13,9},{2,6},{6,2},{1... | collective-permute-start | bytes 196616 | tf_op jit(solution)/shard_map/ppermute | solution.py:497
  122.2 6.2 %collective-permute-start.36 = (bf16[2,2,32,256]{3,2,1,0:T(8,128)(2,1)S(1)}, bf16[2,2,32,256]{3,2,1,0:T(8,128)(2,1)S(1)}, u32[]{:S(2)}, u32[]{:S(2)}) collective-permute-start(bf16[2,2,32,256]{3,2,1,0:T(8,128)(2,1)S(1)} %shard_map.93.rest_0_), channel_id=1, source_target_pairs={{0,4},{4,0},{8,12},{12,8},{1,5},{5,1},{9,13},{13,9},{2,6},{6,2},{1... | collective-permute-start | bytes 196616 | tf_op jit(solution)/shard_map/ppermute | solution.py:497
  (17 other events, 173.0 us)

commit v24 on v14

--- a/solution.py
+++ b/solution.py
@@ -526,12 +526,12 @@
     kept_pair = [exchanged(v, "sblk", 1) for v in kept]
     sums, spectra = summed(dealt_out(first_spectra(initial, places, freq_devs, per_dev)))
     far = exchanged(spectra, "rblk", 1)
-    moved_pair = []
-    for index in range(PARTS):
-        if index:
-            moved[index], far = lax.optimization_barrier((moved[index], far))
-        else:
-            moved[index], spectra = lax.optimization_barrier((moved[index], spectra))
+    parts = [((kept[i], None), (kept_pair[i], None)) for i in range(PARTS)]
+    moved[0], spectra = lax.optimization_barrier((moved[0], spectra))
+    held = down_products(None, [spectra], parts, 0, 0, freq_place)
+    moved_pair = [exchanged(moved[0], "sblk", 1)]
+    for index in range(1, PARTS):
+        moved[index], held = lax.optimization_barrier((moved[index], held))
         moved_pair.append(exchanged(moved[index], "sblk", 1))
     parts = [((kept[i], moved[i]), (kept_pair[i], moved_pair[i])) for i in range(PARTS)]
 
@@ -541,12 +541,8 @@
 
     near, far, result = [spectra], [far], None
     for step in range(ITERS):
-        held = down_products(None, near, parts, 0, 0, freq_place)
-        at = 0 if step else PARTS - 1
-        if at:
-            held = down_products(held, far, parts[:at], 1, 0, freq_place)
-        first = at * 2 * kept[0].shape[1]
-        messages = dealt_out(down_products(held, far, parts[at:], 1, first, freq_place, freq_devs))
+        held = down_products(None, near, parts, 0, 0, freq_place) if step else held
+        messages = dealt_out(down_products(held, far, parts, 1, 0, freq_place, freq_devs))
         messages = dealt_out(windowed(messages, src_tables, matrix, freq_place, per_dev, share))
         received = [exchanged(v, "rblk", 1) for v in up_products(messages, parts, freq_place, half_rows, 1)]
         keep = up_products(messages, parts, freq_place, half_rows, 0)

time: 130 us -> 133 us (1.023)
  starting transfers between devices: 54.5 us -> 57.7 us
    ppermute x41, starting transfers between devices: 54.5 us -> 57.7 us  [exchanged(): lax.ppermute(value, axis, [(i, i ^ step) for i in range(lax.axis_size(axi...]
    pallas_call x24 -> x23, Pallas kernels: 14.2 us -> 14.1 us  [call(): pl.pallas_call(body, grid_spec=pltpu.PrefetchScalarGridSpec(num_scalar_pr...]
  transfers between devices with their start and end apart: 41 -> 41, of which waited for: 22 -> 22; matrix products, arithmetic and copies ran while one was open for 0% -> 0% of each run, Pallas kernels for 6% -> 5%
where the time goes in v24:
time: 133 us; the launch traced here: 132 us
  starting transfers between devices  57.7 us (43%)
  waiting for transfers between devices  55.8 us (42%)
  Pallas kernels  14.1 us (11%)
  local copies, waits for them, and re-layouts  4.57 us (3%)
    ppermute x41, starting transfers between devices, exchanged(): lax.ppermute(value, axis, [(i, i ^ step) for i in range(lax.axis_size(axi...  57.7 us
    ppermute x41, waiting for transfers between devices, exchanged(): lax.ppermute(value, axis, [(i, i ^ step) for i in range(lax.axis_size(axi...  55.8 us
    pallas_call x23, Pallas kernels, call(): pl.pallas_call(body, grid_spec=pltpu.PrefetchScalarGridSpec(num_scalar_pr...  14.1 us
    unnamed x15, local copies, waits for them, and re-layouts  4.57 us
  transfers between devices with their start and end apart: 41, of which 22 were waited for; matrix products, arithmetic and copies ran while one was open for 0% of the time, Pallas kernels for 5%

profile of v24, /device:TPU:0, one launch (start us, length us, event | category | flops | bytes accessed | tf_op | source)
XLA Modules:
  0.0 132.4 jit_solution(6921456008810380432)
XLA Ops:
  2.6 3.0 %collective-permute-start.7 = (bf16[2,256,512]{2,1,0:T(8,128)(2,1)S(1)}, bf16[2,256,512]{2,1,0:T(8,128)(2,1)S(1)}, u32[]{:S(2)}, u32[]{:S(2)}) collective-permute-start(bf16[2,256,512]{2,1,0:T(8,128)(2,1)S(1)} %get-tuple-element.67), channel_id=1, source_target_pairs={{0,2},{2,0},{1,3},{3,1},{4,6},{6,4},{5,7},{7,5},{8,10},{10,8},{9,1... | collective-permute-start | bytes 1572872 | tf_op jit(solution)/shard_map/ppermute | solution.py:495
  6.2 2.2 %copy-done = bf16[64,128,256]{2,1,0:T(8,128)(2,1)S(1)} copy-done((bf16[64,128,256]{2,1,0:T(8,128)(2,1)S(1)}, bf16[64,128,256]{2,1,0:T(8,128)(2,1)}, u32[]{:S(2)}) %copy-start) | copy-done | bytes 4194328
  9.2 3.1 %collective-permute-start.3 = (bf16[2,2,64,256]{3,2,1,0:T(8,128)(2,1)S(1)}, bf16[2,2,64,256]{3,2,1,0:T(8,128)(2,1)S(1)}, u32[]{:S(2)}, u32[]{:S(2)}) collective-permute-start(bf16[2,2,64,256]{3,2,1,0:T(8,128)(2,1)S(1)} %get-tuple-element.59), channel_id=1, source_target_pairs={{0,8},{4,12},{8,0},{12,4},{1,9},{5,13},{9,1},{13,5},{2,10},{6,14},... | collective-permute-start | bytes 393224 | tf_op jit(solution)/shard_map/ppermute | solution.py:495
  12.3 6.2 %collective-permute-done.3.refs_1_ = bf16[2,2,64,256]{3,2,1,0:T(8,128)(2,1)S(1)} collective-permute-done((bf16[2,2,64,256]{3,2,1,0:T(8,128)(2,1)S(1)}, bf16[2,2,64,256]{3,2,1,0:T(8,128)(2,1)S(1)}, u32[]{:S(2)}, u32[]{:S(2)}) %collective-permute-start.3) | collective-permute-done | bytes 131104 | tf_op jit(solution)/shard_map/ppermute | solution.py:495
  18.5 3.5 %collective-permute-start.4 = (bf16[2,2,64,256]{3,2,1,0:T(8,128)(2,1)S(1)}, bf16[2,2,64,256]{3,2,1,0:T(8,128)(2,1)S(1)}, u32[]{:S(2)}, u32[]{:S(2)}) collective-permute-start(bf16[2,2,64,256]{3,2,1,0:T(8,128)(2,1)S(1)} %get-tuple-element.60), channel_id=1, source_target_pairs={{0,12},{4,8},{8,4},{12,0},{1,13},{5,9},{9,5},{13,1},{2,14},{6,10},... | collective-permute-start | bytes 393224 | tf_op jit(solution)/shard_map/ppermute | solution.py:495
  22.0 3.8 %collective-permute-done.4.refs_2_ = bf16[2,2,64,256]{3,2,1,0:T(8,128)(2,1)S(1)} collective-permute-done((bf16[2,2,64,256]{3,2,1,0:T(8,128)(2,1)S(1)}, bf16[2,2,64,256]{3,2,1,0:T(8,128)(2,1)S(1)}, u32[]{:S(2)}, u32[]{:S(2)}) %collective-permute-start.4) | collective-permute-done | bytes 131104 | tf_op jit(solution)/shard_map/ppermute | solution.py:495
  27.4 3.3 %collective-permute-done.5.refs_3_ = bf16[2,2,64,256]{3,2,1,0:T(8,128)(2,1)S(1)} collective-permute-done((bf16[2,2,64,256]{3,2,1,0:T(8,128)(2,1)S(1)}, bf16[2,2,64,256]{3,2,1,0:T(8,128)(2,1)S(1)}, u32[]{:S(2)}, u32[]{:S(2)}) %collective-permute-start.5) | collective-permute-done | bytes 131104 | tf_op jit(solution)/shard_map/ppermute | solution.py:495
  33.8 4.0 %collective-permute-done.8.rest_1_ = bf16[2,2,64,256]{3,2,1,0:T(8,128)(2,1)S(1)} collective-permute-done((bf16[2,2,64,256]{3,2,1,0:T(8,128)(2,1)S(1)}, bf16[2,2,64,256]{3,2,1,0:T(8,128)(2,1)S(1)}, u32[]{:S(2)}, u32[]{:S(2)}) %collective-permute-start.8) | collective-permute-done | bytes 131104 | tf_op jit(solution)/shard_map/ppermute | solution.py:495
  38.7 2.0 %collective-permute-start.11 = (bf16[64,1024]{1,0:T(8,128)(2,1)S(1)}, bf16[64,1024]{1,0:T(8,128)(2,1)S(1)}, u32[]{:S(2)}, u32[]{:S(2)}) collective-permute-start(bf16[64,1024]{1,0:T(8,128)(2,1)S(1)} %get-tuple-element.74), channel_id=1, source_target_pairs={{0,8},{4,12},{8,0},{12,4},{1,9},{5,13},{9,1},{13,5},{2,10},{6,14},... | collective-permute-start | bytes 393224 | tf_op jit(solution)/shard_map/ppermute | solution.py:495
  40.7 2.0 %collective-permute-start.12 = (bf16[64,1024]{1,0:T(8,128)(2,1)S(1)}, bf16[64,1024]{1,0:T(8,128)(2,1)S(1)}, u32[]{:S(2)}, u32[]{:S(2)}) collective-permute-start(bf16[64,1024]{1,0:T(8,128)(2,1)S(1)} %get-tuple-element.75), channel_id=1, source_target_pairs={{0,12},{4,8},{8,4},{12,0},{1,13},{5,9},{9,5},{13,1},{2,14},{6,10},... | collective-permute-start | bytes 393224 | tf_op jit(solution)/shard_map/ppermute | solution.py:495
  45.4 5.8 %collective-permute-done.11.rest_1_ = bf16[64,1024]{1,0:T(8,128)(2,1)S(1)} collective-permute-done((bf16[64,1024]{1,0:T(8,128)(2,1)S(1)}, bf16[64,1024]{1,0:T(8,128)(2,1)S(1)}, u32[]{:S(2)}, u32[]{:S(2)}) %collective-permute-start.11) | collective-permute-done | bytes 131104 | tf_op jit(solution)/shard_map/ppermute | solution.py:495
  52.3 3.5 %collective-permute-start.14 = (bf16[64,1024]{1,0:T(8,128)(2,1)S(1)}, bf16[64,1024]{1,0:T(8,128)(2,1)S(1)}, u32[]{:S(2)}, u32[]{:S(2)}) collective-permute-start(bf16[64,1024]{1,0:T(8,128)(2,1)S(1)} %get-tuple-element.78), channel_id=1, source_target_pairs={{0,8},{4,12},{8,0},{12,4},{1,9},{5,13},{9,1},{13,5},{2,10},{6,14},... | collective-permute-start | bytes 393224 | tf_op jit(solution)/shard_map/ppermute | solution.py:495
  56.7 8.4 %collective-permute-done.14.rest_5_ = bf16[64,1024]{1,0:T(8,128)(2,1)S(1)} collective-permute-done((bf16[64,1024]{1,0:T(8,128)(2,1)S(1)}, bf16[64,1024]{1,0:T(8,128)(2,1)S(1)}, u32[]{:S(2)}, u32[]{:S(2)}) %collective-permute-start.14) | collective-permute-done | bytes 131104 | tf_op jit(solution)/shard_map/ppermute | solution.py:495
  69.3 1.8 %collective-permute-done.17.r_ref = bf16[2,2,32,256]{3,2,1,0:T(8,128)(2,1)S(1)} collective-permute-done((bf16[2,2,32,256]{3,2,1,0:T(8,128)(2,1)S(1)}, bf16[2,2,32,256]{3,2,1,0:T(8,128)(2,1)S(1)}, u32[]{:S(2)}, u32[]{:S(2)}) %collective-permute-start.17) | collective-permute-done | bytes 65568 | tf_op jit(solution)/shard_map/ppermute | solution.py:495
  71.1 1.9 %collective-permute-start.18 = (bf16[2,2,32,256]{3,2,1,0:T(8,128)(2,1)S(1)}, bf16[2,2,32,256]{3,2,1,0:T(8,128)(2,1)S(1)}, u32[]{:S(2)}, u32[]{:S(2)}) collective-permute-start(bf16[2,2,32,256]{3,2,1,0:T(8,128)(2,1)S(1)} %shard_map.83.rest_0_), channel_id=1, source_target_pairs={{0,8},{4,12},{8,0},{12,4},{1,9},{5,13},{9,1},{13,5},{2,10},{6,14},... | collective-permute-start | bytes 196616 | tf_op jit(solution)/shard_map/ppermute | solution.py:495
  74.4 2.4 %collective-permute-start.20 = (bf16[2,2,32,256]{3,2,1,0:T(8,128)(2,1)S(1)}, bf16[2,2,32,256]{3,2,1,0:T(8,128)(2,1)S(1)}, u32[]{:S(2)}, u32[]{:S(2)}) collective-permute-start(bf16[2,2,32,256]{3,2,1,0:T(8,128)(2,1)S(1)} %shard_map.83.rest_0_), channel_id=1, source_target_pairs={{0,4},{4,0},{8,12},{12,8},{1,5},{5,1},{9,13},{13,9},{2,6},{6,2},{1... | collective-permute-start | bytes 196616 | tf_op jit(solution)/shard_map/ppermute | solution.py:495
  76.8 2.8 %collective-permute-start.19 = (bf16[2,2,32,256]{3,2,1,0:T(8,128)(2,1)S(1)}, bf16[2,2,32,256]{3,2,1,0:T(8,128)(2,1)S(1)}, u32[]{:S(2)}, u32[]{:S(2)}) collective-permute-start(bf16[2,2,32,256]{3,2,1,0:T(8,128)(2,1)S(1)} %collective-permute-done.18.rest_1_), channel_id=1, source_target_pairs={{0,4},{4,0},{8,12},{12,8},{1,5},{5,1},{9,13},{13,9},{2,6},{6,2},{1... | collective-permute-start | bytes 196616 | tf_op jit(solution)/shard_map/ppermute | solution.py:495
  79.7 2.0 %collective-permute-start.23 = (bf16[2,2,32,256]{3,2,1,0:T(8,128)(2,1)S(1)}, bf16[2,2,32,256]{3,2,1,0:T(8,128)(2,1)S(1)}, u32[]{:S(2)}, u32[]{:S(2)}) collective-permute-start(bf16[2,2,32,256]{3,2,1,0:T(8,128)(2,1)S(1)} %collective-permute-done.22.rest_1_), channel_id=1, source_target_pairs={{0,4},{4,0},{8,12},{12,8},{1,5},{5,1},{9,13},{13,9},{2,6},{6,2},{1... | collective-permute-start | bytes 196616 | tf_op jit(solution)/shard_map/ppermute | solution.py:495
  86.7 2.5 %collective-permute-done.26.rest_2_ = bf16[2,2,32,256]{3,2,1,0:T(8,128)(2,1)S(1)} collective-permute-done((bf16[2,2,32,256]{3,2,1,0:T(8,128)(2,1)S(1)}, bf16[2,2,32,256]{3,2,1,0:T(8,128)(2,1)S(1)}, u32[]{:S(2)}, u32[]{:S(2)}) %collective-permute-start.26) | collective-permute-done | bytes 65568 | tf_op jit(solution)/shard_map/ppermute | solution.py:495
  90.8 3.0 %collective-permute-start.28 = (bf16[64,1024]{1,0:T(8,128)(2,1)S(1)}, bf16[64,1024]{1,0:T(8,128)(2,1)S(1)}, u32[]{:S(2)}, u32[]{:S(2)}) collective-permute-start(bf16[64,1024]{1,0:T(8,128)(2,1)S(1)} %get-tuple-element.87), channel_id=1, source_target_pairs={{0,12},{4,8},{8,4},{12,0},{1,13},{5,9},{9,5},{13,1},{2,14},{6,10},... | collective-permute-start | bytes 393224 | tf_op jit(solution)/shard_map/ppermute | solution.py:495
  93.8 5.1 %collective-permute-done.27.rest_1_ = bf16[64,1024]{1,0:T(8,128)(2,1)S(1)} collective-permute-done((bf16[64,1024]{1,0:T(8,128)(2,1)S(1)}, bf16[64,1024]{1,0:T(8,128)(2,1)S(1)}, u32[]{:S(2)}, u32[]{:S(2)}) %collective-permute-start.27) | collective-permute-done | bytes 131104 | tf_op jit(solution)/shard_map/ppermute | solution.py:495
  101.4 1.6 %collective-permute-start.30 = (bf16[64,1024]{1,0:T(8,128)(2,1)S(1)}, bf16[64,1024]{1,0:T(8,128)(2,1)S(1)}, u32[]{:S(2)}, u32[]{:S(2)}) collective-permute-start(bf16[64,1024]{1,0:T(8,128)(2,1)S(1)} %get-tuple-element.90), channel_id=1, source_target_pairs={{0,8},{4,12},{8,0},{12,4},{1,9},{5,13},{9,1},{13,5},{2,10},{6,14},... | collective-permute-start | bytes 393224 | tf_op jit(solution)/shard_map/ppermute | solution.py:495
  103.0 3.4 %collective-permute-start.31 = (bf16[64,1024]{1,0:T(8,128)(2,1)S(1)}, bf16[64,1024]{1,0:T(8,128)(2,1)S(1)}, u32[]{:S(2)}, u32[]{:S(2)}) collective-permute-start(bf16[64,1024]{1,0:T(8,128)(2,1)S(1)} %get-tuple-element.91), channel_id=1, source_target_pairs={{0,12},{4,8},{8,4},{12,0},{1,13},{5,9},{9,5},{13,1},{2,14},{6,10},... | collective-permute-start | bytes 393224 | tf_op jit(solution)/shard_map/ppermute | solution.py:495
  107.3 3.6 %collective-permute-done.31.rest_6_ = bf16[64,1024]{1,0:T(8,128)(2,1)S(1)} collective-permute-done((bf16[64,1024]{1,0:T(8,128)(2,1)S(1)}, bf16[64,1024]{1,0:T(8,128)(2,1)S(1)}, u32[]{:S(2)}, u32[]{:S(2)}) %collective-permute-start.31) | collective-permute-done | bytes 131104 | tf_op jit(solution)/shard_map/ppermute | solution.py:495
  111.0 2.0 %collective-permute-done.32.rest_7_ = bf16[64,1024]{1,0:T(8,128)(2,1)S(1)} collective-permute-done((bf16[64,1024]{1,0:T(8,128)(2,1)S(1)}, bf16[64,1024]{1,0:T(8,128)(2,1)S(1)}, u32[]{:S(2)}, u32[]{:S(2)}) %collective-permute-start.32) | collective-permute-done | bytes 131104 | tf_op jit(solution)/shard_map/ppermute | solution.py:495
  113.4 1.9 %collective-permute-start.37 = (bf16[2,2,32,256]{3,2,1,0:T(8,128)(2,1)S(1)}, bf16[2,2,32,256]{3,2,1,0:T(8,128)(2,1)S(1)}, u32[]{:S(2)}, u32[]{:S(2)}) collective-permute-start(bf16[2,2,32,256]{3,2,1,0:T(8,128)(2,1)S(1)} %get-tuple-element.96), channel_id=1, source_target_pairs={{0,2},{2,0},{1,3},{3,1},{4,6},{6,4},{5,7},{7,5},{8,10},{10,8},{9,1... | collective-permute-start | bytes 196616 | tf_op jit(solution)/shard_map/ppermute | solution.py:495
  116.0 1.8 %collective-permute-done.37.r_ref = bf16[2,2,32,256]{3,2,1,0:T(8,128)(2,1)S(1)} collective-permute-done((bf16[2,2,32,256]{3,2,1,0:T(8,128)(2,1)S(1)}, bf16[2,2,32,256]{3,2,1,0:T(8,128)(2,1)S(1)}, u32[]{:S(2)}, u32[]{:S(2)}) %collective-permute-start.37) | collective-permute-done | bytes 65568 | tf_op jit(solution)/shard_map/ppermute | solution.py:495
  117.8 2.7 %collective-permute-start.38 = (bf16[2,2,32,256]{3,2,1,0:T(8,128)(2,1)S(1)}, bf16[2,2,32,256]{3,2,1,0:T(8,128)(2,1)S(1)}, u32[]{:S(2)}, u32[]{:S(2)}) collective-permute-start(bf16[2,2,32,256]{3,2,1,0:T(8,128)(2,1)S(1)} %shard_map.93.rest_0_), channel_id=1, source_target_pairs={{0,8},{4,12},{8,0},{12,4},{1,9},{5,13},{9,1},{13,5},{2,10},{6,14},... | collective-permute-start | bytes 196616 | tf_op jit(solution)/shard_map/ppermute | solution.py:495
  120.5 2.0 %collective-permute-start.34 = (bf16[2,2,32,256]{3,2,1,0:T(8,128)(2,1)S(1)}, bf16[2,2,32,256]{3,2,1,0:T(8,128)(2,1)S(1)}, u32[]{:S(2)}, u32[]{:S(2)}) collective-permute-start(bf16[2,2,32,256]{3,2,1,0:T(8,128)(2,1)S(1)} %shard_map.92.rest_0_), channel_id=1, source_target_pairs={{0,8},{4,12},{8,0},{12,4},{1,9},{5,13},{9,1},{13,5},{2,10},{6,14},... | collective-permute-start | bytes 196616 | tf_op jit(solution)/shard_map/ppermute | solution.py:495
  122.5 1.6 %collective-permute-start.40 = (bf16[2,2,32,256]{3,2,1,0:T(8,128)(2,1)S(1)}, bf16[2,2,32,256]{3,2,1,0:T(8,128)(2,1)S(1)}, u32[]{:S(2)}, u32[]{:S(2)}) collective-permute-start(bf16[2,2,32,256]{3,2,1,0:T(8,128)(2,1)S(1)} %shard_map.93.rest_0_), channel_id=1, source_target_pairs={{0,4},{4,0},{8,12},{12,8},{1,5},{5,1},{9,13},{13,9},{2,6},{6,2},{1... | collective-permute-start | bytes 196616 | tf_op jit(solution)/shard_map/ppermute | solution.py:495
  128.4 1.9 %shard_map.94.rest_4_ = bf16[64,128,256]{2,1,0:T(8,128)(2,1)} custom-call(s32[1]{0:T(128)} %bitcast._.freq.place_ref, s32[1]{0:T(128)} %bitcast.1.rblk._, s32[1]{0:T(128)} %bitcast.2.__.sblk, bf16[64,128,256]{2,1,0:T(8,128)(2,1)S(1)} %copy-done.1, s32[128,256]{1,0:T(8,128)S(1)} %copy-done.4, bf16[4,128,128]{2,1,0:T(8,128)(2,1)S(1)} %copy-done.5, ...), custom_call_target="tpu_custom_call" | custom-call | flops 33554432 | bytes 8912896 | tf_op jit(solution)/shard_map/pallas_call | solution.py:78
  130.4 1.9 %shard_map.95 = bf16[64,128,256]{2,1,0:T(8,128)(2,1)} custom-call(s32[1]{0:T(128)} %bitcast._.freq.place_ref, s32[1]{0:T(128)} %bitcast.1.rblk._, s32[1]{0:T(128)} %bitcast.2.__.sblk, bf16[64,128,256]{2,1,0:T(8,128)(2,1)S(1)} %copy-done.1, s32[128,256]{1,0:T(8,128)S(1)} %copy-done.4, ...), custom_call_target="tpu_custom_call", output_to_operand_aliasing={{}: (10, {})} | custom-call | flops 33554432 | bytes 13107200 | tf_op jit(solution)/shard_map/pallas_call | solution.py:78
  (88 shorter events, 35.4 us)
Async XLA Ops:
  2.6 28.3 %collective-permute-start.7 = (bf16[2,256,512]{2,1,0:T(8,128)(2,1)S(1)}, bf16[2,256,512]{2,1,0:T(8,128)(2,1)S(1)}, u32[]{:S(2)}, u32[]{:S(2)}) collective-permute-start(bf16[2,256,512]{2,1,0:T(8,128)(2,1)S(1)} %get-tuple-element.67), channel_id=1, source_target_pairs={{0,2},{2,0},{1,3},{3,1},{4,6},{6,4},{5,7},{7,5},{8,10},{10,8},{9,1... | collective-permute-start | bytes 1572872 | tf_op jit(solution)/shard_map/ppermute | solution.py:495
  5.6 25.4 %collective-permute-start = (bf16[2,256,512]{2,1,0:T(8,128)(2,1)S(1)}, bf16[2,256,512]{2,1,0:T(8,128)(2,1)S(1)}, u32[]{:S(2)}, u32[]{:S(2)}) collective-permute-start(bf16[2,256,512]{2,1,0:T(8,128)(2,1)S(1)} %get-tuple-element.51.rest_1_.rest_0_.rest_2_), channel_id=1, source_target_pairs={{0,1},{1,0},{2,3},{3,2},{4,5},{5,4},{6,7},{7,6},{8,9},{9,8},{10,11... | collective-permute-start | bytes 1572872 | tf_op jit(solution)/shard_map/ppermute | solution.py:495
  5.6 25.4 %collective-permute-start.1 = (bf16[2,256,512]{2,1,0:T(8,128)(2,1)S(1)}, bf16[2,256,512]{2,1,0:T(8,128)(2,1)S(1)}, u32[]{:S(2)}, u32[]{:S(2)}) collective-permute-start(bf16[2,256,512]{2,1,0:T(8,128)(2,1)S(1)} %get-tuple-element.52.rest_3_.rest_2_.rest_4_), channel_id=1, source_target_pairs={{0,1},{1,0},{2,3},{3,2},{4,5},{5,4},{6,7},{7,6},{8,9},{9,8},{10,11... | collective-permute-start | bytes 1572872 | tf_op jit(solution)/shard_map/ppermute | solution.py:495
  6.1 25.7 %collective-permute-start.6 = (bf16[2,256,512]{2,1,0:T(8,128)(2,1)S(1)}, bf16[2,256,512]{2,1,0:T(8,128)(2,1)S(1)}, u32[]{:S(2)}, u32[]{:S(2)}) collective-permute-start(bf16[2,256,512]{2,1,0:T(8,128)(2,1)S(1)} %get-tuple-element.66), channel_id=1, source_target_pairs={{0,2},{2,0},{1,3},{3,1},{4,6},{6,4},{5,7},{7,5},{8,10},{10,8},{9,1... | collective-permute-start | bytes 1572872 | tf_op jit(solution)/shard_map/ppermute | solution.py:495
  9.2 9.3 %collective-permute-start.3 = (bf16[2,2,64,256]{3,2,1,0:T(8,128)(2,1)S(1)}, bf16[2,2,64,256]{3,2,1,0:T(8,128)(2,1)S(1)}, u32[]{:S(2)}, u32[]{:S(2)}) collective-permute-start(bf16[2,2,64,256]{3,2,1,0:T(8,128)(2,1)S(1)} %get-tuple-element.59), channel_id=1, source_target_pairs={{0,8},{4,12},{8,0},{12,4},{1,9},{5,13},{9,1},{13,5},{2,10},{6,14},... | collective-permute-start | bytes 393224 | tf_op jit(solution)/shard_map/ppermute | solution.py:495
  18.5 7.3 %collective-permute-start.4 = (bf16[2,2,64,256]{3,2,1,0:T(8,128)(2,1)S(1)}, bf16[2,2,64,256]{3,2,1,0:T(8,128)(2,1)S(1)}, u32[]{:S(2)}, u32[]{:S(2)}) collective-permute-start(bf16[2,2,64,256]{3,2,1,0:T(8,128)(2,1)S(1)} %get-tuple-element.60), channel_id=1, source_target_pairs={{0,12},{4,8},{8,4},{12,0},{1,13},{5,9},{9,5},{13,1},{2,14},{6,10},... | collective-permute-start | bytes 393224 | tf_op jit(solution)/shard_map/ppermute | solution.py:495
  25.8 5.0 %collective-permute-start.5 = (bf16[2,2,64,256]{3,2,1,0:T(8,128)(2,1)S(1)}, bf16[2,2,64,256]{3,2,1,0:T(8,128)(2,1)S(1)}, u32[]{:S(2)}, u32[]{:S(2)}) collective-permute-start(bf16[2,2,64,256]{3,2,1,0:T(8,128)(2,1)S(1)} %get-tuple-element.61), channel_id=1, source_target_pairs={{0,4},{4,0},{8,12},{12,8},{1,5},{5,1},{9,13},{13,9},{2,6},{6,2},{1... | collective-permute-start | bytes 393224 | tf_op jit(solution)/shard_map/ppermute | solution.py:495
  30.9 7.0 %collective-permute-start.9 = (bf16[2,256,512]{2,1,0:T(8,128)(2,1)S(1)}, bf16[2,256,512]{2,1,0:T(8,128)(2,1)S(1)}, u32[]{:S(2)}, u32[]{:S(2)}) collective-permute-start(bf16[2,256,512]{2,1,0:T(8,128)(2,1)S(1)} %collective-permute-done.7.rest_2_.rest_0_.rest_3_), channel_id=1, source_target_pairs={{0,1},{1,0},{2,3},{3,2},{4,5},{5,4},{6,7},{7,6},{8,9},{9,8},{10,11... | collective-permute-start | bytes 1572872 | tf_op jit(solution)/shard_map/ppermute | solution.py:495
  31.8 6.0 %collective-permute-start.10 = (bf16[2,256,512]{2,1,0:T(8,128)(2,1)S(1)}, bf16[2,256,512]{2,1,0:T(8,128)(2,1)S(1)}, u32[]{:S(2)}, u32[]{:S(2)}) collective-permute-start(bf16[2,256,512]{2,1,0:T(8,128)(2,1)S(1)} %collective-permute-done.6.rest_4_.rest_2_.rest_5_), channel_id=1, source_target_pairs={{0,1},{1,0},{2,3},{3,2},{4,5},{5,4},{6,7},{7,6},{8,9},{9,8},{10,11... | collective-permute-start | bytes 1572872 | tf_op jit(solution)/shard_map/ppermute | solution.py:495
  32.3 5.5 %collective-permute-start.8 = (bf16[2,2,64,256]{3,2,1,0:T(8,128)(2,1)S(1)}, bf16[2,2,64,256]{3,2,1,0:T(8,128)(2,1)S(1)}, u32[]{:S(2)}, u32[]{:S(2)}) collective-permute-start(bf16[2,2,64,256]{3,2,1,0:T(8,128)(2,1)S(1)} %get-tuple-element.69.rest_0_), channel_id=1, source_target_pairs={{0,2},{2,0},{1,3},{3,1},{4,6},{6,4},{5,7},{7,5},{8,10},{10,8},{9,1... | collective-permute-start | bytes 393224 | tf_op jit(solution)/shard_map/ppermute | solution.py:495
  38.7 12.5 %collective-permute-start.11 = (bf16[64,1024]{1,0:T(8,128)(2,1)S(1)}, bf16[64,1024]{1,0:T(8,128)(2,1)S(1)}, u32[]{:S(2)}, u32[]{:S(2)}) collective-permute-start(bf16[64,1024]{1,0:T(8,128)(2,1)S(1)} %get-tuple-element.74), channel_id=1, source_target_pairs={{0,8},{4,12},{8,0},{12,4},{1,9},{5,13},{9,1},{13,5},{2,10},{6,14},... | collective-permute-start | bytes 393224 | tf_op jit(solution)/shard_map/ppermute | solution.py:495
  40.7 10.4 %collective-permute-start.12 = (bf16[64,1024]{1,0:T(8,128)(2,1)S(1)}, bf16[64,1024]{1,0:T(8,128)(2,1)S(1)}, u32[]{:S(2)}, u32[]{:S(2)}) collective-permute-start(bf16[64,1024]{1,0:T(8,128)(2,1)S(1)} %get-tuple-element.75), channel_id=1, source_target_pairs={{0,12},{4,8},{8,4},{12,0},{1,13},{5,9},{9,5},{13,1},{2,14},{6,10},... | collective-permute-start | bytes 393224 | tf_op jit(solution)/shard_map/ppermute | solution.py:495
  42.7 8.5 %collective-permute-start.13 = (bf16[64,1024]{1,0:T(8,128)(2,1)S(1)}, bf16[64,1024]{1,0:T(8,128)(2,1)S(1)}, u32[]{:S(2)}, u32[]{:S(2)}) collective-permute-start(bf16[64,1024]{1,0:T(8,128)(2,1)S(1)} %get-tuple-element.76), channel_id=1, source_target_pairs={{0,4},{4,0},{8,12},{12,8},{1,5},{5,1},{9,13},{13,9},{2,6},{6,2},{1... | collective-permute-start | bytes 393224 | tf_op jit(solution)/shard_map/ppermute | solution.py:495
  52.3 12.8 %collective-permute-start.14 = (bf16[64,1024]{1,0:T(8,128)(2,1)S(1)}, bf16[64,1024]{1,0:T(8,128)(2,1)S(1)}, u32[]{:S(2)}, u32[]{:S(2)}) collective-permute-start(bf16[64,1024]{1,0:T(8,128)(2,1)S(1)} %get-tuple-element.78), channel_id=1, source_target_pairs={{0,8},{4,12},{8,0},{12,4},{1,9},{5,13},{9,1},{13,5},{2,10},{6,14},... | collective-permute-start | bytes 393224 | tf_op jit(solution)/shard_map/ppermute | solution.py:495
  55.8 9.4 %collective-permute-start.15 = (bf16[64,1024]{1,0:T(8,128)(2,1)S(1)}, bf16[64,1024]{1,0:T(8,128)(2,1)S(1)}, u32[]{:S(2)}, u32[]{:S(2)}) collective-permute-start(bf16[64,1024]{1,0:T(8,128)(2,1)S(1)} %get-tuple-element.79), channel_id=1, source_target_pairs={{0,12},{4,8},{8,4},{12,0},{1,13},{5,9},{9,5},{13,1},{2,14},{6,10},... | collective-permute-start | bytes 393224 | tf_op jit(solution)/shard_map/ppermute | solution.py:495
  56.7 9.5 %collective-permute-start.16 = (bf16[64,1024]{1,0:T(8,128)(2,1)S(1)}, bf16[64,1024]{1,0:T(8,128)(2,1)S(1)}, u32[]{:S(2)}, u32[]{:S(2)}) collective-permute-start(bf16[64,1024]{1,0:T(8,128)(2,1)S(1)} %get-tuple-element.80), channel_id=1, source_target_pairs={{0,4},{4,0},{8,12},{12,8},{1,5},{5,1},{9,13},{13,9},{2,6},{6,2},{1... | collective-permute-start | bytes 393224 | tf_op jit(solution)/shard_map/ppermute | solution.py:495
  71.1 5.7 %collective-permute-start.18 = (bf16[2,2,32,256]{3,2,1,0:T(8,128)(2,1)S(1)}, bf16[2,2,32,256]{3,2,1,0:T(8,128)(2,1)S(1)}, u32[]{:S(2)}, u32[]{:S(2)}) collective-permute-start(bf16[2,2,32,256]{3,2,1,0:T(8,128)(2,1)S(1)} %shard_map.83.rest_0_), channel_id=1, source_target_pairs={{0,8},{4,12},{8,0},{12,4},{1,9},{5,13},{9,1},{13,5},{2,10},{6,14},... | collective-permute-start | bytes 196616 | tf_op jit(solution)/shard_map/ppermute | solution.py:495
  73.0 6.7 %collective-permute-start.22 = (bf16[2,2,32,256]{3,2,1,0:T(8,128)(2,1)S(1)}, bf16[2,2,32,256]{3,2,1,0:T(8,128)(2,1)S(1)}, u32[]{:S(2)}, u32[]{:S(2)}) collective-permute-start(bf16[2,2,32,256]{3,2,1,0:T(8,128)(2,1)S(1)} %shard_map.85.rest_0_), channel_id=1, source_target_pairs={{0,8},{4,12},{8,0},{12,4},{1,9},{5,13},{9,1},{13,5},{2,10},{6,14},... | collective-permute-start | bytes 196616 | tf_op jit(solution)/shard_map/ppermute | solution.py:495
  74.4 7.2 %collective-permute-start.20 = (bf16[2,2,32,256]{3,2,1,0:T(8,128)(2,1)S(1)}, bf16[2,2,32,256]{3,2,1,0:T(8,128)(2,1)S(1)}, u32[]{:S(2)}, u32[]{:S(2)}) collective-permute-start(bf16[2,2,32,256]{3,2,1,0:T(8,128)(2,1)S(1)} %shard_map.83.rest_0_), channel_id=1, source_target_pairs={{0,4},{4,0},{8,12},{12,8},{1,5},{5,1},{9,13},{13,9},{2,6},{6,2},{1... | collective-permute-start | bytes 196616 | tf_op jit(solution)/shard_map/ppermute | solution.py:495
  76.8 5.1 %collective-permute-start.19 = (bf16[2,2,32,256]{3,2,1,0:T(8,128)(2,1)S(1)}, bf16[2,2,32,256]{3,2,1,0:T(8,128)(2,1)S(1)}, u32[]{:S(2)}, u32[]{:S(2)}) collective-permute-start(bf16[2,2,32,256]{3,2,1,0:T(8,128)(2,1)S(1)} %collective-permute-done.18.rest_1_), channel_id=1, source_target_pairs={{0,4},{4,0},{8,12},{12,8},{1,5},{5,1},{9,13},{13,9},{2,6},{6,2},{1... | collective-permute-start | bytes 196616 | tf_op jit(solution)/shard_map/ppermute | solution.py:495
  79.7 4.9 %collective-permute-start.23 = (bf16[2,2,32,256]{3,2,1,0:T(8,128)(2,1)S(1)}, bf16[2,2,32,256]{3,2,1,0:T(8,128)(2,1)S(1)}, u32[]{:S(2)}, u32[]{:S(2)}) collective-permute-start(bf16[2,2,32,256]{3,2,1,0:T(8,128)(2,1)S(1)} %collective-permute-done.22.rest_1_), channel_id=1, source_target_pairs={{0,4},{4,0},{8,12},{12,8},{1,5},{5,1},{9,13},{13,9},{2,6},{6,2},{1... | collective-permute-start | bytes 196616 | tf_op jit(solution)/shard_map/ppermute | solution.py:495
  90.1 8.8 %collective-permute-start.27 = (bf16[64,1024]{1,0:T(8,128)(2,1)S(1)}, bf16[64,1024]{1,0:T(8,128)(2,1)S(1)}, u32[]{:S(2)}, u32[]{:S(2)}) collective-permute-start(bf16[64,1024]{1,0:T(8,128)(2,1)S(1)} %get-tuple-element.86), channel_id=1, source_target_pairs={{0,8},{4,12},{8,0},{12,4},{1,9},{5,13},{9,1},{13,5},{2,10},{6,14},... | collective-permute-start | bytes 393224 | tf_op jit(solution)/shard_map/ppermute | solution.py:495
  90.8 8.1 %collective-permute-start.28 = (bf16[64,1024]{1,0:T(8,128)(2,1)S(1)}, bf16[64,1024]{1,0:T(8,128)(2,1)S(1)}, u32[]{:S(2)}, u32[]{:S(2)}) collective-permute-start(bf16[64,1024]{1,0:T(8,128)(2,1)S(1)} %get-tuple-element.87), channel_id=1, source_target_pairs={{0,12},{4,8},{8,4},{12,0},{1,13},{5,9},{9,5},{13,1},{2,14},{6,10},... | collective-permute-start | bytes 393224 | tf_op jit(solution)/shard_map/ppermute | solution.py:495
  93.8 6.5 %collective-permute-start.29 = (bf16[64,1024]{1,0:T(8,128)(2,1)S(1)}, bf16[64,1024]{1,0:T(8,128)(2,1)S(1)}, u32[]{:S(2)}, u32[]{:S(2)}) collective-permute-start(bf16[64,1024]{1,0:T(8,128)(2,1)S(1)} %get-tuple-element.88), channel_id=1, source_target_pairs={{0,4},{4,0},{8,12},{12,8},{1,5},{5,1},{9,13},{13,9},{2,6},{6,2},{1... | collective-permute-start | bytes 393224 | tf_op jit(solution)/shard_map/ppermute | solution.py:495
  101.4 5.9 %collective-permute-start.30 = (bf16[64,1024]{1,0:T(8,128)(2,1)S(1)}, bf16[64,1024]{1,0:T(8,128)(2,1)S(1)}, u32[]{:S(2)}, u32[]{:S(2)}) collective-permute-start(bf16[64,1024]{1,0:T(8,128)(2,1)S(1)} %get-tuple-element.90), channel_id=1, source_target_pairs={{0,8},{4,12},{8,0},{12,4},{1,9},{5,13},{9,1},{13,5},{2,10},{6,14},... | collective-permute-start | bytes 393224 | tf_op jit(solution)/shard_map/ppermute | solution.py:495
  103.0 7.9 %collective-permute-start.31 = (bf16[64,1024]{1,0:T(8,128)(2,1)S(1)}, bf16[64,1024]{1,0:T(8,128)(2,1)S(1)}, u32[]{:S(2)}, u32[]{:S(2)}) collective-permute-start(bf16[64,1024]{1,0:T(8,128)(2,1)S(1)} %get-tuple-element.91), channel_id=1, source_target_pairs={{0,12},{4,8},{8,4},{12,0},{1,13},{5,9},{9,5},{13,1},{2,14},{6,10},... | collective-permute-start | bytes 393224 | tf_op jit(solution)/shard_map/ppermute | solution.py:495
  106.4 6.6 %collective-permute-start.32 = (bf16[64,1024]{1,0:T(8,128)(2,1)S(1)}, bf16[64,1024]{1,0:T(8,128)(2,1)S(1)}, u32[]{:S(2)}, u32[]{:S(2)}) collective-permute-start(bf16[64,1024]{1,0:T(8,128)(2,1)S(1)} %get-tuple-element.92), channel_id=1, source_target_pairs={{0,4},{4,0},{8,12},{12,8},{1,5},{5,1},{9,13},{13,9},{2,6},{6,2},{1... | collective-permute-start | bytes 393224 | tf_op jit(solution)/shard_map/ppermute | solution.py:495
  115.3 5.1 %collective-permute-start.33 = (bf16[2,2,32,256]{3,2,1,0:T(8,128)(2,1)S(1)}, bf16[2,2,32,256]{3,2,1,0:T(8,128)(2,1)S(1)}, u32[]{:S(2)}, u32[]{:S(2)}) collective-permute-start(bf16[2,2,32,256]{3,2,1,0:T(8,128)(2,1)S(1)} %get-tuple-element.94), channel_id=1, source_target_pairs={{0,2},{2,0},{1,3},{3,1},{4,6},{6,4},{5,7},{7,5},{8,10},{10,8},{9,1... | collective-permute-start | bytes 196616 | tf_op jit(solution)/shard_map/ppermute | solution.py:495
  117.8 6.3 %collective-permute-start.38 = (bf16[2,2,32,256]{3,2,1,0:T(8,128)(2,1)S(1)}, bf16[2,2,32,256]{3,2,1,0:T(8,128)(2,1)S(1)}, u32[]{:S(2)}, u32[]{:S(2)}) collective-permute-start(bf16[2,2,32,256]{3,2,1,0:T(8,128)(2,1)S(1)} %shard_map.93.rest_0_), channel_id=1, source_target_pairs={{0,8},{4,12},{8,0},{12,4},{1,9},{5,13},{9,1},{13,5},{2,10},{6,14},... | collective-permute-start | bytes 196616 | tf_op jit(solution)/shard_map/ppermute | solution.py:495
  120.5 5.7 %collective-permute-start.34 = (bf16[2,2,32,256]{3,2,1,0:T(8,128)(2,1)S(1)}, bf16[2,2,32,256]{3,2,1,0:T(8,128)(2,1)S(1)}, u32[]{:S(2)}, u32[]{:S(2)}) collective-permute-start(bf16[2,2,32,256]{3,2,1,0:T(8,128)(2,1)S(1)} %shard_map.92.rest_0_), channel_id=1, source_target_pairs={{0,8},{4,12},{8,0},{12,4},{1,9},{5,13},{9,1},{13,5},{2,10},{6,14},... | collective-permute-start | bytes 196616 | tf_op jit(solution)/shard_map/ppermute | solution.py:495
  122.5 4.9 %collective-permute-start.40 = (bf16[2,2,32,256]{3,2,1,0:T(8,128)(2,1)S(1)}, bf16[2,2,32,256]{3,2,1,0:T(8,128)(2,1)S(1)}, u32[]{:S(2)}, u32[]{:S(2)}) collective-permute-start(bf16[2,2,32,256]{3,2,1,0:T(8,128)(2,1)S(1)} %shard_map.93.rest_0_), channel_id=1, source_target_pairs={{0,4},{4,0},{8,12},{12,8},{1,5},{5,1},{9,13},{13,9},{2,6},{6,2},{1... | collective-permute-start | bytes 196616 | tf_op jit(solution)/shard_map/ppermute | solution.py:495
  124.5 5.8 %collective-permute-start.36 = (bf16[2,2,32,256]{3,2,1,0:T(8,128)(2,1)S(1)}, bf16[2,2,32,256]{3,2,1,0:T(8,128)(2,1)S(1)}, u32[]{:S(2)}, u32[]{:S(2)}) collective-permute-start(bf16[2,2,32,256]{3,2,1,0:T(8,128)(2,1)S(1)} %shard_map.92.rest_0_), channel_id=1, source_target_pairs={{0,4},{4,0},{8,12},{12,8},{1,5},{5,1},{9,13},{13,9},{2,6},{6,2},{1... | collective-permute-start | bytes 196616 | tf_op jit(solution)/shard_map/ppermute | solution.py:495
  (16 other events, 227.4 us)

commit v25 on v24

--- a/solution.py
+++ b/solution.py
@@ -13,7 +13,7 @@
 ITERS = 2
 ROWS = 8
 CHUNKS = 2
-PARTS = 2
+PARTS = 1
 VMEM_BYTES = 6 * 1024 * 1024
 
 BF16 = jnp.bfloat16
@@ -527,12 +527,9 @@
     sums, spectra = summed(dealt_out(first_spectra(initial, places, freq_devs, per_dev)))
     far = exchanged(spectra, "rblk", 1)
     parts = [((kept[i], None), (kept_pair[i], None)) for i in range(PARTS)]
-    moved[0], spectra = lax.optimization_barrier((moved[0], spectra))
     held = down_products(None, [spectra], parts, 0, 0, freq_place)
-    moved_pair = [exchanged(moved[0], "sblk", 1)]
-    for index in range(1, PARTS):
-        moved[index], held = lax.optimization_barrier((moved[index], held))
-        moved_pair.append(exchanged(moved[index], "sblk", 1))
+    moved, held = lax.optimization_barrier((moved, held))
+    moved_pair = [exchanged(v, "sblk", 1) for v in moved]
     parts = [((kept[i], moved[i]), (kept_pair[i], moved_pair[i])) for i in range(PARTS)]
 
     own, other = src_onsets(onset_src, places, half_rows, share, src_width)

time: 133 us -> 132 us (level)
  starting transfers between devices: 57.7 us -> 53.6 us
  waiting for transfers between devices: 55.8 us -> 59 us
    ppermute x41 -> x38, starting transfers between devices: 57.7 us -> 53.6 us  [exchanged(): lax.ppermute(value, axis, [(i, i ^ step) for i in range(lax.axis_size(axi...]
    ppermute x41 -> x38, waiting for transfers between devices: 55.8 us -> 59 us  [exchanged(): lax.ppermute(value, axis, [(i, i ^ step) for i in range(lax.axis_size(axi...]
  transfers between devices with their start and end apart: 41 -> 38, of which waited for: 22 -> 22; matrix products, arithmetic and copies ran while one was open for 0% -> 0% of each run, Pallas kernels for 5% -> 5%
where the time goes in v25:
time: 132 us; the launch traced here: 131 us
  waiting for transfers between devices  59 us (45%)
  starting transfers between devices  53.6 us (41%)
  Pallas kernels  14 us (11%)
  local copies, waits for them, and re-layouts  4.57 us (3%)
    ppermute x38, waiting for transfers between devices, exchanged(): lax.ppermute(value, axis, [(i, i ^ step) for i in range(lax.axis_size(axi...  59 us
    ppermute x38, starting transfers between devices, exchanged(): lax.ppermute(value, axis, [(i, i ^ step) for i in range(lax.axis_size(axi...  53.6 us
    pallas_call x23, Pallas kernels, call(): pl.pallas_call(body, grid_spec=pltpu.PrefetchScalarGridSpec(num_scalar_pr...  14 us
    unnamed x15, local copies, waits for them, and re-layouts  4.57 us
  transfers between devices with their start and end apart: 38, of which 22 were waited for; matrix products, arithmetic and copies ran while one was open for 0% of the time, Pallas kernels for 5%

profile of v25, /device:TPU:0, one launch (start us, length us, event | category | flops | bytes accessed | tf_op | source)
XLA Modules:
  0.0 131.4 jit_solution(11840084464708514587)
XLA Ops:
  0.8 1.6 %copy-done.2 = bf16[2,2,1024,256]{3,2,1,0:T(8,128)(2,1)S(1)} copy-done((bf16[2,2,1024,256]{3,2,1,0:T(8,128)(2,1)S(1)}, bf16[2,2,1024,256]{3,2,1,0:T(8,128)(2,1)}, u32[]{:S(2)}) %copy-start.2) | copy-done | bytes 2097176
  3.1 2.6 %collective-permute-start.5 = (bf16[2,512,512]{2,1,0:T(8,128)(2,1)S(1)}, bf16[2,512,512]{2,1,0:T(8,128)(2,1)S(1)}, u32[]{:S(2)}, u32[]{:S(2)}) collective-permute-start(bf16[2,512,512]{2,1,0:T(8,128)(2,1)S(1)} %get-tuple-element.61), channel_id=1, source_target_pairs={{0,2},{2,0},{1,3},{3,1},{4,6},{6,4},{5,7},{7,5},{8,10},{10,8},{9,1... | collective-permute-start | bytes 3145736 | tf_op jit(solution)/shard_map/ppermute | solution.py:495
  5.7 2.2 %copy-done = bf16[64,128,256]{2,1,0:T(8,128)(2,1)S(1)} copy-done((bf16[64,128,256]{2,1,0:T(8,128)(2,1)S(1)}, bf16[64,128,256]{2,1,0:T(8,128)(2,1)}, u32[]{:S(2)}) %copy-start) | copy-done | bytes 4194328
  8.7 2.7 %collective-permute-start.2 = (bf16[2,2,64,256]{3,2,1,0:T(8,128)(2,1)S(1)}, bf16[2,2,64,256]{3,2,1,0:T(8,128)(2,1)S(1)}, u32[]{:S(2)}, u32[]{:S(2)}) collective-permute-start(bf16[2,2,64,256]{3,2,1,0:T(8,128)(2,1)S(1)} %get-tuple-element.54), channel_id=1, source_target_pairs={{0,8},{4,12},{8,0},{12,4},{1,9},{5,13},{9,1},{13,5},{2,10},{6,14},... | collective-permute-start | bytes 393224 | tf_op jit(solution)/shard_map/ppermute | solution.py:495
  12.9 8.7 %collective-permute-done.2.refs_1_ = bf16[2,2,64,256]{3,2,1,0:T(8,128)(2,1)S(1)} collective-permute-done((bf16[2,2,64,256]{3,2,1,0:T(8,128)(2,1)S(1)}, bf16[2,2,64,256]{3,2,1,0:T(8,128)(2,1)S(1)}, u32[]{:S(2)}, u32[]{:S(2)}) %collective-permute-start.2) | collective-permute-done | bytes 131104 | tf_op jit(solution)/shard_map/ppermute | solution.py:495
  23.1 6.3 %collective-permute-done.5.rest_2_.rest_0_.rest_3_ = bf16[2,512,512]{2,1,0:T(8,128)(2,1)S(1)} collective-permute-done((bf16[2,512,512]{2,1,0:T(8,128)(2,1)S(1)}, bf16[2,512,512]{2,1,0:T(8,128)(2,1)S(1)}, u32[]{:S(2)}, u32[]{:S(2)}) %collective-permute-start.5) | collective-permute-done | bytes 1048608 | tf_op jit(solution)/shard_map/ppermute | solution.py:495
  29.4 1.8 %collective-permute-start.6 = (bf16[2,2,64,256]{3,2,1,0:T(8,128)(2,1)S(1)}, bf16[2,2,64,256]{3,2,1,0:T(8,128)(2,1)S(1)}, u32[]{:S(2)}, u32[]{:S(2)}) collective-permute-start(bf16[2,2,64,256]{3,2,1,0:T(8,128)(2,1)S(1)} %get-tuple-element.62.rest_0_), channel_id=1, source_target_pairs={{0,2},{2,0},{1,3},{3,1},{4,6},{6,4},{5,7},{7,5},{8,10},{10,8},{9,1... | collective-permute-start | bytes 393224 | tf_op jit(solution)/shard_map/ppermute | solution.py:495
  31.2 4.2 %collective-permute-done.6.rest_1_ = bf16[2,2,64,256]{3,2,1,0:T(8,128)(2,1)S(1)} collective-permute-done((bf16[2,2,64,256]{3,2,1,0:T(8,128)(2,1)S(1)}, bf16[2,2,64,256]{3,2,1,0:T(8,128)(2,1)S(1)}, u32[]{:S(2)}, u32[]{:S(2)}) %collective-permute-start.6) | collective-permute-done | bytes 131104 | tf_op jit(solution)/shard_map/ppermute | solution.py:495
  36.2 2.9 %collective-permute-start.8 = (bf16[64,1024]{1,0:T(8,128)(2,1)S(1)}, bf16[64,1024]{1,0:T(8,128)(2,1)S(1)}, u32[]{:S(2)}, u32[]{:S(2)}) collective-permute-start(bf16[64,1024]{1,0:T(8,128)(2,1)S(1)} %get-tuple-element.66), channel_id=1, source_target_pairs={{0,8},{4,12},{8,0},{12,4},{1,9},{5,13},{9,1},{13,5},{2,10},{6,14},... | collective-permute-start | bytes 393224 | tf_op jit(solution)/shard_map/ppermute | solution.py:495
  43.3 5.8 %collective-permute-done.8.rest_1_ = bf16[64,1024]{1,0:T(8,128)(2,1)S(1)} collective-permute-done((bf16[64,1024]{1,0:T(8,128)(2,1)S(1)}, bf16[64,1024]{1,0:T(8,128)(2,1)S(1)}, u32[]{:S(2)}, u32[]{:S(2)}) %collective-permute-start.8) | collective-permute-done | bytes 131104 | tf_op jit(solution)/shard_map/ppermute | solution.py:495
  50.5 4.2 %collective-permute-start.11 = (bf16[64,1024]{1,0:T(8,128)(2,1)S(1)}, bf16[64,1024]{1,0:T(8,128)(2,1)S(1)}, u32[]{:S(2)}, u32[]{:S(2)}) collective-permute-start(bf16[64,1024]{1,0:T(8,128)(2,1)S(1)} %get-tuple-element.70), channel_id=1, source_target_pairs={{0,8},{4,12},{8,0},{12,4},{1,9},{5,13},{9,1},{13,5},{2,10},{6,14},... | collective-permute-start | bytes 393224 | tf_op jit(solution)/shard_map/ppermute | solution.py:495
  55.4 8.9 %collective-permute-done.11.rest_3_ = bf16[64,1024]{1,0:T(8,128)(2,1)S(1)} collective-permute-done((bf16[64,1024]{1,0:T(8,128)(2,1)S(1)}, bf16[64,1024]{1,0:T(8,128)(2,1)S(1)}, u32[]{:S(2)}, u32[]{:S(2)}) %collective-permute-start.11) | collective-permute-done | bytes 131104 | tf_op jit(solution)/shard_map/ppermute | solution.py:495
  68.4 1.8 %collective-permute-done.14.r_ref = bf16[2,2,32,256]{3,2,1,0:T(8,128)(2,1)S(1)} collective-permute-done((bf16[2,2,32,256]{3,2,1,0:T(8,128)(2,1)S(1)}, bf16[2,2,32,256]{3,2,1,0:T(8,128)(2,1)S(1)}, u32[]{:S(2)}, u32[]{:S(2)}) %collective-permute-start.14) | collective-permute-done | bytes 65568 | tf_op jit(solution)/shard_map/ppermute | solution.py:495
  70.2 1.9 %collective-permute-start.15 = (bf16[2,2,32,256]{3,2,1,0:T(8,128)(2,1)S(1)}, bf16[2,2,32,256]{3,2,1,0:T(8,128)(2,1)S(1)}, u32[]{:S(2)}, u32[]{:S(2)}) collective-permute-start(bf16[2,2,32,256]{3,2,1,0:T(8,128)(2,1)S(1)} %shard_map.83.rest_0_), channel_id=1, source_target_pairs={{0,8},{4,12},{8,0},{12,4},{1,9},{5,13},{9,1},{13,5},{2,10},{6,14},... | collective-permute-start | bytes 196616 | tf_op jit(solution)/shard_map/ppermute | solution.py:495
  73.6 2.3 %collective-permute-start.17 = (bf16[2,2,32,256]{3,2,1,0:T(8,128)(2,1)S(1)}, bf16[2,2,32,256]{3,2,1,0:T(8,128)(2,1)S(1)}, u32[]{:S(2)}, u32[]{:S(2)}) collective-permute-start(bf16[2,2,32,256]{3,2,1,0:T(8,128)(2,1)S(1)} %shard_map.83.rest_0_), channel_id=1, source_target_pairs={{0,4},{4,0},{8,12},{12,8},{1,5},{5,1},{9,13},{13,9},{2,6},{6,2},{1... | collective-permute-start | bytes 196616 | tf_op jit(solution)/shard_map/ppermute | solution.py:495
  75.9 2.8 %collective-permute-start.16 = (bf16[2,2,32,256]{3,2,1,0:T(8,128)(2,1)S(1)}, bf16[2,2,32,256]{3,2,1,0:T(8,128)(2,1)S(1)}, u32[]{:S(2)}, u32[]{:S(2)}) collective-permute-start(bf16[2,2,32,256]{3,2,1,0:T(8,128)(2,1)S(1)} %collective-permute-done.15.rest_1_), channel_id=1, source_target_pairs={{0,4},{4,0},{8,12},{12,8},{1,5},{5,1},{9,13},{13,9},{2,6},{6,2},{1... | collective-permute-start | bytes 196616 | tf_op jit(solution)/shard_map/ppermute | solution.py:495
  78.8 2.0 %collective-permute-start.20 = (bf16[2,2,32,256]{3,2,1,0:T(8,128)(2,1)S(1)}, bf16[2,2,32,256]{3,2,1,0:T(8,128)(2,1)S(1)}, u32[]{:S(2)}, u32[]{:S(2)}) collective-permute-start(bf16[2,2,32,256]{3,2,1,0:T(8,128)(2,1)S(1)} %collective-permute-done.19.rest_1_), channel_id=1, source_target_pairs={{0,4},{4,0},{8,12},{12,8},{1,5},{5,1},{9,13},{13,9},{2,6},{6,2},{1... | collective-permute-start | bytes 196616 | tf_op jit(solution)/shard_map/ppermute | solution.py:495
  85.9 2.4 %collective-permute-done.23.rest_2_ = bf16[2,2,32,256]{3,2,1,0:T(8,128)(2,1)S(1)} collective-permute-done((bf16[2,2,32,256]{3,2,1,0:T(8,128)(2,1)S(1)}, bf16[2,2,32,256]{3,2,1,0:T(8,128)(2,1)S(1)}, u32[]{:S(2)}, u32[]{:S(2)}) %collective-permute-start.23) | collective-permute-done | bytes 65568 | tf_op jit(solution)/shard_map/ppermute | solution.py:495
  89.9 3.0 %collective-permute-start.25 = (bf16[64,1024]{1,0:T(8,128)(2,1)S(1)}, bf16[64,1024]{1,0:T(8,128)(2,1)S(1)}, u32[]{:S(2)}, u32[]{:S(2)}) collective-permute-start(bf16[64,1024]{1,0:T(8,128)(2,1)S(1)} %get-tuple-element.79), channel_id=1, source_target_pairs={{0,12},{4,8},{8,4},{12,0},{1,13},{5,9},{9,5},{13,1},{2,14},{6,10},... | collective-permute-start | bytes 393224 | tf_op jit(solution)/shard_map/ppermute | solution.py:495
  92.9 5.1 %collective-permute-done.24.rest_1_ = bf16[64,1024]{1,0:T(8,128)(2,1)S(1)} collective-permute-done((bf16[64,1024]{1,0:T(8,128)(2,1)S(1)}, bf16[64,1024]{1,0:T(8,128)(2,1)S(1)}, u32[]{:S(2)}, u32[]{:S(2)}) %collective-permute-start.24) | collective-permute-done | bytes 131104 | tf_op jit(solution)/shard_map/ppermute | solution.py:495
  100.5 1.7 %collective-permute-start.27 = (bf16[64,1024]{1,0:T(8,128)(2,1)S(1)}, bf16[64,1024]{1,0:T(8,128)(2,1)S(1)}, u32[]{:S(2)}, u32[]{:S(2)}) collective-permute-start(bf16[64,1024]{1,0:T(8,128)(2,1)S(1)} %get-tuple-element.82), channel_id=1, source_target_pairs={{0,8},{4,12},{8,0},{12,4},{1,9},{5,13},{9,1},{13,5},{2,10},{6,14},... | collective-permute-start | bytes 393224 | tf_op jit(solution)/shard_map/ppermute | solution.py:495
  102.2 3.4 %collective-permute-start.28 = (bf16[64,1024]{1,0:T(8,128)(2,1)S(1)}, bf16[64,1024]{1,0:T(8,128)(2,1)S(1)}, u32[]{:S(2)}, u32[]{:S(2)}) collective-permute-start(bf16[64,1024]{1,0:T(8,128)(2,1)S(1)} %get-tuple-element.83), channel_id=1, source_target_pairs={{0,12},{4,8},{8,4},{12,0},{1,13},{5,9},{9,5},{13,1},{2,14},{6,10},... | collective-permute-start | bytes 393224 | tf_op jit(solution)/shard_map/ppermute | solution.py:495
  106.5 3.7 %collective-permute-done.28.rest_4_ = bf16[64,1024]{1,0:T(8,128)(2,1)S(1)} collective-permute-done((bf16[64,1024]{1,0:T(8,128)(2,1)S(1)}, bf16[64,1024]{1,0:T(8,128)(2,1)S(1)}, u32[]{:S(2)}, u32[]{:S(2)}) %collective-permute-start.28) | collective-permute-done | bytes 131104 | tf_op jit(solution)/shard_map/ppermute | solution.py:495
  110.1 2.0 %collective-permute-done.29.rest_5_ = bf16[64,1024]{1,0:T(8,128)(2,1)S(1)} collective-permute-done((bf16[64,1024]{1,0:T(8,128)(2,1)S(1)}, bf16[64,1024]{1,0:T(8,128)(2,1)S(1)}, u32[]{:S(2)}, u32[]{:S(2)}) %collective-permute-start.29) | collective-permute-done | bytes 131104 | tf_op jit(solution)/shard_map/ppermute | solution.py:495
  112.6 1.8 %collective-permute-start.34 = (bf16[2,2,32,256]{3,2,1,0:T(8,128)(2,1)S(1)}, bf16[2,2,32,256]{3,2,1,0:T(8,128)(2,1)S(1)}, u32[]{:S(2)}, u32[]{:S(2)}) collective-permute-start(bf16[2,2,32,256]{3,2,1,0:T(8,128)(2,1)S(1)} %get-tuple-element.88), channel_id=1, source_target_pairs={{0,2},{2,0},{1,3},{3,1},{4,6},{6,4},{5,7},{7,5},{8,10},{10,8},{9,1... | collective-permute-start | bytes 196616 | tf_op jit(solution)/shard_map/ppermute | solution.py:495
  115.2 1.8 %collective-permute-done.34.r_ref = bf16[2,2,32,256]{3,2,1,0:T(8,128)(2,1)S(1)} collective-permute-done((bf16[2,2,32,256]{3,2,1,0:T(8,128)(2,1)S(1)}, bf16[2,2,32,256]{3,2,1,0:T(8,128)(2,1)S(1)}, u32[]{:S(2)}, u32[]{:S(2)}) %collective-permute-start.34) | collective-permute-done | bytes 65568 | tf_op jit(solution)/shard_map/ppermute | solution.py:495
  117.0 2.5 %collective-permute-start.35 = (bf16[2,2,32,256]{3,2,1,0:T(8,128)(2,1)S(1)}, bf16[2,2,32,256]{3,2,1,0:T(8,128)(2,1)S(1)}, u32[]{:S(2)}, u32[]{:S(2)}) collective-permute-start(bf16[2,2,32,256]{3,2,1,0:T(8,128)(2,1)S(1)} %shard_map.93.rest_0_), channel_id=1, source_target_pairs={{0,8},{4,12},{8,0},{12,4},{1,9},{5,13},{9,1},{13,5},{2,10},{6,14},... | collective-permute-start | bytes 196616 | tf_op jit(solution)/shard_map/ppermute | solution.py:495
  119.5 2.0 %collective-permute-start.31 = (bf16[2,2,32,256]{3,2,1,0:T(8,128)(2,1)S(1)}, bf16[2,2,32,256]{3,2,1,0:T(8,128)(2,1)S(1)}, u32[]{:S(2)}, u32[]{:S(2)}) collective-permute-start(bf16[2,2,32,256]{3,2,1,0:T(8,128)(2,1)S(1)} %shard_map.92.rest_0_), channel_id=1, source_target_pairs={{0,8},{4,12},{8,0},{12,4},{1,9},{5,13},{9,1},{13,5},{2,10},{6,14},... | collective-permute-start | bytes 196616 | tf_op jit(solution)/shard_map/ppermute | solution.py:495
  121.5 1.6 %collective-permute-start.37 = (bf16[2,2,32,256]{3,2,1,0:T(8,128)(2,1)S(1)}, bf16[2,2,32,256]{3,2,1,0:T(8,128)(2,1)S(1)}, u32[]{:S(2)}, u32[]{:S(2)}) collective-permute-start(bf16[2,2,32,256]{3,2,1,0:T(8,128)(2,1)S(1)} %shard_map.93.rest_0_), channel_id=1, source_target_pairs={{0,4},{4,0},{8,12},{12,8},{1,5},{5,1},{9,13},{13,9},{2,6},{6,2},{1... | collective-permute-start | bytes 196616 | tf_op jit(solution)/shard_map/ppermute | solution.py:495
  123.6 1.6 %collective-permute-start.33 = (bf16[2,2,32,256]{3,2,1,0:T(8,128)(2,1)S(1)}, bf16[2,2,32,256]{3,2,1,0:T(8,128)(2,1)S(1)}, u32[]{:S(2)}, u32[]{:S(2)}) collective-permute-start(bf16[2,2,32,256]{3,2,1,0:T(8,128)(2,1)S(1)} %shard_map.92.rest_0_), channel_id=1, source_target_pairs={{0,4},{4,0},{8,12},{12,8},{1,5},{5,1},{9,13},{13,9},{2,6},{6,2},{1... | collective-permute-start | bytes 196616 | tf_op jit(solution)/shard_map/ppermute | solution.py:495
  127.5 1.9 %shard_map.94.rest_4_ = bf16[64,128,256]{2,1,0:T(8,128)(2,1)} custom-call(s32[1]{0:T(128)} %bitcast._.freq.place_ref, s32[1]{0:T(128)} %bitcast.1.rblk._, s32[1]{0:T(128)} %bitcast.2.__.sblk, bf16[64,128,256]{2,1,0:T(8,128)(2,1)S(1)} %copy-done.1, s32[128,256]{1,0:T(8,128)S(1)} %copy-done.4, bf16[4,128,128]{2,1,0:T(8,128)(2,1)S(1)} %copy-done.5, ...), custom_call_target="tpu_custom_call" | custom-call | flops 33554432 | bytes 8912896 | tf_op jit(solution)/shard_map/pallas_call | solution.py:78
  129.5 1.9 %shard_map.95 = bf16[64,128,256]{2,1,0:T(8,128)(2,1)} custom-call(s32[1]{0:T(128)} %bitcast._.freq.place_ref, s32[1]{0:T(128)} %bitcast.1.rblk._, s32[1]{0:T(128)} %bitcast.2.__.sblk, bf16[64,128,256]{2,1,0:T(8,128)(2,1)S(1)} %copy-done.1, s32[128,256]{1,0:T(8,128)S(1)} %copy-done.4, ...), custom_call_target="tpu_custom_call", output_to_operand_aliasing={{}: (10, {})} | custom-call | flops 33554432 | bytes 13107200 | tf_op jit(solution)/shard_map/pallas_call | solution.py:78
  (82 shorter events, 32.0 us)
Async XLA Ops:
  2.6 19.7 %collective-permute-start = (bf16[2,512,512]{2,1,0:T(8,128)(2,1)S(1)}, bf16[2,512,512]{2,1,0:T(8,128)(2,1)S(1)}, u32[]{:S(2)}, u32[]{:S(2)}) collective-permute-start(bf16[2,512,512]{2,1,0:T(8,128)(2,1)S(1)} %get-tuple-element.47.rest_1_.rest_0_.rest_2_), channel_id=1, source_target_pairs={{0,1},{1,0},{2,3},{3,2},{4,5},{5,4},{6,7},{7,6},{8,9},{9,8},{10,11... | collective-permute-start | bytes 3145736 | tf_op jit(solution)/shard_map/ppermute | solution.py:495
  3.1 26.3 %collective-permute-start.5 = (bf16[2,512,512]{2,1,0:T(8,128)(2,1)S(1)}, bf16[2,512,512]{2,1,0:T(8,128)(2,1)S(1)}, u32[]{:S(2)}, u32[]{:S(2)}) collective-permute-start(bf16[2,512,512]{2,1,0:T(8,128)(2,1)S(1)} %get-tuple-element.61), channel_id=1, source_target_pairs={{0,2},{2,0},{1,3},{3,1},{4,6},{6,4},{5,7},{7,5},{8,10},{10,8},{9,1... | collective-permute-start | bytes 3145736 | tf_op jit(solution)/shard_map/ppermute | solution.py:495
  8.7 13.0 %collective-permute-start.2 = (bf16[2,2,64,256]{3,2,1,0:T(8,128)(2,1)S(1)}, bf16[2,2,64,256]{3,2,1,0:T(8,128)(2,1)S(1)}, u32[]{:S(2)}, u32[]{:S(2)}) collective-permute-start(bf16[2,2,64,256]{3,2,1,0:T(8,128)(2,1)S(1)} %get-tuple-element.54), channel_id=1, source_target_pairs={{0,8},{4,12},{8,0},{12,4},{1,9},{5,13},{9,1},{13,5},{2,10},{6,14},... | collective-permute-start | bytes 393224 | tf_op jit(solution)/shard_map/ppermute | solution.py:495
  11.3 10.3 %collective-permute-start.3 = (bf16[2,2,64,256]{3,2,1,0:T(8,128)(2,1)S(1)}, bf16[2,2,64,256]{3,2,1,0:T(8,128)(2,1)S(1)}, u32[]{:S(2)}, u32[]{:S(2)}) collective-permute-start(bf16[2,2,64,256]{3,2,1,0:T(8,128)(2,1)S(1)} %get-tuple-element.55), channel_id=1, source_target_pairs={{0,12},{4,8},{8,4},{12,0},{1,13},{5,9},{9,5},{13,1},{2,14},{6,10},... | collective-permute-start | bytes 393224 | tf_op jit(solution)/shard_map/ppermute | solution.py:495
  12.7 9.5 %collective-permute-start.4 = (bf16[2,2,64,256]{3,2,1,0:T(8,128)(2,1)S(1)}, bf16[2,2,64,256]{3,2,1,0:T(8,128)(2,1)S(1)}, u32[]{:S(2)}, u32[]{:S(2)}) collective-permute-start(bf16[2,2,64,256]{3,2,1,0:T(8,128)(2,1)S(1)} %get-tuple-element.56), channel_id=1, source_target_pairs={{0,4},{4,0},{8,12},{12,8},{1,5},{5,1},{9,13},{13,9},{2,6},{6,2},{1... | collective-permute-start | bytes 393224 | tf_op jit(solution)/shard_map/ppermute | solution.py:495
  29.4 5.9 %collective-permute-start.7 = (bf16[2,512,512]{2,1,0:T(8,128)(2,1)S(1)}, bf16[2,512,512]{2,1,0:T(8,128)(2,1)S(1)}, u32[]{:S(2)}, u32[]{:S(2)}) collective-permute-start(bf16[2,512,512]{2,1,0:T(8,128)(2,1)S(1)} %collective-permute-done.5.rest_2_.rest_0_.rest_3_), channel_id=1, source_target_pairs={{0,1},{1,0},{2,3},{3,2},{4,5},{5,4},{6,7},{7,6},{8,9},{9,8},{10,11... | collective-permute-start | bytes 3145736 | tf_op jit(solution)/shard_map/ppermute | solution.py:495
  29.4 5.9 %collective-permute-start.6 = (bf16[2,2,64,256]{3,2,1,0:T(8,128)(2,1)S(1)}, bf16[2,2,64,256]{3,2,1,0:T(8,128)(2,1)S(1)}, u32[]{:S(2)}, u32[]{:S(2)}) collective-permute-start(bf16[2,2,64,256]{3,2,1,0:T(8,128)(2,1)S(1)} %get-tuple-element.62.rest_0_), channel_id=1, source_target_pairs={{0,2},{2,0},{1,3},{3,1},{4,6},{6,4},{5,7},{7,5},{8,10},{10,8},{9,1... | collective-permute-start | bytes 393224 | tf_op jit(solution)/shard_map/ppermute | solution.py:495
  36.2 13.0 %collective-permute-start.8 = (bf16[64,1024]{1,0:T(8,128)(2,1)S(1)}, bf16[64,1024]{1,0:T(8,128)(2,1)S(1)}, u32[]{:S(2)}, u32[]{:S(2)}) collective-permute-start(bf16[64,1024]{1,0:T(8,128)(2,1)S(1)} %get-tuple-element.66), channel_id=1, source_target_pairs={{0,8},{4,12},{8,0},{12,4},{1,9},{5,13},{9,1},{13,5},{2,10},{6,14},... | collective-permute-start | bytes 393224 | tf_op jit(solution)/shard_map/ppermute | solution.py:495
  39.1 10.1 %collective-permute-start.9 = (bf16[64,1024]{1,0:T(8,128)(2,1)S(1)}, bf16[64,1024]{1,0:T(8,128)(2,1)S(1)}, u32[]{:S(2)}, u32[]{:S(2)}) collective-permute-start(bf16[64,1024]{1,0:T(8,128)(2,1)S(1)} %get-tuple-element.67), channel_id=1, source_target_pairs={{0,12},{4,8},{8,4},{12,0},{1,13},{5,9},{9,5},{13,1},{2,14},{6,10},... | collective-permute-start | bytes 393224 | tf_op jit(solution)/shard_map/ppermute | solution.py:495
  40.5 9.1 %collective-permute-start.10 = (bf16[64,1024]{1,0:T(8,128)(2,1)S(1)}, bf16[64,1024]{1,0:T(8,128)(2,1)S(1)}, u32[]{:S(2)}, u32[]{:S(2)}) collective-permute-start(bf16[64,1024]{1,0:T(8,128)(2,1)S(1)} %get-tuple-element.68), channel_id=1, source_target_pairs={{0,4},{4,0},{8,12},{12,8},{1,5},{5,1},{9,13},{13,9},{2,6},{6,2},{1... | collective-permute-start | bytes 393224 | tf_op jit(solution)/shard_map/ppermute | solution.py:495
  50.5 13.8 %collective-permute-start.11 = (bf16[64,1024]{1,0:T(8,128)(2,1)S(1)}, bf16[64,1024]{1,0:T(8,128)(2,1)S(1)}, u32[]{:S(2)}, u32[]{:S(2)}) collective-permute-start(bf16[64,1024]{1,0:T(8,128)(2,1)S(1)} %get-tuple-element.70), channel_id=1, source_target_pairs={{0,8},{4,12},{8,0},{12,4},{1,9},{5,13},{9,1},{13,5},{2,10},{6,14},... | collective-permute-start | bytes 393224 | tf_op jit(solution)/shard_map/ppermute | solution.py:495
  54.7 9.6 %collective-permute-start.12 = (bf16[64,1024]{1,0:T(8,128)(2,1)S(1)}, bf16[64,1024]{1,0:T(8,128)(2,1)S(1)}, u32[]{:S(2)}, u32[]{:S(2)}) collective-permute-start(bf16[64,1024]{1,0:T(8,128)(2,1)S(1)} %get-tuple-element.71), channel_id=1, source_target_pairs={{0,12},{4,8},{8,4},{12,0},{1,13},{5,9},{9,5},{13,1},{2,14},{6,10},... | collective-permute-start | bytes 393224 | tf_op jit(solution)/shard_map/ppermute | solution.py:495
  55.1 10.3 %collective-permute-start.13 = (bf16[64,1024]{1,0:T(8,128)(2,1)S(1)}, bf16[64,1024]{1,0:T(8,128)(2,1)S(1)}, u32[]{:S(2)}, u32[]{:S(2)}) collective-permute-start(bf16[64,1024]{1,0:T(8,128)(2,1)S(1)} %get-tuple-element.72), channel_id=1, source_target_pairs={{0,4},{4,0},{8,12},{12,8},{1,5},{5,1},{9,13},{13,9},{2,6},{6,2},{1... | collective-permute-start | bytes 393224 | tf_op jit(solution)/shard_map/ppermute | solution.py:495
  65.9 4.3 %collective-permute-start.14 = (bf16[2,2,32,256]{3,2,1,0:T(8,128)(2,1)S(1)}, bf16[2,2,32,256]{3,2,1,0:T(8,128)(2,1)S(1)}, u32[]{:S(2)}, u32[]{:S(2)}) collective-permute-start(bf16[2,2,32,256]{3,2,1,0:T(8,128)(2,1)S(1)} %get-tuple-element.74), channel_id=1, source_target_pairs={{0,2},{2,0},{1,3},{3,1},{4,6},{6,4},{5,7},{7,5},{8,10},{10,8},{9,1... | collective-permute-start | bytes 196616 | tf_op jit(solution)/shard_map/ppermute | solution.py:495
  67.4 4.7 %collective-permute-start.18 = (bf16[2,2,32,256]{3,2,1,0:T(8,128)(2,1)S(1)}, bf16[2,2,32,256]{3,2,1,0:T(8,128)(2,1)S(1)}, u32[]{:S(2)}, u32[]{:S(2)}) collective-permute-start(bf16[2,2,32,256]{3,2,1,0:T(8,128)(2,1)S(1)} %get-tuple-element.76), channel_id=1, source_target_pairs={{0,2},{2,0},{1,3},{3,1},{4,6},{6,4},{5,7},{7,5},{8,10},{10,8},{9,1... | collective-permute-start | bytes 196616 | tf_op jit(solution)/shard_map/ppermute | solution.py:495
  70.2 5.7 %collective-permute-start.15 = (bf16[2,2,32,256]{3,2,1,0:T(8,128)(2,1)S(1)}, bf16[2,2,32,256]{3,2,1,0:T(8,128)(2,1)S(1)}, u32[]{:S(2)}, u32[]{:S(2)}) collective-permute-start(bf16[2,2,32,256]{3,2,1,0:T(8,128)(2,1)S(1)} %shard_map.83.rest_0_), channel_id=1, source_target_pairs={{0,8},{4,12},{8,0},{12,4},{1,9},{5,13},{9,1},{13,5},{2,10},{6,14},... | collective-permute-start | bytes 196616 | tf_op jit(solution)/shard_map/ppermute | solution.py:495
  72.2 6.6 %collective-permute-start.19 = (bf16[2,2,32,256]{3,2,1,0:T(8,128)(2,1)S(1)}, bf16[2,2,32,256]{3,2,1,0:T(8,128)(2,1)S(1)}, u32[]{:S(2)}, u32[]{:S(2)}) collective-permute-start(bf16[2,2,32,256]{3,2,1,0:T(8,128)(2,1)S(1)} %shard_map.85.rest_0_), channel_id=1, source_target_pairs={{0,8},{4,12},{8,0},{12,4},{1,9},{5,13},{9,1},{13,5},{2,10},{6,14},... | collective-permute-start | bytes 196616 | tf_op jit(solution)/shard_map/ppermute | solution.py:495
  73.6 7.1 %collective-permute-start.17 = (bf16[2,2,32,256]{3,2,1,0:T(8,128)(2,1)S(1)}, bf16[2,2,32,256]{3,2,1,0:T(8,128)(2,1)S(1)}, u32[]{:S(2)}, u32[]{:S(2)}) collective-permute-start(bf16[2,2,32,256]{3,2,1,0:T(8,128)(2,1)S(1)} %shard_map.83.rest_0_), channel_id=1, source_target_pairs={{0,4},{4,0},{8,12},{12,8},{1,5},{5,1},{9,13},{13,9},{2,6},{6,2},{1... | collective-permute-start | bytes 196616 | tf_op jit(solution)/shard_map/ppermute | solution.py:495
  75.9 5.1 %collective-permute-start.16 = (bf16[2,2,32,256]{3,2,1,0:T(8,128)(2,1)S(1)}, bf16[2,2,32,256]{3,2,1,0:T(8,128)(2,1)S(1)}, u32[]{:S(2)}, u32[]{:S(2)}) collective-permute-start(bf16[2,2,32,256]{3,2,1,0:T(8,128)(2,1)S(1)} %collective-permute-done.15.rest_1_), channel_id=1, source_target_pairs={{0,4},{4,0},{8,12},{12,8},{1,5},{5,1},{9,13},{13,9},{2,6},{6,2},{1... | collective-permute-start | bytes 196616 | tf_op jit(solution)/shard_map/ppermute | solution.py:495
  78.8 4.9 %collective-permute-start.20 = (bf16[2,2,32,256]{3,2,1,0:T(8,128)(2,1)S(1)}, bf16[2,2,32,256]{3,2,1,0:T(8,128)(2,1)S(1)}, u32[]{:S(2)}, u32[]{:S(2)}) collective-permute-start(bf16[2,2,32,256]{3,2,1,0:T(8,128)(2,1)S(1)} %collective-permute-done.19.rest_1_), channel_id=1, source_target_pairs={{0,4},{4,0},{8,12},{12,8},{1,5},{5,1},{9,13},{13,9},{2,6},{6,2},{1... | collective-permute-start | bytes 196616 | tf_op jit(solution)/shard_map/ppermute | solution.py:495
  81.2 4.6 %collective-permute-start.22 = (bf16[2,2,32,256]{3,2,1,0:T(8,128)(2,1)S(1)}, bf16[2,2,32,256]{3,2,1,0:T(8,128)(2,1)S(1)}, u32[]{:S(2)}, u32[]{:S(2)}) collective-permute-start(bf16[2,2,32,256]{3,2,1,0:T(8,128)(2,1)S(1)} %shard_map.84.rest_0_), channel_id=1, source_target_pairs={{0,2},{2,0},{1,3},{3,1},{4,6},{6,4},{5,7},{7,5},{8,10},{10,8},{9,1... | collective-permute-start | bytes 196616 | tf_op jit(solution)/shard_map/ppermute | solution.py:495
  89.2 8.8 %collective-permute-start.24 = (bf16[64,1024]{1,0:T(8,128)(2,1)S(1)}, bf16[64,1024]{1,0:T(8,128)(2,1)S(1)}, u32[]{:S(2)}, u32[]{:S(2)}) collective-permute-start(bf16[64,1024]{1,0:T(8,128)(2,1)S(1)} %get-tuple-element.78), channel_id=1, source_target_pairs={{0,8},{4,12},{8,0},{12,4},{1,9},{5,13},{9,1},{13,5},{2,10},{6,14},... | collective-permute-start | bytes 393224 | tf_op jit(solution)/shard_map/ppermute | solution.py:495
  89.9 8.1 %collective-permute-start.25 = (bf16[64,1024]{1,0:T(8,128)(2,1)S(1)}, bf16[64,1024]{1,0:T(8,128)(2,1)S(1)}, u32[]{:S(2)}, u32[]{:S(2)}) collective-permute-start(bf16[64,1024]{1,0:T(8,128)(2,1)S(1)} %get-tuple-element.79), channel_id=1, source_target_pairs={{0,12},{4,8},{8,4},{12,0},{1,13},{5,9},{9,5},{13,1},{2,14},{6,10},... | collective-permute-start | bytes 393224 | tf_op jit(solution)/shard_map/ppermute | solution.py:495
  92.9 6.6 %collective-permute-start.26 = (bf16[64,1024]{1,0:T(8,128)(2,1)S(1)}, bf16[64,1024]{1,0:T(8,128)(2,1)S(1)}, u32[]{:S(2)}, u32[]{:S(2)}) collective-permute-start(bf16[64,1024]{1,0:T(8,128)(2,1)S(1)} %get-tuple-element.80), channel_id=1, source_target_pairs={{0,4},{4,0},{8,12},{12,8},{1,5},{5,1},{9,13},{13,9},{2,6},{6,2},{1... | collective-permute-start | bytes 393224 | tf_op jit(solution)/shard_map/ppermute | solution.py:495
  100.5 5.9 %collective-permute-start.27 = (bf16[64,1024]{1,0:T(8,128)(2,1)S(1)}, bf16[64,1024]{1,0:T(8,128)(2,1)S(1)}, u32[]{:S(2)}, u32[]{:S(2)}) collective-permute-start(bf16[64,1024]{1,0:T(8,128)(2,1)S(1)} %get-tuple-element.82), channel_id=1, source_target_pairs={{0,8},{4,12},{8,0},{12,4},{1,9},{5,13},{9,1},{13,5},{2,10},{6,14},... | collective-permute-start | bytes 393224 | tf_op jit(solution)/shard_map/ppermute | solution.py:495
  102.2 7.9 %collective-permute-start.28 = (bf16[64,1024]{1,0:T(8,128)(2,1)S(1)}, bf16[64,1024]{1,0:T(8,128)(2,1)S(1)}, u32[]{:S(2)}, u32[]{:S(2)}) collective-permute-start(bf16[64,1024]{1,0:T(8,128)(2,1)S(1)} %get-tuple-element.83), channel_id=1, source_target_pairs={{0,12},{4,8},{8,4},{12,0},{1,13},{5,9},{9,5},{13,1},{2,14},{6,10},... | collective-permute-start | bytes 393224 | tf_op jit(solution)/shard_map/ppermute | solution.py:495
  105.6 6.6 %collective-permute-start.29 = (bf16[64,1024]{1,0:T(8,128)(2,1)S(1)}, bf16[64,1024]{1,0:T(8,128)(2,1)S(1)}, u32[]{:S(2)}, u32[]{:S(2)}) collective-permute-start(bf16[64,1024]{1,0:T(8,128)(2,1)S(1)} %get-tuple-element.84), channel_id=1, source_target_pairs={{0,4},{4,0},{8,12},{12,8},{1,5},{5,1},{9,13},{13,9},{2,6},{6,2},{1... | collective-permute-start | bytes 393224 | tf_op jit(solution)/shard_map/ppermute | solution.py:495
  114.4 5.1 %collective-permute-start.30 = (bf16[2,2,32,256]{3,2,1,0:T(8,128)(2,1)S(1)}, bf16[2,2,32,256]{3,2,1,0:T(8,128)(2,1)S(1)}, u32[]{:S(2)}, u32[]{:S(2)}) collective-permute-start(bf16[2,2,32,256]{3,2,1,0:T(8,128)(2,1)S(1)} %get-tuple-element.86), channel_id=1, source_target_pairs={{0,2},{2,0},{1,3},{3,1},{4,6},{6,4},{5,7},{7,5},{8,10},{10,8},{9,1... | collective-permute-start | bytes 196616 | tf_op jit(solution)/shard_map/ppermute | solution.py:495
  117.0 6.2 %collective-permute-start.35 = (bf16[2,2,32,256]{3,2,1,0:T(8,128)(2,1)S(1)}, bf16[2,2,32,256]{3,2,1,0:T(8,128)(2,1)S(1)}, u32[]{:S(2)}, u32[]{:S(2)}) collective-permute-start(bf16[2,2,32,256]{3,2,1,0:T(8,128)(2,1)S(1)} %shard_map.93.rest_0_), channel_id=1, source_target_pairs={{0,8},{4,12},{8,0},{12,4},{1,9},{5,13},{9,1},{13,5},{2,10},{6,14},... | collective-permute-start | bytes 196616 | tf_op jit(solution)/shard_map/ppermute | solution.py:495
  119.5 5.7 %collective-permute-start.31 = (bf16[2,2,32,256]{3,2,1,0:T(8,128)(2,1)S(1)}, bf16[2,2,32,256]{3,2,1,0:T(8,128)(2,1)S(1)}, u32[]{:S(2)}, u32[]{:S(2)}) collective-permute-start(bf16[2,2,32,256]{3,2,1,0:T(8,128)(2,1)S(1)} %shard_map.92.rest_0_), channel_id=1, source_target_pairs={{0,8},{4,12},{8,0},{12,4},{1,9},{5,13},{9,1},{13,5},{2,10},{6,14},... | collective-permute-start | bytes 196616 | tf_op jit(solution)/shard_map/ppermute | solution.py:495
  121.5 4.9 %collective-permute-start.37 = (bf16[2,2,32,256]{3,2,1,0:T(8,128)(2,1)S(1)}, bf16[2,2,32,256]{3,2,1,0:T(8,128)(2,1)S(1)}, u32[]{:S(2)}, u32[]{:S(2)}) collective-permute-start(bf16[2,2,32,256]{3,2,1,0:T(8,128)(2,1)S(1)} %shard_map.93.rest_0_), channel_id=1, source_target_pairs={{0,4},{4,0},{8,12},{12,8},{1,5},{5,1},{9,13},{13,9},{2,6},{6,2},{1... | collective-permute-start | bytes 196616 | tf_op jit(solution)/shard_map/ppermute | solution.py:495
  123.6 5.8 %collective-permute-start.33 = (bf16[2,2,32,256]{3,2,1,0:T(8,128)(2,1)S(1)}, bf16[2,2,32,256]{3,2,1,0:T(8,128)(2,1)S(1)}, u32[]{:S(2)}, u32[]{:S(2)}) collective-permute-start(bf16[2,2,32,256]{3,2,1,0:T(8,128)(2,1)S(1)} %shard_map.92.rest_0_), channel_id=1, source_target_pairs={{0,4},{4,0},{8,12},{12,8},{1,5},{5,1},{9,13},{13,9},{2,6},{6,2},{1... | collective-permute-start | bytes 196616 | tf_op jit(solution)/shard_map/ppermute | solution.py:495
  (13 other events, 209.4 us)

commit v26 on v14

--- a/solution.py
+++ b/solution.py
@@ -21,8 +21,7 @@
 
 
 def ways(count):
-    far = sorted(range(1, count), key=lambda step: (step.bit_length() < count.bit_length() - 1, step))
-    return [0] + far
+    return [0] + list(range(count - 1, 0, -1))
 
 
 def field_rows(place, freq_devs, per_dev):

time: 130 us -> 133 us (1.023)
  waiting for transfers between devices: 56.2 us -> 69.7 us
  starting transfers between devices: 54.5 us -> 44 us
    ppermute x41, waiting for transfers between devices: 56.2 us -> 69.7 us  [exchanged(): lax.ppermute(value, axis, [(i, i ^ step) for i in range(lax.axis_size(axi...]
    ppermute x41, starting transfers between devices: 54.5 us -> 44 us  [exchanged(): lax.ppermute(value, axis, [(i, i ^ step) for i in range(lax.axis_size(axi...]
  transfers between devices with their start and end apart: 41 -> 41, of which waited for: 22 -> 26; matrix products, arithmetic and copies ran while one was open for 0% -> 0% of each run, Pallas kernels for 6% -> 6%
where the time goes in v26:
time: 133 us
  waiting for transfers between devices  69.7 us (52%)
  starting transfers between devices  44 us (33%)
  Pallas kernels  14.2 us (11%)
  local copies, waits for them, and re-layouts  4.56 us (3%)
    ppermute x41, waiting for transfers between devices, exchanged(): lax.ppermute(value, axis, [(i, i ^ step) for i in range(lax.axis_size(axi...  69.7 us
    ppermute x41, starting transfers between devices, exchanged(): lax.ppermute(value, axis, [(i, i ^ step) for i in range(lax.axis_size(axi...  44 us
    pallas_call x24, Pallas kernels, call(): pl.pallas_call(body, grid_spec=pltpu.PrefetchScalarGridSpec(num_scalar_pr...  14.2 us
    unnamed x15, local copies, waits for them, and re-layouts  4.56 us
  transfers between devices with their start and end apart: 41, of which 26 were waited for; matrix products, arithmetic and copies ran while one was open for 0% of the time, Pallas kernels for 6%

profile of v26, /device:TPU:0, one launch (start us, length us, event | category | flops | bytes accessed | tf_op | source)
XLA Modules:
  0.0 132.8 jit_solution(3570592265614171659)
XLA Ops:
  2.6 3.0 %collective-permute-start.6 = (bf16[2,256,512]{2,1,0:T(8,128)(2,1)S(1)}, bf16[2,256,512]{2,1,0:T(8,128)(2,1)S(1)}, u32[]{:S(2)}, u32[]{:S(2)}) collective-permute-start(bf16[2,256,512]{2,1,0:T(8,128)(2,1)S(1)} %get-tuple-element.66), channel_id=1, source_target_pairs={{0,2},{2,0},{1,3},{3,1},{4,6},{6,4},{5,7},{7,5},{8,10},{10,8},{9,1... | collective-permute-start | bytes 1572872 | tf_op jit(solution)/shard_map/ppermute | solution.py:494
  5.7 2.2 %copy-done = bf16[64,128,256]{2,1,0:T(8,128)(2,1)S(1)} copy-done((bf16[64,128,256]{2,1,0:T(8,128)(2,1)S(1)}, bf16[64,128,256]{2,1,0:T(8,128)(2,1)}, u32[]{:S(2)}) %copy-start) | copy-done | bytes 4194328
  8.6 4.1 %collective-permute-start.3 = (bf16[2,2,64,256]{3,2,1,0:T(8,128)(2,1)S(1)}, bf16[2,2,64,256]{3,2,1,0:T(8,128)(2,1)S(1)}, u32[]{:S(2)}, u32[]{:S(2)}) collective-permute-start(bf16[2,2,64,256]{3,2,1,0:T(8,128)(2,1)S(1)} %get-tuple-element.59), channel_id=1, source_target_pairs={{0,12},{4,8},{8,4},{12,0},{1,13},{5,9},{9,5},{13,1},{2,14},{6,10},... | collective-permute-start | bytes 393224 | tf_op jit(solution)/shard_map/ppermute | solution.py:494
  13.4 3.8 %collective-permute-done.3.refs_1_ = bf16[2,2,64,256]{3,2,1,0:T(8,128)(2,1)S(1)} collective-permute-done((bf16[2,2,64,256]{3,2,1,0:T(8,128)(2,1)S(1)}, bf16[2,2,64,256]{3,2,1,0:T(8,128)(2,1)S(1)}, u32[]{:S(2)}, u32[]{:S(2)}) %collective-permute-start.3) | collective-permute-done | bytes 131104 | tf_op jit(solution)/shard_map/ppermute | solution.py:494
  17.2 6.1 %collective-permute-done.4.refs_2_ = bf16[2,2,64,256]{3,2,1,0:T(8,128)(2,1)S(1)} collective-permute-done((bf16[2,2,64,256]{3,2,1,0:T(8,128)(2,1)S(1)}, bf16[2,2,64,256]{3,2,1,0:T(8,128)(2,1)S(1)}, u32[]{:S(2)}, u32[]{:S(2)}) %collective-permute-start.4) | collective-permute-done | bytes 131104 | tf_op jit(solution)/shard_map/ppermute | solution.py:494
  25.5 6.0 %collective-permute-done.8.rest_1_ = bf16[2,2,64,256]{3,2,1,0:T(8,128)(2,1)S(1)} collective-permute-done((bf16[2,2,64,256]{3,2,1,0:T(8,128)(2,1)S(1)}, bf16[2,2,64,256]{3,2,1,0:T(8,128)(2,1)S(1)}, u32[]{:S(2)}, u32[]{:S(2)}) %collective-permute-start.8) | collective-permute-done | bytes 131104 | tf_op jit(solution)/shard_map/ppermute | solution.py:494
  34.0 3.9 %collective-permute-start.11 = (bf16[64,1024]{1,0:T(8,128)(2,1)S(1)}, bf16[64,1024]{1,0:T(8,128)(2,1)S(1)}, u32[]{:S(2)}, u32[]{:S(2)}) collective-permute-start(bf16[64,1024]{1,0:T(8,128)(2,1)S(1)} %get-tuple-element.74), channel_id=1, source_target_pairs={{0,12},{4,8},{8,4},{12,0},{1,13},{5,9},{9,5},{13,1},{2,14},{6,10},... | collective-permute-start | bytes 393224 | tf_op jit(solution)/shard_map/ppermute | solution.py:494
  42.3 7.0 %collective-permute-done.12.rest_2_ = bf16[64,1024]{1,0:T(8,128)(2,1)S(1)} collective-permute-done((bf16[64,1024]{1,0:T(8,128)(2,1)S(1)}, bf16[64,1024]{1,0:T(8,128)(2,1)S(1)}, u32[]{:S(2)}, u32[]{:S(2)}) %collective-permute-start.12) | collective-permute-done | bytes 131104 | tf_op jit(solution)/shard_map/ppermute | solution.py:494
  50.3 2.6 %collective-permute-start.14 = (bf16[64,1024]{1,0:T(8,128)(2,1)S(1)}, bf16[64,1024]{1,0:T(8,128)(2,1)S(1)}, u32[]{:S(2)}, u32[]{:S(2)}) collective-permute-start(bf16[64,1024]{1,0:T(8,128)(2,1)S(1)} %get-tuple-element.78), channel_id=1, source_target_pairs={{0,12},{4,8},{8,4},{12,0},{1,13},{5,9},{9,5},{13,1},{2,14},{6,10},... | collective-permute-start | bytes 393224 | tf_op jit(solution)/shard_map/ppermute | solution.py:494
  52.9 1.9 %collective-permute-start.16 = (bf16[64,1024]{1,0:T(8,128)(2,1)S(1)}, bf16[64,1024]{1,0:T(8,128)(2,1)S(1)}, u32[]{:S(2)}, u32[]{:S(2)}) collective-permute-start(bf16[64,1024]{1,0:T(8,128)(2,1)S(1)} %get-tuple-element.80), channel_id=1, source_target_pairs={{0,4},{4,0},{8,12},{12,8},{1,5},{5,1},{9,13},{13,9},{2,6},{6,2},{1... | collective-permute-start | bytes 393224 | tf_op jit(solution)/shard_map/ppermute | solution.py:494
  54.8 3.8 %collective-permute-done.14.rest_5_ = bf16[64,1024]{1,0:T(8,128)(2,1)S(1)} collective-permute-done((bf16[64,1024]{1,0:T(8,128)(2,1)S(1)}, bf16[64,1024]{1,0:T(8,128)(2,1)S(1)}, u32[]{:S(2)}, u32[]{:S(2)}) %collective-permute-start.14) | collective-permute-done | bytes 131104 | tf_op jit(solution)/shard_map/ppermute | solution.py:494
  58.6 4.5 %collective-permute-done.15.rest_6_ = bf16[64,1024]{1,0:T(8,128)(2,1)S(1)} collective-permute-done((bf16[64,1024]{1,0:T(8,128)(2,1)S(1)}, bf16[64,1024]{1,0:T(8,128)(2,1)S(1)}, u32[]{:S(2)}, u32[]{:S(2)}) %collective-permute-start.15) | collective-permute-done | bytes 131104 | tf_op jit(solution)/shard_map/ppermute | solution.py:494
  66.1 2.4 %collective-permute-done.17.r_ref = bf16[2,2,32,256]{3,2,1,0:T(8,128)(2,1)S(1)} collective-permute-done((bf16[2,2,32,256]{3,2,1,0:T(8,128)(2,1)S(1)}, bf16[2,2,32,256]{3,2,1,0:T(8,128)(2,1)S(1)}, u32[]{:S(2)}, u32[]{:S(2)}) %collective-permute-start.17) | collective-permute-done | bytes 65568 | tf_op jit(solution)/shard_map/ppermute | solution.py:494
  69.4 2.2 %collective-permute-start.22 = (bf16[2,2,32,256]{3,2,1,0:T(8,128)(2,1)S(1)}, bf16[2,2,32,256]{3,2,1,0:T(8,128)(2,1)S(1)}, u32[]{:S(2)}, u32[]{:S(2)}) collective-permute-start(bf16[2,2,32,256]{3,2,1,0:T(8,128)(2,1)S(1)} %shard_map.86.rest_0_), channel_id=1, source_target_pairs={{0,8},{4,12},{8,0},{12,4},{1,9},{5,13},{9,1},{13,5},{2,10},{6,14},... | collective-permute-start | bytes 196616 | tf_op jit(solution)/shard_map/ppermute | solution.py:494
  72.0 3.0 %collective-permute-done.18.rest_2_ = bf16[2,2,32,256]{3,2,1,0:T(8,128)(2,1)S(1)} collective-permute-done((bf16[2,2,32,256]{3,2,1,0:T(8,128)(2,1)S(1)}, bf16[2,2,32,256]{3,2,1,0:T(8,128)(2,1)S(1)}, u32[]{:S(2)}, u32[]{:S(2)}) %collective-permute-start.18) | collective-permute-done | bytes 65568 | tf_op jit(solution)/shard_map/ppermute | solution.py:494
  75.0 2.0 %collective-permute-start.24 = (bf16[2,2,32,256]{3,2,1,0:T(8,128)(2,1)S(1)}, bf16[2,2,32,256]{3,2,1,0:T(8,128)(2,1)S(1)}, u32[]{:S(2)}, u32[]{:S(2)}) collective-permute-start(bf16[2,2,32,256]{3,2,1,0:T(8,128)(2,1)S(1)} %shard_map.86.rest_0_), channel_id=1, source_target_pairs={{0,4},{4,0},{8,12},{12,8},{1,5},{5,1},{9,13},{13,9},{2,6},{6,2},{1... | collective-permute-start | bytes 196616 | tf_op jit(solution)/shard_map/ppermute | solution.py:494
  77.3 2.0 %collective-permute-done.19.rest_1_ = bf16[2,2,32,256]{3,2,1,0:T(8,128)(2,1)S(1)} collective-permute-done((bf16[2,2,32,256]{3,2,1,0:T(8,128)(2,1)S(1)}, bf16[2,2,32,256]{3,2,1,0:T(8,128)(2,1)S(1)}, u32[]{:S(2)}, u32[]{:S(2)}) %collective-permute-start.19) | collective-permute-done | bytes 65568 | tf_op jit(solution)/shard_map/ppermute | solution.py:494
  83.8 2.0 %collective-permute-done.26.rest_2_ = bf16[2,2,32,256]{3,2,1,0:T(8,128)(2,1)S(1)} collective-permute-done((bf16[2,2,32,256]{3,2,1,0:T(8,128)(2,1)S(1)}, bf16[2,2,32,256]{3,2,1,0:T(8,128)(2,1)S(1)}, u32[]{:S(2)}, u32[]{:S(2)}) %collective-permute-start.26) | collective-permute-done | bytes 65568 | tf_op jit(solution)/shard_map/ppermute | solution.py:494
  86.7 1.6 %collective-permute-start.27 = (bf16[64,1024]{1,0:T(8,128)(2,1)S(1)}, bf16[64,1024]{1,0:T(8,128)(2,1)S(1)}, u32[]{:S(2)}, u32[]{:S(2)}) collective-permute-start(bf16[64,1024]{1,0:T(8,128)(2,1)S(1)} %get-tuple-element.86), channel_id=1, source_target_pairs={{0,12},{4,8},{8,4},{12,0},{1,13},{5,9},{9,5},{13,1},{2,14},{6,10},... | collective-permute-start | bytes 393224 | tf_op jit(solution)/shard_map/ppermute | solution.py:494
  89.0 2.2 %collective-permute-start.29 = (bf16[64,1024]{1,0:T(8,128)(2,1)S(1)}, bf16[64,1024]{1,0:T(8,128)(2,1)S(1)}, u32[]{:S(2)}, u32[]{:S(2)}) collective-permute-start(bf16[64,1024]{1,0:T(8,128)(2,1)S(1)} %get-tuple-element.88), channel_id=1, source_target_pairs={{0,4},{4,0},{8,12},{12,8},{1,5},{5,1},{9,13},{13,9},{2,6},{6,2},{1... | collective-permute-start | bytes 393224 | tf_op jit(solution)/shard_map/ppermute | solution.py:494
  91.2 2.6 %collective-permute-done.27.rest_1_ = bf16[64,1024]{1,0:T(8,128)(2,1)S(1)} collective-permute-done((bf16[64,1024]{1,0:T(8,128)(2,1)S(1)}, bf16[64,1024]{1,0:T(8,128)(2,1)S(1)}, u32[]{:S(2)}, u32[]{:S(2)}) %collective-permute-start.27) | collective-permute-done | bytes 131104 | tf_op jit(solution)/shard_map/ppermute | solution.py:494
  93.8 7.3 %collective-permute-done.28.rest_2_ = bf16[64,1024]{1,0:T(8,128)(2,1)S(1)} collective-permute-done((bf16[64,1024]{1,0:T(8,128)(2,1)S(1)}, bf16[64,1024]{1,0:T(8,128)(2,1)S(1)}, u32[]{:S(2)}, u32[]{:S(2)}) %collective-permute-start.28) | collective-permute-done | bytes 131104 | tf_op jit(solution)/shard_map/ppermute | solution.py:494
  102.1 1.9 %collective-permute-start.30 = (bf16[64,1024]{1,0:T(8,128)(2,1)S(1)}, bf16[64,1024]{1,0:T(8,128)(2,1)S(1)}, u32[]{:S(2)}, u32[]{:S(2)}) collective-permute-start(bf16[64,1024]{1,0:T(8,128)(2,1)S(1)} %get-tuple-element.90), channel_id=1, source_target_pairs={{0,12},{4,8},{8,4},{12,0},{1,13},{5,9},{9,5},{13,1},{2,14},{6,10},... | collective-permute-start | bytes 393224 | tf_op jit(solution)/shard_map/ppermute | solution.py:494
  104.0 2.6 %collective-permute-start.32 = (bf16[64,1024]{1,0:T(8,128)(2,1)S(1)}, bf16[64,1024]{1,0:T(8,128)(2,1)S(1)}, u32[]{:S(2)}, u32[]{:S(2)}) collective-permute-start(bf16[64,1024]{1,0:T(8,128)(2,1)S(1)} %get-tuple-element.92), channel_id=1, source_target_pairs={{0,4},{4,0},{8,12},{12,8},{1,5},{5,1},{9,13},{13,9},{2,6},{6,2},{1... | collective-permute-start | bytes 393224 | tf_op jit(solution)/shard_map/ppermute | solution.py:494
  106.6 3.0 %collective-permute-done.30.rest_5_ = bf16[64,1024]{1,0:T(8,128)(2,1)S(1)} collective-permute-done((bf16[64,1024]{1,0:T(8,128)(2,1)S(1)}, bf16[64,1024]{1,0:T(8,128)(2,1)S(1)}, u32[]{:S(2)}, u32[]{:S(2)}) %collective-permute-start.30) | collective-permute-done | bytes 131104 | tf_op jit(solution)/shard_map/ppermute | solution.py:494
  109.5 4.9 %collective-permute-done.31.rest_6_ = bf16[64,1024]{1,0:T(8,128)(2,1)S(1)} collective-permute-done((bf16[64,1024]{1,0:T(8,128)(2,1)S(1)}, bf16[64,1024]{1,0:T(8,128)(2,1)S(1)}, u32[]{:S(2)}, u32[]{:S(2)}) %collective-permute-start.31) | collective-permute-done | bytes 131104 | tf_op jit(solution)/shard_map/ppermute | solution.py:494
  117.5 1.8 %collective-permute-done.37.r_ref = bf16[2,2,32,256]{3,2,1,0:T(8,128)(2,1)S(1)} collective-permute-done((bf16[2,2,32,256]{3,2,1,0:T(8,128)(2,1)S(1)}, bf16[2,2,32,256]{3,2,1,0:T(8,128)(2,1)S(1)}, u32[]{:S(2)}, u32[]{:S(2)}) %collective-permute-start.37) | collective-permute-done | bytes 65568 | tf_op jit(solution)/shard_map/ppermute | solution.py:494
  120.2 2.2 %collective-permute-start.34 = (bf16[2,2,32,256]{3,2,1,0:T(8,128)(2,1)S(1)}, bf16[2,2,32,256]{3,2,1,0:T(8,128)(2,1)S(1)}, u32[]{:S(2)}, u32[]{:S(2)}) collective-permute-start(bf16[2,2,32,256]{3,2,1,0:T(8,128)(2,1)S(1)} %shard_map.93.rest_0_), channel_id=1, source_target_pairs={{0,8},{4,12},{8,0},{12,4},{1,9},{5,13},{9,1},{13,5},{2,10},{6,14},... | collective-permute-start | bytes 196616 | tf_op jit(solution)/shard_map/ppermute | solution.py:494
  124.5 2.0 %collective-permute-start.36 = (bf16[2,2,32,256]{3,2,1,0:T(8,128)(2,1)S(1)}, bf16[2,2,32,256]{3,2,1,0:T(8,128)(2,1)S(1)}, u32[]{:S(2)}, u32[]{:S(2)}) collective-permute-start(bf16[2,2,32,256]{3,2,1,0:T(8,128)(2,1)S(1)} %shard_map.93.rest_0_), channel_id=1, source_target_pairs={{0,4},{4,0},{8,12},{12,8},{1,5},{5,1},{9,13},{13,9},{2,6},{6,2},{1... | collective-permute-start | bytes 196616 | tf_op jit(solution)/shard_map/ppermute | solution.py:494
  127.0 1.8 %collective-permute-done.39.rest_1_ = bf16[2,2,32,256]{3,2,1,0:T(8,128)(2,1)S(1)} collective-permute-done((bf16[2,2,32,256]{3,2,1,0:T(8,128)(2,1)S(1)}, bf16[2,2,32,256]{3,2,1,0:T(8,128)(2,1)S(1)}, u32[]{:S(2)}, u32[]{:S(2)}) %collective-permute-start.39) | collective-permute-done | bytes 65568 | tf_op jit(solution)/shard_map/ppermute | solution.py:494
  128.8 1.9 %shard_map.95.rest_4_ = bf16[64,128,256]{2,1,0:T(8,128)(2,1)} custom-call(s32[1]{0:T(128)} %bitcast._.freq.place_ref, s32[1]{0:T(128)} %bitcast.1.rblk._, s32[1]{0:T(128)} %bitcast.2.__.sblk, bf16[64,128,256]{2,1,0:T(8,128)(2,1)S(1)} %copy-done.1, s32[128,256]{1,0:T(8,128)S(1)} %copy-done.4, bf16[4,128,128]{2,1,0:T(8,128)(2,1)S(1)} %copy-done.5, ...), custom_call_target="tpu_custom_call" | custom-call | flops 33554432 | bytes 8912896 | tf_op jit(solution)/shard_map/pallas_call | solution.py:77
  130.8 1.9 %shard_map.96 = bf16[64,128,256]{2,1,0:T(8,128)(2,1)} custom-call(s32[1]{0:T(128)} %bitcast._.freq.place_ref, s32[1]{0:T(128)} %bitcast.1.rblk._, s32[1]{0:T(128)} %bitcast.2.__.sblk, bf16[64,128,256]{2,1,0:T(8,128)(2,1)S(1)} %copy-done.1, s32[128,256]{1,0:T(8,128)S(1)} %copy-done.4, ...), custom_call_target="tpu_custom_call", output_to_operand_aliasing={{}: (10, {})} | custom-call | flops 33554432 | bytes 13107200 | tf_op jit(solution)/shard_map/pallas_call | solution.py:77
  (89 shorter events, 32.2 us)
Async XLA Ops:
  2.6 22.9 %collective-permute-start.6 = (bf16[2,256,512]{2,1,0:T(8,128)(2,1)S(1)}, bf16[2,256,512]{2,1,0:T(8,128)(2,1)S(1)}, u32[]{:S(2)}, u32[]{:S(2)}) collective-permute-start(bf16[2,256,512]{2,1,0:T(8,128)(2,1)S(1)} %get-tuple-element.66), channel_id=1, source_target_pairs={{0,2},{2,0},{1,3},{3,1},{4,6},{6,4},{5,7},{7,5},{8,10},{10,8},{9,1... | collective-permute-start | bytes 1572872 | tf_op jit(solution)/shard_map/ppermute | solution.py:494
  5.6 26.0 %collective-permute-start.7 = (bf16[2,256,512]{2,1,0:T(8,128)(2,1)S(1)}, bf16[2,256,512]{2,1,0:T(8,128)(2,1)S(1)}, u32[]{:S(2)}, u32[]{:S(2)}) collective-permute-start(bf16[2,256,512]{2,1,0:T(8,128)(2,1)S(1)} %get-tuple-element.69), channel_id=1, source_target_pairs={{0,2},{2,0},{1,3},{3,1},{4,6},{6,4},{5,7},{7,5},{8,10},{10,8},{9,1... | collective-permute-start | bytes 1572872 | tf_op jit(solution)/shard_map/ppermute | solution.py:494
  8.6 8.6 %collective-permute-start.3 = (bf16[2,2,64,256]{3,2,1,0:T(8,128)(2,1)S(1)}, bf16[2,2,64,256]{3,2,1,0:T(8,128)(2,1)S(1)}, u32[]{:S(2)}, u32[]{:S(2)}) collective-permute-start(bf16[2,2,64,256]{3,2,1,0:T(8,128)(2,1)S(1)} %get-tuple-element.59), channel_id=1, source_target_pairs={{0,12},{4,8},{8,4},{12,0},{1,13},{5,9},{9,5},{13,1},{2,14},{6,10},... | collective-permute-start | bytes 393224 | tf_op jit(solution)/shard_map/ppermute | solution.py:494
  12.7 10.5 %collective-permute-start.4 = (bf16[2,2,64,256]{3,2,1,0:T(8,128)(2,1)S(1)}, bf16[2,2,64,256]{3,2,1,0:T(8,128)(2,1)S(1)}, u32[]{:S(2)}, u32[]{:S(2)}) collective-permute-start(bf16[2,2,64,256]{3,2,1,0:T(8,128)(2,1)S(1)} %get-tuple-element.60), channel_id=1, source_target_pairs={{0,8},{4,12},{8,0},{12,4},{1,9},{5,13},{9,1},{13,5},{2,10},{6,14},... | collective-permute-start | bytes 393224 | tf_op jit(solution)/shard_map/ppermute | solution.py:494
  12.7 10.5 %collective-permute-start.5 = (bf16[2,2,64,256]{3,2,1,0:T(8,128)(2,1)S(1)}, bf16[2,2,64,256]{3,2,1,0:T(8,128)(2,1)S(1)}, u32[]{:S(2)}, u32[]{:S(2)}) collective-permute-start(bf16[2,2,64,256]{3,2,1,0:T(8,128)(2,1)S(1)} %get-tuple-element.61), channel_id=1, source_target_pairs={{0,4},{4,0},{8,12},{12,8},{1,5},{5,1},{9,13},{13,9},{2,6},{6,2},{1... | collective-permute-start | bytes 393224 | tf_op jit(solution)/shard_map/ppermute | solution.py:494
  23.3 8.2 %collective-permute-start.8 = (bf16[2,2,64,256]{3,2,1,0:T(8,128)(2,1)S(1)}, bf16[2,2,64,256]{3,2,1,0:T(8,128)(2,1)S(1)}, u32[]{:S(2)}, u32[]{:S(2)}) collective-permute-start(bf16[2,2,64,256]{3,2,1,0:T(8,128)(2,1)S(1)} %get-tuple-element.68.rest_0_), channel_id=1, source_target_pairs={{0,2},{2,0},{1,3},{3,1},{4,6},{6,4},{5,7},{7,5},{8,10},{10,8},{9,1... | collective-permute-start | bytes 393224 | tf_op jit(solution)/shard_map/ppermute | solution.py:494
  24.9 6.7 %collective-permute-start = (bf16[2,256,512]{2,1,0:T(8,128)(2,1)S(1)}, bf16[2,256,512]{2,1,0:T(8,128)(2,1)S(1)}, u32[]{:S(2)}, u32[]{:S(2)}) collective-permute-start(bf16[2,256,512]{2,1,0:T(8,128)(2,1)S(1)} %get-tuple-element.51.rest_1_.rest_0_.rest_2_), channel_id=1, source_target_pairs={{0,1},{1,0},{2,3},{3,2},{4,5},{5,4},{6,7},{7,6},{8,9},{9,8},{10,11... | collective-permute-start | bytes 1572872 | tf_op jit(solution)/shard_map/ppermute | solution.py:494
  24.9 6.6 %collective-permute-start.1 = (bf16[2,256,512]{2,1,0:T(8,128)(2,1)S(1)}, bf16[2,256,512]{2,1,0:T(8,128)(2,1)S(1)}, u32[]{:S(2)}, u32[]{:S(2)}) collective-permute-start(bf16[2,256,512]{2,1,0:T(8,128)(2,1)S(1)} %get-tuple-element.52.rest_3_.rest_2_.rest_4_), channel_id=1, source_target_pairs={{0,1},{1,0},{2,3},{3,2},{4,5},{5,4},{6,7},{7,6},{8,9},{9,8},{10,11... | collective-permute-start | bytes 1572872 | tf_op jit(solution)/shard_map/ppermute | solution.py:494
  25.4 7.0 %collective-permute-start.9 = (bf16[2,256,512]{2,1,0:T(8,128)(2,1)S(1)}, bf16[2,256,512]{2,1,0:T(8,128)(2,1)S(1)}, u32[]{:S(2)}, u32[]{:S(2)}) collective-permute-start(bf16[2,256,512]{2,1,0:T(8,128)(2,1)S(1)} %collective-permute-done.6.rest_2_.rest_0_.rest_3_), channel_id=1, source_target_pairs={{0,1},{1,0},{2,3},{3,2},{4,5},{5,4},{6,7},{7,6},{8,9},{9,8},{10,11... | collective-permute-start | bytes 1572872 | tf_op jit(solution)/shard_map/ppermute | solution.py:494
  34.0 8.3 %collective-permute-start.11 = (bf16[64,1024]{1,0:T(8,128)(2,1)S(1)}, bf16[64,1024]{1,0:T(8,128)(2,1)S(1)}, u32[]{:S(2)}, u32[]{:S(2)}) collective-permute-start(bf16[64,1024]{1,0:T(8,128)(2,1)S(1)} %get-tuple-element.74), channel_id=1, source_target_pairs={{0,12},{4,8},{8,4},{12,0},{1,13},{5,9},{9,5},{13,1},{2,14},{6,10},... | collective-permute-start | bytes 393224 | tf_op jit(solution)/shard_map/ppermute | solution.py:494
  37.9 11.4 %collective-permute-start.12 = (bf16[64,1024]{1,0:T(8,128)(2,1)S(1)}, bf16[64,1024]{1,0:T(8,128)(2,1)S(1)}, u32[]{:S(2)}, u32[]{:S(2)}) collective-permute-start(bf16[64,1024]{1,0:T(8,128)(2,1)S(1)} %get-tuple-element.75), channel_id=1, source_target_pairs={{0,8},{4,12},{8,0},{12,4},{1,9},{5,13},{9,1},{13,5},{2,10},{6,14},... | collective-permute-start | bytes 393224 | tf_op jit(solution)/shard_map/ppermute | solution.py:494
  37.9 11.4 %collective-permute-start.13 = (bf16[64,1024]{1,0:T(8,128)(2,1)S(1)}, bf16[64,1024]{1,0:T(8,128)(2,1)S(1)}, u32[]{:S(2)}, u32[]{:S(2)}) collective-permute-start(bf16[64,1024]{1,0:T(8,128)(2,1)S(1)} %get-tuple-element.76), channel_id=1, source_target_pairs={{0,4},{4,0},{8,12},{12,8},{1,5},{5,1},{9,13},{13,9},{2,6},{6,2},{1... | collective-permute-start | bytes 393224 | tf_op jit(solution)/shard_map/ppermute | solution.py:494
  50.3 8.3 %collective-permute-start.14 = (bf16[64,1024]{1,0:T(8,128)(2,1)S(1)}, bf16[64,1024]{1,0:T(8,128)(2,1)S(1)}, u32[]{:S(2)}, u32[]{:S(2)}) collective-permute-start(bf16[64,1024]{1,0:T(8,128)(2,1)S(1)} %get-tuple-element.78), channel_id=1, source_target_pairs={{0,12},{4,8},{8,4},{12,0},{1,13},{5,9},{9,5},{13,1},{2,14},{6,10},... | collective-permute-start | bytes 393224 | tf_op jit(solution)/shard_map/ppermute | solution.py:494
  52.9 10.2 %collective-permute-start.15 = (bf16[64,1024]{1,0:T(8,128)(2,1)S(1)}, bf16[64,1024]{1,0:T(8,128)(2,1)S(1)}, u32[]{:S(2)}, u32[]{:S(2)}) collective-permute-start(bf16[64,1024]{1,0:T(8,128)(2,1)S(1)} %get-tuple-element.79), channel_id=1, source_target_pairs={{0,8},{4,12},{8,0},{12,4},{1,9},{5,13},{9,1},{13,5},{2,10},{6,14},... | collective-permute-start | bytes 393224 | tf_op jit(solution)/shard_map/ppermute | solution.py:494
  52.9 10.2 %collective-permute-start.16 = (bf16[64,1024]{1,0:T(8,128)(2,1)S(1)}, bf16[64,1024]{1,0:T(8,128)(2,1)S(1)}, u32[]{:S(2)}, u32[]{:S(2)}) collective-permute-start(bf16[64,1024]{1,0:T(8,128)(2,1)S(1)} %get-tuple-element.80), channel_id=1, source_target_pairs={{0,4},{4,0},{8,12},{12,8},{1,5},{5,1},{9,13},{13,9},{2,6},{6,2},{1... | collective-permute-start | bytes 393224 | tf_op jit(solution)/shard_map/ppermute | solution.py:494
  63.6 5.0 %collective-permute-start.17 = (bf16[2,2,32,256]{3,2,1,0:T(8,128)(2,1)S(1)}, bf16[2,2,32,256]{3,2,1,0:T(8,128)(2,1)S(1)}, u32[]{:S(2)}, u32[]{:S(2)}) collective-permute-start(bf16[2,2,32,256]{3,2,1,0:T(8,128)(2,1)S(1)} %get-tuple-element.82), channel_id=1, source_target_pairs={{0,2},{2,0},{1,3},{3,1},{4,6},{6,4},{5,7},{7,5},{8,10},{10,8},{9,1... | collective-permute-start | bytes 196616 | tf_op jit(solution)/shard_map/ppermute | solution.py:494
  68.6 6.4 %collective-permute-start.18 = (bf16[2,2,32,256]{3,2,1,0:T(8,128)(2,1)S(1)}, bf16[2,2,32,256]{3,2,1,0:T(8,128)(2,1)S(1)}, u32[]{:S(2)}, u32[]{:S(2)}) collective-permute-start(bf16[2,2,32,256]{3,2,1,0:T(8,128)(2,1)S(1)} %shard_map.84.rest_0_), channel_id=1, source_target_pairs={{0,8},{4,12},{8,0},{12,4},{1,9},{5,13},{9,1},{13,5},{2,10},{6,14},... | collective-permute-start | bytes 196616 | tf_op jit(solution)/shard_map/ppermute | solution.py:494
  69.4 7.6 %collective-permute-start.22 = (bf16[2,2,32,256]{3,2,1,0:T(8,128)(2,1)S(1)}, bf16[2,2,32,256]{3,2,1,0:T(8,128)(2,1)S(1)}, u32[]{:S(2)}, u32[]{:S(2)}) collective-permute-start(bf16[2,2,32,256]{3,2,1,0:T(8,128)(2,1)S(1)} %shard_map.86.rest_0_), channel_id=1, source_target_pairs={{0,8},{4,12},{8,0},{12,4},{1,9},{5,13},{9,1},{13,5},{2,10},{6,14},... | collective-permute-start | bytes 196616 | tf_op jit(solution)/shard_map/ppermute | solution.py:494
  71.6 5.6 %collective-permute-start.20 = (bf16[2,2,32,256]{3,2,1,0:T(8,128)(2,1)S(1)}, bf16[2,2,32,256]{3,2,1,0:T(8,128)(2,1)S(1)}, u32[]{:S(2)}, u32[]{:S(2)}) collective-permute-start(bf16[2,2,32,256]{3,2,1,0:T(8,128)(2,1)S(1)} %shard_map.84.rest_0_), channel_id=1, source_target_pairs={{0,4},{4,0},{8,12},{12,8},{1,5},{5,1},{9,13},{13,9},{2,6},{6,2},{1... | collective-permute-start | bytes 196616 | tf_op jit(solution)/shard_map/ppermute | solution.py:494
  75.0 5.4 %collective-permute-start.24 = (bf16[2,2,32,256]{3,2,1,0:T(8,128)(2,1)S(1)}, bf16[2,2,32,256]{3,2,1,0:T(8,128)(2,1)S(1)}, u32[]{:S(2)}, u32[]{:S(2)}) collective-permute-start(bf16[2,2,32,256]{3,2,1,0:T(8,128)(2,1)S(1)} %shard_map.86.rest_0_), channel_id=1, source_target_pairs={{0,4},{4,0},{8,12},{12,8},{1,5},{5,1},{9,13},{13,9},{2,6},{6,2},{1... | collective-permute-start | bytes 196616 | tf_op jit(solution)/shard_map/ppermute | solution.py:494
  79.5 4.3 %collective-permute-start.25 = (bf16[2,2,32,256]{3,2,1,0:T(8,128)(2,1)S(1)}, bf16[2,2,32,256]{3,2,1,0:T(8,128)(2,1)S(1)}, u32[]{:S(2)}, u32[]{:S(2)}) collective-permute-start(bf16[2,2,32,256]{3,2,1,0:T(8,128)(2,1)S(1)} %shard_map.85.rest_0_), channel_id=1, source_target_pairs={{0,2},{2,0},{1,3},{3,1},{4,6},{6,4},{5,7},{7,5},{8,10},{10,8},{9,1... | collective-permute-start | bytes 196616 | tf_op jit(solution)/shard_map/ppermute | solution.py:494
  81.5 4.3 %collective-permute-start.26 = (bf16[2,2,32,256]{3,2,1,0:T(8,128)(2,1)S(1)}, bf16[2,2,32,256]{3,2,1,0:T(8,128)(2,1)S(1)}, u32[]{:S(2)}, u32[]{:S(2)}) collective-permute-start(bf16[2,2,32,256]{3,2,1,0:T(8,128)(2,1)S(1)} %shard_map.87.rest_1_), channel_id=1, source_target_pairs={{0,2},{2,0},{1,3},{3,1},{4,6},{6,4},{5,7},{7,5},{8,10},{10,8},{9,1... | collective-permute-start | bytes 196616 | tf_op jit(solution)/shard_map/ppermute | solution.py:494
  86.7 7.0 %collective-permute-start.27 = (bf16[64,1024]{1,0:T(8,128)(2,1)S(1)}, bf16[64,1024]{1,0:T(8,128)(2,1)S(1)}, u32[]{:S(2)}, u32[]{:S(2)}) collective-permute-start(bf16[64,1024]{1,0:T(8,128)(2,1)S(1)} %get-tuple-element.86), channel_id=1, source_target_pairs={{0,12},{4,8},{8,4},{12,0},{1,13},{5,9},{9,5},{13,1},{2,14},{6,10},... | collective-permute-start | bytes 393224 | tf_op jit(solution)/shard_map/ppermute | solution.py:494
  88.4 12.7 %collective-permute-start.28 = (bf16[64,1024]{1,0:T(8,128)(2,1)S(1)}, bf16[64,1024]{1,0:T(8,128)(2,1)S(1)}, u32[]{:S(2)}, u32[]{:S(2)}) collective-permute-start(bf16[64,1024]{1,0:T(8,128)(2,1)S(1)} %get-tuple-element.87), channel_id=1, source_target_pairs={{0,8},{4,12},{8,0},{12,4},{1,9},{5,13},{9,1},{13,5},{2,10},{6,14},... | collective-permute-start | bytes 393224 | tf_op jit(solution)/shard_map/ppermute | solution.py:494
  89.0 12.1 %collective-permute-start.29 = (bf16[64,1024]{1,0:T(8,128)(2,1)S(1)}, bf16[64,1024]{1,0:T(8,128)(2,1)S(1)}, u32[]{:S(2)}, u32[]{:S(2)}) collective-permute-start(bf16[64,1024]{1,0:T(8,128)(2,1)S(1)} %get-tuple-element.88), channel_id=1, source_target_pairs={{0,4},{4,0},{8,12},{12,8},{1,5},{5,1},{9,13},{13,9},{2,6},{6,2},{1... | collective-permute-start | bytes 393224 | tf_op jit(solution)/shard_map/ppermute | solution.py:494
  102.1 7.4 %collective-permute-start.30 = (bf16[64,1024]{1,0:T(8,128)(2,1)S(1)}, bf16[64,1024]{1,0:T(8,128)(2,1)S(1)}, u32[]{:S(2)}, u32[]{:S(2)}) collective-permute-start(bf16[64,1024]{1,0:T(8,128)(2,1)S(1)} %get-tuple-element.90), channel_id=1, source_target_pairs={{0,12},{4,8},{8,4},{12,0},{1,13},{5,9},{9,5},{13,1},{2,14},{6,10},... | collective-permute-start | bytes 393224 | tf_op jit(solution)/shard_map/ppermute | solution.py:494
  104.0 10.5 %collective-permute-start.31 = (bf16[64,1024]{1,0:T(8,128)(2,1)S(1)}, bf16[64,1024]{1,0:T(8,128)(2,1)S(1)}, u32[]{:S(2)}, u32[]{:S(2)}) collective-permute-start(bf16[64,1024]{1,0:T(8,128)(2,1)S(1)} %get-tuple-element.91), channel_id=1, source_target_pairs={{0,8},{4,12},{8,0},{12,4},{1,9},{5,13},{9,1},{13,5},{2,10},{6,14},... | collective-permute-start | bytes 393224 | tf_op jit(solution)/shard_map/ppermute | solution.py:494
  104.0 10.5 %collective-permute-start.32 = (bf16[64,1024]{1,0:T(8,128)(2,1)S(1)}, bf16[64,1024]{1,0:T(8,128)(2,1)S(1)}, u32[]{:S(2)}, u32[]{:S(2)}) collective-permute-start(bf16[64,1024]{1,0:T(8,128)(2,1)S(1)} %get-tuple-element.92), channel_id=1, source_target_pairs={{0,4},{4,0},{8,12},{12,8},{1,5},{5,1},{9,13},{13,9},{2,6},{6,2},{1... | collective-permute-start | bytes 393224 | tf_op jit(solution)/shard_map/ppermute | solution.py:494
  119.3 5.2 %collective-permute-start.38 = (bf16[2,2,32,256]{3,2,1,0:T(8,128)(2,1)S(1)}, bf16[2,2,32,256]{3,2,1,0:T(8,128)(2,1)S(1)}, u32[]{:S(2)}, u32[]{:S(2)}) collective-permute-start(bf16[2,2,32,256]{3,2,1,0:T(8,128)(2,1)S(1)} %shard_map.94.rest_0_), channel_id=1, source_target_pairs={{0,8},{4,12},{8,0},{12,4},{1,9},{5,13},{9,1},{13,5},{2,10},{6,14},... | collective-permute-start | bytes 196616 | tf_op jit(solution)/shard_map/ppermute | solution.py:494
  120.2 6.4 %collective-permute-start.34 = (bf16[2,2,32,256]{3,2,1,0:T(8,128)(2,1)S(1)}, bf16[2,2,32,256]{3,2,1,0:T(8,128)(2,1)S(1)}, u32[]{:S(2)}, u32[]{:S(2)}) collective-permute-start(bf16[2,2,32,256]{3,2,1,0:T(8,128)(2,1)S(1)} %shard_map.93.rest_0_), channel_id=1, source_target_pairs={{0,8},{4,12},{8,0},{12,4},{1,9},{5,13},{9,1},{13,5},{2,10},{6,14},... | collective-permute-start | bytes 196616 | tf_op jit(solution)/shard_map/ppermute | solution.py:494
  122.4 4.7 %collective-permute-start.40 = (bf16[2,2,32,256]{3,2,1,0:T(8,128)(2,1)S(1)}, bf16[2,2,32,256]{3,2,1,0:T(8,128)(2,1)S(1)}, u32[]{:S(2)}, u32[]{:S(2)}) collective-permute-start(bf16[2,2,32,256]{3,2,1,0:T(8,128)(2,1)S(1)} %shard_map.94.rest_0_), channel_id=1, source_target_pairs={{0,4},{4,0},{8,12},{12,8},{1,5},{5,1},{9,13},{13,9},{2,6},{6,2},{1... | collective-permute-start | bytes 196616 | tf_op jit(solution)/shard_map/ppermute | solution.py:494
  124.5 6.2 %collective-permute-start.36 = (bf16[2,2,32,256]{3,2,1,0:T(8,128)(2,1)S(1)}, bf16[2,2,32,256]{3,2,1,0:T(8,128)(2,1)S(1)}, u32[]{:S(2)}, u32[]{:S(2)}) collective-permute-start(bf16[2,2,32,256]{3,2,1,0:T(8,128)(2,1)S(1)} %shard_map.93.rest_0_), channel_id=1, source_target_pairs={{0,4},{4,0},{8,12},{12,8},{1,5},{5,1},{9,13},{13,9},{2,6},{6,2},{1... | collective-permute-start | bytes 196616 | tf_op jit(solution)/shard_map/ppermute | solution.py:494
  (16 other events, 174.0 us)

commit v27 on v14

--- a/solution.py
+++ b/solution.py
@@ -444,7 +444,7 @@
     freq_devs = len(messages)
     half_rows, own, rcv = initial.shape
     per_dev = messages[0].shape[1]
-    tile = 2 * ROWS
+    tile = ROWS
     count = table.shape[2]
 
     def body(place_ref, _, sblk, x_ref, o_ref, t_ref, *rest):
@@ -459,19 +459,17 @@
             for row in range(ROWS):
                 spread_ref[row * own : (row + 1) * own] = jnp.where(lane == row, base, 0.0).astype(BF16)
 
-        here = pl.ds(pl.multiple_of(step * tile, tile), tile)
-        data = [ref[:, :, here, :].astype(F32) for ref in refs]
+        pair = pl.ds(pl.multiple_of(step // 2 * (2 * ROWS), 2 * ROWS), 2 * ROWS)
+        data = [ref[:, :, pair, :].astype(F32) for ref in refs]
+        data = [jnp.where(step % 2 == 0, v[:, :, :ROWS], v[:, :, ROWS:]) for v in data]
         onsets = o_ref[pl.ds(pl.multiple_of(sblk[0] * half_rows + first + step * tile, tile), tile), :]
         time = lax.broadcasted_iota(jnp.int32, (own, rcv), 0) + place_ref[0] * own
-        for half in range(2):
-            cut = slice(half * ROWS, (half + 1) * ROWS)
-            flat = jnp.stack([v[:, :, cut] for v in data]).reshape(count, rcv).astype(BF16)
-            change = jnp.dot(spread_ref[...], flat, preferred_element_type=F32)
-            for row in range(ROWS):
-                spot = half * ROWS + row
-                on = time < onsets[spot : spot + 1, :]
-                moved = jnp.where(on, change[row * own : (row + 1) * own], 0.0)
-                out[spot] = (x_ref[first + step * tile + spot].astype(F32) - moved).astype(BF16)
+        flat = jnp.stack(data).reshape(count, rcv).astype(BF16)
+        change = jnp.dot(spread_ref[...], flat, preferred_element_type=F32)
+        for row in range(ROWS):
+            on = time < onsets[row : row + 1, :]
+            moved = jnp.where(on, change[row * own : (row + 1) * own], 0.0)
+            out[row] = (x_ref[first + step * tile + row].astype(F32) - moved).astype(BF16)
 
     inputs = [(v, whole(v)) for v in (initial, onset, table, *messages)]
     aliases = {}

time: 130 us -> 131 us (level)
  transfers between devices with their start and end apart: 41 -> 41, of which waited for: 22 -> 21; matrix products, arithmetic and copies ran while one was open for 0% -> 0% of each run, Pallas kernels for 6% -> 6%
where the time goes in v27:
time: 131 us
  waiting for transfers between devices  56.1 us (43%)
  starting transfers between devices  54.5 us (42%)
  Pallas kernels  15.5 us (12%)
  local copies, waits for them, and re-layouts  4.56 us (3%)
    ppermute x41, waiting for transfers between devices, exchanged(): lax.ppermute(value, axis, [(i, i ^ step) for i in range(lax.axis_size(axi...  56.1 us
    ppermute x41, starting transfers between devices, exchanged(): lax.ppermute(value, axis, [(i, i ^ step) for i in range(lax.axis_size(axi...  54.5 us
    pallas_call x24, Pallas kernels, call(): pl.pallas_call(body, grid_spec=pltpu.PrefetchScalarGridSpec(num_scalar_pr...  15.5 us
    unnamed x15, local copies, waits for them, and re-layouts  4.56 us
  transfers between devices with their start and end apart: 41, of which 21 were waited for; matrix products, arithmetic and copies ran while one was open for 0% of the time, Pallas kernels for 6%

profile of v27, /device:TPU:0, one launch (start us, length us, event | category | flops | bytes accessed | tf_op | source)
XLA Modules:
  0.0 130.8 jit_solution(1649416960162223181)
XLA Ops:
  0.8 1.6 %copy-done.2 = bf16[2,2,1024,256]{3,2,1,0:T(8,128)(2,1)S(1)} copy-done((bf16[2,2,1024,256]{3,2,1,0:T(8,128)(2,1)S(1)}, bf16[2,2,1024,256]{3,2,1,0:T(8,128)(2,1)}, u32[]{:S(2)}) %copy-start.2) | copy-done | bytes 2097176
  2.6 3.0 %collective-permute-start.6 = (bf16[2,256,512]{2,1,0:T(8,128)(2,1)S(1)}, bf16[2,256,512]{2,1,0:T(8,128)(2,1)S(1)}, u32[]{:S(2)}, u32[]{:S(2)}) collective-permute-start(bf16[2,256,512]{2,1,0:T(8,128)(2,1)S(1)} %get-tuple-element.66), channel_id=1, source_target_pairs={{0,2},{2,0},{1,3},{3,1},{4,6},{6,4},{5,7},{7,5},{8,10},{10,8},{9,1... | collective-permute-start | bytes 1572872 | tf_op jit(solution)/shard_map/ppermute | solution.py:493
  5.7 2.2 %copy-done = bf16[64,128,256]{2,1,0:T(8,128)(2,1)S(1)} copy-done((bf16[64,128,256]{2,1,0:T(8,128)(2,1)S(1)}, bf16[64,128,256]{2,1,0:T(8,128)(2,1)}, u32[]{:S(2)}) %copy-start) | copy-done | bytes 4194328
  8.6 3.1 %collective-permute-start.3 = (bf16[2,2,64,256]{3,2,1,0:T(8,128)(2,1)S(1)}, bf16[2,2,64,256]{3,2,1,0:T(8,128)(2,1)S(1)}, u32[]{:S(2)}, u32[]{:S(2)}) collective-permute-start(bf16[2,2,64,256]{3,2,1,0:T(8,128)(2,1)S(1)} %get-tuple-element.59), channel_id=1, source_target_pairs={{0,8},{4,12},{8,0},{12,4},{1,9},{5,13},{9,1},{13,5},{2,10},{6,14},... | collective-permute-start | bytes 393224 | tf_op jit(solution)/shard_map/ppermute | solution.py:493
  13.3 8.2 %collective-permute-done.3.refs_1_ = bf16[2,2,64,256]{3,2,1,0:T(8,128)(2,1)S(1)} collective-permute-done((bf16[2,2,64,256]{3,2,1,0:T(8,128)(2,1)S(1)}, bf16[2,2,64,256]{3,2,1,0:T(8,128)(2,1)S(1)}, u32[]{:S(2)}, u32[]{:S(2)}) %collective-permute-start.3) | collective-permute-done | bytes 131104 | tf_op jit(solution)/shard_map/ppermute | solution.py:493
  21.8 1.6 %collective-permute-start.8 = (bf16[2,2,64,256]{3,2,1,0:T(8,128)(2,1)S(1)}, bf16[2,2,64,256]{3,2,1,0:T(8,128)(2,1)S(1)}, u32[]{:S(2)}, u32[]{:S(2)}) collective-permute-start(bf16[2,2,64,256]{3,2,1,0:T(8,128)(2,1)S(1)} %get-tuple-element.68.rest_0_), channel_id=1, source_target_pairs={{0,2},{2,0},{1,3},{3,1},{4,6},{6,4},{5,7},{7,5},{8,10},{10,8},{9,1... | collective-permute-start | bytes 393224 | tf_op jit(solution)/shard_map/ppermute | solution.py:493
  24.0 7.6 %collective-permute-done.8.rest_1_ = bf16[2,2,64,256]{3,2,1,0:T(8,128)(2,1)S(1)} collective-permute-done((bf16[2,2,64,256]{3,2,1,0:T(8,128)(2,1)S(1)}, bf16[2,2,64,256]{3,2,1,0:T(8,128)(2,1)S(1)}, u32[]{:S(2)}, u32[]{:S(2)}) %collective-permute-start.8) | collective-permute-done | bytes 131104 | tf_op jit(solution)/shard_map/ppermute | solution.py:493
  34.0 2.9 %collective-permute-start.11 = (bf16[64,1024]{1,0:T(8,128)(2,1)S(1)}, bf16[64,1024]{1,0:T(8,128)(2,1)S(1)}, u32[]{:S(2)}, u32[]{:S(2)}) collective-permute-start(bf16[64,1024]{1,0:T(8,128)(2,1)S(1)} %get-tuple-element.74), channel_id=1, source_target_pairs={{0,8},{4,12},{8,0},{12,4},{1,9},{5,13},{9,1},{13,5},{2,10},{6,14},... | collective-permute-start | bytes 393224 | tf_op jit(solution)/shard_map/ppermute | solution.py:493
  41.1 5.8 %collective-permute-done.11.rest_1_ = bf16[64,1024]{1,0:T(8,128)(2,1)S(1)} collective-permute-done((bf16[64,1024]{1,0:T(8,128)(2,1)S(1)}, bf16[64,1024]{1,0:T(8,128)(2,1)S(1)}, u32[]{:S(2)}, u32[]{:S(2)}) %collective-permute-start.11) | collective-permute-done | bytes 131104 | tf_op jit(solution)/shard_map/ppermute | solution.py:493
  48.7 4.2 %collective-permute-start.14 = (bf16[64,1024]{1,0:T(8,128)(2,1)S(1)}, bf16[64,1024]{1,0:T(8,128)(2,1)S(1)}, u32[]{:S(2)}, u32[]{:S(2)}) collective-permute-start(bf16[64,1024]{1,0:T(8,128)(2,1)S(1)} %get-tuple-element.78), channel_id=1, source_target_pairs={{0,8},{4,12},{8,0},{12,4},{1,9},{5,13},{9,1},{13,5},{2,10},{6,14},... | collective-permute-start | bytes 393224 | tf_op jit(solution)/shard_map/ppermute | solution.py:493
  53.5 9.0 %collective-permute-done.14.rest_5_ = bf16[64,1024]{1,0:T(8,128)(2,1)S(1)} collective-permute-done((bf16[64,1024]{1,0:T(8,128)(2,1)S(1)}, bf16[64,1024]{1,0:T(8,128)(2,1)S(1)}, u32[]{:S(2)}, u32[]{:S(2)}) %collective-permute-start.14) | collective-permute-done | bytes 131104 | tf_op jit(solution)/shard_map/ppermute | solution.py:493
  64.1 1.6 %collective-permute-start.17 = (bf16[2,2,32,256]{3,2,1,0:T(8,128)(2,1)S(1)}, bf16[2,2,32,256]{3,2,1,0:T(8,128)(2,1)S(1)}, u32[]{:S(2)}, u32[]{:S(2)}) collective-permute-start(bf16[2,2,32,256]{3,2,1,0:T(8,128)(2,1)S(1)} %get-tuple-element.82), channel_id=1, source_target_pairs={{0,2},{2,0},{1,3},{3,1},{4,6},{6,4},{5,7},{7,5},{8,10},{10,8},{9,1... | collective-permute-start | bytes 196616 | tf_op jit(solution)/shard_map/ppermute | solution.py:493
  66.7 1.8 %collective-permute-done.17.r_ref = bf16[2,2,32,256]{3,2,1,0:T(8,128)(2,1)S(1)} collective-permute-done((bf16[2,2,32,256]{3,2,1,0:T(8,128)(2,1)S(1)}, bf16[2,2,32,256]{3,2,1,0:T(8,128)(2,1)S(1)}, u32[]{:S(2)}, u32[]{:S(2)}) %collective-permute-start.17) | collective-permute-done | bytes 65568 | tf_op jit(solution)/shard_map/ppermute | solution.py:493
  68.4 1.9 %collective-permute-start.18 = (bf16[2,2,32,256]{3,2,1,0:T(8,128)(2,1)S(1)}, bf16[2,2,32,256]{3,2,1,0:T(8,128)(2,1)S(1)}, u32[]{:S(2)}, u32[]{:S(2)}) collective-permute-start(bf16[2,2,32,256]{3,2,1,0:T(8,128)(2,1)S(1)} %shard_map.84.rest_0_), channel_id=1, source_target_pairs={{0,8},{4,12},{8,0},{12,4},{1,9},{5,13},{9,1},{13,5},{2,10},{6,14},... | collective-permute-start | bytes 196616 | tf_op jit(solution)/shard_map/ppermute | solution.py:493
  71.9 2.3 %collective-permute-start.20 = (bf16[2,2,32,256]{3,2,1,0:T(8,128)(2,1)S(1)}, bf16[2,2,32,256]{3,2,1,0:T(8,128)(2,1)S(1)}, u32[]{:S(2)}, u32[]{:S(2)}) collective-permute-start(bf16[2,2,32,256]{3,2,1,0:T(8,128)(2,1)S(1)} %shard_map.84.rest_0_), channel_id=1, source_target_pairs={{0,4},{4,0},{8,12},{12,8},{1,5},{5,1},{9,13},{13,9},{2,6},{6,2},{1... | collective-permute-start | bytes 196616 | tf_op jit(solution)/shard_map/ppermute | solution.py:493
  74.1 2.8 %collective-permute-start.19 = (bf16[2,2,32,256]{3,2,1,0:T(8,128)(2,1)S(1)}, bf16[2,2,32,256]{3,2,1,0:T(8,128)(2,1)S(1)}, u32[]{:S(2)}, u32[]{:S(2)}) collective-permute-start(bf16[2,2,32,256]{3,2,1,0:T(8,128)(2,1)S(1)} %collective-permute-done.18.rest_1_), channel_id=1, source_target_pairs={{0,4},{4,0},{8,12},{12,8},{1,5},{5,1},{9,13},{13,9},{2,6},{6,2},{1... | collective-permute-start | bytes 196616 | tf_op jit(solution)/shard_map/ppermute | solution.py:493
  77.0 2.0 %collective-permute-start.23 = (bf16[2,2,32,256]{3,2,1,0:T(8,128)(2,1)S(1)}, bf16[2,2,32,256]{3,2,1,0:T(8,128)(2,1)S(1)}, u32[]{:S(2)}, u32[]{:S(2)}) collective-permute-start(bf16[2,2,32,256]{3,2,1,0:T(8,128)(2,1)S(1)} %collective-permute-done.22.rest_1_), channel_id=1, source_target_pairs={{0,4},{4,0},{8,12},{12,8},{1,5},{5,1},{9,13},{13,9},{2,6},{6,2},{1... | collective-permute-start | bytes 196616 | tf_op jit(solution)/shard_map/ppermute | solution.py:493
  84.1 2.4 %collective-permute-done.26.rest_2_ = bf16[2,2,32,256]{3,2,1,0:T(8,128)(2,1)S(1)} collective-permute-done((bf16[2,2,32,256]{3,2,1,0:T(8,128)(2,1)S(1)}, bf16[2,2,32,256]{3,2,1,0:T(8,128)(2,1)S(1)}, u32[]{:S(2)}, u32[]{:S(2)}) %collective-permute-start.26) | collective-permute-done | bytes 65568 | tf_op jit(solution)/shard_map/ppermute | solution.py:493
  88.2 3.0 %collective-permute-start.28 = (bf16[64,1024]{1,0:T(8,128)(2,1)S(1)}, bf16[64,1024]{1,0:T(8,128)(2,1)S(1)}, u32[]{:S(2)}, u32[]{:S(2)}) collective-permute-start(bf16[64,1024]{1,0:T(8,128)(2,1)S(1)} %get-tuple-element.87), channel_id=1, source_target_pairs={{0,12},{4,8},{8,4},{12,0},{1,13},{5,9},{9,5},{13,1},{2,14},{6,10},... | collective-permute-start | bytes 393224 | tf_op jit(solution)/shard_map/ppermute | solution.py:493
  91.2 5.1 %collective-permute-done.27.rest_1_ = bf16[64,1024]{1,0:T(8,128)(2,1)S(1)} collective-permute-done((bf16[64,1024]{1,0:T(8,128)(2,1)S(1)}, bf16[64,1024]{1,0:T(8,128)(2,1)S(1)}, u32[]{:S(2)}, u32[]{:S(2)}) %collective-permute-start.27) | collective-permute-done | bytes 131104 | tf_op jit(solution)/shard_map/ppermute | solution.py:493
  98.8 1.7 %collective-permute-start.30 = (bf16[64,1024]{1,0:T(8,128)(2,1)S(1)}, bf16[64,1024]{1,0:T(8,128)(2,1)S(1)}, u32[]{:S(2)}, u32[]{:S(2)}) collective-permute-start(bf16[64,1024]{1,0:T(8,128)(2,1)S(1)} %get-tuple-element.90), channel_id=1, source_target_pairs={{0,8},{4,12},{8,0},{12,4},{1,9},{5,13},{9,1},{13,5},{2,10},{6,14},... | collective-permute-start | bytes 393224 | tf_op jit(solution)/shard_map/ppermute | solution.py:493
  100.4 3.4 %collective-permute-start.31 = (bf16[64,1024]{1,0:T(8,128)(2,1)S(1)}, bf16[64,1024]{1,0:T(8,128)(2,1)S(1)}, u32[]{:S(2)}, u32[]{:S(2)}) collective-permute-start(bf16[64,1024]{1,0:T(8,128)(2,1)S(1)} %get-tuple-element.91), channel_id=1, source_target_pairs={{0,12},{4,8},{8,4},{12,0},{1,13},{5,9},{9,5},{13,1},{2,14},{6,10},... | collective-permute-start | bytes 393224 | tf_op jit(solution)/shard_map/ppermute | solution.py:493
  104.7 3.7 %collective-permute-done.31.rest_6_ = bf16[64,1024]{1,0:T(8,128)(2,1)S(1)} collective-permute-done((bf16[64,1024]{1,0:T(8,128)(2,1)S(1)}, bf16[64,1024]{1,0:T(8,128)(2,1)S(1)}, u32[]{:S(2)}, u32[]{:S(2)}) %collective-permute-start.31) | collective-permute-done | bytes 131104 | tf_op jit(solution)/shard_map/ppermute | solution.py:493
  108.4 2.0 %collective-permute-done.32.rest_7_ = bf16[64,1024]{1,0:T(8,128)(2,1)S(1)} collective-permute-done((bf16[64,1024]{1,0:T(8,128)(2,1)S(1)}, bf16[64,1024]{1,0:T(8,128)(2,1)S(1)}, u32[]{:S(2)}, u32[]{:S(2)}) %collective-permute-start.32) | collective-permute-done | bytes 131104 | tf_op jit(solution)/shard_map/ppermute | solution.py:493
  110.9 1.8 %collective-permute-start.37 = (bf16[2,2,32,256]{3,2,1,0:T(8,128)(2,1)S(1)}, bf16[2,2,32,256]{3,2,1,0:T(8,128)(2,1)S(1)}, u32[]{:S(2)}, u32[]{:S(2)}) collective-permute-start(bf16[2,2,32,256]{3,2,1,0:T(8,128)(2,1)S(1)} %get-tuple-element.96), channel_id=1, source_target_pairs={{0,2},{2,0},{1,3},{3,1},{4,6},{6,4},{5,7},{7,5},{8,10},{10,8},{9,1... | collective-permute-start | bytes 196616 | tf_op jit(solution)/shard_map/ppermute | solution.py:493
  113.4 1.8 %collective-permute-done.37.r_ref = bf16[2,2,32,256]{3,2,1,0:T(8,128)(2,1)S(1)} collective-permute-done((bf16[2,2,32,256]{3,2,1,0:T(8,128)(2,1)S(1)}, bf16[2,2,32,256]{3,2,1,0:T(8,128)(2,1)S(1)}, u32[]{:S(2)}, u32[]{:S(2)}) %collective-permute-start.37) | collective-permute-done | bytes 65568 | tf_op jit(solution)/shard_map/ppermute | solution.py:493
  115.2 2.5 %collective-permute-start.38 = (bf16[2,2,32,256]{3,2,1,0:T(8,128)(2,1)S(1)}, bf16[2,2,32,256]{3,2,1,0:T(8,128)(2,1)S(1)}, u32[]{:S(2)}, u32[]{:S(2)}) collective-permute-start(bf16[2,2,32,256]{3,2,1,0:T(8,128)(2,1)S(1)} %shard_map.94.rest_0_), channel_id=1, source_target_pairs={{0,8},{4,12},{8,0},{12,4},{1,9},{5,13},{9,1},{13,5},{2,10},{6,14},... | collective-permute-start | bytes 196616 | tf_op jit(solution)/shard_map/ppermute | solution.py:493
  117.7 2.0 %collective-permute-start.34 = (bf16[2,2,32,256]{3,2,1,0:T(8,128)(2,1)S(1)}, bf16[2,2,32,256]{3,2,1,0:T(8,128)(2,1)S(1)}, u32[]{:S(2)}, u32[]{:S(2)}) collective-permute-start(bf16[2,2,32,256]{3,2,1,0:T(8,128)(2,1)S(1)} %shard_map.93.rest_0_), channel_id=1, source_target_pairs={{0,8},{4,12},{8,0},{12,4},{1,9},{5,13},{9,1},{13,5},{2,10},{6,14},... | collective-permute-start | bytes 196616 | tf_op jit(solution)/shard_map/ppermute | solution.py:493
  119.7 1.7 %collective-permute-start.40 = (bf16[2,2,32,256]{3,2,1,0:T(8,128)(2,1)S(1)}, bf16[2,2,32,256]{3,2,1,0:T(8,128)(2,1)S(1)}, u32[]{:S(2)}, u32[]{:S(2)}) collective-permute-start(bf16[2,2,32,256]{3,2,1,0:T(8,128)(2,1)S(1)} %shard_map.94.rest_0_), channel_id=1, source_target_pairs={{0,4},{4,0},{8,12},{12,8},{1,5},{5,1},{9,13},{13,9},{2,6},{6,2},{1... | collective-permute-start | bytes 196616 | tf_op jit(solution)/shard_map/ppermute | solution.py:493
  121.8 1.7 %collective-permute-start.36 = (bf16[2,2,32,256]{3,2,1,0:T(8,128)(2,1)S(1)}, bf16[2,2,32,256]{3,2,1,0:T(8,128)(2,1)S(1)}, u32[]{:S(2)}, u32[]{:S(2)}) collective-permute-start(bf16[2,2,32,256]{3,2,1,0:T(8,128)(2,1)S(1)} %shard_map.93.rest_0_), channel_id=1, source_target_pairs={{0,4},{4,0},{8,12},{12,8},{1,5},{5,1},{9,13},{13,9},{2,6},{6,2},{1... | collective-permute-start | bytes 196616 | tf_op jit(solution)/shard_map/ppermute | solution.py:493
  125.7 2.5 %shard_map.95.rest_4_ = bf16[64,128,256]{2,1,0:T(8,128)(2,1)} custom-call(s32[1]{0:T(128)} %bitcast._.freq.place_ref, s32[1]{0:T(128)} %bitcast.1.rblk._, s32[1]{0:T(128)} %bitcast.2.__.sblk, bf16[64,128,256]{2,1,0:T(8,128)(2,1)S(1)} %copy-done.1, s32[128,256]{1,0:T(8,128)S(1)} %copy-done.4, bf16[4,128,128]{2,1,0:T(8,128)(2,1)S(1)} %copy-done.5, ...), custom_call_target="tpu_custom_call" | custom-call | flops 33554432 | bytes 8912896 | tf_op jit(solution)/shard_map/pallas_call | solution.py:78
  128.2 2.6 %shard_map.96 = bf16[64,128,256]{2,1,0:T(8,128)(2,1)} custom-call(s32[1]{0:T(128)} %bitcast._.freq.place_ref, s32[1]{0:T(128)} %bitcast.1.rblk._, s32[1]{0:T(128)} %bitcast.2.__.sblk, bf16[64,128,256]{2,1,0:T(8,128)(2,1)S(1)} %copy-done.1, s32[128,256]{1,0:T(8,128)S(1)} %copy-done.4, ...), custom_call_target="tpu_custom_call", output_to_operand_aliasing={{}: (10, {})} | custom-call | flops 33554432 | bytes 13107200 | tf_op jit(solution)/shard_map/pallas_call | solution.py:78
  (89 shorter events, 31.3 us)
Async XLA Ops:
  2.6 21.3 %collective-permute-start.6 = (bf16[2,256,512]{2,1,0:T(8,128)(2,1)S(1)}, bf16[2,256,512]{2,1,0:T(8,128)(2,1)S(1)}, u32[]{:S(2)}, u32[]{:S(2)}) collective-permute-start(bf16[2,256,512]{2,1,0:T(8,128)(2,1)S(1)} %get-tuple-element.66), channel_id=1, source_target_pairs={{0,2},{2,0},{1,3},{3,1},{4,6},{6,4},{5,7},{7,5},{8,10},{10,8},{9,1... | collective-permute-start | bytes 1572872 | tf_op jit(solution)/shard_map/ppermute | solution.py:493
  5.6 26.0 %collective-permute-start.7 = (bf16[2,256,512]{2,1,0:T(8,128)(2,1)S(1)}, bf16[2,256,512]{2,1,0:T(8,128)(2,1)S(1)}, u32[]{:S(2)}, u32[]{:S(2)}) collective-permute-start(bf16[2,256,512]{2,1,0:T(8,128)(2,1)S(1)} %get-tuple-element.69), channel_id=1, source_target_pairs={{0,2},{2,0},{1,3},{3,1},{4,6},{6,4},{5,7},{7,5},{8,10},{10,8},{9,1... | collective-permute-start | bytes 1572872 | tf_op jit(solution)/shard_map/ppermute | solution.py:493
  8.6 12.9 %collective-permute-start.3 = (bf16[2,2,64,256]{3,2,1,0:T(8,128)(2,1)S(1)}, bf16[2,2,64,256]{3,2,1,0:T(8,128)(2,1)S(1)}, u32[]{:S(2)}, u32[]{:S(2)}) collective-permute-start(bf16[2,2,64,256]{3,2,1,0:T(8,128)(2,1)S(1)} %get-tuple-element.59), channel_id=1, source_target_pairs={{0,8},{4,12},{8,0},{12,4},{1,9},{5,13},{9,1},{13,5},{2,10},{6,14},... | collective-permute-start | bytes 393224 | tf_op jit(solution)/shard_map/ppermute | solution.py:493
  11.7 9.8 %collective-permute-start.4 = (bf16[2,2,64,256]{3,2,1,0:T(8,128)(2,1)S(1)}, bf16[2,2,64,256]{3,2,1,0:T(8,128)(2,1)S(1)}, u32[]{:S(2)}, u32[]{:S(2)}) collective-permute-start(bf16[2,2,64,256]{3,2,1,0:T(8,128)(2,1)S(1)} %get-tuple-element.60), channel_id=1, source_target_pairs={{0,12},{4,8},{8,4},{12,0},{1,13},{5,9},{9,5},{13,1},{2,14},{6,10},... | collective-permute-start | bytes 393224 | tf_op jit(solution)/shard_map/ppermute | solution.py:493
  13.1 8.6 %collective-permute-start.5 = (bf16[2,2,64,256]{3,2,1,0:T(8,128)(2,1)S(1)}, bf16[2,2,64,256]{3,2,1,0:T(8,128)(2,1)S(1)}, u32[]{:S(2)}, u32[]{:S(2)}) collective-permute-start(bf16[2,2,64,256]{3,2,1,0:T(8,128)(2,1)S(1)} %get-tuple-element.61), channel_id=1, source_target_pairs={{0,4},{4,0},{8,12},{12,8},{1,5},{5,1},{9,13},{13,9},{2,6},{6,2},{1... | collective-permute-start | bytes 393224 | tf_op jit(solution)/shard_map/ppermute | solution.py:493
  21.8 9.8 %collective-permute-start.8 = (bf16[2,2,64,256]{3,2,1,0:T(8,128)(2,1)S(1)}, bf16[2,2,64,256]{3,2,1,0:T(8,128)(2,1)S(1)}, u32[]{:S(2)}, u32[]{:S(2)}) collective-permute-start(bf16[2,2,64,256]{3,2,1,0:T(8,128)(2,1)S(1)} %get-tuple-element.68.rest_0_), channel_id=1, source_target_pairs={{0,2},{2,0},{1,3},{3,1},{4,6},{6,4},{5,7},{7,5},{8,10},{10,8},{9,1... | collective-permute-start | bytes 393224 | tf_op jit(solution)/shard_map/ppermute | solution.py:493
  23.4 8.2 %collective-permute-start = (bf16[2,256,512]{2,1,0:T(8,128)(2,1)S(1)}, bf16[2,256,512]{2,1,0:T(8,128)(2,1)S(1)}, u32[]{:S(2)}, u32[]{:S(2)}) collective-permute-start(bf16[2,256,512]{2,1,0:T(8,128)(2,1)S(1)} %get-tuple-element.51.rest_1_.rest_0_.rest_2_), channel_id=1, source_target_pairs={{0,1},{1,0},{2,3},{3,2},{4,5},{5,4},{6,7},{7,6},{8,9},{9,8},{10,11... | collective-permute-start | bytes 1572872 | tf_op jit(solution)/shard_map/ppermute | solution.py:493
  23.4 8.2 %collective-permute-start.1 = (bf16[2,256,512]{2,1,0:T(8,128)(2,1)S(1)}, bf16[2,256,512]{2,1,0:T(8,128)(2,1)S(1)}, u32[]{:S(2)}, u32[]{:S(2)}) collective-permute-start(bf16[2,256,512]{2,1,0:T(8,128)(2,1)S(1)} %get-tuple-element.52.rest_3_.rest_2_.rest_4_), channel_id=1, source_target_pairs={{0,1},{1,0},{2,3},{3,2},{4,5},{5,4},{6,7},{7,6},{8,9},{9,8},{10,11... | collective-permute-start | bytes 1572872 | tf_op jit(solution)/shard_map/ppermute | solution.py:493
  23.9 8.5 %collective-permute-start.9 = (bf16[2,256,512]{2,1,0:T(8,128)(2,1)S(1)}, bf16[2,256,512]{2,1,0:T(8,128)(2,1)S(1)}, u32[]{:S(2)}, u32[]{:S(2)}) collective-permute-start(bf16[2,256,512]{2,1,0:T(8,128)(2,1)S(1)} %collective-permute-done.6.rest_2_.rest_0_.rest_3_), channel_id=1, source_target_pairs={{0,1},{1,0},{2,3},{3,2},{4,5},{5,4},{6,7},{7,6},{8,9},{9,8},{10,11... | collective-permute-start | bytes 1572872 | tf_op jit(solution)/shard_map/ppermute | solution.py:493
  34.0 12.9 %collective-permute-start.11 = (bf16[64,1024]{1,0:T(8,128)(2,1)S(1)}, bf16[64,1024]{1,0:T(8,128)(2,1)S(1)}, u32[]{:S(2)}, u32[]{:S(2)}) collective-permute-start(bf16[64,1024]{1,0:T(8,128)(2,1)S(1)} %get-tuple-element.74), channel_id=1, source_target_pairs={{0,8},{4,12},{8,0},{12,4},{1,9},{5,13},{9,1},{13,5},{2,10},{6,14},... | collective-permute-start | bytes 393224 | tf_op jit(solution)/shard_map/ppermute | solution.py:493
  36.9 10.0 %collective-permute-start.12 = (bf16[64,1024]{1,0:T(8,128)(2,1)S(1)}, bf16[64,1024]{1,0:T(8,128)(2,1)S(1)}, u32[]{:S(2)}, u32[]{:S(2)}) collective-permute-start(bf16[64,1024]{1,0:T(8,128)(2,1)S(1)} %get-tuple-element.75), channel_id=1, source_target_pairs={{0,12},{4,8},{8,4},{12,0},{1,13},{5,9},{9,5},{13,1},{2,14},{6,10},... | collective-permute-start | bytes 393224 | tf_op jit(solution)/shard_map/ppermute | solution.py:493
  38.2 9.5 %collective-permute-start.13 = (bf16[64,1024]{1,0:T(8,128)(2,1)S(1)}, bf16[64,1024]{1,0:T(8,128)(2,1)S(1)}, u32[]{:S(2)}, u32[]{:S(2)}) collective-permute-start(bf16[64,1024]{1,0:T(8,128)(2,1)S(1)} %get-tuple-element.76), channel_id=1, source_target_pairs={{0,4},{4,0},{8,12},{12,8},{1,5},{5,1},{9,13},{13,9},{2,6},{6,2},{1... | collective-permute-start | bytes 393224 | tf_op jit(solution)/shard_map/ppermute | solution.py:493
  48.7 13.8 %collective-permute-start.14 = (bf16[64,1024]{1,0:T(8,128)(2,1)S(1)}, bf16[64,1024]{1,0:T(8,128)(2,1)S(1)}, u32[]{:S(2)}, u32[]{:S(2)}) collective-permute-start(bf16[64,1024]{1,0:T(8,128)(2,1)S(1)} %get-tuple-element.78), channel_id=1, source_target_pairs={{0,8},{4,12},{8,0},{12,4},{1,9},{5,13},{9,1},{13,5},{2,10},{6,14},... | collective-permute-start | bytes 393224 | tf_op jit(solution)/shard_map/ppermute | solution.py:493
  52.9 9.6 %collective-permute-start.15 = (bf16[64,1024]{1,0:T(8,128)(2,1)S(1)}, bf16[64,1024]{1,0:T(8,128)(2,1)S(1)}, u32[]{:S(2)}, u32[]{:S(2)}) collective-permute-start(bf16[64,1024]{1,0:T(8,128)(2,1)S(1)} %get-tuple-element.79), channel_id=1, source_target_pairs={{0,12},{4,8},{8,4},{12,0},{1,13},{5,9},{9,5},{13,1},{2,14},{6,10},... | collective-permute-start | bytes 393224 | tf_op jit(solution)/shard_map/ppermute | solution.py:493
  53.3 10.3 %collective-permute-start.16 = (bf16[64,1024]{1,0:T(8,128)(2,1)S(1)}, bf16[64,1024]{1,0:T(8,128)(2,1)S(1)}, u32[]{:S(2)}, u32[]{:S(2)}) collective-permute-start(bf16[64,1024]{1,0:T(8,128)(2,1)S(1)} %get-tuple-element.80), channel_id=1, source_target_pairs={{0,4},{4,0},{8,12},{12,8},{1,5},{5,1},{9,13},{13,9},{2,6},{6,2},{1... | collective-permute-start | bytes 393224 | tf_op jit(solution)/shard_map/ppermute | solution.py:493
  68.4 5.7 %collective-permute-start.18 = (bf16[2,2,32,256]{3,2,1,0:T(8,128)(2,1)S(1)}, bf16[2,2,32,256]{3,2,1,0:T(8,128)(2,1)S(1)}, u32[]{:S(2)}, u32[]{:S(2)}) collective-permute-start(bf16[2,2,32,256]{3,2,1,0:T(8,128)(2,1)S(1)} %shard_map.84.rest_0_), channel_id=1, source_target_pairs={{0,8},{4,12},{8,0},{12,4},{1,9},{5,13},{9,1},{13,5},{2,10},{6,14},... | collective-permute-start | bytes 196616 | tf_op jit(solution)/shard_map/ppermute | solution.py:493
  70.4 6.6 %collective-permute-start.22 = (bf16[2,2,32,256]{3,2,1,0:T(8,128)(2,1)S(1)}, bf16[2,2,32,256]{3,2,1,0:T(8,128)(2,1)S(1)}, u32[]{:S(2)}, u32[]{:S(2)}) collective-permute-start(bf16[2,2,32,256]{3,2,1,0:T(8,128)(2,1)S(1)} %shard_map.86.rest_0_), channel_id=1, source_target_pairs={{0,8},{4,12},{8,0},{12,4},{1,9},{5,13},{9,1},{13,5},{2,10},{6,14},... | collective-permute-start | bytes 196616 | tf_op jit(solution)/shard_map/ppermute | solution.py:493
  71.9 7.1 %collective-permute-start.20 = (bf16[2,2,32,256]{3,2,1,0:T(8,128)(2,1)S(1)}, bf16[2,2,32,256]{3,2,1,0:T(8,128)(2,1)S(1)}, u32[]{:S(2)}, u32[]{:S(2)}) collective-permute-start(bf16[2,2,32,256]{3,2,1,0:T(8,128)(2,1)S(1)} %shard_map.84.rest_0_), channel_id=1, source_target_pairs={{0,4},{4,0},{8,12},{12,8},{1,5},{5,1},{9,13},{13,9},{2,6},{6,2},{1... | collective-permute-start | bytes 196616 | tf_op jit(solution)/shard_map/ppermute | solution.py:493
  74.1 5.1 %collective-permute-start.19 = (bf16[2,2,32,256]{3,2,1,0:T(8,128)(2,1)S(1)}, bf16[2,2,32,256]{3,2,1,0:T(8,128)(2,1)S(1)}, u32[]{:S(2)}, u32[]{:S(2)}) collective-permute-start(bf16[2,2,32,256]{3,2,1,0:T(8,128)(2,1)S(1)} %collective-permute-done.18.rest_1_), channel_id=1, source_target_pairs={{0,4},{4,0},{8,12},{12,8},{1,5},{5,1},{9,13},{13,9},{2,6},{6,2},{1... | collective-permute-start | bytes 196616 | tf_op jit(solution)/shard_map/ppermute | solution.py:493
  77.0 4.9 %collective-permute-start.23 = (bf16[2,2,32,256]{3,2,1,0:T(8,128)(2,1)S(1)}, bf16[2,2,32,256]{3,2,1,0:T(8,128)(2,1)S(1)}, u32[]{:S(2)}, u32[]{:S(2)}) collective-permute-start(bf16[2,2,32,256]{3,2,1,0:T(8,128)(2,1)S(1)} %collective-permute-done.22.rest_1_), channel_id=1, source_target_pairs={{0,4},{4,0},{8,12},{12,8},{1,5},{5,1},{9,13},{13,9},{2,6},{6,2},{1... | collective-permute-start | bytes 196616 | tf_op jit(solution)/shard_map/ppermute | solution.py:493
  87.4 8.8 %collective-permute-start.27 = (bf16[64,1024]{1,0:T(8,128)(2,1)S(1)}, bf16[64,1024]{1,0:T(8,128)(2,1)S(1)}, u32[]{:S(2)}, u32[]{:S(2)}) collective-permute-start(bf16[64,1024]{1,0:T(8,128)(2,1)S(1)} %get-tuple-element.86), channel_id=1, source_target_pairs={{0,8},{4,12},{8,0},{12,4},{1,9},{5,13},{9,1},{13,5},{2,10},{6,14},... | collective-permute-start | bytes 393224 | tf_op jit(solution)/shard_map/ppermute | solution.py:493
  88.2 8.1 %collective-permute-start.28 = (bf16[64,1024]{1,0:T(8,128)(2,1)S(1)}, bf16[64,1024]{1,0:T(8,128)(2,1)S(1)}, u32[]{:S(2)}, u32[]{:S(2)}) collective-permute-start(bf16[64,1024]{1,0:T(8,128)(2,1)S(1)} %get-tuple-element.87), channel_id=1, source_target_pairs={{0,12},{4,8},{8,4},{12,0},{1,13},{5,9},{9,5},{13,1},{2,14},{6,10},... | collective-permute-start | bytes 393224 | tf_op jit(solution)/shard_map/ppermute | solution.py:493
  91.2 6.6 %collective-permute-start.29 = (bf16[64,1024]{1,0:T(8,128)(2,1)S(1)}, bf16[64,1024]{1,0:T(8,128)(2,1)S(1)}, u32[]{:S(2)}, u32[]{:S(2)}) collective-permute-start(bf16[64,1024]{1,0:T(8,128)(2,1)S(1)} %get-tuple-element.88), channel_id=1, source_target_pairs={{0,4},{4,0},{8,12},{12,8},{1,5},{5,1},{9,13},{13,9},{2,6},{6,2},{1... | collective-permute-start | bytes 393224 | tf_op jit(solution)/shard_map/ppermute | solution.py:493
  98.8 5.9 %collective-permute-start.30 = (bf16[64,1024]{1,0:T(8,128)(2,1)S(1)}, bf16[64,1024]{1,0:T(8,128)(2,1)S(1)}, u32[]{:S(2)}, u32[]{:S(2)}) collective-permute-start(bf16[64,1024]{1,0:T(8,128)(2,1)S(1)} %get-tuple-element.90), channel_id=1, source_target_pairs={{0,8},{4,12},{8,0},{12,4},{1,9},{5,13},{9,1},{13,5},{2,10},{6,14},... | collective-permute-start | bytes 393224 | tf_op jit(solution)/shard_map/ppermute | solution.py:493
  100.4 7.9 %collective-permute-start.31 = (bf16[64,1024]{1,0:T(8,128)(2,1)S(1)}, bf16[64,1024]{1,0:T(8,128)(2,1)S(1)}, u32[]{:S(2)}, u32[]{:S(2)}) collective-permute-start(bf16[64,1024]{1,0:T(8,128)(2,1)S(1)} %get-tuple-element.91), channel_id=1, source_target_pairs={{0,12},{4,8},{8,4},{12,0},{1,13},{5,9},{9,5},{13,1},{2,14},{6,10},... | collective-permute-start | bytes 393224 | tf_op jit(solution)/shard_map/ppermute | solution.py:493
  103.8 6.6 %collective-permute-start.32 = (bf16[64,1024]{1,0:T(8,128)(2,1)S(1)}, bf16[64,1024]{1,0:T(8,128)(2,1)S(1)}, u32[]{:S(2)}, u32[]{:S(2)}) collective-permute-start(bf16[64,1024]{1,0:T(8,128)(2,1)S(1)} %get-tuple-element.92), channel_id=1, source_target_pairs={{0,4},{4,0},{8,12},{12,8},{1,5},{5,1},{9,13},{13,9},{2,6},{6,2},{1... | collective-permute-start | bytes 393224 | tf_op jit(solution)/shard_map/ppermute | solution.py:493
  112.7 5.0 %collective-permute-start.33 = (bf16[2,2,32,256]{3,2,1,0:T(8,128)(2,1)S(1)}, bf16[2,2,32,256]{3,2,1,0:T(8,128)(2,1)S(1)}, u32[]{:S(2)}, u32[]{:S(2)}) collective-permute-start(bf16[2,2,32,256]{3,2,1,0:T(8,128)(2,1)S(1)} %get-tuple-element.94), channel_id=1, source_target_pairs={{0,2},{2,0},{1,3},{3,1},{4,6},{6,4},{5,7},{7,5},{8,10},{10,8},{9,1... | collective-permute-start | bytes 196616 | tf_op jit(solution)/shard_map/ppermute | solution.py:493
  115.2 6.2 %collective-permute-start.38 = (bf16[2,2,32,256]{3,2,1,0:T(8,128)(2,1)S(1)}, bf16[2,2,32,256]{3,2,1,0:T(8,128)(2,1)S(1)}, u32[]{:S(2)}, u32[]{:S(2)}) collective-permute-start(bf16[2,2,32,256]{3,2,1,0:T(8,128)(2,1)S(1)} %shard_map.94.rest_0_), channel_id=1, source_target_pairs={{0,8},{4,12},{8,0},{12,4},{1,9},{5,13},{9,1},{13,5},{2,10},{6,14},... | collective-permute-start | bytes 196616 | tf_op jit(solution)/shard_map/ppermute | solution.py:493
  117.7 5.7 %collective-permute-start.34 = (bf16[2,2,32,256]{3,2,1,0:T(8,128)(2,1)S(1)}, bf16[2,2,32,256]{3,2,1,0:T(8,128)(2,1)S(1)}, u32[]{:S(2)}, u32[]{:S(2)}) collective-permute-start(bf16[2,2,32,256]{3,2,1,0:T(8,128)(2,1)S(1)} %shard_map.93.rest_0_), channel_id=1, source_target_pairs={{0,8},{4,12},{8,0},{12,4},{1,9},{5,13},{9,1},{13,5},{2,10},{6,14},... | collective-permute-start | bytes 196616 | tf_op jit(solution)/shard_map/ppermute | solution.py:493
  119.7 4.9 %collective-permute-start.40 = (bf16[2,2,32,256]{3,2,1,0:T(8,128)(2,1)S(1)}, bf16[2,2,32,256]{3,2,1,0:T(8,128)(2,1)S(1)}, u32[]{:S(2)}, u32[]{:S(2)}) collective-permute-start(bf16[2,2,32,256]{3,2,1,0:T(8,128)(2,1)S(1)} %shard_map.94.rest_0_), channel_id=1, source_target_pairs={{0,4},{4,0},{8,12},{12,8},{1,5},{5,1},{9,13},{13,9},{2,6},{6,2},{1... | collective-permute-start | bytes 196616 | tf_op jit(solution)/shard_map/ppermute | solution.py:493
  121.8 6.5 %collective-permute-start.36 = (bf16[2,2,32,256]{3,2,1,0:T(8,128)(2,1)S(1)}, bf16[2,2,32,256]{3,2,1,0:T(8,128)(2,1)S(1)}, u32[]{:S(2)}, u32[]{:S(2)}) collective-permute-start(bf16[2,2,32,256]{3,2,1,0:T(8,128)(2,1)S(1)} %shard_map.93.rest_0_), channel_id=1, source_target_pairs={{0,4},{4,0},{8,12},{12,8},{1,5},{5,1},{9,13},{13,9},{2,6},{6,2},{1... | collective-permute-start | bytes 196616 | tf_op jit(solution)/shard_map/ppermute | solution.py:493
  123.5 4.8 %collective-permute-start.35 = (bf16[2,2,32,256]{3,2,1,0:T(8,128)(2,1)S(1)}, bf16[2,2,32,256]{3,2,1,0:T(8,128)(2,1)S(1)}, u32[]{:S(2)}, u32[]{:S(2)}) collective-permute-start(bf16[2,2,32,256]{3,2,1,0:T(8,128)(2,1)S(1)} %collective-permute-done.34.rest_1_), channel_id=1, source_target_pairs={{0,4},{4,0},{8,12},{12,8},{1,5},{5,1},{9,13},{13,9},{2,6},{6,2},{1... | collective-permute-start | bytes 196616 | tf_op jit(solution)/shard_map/ppermute | solution.py:493
  (16 other events, 170.3 us)
